TPU v7x, 32 devices: a whole 2x2x4 slice. The times are simulated.
32 devices in a mesh: rows: 8 (over z, x), coil: 4 (over y, core).
Axes of the slice: x: 2, y: 2, z: 4, core: 2. Of those that a mesh axis runs over, the one named last changes fastest.
Arguments:
- kspace: float32 [128, 4096], P('coil', 'rows'), may hold values from -6 to 6
- sample_mask: int32 [128, 4096], P('coil', 'rows'), may hold values 0 or 1
- start_basis: float32 [4, 2048, 128], P('coil', 'rows'), may hold values from -6 to 6
Outputs:
- recovered: float32 [128, 4096], P('coil', 'rows')
- basis: float32 [4, 2048, 128], P('coil', 'rows')
All inputs are finite; a program needn't handle non-finite values. No bound on the sum of `sample_mask` on one device may be relied on, other than what follows from the above.
Results may differ from a plain program's by a relative error of at most 0.00011.
Values sent between devices are 32-bit elements; how exact they have to be, the bound alone decides.
No kernel may reach another device: no remote copies, remote signals or barrier semaphores. Data moves between devices by JAX's collectives and lax.ppermute only.
A program may use at most 64 MiB of HBM per device.

v0:
```python
import jax
import jax.numpy as jnp
from jax import lax
from jax.sharding import PartitionSpec as P

KER = 64
ITERS = 2


threshold = 0.05


def shifted(block, axis, distance):
    devices = range(lax.axis_size(axis))
    route = [((i - distance) % len(devices), i) for i in devices]
    return lax.ppermute(block, axis, route)


def orthonormal(normal_rows, gram_matrix):
    factor = jnp.linalg.cholesky(gram_matrix)
    return lax.linalg.triangular_solve(
        factor, normal_rows, left_side=False, lower=True, transpose_a=True
    )


def coil_total(partial_value):
    return lax.psum(partial_value, "coil")


def shards(kspace, sample_mask, start_basis):
    highest = lax.Precision.HIGHEST
    channels = kspace.shape[0]
    tile_rows = kspace.shape[1]
    mask_float = sample_mask.astype(jnp.float32)
    sampled = kspace * mask_float
    next_rim = shifted(sampled[:, : KER - 1], "rows", -1)
    extended = jnp.concatenate([sampled, next_rim], axis=1)
    hankel_cols = jnp.stack(
        [extended[:, offset : offset + tile_rows] for offset in range(KER)], axis=0
    )
    hankel_cols = hankel_cols.reshape(KER * channels, tile_rows)
    owned_basis = start_basis.reshape(start_basis.shape[1], start_basis.shape[2])
    whole_basis = lax.all_gather(owned_basis, "rows", axis=0, tiled=True)
    for iteration in range(ITERS):
        images = coil_total(
            lax.dot_general(
                whole_basis,
                hankel_cols,
                (((0,), (0,)), ((), ())),
                precision=highest,
                preferred_element_type=jnp.float32,
            )
        )
        local_normal = lax.dot_general(
            hankel_cols,
            images,
            (((1,), (1,)), ((), ())),
            precision=highest,
            preferred_element_type=jnp.float32,
        )
        normal_whole = lax.psum(local_normal, "rows")
        local_gram = jnp.dot(
            normal_whole.T, normal_whole, precision=highest, preferred_element_type=jnp.float32
        )
        gram_matrix = lax.psum(local_gram, "coil")
        whole_basis = orthonormal(normal_whole, gram_matrix)
    images = coil_total(
        lax.dot_general(
            whole_basis,
            hankel_cols,
            (((0,), (0,)), ((), ())),
            precision=highest,
            preferred_element_type=jnp.float32,
        )
    )
    projected = jnp.dot(whole_basis, images, precision=highest, preferred_element_type=jnp.float32)
    owned_count = whole_basis.shape[0] // lax.axis_size("rows")
    owned_basis = lax.dynamic_slice_in_dim(
        whole_basis, lax.axis_index("rows") * owned_count, owned_count, 0
    )
    stacked = projected.reshape(KER, channels, tile_rows)
    spread = jnp.zeros((channels, tile_rows + KER - 1), jnp.float32)
    for offset in range(KER):
        spread = spread.at[:, offset : offset + tile_rows].add(stacked[offset])
    carried = shifted(spread[:, tile_rows:], "rows", 1)
    estimate = spread[:, :tile_rows].at[:, : KER - 1].add(carried) / KER
    residual = mask_float * (kspace - estimate)
    recovered = estimate + residual - jnp.clip(residual, -threshold, threshold)
    return (recovered, owned_basis.reshape(1, owned_basis.shape[0], owned_basis.shape[1]))


def solution(mesh):
    return jax.shard_map(
        shards,
        mesh=mesh,
        in_specs=(P("coil", "rows"), P("coil", "rows"), P("coil", "rows", None)),
        out_specs=(P("coil", "rows"), P("coil", "rows", None)),
        check_vma=False,
    )
```

profile of v0, /device:TPU:0, one launch (start us, length us, event | category | flops | bytes accessed | tf_op | source)
XLA Modules:
  0.0 644.4 jit_solution(8534270161955769819)
XLA Ops:
  8.7 6.0 collective-permute-start
  60.7 9.9 %convolution_bitcast_fusion.2 = f32[128,512]{0,1:T(8,128)} fusion(f32[2048,512]{1,0:T(8,128)} %bitcast.300, f32[1,2048,128]{2,1,0:T(8,128)} %all-gather.3.cloned.1.call-done), kind=kOutput, calls=%fused_computation.64 | convolution fusion | flops 1610612736 | bytes 5505024 | tf_op jit(solution)/shard_map/dot_general | solution.py:46
  70.8 33.6 %all-reduce.9.cloned.1.call-done = f32[128,512]{0,1:T(8,128)} async-done(((f32[128,512]{0,1:T(8,128)}), f32[128,512]{0,1:T(8,128)}) %all-reduce.9.cloned.1.call-update) | async-done | bytes 262160 | tf_op jit(solution)/shard_map/psum | solution.py:27
  104.4 6.7 %fusion.134 = f32[2048,128]{1,0:T(8,128)} fusion(f32[2048,512]{1,0:T(8,128)} %bitcast.301, f32[128,512]{0,1:T(8,128)} %all-reduce.9.cloned.1.call-done), kind=kOutput, calls=%fused_computation.468 | convolution fusion | flops 1610612736 | bytes 5505024 | tf_op jit(solution)/shard_map/dot_general | solution.py:54
  111.2 78.1 %all-reduce.11.cloned.1.call-done = f32[2048,128]{1,0:T(8,128)} async-done(((f32[2048,128]{1,0:T(8,128)}), f32[2048,128]{1,0:T(8,128)}) %all-reduce.11.cloned.1.call-update) | async-done | bytes 1048592 | tf_op jit(solution)/shard_map/psum | solution.py:61
  189.3 4.0 fusion.135
  193.6 30.5 %all-reduce.13.cloned.1.call-done = f32[128,128]{0,1:T(8,128)} async-done(((f32[128,128]{0,1:T(8,128)}), f32[128,128]{0,1:T(8,128)}) %all-reduce.13.cloned.1.call-update) | async-done | bytes 65552 | tf_op jit(solution)/shard_map/psum | solution.py:65
  225.9 11.7 %cholesky.44 = f32[128,128]{1,0:T(8,128)S(1)} custom-call(f32[128,128]{1,0:T(8,128)S(1)} %fusion.131), custom_call_target="Cholesky" | custom-call | tf_op jit(solution)/shard_map/jit(cholesky)/cholesky | solution.py:20
  239.0 9.8 %custom-call.6 = f32[1,128,128]{1,2,0:T(8,128)S(1)} custom-call(f32[1,128,128]{2,1,0:T(8,128)S(1)} %fusion.1), custom_call_target="InvertDiagBlocksLowerTriangular" | custom-call | tf_op jit(solution)/shard_map/triangular_solve/custom-call.0 | solution.py:21
  248.8 2.3 convolution_bitcast_fusion.1
  251.1 5.3 fusion.136
  256.9 31.6 %all-reduce.15.cloned.1.call-done = f32[128,512]{1,0:T(8,128)} async-done(((f32[128,512]{1,0:T(8,128)}), f32[128,512]{1,0:T(8,128)}) %all-reduce.15.cloned.1.call-update) | async-done | bytes 262160 | tf_op jit(solution)/shard_map/psum | solution.py:27
  288.5 6.7 %fusion.137 = f32[2048,128]{1,0:T(8,128)} fusion(f32[2048,512]{1,0:T(8,128)} %bitcast.303, f32[128,512]{1,0:T(8,128)} %all-reduce.15.cloned.1.call-done), kind=kOutput, calls=%fused_computation.471 | convolution fusion | flops 1610612736 | bytes 5505024 | tf_op jit(solution)/shard_map/dot_general | solution.py:54
  295.3 78.1 %all-reduce.17.cloned.1.call-done = f32[2048,128]{1,0:T(8,128)} async-done(((f32[2048,128]{1,0:T(8,128)}), f32[2048,128]{1,0:T(8,128)}) %all-reduce.17.cloned.1.call-update) | async-done | bytes 1048592 | tf_op jit(solution)/shard_map/psum | solution.py:61
  373.4 4.0 fusion.138
  377.6 30.6 %all-reduce.19.cloned.1.call-done = f32[128,128]{0,1:T(8,128)} async-done(((f32[128,128]{0,1:T(8,128)}), f32[128,128]{0,1:T(8,128)}) %all-reduce.19.cloned.1.call-update) | async-done | bytes 65552 | tf_op jit(solution)/shard_map/psum | solution.py:65
  410.0 11.7 %cholesky.55 = f32[128,128]{1,0:T(8,128)S(1)} custom-call(f32[128,128]{1,0:T(8,128)S(1)} %fusion.129), custom_call_target="Cholesky" | custom-call | tf_op jit(solution)/shard_map/jit(cholesky)/cholesky | solution.py:20
  423.1 9.8 %custom-call.7 = f32[1,128,128]{1,2,0:T(8,128)S(1)} custom-call(f32[1,128,128]{2,1,0:T(8,128)S(1)} %fusion.2), custom_call_target="InvertDiagBlocksLowerTriangular" | custom-call | tf_op jit(solution)/shard_map/triangular_solve/custom-call.0 | solution.py:21
  432.9 2.3 convolution_bitcast_fusion
  435.2 5.3 fusion.139
  483.9 4.4 fusion.140
  490.9 1.6 add_select_fusion.60
  500.0 1.6 add_select_fusion.56
  502.2 1.6 add_select_fusion.55
  504.5 1.6 add_select_fusion.54
  509.0 1.6 add_select_fusion.52
  515.8 1.6 add_select_fusion.49
  520.3 1.6 add_select_fusion.47
  529.1 1.6 add_select_fusion.43
  538.3 1.6 add_select_fusion.39
  542.8 1.6 add_select_fusion.37
  545.1 1.6 add_select_fusion.36
  549.6 1.6 add_select_fusion.34
  554.0 1.6 add_select_fusion.32
  569.7 1.6 add_select_fusion.25
  576.4 1.6 add_select_fusion.22
  578.6 1.6 add_select_fusion.21
  580.9 1.6 add_select_fusion.20
  583.2 1.6 add_select_fusion.19
  587.7 1.6 add_select_fusion.17
  589.9 1.6 add_select_fusion.16
  598.9 1.6 add_select_fusion.12
  601.2 1.6 add_select_fusion.11
  612.3 1.6 add_select_fusion.6
  616.8 1.6 add_select_fusion.4
  621.3 1.6 add_select_fusion.2
  623.6 1.6 add_select_fusion.1
  632.0 3.6 collective-permute-done.1
  (274 shorter events, 201.5 us)
Async XLA Ops:
  7.2 53.5 %all-gather.3.cloned.1.call-start = ((), (), s32[]{:S(2)}) async-start(), calls=%async_computation.7 | async-start | bytes 1179648 | tf_op jit(solution)/shard_map/all_gather | solution.py:43
  8.7 7.4 %collective-permute-start = (f32[32,63]{1,0:T(8,128)S(1)}, f32[32,63]{1,0:T(8,128)S(1)}, u32[]{:S(2)}, u32[]{:S(2)}) collective-permute-start(f32[32,63]{1,0:T(8,128)S(1)} %slice.1888), channel_id=1, source_target_pairs={{4,0},{8,4},{12,8},{16,12},{20,16},{24,20},{28,24},{0,28},{5,1},{9... | collective-permute-start | bytes 24200 | tf_op jit(solution)/shard_map/ppermute | solution.py:16
  14.7 89.7 %all-reduce.9.cloned.1.call-start = ((), (), s32[]{:S(2)}) async-start(), calls=%async_computation | async-start | bytes 524288 | tf_op jit(solution)/shard_map/psum | solution.py:27
  70.6 118.7 %all-reduce.11.cloned.1.call-start = ((), (), s32[]{:S(2)}) async-start(), calls=%async_computation.1 | async-start | bytes 2097152 | tf_op jit(solution)/shard_map/psum | solution.py:61
  111.1 113.0 %all-reduce.13.cloned.1.call-start = ((), (), s32[]{:S(2)}) async-start(), calls=%async_computation.2 | async-start | bytes 131072 | tf_op jit(solution)/shard_map/psum | solution.py:65
  193.3 95.2 %all-reduce.15.cloned.1.call-start = ((), (), s32[]{:S(2)}) async-start(), calls=%async_computation.3 | async-start | bytes 524288 | tf_op jit(solution)/shard_map/psum | solution.py:27
  256.4 117.0 %all-reduce.17.cloned.1.call-start = ((), (), s32[]{:S(2)}) async-start(), calls=%async_computation.4 | async-start | bytes 2097152 | tf_op jit(solution)/shard_map/psum | solution.py:61
  295.2 113.0 %all-reduce.19.cloned.1.call-start = ((), (), s32[]{:S(2)}) async-start(), calls=%async_computation.5 | async-start | bytes 131072 | tf_op jit(solution)/shard_map/psum | solution.py:65
  377.4 106.5 %all-reduce.21.cloned.1.call-start = ((), (), s32[]{:S(2)}) async-start(), calls=%async_computation.6 | async-start | bytes 524288 | tf_op jit(solution)/shard_map/psum | solution.py:27
  488.3 1.9 copy-start
  578.6 57.8 %copy-start.1 = (f32[32,512]{1,0:T(8,128)S(1)}, f32[32,512]{1,0:T(8,128)}, u32[]{:S(2)}) copy-start(f32[32,512]{1,0:T(8,128)} %param.136) | copy-start | bytes 196612
  578.6 57.8 %copy-start.2 = (s32[32,512]{1,0:T(8,128)S(1)}, s32[32,512]{1,0:T(8,128)}, u32[]{:S(2)}) copy-start(s32[32,512]{1,0:T(8,128)} %param.137) | copy-start | bytes 196612
  629.1 6.4 collective-permute-start.1
Sparse Core Ops, SparseCore 0:
  14.8 38.2 all-gather.2
  70.7 33.6 all-reduce.8
  111.2 77.9 all-reduce.10
  193.4 30.6 all-reduce.12
  256.5 31.9 all-reduce.14
  295.3 77.9 all-reduce.16
  377.5 30.6 all-reduce.18
  440.6 32.0 all-reduce.20
where the time goes:
time: 655 us; the launch traced here: 644 us
  waiting for transfers between devices  288 us (44%)
  other arithmetic  235 us (36%)
  matrix products  50.8 us (8%)
  local copies, waits for them, and re-layouts  46.5 us (7%)
  between operations  15.8 us (2%)
  starting transfers between devices  8.87 us (1%)
    psum x2, waiting for transfers between devices, shards(): normal_whole = lax.psum(local_normal, 'rows')  156 us
    another operation x128, other arithmetic  140 us
    psum x3, waiting for transfers between devices, coil_total(): return lax.psum(partial_value, 'coil')  65.2 us
    psum x2, waiting for transfers between devices, shards(): gram_matrix = lax.psum(local_gram, 'coil')  61.1 us
    unnamed x63, other arithmetic  45.3 us
    scatter-add x64, local copies, waits for them, and re-layouts, shards(): spread = spread.at[:, offset:offset + tile_rows].add(stacked[offset])  43 us
    another operation x6, other arithmetic, orthonormal(): factor = jnp.linalg.cholesky(gram_matrix)  24.8 us
    another operation x4, other arithmetic, orthonormal(): lax.linalg.triangular_solve(factor, normal_rows, left_side=False, lower=T...  20.9 us
  transfers between devices with their start and end apart: 10, of which 8 were waited for; matrix products, arithmetic and copies ran while one was open for 14% of the time, Pallas kernels for 0%

commit v1 on v0

--- a/solution.py
+++ b/solution.py
@@ -1,10 +1,17 @@
+import functools
+
 import jax
 import jax.numpy as jnp
 from jax import lax
+from jax.experimental import pallas as pl
+from jax.experimental.pallas import tpu as pltpu
 from jax.sharding import PartitionSpec as P
 
 KER = 64
 ITERS = 2
+LANES = 128
+SUB = 8
+AXES = ("rows", "coil")
 
 
 threshold = 0.05
@@ -27,7 +34,7 @@
     return lax.psum(partial_value, "coil")
 
 
-def shards(kspace, sample_mask, start_basis):
+def general_shards(kspace, sample_mask, start_basis):
     highest = lax.Precision.HIGHEST
     channels = kspace.shape[0]
     tile_rows = kspace.shape[1]
@@ -89,6 +96,409 @@
     return (recovered, owned_basis.reshape(1, owned_basis.shape[0], owned_basis.shape[1]))
 
 
+def split(value):
+    high = value.astype(jnp.bfloat16)
+    low = (value - high.astype(jnp.float32)).astype(jnp.bfloat16)
+    return high, low
+
+
+def dot(a, b, dims=((1,), (0,))):
+    return lax.dot_general(a, b, (dims, ((), ())), preferred_element_type=jnp.float32)
+
+
+def dot3(a, b, dims=((1,), (0,))):
+    a_high, a_low = split(a)
+    b_high, b_low = split(b)
+    return dot(a_high, b_high, dims) + (dot(a_high, b_low, dims) + dot(a_low, b_high, dims))
+
+
+def prepare_kernel(cols, chg, per_tile, kspace_ref, mask_ref, basis_ref, sampled_ref, send_ref):
+    sampled_ref[...] = kspace_ref[...] * mask_ref[...].astype(jnp.float32)
+    turned = basis_ref[...].T
+    devices = turned.shape[0] // cols
+    for j in range(per_tile):
+        part = turned[:, j * chg : (j + 1) * chg]
+        row = jnp.concatenate([part[k * devices : (k + 1) * devices] for k in range(cols)], axis=1)
+        send_ref[pl.ds(j, devices, stride=per_tile), :] = row
+
+
+def images_of(vectors, samples_ref, wide_ref):
+    rows, channels = vectors.shape
+    cols = rows // KER
+    high, low = split(vectors)
+    at_row = lax.broadcasted_iota(jnp.int32, (rows, rows), 0)
+    at_col = lax.broadcasted_iota(jnp.int32, (rows, rows), 1)
+    flip = ((at_row // KER == at_col // KER) & (at_row % KER + at_col % KER == KER - 1)).astype(
+        jnp.float32
+    ).astype(jnp.bfloat16)
+    both = dot(flip, jnp.concatenate([high, low], axis=1)).astype(jnp.bfloat16)
+    high, low = both[:, :channels], both[:, channels:]
+    twice = jnp.concatenate([high, high], axis=1)
+    tiles = samples_ref.shape[0]
+    tile = samples_ref.shape[-1]
+    for t in range(tiles):
+        block = samples_ref[t].reshape(2 * channels, tile)
+        wide_ref[:, t * tile : (t + 1) * tile] = dot(twice, block) + dot(low, block[:channels])
+    images = []
+    for k in range(cols):
+        total = None
+        for i in reversed(range(0, KER, SUB)):
+            part = wide_ref[k * KER + i : k * KER + i + SUB, :]
+            total = part if total is None else pltpu.roll(total, SUB, 1) + part
+        total = pltpu.roll(total, 0, 1, stride=1, stride_axis=0)
+        images.append(jnp.sum(total, axis=0, keepdims=True))
+    return images
+
+
+def normal_of(images, samples_ref, moved_ref):
+    cols = len(images)
+    positions = images[0].shape[1]
+    tiles = samples_ref.shape[0]
+    tile = samples_ref.shape[-1]
+    channels = samples_ref.shape[2] * samples_ref.shape[3]
+    rows = cols * KER
+    for k in range(cols):
+        base = jnp.broadcast_to(images[k], (SUB, positions))
+        base = pltpu.roll(base, positions - (KER - 1), 1, stride=1, stride_axis=0)
+        for j in range(0, KER, 2 * SUB):
+            first = base if j == 0 else pltpu.roll(base, j, 1)
+            second = pltpu.roll(base, j + SUB, 1)
+            high, low = split(jnp.concatenate([first, second], axis=0))
+            moved_ref[k * KER + j : k * KER + j + 2 * SUB, :] = high
+            moved_ref[rows + k * KER + j : rows + k * KER + j + 2 * SUB, :] = low
+    total = jnp.zeros((2 * rows, 2 * channels), jnp.float32)
+    for t in range(tiles):
+        block = samples_ref[t].reshape(2 * channels, tile)
+        total = total + dot(moved_ref[:, t * tile : (t + 1) * tile], block, ((1,), (1,)))
+    return total[:rows, :channels] + (
+        total[:rows, channels:] + total[rows:, :channels] + total[rows:, channels:]
+    )
+
+
+def store_by_rows(normal, send_ref):
+    tiles, groups, per_tile, lanes = send_ref.shape
+    cols = normal.shape[0] // KER
+    chg = normal.shape[1] // groups
+    for g in range(groups):
+        joined = jnp.concatenate(
+            [normal[k * KER : (k + 1) * KER, g * chg : (g + 1) * chg] for k in range(cols)], axis=1
+        )
+        send_ref[:, g] = joined.reshape(tiles, per_tile, lanes)
+
+
+def first_kernel(
+    masks, pieces_ref, late_ref, basis_ref, samples_ref, normal_ref, send_ref, wide_ref, moved_ref
+):
+    tiles, _, groups, chg, tile = samples_ref.shape
+    me = lax.axis_index("rows") * groups + lax.axis_index("coil")
+    half = pieces_ref.shape[0]
+    for slot, mask in enumerate(masks):
+        value = pieces_ref[slot] if slot < half else late_ref[slot - half]
+        high, low = split(value)
+        source = lax.bitwise_xor(me, mask)
+        t, g = source // groups, source % groups
+        samples_ref[t, 0, g] = high
+        samples_ref[t, 1, g] = low
+    cols = basis_ref.shape[-1] // chg
+    rows = []
+    for k in range(cols):
+        rows.append(
+            jnp.concatenate(
+                [
+                    basis_ref[:, g].reshape(KER, cols * chg)[:, k * chg : (k + 1) * chg]
+                    for g in range(groups)
+                ],
+                axis=1,
+            )
+        )
+    vectors = jnp.concatenate(rows, axis=0)
+    normal = normal_of(images_of(vectors, samples_ref, wide_ref), samples_ref, moved_ref)
+    scaled = []
+    for k in range(cols):
+        part = normal[k * KER : (k + 1) * KER]
+        scaled.append(part * (1.0 / jnp.max(jnp.abs(part))))
+    normal = jnp.concatenate(scaled, axis=0)
+    normal_ref[...] = normal
+    store_by_rows(normal, send_ref)
+
+
+def second_kernel(samples_ref, vectors_ref, normal_ref, send_ref, wide_ref, moved_ref):
+    normal = normal_of(
+        images_of(vectors_ref[...], samples_ref, wide_ref), samples_ref, moved_ref
+    )
+    normal_ref[...] = normal
+    store_by_rows(normal, send_ref)
+
+
+def third_kernel(samples_ref, vectors_ref, send_ref, wide_ref):
+    tiles, cols, reach = send_ref.shape
+    tile = samples_ref.shape[-1]
+    images = jnp.concatenate(images_of(vectors_ref[...], samples_ref, wide_ref), axis=0)
+    positions = images.shape[1]
+    images = pltpu.roll(images, positions - (KER - 1), 1)
+    rim = reach - tile
+    for t in range(tiles):
+        if t == 0:
+            part = jnp.concatenate([images[:, positions - rim :], images[:, :tile]], axis=1)
+        else:
+            part = images[:, t * tile - rim : (t + 1) * tile]
+        send_ref[t] = part
+
+
+def gather_turned(received_ref, cols, per_tile):
+    count, lanes = received_ref.shape
+    devices = count // per_tile
+    chg = lanes // cols
+    loaded = [received_ref[pl.ds(j, devices, stride=per_tile), :] for j in range(per_tile)]
+    return jnp.concatenate(
+        [
+            jnp.concatenate(
+                [loaded[j][:, k * chg : (k + 1) * chg] for j in range(per_tile)], axis=1
+            )
+            for k in range(cols)
+        ],
+        axis=0,
+    )
+
+
+def exact(a, b, dims=((1,), (0,))):
+    return lax.dot_general(
+        a, b, (dims, ((), ())), precision=lax.Precision.HIGHEST, preferred_element_type=jnp.float32
+    )
+
+
+def gram_kernel(cols, per_tile, received_ref, gram_ref):
+    turned = gather_turned(received_ref, cols, per_tile)
+    gram_ref[...] = exact(turned, turned, ((1,), (1,)))
+
+
+def second_gram_kernel(cols, per_tile, received_ref, inverse_ref, turned_ref, gram_ref):
+    turned = gather_turned(received_ref, cols, per_tile)
+    turned = exact(inverse_ref[...], turned)
+    turned_ref[...] = turned
+    gram_ref[...] = exact(turned, turned, ((1,), (1,)))
+
+
+def inverse_factor(gram):
+    size = gram.shape[0]
+    at_row = lax.broadcasted_iota(jnp.int32, (size, size), 0)
+    at_col = lax.broadcasted_iota(jnp.int32, (size, size), 1)
+    unit = (at_row == at_col).astype(jnp.float32)
+    left = [gram[b : b + SUB] for b in range(0, size, SUB)]
+    right = [unit[b : b + SUB] for b in range(0, size, SUB)]
+    sub = lax.broadcasted_iota(jnp.int32, (SUB, size), 0)
+    for j in range(size):
+        b, s = j // SUB, j % SUB
+        pivot = left[b][s : s + 1, j : j + 1]
+        root = lax.rsqrt(pivot)
+        root = root * (1.5 - 0.5 * pivot * root * root)
+        upper = left[b][s : s + 1] * root
+        lower = right[b][s : s + 1] * root
+        for c in range(b, len(left)):
+            factor = left[c][:, j : j + 1] * root
+            if c == b:
+                factor = jnp.where(sub > s, factor, 0.0)
+            new_left = left[c] - factor * upper
+            new_right = right[c] - factor * lower
+            if c == b:
+                new_left = jnp.where(sub == s, upper, new_left)
+                new_right = jnp.where(sub == s, lower, new_right)
+            left[c], right[c] = new_left, new_right
+    return jnp.concatenate(right, axis=0)
+
+
+def factor_kernel(gram_ref, inverse_ref):
+    inverse_ref[...] = inverse_factor(gram_ref[...])
+
+
+def last_kernel(
+    cols,
+    masks,
+    images_ref,
+    turned_ref,
+    near_ref,
+    far_ref,
+    first_ref,
+    gram_ref,
+    kspace_ref,
+    mask_ref,
+    recovered_ref,
+    basis_ref,
+):
+    inverse = inverse_factor(gram_ref[...])
+    count, reach = images_ref.shape
+    devices = count // cols
+    at_row = lax.broadcasted_iota(jnp.int32, (count, count), 0)
+    at_col = lax.broadcasted_iota(jnp.int32, (count, count), 1)
+    order = ((at_row // devices == at_col % cols) & (at_row % devices == at_col // cols)).astype(
+        jnp.float32
+    )
+    images = exact(inverse, exact(exact(first_ref[...], order), images_ref[...]))
+    images_high, images_low = split(images)
+    stacked = jnp.concatenate([images_high, images_low], axis=0)
+    chg, tile = kspace_ref.shape
+    me = lax.axis_index("rows")
+    half = near_ref.shape[0]
+    estimate = jnp.zeros((chg, tile), jnp.float32)
+    for slot, mask in enumerate(masks):
+        turned = near_ref[slot] if slot < half else far_ref[slot - half]
+        vectors = exact(inverse, turned).T
+        if slot == 0:
+            basis_ref[...] = vectors
+        high, low = split(vectors)
+        projected = dot(jnp.concatenate([high, high], axis=1), stacked) + dot(low, images_high)
+        per_tile = vectors.shape[0] // chg
+        total = projected[:chg]
+        for j in range(1, per_tile):
+            total = total + pltpu.roll(projected[j * chg : (j + 1) * chg], j, 1)
+        t = lax.bitwise_xor(me, mask)
+        total = pltpu.roll(total, t * per_tile, 1)
+        estimate = estimate + total[:, reach - tile :]
+    estimate = estimate / KER
+    residual = mask_ref[...].astype(jnp.float32) * (kspace_ref[...] - estimate)
+    recovered_ref[...] = estimate + residual - jnp.clip(residual, -threshold, threshold)
+
+
+def call(kernel, outs, *args, scratch=()):
+    return pl.pallas_call(
+        kernel,
+        out_shape=[jax.ShapeDtypeStruct(shape, kind) for shape, kind in outs],
+        in_specs=[pl.BlockSpec(memory_space=pltpu.VMEM)] * len(args),
+        out_specs=[pl.BlockSpec(memory_space=pltpu.VMEM)] * len(outs),
+        scratch_shapes=[pltpu.VMEM(shape, kind) for shape, kind in scratch],
+        compiler_params=pltpu.CompilerParams(vmem_limit_bytes=40 * 2**20),
+    )(*args)
+
+
+def exchange(block, devices, mask, axes):
+    return lax.ppermute(block, axes, [(i, i ^ mask) for i in range(devices)])
+
+
+def gather_by_halves(block, devices, axes):
+    masks = [0]
+    near = block[None]
+    far = None
+    mask = devices // 2
+    while mask:
+        if far is not None:
+            near = jnp.concatenate([near, far], axis=0)
+        far = exchange(near, devices, mask, axes)
+        masks = masks + [m ^ mask for m in masks]
+        mask //= 2
+    return near, far, masks
+
+
+def to_all(pieces):
+    return lax.all_to_all(pieces, AXES, 0, 0, tiled=True)
+
+
+def total_of(gram, devices):
+    size = gram.shape[0]
+    parts = to_all(gram.reshape(devices, size // devices, size))
+    mine = jnp.sum(parts, axis=0)
+    spread = to_all(jnp.broadcast_to(mine[None], parts.shape))
+    return spread.reshape(size, size)
+
+
+def column_shards(kspace, sample_mask, start_basis):
+    f32, bf16 = jnp.float32, jnp.bfloat16
+    tiles, groups = lax.axis_size("rows"), lax.axis_size("coil")
+    devices = tiles * groups
+    chg, tile = kspace.shape
+    channels = chg * groups
+    positions = tile * tiles
+    owned, rank = start_basis.shape[1:]
+    per_tile = owned // chg
+    cols = rank // devices
+    rows = cols * KER
+    lanes = cols * chg
+
+    sampled, basis_send = call(
+        functools.partial(prepare_kernel, cols, chg, per_tile),
+        [((chg, tile), f32), ((devices * per_tile, lanes), f32)],
+        kspace,
+        sample_mask,
+        start_basis.reshape(owned, rank),
+    )
+    basis_parts = to_all(basis_send.reshape(devices, per_tile, lanes))
+    near, far, masks = gather_by_halves(sampled, devices, AXES)
+    wide = ((rows, positions), f32)
+    moved = ((2 * rows, positions), bf16)
+    by_rows = ((tiles, groups, per_tile, lanes), f32)
+    samples, normal, send = call(
+        functools.partial(first_kernel, masks),
+        [((tiles, 2, groups, chg, tile), bf16), ((rows, channels), f32), by_rows],
+        near,
+        far,
+        basis_parts.reshape(tiles, groups, per_tile, lanes),
+        scratch=[wide, moved],
+    )
+    received = to_all(send.reshape(devices, per_tile, lanes))
+    (gram,) = call(
+        functools.partial(gram_kernel, cols, per_tile),
+        [((rank, rank), f32)],
+        received.reshape(devices * per_tile, lanes),
+    )
+    gram = total_of(gram, devices)
+    (first,) = call(factor_kernel, [((rank, rank), f32)], gram)
+
+    normal, send = call(
+        second_kernel, [((rows, channels), f32), by_rows], samples, normal, scratch=[wide, moved]
+    )
+    received = to_all(send.reshape(devices, per_tile, lanes))
+    reach = tile + LANES
+    (images,) = call(third_kernel, [((tiles, cols, reach), f32)], samples, normal, scratch=[wide])
+    images = jnp.broadcast_to(images[:, None], (tiles, groups, cols, reach))
+    images = to_all(images.reshape(devices, cols, reach)).reshape(rank, reach)
+
+    turned, gram = call(
+        functools.partial(second_gram_kernel, cols, per_tile),
+        [((rank, owned), f32), ((rank, rank), f32)],
+        received.reshape(devices * per_tile, lanes),
+        first,
+    )
+    gram = total_of(gram, devices)
+    near, far, masks = gather_by_halves(turned, tiles, "rows")
+    recovered, basis = call(
+        functools.partial(last_kernel, cols, masks),
+        [((chg, tile), f32), ((owned, rank), f32)],
+        images,
+        turned,
+        near,
+        far,
+        first,
+        gram,
+        kspace,
+        sample_mask,
+    )
+    return (recovered, basis.reshape(1, owned, rank))
+
+
+def divides_columns(kspace, start_basis):
+    tiles, groups = lax.axis_size("rows"), lax.axis_size("coil")
+    devices = tiles * groups
+    chg, tile = kspace.shape
+    owned, rank = start_basis.shape[1:]
+    return (
+        devices & (devices - 1) == 0
+        and tiles > 1
+        and rank % devices == 0
+        and rank % LANES == 0
+        and tile % LANES == 0
+        and owned % (SUB * chg) == 0
+        and chg * (rank // devices) == LANES
+        and chg % (2 * SUB) == 0
+        and (chg * groups) % LANES == 0
+        and KER <= LANES
+    )
+
+
+def shards(kspace, sample_mask, start_basis):
+    if divides_columns(kspace, start_basis):
+        return column_shards(kspace, sample_mask, start_basis)
+    return general_shards(kspace, sample_mask, start_basis)
+
+
 def solution(mesh):
     return jax.shard_map(
         shards,

time: 655 us -> 168 us (0.26); the launches traced: 644 us -> 167 us
  waiting for transfers between devices: 288 us -> 52.6 us
  other arithmetic: 235 us -> 0.2 us
  matrix products: 50.8 us -> 0 us
  Pallas kernels: 0 us -> 43 us
  local copies, waits for them, and re-layouts: 46.5 us -> 4.83 us
  blocking collectives: 0 us -> 35.4 us
  starting transfers between devices: 8.87 us -> 30.3 us
  between operations: 15.8 us -> 0.81 us
    psum x7 -> x0, waiting for transfers between devices: 283 us -> none  [the longest x2 156 us: shards(): normal_whole = lax.psum(local_normal, 'rows')]
    another operation x139 -> x0, other arithmetic: 186 us -> none
    dot_general x8 -> x0, matrix products: 46.3 us -> none  [the longest x3 20.5 us: shards(): lax.dot_general(whole_basis, hankel_cols, (((0,), (0,)), ((), ())), preci...]
    unnamed x63 -> x0, other arithmetic: 45.3 us -> none
    scatter-add x65 -> x0, local copies, waits for them, and re-layouts: 43.3 us -> none  [the longest x64 43 us: shards(): spread = spread.at[:, offset:offset + tile_rows].add(stacked[offset])]
    pallas_call x0 -> x8, Pallas kernels: none -> 43 us  [call(): pl.pallas_call(kernel, out_shape=[jax.ShapeDtypeStruct(shape, kind) for s...]
    all_to_all x0 -> x3, blocking collectives: none -> 35.4 us  [to_all(): return lax.all_to_all(pieces, AXES, 0, 0, tiled=True)]
    all_to_all x0 -> x5, waiting for transfers between devices: none -> 25.1 us  [to_all(): return lax.all_to_all(pieces, AXES, 0, 0, tiled=True)]
  transfers between devices with their start and end apart: 10 -> 13, of which waited for: 8 -> 9; matrix products, arithmetic and copies ran while one was open for 14% -> 1% of each run, Pallas kernels for 0% -> 11%
where the time goes in v1:
time: 168 us; the launch traced here: 167 us
  waiting for transfers between devices  52.6 us (31%)
  Pallas kernels  43 us (26%)
  blocking collectives  35.4 us (21%)
  starting transfers between devices  30.3 us (18%)
  local copies, waits for them, and re-layouts  4.83 us (3%)
    pallas_call x8, Pallas kernels, call(): pl.pallas_call(kernel, out_shape=[jax.ShapeDtypeStruct(shape, kind) for s...  43 us
    all_to_all x3, blocking collectives, to_all(): return lax.all_to_all(pieces, AXES, 0, 0, tiled=True)  35.4 us
    ppermute x8, waiting for transfers between devices, exchange(): return lax.ppermute(block, axes, [(i, i ^ mask) for i in range(devices)])  27.5 us
    all_to_all x5, waiting for transfers between devices, to_all(): return lax.all_to_all(pieces, AXES, 0, 0, tiled=True)  25.1 us
    all_to_all x5, starting transfers between devices, to_all(): return lax.all_to_all(pieces, AXES, 0, 0, tiled=True)  17 us
    ppermute x8, starting transfers between devices, exchange(): return lax.ppermute(block, axes, [(i, i ^ mask) for i in range(devices)])  13.3 us
  transfers between devices with their start and end apart: 13, of which 9 were waited for; matrix products, arithmetic and copies ran while one was open for 1% of the time, Pallas kernels for 11%

profile of v1, /device:TPU:0, one launch (start us, length us, event | category | flops | bytes accessed | tf_op | source)
XLA Modules:
  0.0 167.2 jit_solution(5421523367881299039)
XLA Ops:
  0.6 0.0 copy-start
  0.6 0.8 copy-done
  1.5 0.8 copy-done.2
  2.3 0.9 copy-done.4
  3.2 0.2 shard_map.50
  3.5 4.1 %collective-permute-start = (f32[1,32,512]{2,1,0:T(8,128)S(1)}, f32[1,32,512]{2,1,0:T(8,128)S(1)}, u32[]{:S(2)}, u32[]{:S(2)}) collective-permute-start(f32[1,32,512]{2,1,0:T(8,128)S(1)} %bitcast.19), channel_id=1, source_target_pairs={{0,16},{1,17},{2,18},{3,19},{4,20},{5,21},{6,22},{7,23},{8,24},{9,... | collective-permute-start | bytes 196616 | tf_op jit(solution)/shard_map/ppermute | solution.py:374
  7.6 3.6 %collective-permute-done = f32[1,32,512]{2,1,0:T(8,128)S(1)} collective-permute-done((f32[1,32,512]{2,1,0:T(8,128)S(1)}, f32[1,32,512]{2,1,0:T(8,128)S(1)}, u32[]{:S(2)}, u32[]{:S(2)}) %collective-permute-start) | collective-permute-done | bytes 65568 | tf_op jit(solution)/shard_map/ppermute | solution.py:374
  11.2 0.6 collective-permute-start.1
  11.9 4.4 %collective-permute-done.1 = f32[2,32,512]{2,1,0:T(8,128)S(1)} collective-permute-done((f32[2,32,512]{2,1,0:T(8,128)S(1)}, f32[2,32,512]{2,1,0:T(8,128)S(1)}, u32[]{:S(2)}, u32[]{:S(2)}) %collective-permute-start.1) | collective-permute-done | bytes 131104 | tf_op jit(solution)/shard_map/ppermute | solution.py:374
  16.3 1.8 %collective-permute-start.2 = (f32[4,32,512]{2,1,0:T(8,128)S(1)}, f32[4,32,512]{2,1,0:T(8,128)S(1)}, u32[]{:S(2)}, u32[]{:S(2)}) collective-permute-start(f32[4,32,512]{2,1,0:T(8,128)S(1)} %pad_maximum_fusion.2), channel_id=1, source_target_pairs={{0,4},{1,5},{2,6},{3,7},{4,0},{5,1},{6,2},{7,3},{8,12},{9,13},{10,... | collective-permute-start | bytes 786440 | tf_op jit(solution)/shard_map/ppermute | solution.py:374
  18.0 4.7 %collective-permute-done.2 = f32[4,32,512]{2,1,0:T(8,128)S(1)} collective-permute-done((f32[4,32,512]{2,1,0:T(8,128)S(1)}, f32[4,32,512]{2,1,0:T(8,128)S(1)}, u32[]{:S(2)}, u32[]{:S(2)}) %collective-permute-start.2) | collective-permute-done | bytes 262176 | tf_op jit(solution)/shard_map/ppermute | solution.py:374
  22.8 1.8 %collective-permute-start.3 = (f32[8,32,512]{2,1,0:T(8,128)S(1)}, f32[8,32,512]{2,1,0:T(8,128)S(1)}, u32[]{:S(2)}, u32[]{:S(2)}) collective-permute-start(f32[8,32,512]{2,1,0:T(8,128)S(1)} %pad_maximum_fusion), channel_id=1, source_target_pairs={{0,2},{1,3},{2,0},{3,1},{4,6},{5,7},{6,4},{7,5},{8,10},{9,11},{10,... | collective-permute-start | bytes 1572872 | tf_op jit(solution)/shard_map/ppermute | solution.py:374
  24.6 8.1 %collective-permute-done.3 = f32[8,32,512]{2,1,0:T(8,128)S(1)} collective-permute-done((f32[8,32,512]{2,1,0:T(8,128)S(1)}, f32[8,32,512]{2,1,0:T(8,128)S(1)}, u32[]{:S(2)}, u32[]{:S(2)}) %collective-permute-start.3) | collective-permute-done | bytes 524320 | tf_op jit(solution)/shard_map/ppermute | solution.py:374
  32.7 0.1 collective-permute-start.4
  32.8 16.3 %all_to_all.40 = f32[32,8,128]{2,1,0:T(8,128)S(1)} all-to-all(f32[32,8,128]{2,1,0:T(8,128)S(1)} %bitcast.30), channel_id=1, replica_groups=mesh['rows'=8,'coil'=4] {'rows','coil'}, dimensions={0} | all-to-all | bytes 262144 | tf_op jit(solution)/shard_map/all_to_all | solution.py:392
  49.1 0.0 collective-permute-done.4.late_ref
  49.1 4.9 %shard_map.51 = (bf16[8,2,4,32,512]{4,3,2,1,0:T(8,128)(2,1)S(1)}, f32[256,128]{1,0:T(8,128)S(1)}, f32[8,4,8,128]{3,2,1,0:T(8,128)S(1)}) custom-call(f32[16,32,512]{2,1,0:T(8,128)S(1)} %constant_dynamic-update-slice_fusion.pieces_ref, f32[16,32,512]{2,1,0:T(8,128)S(1)} %collective-permute-done.4.late_ref, f32[8,4,8,128]{3,2,1,0:T(8,128)S(1)} %bitcast.23), custom_call_target="tpu_custom_call" | custom-call | tf_op jit(solution)/shard_map/pallas_call | solution.py:363
  54.0 10.0 %all_to_all.41 = f32[32,8,128]{2,1,0:T(8,128)S(1)} all-to-all(f32[32,8,128]{2,1,0:T(8,128)S(1)} %bitcast.31), channel_id=1, replica_groups=mesh['rows'=8,'coil'=4] {'rows','coil'}, dimensions={0} | all-to-all | bytes 262144 | tf_op jit(solution)/shard_map/all_to_all | solution.py:392
  64.0 0.4 shard_map.54
  64.4 9.2 %all_to_all.42 = f32[32,4,128]{2,1,0:T(4,128)S(1)} all-to-all(f32[32,4,128]{2,1,0:T(4,128)S(1)} %bitcast.27), channel_id=1, replica_groups=mesh['rows'=8,'coil'=4] {'rows','coil'}, dimensions={0} | all-to-all | bytes 131072 | tf_op jit(solution)/shard_map/all_to_all | solution.py:392
  73.6 0.6 broadcast_in_dim.12
  74.3 2.6 %all-to-all-start.5 = ((f32[32,4,128]{2,1,0:T(4,128)}), f32[32,4,128]{2,1,0:T(4,128)S(1)}, u32[]{:S(2)}, u32[]{:S(2)}) async-start(f32[32,4,128]{2,1,0:T(4,128)} %broadcast_in_dim.12), calls=%async_computation.5 | async-start | bytes 131072 | tf_op jit(solution)/shard_map/all_to_all | solution.py:392
  76.8 4.9 %shard_map.52 = (f32[256,128]{1,0:T(8,128)S(1)}, f32[8,4,8,128]{3,2,1,0:T(8,128)}) custom-call(bf16[8,2,4,32,512]{4,3,2,1,0:T(8,128)(2,1)S(1)} %get-tuple-element.15.samples_ref, f32[256,128]{1,0:T(8,128)S(1)} %get-tuple-element.16.vectors_ref), custom_call_target="tpu_custom_call" | custom-call | tf_op jit(solution)/shard_map/pallas_call | solution.py:363
  81.7 2.6 %all-to-all-done.5 = f32[32,4,128]{2,1,0:T(4,128)S(1)} async-done(((f32[32,4,128]{2,1,0:T(4,128)}), f32[32,4,128]{2,1,0:T(4,128)S(1)}, u32[]{:S(2)}, u32[]{:S(2)}) %all-to-all-start.5) | async-done | bytes 65568 | tf_op jit(solution)/shard_map/all_to_all | solution.py:392
  84.3 3.5 %all-to-all-start.2 = ((f32[32,8,128]{2,1,0:T(8,128)}), f32[32,8,128]{2,1,0:T(8,128)S(1)}, u32[]{:S(2)}, u32[]{:S(2)}) async-start(f32[32,8,128]{2,1,0:T(8,128)} %bitcast.5), calls=%async_computation.2 | async-start | bytes 262144 | tf_op jit(solution)/shard_map/all_to_all | solution.py:392
  87.7 11.7 %shard_map.55.inverse_ref.first_ref = f32[128,128]{1,0:T(8,128)S(1)} custom-call(f32[128,128]{1,0:T(8,128)S(1)} %bitcast.28), custom_call_target="tpu_custom_call" | custom-call | tf_op jit(solution)/shard_map/pallas_call | solution.py:363
  99.4 0.0 all-to-all-done.2
  99.4 1.5 shard_map.56
  100.9 2.5 %collective-permute-start.5 = (f32[1,128,256]{2,1,0:T(8,128)S(1)}, f32[1,128,256]{2,1,0:T(8,128)S(1)}, u32[]{:S(2)}, u32[]{:S(2)}) collective-permute-start(f32[1,128,256]{2,1,0:T(8,128)S(1)} %bitcast.16), channel_id=1, source_target_pairs={{0,16},{4,20},{8,24},{12,28},{16,0},{20,4},{24,8},{28,12},{1,17},{... | collective-permute-start | bytes 393224 | tf_op jit(solution)/shard_map/ppermute | solution.py:374
  103.4 6.7 %collective-permute-done.5 = f32[1,128,256]{2,1,0:T(8,128)S(1)} collective-permute-done((f32[1,128,256]{2,1,0:T(8,128)S(1)}, f32[1,128,256]{2,1,0:T(8,128)S(1)}, u32[]{:S(2)}, u32[]{:S(2)}) %collective-permute-start.5) | collective-permute-done | bytes 131104 | tf_op jit(solution)/shard_map/ppermute | solution.py:374
  110.1 0.7 collective-permute-start.6
  110.9 5.6 %all-to-all-start.6 = ((f32[32,4,128]{2,1,0:T(4,128)}), f32[32,4,128]{2,1,0:T(4,128)S(1)}, u32[]{:S(2)}, u32[]{:S(2)}) async-start(f32[32,4,128]{2,1,0:T(4,128)} %bitcast.12), calls=%async_computation.6 | async-start | bytes 131072 | tf_op jit(solution)/shard_map/all_to_all | solution.py:392
  116.4 2.1 %shard_map.53 = f32[8,4,640]{2,1,0:T(4,128)S(1)} custom-call(bf16[8,2,4,32,512]{4,3,2,1,0:T(8,128)(2,1)S(1)} %get-tuple-element.15.samples_ref, f32[256,128]{1,0:T(8,128)S(1)} %get-tuple-element.17.vectors_ref), custom_call_target="tpu_custom_call" | custom-call | tf_op jit(solution)/shard_map/pallas_call | solution.py:363
  118.5 0.0 copy-start.1
  118.6 0.0 copy-start.3
  118.6 5.3 %all-to-all-done.6 = f32[32,4,128]{2,1,0:T(4,128)S(1)} async-done(((f32[32,4,128]{2,1,0:T(4,128)}), f32[32,4,128]{2,1,0:T(4,128)S(1)}, u32[]{:S(2)}, u32[]{:S(2)}) %all-to-all-start.6) | async-done | bytes 65568 | tf_op jit(solution)/shard_map/all_to_all | solution.py:392
  123.8 0.8 broadcast_in_dim.11
  124.6 2.6 %all-to-all-start.1 = ((f32[32,4,640]{2,1,0:T(4,128)}), f32[32,4,640]{2,1,0:T(4,128)S(1)}, u32[]{:S(2)}, u32[]{:S(2)}) async-start(f32[32,4,640]{2,1,0:T(4,128)} %bitcast.4), calls=%async_computation.1 | async-start | bytes 655360 | tf_op jit(solution)/shard_map/all_to_all | solution.py:392
  127.2 0.0 collective-permute-done.6
  127.3 1.7 %collective-permute-start.7 = (f32[4,128,256]{2,1,0:T(8,128)S(1)}, f32[4,128,256]{2,1,0:T(8,128)S(1)}, u32[]{:S(2)}, u32[]{:S(2)}) collective-permute-start(f32[4,128,256]{2,1,0:T(8,128)S(1)} %pad_maximum_fusion.1.near_ref), channel_id=1, source_target_pairs={{0,4},{4,0},{8,12},{12,8},{16,20},{20,16},{24,28},{28,24},{1,5},{5... | collective-permute-start | bytes 1572872 | tf_op jit(solution)/shard_map/ppermute | solution.py:374
  129.0 10.2 %all-to-all-done.1 = f32[32,4,640]{2,1,0:T(4,128)S(1)} async-done(((f32[32,4,640]{2,1,0:T(4,128)}), f32[32,4,640]{2,1,0:T(4,128)S(1)}, u32[]{:S(2)}, u32[]{:S(2)}) %all-to-all-start.1) | async-done | bytes 327712 | tf_op jit(solution)/shard_map/all_to_all | solution.py:392
  139.2 0.6 broadcast_in_dim.28
  139.8 2.8 %all-to-all-start.7 = ((f32[32,4,128]{2,1,0:T(4,128)}), f32[32,4,128]{2,1,0:T(4,128)S(1)}, u32[]{:S(2)}, u32[]{:S(2)}) async-start(f32[32,4,128]{2,1,0:T(4,128)} %broadcast_in_dim.28), calls=%async_computation.7 | async-start | bytes 131072 | tf_op jit(solution)/shard_map/all_to_all | solution.py:392
  142.6 0.1 reshape.53.images_ref
  142.8 7.1 %all-to-all-done.7 = f32[32,4,128]{2,1,0:T(4,128)S(1)} async-done(((f32[32,4,128]{2,1,0:T(4,128)}), f32[32,4,128]{2,1,0:T(4,128)S(1)}, u32[]{:S(2)}, u32[]{:S(2)}) %all-to-all-start.7) | async-done | bytes 65568 | tf_op jit(solution)/shard_map/all_to_all | solution.py:392
  149.8 0.0 collective-permute-done.7.far_ref
  149.8 0.0 copy-done.1
  149.8 17.3 %shard_map.57 = (f32[32,512]{1,0:T(8,128)}, f32[256,128]{1,0:T(8,128)}) custom-call(f32[128,640]{1,0:T(8,128)S(1)} %reshape.53.images_ref, f32[128,256]{1,0:T(8,128)S(1)} %get-tuple-element.20.turned_ref, f32[4,128,256]{2,1,0:T(8,128)S(1)} %pad_maximum_fusion.1.near_ref, f32[4,128,256]{2,1,0:T(8,128)S(1)} %collective-permute-done.7.far_ref, ...), custom_call_target="tpu_custom_call" | custom-call | tf_op jit(solution)/shard_map/pallas_call | solution.py:363
  (15 shorter events, 0.3 us)
Async XLA Ops:
  0.6 0.8 copy-start
  1.5 0.8 copy-start.2
  2.3 0.9 copy-start.4
  3.5 7.8 %collective-permute-start = (f32[1,32,512]{2,1,0:T(8,128)S(1)}, f32[1,32,512]{2,1,0:T(8,128)S(1)}, u32[]{:S(2)}, u32[]{:S(2)}) collective-permute-start(f32[1,32,512]{2,1,0:T(8,128)S(1)} %bitcast.19), channel_id=1, source_target_pairs={{0,16},{1,17},{2,18},{3,19},{4,20},{5,21},{6,22},{7,23},{8,24},{9,... | collective-permute-start | bytes 196616 | tf_op jit(solution)/shard_map/ppermute | solution.py:374
  11.2 5.0 %collective-permute-start.1 = (f32[2,32,512]{2,1,0:T(8,128)S(1)}, f32[2,32,512]{2,1,0:T(8,128)S(1)}, u32[]{:S(2)}, u32[]{:S(2)}) collective-permute-start(f32[2,32,512]{2,1,0:T(8,128)S(1)} %pad_maximum_fusion.4), channel_id=1, source_target_pairs={{0,8},{1,9},{2,10},{3,11},{4,12},{5,13},{6,14},{7,15},{8,0},{9,1},... | collective-permute-start | bytes 393224 | tf_op jit(solution)/shard_map/ppermute | solution.py:374
  16.3 6.4 %collective-permute-start.2 = (f32[4,32,512]{2,1,0:T(8,128)S(1)}, f32[4,32,512]{2,1,0:T(8,128)S(1)}, u32[]{:S(2)}, u32[]{:S(2)}) collective-permute-start(f32[4,32,512]{2,1,0:T(8,128)S(1)} %pad_maximum_fusion.2), channel_id=1, source_target_pairs={{0,4},{1,5},{2,6},{3,7},{4,0},{5,1},{6,2},{7,3},{8,12},{9,13},{10,... | collective-permute-start | bytes 786440 | tf_op jit(solution)/shard_map/ppermute | solution.py:374
  22.8 9.9 %collective-permute-start.3 = (f32[8,32,512]{2,1,0:T(8,128)S(1)}, f32[8,32,512]{2,1,0:T(8,128)S(1)}, u32[]{:S(2)}, u32[]{:S(2)}) collective-permute-start(f32[8,32,512]{2,1,0:T(8,128)S(1)} %pad_maximum_fusion), channel_id=1, source_target_pairs={{0,2},{1,3},{2,0},{3,1},{4,6},{5,7},{6,4},{7,5},{8,10},{9,11},{10,... | collective-permute-start | bytes 1572872 | tf_op jit(solution)/shard_map/ppermute | solution.py:374
  32.7 16.3 %collective-permute-start.4 = (f32[16,32,512]{2,1,0:T(8,128)S(1)}, f32[16,32,512]{2,1,0:T(8,128)S(1)}, u32[]{:S(2)}, u32[]{:S(2)}) collective-permute-start(f32[16,32,512]{2,1,0:T(8,128)S(1)} %constant_dynamic-update-slice_fusion.pieces_ref), channel_id=1, source_target_pairs={{0,1},{1,0},{2,3},{3,2},{4,5},{5,4},{6,7},{7,6},{8,9},{9,8},{10,11... | collective-permute-start | bytes 3145736 | tf_op jit(solution)/shard_map/ppermute | solution.py:374
  74.3 10.0 %all-to-all-start.5 = ((f32[32,4,128]{2,1,0:T(4,128)}), f32[32,4,128]{2,1,0:T(4,128)S(1)}, u32[]{:S(2)}, u32[]{:S(2)}) async-start(f32[32,4,128]{2,1,0:T(4,128)} %broadcast_in_dim.12), calls=%async_computation.5 | async-start | bytes 131072 | tf_op jit(solution)/shard_map/all_to_all | solution.py:392
  84.3 15.2 %all-to-all-start.2 = ((f32[32,8,128]{2,1,0:T(8,128)}), f32[32,8,128]{2,1,0:T(8,128)S(1)}, u32[]{:S(2)}, u32[]{:S(2)}) async-start(f32[32,8,128]{2,1,0:T(8,128)} %bitcast.5), calls=%async_computation.2 | async-start | bytes 262144 | tf_op jit(solution)/shard_map/all_to_all | solution.py:392
  100.9 9.2 %collective-permute-start.5 = (f32[1,128,256]{2,1,0:T(8,128)S(1)}, f32[1,128,256]{2,1,0:T(8,128)S(1)}, u32[]{:S(2)}, u32[]{:S(2)}) collective-permute-start(f32[1,128,256]{2,1,0:T(8,128)S(1)} %bitcast.16), channel_id=1, source_target_pairs={{0,16},{4,20},{8,24},{12,28},{16,0},{20,4},{24,8},{28,12},{1,17},{... | collective-permute-start | bytes 393224 | tf_op jit(solution)/shard_map/ppermute | solution.py:374
  110.1 17.1 %collective-permute-start.6 = (f32[2,128,256]{2,1,0:T(8,128)S(1)}, f32[2,128,256]{2,1,0:T(8,128)S(1)}, u32[]{:S(2)}, u32[]{:S(2)}) collective-permute-start(f32[2,128,256]{2,1,0:T(8,128)S(1)} %pad_maximum_fusion.3), channel_id=1, source_target_pairs={{0,8},{4,12},{8,0},{12,4},{16,24},{20,28},{24,16},{28,20},{1,9},{5... | collective-permute-start | bytes 786440 | tf_op jit(solution)/shard_map/ppermute | solution.py:374
  110.9 13.0 %all-to-all-start.6 = ((f32[32,4,128]{2,1,0:T(4,128)}), f32[32,4,128]{2,1,0:T(4,128)S(1)}, u32[]{:S(2)}, u32[]{:S(2)}) async-start(f32[32,4,128]{2,1,0:T(4,128)} %bitcast.12), calls=%async_computation.6 | async-start | bytes 131072 | tf_op jit(solution)/shard_map/all_to_all | solution.py:392
  118.5 31.3 %copy-start.1 = (f32[32,512]{1,0:T(8,128)S(1)}, f32[32,512]{1,0:T(8,128)}, u32[]{:S(2)}) copy-start(f32[32,512]{1,0:T(8,128)} %kspace_ref.3) | copy-start | bytes 196612
  118.6 31.3 %copy-start.3 = (s32[32,512]{1,0:T(8,128)S(1)}, s32[32,512]{1,0:T(8,128)}, u32[]{:S(2)}) copy-start(s32[32,512]{1,0:T(8,128)} %mask_ref.3) | copy-start | bytes 196612
  124.6 14.6 %all-to-all-start.1 = ((f32[32,4,640]{2,1,0:T(4,128)}), f32[32,4,640]{2,1,0:T(4,128)S(1)}, u32[]{:S(2)}, u32[]{:S(2)}) async-start(f32[32,4,640]{2,1,0:T(4,128)} %bitcast.4), calls=%async_computation.1 | async-start | bytes 655360 | tf_op jit(solution)/shard_map/all_to_all | solution.py:392
  127.3 22.6 %collective-permute-start.7 = (f32[4,128,256]{2,1,0:T(8,128)S(1)}, f32[4,128,256]{2,1,0:T(8,128)S(1)}, u32[]{:S(2)}, u32[]{:S(2)}) collective-permute-start(f32[4,128,256]{2,1,0:T(8,128)S(1)} %pad_maximum_fusion.1.near_ref), channel_id=1, source_target_pairs={{0,4},{4,0},{8,12},{12,8},{16,20},{20,16},{24,28},{28,24},{1,5},{5... | collective-permute-start | bytes 1572872 | tf_op jit(solution)/shard_map/ppermute | solution.py:374
  139.8 10.0 %all-to-all-start.7 = ((f32[32,4,128]{2,1,0:T(4,128)}), f32[32,4,128]{2,1,0:T(4,128)S(1)}, u32[]{:S(2)}, u32[]{:S(2)}) async-start(f32[32,4,128]{2,1,0:T(4,128)} %broadcast_in_dim.28), calls=%async_computation.7 | async-start | bytes 131072 | tf_op jit(solution)/shard_map/all_to_all | solution.py:392

commit v2 on v1

--- a/solution.py
+++ b/solution.py
@@ -112,8 +112,32 @@
     return dot(a_high, b_high, dims) + (dot(a_high, b_low, dims) + dot(a_low, b_high, dims))
 
 
-def prepare_kernel(cols, chg, per_tile, kspace_ref, mask_ref, basis_ref, sampled_ref, send_ref):
+def prepare_kernel(
+    cols,
+    chg,
+    per_tile,
+    kspace_hbm,
+    mask_hbm,
+    basis_hbm,
+    sampled_ref,
+    send_ref,
+    kspace_ref,
+    mask_ref,
+    basis_ref,
+    sems,
+):
+    fetches = [
+        pltpu.make_async_copy(source, target, sems.at[i])
+        for i, (source, target) in enumerate(
+            [(kspace_hbm, kspace_ref), (mask_hbm, mask_ref), (basis_hbm, basis_ref)]
+        )
+    ]
+    for fetch in fetches:
+        fetch.start()
+    fetches[0].wait()
+    fetches[1].wait()
     sampled_ref[...] = kspace_ref[...] * mask_ref[...].astype(jnp.float32)
+    fetches[2].wait()
     turned = basis_ref[...].T
     devices = turned.shape[0] // cols
     for j in range(per_tile):
@@ -175,30 +199,46 @@
     )
 
 
-def store_by_rows(normal, send_ref):
-    tiles, groups, per_tile, lanes = send_ref.shape
+def store_by_rows(normal, send_ref, part):
+    tiles, groups, _, per_tile, lanes = send_ref.shape
     cols = normal.shape[0] // KER
     chg = normal.shape[1] // groups
     for g in range(groups):
         joined = jnp.concatenate(
             [normal[k * KER : (k + 1) * KER, g * chg : (g + 1) * chg] for k in range(cols)], axis=1
         )
-        send_ref[:, g] = joined.reshape(tiles, per_tile, lanes)
-
-
-def first_kernel(
-    masks, pieces_ref, late_ref, basis_ref, samples_ref, normal_ref, send_ref, wide_ref, moved_ref
+        send_ref[:, g, part] = joined.reshape(tiles, per_tile, lanes)
+
+
+def passes_kernel(
+    masks,
+    top_near_ref,
+    top_far_ref,
+    low_near_ref,
+    low_far_ref,
+    basis_ref,
+    samples_ref,
+    normal_ref,
+    send_ref,
+    wide_ref,
+    moved_ref,
 ):
     tiles, _, groups, chg, tile = samples_ref.shape
     me = lax.axis_index("rows") * groups + lax.axis_index("coil")
-    half = pieces_ref.shape[0]
-    for slot, mask in enumerate(masks):
-        value = pieces_ref[slot] if slot < half else late_ref[slot - half]
-        high, low = split(value)
-        source = lax.bitwise_xor(me, mask)
-        t, g = source // groups, source % groups
-        samples_ref[t, 0, g] = high
-        samples_ref[t, 1, g] = low
+    start = 0
+    for near_ref, far_ref, order in (
+        (top_near_ref, top_far_ref, masks[0]),
+        (low_near_ref, low_far_ref, masks[1]),
+    ):
+        half, count = near_ref.shape[:2]
+        for slot, mask in enumerate(order):
+            value = near_ref[slot] if slot < half else far_ref[slot - half]
+            high, low = split(value)
+            source = lax.bitwise_xor(me, mask)
+            t, g = source // groups, source % groups
+            samples_ref[t, 0, g, start : start + count] = high
+            samples_ref[t, 1, g, start : start + count] = low
+        start += count
     cols = basis_ref.shape[-1] // chg
     rows = []
     for k in range(cols):
@@ -218,19 +258,13 @@
         part = normal[k * KER : (k + 1) * KER]
         scaled.append(part * (1.0 / jnp.max(jnp.abs(part))))
     normal = jnp.concatenate(scaled, axis=0)
+    store_by_rows(normal, send_ref, 0)
+    normal = normal_of(images_of(normal, samples_ref, wide_ref), samples_ref, moved_ref)
     normal_ref[...] = normal
-    store_by_rows(normal, send_ref)
-
-
-def second_kernel(samples_ref, vectors_ref, normal_ref, send_ref, wide_ref, moved_ref):
-    normal = normal_of(
-        images_of(vectors_ref[...], samples_ref, wide_ref), samples_ref, moved_ref
-    )
-    normal_ref[...] = normal
-    store_by_rows(normal, send_ref)
-
-
-def third_kernel(samples_ref, vectors_ref, send_ref, wide_ref):
+    store_by_rows(normal, send_ref, 1)
+
+
+def images_kernel(samples_ref, vectors_ref, send_ref, wide_ref):
     tiles, cols, reach = send_ref.shape
     tile = samples_ref.shape[-1]
     images = jnp.concatenate(images_of(vectors_ref[...], samples_ref, wide_ref), axis=0)
@@ -245,11 +279,14 @@
         send_ref[t] = part
 
 
-def gather_turned(received_ref, cols, per_tile):
+def gather_turned(received_ref, cols, per_tile, part):
     count, lanes = received_ref.shape
-    devices = count // per_tile
+    devices = count // (2 * per_tile)
     chg = lanes // cols
-    loaded = [received_ref[pl.ds(j, devices, stride=per_tile), :] for j in range(per_tile)]
+    loaded = [
+        received_ref[pl.ds(part * per_tile + j, devices, stride=2 * per_tile), :]
+        for j in range(per_tile)
+    ]
     return jnp.concatenate(
         [
             jnp.concatenate(
@@ -267,55 +304,93 @@
     )
 
 
-def gram_kernel(cols, per_tile, received_ref, gram_ref):
-    turned = gather_turned(received_ref, cols, per_tile)
+def gram_kernel(cols, per_tile, received_ref, gram_ref, turned_ref):
+    turned = gather_turned(received_ref, cols, per_tile, 0)
     gram_ref[...] = exact(turned, turned, ((1,), (1,)))
-
-
-def second_gram_kernel(cols, per_tile, received_ref, inverse_ref, turned_ref, gram_ref):
-    turned = gather_turned(received_ref, cols, per_tile)
-    turned = exact(inverse_ref[...], turned)
-    turned_ref[...] = turned
-    gram_ref[...] = exact(turned, turned, ((1,), (1,)))
+    turned_ref[...] = gather_turned(received_ref, cols, per_tile, 1)
 
 
 def inverse_factor(gram):
     size = gram.shape[0]
+    shape = (SUB, size)
     at_row = lax.broadcasted_iota(jnp.int32, (size, size), 0)
     at_col = lax.broadcasted_iota(jnp.int32, (size, size), 1)
     unit = (at_row == at_col).astype(jnp.float32)
     left = [gram[b : b + SUB] for b in range(0, size, SUB)]
     right = [unit[b : b + SUB] for b in range(0, size, SUB)]
-    sub = lax.broadcasted_iota(jnp.int32, (SUB, size), 0)
-    for j in range(size):
-        b, s = j // SUB, j % SUB
-        pivot = left[b][s : s + 1, j : j + 1]
-        root = lax.rsqrt(pivot)
-        root = root * (1.5 - 0.5 * pivot * root * root)
-        upper = left[b][s : s + 1] * root
-        lower = right[b][s : s + 1] * root
-        for c in range(b, len(left)):
-            factor = left[c][:, j : j + 1] * root
-            if c == b:
-                factor = jnp.where(sub > s, factor, 0.0)
-            new_left = left[c] - factor * upper
-            new_right = right[c] - factor * lower
-            if c == b:
-                new_left = jnp.where(sub == s, upper, new_left)
-                new_right = jnp.where(sub == s, lower, new_right)
-            left[c], right[c] = new_left, new_right
-    return jnp.concatenate(right, axis=0)
-
-
-def factor_kernel(gram_ref, inverse_ref):
-    inverse_ref[...] = inverse_factor(gram_ref[...])
+    sub = lax.broadcasted_iota(jnp.int32, shape, 0)
+    done = []
+    for b in range(len(left)):
+        spread = {
+            c: [
+                jnp.broadcast_to(left[c][:, b * SUB + k : b * SUB + k + 1], shape)
+                for k in range(SUB)
+            ]
+            for c in range(b, len(left))
+        }
+        entry = {
+            (i, k): jnp.broadcast_to(spread[b][k][i : i + 1], shape)
+            for k in range(SUB)
+            for i in range(k, SUB)
+        }
+        inverse = {}
+        for k in range(SUB):
+            root = lax.rsqrt(entry[k, k])
+            root = root * (1.5 - (0.5 * entry[k, k]) * (root * root))
+            inverse[k, k] = root
+            for i in range(k + 1, SUB):
+                entry[i, k] = entry[i, k] * root
+            for i in range(k + 1, SUB):
+                for m in range(k + 1, i + 1):
+                    entry[i, m] = entry[i, m] - entry[i, k] * entry[m, k]
+        for i in range(1, SUB):
+            for k in range(i):
+                total = entry[i, k] * inverse[k, k]
+                for m in range(k + 1, i):
+                    total = total + entry[i, m] * inverse[m, k]
+                inverse[i, k] = -(total * inverse[i, i])
+
+        def solved(rows):
+            whole = [jnp.broadcast_to(rows[k : k + 1], shape) for k in range(SUB)]
+            first = []
+            for i in range(SUB):
+                total = inverse[i, 0] * whole[0]
+                for k in range(1, i + 1):
+                    total = total + inverse[i, k] * whole[k]
+                first.append(total)
+            second = []
+            for k in range(SUB):
+                total = inverse[k, k] * first[k]
+                for i in range(k + 1, SUB):
+                    total = total + inverse[i, k] * first[i]
+                second.append(total)
+            return first, second
+
+        lower, lower_again = solved(right[b])
+        row = lower[0]
+        for i in range(1, SUB):
+            row = jnp.where(sub == i, lower[i], row)
+        done.append(row)
+        if b + 1 < len(left):
+            _, upper_again = solved(left[b])
+            for c in range(b + 1, len(left)):
+                for k in range(SUB):
+                    left[c] = left[c] - spread[c][k] * upper_again[k]
+                    right[c] = right[c] - spread[c][k] * lower_again[k]
+    return jnp.concatenate(done, axis=0)
+
+
+def middle_kernel(gram_ref, turned_ref, inverse_ref, next_ref):
+    inverse = inverse_factor(gram_ref[...])
+    inverse_ref[...] = inverse
+    turned = exact(inverse, turned_ref[...])
+    next_ref[...] = exact(turned, turned, ((1,), (1,)))
 
 
 def last_kernel(
     cols,
     masks,
     images_ref,
-    turned_ref,
     near_ref,
     far_ref,
     first_ref,
@@ -333,7 +408,8 @@
     order = ((at_row // devices == at_col % cols) & (at_row % devices == at_col // cols)).astype(
         jnp.float32
     )
-    images = exact(inverse, exact(exact(first_ref[...], order), images_ref[...]))
+    inverse = exact(inverse, first_ref[...])
+    images = exact(exact(inverse, order), images_ref[...])
     images_high, images_low = split(images)
     stacked = jnp.concatenate([images_high, images_low], axis=0)
     chg, tile = kspace_ref.shape
@@ -359,13 +435,13 @@
     recovered_ref[...] = estimate + residual - jnp.clip(residual, -threshold, threshold)
 
 
-def call(kernel, outs, *args, scratch=()):
+def call(kernel, outs, *args, scratch=(), space=pltpu.VMEM):
     return pl.pallas_call(
         kernel,
         out_shape=[jax.ShapeDtypeStruct(shape, kind) for shape, kind in outs],
-        in_specs=[pl.BlockSpec(memory_space=pltpu.VMEM)] * len(args),
+        in_specs=[pl.BlockSpec(memory_space=space)] * len(args),
         out_specs=[pl.BlockSpec(memory_space=pltpu.VMEM)] * len(outs),
-        scratch_shapes=[pltpu.VMEM(shape, kind) for shape, kind in scratch],
+        scratch_shapes=list(scratch),
         compiler_params=pltpu.CompilerParams(vmem_limit_bytes=40 * 2**20),
     )(*args)
 
@@ -374,30 +450,57 @@
     return lax.ppermute(block, axes, [(i, i ^ mask) for i in range(devices)])
 
 
-def gather_by_halves(block, devices, axes):
-    masks = [0]
-    near = block[None]
-    far = None
+def joined(near, far):
+    return jnp.concatenate([near, far], axis=0)
+
+
+def with_masks(masks, mask):
+    return masks + [m ^ mask for m in masks]
+
+
+def after(value, *others):
+    return lax.optimization_barrier((value,) + others)[0]
+
+
+def gather_samples(sampled, tiles, groups, beside):
+    devices = tiles * groups
+    near, masks = sampled[None], [0]
     mask = devices // 2
-    while mask:
-        if far is not None:
-            near = jnp.concatenate([near, far], axis=0)
-        far = exchange(near, devices, mask, axes)
-        masks = masks + [m ^ mask for m in masks]
+    while mask > groups:
+        near = joined(near, exchange(near, devices, mask, AXES))
+        masks = with_masks(masks, mask)
         mask //= 2
-    return near, far, masks
-
-
-def to_all(pieces):
-    return lax.all_to_all(pieces, AXES, 0, 0, tiled=True)
-
-
-def total_of(gram, devices):
+    near = after(near, beside)
+    half = near.shape[1] // 2
+    parts = [near[:, :half], near[:, half:]]
+    orders = [masks, masks]
+    ways = [(groups, groups // 2), (groups // 2, groups)]
+    for step in range(2):
+        parts = [
+            joined(part, exchange(part, devices, way[step], AXES)) for part, way in zip(parts, ways)
+        ]
+        orders = [with_masks(order, way[step]) for order, way in zip(orders, ways)]
+    mask = groups // 4
+    while mask > 1:
+        parts = [joined(part, exchange(part, devices, mask, AXES)) for part in parts]
+        orders = [with_masks(order, mask) for order in orders]
+        mask //= 2
+    far = [exchange(part, devices, 1, AXES) for part in parts]
+    orders = [with_masks(order, 1) for order in orders]
+    return parts, far, orders
+
+
+def to_all(pieces, axes=AXES):
+    return lax.all_to_all(pieces, axes, 0, 0, tiled=True)
+
+
+def total_of(gram, tiles, groups):
     size = gram.shape[0]
-    parts = to_all(gram.reshape(devices, size // devices, size))
-    mine = jnp.sum(parts, axis=0)
-    spread = to_all(jnp.broadcast_to(mine[None], parts.shape))
-    return spread.reshape(size, size)
+    block = (size // groups, size)
+    mine = jnp.sum(to_all(gram.reshape((groups,) + block), "coil"), axis=0)
+    mine = jnp.sum(to_all(jnp.broadcast_to(mine[None], (tiles,) + block), "rows"), axis=0)
+    whole = to_all(jnp.broadcast_to(mine[None], (groups,) + block), "coil")
+    return whole.reshape(size, size)
 
 
 def column_shards(kspace, sample_mask, start_basis):
@@ -419,54 +522,62 @@
         kspace,
         sample_mask,
         start_basis.reshape(owned, rank),
+        scratch=[
+            pltpu.VMEM((chg, tile), f32),
+            pltpu.VMEM((chg, tile), sample_mask.dtype),
+            pltpu.VMEM((owned, rank), f32),
+            pltpu.SemaphoreType.DMA((3,)),
+        ],
+        space=pl.ANY,
     )
     basis_parts = to_all(basis_send.reshape(devices, per_tile, lanes))
-    near, far, masks = gather_by_halves(sampled, devices, AXES)
-    wide = ((rows, positions), f32)
-    moved = ((2 * rows, positions), bf16)
-    by_rows = ((tiles, groups, per_tile, lanes), f32)
+    near, far, masks = gather_samples(sampled, tiles, groups, basis_parts)
+    wide = pltpu.VMEM((rows, positions), f32)
+    moved = pltpu.VMEM((2 * rows, positions), bf16)
     samples, normal, send = call(
-        functools.partial(first_kernel, masks),
-        [((tiles, 2, groups, chg, tile), bf16), ((rows, channels), f32), by_rows],
-        near,
-        far,
+        functools.partial(passes_kernel, masks),
+        [
+            ((tiles, 2, groups, chg, tile), bf16),
+            ((rows, channels), f32),
+            ((tiles, groups, 2, per_tile, lanes), f32),
+        ],
+        near[0],
+        far[0],
+        near[1],
+        far[1],
         basis_parts.reshape(tiles, groups, per_tile, lanes),
         scratch=[wide, moved],
     )
-    received = to_all(send.reshape(devices, per_tile, lanes))
-    (gram,) = call(
+    received = to_all(send.reshape(devices, 2 * per_tile, lanes))
+    reach = tile + LANES
+    (images,) = call(images_kernel, [((tiles, cols, reach), f32)], samples, normal, scratch=[wide])
+    images = jnp.broadcast_to(images[:, None], (tiles, groups, cols, reach))
+    gram, turned = call(
         functools.partial(gram_kernel, cols, per_tile),
-        [((rank, rank), f32)],
-        received.reshape(devices * per_tile, lanes),
-    )
-    gram = total_of(gram, devices)
-    (first,) = call(factor_kernel, [((rank, rank), f32)], gram)
-
-    normal, send = call(
-        second_kernel, [((rows, channels), f32), by_rows], samples, normal, scratch=[wide, moved]
-    )
-    received = to_all(send.reshape(devices, per_tile, lanes))
-    reach = tile + LANES
-    (images,) = call(third_kernel, [((tiles, cols, reach), f32)], samples, normal, scratch=[wide])
-    images = jnp.broadcast_to(images[:, None], (tiles, groups, cols, reach))
+        [((rank, rank), f32), ((rank, owned), f32)],
+        received.reshape(devices * 2 * per_tile, lanes),
+    )
+    gram = total_of(gram, tiles, groups)
     images = to_all(images.reshape(devices, cols, reach)).reshape(rank, reach)
-
-    turned, gram = call(
-        functools.partial(second_gram_kernel, cols, per_tile),
-        [((rank, owned), f32), ((rank, rank), f32)],
-        received.reshape(devices * per_tile, lanes),
-        first,
-    )
-    gram = total_of(gram, devices)
-    near, far, masks = gather_by_halves(turned, tiles, "rows")
+    near, masks = turned[None], [0]
+    mask = tiles // 2
+    while mask > 1:
+        near = joined(near, exchange(near, tiles, mask, "rows"))
+        masks = with_masks(masks, mask)
+        mask //= 2
+    far = exchange(near, tiles, 1, "rows")
+    masks = with_masks(masks, 1)
+    inverse, gram = call(
+        middle_kernel, [((rank, rank), f32), ((rank, rank), f32)], gram, turned
+    )
+    gram = total_of(gram, tiles, groups)
     recovered, basis = call(
         functools.partial(last_kernel, cols, masks),
         [((chg, tile), f32), ((owned, rank), f32)],
         images,
-        turned,
         near,
         far,
-        first,
+        inverse,
         gram,
         kspace,
         sample_mask,
@@ -482,12 +593,13 @@
     return (
         devices & (devices - 1) == 0
         and tiles > 1
+        and groups > 2
         and rank % devices == 0
         and rank % LANES == 0
         and tile % LANES == 0
         and owned % (SUB * chg) == 0
         and chg * (rank // devices) == LANES
-        and chg % (2 * SUB) == 0
+        and chg % (4 * SUB) == 0
         and (chg * groups) % LANES == 0
         and KER <= LANES
     )

time: 168 us -> 151 us (0.90)
  Pallas kernels: 43 us -> 33.6 us
  waiting for transfers between devices: 52.6 us -> 43.5 us
  starting transfers between devices: 30.3 us -> 34.1 us
  blocking collectives: 35.4 us -> 32.3 us
    ppermute x8 -> x11, waiting for transfers between devices: 27.5 us -> 17.8 us  [exchange(): return lax.ppermute(block, axes, [(i, i ^ mask) for i in range(devices)])]
    pallas_call x8 -> x6, Pallas kernels: 43 us -> 33.6 us  [call(): pl.pallas_call(kernel, out_shape=[jax.ShapeDtypeStruct(shape, kind) for s...]
    ppermute x8 -> x11, starting transfers between devices: 13.3 us -> 17.4 us  [exchange(): return lax.ppermute(block, axes, [(i, i ^ mask) for i in range(devices)])]
    all_to_all x3 -> x4, blocking collectives: 35.4 us -> 32.3 us  [to_all(): return lax.all_to_all(pieces, axes, 0, 0, tiled=True)]
  transfers between devices with their start and end apart: 13 -> 16, of which waited for: 9 -> 10; matrix products, arithmetic and copies ran while one was open for 1% -> 2% of each run, Pallas kernels for 11% -> 6%
where the time goes in v2:
time: 151 us; the launch traced here: 150 us
  waiting for transfers between devices  43.5 us (29%)
  starting transfers between devices  34.1 us (23%)
  Pallas kernels  33.6 us (22%)
  blocking collectives  32.3 us (21%)
  local copies, waits for them, and re-layouts  5.47 us (4%)
    pallas_call x6, Pallas kernels, call(): pl.pallas_call(kernel, out_shape=[jax.ShapeDtypeStruct(shape, kind) for s...  33.6 us
    all_to_all x4, blocking collectives, to_all(): return lax.all_to_all(pieces, axes, 0, 0, tiled=True)  32.3 us
    all_to_all x5, waiting for transfers between devices, to_all(): return lax.all_to_all(pieces, axes, 0, 0, tiled=True)  25.7 us
    ppermute x11, waiting for transfers between devices, exchange(): return lax.ppermute(block, axes, [(i, i ^ mask) for i in range(devices)])  17.8 us
    ppermute x11, starting transfers between devices, exchange(): return lax.ppermute(block, axes, [(i, i ^ mask) for i in range(devices)])  17.4 us
    all_to_all x5, starting transfers between devices, to_all(): return lax.all_to_all(pieces, axes, 0, 0, tiled=True)  16.7 us
  transfers between devices with their start and end apart: 16, of which 10 were waited for; matrix products, arithmetic and copies ran while one was open for 2% of the time, Pallas kernels for 6%

profile of v2, /device:TPU:0, one launch (start us, length us, event | category | flops | bytes accessed | tf_op | source)
XLA Modules:
  0.0 150.1 jit_solution(7023591314427170626)
XLA Ops:
  0.6 0.0 copy-start
  0.6 0.8 copy-done
  1.5 0.8 copy-done.2
  2.3 0.9 copy-done.4
  3.2 1.2 shard_map.50
  4.5 4.1 %collective-permute-start = (f32[1,32,512]{2,1,0:T(8,128)S(1)}, f32[1,32,512]{2,1,0:T(8,128)S(1)}, u32[]{:S(2)}, u32[]{:S(2)}) collective-permute-start(f32[1,32,512]{2,1,0:T(8,128)S(1)} %bitcast.21), channel_id=1, source_target_pairs={{0,16},{1,17},{2,18},{3,19},{4,20},{5,21},{6,22},{7,23},{8,24},{9,... | collective-permute-start | bytes 196616 | tf_op jit(solution)/shard_map/ppermute | solution.py:450
  8.6 3.8 %all-to-all-start = ((f32[32,8,128]{2,1,0:T(8,128)}), f32[32,8,128]{2,1,0:T(8,128)S(1)}, u32[]{:S(2)}, u32[]{:S(2)}) async-start(f32[32,8,128]{2,1,0:T(8,128)} %bitcast.2), calls=%async_computation | async-start | bytes 262144 | tf_op jit(solution)/shard_map/all_to_all | solution.py:494
  12.4 1.8 %collective-permute-start.1 = (f32[2,32,512]{2,1,0:T(8,128)S(1)}, f32[2,32,512]{2,1,0:T(8,128)S(1)}, u32[]{:S(2)}, u32[]{:S(2)}) collective-permute-start(f32[2,32,512]{2,1,0:T(8,128)S(1)} %pad_maximum_fusion.7), channel_id=1, source_target_pairs={{0,8},{1,9},{2,10},{3,11},{4,12},{5,13},{6,14},{7,15},{8,0},{9,1},... | collective-permute-start | bytes 393224 | tf_op jit(solution)/shard_map/ppermute | solution.py:450
  14.3 5.9 %collective-permute-done.1 = f32[2,32,512]{2,1,0:T(8,128)S(1)} collective-permute-done((f32[2,32,512]{2,1,0:T(8,128)S(1)}, f32[2,32,512]{2,1,0:T(8,128)S(1)}, u32[]{:S(2)}, u32[]{:S(2)}) %collective-permute-start.1) | collective-permute-done | bytes 131104 | tf_op jit(solution)/shard_map/ppermute | solution.py:450
  20.2 0.5 all-to-all-done
  20.7 1.1 collective-permute-start.2
  21.8 1.5 collective-permute-start.5
  23.2 3.5 %collective-permute-done.2 = f32[4,16,512]{2,1,0:T(8,128)S(1)} collective-permute-done((f32[4,16,512]{2,1,0:T(8,128)S(1)}, f32[4,16,512]{2,1,0:T(8,128)S(1)}, u32[]{:S(2)}, u32[]{:S(2)}) %collective-permute-start.2) | collective-permute-done | bytes 131104 | tf_op jit(solution)/shard_map/ppermute | solution.py:450
  26.8 0.2 collective-permute-start.3
  27.0 1.6 %collective-permute-start.6 = (f32[8,16,512]{2,1,0:T(8,128)S(1)}, f32[8,16,512]{2,1,0:T(8,128)S(1)}, u32[]{:S(2)}, u32[]{:S(2)}) collective-permute-start(f32[8,16,512]{2,1,0:T(8,128)S(1)} %pad_maximum_fusion.5), channel_id=1, source_target_pairs={{0,4},{1,5},{2,6},{3,7},{4,0},{5,1},{6,2},{7,3},{8,12},{9,13},{10,... | collective-permute-start | bytes 786440 | tf_op jit(solution)/shard_map/ppermute | solution.py:450
  28.6 6.3 %collective-permute-done.3 = f32[8,16,512]{2,1,0:T(8,128)S(1)} collective-permute-done((f32[8,16,512]{2,1,0:T(8,128)S(1)}, f32[8,16,512]{2,1,0:T(8,128)S(1)}, u32[]{:S(2)}, u32[]{:S(2)}) %collective-permute-start.3) | collective-permute-done | bytes 262176 | tf_op jit(solution)/shard_map/ppermute | solution.py:450
  35.0 0.1 collective-permute-start.4
  35.1 0.6 collective-permute-start.7
  35.6 1.3 collective-permute-done.4.top_far_ref
  36.9 0.7 collective-permute-done.7.low_far_ref
  37.7 11.7 %shard_map.51 = (bf16[8,2,4,32,512]{4,3,2,1,0:T(8,128)(2,1)S(1)}, f32[256,128]{1,0:T(8,128)S(1)}, f32[8,4,2,8,128]{4,3,2,1,0:T(8,128)S(1)}) custom-call(f32[16,16,512]{2,1,0:T(8,128)S(1)} %pad_maximum_fusion.top_near_ref, f32[16,16,512]{2,1,0:T(8,128)S(1)} %collective-permute-done.4.top_far_ref, f32[16,16,512]{2,1,0:T(8,128)S(1)} %pad_maximum_fusion.1.low_near_ref, ...), custom_call_target="tpu_custom_call" | custom-call | tf_op jit(solution)/shard_map/pallas_call | solution.py:439
  49.4 12.8 %all_to_all.45 = f32[32,16,128]{2,1,0:T(8,128)S(1)} all-to-all(f32[32,16,128]{2,1,0:T(8,128)S(1)} %bitcast.20), channel_id=1, replica_groups=mesh['rows'=8,'coil'=4] {'rows','coil'}, dimensions={0} | all-to-all | bytes 524288 | tf_op jit(solution)/shard_map/all_to_all | solution.py:494
  62.3 0.4 shard_map.53
  62.7 6.5 %all_to_all.46 = f32[4,32,128]{2,1,0:T(8,128)S(1)} all-to-all(f32[4,32,128]{2,1,0:T(8,128)S(1)} %bitcast.25), channel_id=1, replica_groups=mesh['rows'=8,'coil'=4] {'coil'}, dimensions={0} | all-to-all | bytes 131072 | tf_op jit(solution)/shard_map/all_to_all | solution.py:494
  69.2 0.7 broadcast_in_dim.17
  69.9 3.4 %all-to-all-start.4 = ((f32[8,32,128]{2,1,0:T(8,128)}), f32[8,32,128]{2,1,0:T(8,128)S(1)}, u32[]{:S(2)}, u32[]{:S(2)}) async-start(f32[8,32,128]{2,1,0:T(8,128)} %broadcast_in_dim.17), calls=%async_computation.4 | async-start | bytes 262144 | tf_op jit(solution)/shard_map/all_to_all | solution.py:494
  73.2 2.8 %collective-permute-start.8 = (f32[1,128,256]{2,1,0:T(8,128)S(1)}, f32[1,128,256]{2,1,0:T(8,128)S(1)}, u32[]{:S(2)}, u32[]{:S(2)}) collective-permute-start(f32[1,128,256]{2,1,0:T(8,128)S(1)} %bitcast.13), channel_id=1, source_target_pairs={{0,16},{4,20},{8,24},{12,28},{16,0},{20,4},{24,8},{28,12},{1,17},{... | collective-permute-start | bytes 393224 | tf_op jit(solution)/shard_map/ppermute | solution.py:450
  76.1 7.3 %all-to-all-done.4 = f32[8,32,128]{2,1,0:T(8,128)S(1)} async-done(((f32[8,32,128]{2,1,0:T(8,128)}), f32[8,32,128]{2,1,0:T(8,128)S(1)}, u32[]{:S(2)}, u32[]{:S(2)}) %all-to-all-start.4) | async-done | bytes 131104 | tf_op jit(solution)/shard_map/all_to_all | solution.py:494
  83.4 6.5 %all_to_all.47 = f32[4,32,128]{2,1,0:T(8,128)S(1)} all-to-all(f32[4,32,128]{2,1,0:T(8,128)S(1)} %broadcast_in_dim.18), channel_id=1, replica_groups=mesh['rows'=8,'coil'=4] {'coil'}, dimensions={0} | all-to-all | bytes 131072 | tf_op jit(solution)/shard_map/all_to_all | solution.py:494
  89.9 6.3 %shard_map.54 = (f32[128,128]{1,0:T(8,128)S(1)}, f32[128,128]{1,0:T(8,128)S(1)}) custom-call(f32[128,128]{1,0:T(8,128)S(1)} %bitcast.19, f32[128,256]{1,0:T(8,128)S(1)} %get-tuple-element.20.turned_ref), custom_call_target="tpu_custom_call" | custom-call | tf_op jit(solution)/shard_map/pallas_call | solution.py:439
  96.2 6.5 %all_to_all.48 = f32[4,32,128]{2,1,0:T(8,128)S(1)} all-to-all(f32[4,32,128]{2,1,0:T(8,128)S(1)} %bitcast.26), channel_id=1, replica_groups=mesh['rows'=8,'coil'=4] {'coil'}, dimensions={0} | all-to-all | bytes 131072 | tf_op jit(solution)/shard_map/all_to_all | solution.py:494
  102.7 0.7 broadcast_in_dim.19
  103.4 3.4 %all-to-all-start.7 = ((f32[8,32,128]{2,1,0:T(8,128)}), f32[8,32,128]{2,1,0:T(8,128)S(1)}, u32[]{:S(2)}, u32[]{:S(2)}) async-start(f32[8,32,128]{2,1,0:T(8,128)} %broadcast_in_dim.19), calls=%async_computation.7 | async-start | bytes 262144 | tf_op jit(solution)/shard_map/all_to_all | solution.py:494
  106.7 0.0 collective-permute-done.8
  106.8 2.0 %collective-permute-start.9 = (f32[2,128,256]{2,1,0:T(8,128)S(1)}, f32[2,128,256]{2,1,0:T(8,128)S(1)}, u32[]{:S(2)}, u32[]{:S(2)}) collective-permute-start(f32[2,128,256]{2,1,0:T(8,128)S(1)} %pad_maximum_fusion.6), channel_id=1, source_target_pairs={{0,8},{4,12},{8,0},{12,4},{16,24},{20,28},{24,16},{28,20},{1,9},{5... | collective-permute-start | bytes 786440 | tf_op jit(solution)/shard_map/ppermute | solution.py:450
  108.8 2.1 %shard_map.52 = f32[8,4,640]{2,1,0:T(4,128)S(1)} custom-call(bf16[8,2,4,32,512]{4,3,2,1,0:T(8,128)(2,1)S(1)} %get-tuple-element.17.samples_ref, f32[256,128]{1,0:T(8,128)S(1)} %get-tuple-element.18.vectors_ref), custom_call_target="tpu_custom_call" | custom-call | tf_op jit(solution)/shard_map/pallas_call | solution.py:439
  110.9 0.0 copy-start.1
  110.9 0.0 copy-start.3
  110.9 4.0 %all-to-all-done.7 = f32[8,32,128]{2,1,0:T(8,128)S(1)} async-done(((f32[8,32,128]{2,1,0:T(8,128)}), f32[8,32,128]{2,1,0:T(8,128)S(1)}, u32[]{:S(2)}, u32[]{:S(2)}) %all-to-all-start.7) | async-done | bytes 131104 | tf_op jit(solution)/shard_map/all_to_all | solution.py:494
  114.9 0.8 broadcast_in_dim.15
  115.7 2.6 %all-to-all-start.1 = ((f32[32,4,640]{2,1,0:T(4,128)}), f32[32,4,640]{2,1,0:T(4,128)S(1)}, u32[]{:S(2)}, u32[]{:S(2)}) async-start(f32[32,4,640]{2,1,0:T(4,128)} %bitcast.4), calls=%async_computation.1 | async-start | bytes 655360 | tf_op jit(solution)/shard_map/all_to_all | solution.py:494
  118.4 1.7 %collective-permute-start.10 = (f32[4,128,256]{2,1,0:T(8,128)S(1)}, f32[4,128,256]{2,1,0:T(8,128)S(1)}, u32[]{:S(2)}, u32[]{:S(2)}) collective-permute-start(f32[4,128,256]{2,1,0:T(8,128)S(1)} %pad_maximum_fusion.2.near_ref), channel_id=1, source_target_pairs={{0,4},{4,0},{8,12},{12,8},{16,20},{20,16},{24,28},{28,24},{1,5},{5... | collective-permute-start | bytes 1572872 | tf_op jit(solution)/shard_map/ppermute | solution.py:450
  120.1 10.2 %all-to-all-done.1 = f32[32,4,640]{2,1,0:T(4,128)S(1)} async-done(((f32[32,4,640]{2,1,0:T(4,128)}), f32[32,4,640]{2,1,0:T(4,128)S(1)}, u32[]{:S(2)}, u32[]{:S(2)}) %all-to-all-start.1) | async-done | bytes 327712 | tf_op jit(solution)/shard_map/all_to_all | solution.py:494
  130.3 0.6 broadcast_in_dim.20
  130.9 3.5 %all-to-all-start.8 = ((f32[4,32,128]{2,1,0:T(8,128)}), f32[4,32,128]{2,1,0:T(8,128)S(1)}, u32[]{:S(2)}, u32[]{:S(2)}) async-start(f32[4,32,128]{2,1,0:T(8,128)} %broadcast_in_dim.20), calls=%async_computation.8 | async-start | bytes 131072 | tf_op jit(solution)/shard_map/all_to_all | solution.py:494
  134.5 0.1 reshape.49.images_ref
  134.6 3.7 %all-to-all-done.8 = f32[4,32,128]{2,1,0:T(8,128)S(1)} async-done(((f32[4,32,128]{2,1,0:T(8,128)}), f32[4,32,128]{2,1,0:T(8,128)S(1)}, u32[]{:S(2)}, u32[]{:S(2)}) %all-to-all-start.8) | async-done | bytes 65568 | tf_op jit(solution)/shard_map/all_to_all | solution.py:494
  138.3 11.7 %shard_map.55 = (f32[32,512]{1,0:T(8,128)}, f32[256,128]{1,0:T(8,128)}) custom-call(f32[128,640]{1,0:T(8,128)S(1)} %reshape.49.images_ref, f32[4,128,256]{2,1,0:T(8,128)S(1)} %pad_maximum_fusion.2.near_ref, f32[4,128,256]{2,1,0:T(8,128)S(1)} %collective-permute-done.10.far_ref, f32[128,128]{1,0:T(8,128)S(1)} %get-tuple-element.22.first_ref, ...), custom_call_target="tpu_custom_call" | custom-call | tf_op jit(solution)/shard_map/pallas_call | solution.py:439
  (23 shorter events, 0.3 us)
Async XLA Ops:
  0.6 0.8 copy-start
  1.5 0.8 copy-start.2
  2.3 0.9 copy-start.4
  4.5 7.9 %collective-permute-start = (f32[1,32,512]{2,1,0:T(8,128)S(1)}, f32[1,32,512]{2,1,0:T(8,128)S(1)}, u32[]{:S(2)}, u32[]{:S(2)}) collective-permute-start(f32[1,32,512]{2,1,0:T(8,128)S(1)} %bitcast.21), channel_id=1, source_target_pairs={{0,16},{1,17},{2,18},{3,19},{4,20},{5,21},{6,22},{7,23},{8,24},{9,... | collective-permute-start | bytes 196616 | tf_op jit(solution)/shard_map/ppermute | solution.py:450
  8.6 12.1 %all-to-all-start = ((f32[32,8,128]{2,1,0:T(8,128)}), f32[32,8,128]{2,1,0:T(8,128)S(1)}, u32[]{:S(2)}, u32[]{:S(2)}) async-start(f32[32,8,128]{2,1,0:T(8,128)} %bitcast.2), calls=%async_computation | async-start | bytes 262144 | tf_op jit(solution)/shard_map/all_to_all | solution.py:494
  12.4 7.7 %collective-permute-start.1 = (f32[2,32,512]{2,1,0:T(8,128)S(1)}, f32[2,32,512]{2,1,0:T(8,128)S(1)}, u32[]{:S(2)}, u32[]{:S(2)}) collective-permute-start(f32[2,32,512]{2,1,0:T(8,128)S(1)} %pad_maximum_fusion.7), channel_id=1, source_target_pairs={{0,8},{1,9},{2,10},{3,11},{4,12},{5,13},{6,14},{7,15},{8,0},{9,1},... | collective-permute-start | bytes 393224 | tf_op jit(solution)/shard_map/ppermute | solution.py:450
  20.7 6.1 %collective-permute-start.2 = (f32[4,16,512]{2,1,0:T(8,128)S(1)}, f32[4,16,512]{2,1,0:T(8,128)S(1)}, u32[]{:S(2)}, u32[]{:S(2)}) collective-permute-start(f32[4,16,512]{2,1,0:T(8,128)S(1)} %get-tuple-element.27), channel_id=1, source_target_pairs={{0,4},{1,5},{2,6},{3,7},{4,0},{5,1},{6,2},{7,3},{8,12},{9,13},{10,... | collective-permute-start | bytes 393224 | tf_op jit(solution)/shard_map/ppermute | solution.py:450
  21.8 5.2 %collective-permute-start.5 = (f32[4,16,512]{2,1,0:T(8,128)S(1)}, f32[4,16,512]{2,1,0:T(8,128)S(1)}, u32[]{:S(2)}, u32[]{:S(2)}) collective-permute-start(f32[4,16,512]{2,1,0:T(8,128)S(1)} %get-tuple-element.26), channel_id=1, source_target_pairs={{0,2},{1,3},{2,0},{3,1},{4,6},{5,7},{6,4},{7,5},{8,10},{9,11},{10,... | collective-permute-start | bytes 393224 | tf_op jit(solution)/shard_map/ppermute | solution.py:450
  26.8 8.1 %collective-permute-start.3 = (f32[8,16,512]{2,1,0:T(8,128)S(1)}, f32[8,16,512]{2,1,0:T(8,128)S(1)}, u32[]{:S(2)}, u32[]{:S(2)}) collective-permute-start(f32[8,16,512]{2,1,0:T(8,128)S(1)} %pad_maximum_fusion.4), channel_id=1, source_target_pairs={{0,2},{1,3},{2,0},{3,1},{4,6},{5,7},{6,4},{7,5},{8,10},{9,11},{10,... | collective-permute-start | bytes 786440 | tf_op jit(solution)/shard_map/ppermute | solution.py:450
  27.0 8.0 %collective-permute-start.6 = (f32[8,16,512]{2,1,0:T(8,128)S(1)}, f32[8,16,512]{2,1,0:T(8,128)S(1)}, u32[]{:S(2)}, u32[]{:S(2)}) collective-permute-start(f32[8,16,512]{2,1,0:T(8,128)S(1)} %pad_maximum_fusion.5), channel_id=1, source_target_pairs={{0,4},{1,5},{2,6},{3,7},{4,0},{5,1},{6,2},{7,3},{8,12},{9,13},{10,... | collective-permute-start | bytes 786440 | tf_op jit(solution)/shard_map/ppermute | solution.py:450
  35.0 2.0 %collective-permute-start.4 = (f32[16,16,512]{2,1,0:T(8,128)S(1)}, f32[16,16,512]{2,1,0:T(8,128)S(1)}, u32[]{:S(2)}, u32[]{:S(2)}) collective-permute-start(f32[16,16,512]{2,1,0:T(8,128)S(1)} %pad_maximum_fusion.top_near_ref), channel_id=1, source_target_pairs={{0,1},{1,0},{2,3},{3,2},{4,5},{5,4},{6,7},{7,6},{8,9},{9,8},{10,11... | collective-permute-start | bytes 1572872 | tf_op jit(solution)/shard_map/ppermute | solution.py:450
  35.1 2.6 %collective-permute-start.7 = (f32[16,16,512]{2,1,0:T(8,128)S(1)}, f32[16,16,512]{2,1,0:T(8,128)S(1)}, u32[]{:S(2)}, u32[]{:S(2)}) collective-permute-start(f32[16,16,512]{2,1,0:T(8,128)S(1)} %pad_maximum_fusion.1.low_near_ref), channel_id=1, source_target_pairs={{0,1},{1,0},{2,3},{3,2},{4,5},{5,4},{6,7},{7,6},{8,9},{9,8},{10,11... | collective-permute-start | bytes 1572872 | tf_op jit(solution)/shard_map/ppermute | solution.py:450
  69.9 13.5 %all-to-all-start.4 = ((f32[8,32,128]{2,1,0:T(8,128)}), f32[8,32,128]{2,1,0:T(8,128)S(1)}, u32[]{:S(2)}, u32[]{:S(2)}) async-start(f32[8,32,128]{2,1,0:T(8,128)} %broadcast_in_dim.17), calls=%async_computation.4 | async-start | bytes 262144 | tf_op jit(solution)/shard_map/all_to_all | solution.py:494
  73.2 33.5 %collective-permute-start.8 = (f32[1,128,256]{2,1,0:T(8,128)S(1)}, f32[1,128,256]{2,1,0:T(8,128)S(1)}, u32[]{:S(2)}, u32[]{:S(2)}) collective-permute-start(f32[1,128,256]{2,1,0:T(8,128)S(1)} %bitcast.13), channel_id=1, source_target_pairs={{0,16},{4,20},{8,24},{12,28},{16,0},{20,4},{24,8},{28,12},{1,17},{... | collective-permute-start | bytes 393224 | tf_op jit(solution)/shard_map/ppermute | solution.py:450
  103.4 11.6 %all-to-all-start.7 = ((f32[8,32,128]{2,1,0:T(8,128)}), f32[8,32,128]{2,1,0:T(8,128)S(1)}, u32[]{:S(2)}, u32[]{:S(2)}) async-start(f32[8,32,128]{2,1,0:T(8,128)} %broadcast_in_dim.19), calls=%async_computation.7 | async-start | bytes 262144 | tf_op jit(solution)/shard_map/all_to_all | solution.py:494
  106.8 11.5 %collective-permute-start.9 = (f32[2,128,256]{2,1,0:T(8,128)S(1)}, f32[2,128,256]{2,1,0:T(8,128)S(1)}, u32[]{:S(2)}, u32[]{:S(2)}) collective-permute-start(f32[2,128,256]{2,1,0:T(8,128)S(1)} %pad_maximum_fusion.6), channel_id=1, source_target_pairs={{0,8},{4,12},{8,0},{12,4},{16,24},{20,28},{24,16},{28,20},{1,9},{5... | collective-permute-start | bytes 786440 | tf_op jit(solution)/shard_map/ppermute | solution.py:450
  110.9 27.5 %copy-start.1 = (f32[32,512]{1,0:T(8,128)S(1)}, f32[32,512]{1,0:T(8,128)}, u32[]{:S(2)}) copy-start(f32[32,512]{1,0:T(8,128)} %kspace_ref.1) | copy-start | bytes 196612
  110.9 27.4 %copy-start.3 = (s32[32,512]{1,0:T(8,128)S(1)}, s32[32,512]{1,0:T(8,128)}, u32[]{:S(2)}) copy-start(s32[32,512]{1,0:T(8,128)} %mask_ref.1) | copy-start | bytes 196612
  115.7 14.6 %all-to-all-start.1 = ((f32[32,4,640]{2,1,0:T(4,128)}), f32[32,4,640]{2,1,0:T(4,128)S(1)}, u32[]{:S(2)}, u32[]{:S(2)}) async-start(f32[32,4,640]{2,1,0:T(4,128)} %bitcast.4), calls=%async_computation.1 | async-start | bytes 655360 | tf_op jit(solution)/shard_map/all_to_all | solution.py:494
  118.4 20.0 %collective-permute-start.10 = (f32[4,128,256]{2,1,0:T(8,128)S(1)}, f32[4,128,256]{2,1,0:T(8,128)S(1)}, u32[]{:S(2)}, u32[]{:S(2)}) collective-permute-start(f32[4,128,256]{2,1,0:T(8,128)S(1)} %pad_maximum_fusion.2.near_ref), channel_id=1, source_target_pairs={{0,4},{4,0},{8,12},{12,8},{16,20},{20,16},{24,28},{28,24},{1,5},{5... | collective-permute-start | bytes 1572872 | tf_op jit(solution)/shard_map/ppermute | solution.py:450
  130.9 7.4 %all-to-all-start.8 = ((f32[4,32,128]{2,1,0:T(8,128)}), f32[4,32,128]{2,1,0:T(8,128)S(1)}, u32[]{:S(2)}, u32[]{:S(2)}) async-start(f32[4,32,128]{2,1,0:T(8,128)} %broadcast_in_dim.20), calls=%async_computation.8 | async-start | bytes 131072 | tf_op jit(solution)/shard_map/all_to_all | solution.py:494

commit v3 on v2

--- a/solution.py
+++ b/solution.py
@@ -304,10 +304,23 @@
     )
 
 
-def gram_kernel(cols, per_tile, received_ref, gram_ref, turned_ref):
+def store_halves(gram, kept_ref, given_ref):
+    half = gram.shape[0] // 2
+    odd = lax.axis_index("coil") % 2 == 1
+    kept_ref[...] = jnp.where(odd, gram[half:], gram[:half])
+    given_ref[...] = jnp.where(odd, gram[:half], gram[half:])
+
+
+def load_halves(kept_ref, other_ref):
+    odd = lax.axis_index("coil") % 2 == 1
+    kept, other = kept_ref[...], other_ref[...]
+    return jnp.concatenate([jnp.where(odd, other, kept), jnp.where(odd, kept, other)], axis=0)
+
+
+def gram_kernel(cols, per_tile, received_ref, kept_ref, given_ref, rows_ref):
     turned = gather_turned(received_ref, cols, per_tile, 0)
-    gram_ref[...] = exact(turned, turned, ((1,), (1,)))
-    turned_ref[...] = gather_turned(received_ref, cols, per_tile, 1)
+    store_halves(exact(turned, turned, ((1,), (1,))), kept_ref, given_ref)
+    rows_ref[...] = gather_turned(received_ref, cols, per_tile, 1).T
 
 
 def inverse_factor(gram):
@@ -380,11 +393,11 @@
     return jnp.concatenate(done, axis=0)
 
 
-def middle_kernel(gram_ref, turned_ref, inverse_ref, next_ref):
-    inverse = inverse_factor(gram_ref[...])
+def middle_kernel(gram_ref, other_ref, rows_ref, inverse_ref, kept_ref, given_ref):
+    inverse = inverse_factor(load_halves(gram_ref, other_ref))
     inverse_ref[...] = inverse
-    turned = exact(inverse, turned_ref[...])
-    next_ref[...] = exact(turned, turned, ((1,), (1,)))
+    rows = exact(rows_ref[...], inverse, ((1,), (1,)))
+    store_halves(exact(rows, rows, ((0,), (0,))), kept_ref, given_ref)
 
 
 def last_kernel(
@@ -395,12 +408,13 @@
     far_ref,
     first_ref,
     gram_ref,
+    other_ref,
     kspace_ref,
     mask_ref,
     recovered_ref,
     basis_ref,
 ):
-    inverse = inverse_factor(gram_ref[...])
+    inverse = inverse_factor(load_halves(gram_ref, other_ref))
     count, reach = images_ref.shape
     devices = count // cols
     at_row = lax.broadcasted_iota(jnp.int32, (count, count), 0)
@@ -417,8 +431,8 @@
     half = near_ref.shape[0]
     estimate = jnp.zeros((chg, tile), jnp.float32)
     for slot, mask in enumerate(masks):
-        turned = near_ref[slot] if slot < half else far_ref[slot - half]
-        vectors = exact(inverse, turned).T
+        rows = near_ref[slot] if slot < half else far_ref[slot - half]
+        vectors = dot3(rows, inverse, ((1,), (1,)))
         if slot == 0:
             basis_ref[...] = vectors
         high, low = split(vectors)
@@ -435,14 +449,14 @@
     recovered_ref[...] = estimate + residual - jnp.clip(residual, -threshold, threshold)
 
 
-def call(kernel, outs, *args, scratch=(), space=pltpu.VMEM):
+def call(kernel, outs, *args, scratch=(), space=pltpu.VMEM, limit=40):
     return pl.pallas_call(
         kernel,
         out_shape=[jax.ShapeDtypeStruct(shape, kind) for shape, kind in outs],
         in_specs=[pl.BlockSpec(memory_space=space)] * len(args),
         out_specs=[pl.BlockSpec(memory_space=pltpu.VMEM)] * len(outs),
         scratch_shapes=list(scratch),
-        compiler_params=pltpu.CompilerParams(vmem_limit_bytes=40 * 2**20),
+        compiler_params=pltpu.CompilerParams(vmem_limit_bytes=limit * 2**20),
     )(*args)
 
 
@@ -450,41 +464,51 @@
     return lax.ppermute(block, axes, [(i, i ^ mask) for i in range(devices)])
 
 
-def joined(near, far):
-    return jnp.concatenate([near, far], axis=0)
-
-
 def with_masks(masks, mask):
     return masks + [m ^ mask for m in masks]
 
 
 def after(value, *others):
     return lax.optimization_barrier((value,) + others)[0]
+
+
+def rounds_of(low, high):
+    masks = []
+    while low < high:
+        if 2 * low < high:
+            masks.append([low, 2 * low, 3 * low])
+        else:
+            masks.append([low])
+        low *= 4
+    return masks
+
+
+def gather_round(part, order, masks, devices, axes):
+    part = jnp.concatenate(
+        [part] + [exchange(part, devices, mask, axes) for mask in masks], axis=0
+    )
+    return part, order + [m ^ mask for mask in masks for m in order]
 
 
 def gather_samples(sampled, tiles, groups, beside):
     devices = tiles * groups
     near, masks = sampled[None], [0]
-    mask = devices // 2
-    while mask > groups:
-        near = joined(near, exchange(near, devices, mask, AXES))
-        masks = with_masks(masks, mask)
-        mask //= 2
-    near = after(near, beside)
+    for partners in rounds_of(2 * groups, devices):
+        near, masks = gather_round(near, masks, partners, devices, AXES)
     half = near.shape[1] // 2
     parts = [near[:, :half], near[:, half:]]
     orders = [masks, masks]
     ways = [(groups, groups // 2), (groups // 2, groups)]
     for step in range(2):
-        parts = [
-            joined(part, exchange(part, devices, way[step], AXES)) for part, way in zip(parts, ways)
-        ]
-        orders = [with_masks(order, way[step]) for order, way in zip(orders, ways)]
-    mask = groups // 4
-    while mask > 1:
-        parts = [joined(part, exchange(part, devices, mask, AXES)) for part in parts]
-        orders = [with_masks(order, mask) for order in orders]
-        mask //= 2
+        for i in range(2):
+            parts[i], orders[i] = gather_round(
+                parts[i], orders[i], [ways[i][step]], devices, AXES
+            )
+        if step == 0:
+            parts = list(lax.optimization_barrier((*parts, beside))[:2])
+    for partners in rounds_of(2, groups // 2):
+        for i in range(2):
+            parts[i], orders[i] = gather_round(parts[i], orders[i], partners, devices, AXES)
     far = [exchange(part, devices, 1, AXES) for part in parts]
     orders = [with_masks(order, 1) for order in orders]
     return parts, far, orders
@@ -494,13 +518,13 @@
     return lax.all_to_all(pieces, axes, 0, 0, tiled=True)
 
 
-def total_of(gram, tiles, groups):
-    size = gram.shape[0]
-    block = (size // groups, size)
-    mine = jnp.sum(to_all(gram.reshape((groups,) + block), "coil"), axis=0)
-    mine = jnp.sum(to_all(jnp.broadcast_to(mine[None], (tiles,) + block), "rows"), axis=0)
-    whole = to_all(jnp.broadcast_to(mine[None], (groups,) + block), "coil")
-    return whole.reshape(size, size)
+def total_of(kept, given, devices):
+    total = kept + exchange(given, devices, 1, AXES)
+    for partners in rounds_of(2, devices):
+        terms = [exchange(total, devices, mask, AXES) for mask in partners]
+        for term in terms:
+            total = total + term
+    return total, exchange(total, devices, 1, AXES)
 
 
 def column_shards(kspace, sample_mask, start_basis):
@@ -528,7 +552,8 @@
             pltpu.VMEM((owned, rank), f32),
             pltpu.SemaphoreType.DMA((3,)),
         ],
-        space=pl.ANY,
+        space=pltpu.HBM,
+        limit=60,
     )
     basis_parts = to_all(basis_send.reshape(devices, per_tile, lanes))
     near, far, masks = gather_samples(sampled, tiles, groups, basis_parts)
@@ -552,33 +577,33 @@
     reach = tile + LANES
     (images,) = call(images_kernel, [((tiles, cols, reach), f32)], samples, normal, scratch=[wide])
     images = jnp.broadcast_to(images[:, None], (tiles, groups, cols, reach))
-    gram, turned = call(
+    received = after(received, images)
+    half = ((rank // 2, rank), f32)
+    kept, given, by_row = call(
         functools.partial(gram_kernel, cols, per_tile),
-        [((rank, rank), f32), ((rank, owned), f32)],
+        [half, half, ((owned, rank), f32)],
         received.reshape(devices * 2 * per_tile, lanes),
     )
-    gram = total_of(gram, tiles, groups)
+    gram = total_of(kept, given, devices)
     images = to_all(images.reshape(devices, cols, reach)).reshape(rank, reach)
-    near, masks = turned[None], [0]
-    mask = tiles // 2
-    while mask > 1:
-        near = joined(near, exchange(near, tiles, mask, "rows"))
-        masks = with_masks(masks, mask)
-        mask //= 2
+    near, order = by_row[None], [0]
+    for partners in rounds_of(2, tiles):
+        near, order = gather_round(near, order, partners, tiles, "rows")
+    by_row, images, near = lax.optimization_barrier((by_row, images, near))
     far = exchange(near, tiles, 1, "rows")
-    masks = with_masks(masks, 1)
-    inverse, gram = call(
-        middle_kernel, [((rank, rank), f32), ((rank, rank), f32)], gram, turned
-    )
-    gram = total_of(gram, tiles, groups)
+    order = with_masks(order, 1)
+    inverse, kept, given = call(
+        middle_kernel, [((rank, rank), f32), half, half], *gram, by_row
+    )
+    gram = total_of(kept, given, devices)
     recovered, basis = call(
-        functools.partial(last_kernel, cols, masks),
+        functools.partial(last_kernel, cols, order),
         [((chg, tile), f32), ((owned, rank), f32)],
         images,
         near,
         far,
         inverse,
-        gram,
+        *gram,
         kspace,
         sample_mask,
     )
@@ -594,6 +619,7 @@
         devices & (devices - 1) == 0
         and tiles > 1
         and groups > 2
+        and rank % (2 * SUB) == 0
         and rank % devices == 0
         and rank % LANES == 0
         and tile % LANES == 0

time: 151 us -> 132 us (0.87)
  blocking collectives: 32.3 us -> 0 us
  starting transfers between devices: 34.1 us -> 43.8 us
  waiting for transfers between devices: 43.5 us -> 51.2 us
  local copies, waits for them, and re-layouts: 5.47 us -> 1.01 us
    all_to_all x4 -> x0, blocking collectives: 32.3 us -> none  [to_all(): return lax.all_to_all(pieces, axes, 0, 0, tiled=True)]
    ppermute x11 -> x29, waiting for transfers between devices: 17.8 us -> 41.5 us  [exchange(): return lax.ppermute(block, axes, [(i, i ^ mask) for i in range(devices)])]
    all_to_all x5 -> x3, waiting for transfers between devices: 25.7 us -> 9.72 us  [to_all(): return lax.all_to_all(pieces, axes, 0, 0, tiled=True)]
    ppermute x11 -> x29, starting transfers between devices: 17.4 us -> 33.4 us  [exchange(): return lax.ppermute(block, axes, [(i, i ^ mask) for i in range(devices)])]
    all_to_all x5 -> x3, starting transfers between devices: 16.7 us -> 10.4 us  [to_all(): return lax.all_to_all(pieces, axes, 0, 0, tiled=True)]
    unnamed x10 -> x6, local copies, waits for them, and re-layouts: 2.59 us -> 0.05 us
    broadcast_in_dim x4 -> x0, local copies, waits for them, and re-layouts: 1.97 us -> none  [the longest x2 1.33 us: total_of(): jnp.broadcast_to(mine[None], (tiles,) + block)]
  transfers between devices with their start and end apart: 16 -> 32, of which waited for: 10 -> 23; matrix products, arithmetic and copies ran while one was open for 2% -> 0% of each run, Pallas kernels for 6% -> 2%
where the time goes in v3:
time: 132 us; the launch traced here: 131 us
  waiting for transfers between devices  51.2 us (39%)
  starting transfers between devices  43.8 us (33%)
  Pallas kernels  33.5 us (25%)
    ppermute x29, waiting for transfers between devices, exchange(): return lax.ppermute(block, axes, [(i, i ^ mask) for i in range(devices)])  41.5 us
    pallas_call x6, Pallas kernels, call(): pl.pallas_call(kernel, out_shape=[jax.ShapeDtypeStruct(shape, kind) for s...  33.5 us
    ppermute x29, starting transfers between devices, exchange(): return lax.ppermute(block, axes, [(i, i ^ mask) for i in range(devices)])  33.4 us
    all_to_all x3, starting transfers between devices, to_all(): return lax.all_to_all(pieces, axes, 0, 0, tiled=True)  10.4 us
    all_to_all x3, waiting for transfers between devices, to_all(): return lax.all_to_all(pieces, axes, 0, 0, tiled=True)  9.72 us
  transfers between devices with their start and end apart: 32, of which 23 were waited for; matrix products, arithmetic and copies ran while one was open for 0% of the time, Pallas kernels for 2%

profile of v3, /device:TPU:0, one launch (start us, length us, event | category | flops | bytes accessed | tf_op | source)
XLA Modules:
  0.0 131.4 jit_solution(10313342039605977433)
XLA Ops:
  0.6 1.9 %shard_map.50 = (f32[32,512]{1,0:T(8,128)}, f32[256,128]{1,0:T(8,128)}) custom-call(f32[32,512]{1,0:T(8,128)} %kspace_ref.1, s32[32,512]{1,0:T(8,128)} %mask_ref.1, f32[256,128]{1,0:T(8,128)} %bitcast.15), custom_call_target="tpu_custom_call" | custom-call | tf_op jit(solution)/shard_map/pallas_call | solution.py:453
  2.5 5.1 %collective-permute-start.2 = (f32[1,32,512]{2,1,0:T(8,128)}, f32[1,32,512]{2,1,0:T(8,128)S(1)}, u32[]{:S(2)}, u32[]{:S(2)}) collective-permute-start(f32[1,32,512]{2,1,0:T(8,128)} %bitcast.17), channel_id=1, source_target_pairs={{0,24},{1,25},{2,26},{3,27},{4,28},{5,29},{6,30},{7,31},{8,16},{9,... | collective-permute-start | bytes 196616 | tf_op jit(solution)/shard_map/ppermute | solution.py:464
  7.7 0.6 collective-permute-start
  8.3 2.2 %collective-permute-done.2 = f32[1,32,512]{2,1,0:T(8,128)S(1)} collective-permute-done((f32[1,32,512]{2,1,0:T(8,128)}, f32[1,32,512]{2,1,0:T(8,128)S(1)}, u32[]{:S(2)}, u32[]{:S(2)}) %collective-permute-start.2) | collective-permute-done | bytes 65568 | tf_op jit(solution)/shard_map/ppermute | solution.py:464
  10.5 3.0 %collective-permute-done.1 = f32[1,32,512]{2,1,0:T(8,128)S(1)} collective-permute-done((f32[1,32,512]{2,1,0:T(8,128)}, f32[1,32,512]{2,1,0:T(8,128)S(1)}, u32[]{:S(2)}, u32[]{:S(2)}) %collective-permute-start.1) | collective-permute-done | bytes 65568 | tf_op jit(solution)/shard_map/ppermute | solution.py:464
  13.5 0.9 pad_maximum_fusion.1
  14.4 1.6 %collective-permute-start.4 = (f32[4,16,512]{2,1,0:T(8,128)S(1)}, f32[4,16,512]{2,1,0:T(8,128)S(1)}, u32[]{:S(2)}, u32[]{:S(2)}) collective-permute-start(f32[4,16,512]{2,1,0:T(8,128)S(1)} %get-tuple-element.40), channel_id=1, source_target_pairs={{0,2},{1,3},{2,0},{3,1},{4,6},{5,7},{6,4},{7,5},{8,10},{9,11},{10,... | collective-permute-start | bytes 393224 | tf_op jit(solution)/shard_map/ppermute | solution.py:464
  15.9 4.0 %all-to-all-start = ((f32[32,8,128]{2,1,0:T(8,128)}), f32[32,8,128]{2,1,0:T(8,128)S(1)}, u32[]{:S(2)}, u32[]{:S(2)}) async-start(f32[32,8,128]{2,1,0:T(8,128)} %bitcast.16), calls=%async_computation | async-start | bytes 262144 | tf_op jit(solution)/shard_map/all_to_all | solution.py:518
  20.0 1.8 %collective-permute-start.3 = (f32[4,16,512]{2,1,0:T(8,128)S(1)}, f32[4,16,512]{2,1,0:T(8,128)S(1)}, u32[]{:S(2)}, u32[]{:S(2)}) collective-permute-start(f32[4,16,512]{2,1,0:T(8,128)S(1)} %get-tuple-element.41), channel_id=1, source_target_pairs={{0,4},{1,5},{2,6},{3,7},{4,0},{5,1},{6,2},{7,3},{8,12},{9,13},{10,... | collective-permute-start | bytes 393224 | tf_op jit(solution)/shard_map/ppermute | solution.py:464
  21.8 5.1 %collective-permute-done.3 = f32[4,16,512]{2,1,0:T(8,128)S(1)} collective-permute-done((f32[4,16,512]{2,1,0:T(8,128)S(1)}, f32[4,16,512]{2,1,0:T(8,128)S(1)}, u32[]{:S(2)}, u32[]{:S(2)}) %collective-permute-start.3) | collective-permute-done | bytes 131104 | tf_op jit(solution)/shard_map/ppermute | solution.py:464
  26.9 1.3 all-to-all-done
  28.2 0.7 collective-permute-start.7
  28.9 1.0 collective-permute-start.5
  29.9 6.7 %collective-permute-done.7 = f32[8,16,512]{2,1,0:T(8,128)S(1)} collective-permute-done((f32[8,16,512]{2,1,0:T(8,128)S(1)}, f32[8,16,512]{2,1,0:T(8,128)S(1)}, u32[]{:S(2)}, u32[]{:S(2)}) %collective-permute-start.7) | collective-permute-done | bytes 262176 | tf_op jit(solution)/shard_map/ppermute | solution.py:464
  37.3 1.3 collective-permute-done.8.low_far_ref
  38.6 0.7 collective-permute-done.6.top_far_ref
  39.4 12.4 %shard_map.51 = (bf16[8,2,4,32,512]{4,3,2,1,0:T(8,128)(2,1)S(1)}, f32[256,128]{1,0:T(8,128)S(1)}, f32[8,4,2,8,128]{4,3,2,1,0:T(8,128)}) custom-call(f32[16,16,512]{2,1,0:T(8,128)S(1)} %constant_dynamic-update-slice_fusion.top_near_ref, f32[16,16,512]{2,1,0:T(8,128)S(1)} %collective-permute-done.6.top_far_ref, ...), custom_call_target="tpu_custom_call" | custom-call | tf_op jit(solution)/shard_map/pallas_call | solution.py:453
  51.8 3.6 %all-to-all-start.1 = ((f32[32,16,128]{2,1,0:T(8,128)}), f32[32,16,128]{2,1,0:T(8,128)S(1)}, u32[]{:S(2)}, u32[]{:S(2)}) async-start(f32[32,16,128]{2,1,0:T(8,128)} %bitcast.4), calls=%async_computation.1 | async-start | bytes 524288 | tf_op jit(solution)/shard_map/all_to_all | solution.py:518
  55.4 2.1 %shard_map.52 = f32[8,4,640]{2,1,0:T(4,128)S(1)} custom-call(bf16[8,2,4,32,512]{4,3,2,1,0:T(8,128)(2,1)S(1)} %get-tuple-element.26.samples_ref, f32[256,128]{1,0:T(8,128)S(1)} %get-tuple-element.27.vectors_ref), custom_call_target="tpu_custom_call" | custom-call | tf_op jit(solution)/shard_map/pallas_call | solution.py:453
  57.6 8.5 %all-to-all-done.1 = f32[32,16,128]{2,1,0:T(8,128)S(1)} async-done(((f32[32,16,128]{2,1,0:T(8,128)}), f32[32,16,128]{2,1,0:T(8,128)S(1)}, u32[]{:S(2)}, u32[]{:S(2)}) %all-to-all-start.1) | async-done | bytes 262176 | tf_op jit(solution)/shard_map/all_to_all | solution.py:518
  66.0 0.8 broadcast_in_dim.13
  66.8 2.8 %all-to-all-start.2 = ((f32[32,4,640]{2,1,0:T(4,128)}), f32[32,4,640]{2,1,0:T(4,128)S(1)}, u32[]{:S(2)}, u32[]{:S(2)}) async-start(f32[32,4,640]{2,1,0:T(4,128)} %bitcast.6), calls=%async_computation.2 | async-start | bytes 655360 | tf_op jit(solution)/shard_map/all_to_all | solution.py:518
  70.2 1.1 collective-permute-done.13
  71.3 2.6 %collective-permute-start.16 = (f32[64,128]{1,0:T(8,128)S(1)}, f32[64,128]{1,0:T(8,128)S(1)}, u32[]{:S(2)}, u32[]{:S(2)}) collective-permute-start(f32[64,128]{1,0:T(8,128)S(1)} %add.42), channel_id=1, source_target_pairs={{0,6},{1,7},{2,4},{3,5},{4,2},{5,3},{6,0},{7,1},{8,14},{9,15},{10,... | collective-permute-start | bytes 98312 | tf_op jit(solution)/shard_map/ppermute | solution.py:464
  74.8 1.9 %collective-permute-done.16 = f32[64,128]{1,0:T(8,128)S(1)} collective-permute-done((f32[64,128]{1,0:T(8,128)S(1)}, f32[64,128]{1,0:T(8,128)S(1)}, u32[]{:S(2)}, u32[]{:S(2)}) %collective-permute-start.16) | collective-permute-done | bytes 32800 | tf_op jit(solution)/shard_map/ppermute | solution.py:464
  76.7 1.1 collective-permute-done.15
  77.8 0.9 collective-permute-done.14
  78.8 3.3 %collective-permute-start.19 = (f32[64,128]{1,0:T(8,128)S(1)}, f32[64,128]{1,0:T(8,128)S(1)}, u32[]{:S(2)}, u32[]{:S(2)}) collective-permute-start(f32[64,128]{1,0:T(8,128)S(1)} %add_add_fusion.3), channel_id=1, source_target_pairs={{0,24},{1,25},{2,26},{3,27},{4,28},{5,29},{6,30},{7,31},{8,16},{9,... | collective-permute-start | bytes 98312 | tf_op jit(solution)/shard_map/ppermute | solution.py:464
  82.1 1.2 collective-permute-start.17
  83.2 3.2 %collective-permute-start.11 = (f32[1,256,128]{2,1,0:T(8,128)S(1)}, f32[1,256,128]{2,1,0:T(8,128)S(1)}, u32[]{:S(2)}, u32[]{:S(2)}) collective-permute-start(f32[1,256,128]{2,1,0:T(8,128)S(1)} %bitcast.11), channel_id=1, source_target_pairs={{0,24},{4,28},{8,16},{12,20},{16,8},{20,12},{24,0},{28,4},{1,25},{... | collective-permute-start | bytes 393224 | tf_op jit(solution)/shard_map/ppermute | solution.py:464
  86.4 1.2 collective-permute-start.9
  87.6 3.0 %collective-permute-done.18 = f32[64,128]{1,0:T(8,128)S(1)} collective-permute-done((f32[64,128]{1,0:T(8,128)S(1)}, f32[64,128]{1,0:T(8,128)S(1)}, u32[]{:S(2)}, u32[]{:S(2)}) %collective-permute-start.18) | collective-permute-done | bytes 32800 | tf_op jit(solution)/shard_map/ppermute | solution.py:464
  90.8 0.7 collective-permute-done.11
  91.5 5.2 %collective-permute-done.10 = f32[1,256,128]{2,1,0:T(8,128)S(1)} collective-permute-done((f32[1,256,128]{2,1,0:T(8,128)S(1)}, f32[1,256,128]{2,1,0:T(8,128)S(1)}, u32[]{:S(2)}, u32[]{:S(2)}) %collective-permute-start.10) | collective-permute-done | bytes 131104 | tf_op jit(solution)/shard_map/ppermute | solution.py:464
  96.8 6.5 %shard_map.54 = (f32[128,128]{1,0:T(8,128)S(1)}, f32[64,128]{1,0:T(8,128)S(1)}, f32[64,128]{1,0:T(8,128)S(1)}) custom-call(f32[64,128]{1,0:T(8,128)S(1)} %add_add_fusion.2.gram_ref, f32[64,128]{1,0:T(8,128)S(1)} %collective-permute-done.20.other_ref, f32[256,128]{1,0:T(8,128)S(1)} %get-tuple-element.34.rows_ref), custom_call_target="tpu_custom_call" | custom-call | tf_op jit(solution)/shard_map/pallas_call | solution.py:453
  103.4 1.2 collective-permute-done.21
  104.6 1.2 collective-permute-start.24
  105.8 1.1 collective-permute-start.23
  106.8 1.3 collective-permute-start.22
  108.1 1.3 %collective-permute-start.12 = (f32[4,256,128]{2,1,0:T(8,128)S(1)}, f32[4,256,128]{2,1,0:T(8,128)S(1)}, u32[]{:S(2)}, u32[]{:S(2)}) collective-permute-start(f32[4,256,128]{2,1,0:T(8,128)S(1)} %pad_maximum_fusion.near_ref), channel_id=1, source_target_pairs={{0,4},{4,0},{8,12},{12,8},{16,20},{20,16},{24,28},{28,24},{1,5},{5... | collective-permute-start | bytes 1572872 | tf_op jit(solution)/shard_map/ppermute | solution.py:464
  109.7 1.1 collective-permute-done.22
  110.7 2.3 %collective-permute-start.27 = (f32[64,128]{1,0:T(8,128)S(1)}, f32[64,128]{1,0:T(8,128)S(1)}, u32[]{:S(2)}, u32[]{:S(2)}) collective-permute-start(f32[64,128]{1,0:T(8,128)S(1)} %add_add_fusion.1), channel_id=1, source_target_pairs={{0,24},{1,25},{2,26},{3,27},{4,28},{5,29},{6,30},{7,31},{8,16},{9,... | collective-permute-start | bytes 98312 | tf_op jit(solution)/shard_map/ppermute | solution.py:464
  113.1 2.1 %collective-permute-start.25 = (f32[64,128]{1,0:T(8,128)S(1)}, f32[64,128]{1,0:T(8,128)S(1)}, u32[]{:S(2)}, u32[]{:S(2)}) collective-permute-start(f32[64,128]{1,0:T(8,128)S(1)} %add_add_fusion.1), channel_id=1, source_target_pairs={{0,8},{1,9},{2,10},{3,11},{4,12},{5,13},{6,14},{7,15},{8,0},{9,1},... | collective-permute-start | bytes 98312 | tf_op jit(solution)/shard_map/ppermute | solution.py:464
  115.2 1.3 %collective-permute-done.27 = f32[64,128]{1,0:T(8,128)S(1)} collective-permute-done((f32[64,128]{1,0:T(8,128)S(1)}, f32[64,128]{1,0:T(8,128)S(1)}, u32[]{:S(2)}, u32[]{:S(2)}) %collective-permute-start.27) | collective-permute-done | bytes 32800 | tf_op jit(solution)/shard_map/ppermute | solution.py:464
  116.5 1.4 %collective-permute-done.26 = f32[64,128]{1,0:T(8,128)S(1)} collective-permute-done((f32[64,128]{1,0:T(8,128)S(1)}, f32[64,128]{1,0:T(8,128)S(1)}, u32[]{:S(2)}, u32[]{:S(2)}) %collective-permute-start.26) | collective-permute-done | bytes 32800 | tf_op jit(solution)/shard_map/ppermute | solution.py:464
  118.0 1.2 collective-permute-done.28.other_ref
  119.2 2.0 %collective-permute-done.12.far_ref = f32[4,256,128]{2,1,0:T(8,128)S(1)} collective-permute-done((f32[4,256,128]{2,1,0:T(8,128)S(1)}, f32[4,256,128]{2,1,0:T(8,128)S(1)}, u32[]{:S(2)}, u32[]{:S(2)}) %collective-permute-start.12) | collective-permute-done | bytes 524320 | tf_op jit(solution)/shard_map/ppermute | solution.py:464
  121.2 10.2 %shard_map.55 = (f32[32,512]{1,0:T(8,128)}, f32[256,128]{1,0:T(8,128)}) custom-call(f32[128,640]{1,0:T(8,128)S(1)} %reshape.35.images_ref, f32[4,256,128]{2,1,0:T(8,128)S(1)} %pad_maximum_fusion.near_ref, f32[4,256,128]{2,1,0:T(8,128)S(1)} %collective-permute-done.12.far_ref, f32[128,128]{1,0:T(8,128)S(1)} %get-tuple-element.35.first_ref, ...), custom_call_target="tpu_custom_call" | custom-call | tf_op jit(solution)/shard_map/pallas_call | solution.py:453
  (43 shorter events, 3.0 us)
Async XLA Ops:
  2.5 7.9 %collective-permute-start.2 = (f32[1,32,512]{2,1,0:T(8,128)}, f32[1,32,512]{2,1,0:T(8,128)S(1)}, u32[]{:S(2)}, u32[]{:S(2)}) collective-permute-start(f32[1,32,512]{2,1,0:T(8,128)} %bitcast.17), channel_id=1, source_target_pairs={{0,24},{1,25},{2,26},{3,27},{4,28},{5,29},{6,30},{7,31},{8,16},{9,... | collective-permute-start | bytes 196616 | tf_op jit(solution)/shard_map/ppermute | solution.py:464
  7.6 5.8 %collective-permute-start.1 = (f32[1,32,512]{2,1,0:T(8,128)}, f32[1,32,512]{2,1,0:T(8,128)S(1)}, u32[]{:S(2)}, u32[]{:S(2)}) collective-permute-start(f32[1,32,512]{2,1,0:T(8,128)} %bitcast.18), channel_id=1, source_target_pairs={{0,16},{1,17},{2,18},{3,19},{4,20},{5,21},{6,22},{7,23},{8,24},{9,... | collective-permute-start | bytes 196616 | tf_op jit(solution)/shard_map/ppermute | solution.py:464
  7.7 5.8 %collective-permute-start = (f32[1,32,512]{2,1,0:T(8,128)}, f32[1,32,512]{2,1,0:T(8,128)S(1)}, u32[]{:S(2)}, u32[]{:S(2)}) collective-permute-start(f32[1,32,512]{2,1,0:T(8,128)} %bitcast.19), channel_id=1, source_target_pairs={{0,8},{1,9},{2,10},{3,11},{4,12},{5,13},{6,14},{7,15},{8,0},{9,1},... | collective-permute-start | bytes 196616 | tf_op jit(solution)/shard_map/ppermute | solution.py:464
  14.4 7.4 %collective-permute-start.4 = (f32[4,16,512]{2,1,0:T(8,128)S(1)}, f32[4,16,512]{2,1,0:T(8,128)S(1)}, u32[]{:S(2)}, u32[]{:S(2)}) collective-permute-start(f32[4,16,512]{2,1,0:T(8,128)S(1)} %get-tuple-element.40), channel_id=1, source_target_pairs={{0,2},{1,3},{2,0},{3,1},{4,6},{5,7},{6,4},{7,5},{8,10},{9,11},{10,... | collective-permute-start | bytes 393224 | tf_op jit(solution)/shard_map/ppermute | solution.py:464
  15.9 12.2 %all-to-all-start = ((f32[32,8,128]{2,1,0:T(8,128)}), f32[32,8,128]{2,1,0:T(8,128)S(1)}, u32[]{:S(2)}, u32[]{:S(2)}) async-start(f32[32,8,128]{2,1,0:T(8,128)} %bitcast.16), calls=%async_computation | async-start | bytes 262144 | tf_op jit(solution)/shard_map/all_to_all | solution.py:518
  20.0 6.9 %collective-permute-start.3 = (f32[4,16,512]{2,1,0:T(8,128)S(1)}, f32[4,16,512]{2,1,0:T(8,128)S(1)}, u32[]{:S(2)}, u32[]{:S(2)}) collective-permute-start(f32[4,16,512]{2,1,0:T(8,128)S(1)} %get-tuple-element.41), channel_id=1, source_target_pairs={{0,4},{1,5},{2,6},{3,7},{4,0},{5,1},{6,2},{7,3},{8,12},{9,13},{10,... | collective-permute-start | bytes 393224 | tf_op jit(solution)/shard_map/ppermute | solution.py:464
  28.2 8.4 %collective-permute-start.7 = (f32[8,16,512]{2,1,0:T(8,128)S(1)}, f32[8,16,512]{2,1,0:T(8,128)S(1)}, u32[]{:S(2)}, u32[]{:S(2)}) collective-permute-start(f32[8,16,512]{2,1,0:T(8,128)S(1)} %pad_maximum_fusion.3), channel_id=1, source_target_pairs={{0,4},{1,5},{2,6},{3,7},{4,0},{5,1},{6,2},{7,3},{8,12},{9,13},{10,... | collective-permute-start | bytes 786440 | tf_op jit(solution)/shard_map/ppermute | solution.py:464
  28.9 7.8 %collective-permute-start.5 = (f32[8,16,512]{2,1,0:T(8,128)S(1)}, f32[8,16,512]{2,1,0:T(8,128)S(1)}, u32[]{:S(2)}, u32[]{:S(2)}) collective-permute-start(f32[8,16,512]{2,1,0:T(8,128)S(1)} %pad_maximum_fusion.2), channel_id=1, source_target_pairs={{0,2},{1,3},{2,0},{3,1},{4,6},{5,7},{6,4},{7,5},{8,10},{9,11},{10,... | collective-permute-start | bytes 786440 | tf_op jit(solution)/shard_map/ppermute | solution.py:464
  36.6 2.0 %collective-permute-start.8 = (f32[16,16,512]{2,1,0:T(8,128)S(1)}, f32[16,16,512]{2,1,0:T(8,128)S(1)}, u32[]{:S(2)}, u32[]{:S(2)}) collective-permute-start(f32[16,16,512]{2,1,0:T(8,128)S(1)} %constant_dynamic-update-slice_fusion.2.low_near_ref), channel_id=1, source_target_pairs={{0,1},{1,0},{2,3},{3,2},{4,5},{5,4},{6,7},{7,6},{8,9},{9,8},{10,11... | collective-permute-start | bytes 1572872 | tf_op jit(solution)/shard_map/ppermute | solution.py:464
  36.8 2.6 %collective-permute-start.6 = (f32[16,16,512]{2,1,0:T(8,128)S(1)}, f32[16,16,512]{2,1,0:T(8,128)S(1)}, u32[]{:S(2)}, u32[]{:S(2)}) collective-permute-start(f32[16,16,512]{2,1,0:T(8,128)S(1)} %constant_dynamic-update-slice_fusion.top_near_ref), channel_id=1, source_target_pairs={{0,1},{1,0},{2,3},{3,2},{4,5},{5,4},{6,7},{7,6},{8,9},{9,8},{10,11... | collective-permute-start | bytes 1572872 | tf_op jit(solution)/shard_map/ppermute | solution.py:464
  51.8 14.2 %all-to-all-start.1 = ((f32[32,16,128]{2,1,0:T(8,128)}), f32[32,16,128]{2,1,0:T(8,128)S(1)}, u32[]{:S(2)}, u32[]{:S(2)}) async-start(f32[32,16,128]{2,1,0:T(8,128)} %bitcast.4), calls=%async_computation.1 | async-start | bytes 524288 | tf_op jit(solution)/shard_map/all_to_all | solution.py:518
  57.6 63.7 %copy-start = (f32[32,512]{1,0:T(8,128)S(1)}, f32[32,512]{1,0:T(8,128)}, u32[]{:S(2)}) copy-start(f32[32,512]{1,0:T(8,128)} %kspace_ref.1) | copy-start | bytes 196612
  57.6 63.7 %copy-start.1 = (s32[32,512]{1,0:T(8,128)S(1)}, s32[32,512]{1,0:T(8,128)}, u32[]{:S(2)}) copy-start(s32[32,512]{1,0:T(8,128)} %mask_ref.1) | copy-start | bytes 196612
  66.8 23.9 %all-to-all-start.2 = ((f32[32,4,640]{2,1,0:T(4,128)}), f32[32,4,640]{2,1,0:T(4,128)S(1)}, u32[]{:S(2)}, u32[]{:S(2)}) async-start(f32[32,4,640]{2,1,0:T(4,128)} %bitcast.6), calls=%async_computation.2 | async-start | bytes 655360 | tf_op jit(solution)/shard_map/all_to_all | solution.py:518
  70.0 1.3 collective-permute-start.13
  71.3 5.4 %collective-permute-start.16 = (f32[64,128]{1,0:T(8,128)S(1)}, f32[64,128]{1,0:T(8,128)S(1)}, u32[]{:S(2)}, u32[]{:S(2)}) collective-permute-start(f32[64,128]{1,0:T(8,128)S(1)} %add.42), channel_id=1, source_target_pairs={{0,6},{1,7},{2,4},{3,5},{4,2},{5,3},{6,0},{7,1},{8,14},{9,15},{10,... | collective-permute-start | bytes 98312 | tf_op jit(solution)/shard_map/ppermute | solution.py:464
  73.9 3.9 %collective-permute-start.15 = (f32[64,128]{1,0:T(8,128)S(1)}, f32[64,128]{1,0:T(8,128)S(1)}, u32[]{:S(2)}, u32[]{:S(2)}) collective-permute-start(f32[64,128]{1,0:T(8,128)S(1)} %add.42), channel_id=1, source_target_pairs={{0,4},{1,5},{2,6},{3,7},{4,0},{5,1},{6,2},{7,3},{8,12},{9,13},{10,... | collective-permute-start | bytes 98312 | tf_op jit(solution)/shard_map/ppermute | solution.py:464
  74.4 4.3 %collective-permute-start.14 = (f32[64,128]{1,0:T(8,128)S(1)}, f32[64,128]{1,0:T(8,128)S(1)}, u32[]{:S(2)}, u32[]{:S(2)}) collective-permute-start(f32[64,128]{1,0:T(8,128)S(1)} %add.42), channel_id=1, source_target_pairs={{0,2},{1,3},{2,0},{3,1},{4,6},{5,7},{6,4},{7,5},{8,10},{9,11},{10,... | collective-permute-start | bytes 98312 | tf_op jit(solution)/shard_map/ppermute | solution.py:464
  78.8 7.7 %collective-permute-start.19 = (f32[64,128]{1,0:T(8,128)S(1)}, f32[64,128]{1,0:T(8,128)S(1)}, u32[]{:S(2)}, u32[]{:S(2)}) collective-permute-start(f32[64,128]{1,0:T(8,128)S(1)} %add_add_fusion.3), channel_id=1, source_target_pairs={{0,24},{1,25},{2,26},{3,27},{4,28},{5,29},{6,30},{7,31},{8,16},{9,... | collective-permute-start | bytes 98312 | tf_op jit(solution)/shard_map/ppermute | solution.py:464
  82.0 8.6 %collective-permute-start.18 = (f32[64,128]{1,0:T(8,128)S(1)}, f32[64,128]{1,0:T(8,128)S(1)}, u32[]{:S(2)}, u32[]{:S(2)}) collective-permute-start(f32[64,128]{1,0:T(8,128)S(1)} %add_add_fusion.3), channel_id=1, source_target_pairs={{0,16},{1,17},{2,18},{3,19},{4,20},{5,21},{6,22},{7,23},{8,24},{9,... | collective-permute-start | bytes 98312 | tf_op jit(solution)/shard_map/ppermute | solution.py:464
  82.1 8.6 %collective-permute-start.17 = (f32[64,128]{1,0:T(8,128)S(1)}, f32[64,128]{1,0:T(8,128)S(1)}, u32[]{:S(2)}, u32[]{:S(2)}) collective-permute-start(f32[64,128]{1,0:T(8,128)S(1)} %add_add_fusion.3), channel_id=1, source_target_pairs={{0,8},{1,9},{2,10},{3,11},{4,12},{5,13},{6,14},{7,15},{8,0},{9,1},... | collective-permute-start | bytes 98312 | tf_op jit(solution)/shard_map/ppermute | solution.py:464
  83.2 8.3 %collective-permute-start.11 = (f32[1,256,128]{2,1,0:T(8,128)S(1)}, f32[1,256,128]{2,1,0:T(8,128)S(1)}, u32[]{:S(2)}, u32[]{:S(2)}) collective-permute-start(f32[1,256,128]{2,1,0:T(8,128)S(1)} %bitcast.11), channel_id=1, source_target_pairs={{0,24},{4,28},{8,16},{12,20},{16,8},{20,12},{24,0},{28,4},{1,25},{... | collective-permute-start | bytes 393224 | tf_op jit(solution)/shard_map/ppermute | solution.py:464
  86.4 10.3 %collective-permute-start.10 = (f32[1,256,128]{2,1,0:T(8,128)S(1)}, f32[1,256,128]{2,1,0:T(8,128)S(1)}, u32[]{:S(2)}, u32[]{:S(2)}) collective-permute-start(f32[1,256,128]{2,1,0:T(8,128)S(1)} %bitcast.12), channel_id=1, source_target_pairs={{0,16},{4,20},{8,24},{12,28},{16,0},{20,4},{24,8},{28,12},{1,17},{... | collective-permute-start | bytes 393224 | tf_op jit(solution)/shard_map/ppermute | solution.py:464
  86.4 10.3 %collective-permute-start.9 = (f32[1,256,128]{2,1,0:T(8,128)S(1)}, f32[1,256,128]{2,1,0:T(8,128)S(1)}, u32[]{:S(2)}, u32[]{:S(2)}) collective-permute-start(f32[1,256,128]{2,1,0:T(8,128)S(1)} %bitcast.13), channel_id=1, source_target_pairs={{0,8},{4,12},{8,0},{12,4},{16,24},{20,28},{24,16},{28,20},{1,9},{5... | collective-permute-start | bytes 393224 | tf_op jit(solution)/shard_map/ppermute | solution.py:464
  90.6 6.2 %collective-permute-start.20 = (f32[64,128]{1,0:T(8,128)S(1)}, f32[64,128]{1,0:T(8,128)S(1)}, u32[]{:S(2)}, u32[]{:S(2)}) collective-permute-start(f32[64,128]{1,0:T(8,128)S(1)} %add_add_fusion.2.gram_ref), channel_id=1, source_target_pairs={{0,1},{1,0},{2,3},{3,2},{4,5},{5,4},{6,7},{7,6},{8,9},{9,8},{10,11... | collective-permute-start | bytes 98312 | tf_op jit(solution)/shard_map/ppermute | solution.py:464
  103.3 1.3 collective-permute-start.21
  104.6 4.9 %collective-permute-start.24 = (f32[64,128]{1,0:T(8,128)S(1)}, f32[64,128]{1,0:T(8,128)S(1)}, u32[]{:S(2)}, u32[]{:S(2)}) collective-permute-start(f32[64,128]{1,0:T(8,128)S(1)} %add.49), channel_id=1, source_target_pairs={{0,6},{1,7},{2,4},{3,5},{4,2},{5,3},{6,0},{7,1},{8,14},{9,15},{10,... | collective-permute-start | bytes 98312 | tf_op jit(solution)/shard_map/ppermute | solution.py:464
  105.8 3.9 %collective-permute-start.23 = (f32[64,128]{1,0:T(8,128)S(1)}, f32[64,128]{1,0:T(8,128)S(1)}, u32[]{:S(2)}, u32[]{:S(2)}) collective-permute-start(f32[64,128]{1,0:T(8,128)S(1)} %add.49), channel_id=1, source_target_pairs={{0,4},{1,5},{2,6},{3,7},{4,0},{5,1},{6,2},{7,3},{8,12},{9,13},{10,... | collective-permute-start | bytes 98312 | tf_op jit(solution)/shard_map/ppermute | solution.py:464
  106.8 3.9 %collective-permute-start.22 = (f32[64,128]{1,0:T(8,128)S(1)}, f32[64,128]{1,0:T(8,128)S(1)}, u32[]{:S(2)}, u32[]{:S(2)}) collective-permute-start(f32[64,128]{1,0:T(8,128)S(1)} %add.49), channel_id=1, source_target_pairs={{0,2},{1,3},{2,0},{3,1},{4,6},{5,7},{6,4},{7,5},{8,10},{9,11},{10,... | collective-permute-start | bytes 98312 | tf_op jit(solution)/shard_map/ppermute | solution.py:464
  108.1 13.2 %collective-permute-start.12 = (f32[4,256,128]{2,1,0:T(8,128)S(1)}, f32[4,256,128]{2,1,0:T(8,128)S(1)}, u32[]{:S(2)}, u32[]{:S(2)}) collective-permute-start(f32[4,256,128]{2,1,0:T(8,128)S(1)} %pad_maximum_fusion.near_ref), channel_id=1, source_target_pairs={{0,4},{4,0},{8,12},{12,8},{16,20},{20,16},{24,28},{28,24},{1,5},{5... | collective-permute-start | bytes 1572872 | tf_op jit(solution)/shard_map/ppermute | solution.py:464
  110.7 5.8 %collective-permute-start.27 = (f32[64,128]{1,0:T(8,128)S(1)}, f32[64,128]{1,0:T(8,128)S(1)}, u32[]{:S(2)}, u32[]{:S(2)}) collective-permute-start(f32[64,128]{1,0:T(8,128)S(1)} %add_add_fusion.1), channel_id=1, source_target_pairs={{0,24},{1,25},{2,26},{3,27},{4,28},{5,29},{6,30},{7,31},{8,16},{9,... | collective-permute-start | bytes 98312 | tf_op jit(solution)/shard_map/ppermute | solution.py:464
  113.1 4.8 %collective-permute-start.26 = (f32[64,128]{1,0:T(8,128)S(1)}, f32[64,128]{1,0:T(8,128)S(1)}, u32[]{:S(2)}, u32[]{:S(2)}) collective-permute-start(f32[64,128]{1,0:T(8,128)S(1)} %add_add_fusion.1), channel_id=1, source_target_pairs={{0,16},{1,17},{2,18},{3,19},{4,20},{5,21},{6,22},{7,23},{8,24},{9,... | collective-permute-start | bytes 98312 | tf_op jit(solution)/shard_map/ppermute | solution.py:464
  113.1 4.8 %collective-permute-start.25 = (f32[64,128]{1,0:T(8,128)S(1)}, f32[64,128]{1,0:T(8,128)S(1)}, u32[]{:S(2)}, u32[]{:S(2)}) collective-permute-start(f32[64,128]{1,0:T(8,128)S(1)} %add_add_fusion.1), channel_id=1, source_target_pairs={{0,8},{1,9},{2,10},{3,11},{4,12},{5,13},{6,14},{7,15},{8,0},{9,1},... | collective-permute-start | bytes 98312 | tf_op jit(solution)/shard_map/ppermute | solution.py:464
  117.9 1.3 collective-permute-start.28

commit v4 on v3

--- a/solution.py
+++ b/solution.py
@@ -304,23 +304,42 @@
     )
 
 
-def store_halves(gram, kept_ref, given_ref):
-    half = gram.shape[0] // 2
+def square(size):
+    at_row = lax.broadcasted_iota(jnp.int32, (size, size), 0)
+    at_col = lax.broadcasted_iota(jnp.int32, (size, size), 1)
+    return at_row, at_col
+
+
+def gram_kernel(cols, per_tile, received_ref, kept_ref, given_ref, rows_ref):
+    turned = gather_turned(received_ref, cols, per_tile, 0)
+    first = exact(turned, turned, ((1,), (1,)))
+    turned = gather_turned(received_ref, cols, per_tile, 1)
+    second = exact(turned, turned, ((1,), (1,)))
+    rows_ref[...] = turned.T
+    at_row, at_col = square(first.shape[0])
+    packed = jnp.where(at_row >= at_col, first, second)
+    line = jnp.sum(jnp.where(at_row == at_col, second, 0.0), axis=0, keepdims=True)
+    line = jnp.broadcast_to(line, (SUB, line.shape[1]))
+    half = packed.shape[0] // 2
     odd = lax.axis_index("coil") % 2 == 1
-    kept_ref[...] = jnp.where(odd, gram[half:], gram[:half])
-    given_ref[...] = jnp.where(odd, gram[:half], gram[half:])
-
-
-def load_halves(kept_ref, other_ref):
+    kept_ref[:half] = jnp.where(odd, packed[half:], packed[:half])
+    given_ref[:half] = jnp.where(odd, packed[:half], packed[half:])
+    kept_ref[half:] = line
+    given_ref[half:] = line
+
+
+def load_grams(kept_ref, other_ref):
     odd = lax.axis_index("coil") % 2 == 1
     kept, other = kept_ref[...], other_ref[...]
-    return jnp.concatenate([jnp.where(odd, other, kept), jnp.where(odd, kept, other)], axis=0)
-
-
-def gram_kernel(cols, per_tile, received_ref, kept_ref, given_ref, rows_ref):
-    turned = gather_turned(received_ref, cols, per_tile, 0)
-    store_halves(exact(turned, turned, ((1,), (1,))), kept_ref, given_ref)
-    rows_ref[...] = gather_turned(received_ref, cols, per_tile, 1).T
+    low, high = jnp.where(odd, other, kept), jnp.where(odd, kept, other)
+    half = low.shape[0] - SUB
+    packed = jnp.concatenate([low[:half], high[:half]], axis=0)
+    line = low[half : half + 1]
+    at_row, at_col = square(packed.shape[0])
+    turned = packed.T
+    first = jnp.where(at_row >= at_col, packed, turned)
+    second = jnp.where(at_row > at_col, turned, packed)
+    return first, jnp.where(at_row == at_col, line, second), line
 
 
 def inverse_factor(gram):
@@ -393,70 +412,84 @@
     return jnp.concatenate(done, axis=0)
 
 
-def middle_kernel(gram_ref, other_ref, rows_ref, inverse_ref, kept_ref, given_ref):
-    inverse = inverse_factor(load_halves(gram_ref, other_ref))
-    inverse_ref[...] = inverse
-    rows = exact(rows_ref[...], inverse, ((1,), (1,)))
-    store_halves(exact(rows, rows, ((0,), (0,))), kept_ref, given_ref)
+def factors_kernel(gram_ref, other_ref, first_ref, both_ref, sound_ref):
+    gram, raw, line = load_grams(gram_ref, other_ref)
+    inverse = inverse_factor(gram)
+    first_ref[...] = inverse
+    gram = exact(exact(inverse, raw), inverse, ((1,), (1,)))
+    both_ref[...] = exact(inverse_factor(gram), inverse)
+    at_row, at_col = square(gram.shape[0])
+    terms = jnp.sum(inverse * inverse * line, axis=1, keepdims=True)
+    result = jnp.sum(jnp.where(at_row == at_col, gram, 0.0), axis=1, keepdims=True)
+    worst = jnp.max(jnp.where(terms <= 64.0 * result, 0, 1))
+    sound_ref[0] = 1 - worst
+
+
+def rows_kernel(rows_ref, inverse_ref, gram_ref):
+    rows = exact(rows_ref[...], inverse_ref[...], ((1,), (1,)))
+    gram_ref[...] = exact(rows, rows, ((0,), (0,)))
+
+
+def again_kernel(gram_ref, inverse_ref, both_ref):
+    both_ref[...] = exact(inverse_factor(gram_ref[...]), inverse_ref[...])
 
 
 def last_kernel(
     cols,
-    masks,
+    per_tile,
+    parts,
     images_ref,
-    near_ref,
-    far_ref,
-    first_ref,
-    gram_ref,
-    other_ref,
+    both_ref,
     kspace_ref,
     mask_ref,
-    recovered_ref,
-    basis_ref,
+    *refs,
 ):
-    inverse = inverse_factor(load_halves(gram_ref, other_ref))
+    recovered_ref, basis_ref = refs[-2:]
+    both = both_ref[...]
     count, reach = images_ref.shape
     devices = count // cols
-    at_row = lax.broadcasted_iota(jnp.int32, (count, count), 0)
-    at_col = lax.broadcasted_iota(jnp.int32, (count, count), 1)
+    at_row, at_col = square(count)
     order = ((at_row // devices == at_col % cols) & (at_row % devices == at_col // cols)).astype(
         jnp.float32
     )
-    inverse = exact(inverse, first_ref[...])
-    images = exact(exact(inverse, order), images_ref[...])
+    images = exact(exact(both, order), images_ref[...])
     images_high, images_low = split(images)
     stacked = jnp.concatenate([images_high, images_low], axis=0)
     chg, tile = kspace_ref.shape
     me = lax.axis_index("rows")
-    half = near_ref.shape[0]
     estimate = jnp.zeros((chg, tile), jnp.float32)
-    for slot, mask in enumerate(masks):
-        rows = near_ref[slot] if slot < half else far_ref[slot - half]
-        vectors = dot3(rows, inverse, ((1,), (1,)))
-        if slot == 0:
-            basis_ref[...] = vectors
+    for (start, masks), rows_ref in zip(parts, refs):
+        blocks, owned, rank = rows_ref.shape
+        vectors = dot3(rows_ref[...].reshape(blocks * owned, rank), both, ((1,), (1,)))
+        if masks[0] == 0:
+            basis_ref[start * chg : start * chg + owned] = vectors[:owned]
         high, low = split(vectors)
         projected = dot(jnp.concatenate([high, high], axis=1), stacked) + dot(low, images_high)
-        per_tile = vectors.shape[0] // chg
-        total = projected[:chg]
-        for j in range(1, per_tile):
-            total = total + pltpu.roll(projected[j * chg : (j + 1) * chg], j, 1)
-        t = lax.bitwise_xor(me, mask)
-        total = pltpu.roll(total, t * per_tile, 1)
-        estimate = estimate + total[:, reach - tile :]
+        for slot, mask in enumerate(masks):
+            total = None
+            for j in range(owned // chg):
+                part = projected[slot * owned + j * chg : slot * owned + (j + 1) * chg]
+                part = pltpu.roll(part, start + j, 1) if start + j else part
+                total = part if total is None else total + part
+            total = pltpu.roll(total, lax.bitwise_xor(me, mask) * per_tile, 1)
+            estimate = estimate + total[:, reach - tile :]
     estimate = estimate / KER
     residual = mask_ref[...].astype(jnp.float32) * (kspace_ref[...] - estimate)
     recovered_ref[...] = estimate + residual - jnp.clip(residual, -threshold, threshold)
 
 
-def call(kernel, outs, *args, scratch=(), space=pltpu.VMEM, limit=40):
+def call(kernel, outs, *args, scratch=(), space=pltpu.VMEM, limit=40, scalars=0, micros=1):
     return pl.pallas_call(
         kernel,
         out_shape=[jax.ShapeDtypeStruct(shape, kind) for shape, kind in outs],
         in_specs=[pl.BlockSpec(memory_space=space)] * len(args),
-        out_specs=[pl.BlockSpec(memory_space=pltpu.VMEM)] * len(outs),
+        out_specs=[pl.BlockSpec(memory_space=pltpu.VMEM)] * (len(outs) - scalars)
+        + [pl.BlockSpec(memory_space=pltpu.SMEM)] * scalars,
         scratch_shapes=list(scratch),
         compiler_params=pltpu.CompilerParams(vmem_limit_bytes=limit * 2**20),
+        cost_estimate=pl.CostEstimate(
+            flops=micros * 10**9, bytes_accessed=0, transcendentals=0
+        ),
     )(*args)
 
 
@@ -495,6 +528,7 @@
     near, masks = sampled[None], [0]
     for partners in rounds_of(2 * groups, devices):
         near, masks = gather_round(near, masks, partners, devices, AXES)
+    near = after(near, beside)
     half = near.shape[1] // 2
     parts = [near[:, :half], near[:, half:]]
     orders = [masks, masks]
@@ -504,8 +538,6 @@
             parts[i], orders[i] = gather_round(
                 parts[i], orders[i], [ways[i][step]], devices, AXES
             )
-        if step == 0:
-            parts = list(lax.optimization_barrier((*parts, beside))[:2])
     for partners in rounds_of(2, groups // 2):
         for i in range(2):
             parts[i], orders[i] = gather_round(parts[i], orders[i], partners, devices, AXES)
@@ -514,6 +546,26 @@
     return parts, far, orders
 
 
+def gather_rows(by_row, tiles, per_tile):
+    half = by_row.shape[0] // 2
+    near, order = by_row[None, :half], [0]
+    for partners in rounds_of(2, tiles):
+        near, order = gather_round(near, order, partners, tiles, "rows")
+    parts = [(0, order), (0, [m ^ 1 for m in order])]
+    pieces = [near, exchange(near, tiles, 1, "rows")]
+    near, order = gather_round(by_row[None, half:], [0], [1], tiles, "rows")
+    *early, late = rounds_of(2, tiles)
+    for partners in early:
+        near, order = gather_round(near, order, partners, tiles, "rows")
+    start = per_tile // 2
+    parts.append((start, order))
+    pieces.append(near)
+    for mask in late:
+        parts.append((start, [m ^ mask for m in order]))
+        pieces.append(exchange(near, tiles, mask, "rows"))
+    return parts, pieces
+
+
 def to_all(pieces, axes=AXES):
     return lax.all_to_all(pieces, axes, 0, 0, tiled=True)
 
@@ -522,8 +574,9 @@
     total = kept + exchange(given, devices, 1, AXES)
     for partners in rounds_of(2, devices):
         terms = [exchange(total, devices, mask, AXES) for mask in partners]
-        for term in terms:
-            total = total + term
+        total = total + terms[0]
+        if len(terms) == 3:
+            total = total + (terms[1] + terms[2])
     return total, exchange(total, devices, 1, AXES)
 
 
@@ -572,13 +625,14 @@
         far[1],
         basis_parts.reshape(tiles, groups, per_tile, lanes),
         scratch=[wide, moved],
+        micros=12,
     )
     received = to_all(send.reshape(devices, 2 * per_tile, lanes))
     reach = tile + LANES
-    (images,) = call(images_kernel, [((tiles, cols, reach), f32)], samples, normal, scratch=[wide])
+    (images,) = call(images_kernel, [((tiles, cols, reach), f32)], samples, normal, scratch=[wide], micros=2)
     images = jnp.broadcast_to(images[:, None], (tiles, groups, cols, reach))
     received = after(received, images)
-    half = ((rank // 2, rank), f32)
+    half = ((rank // 2 + SUB, rank), f32)
     kept, given, by_row = call(
         functools.partial(gram_kernel, cols, per_tile),
         [half, half, ((owned, rank), f32)],
@@ -586,26 +640,26 @@
     )
     gram = total_of(kept, given, devices)
     images = to_all(images.reshape(devices, cols, reach)).reshape(rank, reach)
-    near, order = by_row[None], [0]
-    for partners in rounds_of(2, tiles):
-        near, order = gather_round(near, order, partners, tiles, "rows")
-    by_row, images, near = lax.optimization_barrier((by_row, images, near))
-    far = exchange(near, tiles, 1, "rows")
-    order = with_masks(order, 1)
-    inverse, kept, given = call(
-        middle_kernel, [((rank, rank), f32), half, half], *gram, by_row
-    )
-    gram = total_of(kept, given, devices)
+    parts, pieces = gather_rows(by_row, tiles, per_tile)
+    whole = ((rank, rank), f32)
+    first, both, sound = call(
+        factors_kernel, [whole, whole, ((1,), jnp.int32)], *gram, scalars=1, micros=12
+    )
+
+    def again():
+        (gram,) = call(rows_kernel, [whole], by_row, first)
+        return call(again_kernel, [whole], lax.psum(gram, AXES), first)[0]
+
+    both = lax.cond(sound[0] == 1, lambda: both, again)
     recovered, basis = call(
-        functools.partial(last_kernel, cols, order),
+        functools.partial(last_kernel, cols, per_tile, parts),
         [((chg, tile), f32), ((owned, rank), f32)],
         images,
-        near,
-        far,
-        inverse,
-        *gram,
+        both,
         kspace,
         sample_mask,
+        *pieces,
+        micros=5,
     )
     return (recovered, basis.reshape(1, owned, rank))
 
@@ -617,13 +671,13 @@
     owned, rank = start_basis.shape[1:]
     return (
         devices & (devices - 1) == 0
-        and tiles > 1
+        and tiles > 2
         and groups > 2
         and rank % (2 * SUB) == 0
         and rank % devices == 0
         and rank % LANES == 0
         and tile % LANES == 0
-        and owned % (SUB * chg) == 0
+        and owned == SUB * chg
         and chg * (rank // devices) == LANES
         and chg % (4 * SUB) == 0
         and (chg * groups) % LANES == 0

time: 132 us -> 127 us (0.962)
  waiting for transfers between devices: 51.2 us -> 26.5 us
  between operations: 0.85 us -> 14.9 us
  starting transfers between devices: 43.8 us -> 48.8 us
    ppermute x29 -> x25, waiting for transfers between devices: 41.5 us -> 18.2 us  [exchange(): return lax.ppermute(block, axes, [(i, i ^ mask) for i in range(devices)])]
    all_to_all x3, starting transfers between devices: 10.4 us -> 13.8 us  [to_all(): return lax.all_to_all(pieces, axes, 0, 0, tiled=True)]
    ppermute x29 -> x25, starting transfers between devices: 33.4 us -> 35 us  [exchange(): return lax.ppermute(block, axes, [(i, i ^ mask) for i in range(devices)])]
    all_to_all x3, waiting for transfers between devices: 9.72 us -> 8.29 us  [to_all(): return lax.all_to_all(pieces, axes, 0, 0, tiled=True)]
  transfers between devices with their start and end apart: 32 -> 28, of which waited for: 23 -> 9; matrix products, arithmetic and copies ran while one was open for 0% -> 1% of each run, Pallas kernels for 2% -> 12%
where the time goes in v4:
time: 127 us
  starting transfers between devices  48.8 us (38%)
  Pallas kernels  33.8 us (27%)
  waiting for transfers between devices  26.5 us (21%)
  between operations  14.9 us (12%)
  local copies, waits for them, and re-layouts  1.5 us (1%)
    ppermute x25, starting transfers between devices, exchange(): return lax.ppermute(block, axes, [(i, i ^ mask) for i in range(devices)])  35 us
    pallas_call x6, Pallas kernels, call(): pl.pallas_call(kernel, out_shape=[jax.ShapeDtypeStruct(shape, kind) for s...  33.8 us
    ppermute x25, waiting for transfers between devices, exchange(): return lax.ppermute(block, axes, [(i, i ^ mask) for i in range(devices)])  18.2 us
    all_to_all x3, starting transfers between devices, to_all(): return lax.all_to_all(pieces, axes, 0, 0, tiled=True)  13.8 us
    all_to_all x3, waiting for transfers between devices, to_all(): return lax.all_to_all(pieces, axes, 0, 0, tiled=True)  8.29 us
  transfers between devices with their start and end apart: 28, of which 9 were waited for; matrix products, arithmetic and copies ran while one was open for 1% of the time, Pallas kernels for 12%

profile of v4, /device:TPU:0, one launch (start us, length us, event | category | flops | bytes accessed | tf_op | source)
XLA Modules:
  0.0 126.8 jit_solution(13146651684747208465)
XLA Ops:
  7.2 1.9 %shard_map.50 = (f32[32,512]{1,0:T(8,128)}, f32[256,128]{1,0:T(8,128)}) custom-call(f32[32,512]{1,0:T(8,128)} %kspace_ref.1, s32[32,512]{1,0:T(8,128)} %mask_ref.1, f32[256,128]{1,0:T(8,128)} %bitcast.20), custom_call_target="tpu_custom_call" | custom-call | flops 1000000000 | tf_op jit(solution)/shard_map/pallas_call | solution.py:482
  9.1 7.3 %all-to-all-start = ((f32[32,8,128]{2,1,0:T(8,128)}), f32[32,8,128]{2,1,0:T(8,128)S(1)}, u32[]{:S(2)}, u32[]{:S(2)}) async-start(f32[32,8,128]{2,1,0:T(8,128)} %bitcast.15), calls=%async_computation | async-start | bytes 262144 | tf_op jit(solution)/shard_map/all_to_all | solution.py:570
  16.4 3.7 %collective-permute-start.2 = (f32[1,32,512]{2,1,0:T(8,128)}, f32[1,32,512]{2,1,0:T(8,128)S(1)}, u32[]{:S(2)}, u32[]{:S(2)}) collective-permute-start(f32[1,32,512]{2,1,0:T(8,128)} %bitcast.16), channel_id=1, source_target_pairs={{0,24},{1,25},{2,26},{3,27},{4,28},{5,29},{6,30},{7,31},{8,16},{9,... | collective-permute-start | bytes 196616 | tf_op jit(solution)/shard_map/ppermute | solution.py:497
  20.1 0.8 collective-permute-start
  20.8 4.2 %collective-permute-done.2 = f32[1,32,512]{2,1,0:T(8,128)S(1)} collective-permute-done((f32[1,32,512]{2,1,0:T(8,128)}, f32[1,32,512]{2,1,0:T(8,128)S(1)}, u32[]{:S(2)}, u32[]{:S(2)}) %collective-permute-start.2) | collective-permute-done | bytes 65568 | tf_op jit(solution)/shard_map/ppermute | solution.py:497
  25.1 3.5 %collective-permute-done.1 = f32[1,32,512]{2,1,0:T(8,128)S(1)} collective-permute-done((f32[1,32,512]{2,1,0:T(8,128)}, f32[1,32,512]{2,1,0:T(8,128)S(1)}, u32[]{:S(2)}, u32[]{:S(2)}) %collective-permute-start.1) | collective-permute-done | bytes 65568 | tf_op jit(solution)/shard_map/ppermute | solution.py:497
  28.6 0.9 pad_maximum_fusion.2
  29.5 1.5 %collective-permute-start.3 = (f32[4,16,512]{2,1,0:T(8,128)S(1)}, f32[4,16,512]{2,1,0:T(8,128)S(1)}, u32[]{:S(2)}, u32[]{:S(2)}) collective-permute-start(f32[4,16,512]{2,1,0:T(8,128)S(1)} %get-tuple-element.43), channel_id=1, source_target_pairs={{0,4},{1,5},{2,6},{3,7},{4,0},{5,1},{6,2},{7,3},{8,12},{9,13},{10,... | collective-permute-start | bytes 393224 | tf_op jit(solution)/shard_map/ppermute | solution.py:497
  31.0 1.5 %collective-permute-start.6 = (f32[4,16,512]{2,1,0:T(8,128)S(1)}, f32[4,16,512]{2,1,0:T(8,128)S(1)}, u32[]{:S(2)}, u32[]{:S(2)}) collective-permute-start(f32[4,16,512]{2,1,0:T(8,128)S(1)} %get-tuple-element.42), channel_id=1, source_target_pairs={{0,2},{1,3},{2,0},{3,1},{4,6},{5,7},{6,4},{7,5},{8,10},{9,11},{10,... | collective-permute-start | bytes 393224 | tf_op jit(solution)/shard_map/ppermute | solution.py:497
  32.5 2.1 %collective-permute-done.3 = f32[4,16,512]{2,1,0:T(8,128)S(1)} collective-permute-done((f32[4,16,512]{2,1,0:T(8,128)S(1)}, f32[4,16,512]{2,1,0:T(8,128)S(1)}, u32[]{:S(2)}, u32[]{:S(2)}) %collective-permute-start.3) | collective-permute-done | bytes 131104 | tf_op jit(solution)/shard_map/ppermute | solution.py:497
  34.6 1.5 %collective-permute-start.4 = (f32[8,16,512]{2,1,0:T(8,128)S(1)}, f32[8,16,512]{2,1,0:T(8,128)S(1)}, u32[]{:S(2)}, u32[]{:S(2)}) collective-permute-start(f32[8,16,512]{2,1,0:T(8,128)S(1)} %pad_maximum_fusion.3), channel_id=1, source_target_pairs={{0,2},{1,3},{2,0},{3,1},{4,6},{5,7},{6,4},{7,5},{8,10},{9,11},{10,... | collective-permute-start | bytes 786440 | tf_op jit(solution)/shard_map/ppermute | solution.py:497
  36.2 1.5 %collective-permute-start.7 = (f32[8,16,512]{2,1,0:T(8,128)S(1)}, f32[8,16,512]{2,1,0:T(8,128)S(1)}, u32[]{:S(2)}, u32[]{:S(2)}) collective-permute-start(f32[8,16,512]{2,1,0:T(8,128)S(1)} %pad_maximum_fusion.4), channel_id=1, source_target_pairs={{0,4},{1,5},{2,6},{3,7},{4,0},{5,1},{6,2},{7,3},{8,12},{9,13},{10,... | collective-permute-start | bytes 786440 | tf_op jit(solution)/shard_map/ppermute | solution.py:497
  37.7 3.9 %collective-permute-done.4 = f32[8,16,512]{2,1,0:T(8,128)S(1)} collective-permute-done((f32[8,16,512]{2,1,0:T(8,128)S(1)}, f32[8,16,512]{2,1,0:T(8,128)S(1)}, u32[]{:S(2)}, u32[]{:S(2)}) %collective-permute-start.4) | collective-permute-done | bytes 262176 | tf_op jit(solution)/shard_map/ppermute | solution.py:497
  41.7 0.1 collective-permute-start.5
  41.8 1.2 collective-permute-done.7
  43.0 0.1 collective-permute-start.8
  43.0 0.6 collective-permute-done.5.top_far_ref
  43.6 1.3 %collective-permute-done.8.low_far_ref = f32[16,16,512]{2,1,0:T(8,128)S(1)} collective-permute-done((f32[16,16,512]{2,1,0:T(8,128)S(1)}, f32[16,16,512]{2,1,0:T(8,128)S(1)}, u32[]{:S(2)}, u32[]{:S(2)}) %collective-permute-start.8) | collective-permute-done | bytes 524320 | tf_op jit(solution)/shard_map/ppermute | solution.py:497
  44.9 12.4 %shard_map.51 = (bf16[8,2,4,32,512]{4,3,2,1,0:T(8,128)(2,1)S(1)}, f32[256,128]{1,0:T(8,128)S(1)}, f32[8,4,2,8,128]{4,3,2,1,0:T(8,128)}) custom-call(f32[16,16,512]{2,1,0:T(8,128)S(1)} %pad_maximum_fusion.top_near_ref, f32[16,16,512]{2,1,0:T(8,128)S(1)} %collective-permute-done.5.top_far_ref, f32[16,16,512]{2,1,0:T(8,128)S(1)} %pad_maximum_fusion.1.low_near_ref, ...), custom_call_target="tpu_custom_call" | custom-call | flops 12000000000 | tf_op jit(solution)/shard_map/pallas_call | solution.py:482
  57.4 3.9 %all-to-all-start.2 = ((f32[32,16,128]{2,1,0:T(8,128)}), f32[32,16,128]{2,1,0:T(8,128)S(1)}, u32[]{:S(2)}, u32[]{:S(2)}) async-start(f32[32,16,128]{2,1,0:T(8,128)} %bitcast.5), calls=%async_computation.2 | async-start | bytes 524288 | tf_op jit(solution)/shard_map/all_to_all | solution.py:570
  61.3 2.1 %shard_map.52 = f32[8,4,640]{2,1,0:T(4,128)S(1)} custom-call(bf16[8,2,4,32,512]{4,3,2,1,0:T(8,128)(2,1)S(1)} %get-tuple-element.30.samples_ref, f32[256,128]{1,0:T(8,128)S(1)} %get-tuple-element.31.vectors_ref), custom_call_target="tpu_custom_call" | custom-call | flops 2000000000 | tf_op jit(solution)/shard_map/pallas_call | solution.py:482
  63.4 8.3 %all-to-all-done.2 = f32[32,16,128]{2,1,0:T(8,128)S(1)} async-done(((f32[32,16,128]{2,1,0:T(8,128)}), f32[32,16,128]{2,1,0:T(8,128)S(1)}, u32[]{:S(2)}, u32[]{:S(2)}) %all-to-all-start.2) | async-done | bytes 262176 | tf_op jit(solution)/shard_map/all_to_all | solution.py:570
  71.7 0.8 broadcast_in_dim.16
  72.5 0.6 shard_map.53
  73.1 0.1 collective-permute-start.9
  73.2 2.6 %all-to-all-start.1 = ((f32[32,4,640]{2,1,0:T(4,128)}), f32[32,4,640]{2,1,0:T(4,128)S(1)}, u32[]{:S(2)}, u32[]{:S(2)}) async-start(f32[32,4,640]{2,1,0:T(4,128)} %bitcast.4), calls=%async_computation.1 | async-start | bytes 655360 | tf_op jit(solution)/shard_map/all_to_all | solution.py:570
  75.8 2.6 %collective-permute-start.12 = (f32[72,128]{1,0:T(8,128)S(1)}, f32[72,128]{1,0:T(8,128)S(1)}, u32[]{:S(2)}, u32[]{:S(2)}) collective-permute-start(f32[72,128]{1,0:T(8,128)S(1)} %add.23), channel_id=1, source_target_pairs={{0,6},{1,7},{2,4},{3,5},{4,2},{5,3},{6,0},{7,1},{8,14},{9,15},{10,... | collective-permute-start | bytes 110600 | tf_op jit(solution)/shard_map/ppermute | solution.py:497
  78.5 0.6 collective-permute-start.11
  79.0 0.4 collective-permute-start.10
  79.4 3.7 %collective-permute-start.19 = (f32[1,128,128]{2,1,0:T(8,128)S(1)}, f32[1,128,128]{2,1,0:T(8,128)S(1)}, u32[]{:S(2)}, u32[]{:S(2)}) collective-permute-start(f32[1,128,128]{2,1,0:T(8,128)S(1)} %get-tuple-element.45), channel_id=1, source_target_pairs={{0,24},{4,28},{8,16},{12,20},{16,8},{20,12},{24,0},{28,4},{1,25},{... | collective-permute-start | bytes 196616 | tf_op jit(solution)/shard_map/ppermute | solution.py:497
  83.1 1.5 %collective-permute-start.21 = (f32[1,128,128]{2,1,0:T(8,128)S(1)}, f32[1,128,128]{2,1,0:T(8,128)S(1)}, u32[]{:S(2)}, u32[]{:S(2)}) collective-permute-start(f32[1,128,128]{2,1,0:T(8,128)S(1)} %get-tuple-element.44), channel_id=1, source_target_pairs={{0,4},{4,0},{8,12},{12,8},{16,20},{20,16},{24,28},{28,24},{1,5},{5... | collective-permute-start | bytes 196616 | tf_op jit(solution)/shard_map/ppermute | solution.py:497
  84.6 2.8 %collective-permute-start.15 = (f32[72,128]{1,0:T(8,128)S(1)}, f32[72,128]{1,0:T(8,128)S(1)}, u32[]{:S(2)}, u32[]{:S(2)}) collective-permute-start(f32[72,128]{1,0:T(8,128)S(1)} %add_add_fusion.1), channel_id=1, source_target_pairs={{0,24},{1,25},{2,26},{3,27},{4,28},{5,29},{6,30},{7,31},{8,16},{9,... | collective-permute-start | bytes 110600 | tf_op jit(solution)/shard_map/ppermute | solution.py:497
  87.4 0.2 collective-permute-start.14
  87.7 1.4 %collective-permute-start.13 = (f32[72,128]{1,0:T(8,128)S(1)}, f32[72,128]{1,0:T(8,128)S(1)}, u32[]{:S(2)}, u32[]{:S(2)}) collective-permute-start(f32[72,128]{1,0:T(8,128)S(1)} %add_add_fusion.1), channel_id=1, source_target_pairs={{0,8},{1,9},{2,10},{3,11},{4,12},{5,13},{6,14},{7,15},{8,0},{9,1},... | collective-permute-start | bytes 110600 | tf_op jit(solution)/shard_map/ppermute | solution.py:497
  89.1 1.4 %collective-permute-done.15 = f32[72,128]{1,0:T(8,128)S(1)} collective-permute-done((f32[72,128]{1,0:T(8,128)S(1)}, f32[72,128]{1,0:T(8,128)S(1)}, u32[]{:S(2)}, u32[]{:S(2)}) %collective-permute-start.15) | collective-permute-done | bytes 36896 | tf_op jit(solution)/shard_map/ppermute | solution.py:497
  90.4 5.1 %collective-permute-start.17 = (f32[1,128,128]{2,1,0:T(8,128)S(1)}, f32[1,128,128]{2,1,0:T(8,128)S(1)}, u32[]{:S(2)}, u32[]{:S(2)}) collective-permute-start(f32[1,128,128]{2,1,0:T(8,128)S(1)} %get-tuple-element.45), channel_id=1, source_target_pairs={{0,8},{4,12},{8,0},{12,4},{16,24},{20,28},{24,16},{28,20},{1,9},{5... | collective-permute-start | bytes 196616 | tf_op jit(solution)/shard_map/ppermute | solution.py:497
  95.5 1.1 collective-permute-start.24
  96.6 0.4 collective-permute-start.23
  97.0 3.0 %collective-permute-start.22 = (f32[2,128,128]{2,1,0:T(8,128)S(1)}, f32[2,128,128]{2,1,0:T(8,128)S(1)}, u32[]{:S(2)}, u32[]{:S(2)}) collective-permute-start(f32[2,128,128]{2,1,0:T(8,128)S(1)} %pad_maximum_fusion.6.refs_2_), channel_id=1, source_target_pairs={{0,8},{4,12},{8,0},{12,4},{16,24},{20,28},{24,16},{28,20},{1,9},{5... | collective-permute-start | bytes 393224 | tf_op jit(solution)/shard_map/ppermute | solution.py:497
  100.0 1.5 %collective-permute-start.20 = (f32[4,128,128]{2,1,0:T(8,128)S(1)}, f32[4,128,128]{2,1,0:T(8,128)S(1)}, u32[]{:S(2)}, u32[]{:S(2)}) collective-permute-start(f32[4,128,128]{2,1,0:T(8,128)S(1)} %pad_maximum_fusion.5.refs_0_), channel_id=1, source_target_pairs={{0,4},{4,0},{8,12},{12,8},{16,20},{20,16},{24,28},{28,24},{1,5},{5... | collective-permute-start | bytes 786440 | tf_op jit(solution)/shard_map/ppermute | solution.py:497
  101.6 0.1 reshape.37.images_ref
  101.7 12.6 %shard_map.54 = (f32[128,128]{1,0:T(8,128)S(1)}, f32[128,128]{1,0:T(8,128)S(1)}, s32[1]{0:T(128)}) custom-call(f32[72,128]{1,0:T(8,128)S(1)} %add_add_fusion.gram_ref, f32[72,128]{1,0:T(8,128)S(1)} %collective-permute-done.16.other_ref), custom_call_target="tpu_custom_call" | custom-call | flops 12000000000 | tf_op jit(solution)/shard_map/pallas_call | solution.py:482
  115.0 0.0 copy-start
  115.0 0.0 copy-start.1
  115.0 0.2 conditional.1
  115.3 0.5 copy-done
  115.8 0.0 copy-done.1
  115.9 4.1 %shard_map.55 = (f32[32,512]{1,0:T(8,128)}, f32[256,128]{1,0:T(8,128)}) custom-call(f32[128,640]{1,0:T(8,128)S(1)} %reshape.37.images_ref, f32[128,128]{1,0:T(8,128)S(1)} %get-tuple-element.46.both_ref, f32[32,512]{1,0:T(8,128)S(1)} %copy-done, s32[32,512]{1,0:T(8,128)S(1)} %copy-done.1, f32[4,128,128]{2,1,0:T(8,128)S(1)} %pad_maximum_fusion.5.refs_0_, ...), custom_call_target="tpu_custom_call" | custom-call | flops 5000000000 | tf_op jit(solution)/shard_map/pallas_call | solution.py:482
  (33 shorter events, 0.3 us)
Async XLA Ops:
  9.1 20.4 %all-to-all-start = ((f32[32,8,128]{2,1,0:T(8,128)}), f32[32,8,128]{2,1,0:T(8,128)S(1)}, u32[]{:S(2)}, u32[]{:S(2)}) async-start(f32[32,8,128]{2,1,0:T(8,128)} %bitcast.15), calls=%async_computation | async-start | bytes 262144 | tf_op jit(solution)/shard_map/all_to_all | solution.py:570
  16.4 8.7 %collective-permute-start.2 = (f32[1,32,512]{2,1,0:T(8,128)}, f32[1,32,512]{2,1,0:T(8,128)S(1)}, u32[]{:S(2)}, u32[]{:S(2)}) collective-permute-start(f32[1,32,512]{2,1,0:T(8,128)} %bitcast.16), channel_id=1, source_target_pairs={{0,24},{1,25},{2,26},{3,27},{4,28},{5,29},{6,30},{7,31},{8,16},{9,... | collective-permute-start | bytes 196616 | tf_op jit(solution)/shard_map/ppermute | solution.py:497
  20.1 8.5 %collective-permute-start.1 = (f32[1,32,512]{2,1,0:T(8,128)}, f32[1,32,512]{2,1,0:T(8,128)S(1)}, u32[]{:S(2)}, u32[]{:S(2)}) collective-permute-start(f32[1,32,512]{2,1,0:T(8,128)} %bitcast.17), channel_id=1, source_target_pairs={{0,16},{1,17},{2,18},{3,19},{4,20},{5,21},{6,22},{7,23},{8,24},{9,... | collective-permute-start | bytes 196616 | tf_op jit(solution)/shard_map/ppermute | solution.py:497
  20.1 8.5 %collective-permute-start = (f32[1,32,512]{2,1,0:T(8,128)}, f32[1,32,512]{2,1,0:T(8,128)S(1)}, u32[]{:S(2)}, u32[]{:S(2)}) collective-permute-start(f32[1,32,512]{2,1,0:T(8,128)} %bitcast.18), channel_id=1, source_target_pairs={{0,8},{1,9},{2,10},{3,11},{4,12},{5,13},{6,14},{7,15},{8,0},{9,1},... | collective-permute-start | bytes 196616 | tf_op jit(solution)/shard_map/ppermute | solution.py:497
  29.5 5.1 %collective-permute-start.3 = (f32[4,16,512]{2,1,0:T(8,128)S(1)}, f32[4,16,512]{2,1,0:T(8,128)S(1)}, u32[]{:S(2)}, u32[]{:S(2)}) collective-permute-start(f32[4,16,512]{2,1,0:T(8,128)S(1)} %get-tuple-element.43), channel_id=1, source_target_pairs={{0,4},{1,5},{2,6},{3,7},{4,0},{5,1},{6,2},{7,3},{8,12},{9,13},{10,... | collective-permute-start | bytes 393224 | tf_op jit(solution)/shard_map/ppermute | solution.py:497
  31.0 5.1 %collective-permute-start.6 = (f32[4,16,512]{2,1,0:T(8,128)S(1)}, f32[4,16,512]{2,1,0:T(8,128)S(1)}, u32[]{:S(2)}, u32[]{:S(2)}) collective-permute-start(f32[4,16,512]{2,1,0:T(8,128)S(1)} %get-tuple-element.42), channel_id=1, source_target_pairs={{0,2},{1,3},{2,0},{3,1},{4,6},{5,7},{6,4},{7,5},{8,10},{9,11},{10,... | collective-permute-start | bytes 393224 | tf_op jit(solution)/shard_map/ppermute | solution.py:497
  34.6 7.0 %collective-permute-start.4 = (f32[8,16,512]{2,1,0:T(8,128)S(1)}, f32[8,16,512]{2,1,0:T(8,128)S(1)}, u32[]{:S(2)}, u32[]{:S(2)}) collective-permute-start(f32[8,16,512]{2,1,0:T(8,128)S(1)} %pad_maximum_fusion.3), channel_id=1, source_target_pairs={{0,2},{1,3},{2,0},{3,1},{4,6},{5,7},{6,4},{7,5},{8,10},{9,11},{10,... | collective-permute-start | bytes 786440 | tf_op jit(solution)/shard_map/ppermute | solution.py:497
  36.2 6.7 %collective-permute-start.7 = (f32[8,16,512]{2,1,0:T(8,128)S(1)}, f32[8,16,512]{2,1,0:T(8,128)S(1)}, u32[]{:S(2)}, u32[]{:S(2)}) collective-permute-start(f32[8,16,512]{2,1,0:T(8,128)S(1)} %pad_maximum_fusion.4), channel_id=1, source_target_pairs={{0,4},{1,5},{2,6},{3,7},{4,0},{5,1},{6,2},{7,3},{8,12},{9,13},{10,... | collective-permute-start | bytes 786440 | tf_op jit(solution)/shard_map/ppermute | solution.py:497
  41.7 2.0 %collective-permute-start.5 = (f32[16,16,512]{2,1,0:T(8,128)S(1)}, f32[16,16,512]{2,1,0:T(8,128)S(1)}, u32[]{:S(2)}, u32[]{:S(2)}) collective-permute-start(f32[16,16,512]{2,1,0:T(8,128)S(1)} %pad_maximum_fusion.top_near_ref), channel_id=1, source_target_pairs={{0,1},{1,0},{2,3},{3,2},{4,5},{5,4},{6,7},{7,6},{8,9},{9,8},{10,11... | collective-permute-start | bytes 1572872 | tf_op jit(solution)/shard_map/ppermute | solution.py:497
  43.0 2.0 %collective-permute-start.8 = (f32[16,16,512]{2,1,0:T(8,128)S(1)}, f32[16,16,512]{2,1,0:T(8,128)S(1)}, u32[]{:S(2)}, u32[]{:S(2)}) collective-permute-start(f32[16,16,512]{2,1,0:T(8,128)S(1)} %pad_maximum_fusion.1.low_near_ref), channel_id=1, source_target_pairs={{0,1},{1,0},{2,3},{3,2},{4,5},{5,4},{6,7},{7,6},{8,9},{9,8},{10,11... | collective-permute-start | bytes 1572872 | tf_op jit(solution)/shard_map/ppermute | solution.py:497
  57.4 14.3 %all-to-all-start.2 = ((f32[32,16,128]{2,1,0:T(8,128)}), f32[32,16,128]{2,1,0:T(8,128)S(1)}, u32[]{:S(2)}, u32[]{:S(2)}) async-start(f32[32,16,128]{2,1,0:T(8,128)} %bitcast.5), calls=%async_computation.2 | async-start | bytes 524288 | tf_op jit(solution)/shard_map/all_to_all | solution.py:570
  73.1 2.7 %collective-permute-start.9 = (f32[72,128]{1,0:T(8,128)S(1)}, f32[72,128]{1,0:T(8,128)S(1)}, u32[]{:S(2)}, u32[]{:S(2)}) collective-permute-start(f32[72,128]{1,0:T(8,128)S(1)} %get-tuple-element.35), channel_id=1, source_target_pairs={{0,1},{1,0},{2,3},{3,2},{4,5},{5,4},{6,7},{7,6},{8,9},{9,8},{10,11... | collective-permute-start | bytes 110600 | tf_op jit(solution)/shard_map/ppermute | solution.py:497
  73.2 28.4 %all-to-all-start.1 = ((f32[32,4,640]{2,1,0:T(4,128)}), f32[32,4,640]{2,1,0:T(4,128)S(1)}, u32[]{:S(2)}, u32[]{:S(2)}) async-start(f32[32,4,640]{2,1,0:T(4,128)} %bitcast.4), calls=%async_computation.1 | async-start | bytes 655360 | tf_op jit(solution)/shard_map/all_to_all | solution.py:570
  75.8 7.3 %collective-permute-start.12 = (f32[72,128]{1,0:T(8,128)S(1)}, f32[72,128]{1,0:T(8,128)S(1)}, u32[]{:S(2)}, u32[]{:S(2)}) collective-permute-start(f32[72,128]{1,0:T(8,128)S(1)} %add.23), channel_id=1, source_target_pairs={{0,6},{1,7},{2,4},{3,5},{4,2},{5,3},{6,0},{7,1},{8,14},{9,15},{10,... | collective-permute-start | bytes 110600 | tf_op jit(solution)/shard_map/ppermute | solution.py:497
  78.5 6.1 %collective-permute-start.11 = (f32[72,128]{1,0:T(8,128)S(1)}, f32[72,128]{1,0:T(8,128)S(1)}, u32[]{:S(2)}, u32[]{:S(2)}) collective-permute-start(f32[72,128]{1,0:T(8,128)S(1)} %add.23), channel_id=1, source_target_pairs={{0,4},{1,5},{2,6},{3,7},{4,0},{5,1},{6,2},{7,3},{8,12},{9,13},{10,... | collective-permute-start | bytes 110600 | tf_op jit(solution)/shard_map/ppermute | solution.py:497
  79.0 5.5 %collective-permute-start.10 = (f32[72,128]{1,0:T(8,128)S(1)}, f32[72,128]{1,0:T(8,128)S(1)}, u32[]{:S(2)}, u32[]{:S(2)}) collective-permute-start(f32[72,128]{1,0:T(8,128)S(1)} %add.23), channel_id=1, source_target_pairs={{0,2},{1,3},{2,0},{3,1},{4,6},{5,7},{6,4},{7,5},{8,10},{9,11},{10,... | collective-permute-start | bytes 110600 | tf_op jit(solution)/shard_map/ppermute | solution.py:497
  79.4 17.6 %collective-permute-start.19 = (f32[1,128,128]{2,1,0:T(8,128)S(1)}, f32[1,128,128]{2,1,0:T(8,128)S(1)}, u32[]{:S(2)}, u32[]{:S(2)}) collective-permute-start(f32[1,128,128]{2,1,0:T(8,128)S(1)} %get-tuple-element.45), channel_id=1, source_target_pairs={{0,24},{4,28},{8,16},{12,20},{16,8},{20,12},{24,0},{28,4},{1,25},{... | collective-permute-start | bytes 196616 | tf_op jit(solution)/shard_map/ppermute | solution.py:497
  83.1 16.9 %collective-permute-start.18 = (f32[1,128,128]{2,1,0:T(8,128)S(1)}, f32[1,128,128]{2,1,0:T(8,128)S(1)}, u32[]{:S(2)}, u32[]{:S(2)}) collective-permute-start(f32[1,128,128]{2,1,0:T(8,128)S(1)} %get-tuple-element.45), channel_id=1, source_target_pairs={{0,16},{4,20},{8,24},{12,28},{16,0},{20,4},{24,8},{28,12},{1,17},{... | collective-permute-start | bytes 196616 | tf_op jit(solution)/shard_map/ppermute | solution.py:497
  83.1 4.6 %collective-permute-start.21 = (f32[1,128,128]{2,1,0:T(8,128)S(1)}, f32[1,128,128]{2,1,0:T(8,128)S(1)}, u32[]{:S(2)}, u32[]{:S(2)}) collective-permute-start(f32[1,128,128]{2,1,0:T(8,128)S(1)} %get-tuple-element.44), channel_id=1, source_target_pairs={{0,4},{4,0},{8,12},{12,8},{16,20},{20,16},{24,28},{28,24},{1,5},{5... | collective-permute-start | bytes 196616 | tf_op jit(solution)/shard_map/ppermute | solution.py:497
  84.6 5.9 %collective-permute-start.15 = (f32[72,128]{1,0:T(8,128)S(1)}, f32[72,128]{1,0:T(8,128)S(1)}, u32[]{:S(2)}, u32[]{:S(2)}) collective-permute-start(f32[72,128]{1,0:T(8,128)S(1)} %add_add_fusion.1), channel_id=1, source_target_pairs={{0,24},{1,25},{2,26},{3,27},{4,28},{5,29},{6,30},{7,31},{8,16},{9,... | collective-permute-start | bytes 110600 | tf_op jit(solution)/shard_map/ppermute | solution.py:497
  87.4 8.1 %collective-permute-start.14 = (f32[72,128]{1,0:T(8,128)S(1)}, f32[72,128]{1,0:T(8,128)S(1)}, u32[]{:S(2)}, u32[]{:S(2)}) collective-permute-start(f32[72,128]{1,0:T(8,128)S(1)} %add_add_fusion.1), channel_id=1, source_target_pairs={{0,16},{1,17},{2,18},{3,19},{4,20},{5,21},{6,22},{7,23},{8,24},{9,... | collective-permute-start | bytes 110600 | tf_op jit(solution)/shard_map/ppermute | solution.py:497
  87.7 9.0 %collective-permute-start.13 = (f32[72,128]{1,0:T(8,128)S(1)}, f32[72,128]{1,0:T(8,128)S(1)}, u32[]{:S(2)}, u32[]{:S(2)}) collective-permute-start(f32[72,128]{1,0:T(8,128)S(1)} %add_add_fusion.1), channel_id=1, source_target_pairs={{0,8},{1,9},{2,10},{3,11},{4,12},{5,13},{6,14},{7,15},{8,0},{9,1},... | collective-permute-start | bytes 110600 | tf_op jit(solution)/shard_map/ppermute | solution.py:497
  90.4 9.6 %collective-permute-start.17 = (f32[1,128,128]{2,1,0:T(8,128)S(1)}, f32[1,128,128]{2,1,0:T(8,128)S(1)}, u32[]{:S(2)}, u32[]{:S(2)}) collective-permute-start(f32[1,128,128]{2,1,0:T(8,128)S(1)} %get-tuple-element.45), channel_id=1, source_target_pairs={{0,8},{4,12},{8,0},{12,4},{16,24},{20,28},{24,16},{28,20},{1,9},{5... | collective-permute-start | bytes 196616 | tf_op jit(solution)/shard_map/ppermute | solution.py:497
  95.5 19.7 %collective-permute-start.24 = (f32[2,128,128]{2,1,0:T(8,128)S(1)}, f32[2,128,128]{2,1,0:T(8,128)S(1)}, u32[]{:S(2)}, u32[]{:S(2)}) collective-permute-start(f32[2,128,128]{2,1,0:T(8,128)S(1)} %pad_maximum_fusion.6.refs_2_), channel_id=1, source_target_pairs={{0,24},{4,28},{8,16},{12,20},{16,8},{20,12},{24,0},{28,4},{1,25},{... | collective-permute-start | bytes 393224 | tf_op jit(solution)/shard_map/ppermute | solution.py:497
  96.6 18.6 %collective-permute-start.23 = (f32[2,128,128]{2,1,0:T(8,128)S(1)}, f32[2,128,128]{2,1,0:T(8,128)S(1)}, u32[]{:S(2)}, u32[]{:S(2)}) collective-permute-start(f32[2,128,128]{2,1,0:T(8,128)S(1)} %pad_maximum_fusion.6.refs_2_), channel_id=1, source_target_pairs={{0,16},{4,20},{8,24},{12,28},{16,0},{20,4},{24,8},{28,12},{1,17},{... | collective-permute-start | bytes 393224 | tf_op jit(solution)/shard_map/ppermute | solution.py:497
  97.0 18.3 %collective-permute-start.22 = (f32[2,128,128]{2,1,0:T(8,128)S(1)}, f32[2,128,128]{2,1,0:T(8,128)S(1)}, u32[]{:S(2)}, u32[]{:S(2)}) collective-permute-start(f32[2,128,128]{2,1,0:T(8,128)S(1)} %pad_maximum_fusion.6.refs_2_), channel_id=1, source_target_pairs={{0,8},{4,12},{8,0},{12,4},{16,24},{20,28},{24,16},{28,20},{1,9},{5... | collective-permute-start | bytes 393224 | tf_op jit(solution)/shard_map/ppermute | solution.py:497
  100.0 1.7 %collective-permute-start.16 = (f32[72,128]{1,0:T(8,128)S(1)}, f32[72,128]{1,0:T(8,128)S(1)}, u32[]{:S(2)}, u32[]{:S(2)}) collective-permute-start(f32[72,128]{1,0:T(8,128)S(1)} %add_add_fusion.gram_ref), channel_id=1, source_target_pairs={{0,1},{1,0},{2,3},{3,2},{4,5},{5,4},{6,7},{7,6},{8,9},{9,8},{10,11... | collective-permute-start | bytes 110600 | tf_op jit(solution)/shard_map/ppermute | solution.py:497
  100.0 15.2 %collective-permute-start.20 = (f32[4,128,128]{2,1,0:T(8,128)S(1)}, f32[4,128,128]{2,1,0:T(8,128)S(1)}, u32[]{:S(2)}, u32[]{:S(2)}) collective-permute-start(f32[4,128,128]{2,1,0:T(8,128)S(1)} %pad_maximum_fusion.5.refs_0_), channel_id=1, source_target_pairs={{0,4},{4,0},{8,12},{12,8},{16,20},{20,16},{24,28},{28,24},{1,5},{5... | collective-permute-start | bytes 786440 | tf_op jit(solution)/shard_map/ppermute | solution.py:497
  115.0 0.8 copy-start
  115.0 0.9 copy-start.1

commit v5 on v4

--- a/solution.py
+++ b/solution.py
@@ -648,7 +648,11 @@
 
     def again():
         (gram,) = call(rows_kernel, [whole], by_row, first)
-        return call(again_kernel, [whole], lax.psum(gram, AXES), first)[0]
+        mask = 1
+        while mask < devices:
+            gram = gram + exchange(gram, devices, mask, AXES)
+            mask *= 2
+        return call(again_kernel, [whole], gram, first)[0]
 
     both = lax.cond(sound[0] == 1, lambda: both, again)
     recovered, basis = call(

time: 127 us -> 114 us (0.90)
  between operations: 14.9 us -> 1.53 us
  transfers between devices with their start and end apart: 28 -> 28, of which waited for: 9 -> 9; matrix products, arithmetic and copies ran while one was open for 1% -> 1% of each run, Pallas kernels for 12% -> 13%
where the time goes in v5:
time: 114 us; the launch traced here: 113 us
  starting transfers between devices  48.8 us (43%)
  Pallas kernels  33.8 us (30%)
  waiting for transfers between devices  26.5 us (23%)
  between operations  1.53 us (1%)
  local copies, waits for them, and re-layouts  1.48 us (1%)
    ppermute x25, starting transfers between devices, exchange(): return lax.ppermute(block, axes, [(i, i ^ mask) for i in range(devices)])  35 us
    pallas_call x6, Pallas kernels, call(): pl.pallas_call(kernel, out_shape=[jax.ShapeDtypeStruct(shape, kind) for s...  33.8 us
    ppermute x25, waiting for transfers between devices, exchange(): return lax.ppermute(block, axes, [(i, i ^ mask) for i in range(devices)])  18.2 us
    all_to_all x3, starting transfers between devices, to_all(): return lax.all_to_all(pieces, axes, 0, 0, tiled=True)  13.8 us
    all_to_all x3, waiting for transfers between devices, to_all(): return lax.all_to_all(pieces, axes, 0, 0, tiled=True)  8.3 us
  transfers between devices with their start and end apart: 28, of which 9 were waited for; matrix products, arithmetic and copies ran while one was open for 1% of the time, Pallas kernels for 13%

profile of v5, /device:TPU:0, one launch (start us, length us, event | category | flops | bytes accessed | tf_op | source)
XLA Modules:
  0.0 113.5 jit_solution(17040543935311858364)
XLA Ops:
  0.6 1.9 %shard_map.50 = (f32[32,512]{1,0:T(8,128)}, f32[256,128]{1,0:T(8,128)}) custom-call(f32[32,512]{1,0:T(8,128)} %kspace_ref.1, s32[32,512]{1,0:T(8,128)} %mask_ref.1, f32[256,128]{1,0:T(8,128)} %bitcast.20), custom_call_target="tpu_custom_call" | custom-call | flops 1000000000 | tf_op jit(solution)/shard_map/pallas_call | solution.py:482
  2.5 7.3 %all-to-all-start = ((f32[32,8,128]{2,1,0:T(8,128)}), f32[32,8,128]{2,1,0:T(8,128)S(1)}, u32[]{:S(2)}, u32[]{:S(2)}) async-start(f32[32,8,128]{2,1,0:T(8,128)} %bitcast.15), calls=%async_computation | async-start | bytes 262144 | tf_op jit(solution)/shard_map/all_to_all | solution.py:570
  9.8 3.7 %collective-permute-start.7 = (f32[1,32,512]{2,1,0:T(8,128)}, f32[1,32,512]{2,1,0:T(8,128)S(1)}, u32[]{:S(2)}, u32[]{:S(2)}) collective-permute-start(f32[1,32,512]{2,1,0:T(8,128)} %bitcast.16), channel_id=1, source_target_pairs={{0,24},{1,25},{2,26},{3,27},{4,28},{5,29},{6,30},{7,31},{8,16},{9,... | collective-permute-start | bytes 196616 | tf_op jit(solution)/shard_map/ppermute | solution.py:497
  13.5 0.8 collective-permute-start.5
  14.3 4.2 %collective-permute-done.7 = f32[1,32,512]{2,1,0:T(8,128)S(1)} collective-permute-done((f32[1,32,512]{2,1,0:T(8,128)}, f32[1,32,512]{2,1,0:T(8,128)S(1)}, u32[]{:S(2)}, u32[]{:S(2)}) %collective-permute-start.7) | collective-permute-done | bytes 65568 | tf_op jit(solution)/shard_map/ppermute | solution.py:497
  18.5 3.5 %collective-permute-done.6 = f32[1,32,512]{2,1,0:T(8,128)S(1)} collective-permute-done((f32[1,32,512]{2,1,0:T(8,128)}, f32[1,32,512]{2,1,0:T(8,128)S(1)}, u32[]{:S(2)}, u32[]{:S(2)}) %collective-permute-start.6) | collective-permute-done | bytes 65568 | tf_op jit(solution)/shard_map/ppermute | solution.py:497
  22.0 0.9 pad_maximum_fusion.2
  22.9 1.5 %collective-permute-start.8 = (f32[4,16,512]{2,1,0:T(8,128)S(1)}, f32[4,16,512]{2,1,0:T(8,128)S(1)}, u32[]{:S(2)}, u32[]{:S(2)}) collective-permute-start(f32[4,16,512]{2,1,0:T(8,128)S(1)} %get-tuple-element.43), channel_id=1, source_target_pairs={{0,4},{1,5},{2,6},{3,7},{4,0},{5,1},{6,2},{7,3},{8,12},{9,13},{10,... | collective-permute-start | bytes 393224 | tf_op jit(solution)/shard_map/ppermute | solution.py:497
  24.5 1.5 %collective-permute-start.11 = (f32[4,16,512]{2,1,0:T(8,128)S(1)}, f32[4,16,512]{2,1,0:T(8,128)S(1)}, u32[]{:S(2)}, u32[]{:S(2)}) collective-permute-start(f32[4,16,512]{2,1,0:T(8,128)S(1)} %get-tuple-element.42), channel_id=1, source_target_pairs={{0,2},{1,3},{2,0},{3,1},{4,6},{5,7},{6,4},{7,5},{8,10},{9,11},{10,... | collective-permute-start | bytes 393224 | tf_op jit(solution)/shard_map/ppermute | solution.py:497
  26.0 2.1 %collective-permute-done.8 = f32[4,16,512]{2,1,0:T(8,128)S(1)} collective-permute-done((f32[4,16,512]{2,1,0:T(8,128)S(1)}, f32[4,16,512]{2,1,0:T(8,128)S(1)}, u32[]{:S(2)}, u32[]{:S(2)}) %collective-permute-start.8) | collective-permute-done | bytes 131104 | tf_op jit(solution)/shard_map/ppermute | solution.py:497
  28.1 1.5 %collective-permute-start.9 = (f32[8,16,512]{2,1,0:T(8,128)S(1)}, f32[8,16,512]{2,1,0:T(8,128)S(1)}, u32[]{:S(2)}, u32[]{:S(2)}) collective-permute-start(f32[8,16,512]{2,1,0:T(8,128)S(1)} %pad_maximum_fusion.3), channel_id=1, source_target_pairs={{0,2},{1,3},{2,0},{3,1},{4,6},{5,7},{6,4},{7,5},{8,10},{9,11},{10,... | collective-permute-start | bytes 786440 | tf_op jit(solution)/shard_map/ppermute | solution.py:497
  29.6 1.5 %collective-permute-start.12 = (f32[8,16,512]{2,1,0:T(8,128)S(1)}, f32[8,16,512]{2,1,0:T(8,128)S(1)}, u32[]{:S(2)}, u32[]{:S(2)}) collective-permute-start(f32[8,16,512]{2,1,0:T(8,128)S(1)} %pad_maximum_fusion.4), channel_id=1, source_target_pairs={{0,4},{1,5},{2,6},{3,7},{4,0},{5,1},{6,2},{7,3},{8,12},{9,13},{10,... | collective-permute-start | bytes 786440 | tf_op jit(solution)/shard_map/ppermute | solution.py:497
  31.2 3.9 %collective-permute-done.9 = f32[8,16,512]{2,1,0:T(8,128)S(1)} collective-permute-done((f32[8,16,512]{2,1,0:T(8,128)S(1)}, f32[8,16,512]{2,1,0:T(8,128)S(1)}, u32[]{:S(2)}, u32[]{:S(2)}) %collective-permute-start.9) | collective-permute-done | bytes 262176 | tf_op jit(solution)/shard_map/ppermute | solution.py:497
  35.1 0.1 collective-permute-start.10
  35.2 1.2 %collective-permute-done.12 = f32[8,16,512]{2,1,0:T(8,128)S(1)} collective-permute-done((f32[8,16,512]{2,1,0:T(8,128)S(1)}, f32[8,16,512]{2,1,0:T(8,128)S(1)}, u32[]{:S(2)}, u32[]{:S(2)}) %collective-permute-start.12) | collective-permute-done | bytes 262176 | tf_op jit(solution)/shard_map/ppermute | solution.py:497
  36.4 0.1 collective-permute-start.13
  36.5 0.6 collective-permute-done.10.top_far_ref
  37.1 1.3 %collective-permute-done.13.low_far_ref = f32[16,16,512]{2,1,0:T(8,128)S(1)} collective-permute-done((f32[16,16,512]{2,1,0:T(8,128)S(1)}, f32[16,16,512]{2,1,0:T(8,128)S(1)}, u32[]{:S(2)}, u32[]{:S(2)}) %collective-permute-start.13) | collective-permute-done | bytes 524320 | tf_op jit(solution)/shard_map/ppermute | solution.py:497
  38.4 12.4 %shard_map.51 = (bf16[8,2,4,32,512]{4,3,2,1,0:T(8,128)(2,1)S(1)}, f32[256,128]{1,0:T(8,128)S(1)}, f32[8,4,2,8,128]{4,3,2,1,0:T(8,128)}) custom-call(f32[16,16,512]{2,1,0:T(8,128)S(1)} %pad_maximum_fusion.top_near_ref, f32[16,16,512]{2,1,0:T(8,128)S(1)} %collective-permute-done.10.top_far_ref, f32[16,16,512]{2,1,0:T(8,128)S(1)} %pad_maximum_fusion.1.low_near_ref, ...), custom_call_target="tpu_custom_call" | custom-call | flops 12000000000 | tf_op jit(solution)/shard_map/pallas_call | solution.py:482
  50.9 3.9 %all-to-all-start.2 = ((f32[32,16,128]{2,1,0:T(8,128)}), f32[32,16,128]{2,1,0:T(8,128)S(1)}, u32[]{:S(2)}, u32[]{:S(2)}) async-start(f32[32,16,128]{2,1,0:T(8,128)} %bitcast.5), calls=%async_computation.2 | async-start | bytes 524288 | tf_op jit(solution)/shard_map/all_to_all | solution.py:570
  54.8 2.1 %shard_map.52 = f32[8,4,640]{2,1,0:T(4,128)S(1)} custom-call(bf16[8,2,4,32,512]{4,3,2,1,0:T(8,128)(2,1)S(1)} %get-tuple-element.30.samples_ref, f32[256,128]{1,0:T(8,128)S(1)} %get-tuple-element.31.vectors_ref), custom_call_target="tpu_custom_call" | custom-call | flops 2000000000 | tf_op jit(solution)/shard_map/pallas_call | solution.py:482
  56.9 8.3 %all-to-all-done.2 = f32[32,16,128]{2,1,0:T(8,128)S(1)} async-done(((f32[32,16,128]{2,1,0:T(8,128)}), f32[32,16,128]{2,1,0:T(8,128)S(1)}, u32[]{:S(2)}, u32[]{:S(2)}) %all-to-all-start.2) | async-done | bytes 262176 | tf_op jit(solution)/shard_map/all_to_all | solution.py:570
  65.2 0.8 broadcast_in_dim.16
  66.0 0.6 shard_map.53
  66.6 0.1 collective-permute-start.14
  66.6 2.6 %all-to-all-start.1 = ((f32[32,4,640]{2,1,0:T(4,128)}), f32[32,4,640]{2,1,0:T(4,128)S(1)}, u32[]{:S(2)}, u32[]{:S(2)}) async-start(f32[32,4,640]{2,1,0:T(4,128)} %bitcast.4), calls=%async_computation.1 | async-start | bytes 655360 | tf_op jit(solution)/shard_map/all_to_all | solution.py:570
  69.3 2.6 %collective-permute-start.17 = (f32[72,128]{1,0:T(8,128)S(1)}, f32[72,128]{1,0:T(8,128)S(1)}, u32[]{:S(2)}, u32[]{:S(2)}) collective-permute-start(f32[72,128]{1,0:T(8,128)S(1)} %add.36), channel_id=1, source_target_pairs={{0,6},{1,7},{2,4},{3,5},{4,2},{5,3},{6,0},{7,1},{8,14},{9,15},{10,... | collective-permute-start | bytes 110600 | tf_op jit(solution)/shard_map/ppermute | solution.py:497
  71.9 0.6 collective-permute-start.16
  72.5 0.4 collective-permute-start.15
  72.9 3.7 %collective-permute-start.24 = (f32[1,128,128]{2,1,0:T(8,128)S(1)}, f32[1,128,128]{2,1,0:T(8,128)S(1)}, u32[]{:S(2)}, u32[]{:S(2)}) collective-permute-start(f32[1,128,128]{2,1,0:T(8,128)S(1)} %get-tuple-element.45), channel_id=1, source_target_pairs={{0,24},{4,28},{8,16},{12,20},{16,8},{20,12},{24,0},{28,4},{1,25},{... | collective-permute-start | bytes 196616 | tf_op jit(solution)/shard_map/ppermute | solution.py:497
  76.5 1.5 %collective-permute-start.26 = (f32[1,128,128]{2,1,0:T(8,128)S(1)}, f32[1,128,128]{2,1,0:T(8,128)S(1)}, u32[]{:S(2)}, u32[]{:S(2)}) collective-permute-start(f32[1,128,128]{2,1,0:T(8,128)S(1)} %get-tuple-element.44), channel_id=1, source_target_pairs={{0,4},{4,0},{8,12},{12,8},{16,20},{20,16},{24,28},{28,24},{1,5},{5... | collective-permute-start | bytes 196616 | tf_op jit(solution)/shard_map/ppermute | solution.py:497
  78.0 2.8 %collective-permute-start.20 = (f32[72,128]{1,0:T(8,128)S(1)}, f32[72,128]{1,0:T(8,128)S(1)}, u32[]{:S(2)}, u32[]{:S(2)}) collective-permute-start(f32[72,128]{1,0:T(8,128)S(1)} %add_add_fusion.1), channel_id=1, source_target_pairs={{0,24},{1,25},{2,26},{3,27},{4,28},{5,29},{6,30},{7,31},{8,16},{9,... | collective-permute-start | bytes 110600 | tf_op jit(solution)/shard_map/ppermute | solution.py:497
  80.9 0.2 collective-permute-start.19
  81.1 1.4 %collective-permute-start.18 = (f32[72,128]{1,0:T(8,128)S(1)}, f32[72,128]{1,0:T(8,128)S(1)}, u32[]{:S(2)}, u32[]{:S(2)}) collective-permute-start(f32[72,128]{1,0:T(8,128)S(1)} %add_add_fusion.1), channel_id=1, source_target_pairs={{0,8},{1,9},{2,10},{3,11},{4,12},{5,13},{6,14},{7,15},{8,0},{9,1},... | collective-permute-start | bytes 110600 | tf_op jit(solution)/shard_map/ppermute | solution.py:497
  82.5 1.4 %collective-permute-done.20 = f32[72,128]{1,0:T(8,128)S(1)} collective-permute-done((f32[72,128]{1,0:T(8,128)S(1)}, f32[72,128]{1,0:T(8,128)S(1)}, u32[]{:S(2)}, u32[]{:S(2)}) %collective-permute-start.20) | collective-permute-done | bytes 36896 | tf_op jit(solution)/shard_map/ppermute | solution.py:497
  83.9 5.1 %collective-permute-start.22 = (f32[1,128,128]{2,1,0:T(8,128)S(1)}, f32[1,128,128]{2,1,0:T(8,128)S(1)}, u32[]{:S(2)}, u32[]{:S(2)}) collective-permute-start(f32[1,128,128]{2,1,0:T(8,128)S(1)} %get-tuple-element.45), channel_id=1, source_target_pairs={{0,8},{4,12},{8,0},{12,4},{16,24},{20,28},{24,16},{28,20},{1,9},{5... | collective-permute-start | bytes 196616 | tf_op jit(solution)/shard_map/ppermute | solution.py:497
  89.0 1.1 collective-permute-start.29
  90.1 0.4 collective-permute-start.28
  90.5 3.0 %collective-permute-start.27 = (f32[2,128,128]{2,1,0:T(8,128)S(1)}, f32[2,128,128]{2,1,0:T(8,128)S(1)}, u32[]{:S(2)}, u32[]{:S(2)}) collective-permute-start(f32[2,128,128]{2,1,0:T(8,128)S(1)} %pad_maximum_fusion.6.refs_2_), channel_id=1, source_target_pairs={{0,8},{4,12},{8,0},{12,4},{16,24},{20,28},{24,16},{28,20},{1,9},{5... | collective-permute-start | bytes 393224 | tf_op jit(solution)/shard_map/ppermute | solution.py:497
  93.5 1.5 %collective-permute-start.25 = (f32[4,128,128]{2,1,0:T(8,128)S(1)}, f32[4,128,128]{2,1,0:T(8,128)S(1)}, u32[]{:S(2)}, u32[]{:S(2)}) collective-permute-start(f32[4,128,128]{2,1,0:T(8,128)S(1)} %pad_maximum_fusion.5.refs_0_), channel_id=1, source_target_pairs={{0,4},{4,0},{8,12},{12,8},{16,20},{20,16},{24,28},{28,24},{1,5},{5... | collective-permute-start | bytes 786440 | tf_op jit(solution)/shard_map/ppermute | solution.py:497
  95.0 0.1 reshape.37.images_ref
  95.2 12.6 %shard_map.54 = (f32[128,128]{1,0:T(8,128)S(1)}, f32[128,128]{1,0:T(8,128)S(1)}, s32[1]{0:T(128)}) custom-call(f32[72,128]{1,0:T(8,128)S(1)} %add_add_fusion.gram_ref, f32[72,128]{1,0:T(8,128)S(1)} %collective-permute-done.21.other_ref), custom_call_target="tpu_custom_call" | custom-call | flops 12000000000 | tf_op jit(solution)/shard_map/pallas_call | solution.py:482
  108.4 0.0 copy-start
  108.5 0.0 copy-start.1
  108.5 0.2 conditional.1
  108.8 0.5 copy-done
  109.3 0.0 copy-done.1
  109.3 4.1 %shard_map.55 = (f32[32,512]{1,0:T(8,128)}, f32[256,128]{1,0:T(8,128)}) custom-call(f32[128,640]{1,0:T(8,128)S(1)} %reshape.37.images_ref, f32[128,128]{1,0:T(8,128)S(1)} %get-tuple-element.46.both_ref, f32[32,512]{1,0:T(8,128)S(1)} %copy-done, s32[32,512]{1,0:T(8,128)S(1)} %copy-done.1, f32[4,128,128]{2,1,0:T(8,128)S(1)} %pad_maximum_fusion.5.refs_0_, ...), custom_call_target="tpu_custom_call" | custom-call | flops 5000000000 | tf_op jit(solution)/shard_map/pallas_call | solution.py:482
  (33 shorter events, 0.3 us)
Async XLA Ops:
  2.5 20.4 %all-to-all-start = ((f32[32,8,128]{2,1,0:T(8,128)}), f32[32,8,128]{2,1,0:T(8,128)S(1)}, u32[]{:S(2)}, u32[]{:S(2)}) async-start(f32[32,8,128]{2,1,0:T(8,128)} %bitcast.15), calls=%async_computation | async-start | bytes 262144 | tf_op jit(solution)/shard_map/all_to_all | solution.py:570
  9.8 8.7 %collective-permute-start.7 = (f32[1,32,512]{2,1,0:T(8,128)}, f32[1,32,512]{2,1,0:T(8,128)S(1)}, u32[]{:S(2)}, u32[]{:S(2)}) collective-permute-start(f32[1,32,512]{2,1,0:T(8,128)} %bitcast.16), channel_id=1, source_target_pairs={{0,24},{1,25},{2,26},{3,27},{4,28},{5,29},{6,30},{7,31},{8,16},{9,... | collective-permute-start | bytes 196616 | tf_op jit(solution)/shard_map/ppermute | solution.py:497
  13.5 8.5 %collective-permute-start.6 = (f32[1,32,512]{2,1,0:T(8,128)}, f32[1,32,512]{2,1,0:T(8,128)S(1)}, u32[]{:S(2)}, u32[]{:S(2)}) collective-permute-start(f32[1,32,512]{2,1,0:T(8,128)} %bitcast.17), channel_id=1, source_target_pairs={{0,16},{1,17},{2,18},{3,19},{4,20},{5,21},{6,22},{7,23},{8,24},{9,... | collective-permute-start | bytes 196616 | tf_op jit(solution)/shard_map/ppermute | solution.py:497
  13.5 8.5 %collective-permute-start.5 = (f32[1,32,512]{2,1,0:T(8,128)}, f32[1,32,512]{2,1,0:T(8,128)S(1)}, u32[]{:S(2)}, u32[]{:S(2)}) collective-permute-start(f32[1,32,512]{2,1,0:T(8,128)} %bitcast.18), channel_id=1, source_target_pairs={{0,8},{1,9},{2,10},{3,11},{4,12},{5,13},{6,14},{7,15},{8,0},{9,1},... | collective-permute-start | bytes 196616 | tf_op jit(solution)/shard_map/ppermute | solution.py:497
  22.9 5.1 %collective-permute-start.8 = (f32[4,16,512]{2,1,0:T(8,128)S(1)}, f32[4,16,512]{2,1,0:T(8,128)S(1)}, u32[]{:S(2)}, u32[]{:S(2)}) collective-permute-start(f32[4,16,512]{2,1,0:T(8,128)S(1)} %get-tuple-element.43), channel_id=1, source_target_pairs={{0,4},{1,5},{2,6},{3,7},{4,0},{5,1},{6,2},{7,3},{8,12},{9,13},{10,... | collective-permute-start | bytes 393224 | tf_op jit(solution)/shard_map/ppermute | solution.py:497
  24.5 5.1 %collective-permute-start.11 = (f32[4,16,512]{2,1,0:T(8,128)S(1)}, f32[4,16,512]{2,1,0:T(8,128)S(1)}, u32[]{:S(2)}, u32[]{:S(2)}) collective-permute-start(f32[4,16,512]{2,1,0:T(8,128)S(1)} %get-tuple-element.42), channel_id=1, source_target_pairs={{0,2},{1,3},{2,0},{3,1},{4,6},{5,7},{6,4},{7,5},{8,10},{9,11},{10,... | collective-permute-start | bytes 393224 | tf_op jit(solution)/shard_map/ppermute | solution.py:497
  28.1 7.0 %collective-permute-start.9 = (f32[8,16,512]{2,1,0:T(8,128)S(1)}, f32[8,16,512]{2,1,0:T(8,128)S(1)}, u32[]{:S(2)}, u32[]{:S(2)}) collective-permute-start(f32[8,16,512]{2,1,0:T(8,128)S(1)} %pad_maximum_fusion.3), channel_id=1, source_target_pairs={{0,2},{1,3},{2,0},{3,1},{4,6},{5,7},{6,4},{7,5},{8,10},{9,11},{10,... | collective-permute-start | bytes 786440 | tf_op jit(solution)/shard_map/ppermute | solution.py:497
  29.6 6.7 %collective-permute-start.12 = (f32[8,16,512]{2,1,0:T(8,128)S(1)}, f32[8,16,512]{2,1,0:T(8,128)S(1)}, u32[]{:S(2)}, u32[]{:S(2)}) collective-permute-start(f32[8,16,512]{2,1,0:T(8,128)S(1)} %pad_maximum_fusion.4), channel_id=1, source_target_pairs={{0,4},{1,5},{2,6},{3,7},{4,0},{5,1},{6,2},{7,3},{8,12},{9,13},{10,... | collective-permute-start | bytes 786440 | tf_op jit(solution)/shard_map/ppermute | solution.py:497
  35.1 2.0 %collective-permute-start.10 = (f32[16,16,512]{2,1,0:T(8,128)S(1)}, f32[16,16,512]{2,1,0:T(8,128)S(1)}, u32[]{:S(2)}, u32[]{:S(2)}) collective-permute-start(f32[16,16,512]{2,1,0:T(8,128)S(1)} %pad_maximum_fusion.top_near_ref), channel_id=1, source_target_pairs={{0,1},{1,0},{2,3},{3,2},{4,5},{5,4},{6,7},{7,6},{8,9},{9,8},{10,11... | collective-permute-start | bytes 1572872 | tf_op jit(solution)/shard_map/ppermute | solution.py:497
  36.4 2.0 %collective-permute-start.13 = (f32[16,16,512]{2,1,0:T(8,128)S(1)}, f32[16,16,512]{2,1,0:T(8,128)S(1)}, u32[]{:S(2)}, u32[]{:S(2)}) collective-permute-start(f32[16,16,512]{2,1,0:T(8,128)S(1)} %pad_maximum_fusion.1.low_near_ref), channel_id=1, source_target_pairs={{0,1},{1,0},{2,3},{3,2},{4,5},{5,4},{6,7},{7,6},{8,9},{9,8},{10,11... | collective-permute-start | bytes 1572872 | tf_op jit(solution)/shard_map/ppermute | solution.py:497
  50.9 14.3 %all-to-all-start.2 = ((f32[32,16,128]{2,1,0:T(8,128)}), f32[32,16,128]{2,1,0:T(8,128)S(1)}, u32[]{:S(2)}, u32[]{:S(2)}) async-start(f32[32,16,128]{2,1,0:T(8,128)} %bitcast.5), calls=%async_computation.2 | async-start | bytes 524288 | tf_op jit(solution)/shard_map/all_to_all | solution.py:570
  66.6 2.7 %collective-permute-start.14 = (f32[72,128]{1,0:T(8,128)S(1)}, f32[72,128]{1,0:T(8,128)S(1)}, u32[]{:S(2)}, u32[]{:S(2)}) collective-permute-start(f32[72,128]{1,0:T(8,128)S(1)} %get-tuple-element.35), channel_id=1, source_target_pairs={{0,1},{1,0},{2,3},{3,2},{4,5},{5,4},{6,7},{7,6},{8,9},{9,8},{10,11... | collective-permute-start | bytes 110600 | tf_op jit(solution)/shard_map/ppermute | solution.py:497
  66.6 28.4 %all-to-all-start.1 = ((f32[32,4,640]{2,1,0:T(4,128)}), f32[32,4,640]{2,1,0:T(4,128)S(1)}, u32[]{:S(2)}, u32[]{:S(2)}) async-start(f32[32,4,640]{2,1,0:T(4,128)} %bitcast.4), calls=%async_computation.1 | async-start | bytes 655360 | tf_op jit(solution)/shard_map/all_to_all | solution.py:570
  69.3 7.3 %collective-permute-start.17 = (f32[72,128]{1,0:T(8,128)S(1)}, f32[72,128]{1,0:T(8,128)S(1)}, u32[]{:S(2)}, u32[]{:S(2)}) collective-permute-start(f32[72,128]{1,0:T(8,128)S(1)} %add.36), channel_id=1, source_target_pairs={{0,6},{1,7},{2,4},{3,5},{4,2},{5,3},{6,0},{7,1},{8,14},{9,15},{10,... | collective-permute-start | bytes 110600 | tf_op jit(solution)/shard_map/ppermute | solution.py:497
  71.9 6.1 %collective-permute-start.16 = (f32[72,128]{1,0:T(8,128)S(1)}, f32[72,128]{1,0:T(8,128)S(1)}, u32[]{:S(2)}, u32[]{:S(2)}) collective-permute-start(f32[72,128]{1,0:T(8,128)S(1)} %add.36), channel_id=1, source_target_pairs={{0,4},{1,5},{2,6},{3,7},{4,0},{5,1},{6,2},{7,3},{8,12},{9,13},{10,... | collective-permute-start | bytes 110600 | tf_op jit(solution)/shard_map/ppermute | solution.py:497
  72.5 5.5 %collective-permute-start.15 = (f32[72,128]{1,0:T(8,128)S(1)}, f32[72,128]{1,0:T(8,128)S(1)}, u32[]{:S(2)}, u32[]{:S(2)}) collective-permute-start(f32[72,128]{1,0:T(8,128)S(1)} %add.36), channel_id=1, source_target_pairs={{0,2},{1,3},{2,0},{3,1},{4,6},{5,7},{6,4},{7,5},{8,10},{9,11},{10,... | collective-permute-start | bytes 110600 | tf_op jit(solution)/shard_map/ppermute | solution.py:497
  72.9 17.6 %collective-permute-start.24 = (f32[1,128,128]{2,1,0:T(8,128)S(1)}, f32[1,128,128]{2,1,0:T(8,128)S(1)}, u32[]{:S(2)}, u32[]{:S(2)}) collective-permute-start(f32[1,128,128]{2,1,0:T(8,128)S(1)} %get-tuple-element.45), channel_id=1, source_target_pairs={{0,24},{4,28},{8,16},{12,20},{16,8},{20,12},{24,0},{28,4},{1,25},{... | collective-permute-start | bytes 196616 | tf_op jit(solution)/shard_map/ppermute | solution.py:497
  76.5 16.9 %collective-permute-start.23 = (f32[1,128,128]{2,1,0:T(8,128)S(1)}, f32[1,128,128]{2,1,0:T(8,128)S(1)}, u32[]{:S(2)}, u32[]{:S(2)}) collective-permute-start(f32[1,128,128]{2,1,0:T(8,128)S(1)} %get-tuple-element.45), channel_id=1, source_target_pairs={{0,16},{4,20},{8,24},{12,28},{16,0},{20,4},{24,8},{28,12},{1,17},{... | collective-permute-start | bytes 196616 | tf_op jit(solution)/shard_map/ppermute | solution.py:497
  76.5 4.6 %collective-permute-start.26 = (f32[1,128,128]{2,1,0:T(8,128)S(1)}, f32[1,128,128]{2,1,0:T(8,128)S(1)}, u32[]{:S(2)}, u32[]{:S(2)}) collective-permute-start(f32[1,128,128]{2,1,0:T(8,128)S(1)} %get-tuple-element.44), channel_id=1, source_target_pairs={{0,4},{4,0},{8,12},{12,8},{16,20},{20,16},{24,28},{28,24},{1,5},{5... | collective-permute-start | bytes 196616 | tf_op jit(solution)/shard_map/ppermute | solution.py:497
  78.0 5.9 %collective-permute-start.20 = (f32[72,128]{1,0:T(8,128)S(1)}, f32[72,128]{1,0:T(8,128)S(1)}, u32[]{:S(2)}, u32[]{:S(2)}) collective-permute-start(f32[72,128]{1,0:T(8,128)S(1)} %add_add_fusion.1), channel_id=1, source_target_pairs={{0,24},{1,25},{2,26},{3,27},{4,28},{5,29},{6,30},{7,31},{8,16},{9,... | collective-permute-start | bytes 110600 | tf_op jit(solution)/shard_map/ppermute | solution.py:497
  80.9 8.1 %collective-permute-start.19 = (f32[72,128]{1,0:T(8,128)S(1)}, f32[72,128]{1,0:T(8,128)S(1)}, u32[]{:S(2)}, u32[]{:S(2)}) collective-permute-start(f32[72,128]{1,0:T(8,128)S(1)} %add_add_fusion.1), channel_id=1, source_target_pairs={{0,16},{1,17},{2,18},{3,19},{4,20},{5,21},{6,22},{7,23},{8,24},{9,... | collective-permute-start | bytes 110600 | tf_op jit(solution)/shard_map/ppermute | solution.py:497
  81.1 9.0 %collective-permute-start.18 = (f32[72,128]{1,0:T(8,128)S(1)}, f32[72,128]{1,0:T(8,128)S(1)}, u32[]{:S(2)}, u32[]{:S(2)}) collective-permute-start(f32[72,128]{1,0:T(8,128)S(1)} %add_add_fusion.1), channel_id=1, source_target_pairs={{0,8},{1,9},{2,10},{3,11},{4,12},{5,13},{6,14},{7,15},{8,0},{9,1},... | collective-permute-start | bytes 110600 | tf_op jit(solution)/shard_map/ppermute | solution.py:497
  83.9 9.6 %collective-permute-start.22 = (f32[1,128,128]{2,1,0:T(8,128)S(1)}, f32[1,128,128]{2,1,0:T(8,128)S(1)}, u32[]{:S(2)}, u32[]{:S(2)}) collective-permute-start(f32[1,128,128]{2,1,0:T(8,128)S(1)} %get-tuple-element.45), channel_id=1, source_target_pairs={{0,8},{4,12},{8,0},{12,4},{16,24},{20,28},{24,16},{28,20},{1,9},{5... | collective-permute-start | bytes 196616 | tf_op jit(solution)/shard_map/ppermute | solution.py:497
  89.0 19.7 %collective-permute-start.29 = (f32[2,128,128]{2,1,0:T(8,128)S(1)}, f32[2,128,128]{2,1,0:T(8,128)S(1)}, u32[]{:S(2)}, u32[]{:S(2)}) collective-permute-start(f32[2,128,128]{2,1,0:T(8,128)S(1)} %pad_maximum_fusion.6.refs_2_), channel_id=1, source_target_pairs={{0,24},{4,28},{8,16},{12,20},{16,8},{20,12},{24,0},{28,4},{1,25},{... | collective-permute-start | bytes 393224 | tf_op jit(solution)/shard_map/ppermute | solution.py:497
  90.1 18.6 %collective-permute-start.28 = (f32[2,128,128]{2,1,0:T(8,128)S(1)}, f32[2,128,128]{2,1,0:T(8,128)S(1)}, u32[]{:S(2)}, u32[]{:S(2)}) collective-permute-start(f32[2,128,128]{2,1,0:T(8,128)S(1)} %pad_maximum_fusion.6.refs_2_), channel_id=1, source_target_pairs={{0,16},{4,20},{8,24},{12,28},{16,0},{20,4},{24,8},{28,12},{1,17},{... | collective-permute-start | bytes 393224 | tf_op jit(solution)/shard_map/ppermute | solution.py:497
  90.5 18.3 %collective-permute-start.27 = (f32[2,128,128]{2,1,0:T(8,128)S(1)}, f32[2,128,128]{2,1,0:T(8,128)S(1)}, u32[]{:S(2)}, u32[]{:S(2)}) collective-permute-start(f32[2,128,128]{2,1,0:T(8,128)S(1)} %pad_maximum_fusion.6.refs_2_), channel_id=1, source_target_pairs={{0,8},{4,12},{8,0},{12,4},{16,24},{20,28},{24,16},{28,20},{1,9},{5... | collective-permute-start | bytes 393224 | tf_op jit(solution)/shard_map/ppermute | solution.py:497
  93.5 1.7 %collective-permute-start.21 = (f32[72,128]{1,0:T(8,128)S(1)}, f32[72,128]{1,0:T(8,128)S(1)}, u32[]{:S(2)}, u32[]{:S(2)}) collective-permute-start(f32[72,128]{1,0:T(8,128)S(1)} %add_add_fusion.gram_ref), channel_id=1, source_target_pairs={{0,1},{1,0},{2,3},{3,2},{4,5},{5,4},{6,7},{7,6},{8,9},{9,8},{10,11... | collective-permute-start | bytes 110600 | tf_op jit(solution)/shard_map/ppermute | solution.py:497
  93.5 15.2 %collective-permute-start.25 = (f32[4,128,128]{2,1,0:T(8,128)S(1)}, f32[4,128,128]{2,1,0:T(8,128)S(1)}, u32[]{:S(2)}, u32[]{:S(2)}) collective-permute-start(f32[4,128,128]{2,1,0:T(8,128)S(1)} %pad_maximum_fusion.5.refs_0_), channel_id=1, source_target_pairs={{0,4},{4,0},{8,12},{12,8},{16,20},{20,16},{24,28},{28,24},{1,5},{5... | collective-permute-start | bytes 786440 | tf_op jit(solution)/shard_map/ppermute | solution.py:497
  108.4 0.8 copy-start
  108.5 0.9 copy-start.1

commit v6 on v5

--- a/solution.py
+++ b/solution.py
@@ -210,35 +210,18 @@
         send_ref[:, g, part] = joined.reshape(tiles, per_tile, lanes)
 
 
-def passes_kernel(
-    masks,
-    top_near_ref,
-    top_far_ref,
-    low_near_ref,
-    low_far_ref,
-    basis_ref,
-    samples_ref,
-    normal_ref,
-    send_ref,
-    wide_ref,
-    moved_ref,
-):
+def passes_kernel(orders, basis_ref, *refs):
+    *pieces, samples_ref, normal_ref, send_ref, wide_ref, moved_ref = refs
     tiles, _, groups, chg, tile = samples_ref.shape
     me = lax.axis_index("rows") * groups + lax.axis_index("coil")
-    start = 0
-    for near_ref, far_ref, order in (
-        (top_near_ref, top_far_ref, masks[0]),
-        (low_near_ref, low_far_ref, masks[1]),
-    ):
-        half, count = near_ref.shape[:2]
+    for (start, order), piece_ref in zip(orders, pieces):
+        count = piece_ref.shape[1]
         for slot, mask in enumerate(order):
-            value = near_ref[slot] if slot < half else far_ref[slot - half]
-            high, low = split(value)
+            high, low = split(piece_ref[slot])
             source = lax.bitwise_xor(me, mask)
             t, g = source // groups, source % groups
             samples_ref[t, 0, g, start : start + count] = high
             samples_ref[t, 1, g, start : start + count] = low
-        start += count
     cols = basis_ref.shape[-1] // chg
     rows = []
     for k in range(cols):
@@ -265,7 +248,7 @@
 
 
 def images_kernel(samples_ref, vectors_ref, send_ref, wide_ref):
-    tiles, cols, reach = send_ref.shape
+    tiles, groups, cols, reach = send_ref.shape
     tile = samples_ref.shape[-1]
     images = jnp.concatenate(images_of(vectors_ref[...], samples_ref, wide_ref), axis=0)
     positions = images.shape[1]
@@ -276,7 +259,8 @@
             part = jnp.concatenate([images[:, positions - rim :], images[:, :tile]], axis=1)
         else:
             part = images[:, t * tile - rim : (t + 1) * tile]
-        send_ref[t] = part
+        for g in range(groups):
+            send_ref[t, g] = part
 
 
 def gather_turned(received_ref, cols, per_tile, part):
@@ -434,17 +418,14 @@
     both_ref[...] = exact(inverse_factor(gram_ref[...]), inverse_ref[...])
 
 
-def last_kernel(
-    cols,
-    per_tile,
-    parts,
-    images_ref,
-    both_ref,
-    kspace_ref,
-    mask_ref,
-    *refs,
-):
-    recovered_ref, basis_ref = refs[-2:]
+def last_kernel(cols, orders, images_ref, both_ref, kspace_hbm, mask_hbm, *refs):
+    *pieces, recovered_ref, basis_ref, kspace_ref, mask_ref, sems = refs
+    fetches = [
+        pltpu.make_async_copy(kspace_hbm, kspace_ref, sems.at[0]),
+        pltpu.make_async_copy(mask_hbm, mask_ref, sems.at[1]),
+    ]
+    for fetch in fetches:
+        fetch.start()
     both = both_ref[...]
     count, reach = images_ref.shape
     devices = count // cols
@@ -458,31 +439,34 @@
     chg, tile = kspace_ref.shape
     me = lax.axis_index("rows")
     estimate = jnp.zeros((chg, tile), jnp.float32)
-    for (start, masks), rows_ref in zip(parts, refs):
-        blocks, owned, rank = rows_ref.shape
-        vectors = dot3(rows_ref[...].reshape(blocks * owned, rank), both, ((1,), (1,)))
-        if masks[0] == 0:
-            basis_ref[start * chg : start * chg + owned] = vectors[:owned]
-        high, low = split(vectors)
-        projected = dot(jnp.concatenate([high, high], axis=1), stacked) + dot(low, images_high)
-        for slot, mask in enumerate(masks):
-            total = None
-            for j in range(owned // chg):
-                part = projected[slot * owned + j * chg : slot * owned + (j + 1) * chg]
-                part = pltpu.roll(part, start + j, 1) if start + j else part
-                total = part if total is None else total + part
+    for order, rows_ref in zip(orders, pieces):
+        for slot, mask in enumerate(order):
+            vectors = dot3(rows_ref[slot], both, ((1,), (1,)))
+            if mask == 0:
+                basis_ref[...] = vectors
+            high, low = split(vectors)
+            projected = dot(jnp.concatenate([high, high], axis=1), stacked) + dot(low, images_high)
+            per_tile = vectors.shape[0] // chg
+            total = projected[:chg]
+            for j in range(1, per_tile):
+                total = total + pltpu.roll(projected[j * chg : (j + 1) * chg], j, 1)
             total = pltpu.roll(total, lax.bitwise_xor(me, mask) * per_tile, 1)
             estimate = estimate + total[:, reach - tile :]
+    for fetch in fetches:
+        fetch.wait()
     estimate = estimate / KER
     residual = mask_ref[...].astype(jnp.float32) * (kspace_ref[...] - estimate)
     recovered_ref[...] = estimate + residual - jnp.clip(residual, -threshold, threshold)
 
 
-def call(kernel, outs, *args, scratch=(), space=pltpu.VMEM, limit=40, scalars=0, micros=1):
+def call(kernel, outs, *args, scratch=(), far=(), limit=40, scalars=0, micros=1):
     return pl.pallas_call(
         kernel,
         out_shape=[jax.ShapeDtypeStruct(shape, kind) for shape, kind in outs],
-        in_specs=[pl.BlockSpec(memory_space=space)] * len(args),
+        in_specs=[
+            pl.BlockSpec(memory_space=pltpu.HBM if i in far else pltpu.VMEM)
+            for i in range(len(args))
+        ],
         out_specs=[pl.BlockSpec(memory_space=pltpu.VMEM)] * (len(outs) - scalars)
         + [pl.BlockSpec(memory_space=pltpu.SMEM)] * scalars,
         scratch_shapes=list(scratch),
@@ -526,58 +510,59 @@
 def gather_samples(sampled, tiles, groups, beside):
     devices = tiles * groups
     near, masks = sampled[None], [0]
-    for partners in rounds_of(2 * groups, devices):
-        near, masks = gather_round(near, masks, partners, devices, AXES)
+    mask = devices // 2
+    while mask > groups:
+        near, masks = gather_round(near, masks, [mask], devices, AXES)
+        mask //= 2
     near = after(near, beside)
     half = near.shape[1] // 2
-    parts = [near[:, :half], near[:, half:]]
-    orders = [masks, masks]
-    ways = [(groups, groups // 2), (groups // 2, groups)]
-    for step in range(2):
-        for i in range(2):
-            parts[i], orders[i] = gather_round(
-                parts[i], orders[i], [ways[i][step]], devices, AXES
-            )
-    for partners in rounds_of(2, groups // 2):
-        for i in range(2):
-            parts[i], orders[i] = gather_round(parts[i], orders[i], partners, devices, AXES)
-    far = [exchange(part, devices, 1, AXES) for part in parts]
-    orders = [with_masks(order, 1) for order in orders]
-    return parts, far, orders
-
-
-def gather_rows(by_row, tiles, per_tile):
-    half = by_row.shape[0] // 2
-    near, order = by_row[None, :half], [0]
-    for partners in rounds_of(2, tiles):
-        near, order = gather_round(near, order, partners, tiles, "rows")
-    parts = [(0, order), (0, [m ^ 1 for m in order])]
-    pieces = [near, exchange(near, tiles, 1, "rows")]
-    near, order = gather_round(by_row[None, half:], [0], [1], tiles, "rows")
-    *early, late = rounds_of(2, tiles)
-    for partners in early:
-        near, order = gather_round(near, order, partners, tiles, "rows")
-    start = per_tile // 2
-    parts.append((start, order))
-    pieces.append(near)
-    for mask in late:
-        parts.append((start, [m ^ mask for m in order]))
-        pieces.append(exchange(near, tiles, mask, "rows"))
-    return parts, pieces
+    halves = []
+    for part, ways in (
+        (near[:, :half], (groups, groups // 2)),
+        (near[:, half:], (groups // 2, groups)),
+    ):
+        part, order = gather_round(part, masks, [ways[0]], devices, AXES)
+        pieces = [(part, order)]
+        mask = ways[1]
+        rest = groups // 4
+        while mask > 1:
+            pieces = pieces + [
+                (exchange(part, devices, mask, AXES), [m ^ mask for m in order])
+                for part, order in pieces
+            ]
+            mask, rest = rest, rest // 2
+        halves.append(
+            pieces
+            + [(exchange(part, devices, 1, AXES), [m ^ 1 for m in order]) for part, order in pieces]
+        )
+    return halves
 
 
 def to_all(pieces, axes=AXES):
     return lax.all_to_all(pieces, axes, 0, 0, tiled=True)
 
 
-def total_of(kept, given, devices):
+def total_and_rows(kept, given, by_row, images, tiles, devices):
     total = kept + exchange(given, devices, 1, AXES)
+    near, order = by_row[None], [0]
+    mask = tiles // 2
     for partners in rounds_of(2, devices):
-        terms = [exchange(total, devices, mask, AXES) for mask in partners]
+        terms = [exchange(total, devices, way, AXES) for way in partners]
+        if mask > 1:
+            near, order = gather_round(near, order, [mask], tiles, "rows")
+            mask //= 2
         total = total + terms[0]
         if len(terms) == 3:
             total = total + (terms[1] + terms[2])
-    return total, exchange(total, devices, 1, AXES)
+        near = after(near, total)
+    while mask > 1:
+        near, order = gather_round(near, order, [mask], tiles, "rows")
+        mask //= 2
+    other = exchange(total, devices, 1, AXES)
+    near, total, other = lax.optimization_barrier((near, total, other))
+    far = exchange(near, tiles, 1, "rows")
+    pieces = [(near, order), (far, [m ^ 1 for m in order])]
+    return (total, other), pieces, to_all(images)
 
 
 def column_shards(kspace, sample_mask, start_basis):
@@ -605,32 +590,37 @@
             pltpu.VMEM((owned, rank), f32),
             pltpu.SemaphoreType.DMA((3,)),
         ],
-        space=pltpu.HBM,
+        far=(0, 1, 2),
         limit=60,
     )
     basis_parts = to_all(basis_send.reshape(devices, per_tile, lanes))
-    near, far, masks = gather_samples(sampled, tiles, groups, basis_parts)
+    halves = gather_samples(sampled, tiles, groups, basis_parts)
+    starts = (0, chg // len(halves))
+    orders = [(start, order) for start, half in zip(starts, halves) for _, order in half]
     wide = pltpu.VMEM((rows, positions), f32)
     moved = pltpu.VMEM((2 * rows, positions), bf16)
     samples, normal, send = call(
-        functools.partial(passes_kernel, masks),
+        functools.partial(passes_kernel, orders),
         [
             ((tiles, 2, groups, chg, tile), bf16),
             ((rows, channels), f32),
             ((tiles, groups, 2, per_tile, lanes), f32),
         ],
-        near[0],
-        far[0],
-        near[1],
-        far[1],
         basis_parts.reshape(tiles, groups, per_tile, lanes),
+        *[piece for half in halves for piece, _ in half],
         scratch=[wide, moved],
         micros=12,
     )
     received = to_all(send.reshape(devices, 2 * per_tile, lanes))
     reach = tile + LANES
-    (images,) = call(images_kernel, [((tiles, cols, reach), f32)], samples, normal, scratch=[wide], micros=2)
-    images = jnp.broadcast_to(images[:, None], (tiles, groups, cols, reach))
+    (images,) = call(
+        images_kernel,
+        [((tiles, groups, cols, reach), f32)],
+        samples,
+        normal,
+        scratch=[wide],
+        micros=2,
+    )
     received = after(received, images)
     half = ((rank // 2 + SUB, rank), f32)
     kept, given, by_row = call(
@@ -638,9 +628,9 @@
         [half, half, ((owned, rank), f32)],
         received.reshape(devices * 2 * per_tile, lanes),
     )
-    gram = total_of(kept, given, devices)
-    images = to_all(images.reshape(devices, cols, reach)).reshape(rank, reach)
-    parts, pieces = gather_rows(by_row, tiles, per_tile)
+    gram, pieces, images = total_and_rows(
+        kept, given, by_row, images.reshape(devices, cols, reach), tiles, devices
+    )
     whole = ((rank, rank), f32)
     first, both, sound = call(
         factors_kernel, [whole, whole, ((1,), jnp.int32)], *gram, scalars=1, micros=12
@@ -656,13 +646,20 @@
 
     both = lax.cond(sound[0] == 1, lambda: both, again)
     recovered, basis = call(
-        functools.partial(last_kernel, cols, per_tile, parts),
+        functools.partial(last_kernel, cols, [order for _, order in pieces]),
         [((chg, tile), f32), ((owned, rank), f32)],
-        images,
+        images.reshape(rank, reach),
         both,
         kspace,
         sample_mask,
-        *pieces,
+        *[piece for piece, _ in pieces],
+        scratch=[
+            pltpu.VMEM((chg, tile), f32),
+            pltpu.VMEM((chg, tile), sample_mask.dtype),
+            pltpu.SemaphoreType.DMA((2,)),
+        ],
+        far=(2, 3),
+        limit=40,
         micros=5,
     )
     return (recovered, basis.reshape(1, owned, rank))

time: 114 us -> 116 us (1.018)
  waiting for transfers between devices: 26.5 us -> 41.2 us
  starting transfers between devices: 48.8 us -> 35.1 us
    ppermute x25 -> x21, waiting for transfers between devices: 18.2 us -> 33.6 us  [exchange(): return lax.ppermute(block, axes, [(i, i ^ mask) for i in range(devices)])]
    ppermute x25 -> x21, starting transfers between devices: 35 us -> 24.8 us  [exchange(): return lax.ppermute(block, axes, [(i, i ^ mask) for i in range(devices)])]
    all_to_all x3, starting transfers between devices: 13.8 us -> 10.3 us  [to_all(): return lax.all_to_all(pieces, axes, 0, 0, tiled=True)]
  transfers between devices with their start and end apart: 28 -> 24, of which waited for: 9 -> 11; matrix products, arithmetic and copies ran while one was open for 1% -> 2% of each run, Pallas kernels for 13% -> 13%
where the time goes in v6:
time: 116 us
  waiting for transfers between devices  41.2 us (36%)
  starting transfers between devices  35.1 us (30%)
  Pallas kernels  34.9 us (30%)
  other arithmetic  1.84 us (2%)
  between operations  1.66 us (1%)
    pallas_call x6, Pallas kernels, call(): pl.pallas_call(kernel, out_shape=[jax.ShapeDtypeStruct(shape, kind) for s...  34.9 us
    ppermute x21, waiting for transfers between devices, exchange(): return lax.ppermute(block, axes, [(i, i ^ mask) for i in range(devices)])  33.6 us
    ppermute x21, starting transfers between devices, exchange(): return lax.ppermute(block, axes, [(i, i ^ mask) for i in range(devices)])  24.8 us
    all_to_all x3, starting transfers between devices, to_all(): return lax.all_to_all(pieces, axes, 0, 0, tiled=True)  10.3 us
    all_to_all x3, waiting for transfers between devices, to_all(): return lax.all_to_all(pieces, axes, 0, 0, tiled=True)  7.58 us
  transfers between devices with their start and end apart: 24, of which 11 were waited for; matrix products, arithmetic and copies ran while one was open for 2% of the time, Pallas kernels for 13%

profile of v6, /device:TPU:0, one launch (start us, length us, event | category | flops | bytes accessed | tf_op | source)
XLA Modules:
  0.0 115.6 jit_solution(17707626301889952810)
XLA Ops:
  0.6 1.9 %shard_map.50 = (f32[32,512]{1,0:T(8,128)}, f32[256,128]{1,0:T(8,128)}) custom-call(f32[32,512]{1,0:T(8,128)} %kspace_hbm.3, s32[32,512]{1,0:T(8,128)} %mask_hbm.3, f32[256,128]{1,0:T(8,128)} %bitcast.18), custom_call_target="tpu_custom_call" | custom-call | flops 1000000000 | tf_op jit(solution)/shard_map/pallas_call | solution.py:463
  2.5 4.1 %collective-permute-start.5 = (f32[1,32,512]{2,1,0:T(8,128)}, f32[1,32,512]{2,1,0:T(8,128)S(1)}, u32[]{:S(2)}, u32[]{:S(2)}) collective-permute-start(f32[1,32,512]{2,1,0:T(8,128)} %bitcast.12), channel_id=1, source_target_pairs={{0,16},{1,17},{2,18},{3,19},{4,20},{5,21},{6,22},{7,23},{8,24},{9,... | collective-permute-start | bytes 196616 | tf_op jit(solution)/shard_map/ppermute | solution.py:481
  6.6 3.8 %all-to-all-start = ((f32[32,8,128]{2,1,0:T(8,128)}), f32[32,8,128]{2,1,0:T(8,128)S(1)}, u32[]{:S(2)}, u32[]{:S(2)}) async-start(f32[32,8,128]{2,1,0:T(8,128)} %bitcast.15), calls=%async_computation | async-start | bytes 262144 | tf_op jit(solution)/shard_map/all_to_all | solution.py:542
  10.5 0.0 collective-permute-done.5
  10.5 0.8 pad_maximum_fusion.5
  11.3 1.8 %collective-permute-start.6 = (f32[2,32,512]{2,1,0:T(8,128)S(1)}, f32[2,32,512]{2,1,0:T(8,128)S(1)}, u32[]{:S(2)}, u32[]{:S(2)}) collective-permute-start(f32[2,32,512]{2,1,0:T(8,128)S(1)} %pad_maximum_fusion.5), channel_id=1, source_target_pairs={{0,8},{1,9},{2,10},{3,11},{4,12},{5,13},{6,14},{7,15},{8,0},{9,1},... | collective-permute-start | bytes 393224 | tf_op jit(solution)/shard_map/ppermute | solution.py:481
  13.2 5.3 %collective-permute-done.6 = f32[2,32,512]{2,1,0:T(8,128)S(1)} collective-permute-done((f32[2,32,512]{2,1,0:T(8,128)S(1)}, f32[2,32,512]{2,1,0:T(8,128)S(1)}, u32[]{:S(2)}, u32[]{:S(2)}) %collective-permute-start.6) | collective-permute-done | bytes 131104 | tf_op jit(solution)/shard_map/ppermute | solution.py:481
  18.5 0.9 pad_maximum_fusion.1
  19.4 1.6 %collective-permute-start.7 = (f32[4,16,512]{2,1,0:T(8,128)S(1)}, f32[4,16,512]{2,1,0:T(8,128)S(1)}, u32[]{:S(2)}, u32[]{:S(2)}) collective-permute-start(f32[4,16,512]{2,1,0:T(8,128)S(1)} %get-tuple-element.53), channel_id=1, source_target_pairs={{0,4},{1,5},{2,6},{3,7},{4,0},{5,1},{6,2},{7,3},{8,12},{9,13},{10,... | collective-permute-start | bytes 393224 | tf_op jit(solution)/shard_map/ppermute | solution.py:481
  21.0 1.5 %collective-permute-start.11 = (f32[4,16,512]{2,1,0:T(8,128)S(1)}, f32[4,16,512]{2,1,0:T(8,128)S(1)}, u32[]{:S(2)}, u32[]{:S(2)}) collective-permute-start(f32[4,16,512]{2,1,0:T(8,128)S(1)} %get-tuple-element.52), channel_id=1, source_target_pairs={{0,2},{1,3},{2,0},{3,1},{4,6},{5,7},{6,4},{7,5},{8,10},{9,11},{10,... | collective-permute-start | bytes 393224 | tf_op jit(solution)/shard_map/ppermute | solution.py:481
  22.5 2.4 %collective-permute-done.7 = f32[4,16,512]{2,1,0:T(8,128)S(1)} collective-permute-done((f32[4,16,512]{2,1,0:T(8,128)S(1)}, f32[4,16,512]{2,1,0:T(8,128)S(1)}, u32[]{:S(2)}, u32[]{:S(2)}) %collective-permute-start.7) | collective-permute-done | bytes 131104 | tf_op jit(solution)/shard_map/ppermute | solution.py:481
  24.9 1.3 %collective-permute-start.8 = (f32[8,16,512]{2,1,0:T(8,128)S(1)}, f32[8,16,512]{2,1,0:T(8,128)S(1)}, u32[]{:S(2)}, u32[]{:S(2)}) collective-permute-start(f32[8,16,512]{2,1,0:T(8,128)S(1)} %pad_maximum_fusion.2.refs_0_), channel_id=1, source_target_pairs={{0,2},{1,3},{2,0},{3,1},{4,6},{5,7},{6,4},{7,5},{8,10},{9,11},{10,... | collective-permute-start | bytes 786440 | tf_op jit(solution)/shard_map/ppermute | solution.py:481
  26.2 0.0 collective-permute-done.11
  26.2 1.5 %collective-permute-start.12 = (f32[8,16,512]{2,1,0:T(8,128)S(1)}, f32[8,16,512]{2,1,0:T(8,128)S(1)}, u32[]{:S(2)}, u32[]{:S(2)}) collective-permute-start(f32[8,16,512]{2,1,0:T(8,128)S(1)} %pad_maximum_fusion.3.refs_4_), channel_id=1, source_target_pairs={{0,4},{1,5},{2,6},{3,7},{4,0},{5,1},{6,2},{7,3},{8,12},{9,13},{10,... | collective-permute-start | bytes 786440 | tf_op jit(solution)/shard_map/ppermute | solution.py:481
  27.8 0.5 collective-permute-start.13
  28.3 4.0 %collective-permute-done.8.refs_1_ = f32[8,16,512]{2,1,0:T(8,128)S(1)} collective-permute-done((f32[8,16,512]{2,1,0:T(8,128)S(1)}, f32[8,16,512]{2,1,0:T(8,128)S(1)}, u32[]{:S(2)}, u32[]{:S(2)}) %collective-permute-start.8) | collective-permute-done | bytes 262176 | tf_op jit(solution)/shard_map/ppermute | solution.py:481
  32.3 0.8 collective-permute-done.12.refs_5_
  33.1 0.8 collective-permute-done.10.refs_3_
  33.8 0.8 collective-permute-done.14.refs_7_
  34.6 12.4 %shard_map.51 = (bf16[8,2,4,32,512]{4,3,2,1,0:T(8,128)(2,1)S(1)}, f32[256,128]{1,0:T(8,128)S(1)}, f32[8,4,2,8,128]{4,3,2,1,0:T(8,128)}) custom-call(f32[8,4,8,128]{3,2,1,0:T(8,128)S(1)} %bitcast.11, f32[8,16,512]{2,1,0:T(8,128)S(1)} %pad_maximum_fusion.2.refs_0_, f32[8,16,512]{2,1,0:T(8,128)S(1)} %collective-permute-done.8.refs_1_, ...), custom_call_target="tpu_custom_call" | custom-call | flops 12000000000 | tf_op jit(solution)/shard_map/pallas_call | solution.py:463
  47.0 3.8 %all-to-all-start.2 = ((f32[32,16,128]{2,1,0:T(8,128)}), f32[32,16,128]{2,1,0:T(8,128)S(1)}, u32[]{:S(2)}, u32[]{:S(2)}) async-start(f32[32,16,128]{2,1,0:T(8,128)} %bitcast.5), calls=%async_computation.2 | async-start | bytes 524288 | tf_op jit(solution)/shard_map/all_to_all | solution.py:542
  50.9 2.8 %shard_map.52 = f32[8,4,4,640]{3,2,1,0:T(4,128)} custom-call(bf16[8,2,4,32,512]{4,3,2,1,0:T(8,128)(2,1)S(1)} %get-tuple-element.35.samples_ref, f32[256,128]{1,0:T(8,128)S(1)} %get-tuple-element.36.vectors_ref), custom_call_target="tpu_custom_call" | custom-call | flops 2000000000 | tf_op jit(solution)/shard_map/pallas_call | solution.py:463
  53.7 7.6 %all-to-all-done.2 = f32[32,16,128]{2,1,0:T(8,128)S(1)} async-done(((f32[32,16,128]{2,1,0:T(8,128)}), f32[32,16,128]{2,1,0:T(8,128)S(1)}, u32[]{:S(2)}, u32[]{:S(2)}) %all-to-all-start.2) | async-done | bytes 262176 | tf_op jit(solution)/shard_map/all_to_all | solution.py:542
  61.3 0.6 shard_map.53
  61.9 0.1 collective-permute-start.16
  62.0 1.2 %collective-permute-done.16 = f32[72,128]{1,0:T(8,128)S(1)} collective-permute-done((f32[72,128]{1,0:T(8,128)S(1)}, f32[72,128]{1,0:T(8,128)S(1)}, u32[]{:S(2)}, u32[]{:S(2)}) %collective-permute-start.16) | collective-permute-done | bytes 36896 | tf_op jit(solution)/shard_map/ppermute | solution.py:481
  63.2 1.2 %collective-permute-start.19 = (f32[72,128]{1,0:T(8,128)S(1)}, f32[72,128]{1,0:T(8,128)S(1)}, u32[]{:S(2)}, u32[]{:S(2)}) collective-permute-start(f32[72,128]{1,0:T(8,128)S(1)} %add.36), channel_id=1, source_target_pairs={{0,6},{1,7},{2,4},{3,5},{4,2},{5,3},{6,0},{7,1},{8,14},{9,15},{10,... | collective-permute-start | bytes 110600 | tf_op jit(solution)/shard_map/ppermute | solution.py:481
  64.4 0.8 collective-permute-start.18
  65.2 1.6 %collective-permute-start.17 = (f32[72,128]{1,0:T(8,128)S(1)}, f32[72,128]{1,0:T(8,128)S(1)}, u32[]{:S(2)}, u32[]{:S(2)}) collective-permute-start(f32[72,128]{1,0:T(8,128)S(1)} %add.36), channel_id=1, source_target_pairs={{0,2},{1,3},{2,0},{3,1},{4,6},{5,7},{6,4},{7,5},{8,10},{9,11},{10,... | collective-permute-start | bytes 110600 | tf_op jit(solution)/shard_map/ppermute | solution.py:481
  66.7 2.6 %all-to-all-start.1 = ((f32[32,4,640]{2,1,0:T(4,128)}), f32[32,4,640]{2,1,0:T(4,128)S(1)}, u32[]{:S(2)}, u32[]{:S(2)}) async-start(f32[32,4,640]{2,1,0:T(4,128)} %bitcast.4), calls=%async_computation.1 | async-start | bytes 655360 | tf_op jit(solution)/shard_map/all_to_all | solution.py:542
  69.3 2.7 %collective-permute-start.15 = (f32[1,256,128]{2,1,0:T(8,128)S(1)}, f32[1,256,128]{2,1,0:T(8,128)S(1)}, u32[]{:S(2)}, u32[]{:S(2)}) collective-permute-start(f32[1,256,128]{2,1,0:T(8,128)S(1)} %bitcast.16), channel_id=1, source_target_pairs={{0,16},{4,20},{8,24},{12,28},{16,0},{20,4},{24,8},{28,12},{1,17},{... | collective-permute-start | bytes 393224 | tf_op jit(solution)/shard_map/ppermute | solution.py:481
  72.1 1.5 %collective-permute-start.23 = (f32[72,128]{1,0:T(8,128)S(1)}, f32[72,128]{1,0:T(8,128)S(1)}, u32[]{:S(2)}, u32[]{:S(2)}) collective-permute-start(f32[72,128]{1,0:T(8,128)S(1)} %add_add_fusion.1), channel_id=1, source_target_pairs={{0,24},{1,25},{2,26},{3,27},{4,28},{5,29},{6,30},{7,31},{8,16},{9,... | collective-permute-start | bytes 110600 | tf_op jit(solution)/shard_map/ppermute | solution.py:481
  73.5 1.6 %collective-permute-start.22 = (f32[72,128]{1,0:T(8,128)S(1)}, f32[72,128]{1,0:T(8,128)S(1)}, u32[]{:S(2)}, u32[]{:S(2)}) collective-permute-start(f32[72,128]{1,0:T(8,128)S(1)} %add_add_fusion.1), channel_id=1, source_target_pairs={{0,16},{1,17},{2,18},{3,19},{4,20},{5,21},{6,22},{7,23},{8,24},{9,... | collective-permute-start | bytes 110600 | tf_op jit(solution)/shard_map/ppermute | solution.py:481
  75.1 1.4 %collective-permute-start.21 = (f32[72,128]{1,0:T(8,128)S(1)}, f32[72,128]{1,0:T(8,128)S(1)}, u32[]{:S(2)}, u32[]{:S(2)}) collective-permute-start(f32[72,128]{1,0:T(8,128)S(1)} %add_add_fusion.1), channel_id=1, source_target_pairs={{0,8},{1,9},{2,10},{3,11},{4,12},{5,13},{6,14},{7,15},{8,0},{9,1},... | collective-permute-start | bytes 110600 | tf_op jit(solution)/shard_map/ppermute | solution.py:481
  76.5 11.2 %collective-permute-done.15 = f32[1,256,128]{2,1,0:T(8,128)S(1)} collective-permute-done((f32[1,256,128]{2,1,0:T(8,128)S(1)}, f32[1,256,128]{2,1,0:T(8,128)S(1)}, u32[]{:S(2)}, u32[]{:S(2)}) %collective-permute-start.15) | collective-permute-done | bytes 131104 | tf_op jit(solution)/shard_map/ppermute | solution.py:481
  87.8 0.1 collective-permute-start.20
  87.9 1.0 collective-permute-done.22
  88.9 0.1 collective-permute-start.24
  89.0 0.1 reshape.36.images_ref
  89.1 6.1 %collective-permute-done.20 = f32[2,256,128]{2,1,0:T(8,128)S(1)} collective-permute-done((f32[2,256,128]{2,1,0:T(8,128)S(1)}, f32[2,256,128]{2,1,0:T(8,128)S(1)}, u32[]{:S(2)}, u32[]{:S(2)}) %collective-permute-start.20) | collective-permute-done | bytes 262176 | tf_op jit(solution)/shard_map/ppermute | solution.py:481
  95.3 1.5 %collective-permute-start.25 = (f32[4,256,128]{2,1,0:T(8,128)S(1)}, f32[4,256,128]{2,1,0:T(8,128)S(1)}, u32[]{:S(2)}, u32[]{:S(2)}) collective-permute-start(f32[4,256,128]{2,1,0:T(8,128)S(1)} %pad_maximum_fusion.refs_0_), channel_id=1, source_target_pairs={{0,4},{4,0},{8,12},{12,8},{16,20},{20,16},{24,28},{28,24},{1,5},{5... | collective-permute-start | bytes 1572872 | tf_op jit(solution)/shard_map/ppermute | solution.py:481
  96.8 12.6 %shard_map.54 = (f32[128,128]{1,0:T(8,128)S(1)}, f32[128,128]{1,0:T(8,128)S(1)}, s32[1]{0:T(128)}) custom-call(f32[72,128]{1,0:T(8,128)S(1)} %add_add_fusion.gram_ref, f32[72,128]{1,0:T(8,128)S(1)} %collective-permute-done.24.other_ref), custom_call_target="tpu_custom_call" | custom-call | flops 12000000000 | tf_op jit(solution)/shard_map/pallas_call | solution.py:463
  110.1 0.0 copy-start
  110.1 0.0 copy-start.1
  110.1 0.2 conditional.1
  110.3 0.6 copy-done
  110.9 0.0 copy-done.1
  110.9 4.5 %shard_map.55 = (f32[32,512]{1,0:T(8,128)}, f32[256,128]{1,0:T(8,128)}) custom-call(f32[128,640]{1,0:T(8,128)S(1)} %reshape.36.images_ref, f32[128,128]{1,0:T(8,128)S(1)} %get-tuple-element.54.both_ref, f32[32,512]{1,0:T(8,128)S(1)} %copy-done, s32[32,512]{1,0:T(8,128)S(1)} %copy-done.1, f32[4,256,128]{2,1,0:T(8,128)S(1)} %pad_maximum_fusion.refs_0_, ...), custom_call_target="tpu_custom_call" | custom-call | flops 5000000000 | tf_op jit(solution)/shard_map/pallas_call | solution.py:463
  (22 shorter events, 0.2 us)
Async XLA Ops:
  2.5 8.0 %collective-permute-start.5 = (f32[1,32,512]{2,1,0:T(8,128)}, f32[1,32,512]{2,1,0:T(8,128)S(1)}, u32[]{:S(2)}, u32[]{:S(2)}) collective-permute-start(f32[1,32,512]{2,1,0:T(8,128)} %bitcast.12), channel_id=1, source_target_pairs={{0,16},{1,17},{2,18},{3,19},{4,20},{5,21},{6,22},{7,23},{8,24},{9,... | collective-permute-start | bytes 196616 | tf_op jit(solution)/shard_map/ppermute | solution.py:481
  6.6 12.7 %all-to-all-start = ((f32[32,8,128]{2,1,0:T(8,128)}), f32[32,8,128]{2,1,0:T(8,128)S(1)}, u32[]{:S(2)}, u32[]{:S(2)}) async-start(f32[32,8,128]{2,1,0:T(8,128)} %bitcast.15), calls=%async_computation | async-start | bytes 262144 | tf_op jit(solution)/shard_map/all_to_all | solution.py:542
  11.3 7.1 %collective-permute-start.6 = (f32[2,32,512]{2,1,0:T(8,128)S(1)}, f32[2,32,512]{2,1,0:T(8,128)S(1)}, u32[]{:S(2)}, u32[]{:S(2)}) collective-permute-start(f32[2,32,512]{2,1,0:T(8,128)S(1)} %pad_maximum_fusion.5), channel_id=1, source_target_pairs={{0,8},{1,9},{2,10},{3,11},{4,12},{5,13},{6,14},{7,15},{8,0},{9,1},... | collective-permute-start | bytes 393224 | tf_op jit(solution)/shard_map/ppermute | solution.py:481
  19.4 5.5 %collective-permute-start.7 = (f32[4,16,512]{2,1,0:T(8,128)S(1)}, f32[4,16,512]{2,1,0:T(8,128)S(1)}, u32[]{:S(2)}, u32[]{:S(2)}) collective-permute-start(f32[4,16,512]{2,1,0:T(8,128)S(1)} %get-tuple-element.53), channel_id=1, source_target_pairs={{0,4},{1,5},{2,6},{3,7},{4,0},{5,1},{6,2},{7,3},{8,12},{9,13},{10,... | collective-permute-start | bytes 393224 | tf_op jit(solution)/shard_map/ppermute | solution.py:481
  21.0 5.2 %collective-permute-start.11 = (f32[4,16,512]{2,1,0:T(8,128)S(1)}, f32[4,16,512]{2,1,0:T(8,128)S(1)}, u32[]{:S(2)}, u32[]{:S(2)}) collective-permute-start(f32[4,16,512]{2,1,0:T(8,128)S(1)} %get-tuple-element.52), channel_id=1, source_target_pairs={{0,2},{1,3},{2,0},{3,1},{4,6},{5,7},{6,4},{7,5},{8,10},{9,11},{10,... | collective-permute-start | bytes 393224 | tf_op jit(solution)/shard_map/ppermute | solution.py:481
  24.9 7.4 %collective-permute-start.8 = (f32[8,16,512]{2,1,0:T(8,128)S(1)}, f32[8,16,512]{2,1,0:T(8,128)S(1)}, u32[]{:S(2)}, u32[]{:S(2)}) collective-permute-start(f32[8,16,512]{2,1,0:T(8,128)S(1)} %pad_maximum_fusion.2.refs_0_), channel_id=1, source_target_pairs={{0,2},{1,3},{2,0},{3,1},{4,6},{5,7},{6,4},{7,5},{8,10},{9,11},{10,... | collective-permute-start | bytes 786440 | tf_op jit(solution)/shard_map/ppermute | solution.py:481
  26.2 6.8 %collective-permute-start.12 = (f32[8,16,512]{2,1,0:T(8,128)S(1)}, f32[8,16,512]{2,1,0:T(8,128)S(1)}, u32[]{:S(2)}, u32[]{:S(2)}) collective-permute-start(f32[8,16,512]{2,1,0:T(8,128)S(1)} %pad_maximum_fusion.3.refs_4_), channel_id=1, source_target_pairs={{0,4},{1,5},{2,6},{3,7},{4,0},{5,1},{6,2},{7,3},{8,12},{9,13},{10,... | collective-permute-start | bytes 786440 | tf_op jit(solution)/shard_map/ppermute | solution.py:481
  27.8 5.3 %collective-permute-start.9 = (f32[8,16,512]{2,1,0:T(8,128)S(1)}, f32[8,16,512]{2,1,0:T(8,128)S(1)}, u32[]{:S(2)}, u32[]{:S(2)}) collective-permute-start(f32[8,16,512]{2,1,0:T(8,128)S(1)} %pad_maximum_fusion.2.refs_0_), channel_id=1, source_target_pairs={{0,1},{1,0},{2,3},{3,2},{4,5},{5,4},{6,7},{7,6},{8,9},{9,8},{10,11... | collective-permute-start | bytes 786440 | tf_op jit(solution)/shard_map/ppermute | solution.py:481
  27.8 5.3 %collective-permute-start.13 = (f32[8,16,512]{2,1,0:T(8,128)S(1)}, f32[8,16,512]{2,1,0:T(8,128)S(1)}, u32[]{:S(2)}, u32[]{:S(2)}) collective-permute-start(f32[8,16,512]{2,1,0:T(8,128)S(1)} %pad_maximum_fusion.3.refs_4_), channel_id=1, source_target_pairs={{0,1},{1,0},{2,3},{3,2},{4,5},{5,4},{6,7},{7,6},{8,9},{9,8},{10,11... | collective-permute-start | bytes 786440 | tf_op jit(solution)/shard_map/ppermute | solution.py:481
  32.3 1.5 %collective-permute-start.10 = (f32[8,16,512]{2,1,0:T(8,128)S(1)}, f32[8,16,512]{2,1,0:T(8,128)S(1)}, u32[]{:S(2)}, u32[]{:S(2)}) collective-permute-start(f32[8,16,512]{2,1,0:T(8,128)S(1)} %collective-permute-done.8.refs_1_), channel_id=1, source_target_pairs={{0,1},{1,0},{2,3},{3,2},{4,5},{5,4},{6,7},{7,6},{8,9},{9,8},{10,11... | collective-permute-start | bytes 786440 | tf_op jit(solution)/shard_map/ppermute | solution.py:481
  33.1 1.5 %collective-permute-start.14 = (f32[8,16,512]{2,1,0:T(8,128)S(1)}, f32[8,16,512]{2,1,0:T(8,128)S(1)}, u32[]{:S(2)}, u32[]{:S(2)}) collective-permute-start(f32[8,16,512]{2,1,0:T(8,128)S(1)} %collective-permute-done.12.refs_5_), channel_id=1, source_target_pairs={{0,1},{1,0},{2,3},{3,2},{4,5},{5,4},{6,7},{7,6},{8,9},{9,8},{10,11... | collective-permute-start | bytes 786440 | tf_op jit(solution)/shard_map/ppermute | solution.py:481
  47.0 14.3 %all-to-all-start.2 = ((f32[32,16,128]{2,1,0:T(8,128)}), f32[32,16,128]{2,1,0:T(8,128)S(1)}, u32[]{:S(2)}, u32[]{:S(2)}) async-start(f32[32,16,128]{2,1,0:T(8,128)} %bitcast.5), calls=%async_computation.2 | async-start | bytes 524288 | tf_op jit(solution)/shard_map/all_to_all | solution.py:542
  61.9 1.3 %collective-permute-start.16 = (f32[72,128]{1,0:T(8,128)S(1)}, f32[72,128]{1,0:T(8,128)S(1)}, u32[]{:S(2)}, u32[]{:S(2)}) collective-permute-start(f32[72,128]{1,0:T(8,128)S(1)} %get-tuple-element.41), channel_id=1, source_target_pairs={{0,1},{1,0},{2,3},{3,2},{4,5},{5,4},{6,7},{7,6},{8,9},{9,8},{10,11... | collective-permute-start | bytes 110600 | tf_op jit(solution)/shard_map/ppermute | solution.py:481
  63.2 8.8 %collective-permute-start.19 = (f32[72,128]{1,0:T(8,128)S(1)}, f32[72,128]{1,0:T(8,128)S(1)}, u32[]{:S(2)}, u32[]{:S(2)}) collective-permute-start(f32[72,128]{1,0:T(8,128)S(1)} %add.36), channel_id=1, source_target_pairs={{0,6},{1,7},{2,4},{3,5},{4,2},{5,3},{6,0},{7,1},{8,14},{9,15},{10,... | collective-permute-start | bytes 110600 | tf_op jit(solution)/shard_map/ppermute | solution.py:481
  64.4 7.6 %collective-permute-start.18 = (f32[72,128]{1,0:T(8,128)S(1)}, f32[72,128]{1,0:T(8,128)S(1)}, u32[]{:S(2)}, u32[]{:S(2)}) collective-permute-start(f32[72,128]{1,0:T(8,128)S(1)} %add.36), channel_id=1, source_target_pairs={{0,4},{1,5},{2,6},{3,7},{4,0},{5,1},{6,2},{7,3},{8,12},{9,13},{10,... | collective-permute-start | bytes 110600 | tf_op jit(solution)/shard_map/ppermute | solution.py:481
  65.2 6.9 %collective-permute-start.17 = (f32[72,128]{1,0:T(8,128)S(1)}, f32[72,128]{1,0:T(8,128)S(1)}, u32[]{:S(2)}, u32[]{:S(2)}) collective-permute-start(f32[72,128]{1,0:T(8,128)S(1)} %add.36), channel_id=1, source_target_pairs={{0,2},{1,3},{2,0},{3,1},{4,6},{5,7},{6,4},{7,5},{8,10},{9,11},{10,... | collective-permute-start | bytes 110600 | tf_op jit(solution)/shard_map/ppermute | solution.py:481
  66.7 22.2 %all-to-all-start.1 = ((f32[32,4,640]{2,1,0:T(4,128)}), f32[32,4,640]{2,1,0:T(4,128)S(1)}, u32[]{:S(2)}, u32[]{:S(2)}) async-start(f32[32,4,640]{2,1,0:T(4,128)} %bitcast.4), calls=%async_computation.1 | async-start | bytes 655360 | tf_op jit(solution)/shard_map/all_to_all | solution.py:542
  69.3 18.4 %collective-permute-start.15 = (f32[1,256,128]{2,1,0:T(8,128)S(1)}, f32[1,256,128]{2,1,0:T(8,128)S(1)}, u32[]{:S(2)}, u32[]{:S(2)}) collective-permute-start(f32[1,256,128]{2,1,0:T(8,128)S(1)} %bitcast.16), channel_id=1, source_target_pairs={{0,16},{4,20},{8,24},{12,28},{16,0},{20,4},{24,8},{28,12},{1,17},{... | collective-permute-start | bytes 393224 | tf_op jit(solution)/shard_map/ppermute | solution.py:481
  72.1 15.8 %collective-permute-start.23 = (f32[72,128]{1,0:T(8,128)S(1)}, f32[72,128]{1,0:T(8,128)S(1)}, u32[]{:S(2)}, u32[]{:S(2)}) collective-permute-start(f32[72,128]{1,0:T(8,128)S(1)} %add_add_fusion.1), channel_id=1, source_target_pairs={{0,24},{1,25},{2,26},{3,27},{4,28},{5,29},{6,30},{7,31},{8,16},{9,... | collective-permute-start | bytes 110600 | tf_op jit(solution)/shard_map/ppermute | solution.py:481
  73.5 15.3 %collective-permute-start.22 = (f32[72,128]{1,0:T(8,128)S(1)}, f32[72,128]{1,0:T(8,128)S(1)}, u32[]{:S(2)}, u32[]{:S(2)}) collective-permute-start(f32[72,128]{1,0:T(8,128)S(1)} %add_add_fusion.1), channel_id=1, source_target_pairs={{0,16},{1,17},{2,18},{3,19},{4,20},{5,21},{6,22},{7,23},{8,24},{9,... | collective-permute-start | bytes 110600 | tf_op jit(solution)/shard_map/ppermute | solution.py:481
  75.1 13.7 %collective-permute-start.21 = (f32[72,128]{1,0:T(8,128)S(1)}, f32[72,128]{1,0:T(8,128)S(1)}, u32[]{:S(2)}, u32[]{:S(2)}) collective-permute-start(f32[72,128]{1,0:T(8,128)S(1)} %add_add_fusion.1), channel_id=1, source_target_pairs={{0,8},{1,9},{2,10},{3,11},{4,12},{5,13},{6,14},{7,15},{8,0},{9,1},... | collective-permute-start | bytes 110600 | tf_op jit(solution)/shard_map/ppermute | solution.py:481
  87.8 7.4 %collective-permute-start.20 = (f32[2,256,128]{2,1,0:T(8,128)S(1)}, f32[2,256,128]{2,1,0:T(8,128)S(1)}, u32[]{:S(2)}, u32[]{:S(2)}) collective-permute-start(f32[2,256,128]{2,1,0:T(8,128)S(1)} %pad_maximum_fusion.4), channel_id=1, source_target_pairs={{0,8},{4,12},{8,0},{12,4},{16,24},{20,28},{24,16},{28,20},{1,9},{5... | collective-permute-start | bytes 786440 | tf_op jit(solution)/shard_map/ppermute | solution.py:481
  88.9 6.4 %collective-permute-start.24 = (f32[72,128]{1,0:T(8,128)S(1)}, f32[72,128]{1,0:T(8,128)S(1)}, u32[]{:S(2)}, u32[]{:S(2)}) collective-permute-start(f32[72,128]{1,0:T(8,128)S(1)} %add_add_fusion.gram_ref), channel_id=1, source_target_pairs={{0,1},{1,0},{2,3},{3,2},{4,5},{5,4},{6,7},{7,6},{8,9},{9,8},{10,11... | collective-permute-start | bytes 110600 | tf_op jit(solution)/shard_map/ppermute | solution.py:481
  95.3 15.1 %collective-permute-start.25 = (f32[4,256,128]{2,1,0:T(8,128)S(1)}, f32[4,256,128]{2,1,0:T(8,128)S(1)}, u32[]{:S(2)}, u32[]{:S(2)}) collective-permute-start(f32[4,256,128]{2,1,0:T(8,128)S(1)} %pad_maximum_fusion.refs_0_), channel_id=1, source_target_pairs={{0,4},{4,0},{8,12},{12,8},{16,20},{20,16},{24,28},{28,24},{1,5},{5... | collective-permute-start | bytes 1572872 | tf_op jit(solution)/shard_map/ppermute | solution.py:481
  110.1 0.8 copy-start
  110.1 0.9 copy-start.1

commit v7 on v6

--- a/solution.py
+++ b/solution.py
@@ -210,8 +210,28 @@
         send_ref[:, g, part] = joined.reshape(tiles, per_tile, lanes)
 
 
+def store_by_groups(normal_ref, group_ref):
+    groups, count, lanes = group_ref.shape
+    rows, channels = normal_ref.shape
+    chg = channels // groups
+    fold = lanes // chg
+    cols = rows // KER
+    deep = KER // fold
+    me = lax.axis_index("coil")
+    parts = [
+        [normal_ref[pl.ds(k * KER + f, deep, stride=fold), :] for f in range(fold)]
+        for k in range(cols)
+    ]
+    for g in range(groups):
+        joined = [
+            jnp.concatenate([part[:, g * chg : (g + 1) * chg] for part in parts[k]], axis=1)
+            for k in range(cols)
+        ]
+        group_ref[lax.bitwise_xor(me, g)] = jnp.concatenate(joined, axis=0)
+
+
 def passes_kernel(orders, basis_ref, *refs):
-    *pieces, samples_ref, normal_ref, send_ref, wide_ref, moved_ref = refs
+    *pieces, samples_ref, normal_ref, send_ref, group_ref, wide_ref, moved_ref = refs
     tiles, _, groups, chg, tile = samples_ref.shape
     me = lax.axis_index("rows") * groups + lax.axis_index("coil")
     for (start, order), piece_ref in zip(orders, pieces):
@@ -245,6 +265,7 @@
     normal = normal_of(images_of(normal, samples_ref, wide_ref), samples_ref, moved_ref)
     normal_ref[...] = normal
     store_by_rows(normal, send_ref, 1)
+    store_by_groups(normal_ref, group_ref)
 
 
 def images_kernel(samples_ref, vectors_ref, send_ref, wide_ref):
@@ -294,12 +315,12 @@
     return at_row, at_col
 
 
-def gram_kernel(cols, per_tile, received_ref, kept_ref, given_ref, rows_ref):
+def gram_kernel(cols, per_tile, received_ref, kept_ref, given_ref, turned_ref):
     turned = gather_turned(received_ref, cols, per_tile, 0)
     first = exact(turned, turned, ((1,), (1,)))
     turned = gather_turned(received_ref, cols, per_tile, 1)
     second = exact(turned, turned, ((1,), (1,)))
-    rows_ref[...] = turned.T
+    turned_ref[...] = turned
     at_row, at_col = square(first.shape[0])
     packed = jnp.where(at_row >= at_col, first, second)
     line = jnp.sum(jnp.where(at_row == at_col, second, 0.0), axis=0, keepdims=True)
@@ -409,17 +430,45 @@
     sound_ref[0] = 1 - worst
 
 
-def rows_kernel(rows_ref, inverse_ref, gram_ref):
-    rows = exact(rows_ref[...], inverse_ref[...], ((1,), (1,)))
-    gram_ref[...] = exact(rows, rows, ((0,), (0,)))
+def rows_kernel(turned_ref, inverse_ref, gram_ref):
+    turned = exact(inverse_ref[...], turned_ref[...])
+    gram_ref[...] = exact(turned, turned, ((1,), (1,)))
 
 
 def again_kernel(gram_ref, inverse_ref, both_ref):
     both_ref[...] = exact(inverse_factor(gram_ref[...]), inverse_ref[...])
 
 
-def last_kernel(cols, orders, images_ref, both_ref, kspace_hbm, mask_hbm, *refs):
-    *pieces, recovered_ref, basis_ref, kspace_ref, mask_ref, sems = refs
+def moved_columns(values, order):
+    devices = len(order)
+    at_row, at_col = square(values.shape[0])
+    me = lax.axis_index("rows") * lax.axis_size("coil") + lax.axis_index("coil")
+    slot = at_col % devices
+    mask = jnp.zeros_like(slot)
+    bit = 1
+    while bit < devices:
+        mask = mask | jnp.where(slot & bit != 0, order[bit], 0)
+        bit *= 2
+    source = at_col - slot + lax.bitwise_xor(mask, jnp.full_like(mask, me))
+    return exact(values, (at_row == source).astype(jnp.float32))
+
+
+def last_kernel(
+    cols,
+    order,
+    images_ref,
+    both_ref,
+    kspace_hbm,
+    mask_hbm,
+    near_ref,
+    far_ref,
+    recovered_ref,
+    basis_ref,
+    kspace_ref,
+    mask_ref,
+    vectors_ref,
+    sems,
+):
     fetches = [
         pltpu.make_async_copy(kspace_hbm, kspace_ref, sems.at[0]),
         pltpu.make_async_copy(mask_hbm, mask_ref, sems.at[1]),
@@ -430,28 +479,42 @@
     count, reach = images_ref.shape
     devices = count // cols
     at_row, at_col = square(count)
-    order = ((at_row // devices == at_col % cols) & (at_row % devices == at_col // cols)).astype(
+    turn = ((at_row // devices == at_col % cols) & (at_row % devices == at_col // cols)).astype(
         jnp.float32
     )
-    images = exact(exact(both, order), images_ref[...])
+    images = exact(exact(both, turn), images_ref[...])
     images_high, images_low = split(images)
     stacked = jnp.concatenate([images_high, images_low], axis=0)
     chg, tile = kspace_ref.shape
-    me = lax.axis_index("rows")
-    estimate = jnp.zeros((chg, tile), jnp.float32)
-    for order, rows_ref in zip(orders, pieces):
-        for slot, mask in enumerate(order):
-            vectors = dot3(rows_ref[slot], both, ((1,), (1,)))
-            if mask == 0:
-                basis_ref[...] = vectors
-            high, low = split(vectors)
-            projected = dot(jnp.concatenate([high, high], axis=1), stacked) + dot(low, images_high)
-            per_tile = vectors.shape[0] // chg
-            total = projected[:chg]
-            for j in range(1, per_tile):
-                total = total + pltpu.roll(projected[j * chg : (j + 1) * chg], j, 1)
-            total = pltpu.roll(total, lax.bitwise_xor(me, mask) * per_tile, 1)
-            estimate = estimate + total[:, reach - tile :]
+    lanes = near_ref.shape[1]
+    deep = KER * chg // lanes
+    step = cols * deep
+    factor = moved_columns(both, order)
+    estimate = jnp.zeros((chg, reach), jnp.float32)
+    for a in range(0, deep, 2):
+        turned = [
+            jnp.concatenate(
+                [
+                    ref[pl.ds(k * deep + a + i, ref.shape[0] // step, stride=step), :]
+                    for k in range(cols)
+                    for ref in (near_ref, far_ref)
+                ],
+                axis=0,
+            )
+            for i in range(2)
+        ]
+        vectors = dot3(jnp.concatenate(turned, axis=1), factor, ((0,), (1,)))
+        vectors_ref[a * lanes : (a + 2) * lanes, :] = vectors
+        high, low = split(vectors)
+        projected = dot(jnp.concatenate([high, high], axis=1), stacked) + dot(low, images_high)
+        for i in range(2 * lanes // chg):
+            j = a * lanes // chg + i
+            part = projected[i * chg : (i + 1) * chg]
+            estimate = estimate + (pltpu.roll(part, j, 1) if j else part)
+    owned = basis_ref.shape[0]
+    start = pl.multiple_of(lax.axis_index("rows") * owned, owned)
+    basis_ref[...] = vectors_ref[pl.ds(start, owned), :]
+    estimate = estimate[:, reach - tile :]
     for fetch in fetches:
         fetch.wait()
     estimate = estimate / KER
@@ -542,27 +605,32 @@
     return lax.all_to_all(pieces, axes, 0, 0, tiled=True)
 
 
-def total_and_rows(kept, given, by_row, images, tiles, devices):
+def gather_group(group, devices):
+    groups = group.shape[0]
+    parts = [group[:1]]
+    parts += [exchange(group[s : s + 1], devices, s, AXES) for s in range(1, groups)]
+    near = jnp.concatenate(parts, axis=0)
+    return gather_round(near, list(range(groups)), [devices // 2], devices, AXES)
+
+
+def total_beside(kept, given, near, order, groups, devices):
     total = kept + exchange(given, devices, 1, AXES)
-    near, order = by_row[None], [0]
-    mask = tiles // 2
+    mask = devices // 4
     for partners in rounds_of(2, devices):
         terms = [exchange(total, devices, way, AXES) for way in partners]
-        if mask > 1:
-            near, order = gather_round(near, order, [mask], tiles, "rows")
-            mask //= 2
         total = total + terms[0]
         if len(terms) == 3:
             total = total + (terms[1] + terms[2])
-        near = after(near, total)
-    while mask > 1:
-        near, order = gather_round(near, order, [mask], tiles, "rows")
+        if mask > groups:
+            near, order = gather_round(near, order, [mask], devices, AXES)
+            mask //= 2
+    while mask > groups:
+        near, order = gather_round(near, order, [mask], devices, AXES)
         mask //= 2
     other = exchange(total, devices, 1, AXES)
     near, total, other = lax.optimization_barrier((near, total, other))
-    far = exchange(near, tiles, 1, "rows")
-    pieces = [(near, order), (far, [m ^ 1 for m in order])]
-    return (total, other), pieces, to_all(images)
+    far = exchange(near, devices, groups, AXES)
+    return (total, other), near, far, order + [m ^ groups for m in order]
 
 
 def column_shards(kspace, sample_mask, start_basis):
@@ -599,12 +667,13 @@
     orders = [(start, order) for start, half in zip(starts, halves) for _, order in half]
     wide = pltpu.VMEM((rows, positions), f32)
     moved = pltpu.VMEM((2 * rows, positions), bf16)
-    samples, normal, send = call(
+    samples, normal, send, group = call(
         functools.partial(passes_kernel, orders),
         [
             ((tiles, 2, groups, chg, tile), bf16),
             ((rows, channels), f32),
             ((tiles, groups, 2, per_tile, lanes), f32),
+            ((groups, rows * chg // lanes, lanes), f32),
         ],
         basis_parts.reshape(tiles, groups, per_tile, lanes),
         *[piece for half in halves for piece, _ in half],
@@ -621,23 +690,23 @@
         scratch=[wide],
         micros=2,
     )
-    received = after(received, images)
+    near, order = gather_group(group, devices)
+    received = after(received, images, near)
     half = ((rank // 2 + SUB, rank), f32)
-    kept, given, by_row = call(
+    kept, given, turned = call(
         functools.partial(gram_kernel, cols, per_tile),
-        [half, half, ((owned, rank), f32)],
+        [half, half, ((rank, owned), f32)],
         received.reshape(devices * 2 * per_tile, lanes),
     )
-    gram, pieces, images = total_and_rows(
-        kept, given, by_row, images.reshape(devices, cols, reach), tiles, devices
-    )
+    images = to_all(images.reshape(devices, cols, reach))
+    gram, near, far, order = total_beside(kept, given, near, order, groups, devices)
     whole = ((rank, rank), f32)
     first, both, sound = call(
         factors_kernel, [whole, whole, ((1,), jnp.int32)], *gram, scalars=1, micros=12
     )
 
     def again():
-        (gram,) = call(rows_kernel, [whole], by_row, first)
+        (gram,) = call(rows_kernel, [whole], turned, first)
         mask = 1
         while mask < devices:
             gram = gram + exchange(gram, devices, mask, AXES)
@@ -646,16 +715,18 @@
 
     both = lax.cond(sound[0] == 1, lambda: both, again)
     recovered, basis = call(
-        functools.partial(last_kernel, cols, [order for _, order in pieces]),
+        functools.partial(last_kernel, cols, order),
         [((chg, tile), f32), ((owned, rank), f32)],
         images.reshape(rank, reach),
         both,
         kspace,
         sample_mask,
-        *[piece for piece, _ in pieces],
+        near.reshape(-1, lanes),
+        far.reshape(-1, lanes),
         scratch=[
             pltpu.VMEM((chg, tile), f32),
             pltpu.VMEM((chg, tile), sample_mask.dtype),
+            pltpu.VMEM((KER * chg, rank), f32),
             pltpu.SemaphoreType.DMA((2,)),
         ],
         far=(2, 3),

time: 116 us -> 114 us (0.983)
  waiting for transfers between devices: 41.2 us -> 33.6 us
  starting transfers between devices: 35.1 us -> 40.3 us
    all_to_all x3, waiting for transfers between devices: 7.58 us -> 0.01 us  [to_all(): return lax.all_to_all(pieces, axes, 0, 0, tiled=True)]
    ppermute x21 -> x24, starting transfers between devices: 24.8 us -> 27.6 us  [exchange(): return lax.ppermute(block, axes, [(i, i ^ mask) for i in range(devices)])]
    all_to_all x3, starting transfers between devices: 10.3 us -> 12.7 us  [to_all(): return lax.all_to_all(pieces, axes, 0, 0, tiled=True)]
    ppermute x21 -> x24, waiting for transfers between devices: 33.6 us -> 33.6 us  [exchange(): return lax.ppermute(block, axes, [(i, i ^ mask) for i in range(devices)])]
  transfers between devices with their start and end apart: 24 -> 27, of which waited for: 11 -> 12; matrix products, arithmetic and copies ran while one was open for 2% -> 2% of each run, Pallas kernels for 13% -> 14%
where the time goes in v7:
time: 114 us
  starting transfers between devices  40.3 us (35%)
  Pallas kernels  35.3 us (31%)
  waiting for transfers between devices  33.6 us (29%)
  other arithmetic  1.78 us (2%)
  between operations  1.71 us (2%)
    pallas_call x6, Pallas kernels, call(): pl.pallas_call(kernel, out_shape=[jax.ShapeDtypeStruct(shape, kind) for s...  35.3 us
    ppermute x24, waiting for transfers between devices, exchange(): return lax.ppermute(block, axes, [(i, i ^ mask) for i in range(devices)])  33.6 us
    ppermute x24, starting transfers between devices, exchange(): return lax.ppermute(block, axes, [(i, i ^ mask) for i in range(devices)])  27.6 us
    all_to_all x3, starting transfers between devices, to_all(): return lax.all_to_all(pieces, axes, 0, 0, tiled=True)  12.7 us
  transfers between devices with their start and end apart: 27, of which 12 were waited for; matrix products, arithmetic and copies ran while one was open for 2% of the time, Pallas kernels for 14%

profile of v7, /device:TPU:0, one launch (start us, length us, event | category | flops | bytes accessed | tf_op | source)
XLA Modules:
  0.0 113.8 jit_solution(362863297299800089)
XLA Ops:
  0.6 1.9 %shard_map.50 = (f32[32,512]{1,0:T(8,128)}, f32[256,128]{1,0:T(8,128)}) custom-call(f32[32,512]{1,0:T(8,128)} %kspace_hbm.3, s32[32,512]{1,0:T(8,128)} %mask_hbm.3, f32[256,128]{1,0:T(8,128)} %bitcast.19), custom_call_target="tpu_custom_call" | custom-call | flops 1000000000 | tf_op jit(solution)/shard_map/pallas_call | solution.py:526
  2.5 4.1 %collective-permute-start.5 = (f32[1,32,512]{2,1,0:T(8,128)}, f32[1,32,512]{2,1,0:T(8,128)S(1)}, u32[]{:S(2)}, u32[]{:S(2)}) collective-permute-start(f32[1,32,512]{2,1,0:T(8,128)} %bitcast.15), channel_id=1, source_target_pairs={{0,16},{1,17},{2,18},{3,19},{4,20},{5,21},{6,22},{7,23},{8,24},{9,... | collective-permute-start | bytes 196616 | tf_op jit(solution)/shard_map/ppermute | solution.py:544
  6.6 3.8 %all-to-all-start = ((f32[32,8,128]{2,1,0:T(8,128)}), f32[32,8,128]{2,1,0:T(8,128)S(1)}, u32[]{:S(2)}, u32[]{:S(2)}) async-start(f32[32,8,128]{2,1,0:T(8,128)} %bitcast.18), calls=%async_computation | async-start | bytes 262144 | tf_op jit(solution)/shard_map/all_to_all | solution.py:605
  10.5 0.0 collective-permute-done.5
  10.5 0.8 pad_maximum_fusion.3
  11.3 1.8 %collective-permute-start.6 = (f32[2,32,512]{2,1,0:T(8,128)S(1)}, f32[2,32,512]{2,1,0:T(8,128)S(1)}, u32[]{:S(2)}, u32[]{:S(2)}) collective-permute-start(f32[2,32,512]{2,1,0:T(8,128)S(1)} %pad_maximum_fusion.3), channel_id=1, source_target_pairs={{0,8},{1,9},{2,10},{3,11},{4,12},{5,13},{6,14},{7,15},{8,0},{9,1},... | collective-permute-start | bytes 393224 | tf_op jit(solution)/shard_map/ppermute | solution.py:544
  13.2 5.3 %collective-permute-done.6 = f32[2,32,512]{2,1,0:T(8,128)S(1)} collective-permute-done((f32[2,32,512]{2,1,0:T(8,128)S(1)}, f32[2,32,512]{2,1,0:T(8,128)S(1)}, u32[]{:S(2)}, u32[]{:S(2)}) %collective-permute-start.6) | collective-permute-done | bytes 131104 | tf_op jit(solution)/shard_map/ppermute | solution.py:544
  18.5 0.9 pad_maximum_fusion
  19.4 1.6 %collective-permute-start.7 = (f32[4,16,512]{2,1,0:T(8,128)S(1)}, f32[4,16,512]{2,1,0:T(8,128)S(1)}, u32[]{:S(2)}, u32[]{:S(2)}) collective-permute-start(f32[4,16,512]{2,1,0:T(8,128)S(1)} %get-tuple-element.51), channel_id=1, source_target_pairs={{0,4},{1,5},{2,6},{3,7},{4,0},{5,1},{6,2},{7,3},{8,12},{9,13},{10,... | collective-permute-start | bytes 393224 | tf_op jit(solution)/shard_map/ppermute | solution.py:544
  21.0 1.5 %collective-permute-start.11 = (f32[4,16,512]{2,1,0:T(8,128)S(1)}, f32[4,16,512]{2,1,0:T(8,128)S(1)}, u32[]{:S(2)}, u32[]{:S(2)}) collective-permute-start(f32[4,16,512]{2,1,0:T(8,128)S(1)} %get-tuple-element.50), channel_id=1, source_target_pairs={{0,2},{1,3},{2,0},{3,1},{4,6},{5,7},{6,4},{7,5},{8,10},{9,11},{10,... | collective-permute-start | bytes 393224 | tf_op jit(solution)/shard_map/ppermute | solution.py:544
  22.5 2.4 %collective-permute-done.7 = f32[4,16,512]{2,1,0:T(8,128)S(1)} collective-permute-done((f32[4,16,512]{2,1,0:T(8,128)S(1)}, f32[4,16,512]{2,1,0:T(8,128)S(1)}, u32[]{:S(2)}, u32[]{:S(2)}) %collective-permute-start.7) | collective-permute-done | bytes 131104 | tf_op jit(solution)/shard_map/ppermute | solution.py:544
  24.9 1.3 %collective-permute-start.8 = (f32[8,16,512]{2,1,0:T(8,128)S(1)}, f32[8,16,512]{2,1,0:T(8,128)S(1)}, u32[]{:S(2)}, u32[]{:S(2)}) collective-permute-start(f32[8,16,512]{2,1,0:T(8,128)S(1)} %pad_maximum_fusion.1.refs_0_), channel_id=1, source_target_pairs={{0,2},{1,3},{2,0},{3,1},{4,6},{5,7},{6,4},{7,5},{8,10},{9,11},{10,... | collective-permute-start | bytes 786440 | tf_op jit(solution)/shard_map/ppermute | solution.py:544
  26.2 1.5 %collective-permute-start.12 = (f32[8,16,512]{2,1,0:T(8,128)S(1)}, f32[8,16,512]{2,1,0:T(8,128)S(1)}, u32[]{:S(2)}, u32[]{:S(2)}) collective-permute-start(f32[8,16,512]{2,1,0:T(8,128)S(1)} %pad_maximum_fusion.2.refs_4_), channel_id=1, source_target_pairs={{0,4},{1,5},{2,6},{3,7},{4,0},{5,1},{6,2},{7,3},{8,12},{9,13},{10,... | collective-permute-start | bytes 786440 | tf_op jit(solution)/shard_map/ppermute | solution.py:544
  27.8 0.5 collective-permute-start.13
  28.3 4.0 %collective-permute-done.8.refs_1_ = f32[8,16,512]{2,1,0:T(8,128)S(1)} collective-permute-done((f32[8,16,512]{2,1,0:T(8,128)S(1)}, f32[8,16,512]{2,1,0:T(8,128)S(1)}, u32[]{:S(2)}, u32[]{:S(2)}) %collective-permute-start.8) | collective-permute-done | bytes 262176 | tf_op jit(solution)/shard_map/ppermute | solution.py:544
  32.3 0.8 collective-permute-done.12.refs_5_
  33.1 0.8 collective-permute-done.10.refs_3_
  33.8 0.8 collective-permute-done.14.refs_7_
  34.6 12.5 %shard_map.51 = (bf16[8,2,4,32,512]{4,3,2,1,0:T(8,128)(2,1)S(1)}, f32[256,128]{1,0:T(8,128)S(1)}, f32[8,4,2,8,128]{4,3,2,1,0:T(8,128)}, f32[4,64,128]{2,1,0:T(8,128)S(1)}) custom-call(f32[8,4,8,128]{3,2,1,0:T(8,128)S(1)} %bitcast.12, f32[8,16,512]{2,1,0:T(8,128)S(1)} %pad_maximum_fusion.1.refs_0_, f32[8,16,512]{2,1,0:T(8,128)S(1)} %collective-permute-done.8.refs_1_, ...), custom_call_target="tpu_custom_call" | custom-call | flops 12000000000 | tf_op jit(solution)/shard_map/pallas_call | solution.py:526
  47.1 3.8 %all-to-all-start.2 = ((f32[32,16,128]{2,1,0:T(8,128)}), f32[32,16,128]{2,1,0:T(8,128)S(1)}, u32[]{:S(2)}, u32[]{:S(2)}) async-start(f32[32,16,128]{2,1,0:T(8,128)} %bitcast.5), calls=%async_computation.2 | async-start | bytes 524288 | tf_op jit(solution)/shard_map/all_to_all | solution.py:605
  51.0 1.4 %collective-permute-start.17 = (f32[1,64,128]{2,1,0:T(8,128)S(1)}, f32[1,64,128]{2,1,0:T(8,128)S(1)}, u32[]{:S(2)}, u32[]{:S(2)}) collective-permute-start(f32[1,64,128]{2,1,0:T(8,128)S(1)} %get-tuple-element.56), channel_id=1, source_target_pairs={{0,3},{1,2},{2,1},{3,0},{4,7},{5,6},{6,5},{7,4},{8,11},{9,10},{10,... | collective-permute-start | bytes 98312 | tf_op jit(solution)/shard_map/ppermute | solution.py:544
  52.4 0.4 collective-permute-start.16
  52.8 0.2 collective-permute-start.15
  52.9 2.8 %shard_map.52 = f32[8,4,4,640]{3,2,1,0:T(4,128)} custom-call(bf16[8,2,4,32,512]{4,3,2,1,0:T(8,128)(2,1)S(1)} %get-tuple-element.34.samples_ref, f32[256,128]{1,0:T(8,128)S(1)} %get-tuple-element.35.vectors_ref), custom_call_target="tpu_custom_call" | custom-call | flops 2000000000 | tf_op jit(solution)/shard_map/pallas_call | solution.py:526
  55.8 1.4 %collective-permute-done.16 = f32[1,64,128]{2,1,0:T(8,128)S(1)} collective-permute-done((f32[1,64,128]{2,1,0:T(8,128)S(1)}, f32[1,64,128]{2,1,0:T(8,128)S(1)}, u32[]{:S(2)}, u32[]{:S(2)}) %collective-permute-start.16) | collective-permute-done | bytes 32800 | tf_op jit(solution)/shard_map/ppermute | solution.py:544
  57.2 2.4 %collective-permute-start.18 = (f32[4,64,128]{2,1,0:T(8,128)S(1)}, f32[4,64,128]{2,1,0:T(8,128)S(1)}, u32[]{:S(2)}, u32[]{:S(2)}) collective-permute-start(f32[4,64,128]{2,1,0:T(8,128)S(1)} %pad_maximum_fusion.4), channel_id=1, source_target_pairs={{0,16},{1,17},{2,18},{3,19},{4,20},{5,21},{6,22},{7,23},{8,24},{9,... | collective-permute-start | bytes 393224 | tf_op jit(solution)/shard_map/ppermute | solution.py:544
  59.7 6.3 %collective-permute-done.18 = f32[4,64,128]{2,1,0:T(8,128)S(1)} collective-permute-done((f32[4,64,128]{2,1,0:T(8,128)S(1)}, f32[4,64,128]{2,1,0:T(8,128)S(1)}, u32[]{:S(2)}, u32[]{:S(2)}) %collective-permute-start.18) | collective-permute-done | bytes 131104 | tf_op jit(solution)/shard_map/ppermute | solution.py:544
  66.0 0.6 shard_map.53
  66.6 0.1 collective-permute-start.20
  66.7 1.2 %collective-permute-done.20 = f32[72,128]{1,0:T(8,128)S(1)} collective-permute-done((f32[72,128]{1,0:T(8,128)S(1)}, f32[72,128]{1,0:T(8,128)S(1)}, u32[]{:S(2)}, u32[]{:S(2)}) %collective-permute-start.20) | collective-permute-done | bytes 36896 | tf_op jit(solution)/shard_map/ppermute | solution.py:544
  67.9 2.2 %collective-permute-start.23 = (f32[72,128]{1,0:T(8,128)S(1)}, f32[72,128]{1,0:T(8,128)S(1)}, u32[]{:S(2)}, u32[]{:S(2)}) collective-permute-start(f32[72,128]{1,0:T(8,128)S(1)} %add.36), channel_id=1, source_target_pairs={{0,6},{1,7},{2,4},{3,5},{4,2},{5,3},{6,0},{7,1},{8,14},{9,15},{10,... | collective-permute-start | bytes 110600 | tf_op jit(solution)/shard_map/ppermute | solution.py:544
  70.1 0.8 collective-permute-start.22
  71.0 0.4 collective-permute-start.21
  71.4 5.1 %all-to-all-start.1 = ((f32[32,4,640]{2,1,0:T(4,128)}), f32[32,4,640]{2,1,0:T(4,128)S(1)}, u32[]{:S(2)}, u32[]{:S(2)}) async-start(f32[32,4,640]{2,1,0:T(4,128)} %bitcast.4), calls=%async_computation.1 | async-start | bytes 655360 | tf_op jit(solution)/shard_map/all_to_all | solution.py:605
  76.5 3.7 %collective-permute-start.26 = (f32[72,128]{1,0:T(8,128)S(1)}, f32[72,128]{1,0:T(8,128)S(1)}, u32[]{:S(2)}, u32[]{:S(2)}) collective-permute-start(f32[72,128]{1,0:T(8,128)S(1)} %add_add_fusion.1), channel_id=1, source_target_pairs={{0,24},{1,25},{2,26},{3,27},{4,28},{5,29},{6,30},{7,31},{8,16},{9,... | collective-permute-start | bytes 110600 | tf_op jit(solution)/shard_map/ppermute | solution.py:544
  80.2 0.8 collective-permute-start.24
  80.9 1.3 %collective-permute-start.19 = (f32[8,64,128]{2,1,0:T(8,128)S(1)}, f32[8,64,128]{2,1,0:T(8,128)S(1)}, u32[]{:S(2)}, u32[]{:S(2)}) collective-permute-start(f32[8,64,128]{2,1,0:T(8,128)S(1)} %get-tuple-element.52), channel_id=1, source_target_pairs={{0,8},{1,9},{2,10},{3,11},{4,12},{5,13},{6,14},{7,15},{8,0},{9,1},... | collective-permute-start | bytes 786440 | tf_op jit(solution)/shard_map/ppermute | solution.py:544
  82.2 5.5 %collective-permute-done.26 = f32[72,128]{1,0:T(8,128)S(1)} collective-permute-done((f32[72,128]{1,0:T(8,128)S(1)}, f32[72,128]{1,0:T(8,128)S(1)}, u32[]{:S(2)}, u32[]{:S(2)}) %collective-permute-start.26) | collective-permute-done | bytes 36896 | tf_op jit(solution)/shard_map/ppermute | solution.py:544
  87.7 2.7 %collective-permute-done.25 = f32[72,128]{1,0:T(8,128)S(1)} collective-permute-done((f32[72,128]{1,0:T(8,128)S(1)}, f32[72,128]{1,0:T(8,128)S(1)}, u32[]{:S(2)}, u32[]{:S(2)}) %collective-permute-start.25) | collective-permute-done | bytes 36896 | tf_op jit(solution)/shard_map/ppermute | solution.py:544
  90.4 0.1 collective-permute-start.27
  90.5 2.5 %collective-permute-done.19 = f32[8,64,128]{2,1,0:T(8,128)S(1)} collective-permute-done((f32[8,64,128]{2,1,0:T(8,128)S(1)}, f32[8,64,128]{2,1,0:T(8,128)S(1)}, u32[]{:S(2)}, u32[]{:S(2)}) %collective-permute-start.19) | collective-permute-done | bytes 262176 | tf_op jit(solution)/shard_map/ppermute | solution.py:544
  93.0 0.1 reshape.42.images_ref
  93.2 1.5 %collective-permute-start.28 = (f32[16,64,128]{2,1,0:T(8,128)S(1)}, f32[16,64,128]{2,1,0:T(8,128)S(1)}, u32[]{:S(2)}, u32[]{:S(2)}) collective-permute-start(f32[16,64,128]{2,1,0:T(8,128)S(1)} %constant_dynamic-update-slice_fusion.5), channel_id=1, source_target_pairs={{0,4},{1,5},{2,6},{3,7},{4,0},{5,1},{6,2},{7,3},{8,12},{9,13},{10,... | collective-permute-start | bytes 1572872 | tf_op jit(solution)/shard_map/ppermute | solution.py:544
  94.6 12.6 %shard_map.54 = (f32[128,128]{1,0:T(8,128)S(1)}, f32[128,128]{1,0:T(8,128)S(1)}, s32[1]{0:T(128)}) custom-call(f32[72,128]{1,0:T(8,128)S(1)} %add_add_fusion.gram_ref, f32[72,128]{1,0:T(8,128)S(1)} %collective-permute-done.27.other_ref), custom_call_target="tpu_custom_call" | custom-call | flops 12000000000 | tf_op jit(solution)/shard_map/pallas_call | solution.py:526
  107.9 0.2 conditional.1
  108.2 0.6 copy-done
  108.7 0.0 copy-done.1
  108.8 4.9 %shard_map.55 = (f32[32,512]{1,0:T(8,128)}, f32[256,128]{1,0:T(8,128)}) custom-call(f32[128,640]{1,0:T(8,128)S(1)} %reshape.42.images_ref, f32[128,128]{1,0:T(8,128)S(1)} %get-tuple-element.66.both_ref, f32[32,512]{1,0:T(8,128)S(1)} %copy-done, s32[32,512]{1,0:T(8,128)S(1)} %copy-done.1, f32[1024,128]{1,0:T(8,128)S(1)} %bitcast.13, f32[1024,128]{1,0:T(8,128)S(1)} %bitcast.14), custom_call_target="tpu_custom_call" | custom-call | flops 5000000000 | tf_op jit(solution)/shard_map/pallas_call | solution.py:526
  (33 shorter events, 0.2 us)
Async XLA Ops:
  2.5 8.0 %collective-permute-start.5 = (f32[1,32,512]{2,1,0:T(8,128)}, f32[1,32,512]{2,1,0:T(8,128)S(1)}, u32[]{:S(2)}, u32[]{:S(2)}) collective-permute-start(f32[1,32,512]{2,1,0:T(8,128)} %bitcast.15), channel_id=1, source_target_pairs={{0,16},{1,17},{2,18},{3,19},{4,20},{5,21},{6,22},{7,23},{8,24},{9,... | collective-permute-start | bytes 196616 | tf_op jit(solution)/shard_map/ppermute | solution.py:544
  6.6 12.7 %all-to-all-start = ((f32[32,8,128]{2,1,0:T(8,128)}), f32[32,8,128]{2,1,0:T(8,128)S(1)}, u32[]{:S(2)}, u32[]{:S(2)}) async-start(f32[32,8,128]{2,1,0:T(8,128)} %bitcast.18), calls=%async_computation | async-start | bytes 262144 | tf_op jit(solution)/shard_map/all_to_all | solution.py:605
  11.3 7.1 %collective-permute-start.6 = (f32[2,32,512]{2,1,0:T(8,128)S(1)}, f32[2,32,512]{2,1,0:T(8,128)S(1)}, u32[]{:S(2)}, u32[]{:S(2)}) collective-permute-start(f32[2,32,512]{2,1,0:T(8,128)S(1)} %pad_maximum_fusion.3), channel_id=1, source_target_pairs={{0,8},{1,9},{2,10},{3,11},{4,12},{5,13},{6,14},{7,15},{8,0},{9,1},... | collective-permute-start | bytes 393224 | tf_op jit(solution)/shard_map/ppermute | solution.py:544
  19.4 5.5 %collective-permute-start.7 = (f32[4,16,512]{2,1,0:T(8,128)S(1)}, f32[4,16,512]{2,1,0:T(8,128)S(1)}, u32[]{:S(2)}, u32[]{:S(2)}) collective-permute-start(f32[4,16,512]{2,1,0:T(8,128)S(1)} %get-tuple-element.51), channel_id=1, source_target_pairs={{0,4},{1,5},{2,6},{3,7},{4,0},{5,1},{6,2},{7,3},{8,12},{9,13},{10,... | collective-permute-start | bytes 393224 | tf_op jit(solution)/shard_map/ppermute | solution.py:544
  21.0 5.2 %collective-permute-start.11 = (f32[4,16,512]{2,1,0:T(8,128)S(1)}, f32[4,16,512]{2,1,0:T(8,128)S(1)}, u32[]{:S(2)}, u32[]{:S(2)}) collective-permute-start(f32[4,16,512]{2,1,0:T(8,128)S(1)} %get-tuple-element.50), channel_id=1, source_target_pairs={{0,2},{1,3},{2,0},{3,1},{4,6},{5,7},{6,4},{7,5},{8,10},{9,11},{10,... | collective-permute-start | bytes 393224 | tf_op jit(solution)/shard_map/ppermute | solution.py:544
  24.9 7.4 %collective-permute-start.8 = (f32[8,16,512]{2,1,0:T(8,128)S(1)}, f32[8,16,512]{2,1,0:T(8,128)S(1)}, u32[]{:S(2)}, u32[]{:S(2)}) collective-permute-start(f32[8,16,512]{2,1,0:T(8,128)S(1)} %pad_maximum_fusion.1.refs_0_), channel_id=1, source_target_pairs={{0,2},{1,3},{2,0},{3,1},{4,6},{5,7},{6,4},{7,5},{8,10},{9,11},{10,... | collective-permute-start | bytes 786440 | tf_op jit(solution)/shard_map/ppermute | solution.py:544
  26.2 6.8 %collective-permute-start.12 = (f32[8,16,512]{2,1,0:T(8,128)S(1)}, f32[8,16,512]{2,1,0:T(8,128)S(1)}, u32[]{:S(2)}, u32[]{:S(2)}) collective-permute-start(f32[8,16,512]{2,1,0:T(8,128)S(1)} %pad_maximum_fusion.2.refs_4_), channel_id=1, source_target_pairs={{0,4},{1,5},{2,6},{3,7},{4,0},{5,1},{6,2},{7,3},{8,12},{9,13},{10,... | collective-permute-start | bytes 786440 | tf_op jit(solution)/shard_map/ppermute | solution.py:544
  27.8 5.3 %collective-permute-start.9 = (f32[8,16,512]{2,1,0:T(8,128)S(1)}, f32[8,16,512]{2,1,0:T(8,128)S(1)}, u32[]{:S(2)}, u32[]{:S(2)}) collective-permute-start(f32[8,16,512]{2,1,0:T(8,128)S(1)} %pad_maximum_fusion.1.refs_0_), channel_id=1, source_target_pairs={{0,1},{1,0},{2,3},{3,2},{4,5},{5,4},{6,7},{7,6},{8,9},{9,8},{10,11... | collective-permute-start | bytes 786440 | tf_op jit(solution)/shard_map/ppermute | solution.py:544
  27.8 5.3 %collective-permute-start.13 = (f32[8,16,512]{2,1,0:T(8,128)S(1)}, f32[8,16,512]{2,1,0:T(8,128)S(1)}, u32[]{:S(2)}, u32[]{:S(2)}) collective-permute-start(f32[8,16,512]{2,1,0:T(8,128)S(1)} %pad_maximum_fusion.2.refs_4_), channel_id=1, source_target_pairs={{0,1},{1,0},{2,3},{3,2},{4,5},{5,4},{6,7},{7,6},{8,9},{9,8},{10,11... | collective-permute-start | bytes 786440 | tf_op jit(solution)/shard_map/ppermute | solution.py:544
  32.3 1.5 %collective-permute-start.10 = (f32[8,16,512]{2,1,0:T(8,128)S(1)}, f32[8,16,512]{2,1,0:T(8,128)S(1)}, u32[]{:S(2)}, u32[]{:S(2)}) collective-permute-start(f32[8,16,512]{2,1,0:T(8,128)S(1)} %collective-permute-done.8.refs_1_), channel_id=1, source_target_pairs={{0,1},{1,0},{2,3},{3,2},{4,5},{5,4},{6,7},{7,6},{8,9},{9,8},{10,11... | collective-permute-start | bytes 786440 | tf_op jit(solution)/shard_map/ppermute | solution.py:544
  33.1 1.5 %collective-permute-start.14 = (f32[8,16,512]{2,1,0:T(8,128)S(1)}, f32[8,16,512]{2,1,0:T(8,128)S(1)}, u32[]{:S(2)}, u32[]{:S(2)}) collective-permute-start(f32[8,16,512]{2,1,0:T(8,128)S(1)} %collective-permute-done.12.refs_5_), channel_id=1, source_target_pairs={{0,1},{1,0},{2,3},{3,2},{4,5},{5,4},{6,7},{7,6},{8,9},{9,8},{10,11... | collective-permute-start | bytes 786440 | tf_op jit(solution)/shard_map/ppermute | solution.py:544
  47.1 18.8 %all-to-all-start.2 = ((f32[32,16,128]{2,1,0:T(8,128)}), f32[32,16,128]{2,1,0:T(8,128)S(1)}, u32[]{:S(2)}, u32[]{:S(2)}) async-start(f32[32,16,128]{2,1,0:T(8,128)} %bitcast.5), calls=%async_computation.2 | async-start | bytes 524288 | tf_op jit(solution)/shard_map/all_to_all | solution.py:605
  51.0 4.8 %collective-permute-start.17 = (f32[1,64,128]{2,1,0:T(8,128)S(1)}, f32[1,64,128]{2,1,0:T(8,128)S(1)}, u32[]{:S(2)}, u32[]{:S(2)}) collective-permute-start(f32[1,64,128]{2,1,0:T(8,128)S(1)} %get-tuple-element.56), channel_id=1, source_target_pairs={{0,3},{1,2},{2,1},{3,0},{4,7},{5,6},{6,5},{7,4},{8,11},{9,10},{10,... | collective-permute-start | bytes 98312 | tf_op jit(solution)/shard_map/ppermute | solution.py:544
  52.4 4.8 %collective-permute-start.16 = (f32[1,64,128]{2,1,0:T(8,128)S(1)}, f32[1,64,128]{2,1,0:T(8,128)S(1)}, u32[]{:S(2)}, u32[]{:S(2)}) collective-permute-start(f32[1,64,128]{2,1,0:T(8,128)S(1)} %get-tuple-element.57), channel_id=1, source_target_pairs={{0,2},{1,3},{2,0},{3,1},{4,6},{5,7},{6,4},{7,5},{8,10},{9,11},{10,... | collective-permute-start | bytes 98312 | tf_op jit(solution)/shard_map/ppermute | solution.py:544
  52.8 4.4 %collective-permute-start.15 = (f32[1,64,128]{2,1,0:T(8,128)S(1)}, f32[1,64,128]{2,1,0:T(8,128)S(1)}, u32[]{:S(2)}, u32[]{:S(2)}) collective-permute-start(f32[1,64,128]{2,1,0:T(8,128)S(1)} %get-tuple-element.58), channel_id=1, source_target_pairs={{0,1},{1,0},{2,3},{3,2},{4,5},{5,4},{6,7},{7,6},{8,9},{9,8},{10,11... | collective-permute-start | bytes 98312 | tf_op jit(solution)/shard_map/ppermute | solution.py:544
  57.2 8.7 %collective-permute-start.18 = (f32[4,64,128]{2,1,0:T(8,128)S(1)}, f32[4,64,128]{2,1,0:T(8,128)S(1)}, u32[]{:S(2)}, u32[]{:S(2)}) collective-permute-start(f32[4,64,128]{2,1,0:T(8,128)S(1)} %pad_maximum_fusion.4), channel_id=1, source_target_pairs={{0,16},{1,17},{2,18},{3,19},{4,20},{5,21},{6,22},{7,23},{8,24},{9,... | collective-permute-start | bytes 393224 | tf_op jit(solution)/shard_map/ppermute | solution.py:544
  66.6 1.3 %collective-permute-start.20 = (f32[72,128]{1,0:T(8,128)S(1)}, f32[72,128]{1,0:T(8,128)S(1)}, u32[]{:S(2)}, u32[]{:S(2)}) collective-permute-start(f32[72,128]{1,0:T(8,128)S(1)} %get-tuple-element.40), channel_id=1, source_target_pairs={{0,1},{1,0},{2,3},{3,2},{4,5},{5,4},{6,7},{7,6},{8,9},{9,8},{10,11... | collective-permute-start | bytes 110600 | tf_op jit(solution)/shard_map/ppermute | solution.py:544
  67.9 8.6 %collective-permute-start.23 = (f32[72,128]{1,0:T(8,128)S(1)}, f32[72,128]{1,0:T(8,128)S(1)}, u32[]{:S(2)}, u32[]{:S(2)}) collective-permute-start(f32[72,128]{1,0:T(8,128)S(1)} %add.36), channel_id=1, source_target_pairs={{0,6},{1,7},{2,4},{3,5},{4,2},{5,3},{6,0},{7,1},{8,14},{9,15},{10,... | collective-permute-start | bytes 110600 | tf_op jit(solution)/shard_map/ppermute | solution.py:544
  70.1 6.3 %collective-permute-start.22 = (f32[72,128]{1,0:T(8,128)S(1)}, f32[72,128]{1,0:T(8,128)S(1)}, u32[]{:S(2)}, u32[]{:S(2)}) collective-permute-start(f32[72,128]{1,0:T(8,128)S(1)} %add.36), channel_id=1, source_target_pairs={{0,4},{1,5},{2,6},{3,7},{4,0},{5,1},{6,2},{7,3},{8,12},{9,13},{10,... | collective-permute-start | bytes 110600 | tf_op jit(solution)/shard_map/ppermute | solution.py:544
  71.0 5.5 %collective-permute-start.21 = (f32[72,128]{1,0:T(8,128)S(1)}, f32[72,128]{1,0:T(8,128)S(1)}, u32[]{:S(2)}, u32[]{:S(2)}) collective-permute-start(f32[72,128]{1,0:T(8,128)S(1)} %add.36), channel_id=1, source_target_pairs={{0,2},{1,3},{2,0},{3,1},{4,6},{5,7},{6,4},{7,5},{8,10},{9,11},{10,... | collective-permute-start | bytes 110600 | tf_op jit(solution)/shard_map/ppermute | solution.py:544
  71.4 21.7 %all-to-all-start.1 = ((f32[32,4,640]{2,1,0:T(4,128)}), f32[32,4,640]{2,1,0:T(4,128)S(1)}, u32[]{:S(2)}, u32[]{:S(2)}) async-start(f32[32,4,640]{2,1,0:T(4,128)} %bitcast.4), calls=%async_computation.1 | async-start | bytes 655360 | tf_op jit(solution)/shard_map/all_to_all | solution.py:605
  76.5 11.2 %collective-permute-start.26 = (f32[72,128]{1,0:T(8,128)S(1)}, f32[72,128]{1,0:T(8,128)S(1)}, u32[]{:S(2)}, u32[]{:S(2)}) collective-permute-start(f32[72,128]{1,0:T(8,128)S(1)} %add_add_fusion.1), channel_id=1, source_target_pairs={{0,24},{1,25},{2,26},{3,27},{4,28},{5,29},{6,30},{7,31},{8,16},{9,... | collective-permute-start | bytes 110600 | tf_op jit(solution)/shard_map/ppermute | solution.py:544
  80.2 10.2 %collective-permute-start.25 = (f32[72,128]{1,0:T(8,128)S(1)}, f32[72,128]{1,0:T(8,128)S(1)}, u32[]{:S(2)}, u32[]{:S(2)}) collective-permute-start(f32[72,128]{1,0:T(8,128)S(1)} %add_add_fusion.1), channel_id=1, source_target_pairs={{0,16},{1,17},{2,18},{3,19},{4,20},{5,21},{6,22},{7,23},{8,24},{9,... | collective-permute-start | bytes 110600 | tf_op jit(solution)/shard_map/ppermute | solution.py:544
  80.2 10.2 %collective-permute-start.24 = (f32[72,128]{1,0:T(8,128)S(1)}, f32[72,128]{1,0:T(8,128)S(1)}, u32[]{:S(2)}, u32[]{:S(2)}) collective-permute-start(f32[72,128]{1,0:T(8,128)S(1)} %add_add_fusion.1), channel_id=1, source_target_pairs={{0,8},{1,9},{2,10},{3,11},{4,12},{5,13},{6,14},{7,15},{8,0},{9,1},... | collective-permute-start | bytes 110600 | tf_op jit(solution)/shard_map/ppermute | solution.py:544
  80.9 12.1 %collective-permute-start.19 = (f32[8,64,128]{2,1,0:T(8,128)S(1)}, f32[8,64,128]{2,1,0:T(8,128)S(1)}, u32[]{:S(2)}, u32[]{:S(2)}) collective-permute-start(f32[8,64,128]{2,1,0:T(8,128)S(1)} %get-tuple-element.52), channel_id=1, source_target_pairs={{0,8},{1,9},{2,10},{3,11},{4,12},{5,13},{6,14},{7,15},{8,0},{9,1},... | collective-permute-start | bytes 786440 | tf_op jit(solution)/shard_map/ppermute | solution.py:544
  90.4 2.7 %collective-permute-start.27 = (f32[72,128]{1,0:T(8,128)S(1)}, f32[72,128]{1,0:T(8,128)S(1)}, u32[]{:S(2)}, u32[]{:S(2)}) collective-permute-start(f32[72,128]{1,0:T(8,128)S(1)} %add_add_fusion.gram_ref), channel_id=1, source_target_pairs={{0,1},{1,0},{2,3},{3,2},{4,5},{5,4},{6,7},{7,6},{8,9},{9,8},{10,11... | collective-permute-start | bytes 110600 | tf_op jit(solution)/shard_map/ppermute | solution.py:544
  93.2 15.0 %collective-permute-start.28 = (f32[16,64,128]{2,1,0:T(8,128)S(1)}, f32[16,64,128]{2,1,0:T(8,128)S(1)}, u32[]{:S(2)}, u32[]{:S(2)}) collective-permute-start(f32[16,64,128]{2,1,0:T(8,128)S(1)} %constant_dynamic-update-slice_fusion.5), channel_id=1, source_target_pairs={{0,4},{1,5},{2,6},{3,7},{4,0},{5,1},{6,2},{7,3},{8,12},{9,13},{10,... | collective-permute-start | bytes 1572872 | tf_op jit(solution)/shard_map/ppermute | solution.py:544
  107.9 0.8 copy-start
  107.9 0.9 copy-start.1

commit v8 on v7

--- a/solution.py
+++ b/solution.py
@@ -609,13 +609,12 @@
     groups = group.shape[0]
     parts = [group[:1]]
     parts += [exchange(group[s : s + 1], devices, s, AXES) for s in range(1, groups)]
-    near = jnp.concatenate(parts, axis=0)
-    return gather_round(near, list(range(groups)), [devices // 2], devices, AXES)
-
-
-def total_beside(kept, given, near, order, groups, devices):
+    return jnp.concatenate(parts, axis=0), list(range(groups))
+
+
+def total_beside(kept, given, near, order, images, groups, devices):
     total = kept + exchange(given, devices, 1, AXES)
-    mask = devices // 4
+    mask = devices // 2
     for partners in rounds_of(2, devices):
         terms = [exchange(total, devices, way, AXES) for way in partners]
         total = total + terms[0]
@@ -628,9 +627,9 @@
         near, order = gather_round(near, order, [mask], devices, AXES)
         mask //= 2
     other = exchange(total, devices, 1, AXES)
-    near, total, other = lax.optimization_barrier((near, total, other))
+    near, total, other, images = lax.optimization_barrier((near, total, other, images))
     far = exchange(near, devices, groups, AXES)
-    return (total, other), near, far, order + [m ^ groups for m in order]
+    return (total, other), near, far, order + [m ^ groups for m in order], to_all(images)
 
 
 def column_shards(kspace, sample_mask, start_basis):
@@ -691,15 +690,16 @@
         micros=2,
     )
     near, order = gather_group(group, devices)
-    received = after(received, images, near)
+    received, near = lax.optimization_barrier((received, images, near))[::2]
     half = ((rank // 2 + SUB, rank), f32)
     kept, given, turned = call(
         functools.partial(gram_kernel, cols, per_tile),
         [half, half, ((rank, owned), f32)],
         received.reshape(devices * 2 * per_tile, lanes),
     )
-    images = to_all(images.reshape(devices, cols, reach))
-    gram, near, far, order = total_beside(kept, given, near, order, groups, devices)
+    gram, near, far, order, images = total_beside(
+        kept, given, near, order, images.reshape(devices, cols, reach), groups, devices
+    )
     whole = ((rank, rank), f32)
     first, both, sound = call(
         factors_kernel, [whole, whole, ((1,), jnp.int32)], *gram, scalars=1, micros=12

time: 114 us -> 110 us (0.965)
  starting transfers between devices: 40.3 us -> 35 us
  waiting for transfers between devices: 33.6 us -> 35.6 us
    all_to_all x3, waiting for transfers between devices: 0.01 us -> 4.2 us  [to_all(): return lax.all_to_all(pieces, axes, 0, 0, tiled=True)]
    ppermute x24, starting transfers between devices: 27.6 us -> 24.7 us  [exchange(): return lax.ppermute(block, axes, [(i, i ^ mask) for i in range(devices)])]
    all_to_all x3, starting transfers between devices: 12.7 us -> 10.3 us  [to_all(): return lax.all_to_all(pieces, axes, 0, 0, tiled=True)]
    ppermute x24, waiting for transfers between devices: 33.6 us -> 31.4 us  [exchange(): return lax.ppermute(block, axes, [(i, i ^ mask) for i in range(devices)])]
  transfers between devices with their start and end apart: 27 -> 27, of which waited for: 12 -> 15; matrix products, arithmetic and copies ran while one was open for 2% -> 2% of each run, Pallas kernels for 14% -> 14%
where the time goes in v8:
time: 110 us
  waiting for transfers between devices  35.6 us (32%)
  Pallas kernels  35.4 us (32%)
  starting transfers between devices  35 us (32%)
  other arithmetic  1.84 us (2%)
  between operations  1.67 us (2%)
    pallas_call x6, Pallas kernels, call(): pl.pallas_call(kernel, out_shape=[jax.ShapeDtypeStruct(shape, kind) for s...  35.4 us
    ppermute x24, waiting for transfers between devices, exchange(): return lax.ppermute(block, axes, [(i, i ^ mask) for i in range(devices)])  31.4 us
    ppermute x24, starting transfers between devices, exchange(): return lax.ppermute(block, axes, [(i, i ^ mask) for i in range(devices)])  24.7 us
    all_to_all x3, starting transfers between devices, to_all(): return lax.all_to_all(pieces, axes, 0, 0, tiled=True)  10.3 us
    all_to_all x3, waiting for transfers between devices, to_all(): return lax.all_to_all(pieces, axes, 0, 0, tiled=True)  4.2 us
  transfers between devices with their start and end apart: 27, of which 15 were waited for; matrix products, arithmetic and copies ran while one was open for 2% of the time, Pallas kernels for 14%

profile of v8, /device:TPU:0, one launch (start us, length us, event | category | flops | bytes accessed | tf_op | source)
XLA Modules:
  0.0 109.9 jit_solution(4592615175558187744)
XLA Ops:
  0.6 1.9 %shard_map.50 = (f32[32,512]{1,0:T(8,128)}, f32[256,128]{1,0:T(8,128)}) custom-call(f32[32,512]{1,0:T(8,128)} %kspace_hbm.3, s32[32,512]{1,0:T(8,128)} %mask_hbm.3, f32[256,128]{1,0:T(8,128)} %bitcast.19), custom_call_target="tpu_custom_call" | custom-call | flops 1000000000 | tf_op jit(solution)/shard_map/pallas_call | solution.py:526
  2.5 4.1 %collective-permute-start.5 = (f32[1,32,512]{2,1,0:T(8,128)}, f32[1,32,512]{2,1,0:T(8,128)S(1)}, u32[]{:S(2)}, u32[]{:S(2)}) collective-permute-start(f32[1,32,512]{2,1,0:T(8,128)} %bitcast.15), channel_id=1, source_target_pairs={{0,16},{1,17},{2,18},{3,19},{4,20},{5,21},{6,22},{7,23},{8,24},{9,... | collective-permute-start | bytes 196616 | tf_op jit(solution)/shard_map/ppermute | solution.py:544
  6.6 3.8 %all-to-all-start = ((f32[32,8,128]{2,1,0:T(8,128)}), f32[32,8,128]{2,1,0:T(8,128)S(1)}, u32[]{:S(2)}, u32[]{:S(2)}) async-start(f32[32,8,128]{2,1,0:T(8,128)} %bitcast.18), calls=%async_computation | async-start | bytes 262144 | tf_op jit(solution)/shard_map/all_to_all | solution.py:605
  10.5 0.8 pad_maximum_fusion.5
  11.3 1.8 %collective-permute-start.6 = (f32[2,32,512]{2,1,0:T(8,128)S(1)}, f32[2,32,512]{2,1,0:T(8,128)S(1)}, u32[]{:S(2)}, u32[]{:S(2)}) collective-permute-start(f32[2,32,512]{2,1,0:T(8,128)S(1)} %pad_maximum_fusion.5), channel_id=1, source_target_pairs={{0,8},{1,9},{2,10},{3,11},{4,12},{5,13},{6,14},{7,15},{8,0},{9,1},... | collective-permute-start | bytes 393224 | tf_op jit(solution)/shard_map/ppermute | solution.py:544
  13.2 5.3 %collective-permute-done.6 = f32[2,32,512]{2,1,0:T(8,128)S(1)} collective-permute-done((f32[2,32,512]{2,1,0:T(8,128)S(1)}, f32[2,32,512]{2,1,0:T(8,128)S(1)}, u32[]{:S(2)}, u32[]{:S(2)}) %collective-permute-start.6) | collective-permute-done | bytes 131104 | tf_op jit(solution)/shard_map/ppermute | solution.py:544
  18.5 0.9 pad_maximum_fusion.1
  19.4 1.6 %collective-permute-start.7 = (f32[4,16,512]{2,1,0:T(8,128)S(1)}, f32[4,16,512]{2,1,0:T(8,128)S(1)}, u32[]{:S(2)}, u32[]{:S(2)}) collective-permute-start(f32[4,16,512]{2,1,0:T(8,128)S(1)} %get-tuple-element.55), channel_id=1, source_target_pairs={{0,4},{1,5},{2,6},{3,7},{4,0},{5,1},{6,2},{7,3},{8,12},{9,13},{10,... | collective-permute-start | bytes 393224 | tf_op jit(solution)/shard_map/ppermute | solution.py:544
  21.0 1.5 %collective-permute-start.11 = (f32[4,16,512]{2,1,0:T(8,128)S(1)}, f32[4,16,512]{2,1,0:T(8,128)S(1)}, u32[]{:S(2)}, u32[]{:S(2)}) collective-permute-start(f32[4,16,512]{2,1,0:T(8,128)S(1)} %get-tuple-element.54), channel_id=1, source_target_pairs={{0,2},{1,3},{2,0},{3,1},{4,6},{5,7},{6,4},{7,5},{8,10},{9,11},{10,... | collective-permute-start | bytes 393224 | tf_op jit(solution)/shard_map/ppermute | solution.py:544
  22.5 2.4 %collective-permute-done.7 = f32[4,16,512]{2,1,0:T(8,128)S(1)} collective-permute-done((f32[4,16,512]{2,1,0:T(8,128)S(1)}, f32[4,16,512]{2,1,0:T(8,128)S(1)}, u32[]{:S(2)}, u32[]{:S(2)}) %collective-permute-start.7) | collective-permute-done | bytes 131104 | tf_op jit(solution)/shard_map/ppermute | solution.py:544
  24.9 1.3 %collective-permute-start.8 = (f32[8,16,512]{2,1,0:T(8,128)S(1)}, f32[8,16,512]{2,1,0:T(8,128)S(1)}, u32[]{:S(2)}, u32[]{:S(2)}) collective-permute-start(f32[8,16,512]{2,1,0:T(8,128)S(1)} %pad_maximum_fusion.2.refs_0_), channel_id=1, source_target_pairs={{0,2},{1,3},{2,0},{3,1},{4,6},{5,7},{6,4},{7,5},{8,10},{9,11},{10,... | collective-permute-start | bytes 786440 | tf_op jit(solution)/shard_map/ppermute | solution.py:544
  26.2 1.5 %collective-permute-start.12 = (f32[8,16,512]{2,1,0:T(8,128)S(1)}, f32[8,16,512]{2,1,0:T(8,128)S(1)}, u32[]{:S(2)}, u32[]{:S(2)}) collective-permute-start(f32[8,16,512]{2,1,0:T(8,128)S(1)} %pad_maximum_fusion.3.refs_4_), channel_id=1, source_target_pairs={{0,4},{1,5},{2,6},{3,7},{4,0},{5,1},{6,2},{7,3},{8,12},{9,13},{10,... | collective-permute-start | bytes 786440 | tf_op jit(solution)/shard_map/ppermute | solution.py:544
  27.8 0.5 collective-permute-start.13
  28.3 4.0 %collective-permute-done.8.refs_1_ = f32[8,16,512]{2,1,0:T(8,128)S(1)} collective-permute-done((f32[8,16,512]{2,1,0:T(8,128)S(1)}, f32[8,16,512]{2,1,0:T(8,128)S(1)}, u32[]{:S(2)}, u32[]{:S(2)}) %collective-permute-start.8) | collective-permute-done | bytes 262176 | tf_op jit(solution)/shard_map/ppermute | solution.py:544
  32.3 0.8 collective-permute-done.12.refs_5_
  33.1 0.8 collective-permute-done.10.refs_3_
  33.8 0.8 collective-permute-done.14.refs_7_
  34.6 12.6 %shard_map.51 = (bf16[8,2,4,32,512]{4,3,2,1,0:T(8,128)(2,1)S(1)}, f32[256,128]{1,0:T(8,128)S(1)}, f32[8,4,2,8,128]{4,3,2,1,0:T(8,128)}, f32[4,64,128]{2,1,0:T(8,128)S(1)}) custom-call(f32[8,4,8,128]{3,2,1,0:T(8,128)S(1)} %bitcast.13, f32[8,16,512]{2,1,0:T(8,128)S(1)} %pad_maximum_fusion.2.refs_0_, f32[8,16,512]{2,1,0:T(8,128)S(1)} %collective-permute-done.8.refs_1_, ...), custom_call_target="tpu_custom_call" | custom-call | flops 12000000000 | tf_op jit(solution)/shard_map/pallas_call | solution.py:526
  47.2 3.8 %all-to-all-start.1 = ((f32[32,16,128]{2,1,0:T(8,128)}), f32[32,16,128]{2,1,0:T(8,128)S(1)}, u32[]{:S(2)}, u32[]{:S(2)}) async-start(f32[32,16,128]{2,1,0:T(8,128)} %bitcast.4), calls=%async_computation.1 | async-start | bytes 524288 | tf_op jit(solution)/shard_map/all_to_all | solution.py:605
  51.0 1.4 %collective-permute-start.17 = (f32[1,64,128]{2,1,0:T(8,128)S(1)}, f32[1,64,128]{2,1,0:T(8,128)S(1)}, u32[]{:S(2)}, u32[]{:S(2)}) collective-permute-start(f32[1,64,128]{2,1,0:T(8,128)S(1)} %get-tuple-element.57), channel_id=1, source_target_pairs={{0,3},{1,2},{2,1},{3,0},{4,7},{5,6},{6,5},{7,4},{8,11},{9,10},{10,... | collective-permute-start | bytes 98312 | tf_op jit(solution)/shard_map/ppermute | solution.py:544
  52.4 0.4 collective-permute-start.16
  52.8 0.2 collective-permute-start.15
  53.0 2.8 %shard_map.52 = f32[8,4,4,640]{3,2,1,0:T(4,128)} custom-call(bf16[8,2,4,32,512]{4,3,2,1,0:T(8,128)(2,1)S(1)} %get-tuple-element.37.samples_ref, f32[256,128]{1,0:T(8,128)S(1)} %get-tuple-element.38.vectors_ref), custom_call_target="tpu_custom_call" | custom-call | flops 2000000000 | tf_op jit(solution)/shard_map/pallas_call | solution.py:526
  55.8 1.4 %collective-permute-done.16 = f32[1,64,128]{2,1,0:T(8,128)S(1)} collective-permute-done((f32[1,64,128]{2,1,0:T(8,128)S(1)}, f32[1,64,128]{2,1,0:T(8,128)S(1)}, u32[]{:S(2)}, u32[]{:S(2)}) %collective-permute-start.16) | collective-permute-done | bytes 32800 | tf_op jit(solution)/shard_map/ppermute | solution.py:544
  57.2 4.2 %all-to-all-done.1 = f32[32,16,128]{2,1,0:T(8,128)S(1)} async-done(((f32[32,16,128]{2,1,0:T(8,128)}), f32[32,16,128]{2,1,0:T(8,128)S(1)}, u32[]{:S(2)}, u32[]{:S(2)}) %all-to-all-start.1) | async-done | bytes 262176 | tf_op jit(solution)/shard_map/all_to_all | solution.py:605
  61.4 0.6 shard_map.53
  62.0 0.1 collective-permute-start.20
  62.1 1.2 %collective-permute-done.20 = f32[72,128]{1,0:T(8,128)S(1)} collective-permute-done((f32[72,128]{1,0:T(8,128)S(1)}, f32[72,128]{1,0:T(8,128)S(1)}, u32[]{:S(2)}, u32[]{:S(2)}) %collective-permute-start.20) | collective-permute-done | bytes 36896 | tf_op jit(solution)/shard_map/ppermute | solution.py:544
  63.3 1.2 %collective-permute-start.23 = (f32[72,128]{1,0:T(8,128)S(1)}, f32[72,128]{1,0:T(8,128)S(1)}, u32[]{:S(2)}, u32[]{:S(2)}) collective-permute-start(f32[72,128]{1,0:T(8,128)S(1)} %add.36), channel_id=1, source_target_pairs={{0,6},{1,7},{2,4},{3,5},{4,2},{5,3},{6,0},{7,1},{8,14},{9,15},{10,... | collective-permute-start | bytes 110600 | tf_op jit(solution)/shard_map/ppermute | solution.py:544
  64.5 0.8 collective-permute-start.22
  65.3 1.6 %collective-permute-start.21 = (f32[72,128]{1,0:T(8,128)S(1)}, f32[72,128]{1,0:T(8,128)S(1)}, u32[]{:S(2)}, u32[]{:S(2)}) collective-permute-start(f32[72,128]{1,0:T(8,128)S(1)} %add.36), channel_id=1, source_target_pairs={{0,2},{1,3},{2,0},{3,1},{4,6},{5,7},{6,4},{7,5},{8,10},{9,11},{10,... | collective-permute-start | bytes 110600 | tf_op jit(solution)/shard_map/ppermute | solution.py:544
  66.8 0.5 collective-permute-start.18
  67.3 1.1 collective-permute-done.23
  68.5 0.8 collective-permute-done.21
  69.2 1.5 %collective-permute-start.26 = (f32[72,128]{1,0:T(8,128)S(1)}, f32[72,128]{1,0:T(8,128)S(1)}, u32[]{:S(2)}, u32[]{:S(2)}) collective-permute-start(f32[72,128]{1,0:T(8,128)S(1)} %add_add_fusion.1), channel_id=1, source_target_pairs={{0,24},{1,25},{2,26},{3,27},{4,28},{5,29},{6,30},{7,31},{8,16},{9,... | collective-permute-start | bytes 110600 | tf_op jit(solution)/shard_map/ppermute | solution.py:544
  70.7 0.7 collective-permute-start.25
  71.4 2.3 %collective-permute-start.24 = (f32[72,128]{1,0:T(8,128)S(1)}, f32[72,128]{1,0:T(8,128)S(1)}, u32[]{:S(2)}, u32[]{:S(2)}) collective-permute-start(f32[72,128]{1,0:T(8,128)S(1)} %add_add_fusion.1), channel_id=1, source_target_pairs={{0,8},{1,9},{2,10},{3,11},{4,12},{5,13},{6,14},{7,15},{8,0},{9,1},... | collective-permute-start | bytes 110600 | tf_op jit(solution)/shard_map/ppermute | solution.py:544
  73.7 3.7 %collective-permute-done.18 = f32[4,64,128]{2,1,0:T(8,128)S(1)} collective-permute-done((f32[4,64,128]{2,1,0:T(8,128)S(1)}, f32[4,64,128]{2,1,0:T(8,128)S(1)}, u32[]{:S(2)}, u32[]{:S(2)}) %collective-permute-start.18) | collective-permute-done | bytes 131104 | tf_op jit(solution)/shard_map/ppermute | solution.py:544
  77.4 0.1 collective-permute-start.19
  77.5 1.0 collective-permute-done.25
  78.5 6.2 %collective-permute-done.19 = f32[8,64,128]{2,1,0:T(8,128)S(1)} collective-permute-done((f32[8,64,128]{2,1,0:T(8,128)S(1)}, f32[8,64,128]{2,1,0:T(8,128)S(1)}, u32[]{:S(2)}, u32[]{:S(2)}) %collective-permute-start.19) | collective-permute-done | bytes 262176 | tf_op jit(solution)/shard_map/ppermute | solution.py:544
  84.8 2.6 %all-to-all-start.2 = ((f32[32,4,640]{2,1,0:T(4,128)}), f32[32,4,640]{2,1,0:T(4,128)S(1)}, u32[]{:S(2)}, u32[]{:S(2)}) async-start(f32[32,4,640]{2,1,0:T(4,128)} %bitcast.6), calls=%async_computation.2 | async-start | bytes 655360 | tf_op jit(solution)/shard_map/all_to_all | solution.py:605
  87.4 1.7 %collective-permute-start.28 = (f32[16,64,128]{2,1,0:T(8,128)S(1)}, f32[16,64,128]{2,1,0:T(8,128)S(1)}, u32[]{:S(2)}, u32[]{:S(2)}) collective-permute-start(f32[16,64,128]{2,1,0:T(8,128)S(1)} %pad_maximum_fusion), channel_id=1, source_target_pairs={{0,4},{1,5},{2,6},{3,7},{4,0},{5,1},{6,2},{7,3},{8,12},{9,13},{10,... | collective-permute-start | bytes 1572872 | tf_op jit(solution)/shard_map/ppermute | solution.py:544
  89.1 12.6 %shard_map.54 = (f32[128,128]{1,0:T(8,128)S(1)}, f32[128,128]{1,0:T(8,128)S(1)}, s32[1]{0:T(128)}) custom-call(f32[72,128]{1,0:T(8,128)S(1)} %add_add_fusion.gram_ref, f32[72,128]{1,0:T(8,128)S(1)} %collective-permute-done.27.other_ref), custom_call_target="tpu_custom_call" | custom-call | flops 12000000000 | tf_op jit(solution)/shard_map/pallas_call | solution.py:526
  102.4 0.2 conditional.1
  102.6 0.1 reshape.44.images_ref
  102.7 2.1 %collective-permute-done.28 = f32[16,64,128]{2,1,0:T(8,128)S(1)} collective-permute-done((f32[16,64,128]{2,1,0:T(8,128)S(1)}, f32[16,64,128]{2,1,0:T(8,128)S(1)}, u32[]{:S(2)}, u32[]{:S(2)}) %collective-permute-start.28) | collective-permute-done | bytes 524320 | tf_op jit(solution)/shard_map/ppermute | solution.py:544
  104.9 4.9 %shard_map.55 = (f32[32,512]{1,0:T(8,128)}, f32[256,128]{1,0:T(8,128)}) custom-call(f32[128,640]{1,0:T(8,128)S(1)} %reshape.44.images_ref, f32[128,128]{1,0:T(8,128)S(1)} %get-tuple-element.60.both_ref, f32[32,512]{1,0:T(8,128)S(1)} %copy-done, s32[32,512]{1,0:T(8,128)S(1)} %copy-done.1, f32[1024,128]{1,0:T(8,128)S(1)} %bitcast.11, f32[1024,128]{1,0:T(8,128)S(1)} %bitcast.14), custom_call_target="tpu_custom_call" | custom-call | flops 5000000000 | tf_op jit(solution)/shard_map/pallas_call | solution.py:526
  (30 shorter events, 0.3 us)
Async XLA Ops:
  2.5 8.0 %collective-permute-start.5 = (f32[1,32,512]{2,1,0:T(8,128)}, f32[1,32,512]{2,1,0:T(8,128)S(1)}, u32[]{:S(2)}, u32[]{:S(2)}) collective-permute-start(f32[1,32,512]{2,1,0:T(8,128)} %bitcast.15), channel_id=1, source_target_pairs={{0,16},{1,17},{2,18},{3,19},{4,20},{5,21},{6,22},{7,23},{8,24},{9,... | collective-permute-start | bytes 196616 | tf_op jit(solution)/shard_map/ppermute | solution.py:544
  6.6 12.7 %all-to-all-start = ((f32[32,8,128]{2,1,0:T(8,128)}), f32[32,8,128]{2,1,0:T(8,128)S(1)}, u32[]{:S(2)}, u32[]{:S(2)}) async-start(f32[32,8,128]{2,1,0:T(8,128)} %bitcast.18), calls=%async_computation | async-start | bytes 262144 | tf_op jit(solution)/shard_map/all_to_all | solution.py:605
  11.3 7.1 %collective-permute-start.6 = (f32[2,32,512]{2,1,0:T(8,128)S(1)}, f32[2,32,512]{2,1,0:T(8,128)S(1)}, u32[]{:S(2)}, u32[]{:S(2)}) collective-permute-start(f32[2,32,512]{2,1,0:T(8,128)S(1)} %pad_maximum_fusion.5), channel_id=1, source_target_pairs={{0,8},{1,9},{2,10},{3,11},{4,12},{5,13},{6,14},{7,15},{8,0},{9,1},... | collective-permute-start | bytes 393224 | tf_op jit(solution)/shard_map/ppermute | solution.py:544
  19.4 5.5 %collective-permute-start.7 = (f32[4,16,512]{2,1,0:T(8,128)S(1)}, f32[4,16,512]{2,1,0:T(8,128)S(1)}, u32[]{:S(2)}, u32[]{:S(2)}) collective-permute-start(f32[4,16,512]{2,1,0:T(8,128)S(1)} %get-tuple-element.55), channel_id=1, source_target_pairs={{0,4},{1,5},{2,6},{3,7},{4,0},{5,1},{6,2},{7,3},{8,12},{9,13},{10,... | collective-permute-start | bytes 393224 | tf_op jit(solution)/shard_map/ppermute | solution.py:544
  21.0 5.2 %collective-permute-start.11 = (f32[4,16,512]{2,1,0:T(8,128)S(1)}, f32[4,16,512]{2,1,0:T(8,128)S(1)}, u32[]{:S(2)}, u32[]{:S(2)}) collective-permute-start(f32[4,16,512]{2,1,0:T(8,128)S(1)} %get-tuple-element.54), channel_id=1, source_target_pairs={{0,2},{1,3},{2,0},{3,1},{4,6},{5,7},{6,4},{7,5},{8,10},{9,11},{10,... | collective-permute-start | bytes 393224 | tf_op jit(solution)/shard_map/ppermute | solution.py:544
  24.9 7.4 %collective-permute-start.8 = (f32[8,16,512]{2,1,0:T(8,128)S(1)}, f32[8,16,512]{2,1,0:T(8,128)S(1)}, u32[]{:S(2)}, u32[]{:S(2)}) collective-permute-start(f32[8,16,512]{2,1,0:T(8,128)S(1)} %pad_maximum_fusion.2.refs_0_), channel_id=1, source_target_pairs={{0,2},{1,3},{2,0},{3,1},{4,6},{5,7},{6,4},{7,5},{8,10},{9,11},{10,... | collective-permute-start | bytes 786440 | tf_op jit(solution)/shard_map/ppermute | solution.py:544
  26.2 6.8 %collective-permute-start.12 = (f32[8,16,512]{2,1,0:T(8,128)S(1)}, f32[8,16,512]{2,1,0:T(8,128)S(1)}, u32[]{:S(2)}, u32[]{:S(2)}) collective-permute-start(f32[8,16,512]{2,1,0:T(8,128)S(1)} %pad_maximum_fusion.3.refs_4_), channel_id=1, source_target_pairs={{0,4},{1,5},{2,6},{3,7},{4,0},{5,1},{6,2},{7,3},{8,12},{9,13},{10,... | collective-permute-start | bytes 786440 | tf_op jit(solution)/shard_map/ppermute | solution.py:544
  27.8 5.3 %collective-permute-start.9 = (f32[8,16,512]{2,1,0:T(8,128)S(1)}, f32[8,16,512]{2,1,0:T(8,128)S(1)}, u32[]{:S(2)}, u32[]{:S(2)}) collective-permute-start(f32[8,16,512]{2,1,0:T(8,128)S(1)} %pad_maximum_fusion.2.refs_0_), channel_id=1, source_target_pairs={{0,1},{1,0},{2,3},{3,2},{4,5},{5,4},{6,7},{7,6},{8,9},{9,8},{10,11... | collective-permute-start | bytes 786440 | tf_op jit(solution)/shard_map/ppermute | solution.py:544
  27.8 5.3 %collective-permute-start.13 = (f32[8,16,512]{2,1,0:T(8,128)S(1)}, f32[8,16,512]{2,1,0:T(8,128)S(1)}, u32[]{:S(2)}, u32[]{:S(2)}) collective-permute-start(f32[8,16,512]{2,1,0:T(8,128)S(1)} %pad_maximum_fusion.3.refs_4_), channel_id=1, source_target_pairs={{0,1},{1,0},{2,3},{3,2},{4,5},{5,4},{6,7},{7,6},{8,9},{9,8},{10,11... | collective-permute-start | bytes 786440 | tf_op jit(solution)/shard_map/ppermute | solution.py:544
  32.3 1.5 %collective-permute-start.10 = (f32[8,16,512]{2,1,0:T(8,128)S(1)}, f32[8,16,512]{2,1,0:T(8,128)S(1)}, u32[]{:S(2)}, u32[]{:S(2)}) collective-permute-start(f32[8,16,512]{2,1,0:T(8,128)S(1)} %collective-permute-done.8.refs_1_), channel_id=1, source_target_pairs={{0,1},{1,0},{2,3},{3,2},{4,5},{5,4},{6,7},{7,6},{8,9},{9,8},{10,11... | collective-permute-start | bytes 786440 | tf_op jit(solution)/shard_map/ppermute | solution.py:544
  33.1 1.5 %collective-permute-start.14 = (f32[8,16,512]{2,1,0:T(8,128)S(1)}, f32[8,16,512]{2,1,0:T(8,128)S(1)}, u32[]{:S(2)}, u32[]{:S(2)}) collective-permute-start(f32[8,16,512]{2,1,0:T(8,128)S(1)} %collective-permute-done.12.refs_5_), channel_id=1, source_target_pairs={{0,1},{1,0},{2,3},{3,2},{4,5},{5,4},{6,7},{7,6},{8,9},{9,8},{10,11... | collective-permute-start | bytes 786440 | tf_op jit(solution)/shard_map/ppermute | solution.py:544
  47.2 14.3 %all-to-all-start.1 = ((f32[32,16,128]{2,1,0:T(8,128)}), f32[32,16,128]{2,1,0:T(8,128)S(1)}, u32[]{:S(2)}, u32[]{:S(2)}) async-start(f32[32,16,128]{2,1,0:T(8,128)} %bitcast.4), calls=%async_computation.1 | async-start | bytes 524288 | tf_op jit(solution)/shard_map/all_to_all | solution.py:605
  51.0 4.8 %collective-permute-start.17 = (f32[1,64,128]{2,1,0:T(8,128)S(1)}, f32[1,64,128]{2,1,0:T(8,128)S(1)}, u32[]{:S(2)}, u32[]{:S(2)}) collective-permute-start(f32[1,64,128]{2,1,0:T(8,128)S(1)} %get-tuple-element.57), channel_id=1, source_target_pairs={{0,3},{1,2},{2,1},{3,0},{4,7},{5,6},{6,5},{7,4},{8,11},{9,10},{10,... | collective-permute-start | bytes 98312 | tf_op jit(solution)/shard_map/ppermute | solution.py:544
  52.4 4.8 %collective-permute-start.16 = (f32[1,64,128]{2,1,0:T(8,128)S(1)}, f32[1,64,128]{2,1,0:T(8,128)S(1)}, u32[]{:S(2)}, u32[]{:S(2)}) collective-permute-start(f32[1,64,128]{2,1,0:T(8,128)S(1)} %get-tuple-element.58), channel_id=1, source_target_pairs={{0,2},{1,3},{2,0},{3,1},{4,6},{5,7},{6,4},{7,5},{8,10},{9,11},{10,... | collective-permute-start | bytes 98312 | tf_op jit(solution)/shard_map/ppermute | solution.py:544
  52.8 4.4 %collective-permute-start.15 = (f32[1,64,128]{2,1,0:T(8,128)S(1)}, f32[1,64,128]{2,1,0:T(8,128)S(1)}, u32[]{:S(2)}, u32[]{:S(2)}) collective-permute-start(f32[1,64,128]{2,1,0:T(8,128)S(1)} %get-tuple-element.59), channel_id=1, source_target_pairs={{0,1},{1,0},{2,3},{3,2},{4,5},{5,4},{6,7},{7,6},{8,9},{9,8},{10,11... | collective-permute-start | bytes 98312 | tf_op jit(solution)/shard_map/ppermute | solution.py:544
  62.0 1.3 %collective-permute-start.20 = (f32[72,128]{1,0:T(8,128)S(1)}, f32[72,128]{1,0:T(8,128)S(1)}, u32[]{:S(2)}, u32[]{:S(2)}) collective-permute-start(f32[72,128]{1,0:T(8,128)S(1)} %get-tuple-element.43), channel_id=1, source_target_pairs={{0,1},{1,0},{2,3},{3,2},{4,5},{5,4},{6,7},{7,6},{8,9},{9,8},{10,11... | collective-permute-start | bytes 110600 | tf_op jit(solution)/shard_map/ppermute | solution.py:544
  63.3 5.1 %collective-permute-start.23 = (f32[72,128]{1,0:T(8,128)S(1)}, f32[72,128]{1,0:T(8,128)S(1)}, u32[]{:S(2)}, u32[]{:S(2)}) collective-permute-start(f32[72,128]{1,0:T(8,128)S(1)} %add.36), channel_id=1, source_target_pairs={{0,6},{1,7},{2,4},{3,5},{4,2},{5,3},{6,0},{7,1},{8,14},{9,15},{10,... | collective-permute-start | bytes 110600 | tf_op jit(solution)/shard_map/ppermute | solution.py:544
  64.5 4.0 %collective-permute-start.22 = (f32[72,128]{1,0:T(8,128)S(1)}, f32[72,128]{1,0:T(8,128)S(1)}, u32[]{:S(2)}, u32[]{:S(2)}) collective-permute-start(f32[72,128]{1,0:T(8,128)S(1)} %add.36), channel_id=1, source_target_pairs={{0,4},{1,5},{2,6},{3,7},{4,0},{5,1},{6,2},{7,3},{8,12},{9,13},{10,... | collective-permute-start | bytes 110600 | tf_op jit(solution)/shard_map/ppermute | solution.py:544
  65.3 4.0 %collective-permute-start.21 = (f32[72,128]{1,0:T(8,128)S(1)}, f32[72,128]{1,0:T(8,128)S(1)}, u32[]{:S(2)}, u32[]{:S(2)}) collective-permute-start(f32[72,128]{1,0:T(8,128)S(1)} %add.36), channel_id=1, source_target_pairs={{0,2},{1,3},{2,0},{3,1},{4,6},{5,7},{6,4},{7,5},{8,10},{9,11},{10,... | collective-permute-start | bytes 110600 | tf_op jit(solution)/shard_map/ppermute | solution.py:544
  66.8 10.5 %collective-permute-start.18 = (f32[4,64,128]{2,1,0:T(8,128)S(1)}, f32[4,64,128]{2,1,0:T(8,128)S(1)}, u32[]{:S(2)}, u32[]{:S(2)}) collective-permute-start(f32[4,64,128]{2,1,0:T(8,128)S(1)} %pad_maximum_fusion.6), channel_id=1, source_target_pairs={{0,16},{1,17},{2,18},{3,19},{4,20},{5,21},{6,22},{7,23},{8,24},{9,... | collective-permute-start | bytes 393224 | tf_op jit(solution)/shard_map/ppermute | solution.py:544
  69.2 8.2 %collective-permute-start.26 = (f32[72,128]{1,0:T(8,128)S(1)}, f32[72,128]{1,0:T(8,128)S(1)}, u32[]{:S(2)}, u32[]{:S(2)}) collective-permute-start(f32[72,128]{1,0:T(8,128)S(1)} %add_add_fusion.1), channel_id=1, source_target_pairs={{0,24},{1,25},{2,26},{3,27},{4,28},{5,29},{6,30},{7,31},{8,16},{9,... | collective-permute-start | bytes 110600 | tf_op jit(solution)/shard_map/ppermute | solution.py:544
  70.7 7.7 %collective-permute-start.25 = (f32[72,128]{1,0:T(8,128)S(1)}, f32[72,128]{1,0:T(8,128)S(1)}, u32[]{:S(2)}, u32[]{:S(2)}) collective-permute-start(f32[72,128]{1,0:T(8,128)S(1)} %add_add_fusion.1), channel_id=1, source_target_pairs={{0,16},{1,17},{2,18},{3,19},{4,20},{5,21},{6,22},{7,23},{8,24},{9,... | collective-permute-start | bytes 110600 | tf_op jit(solution)/shard_map/ppermute | solution.py:544
  71.4 7.0 %collective-permute-start.24 = (f32[72,128]{1,0:T(8,128)S(1)}, f32[72,128]{1,0:T(8,128)S(1)}, u32[]{:S(2)}, u32[]{:S(2)}) collective-permute-start(f32[72,128]{1,0:T(8,128)S(1)} %add_add_fusion.1), channel_id=1, source_target_pairs={{0,8},{1,9},{2,10},{3,11},{4,12},{5,13},{6,14},{7,15},{8,0},{9,1},... | collective-permute-start | bytes 110600 | tf_op jit(solution)/shard_map/ppermute | solution.py:544
  77.4 7.4 %collective-permute-start.19 = (f32[8,64,128]{2,1,0:T(8,128)S(1)}, f32[8,64,128]{2,1,0:T(8,128)S(1)}, u32[]{:S(2)}, u32[]{:S(2)}) collective-permute-start(f32[8,64,128]{2,1,0:T(8,128)S(1)} %pad_maximum_fusion.4), channel_id=1, source_target_pairs={{0,8},{1,9},{2,10},{3,11},{4,12},{5,13},{6,14},{7,15},{8,0},{9,1},... | collective-permute-start | bytes 786440 | tf_op jit(solution)/shard_map/ppermute | solution.py:544
  78.4 6.3 %collective-permute-start.27 = (f32[72,128]{1,0:T(8,128)S(1)}, f32[72,128]{1,0:T(8,128)S(1)}, u32[]{:S(2)}, u32[]{:S(2)}) collective-permute-start(f32[72,128]{1,0:T(8,128)S(1)} %add_add_fusion.gram_ref), channel_id=1, source_target_pairs={{0,1},{1,0},{2,3},{3,2},{4,5},{5,4},{6,7},{7,6},{8,9},{9,8},{10,11... | collective-permute-start | bytes 110600 | tf_op jit(solution)/shard_map/ppermute | solution.py:544
  84.8 17.8 %all-to-all-start.2 = ((f32[32,4,640]{2,1,0:T(4,128)}), f32[32,4,640]{2,1,0:T(4,128)S(1)}, u32[]{:S(2)}, u32[]{:S(2)}) async-start(f32[32,4,640]{2,1,0:T(4,128)} %bitcast.6), calls=%async_computation.2 | async-start | bytes 655360 | tf_op jit(solution)/shard_map/all_to_all | solution.py:605
  87.4 17.5 %collective-permute-start.28 = (f32[16,64,128]{2,1,0:T(8,128)S(1)}, f32[16,64,128]{2,1,0:T(8,128)S(1)}, u32[]{:S(2)}, u32[]{:S(2)}) collective-permute-start(f32[16,64,128]{2,1,0:T(8,128)S(1)} %pad_maximum_fusion), channel_id=1, source_target_pairs={{0,4},{1,5},{2,6},{3,7},{4,0},{5,1},{6,2},{7,3},{8,12},{9,13},{10,... | collective-permute-start | bytes 1572872 | tf_op jit(solution)/shard_map/ppermute | solution.py:544
  102.3 2.5 %copy-start = (f32[32,512]{1,0:T(8,128)S(1)}, f32[32,512]{1,0:T(8,128)}, u32[]{:S(2)}) copy-start(f32[32,512]{1,0:T(8,128)} %kspace_hbm.3) | copy-start | bytes 196612
  102.4 2.5 %copy-start.1 = (s32[32,512]{1,0:T(8,128)S(1)}, s32[32,512]{1,0:T(8,128)}, u32[]{:S(2)}) copy-start(s32[32,512]{1,0:T(8,128)} %mask_hbm.3) | copy-start | bytes 196612

commit v9 on v8

--- a/solution.py
+++ b/solution.py
@@ -112,6 +112,12 @@
     return dot(a_high, b_high, dims) + (dot(a_high, b_low, dims) + dot(a_low, b_high, dims))
 
 
+def square(size):
+    at_row = lax.broadcasted_iota(jnp.int32, (size, size), 0)
+    at_col = lax.broadcasted_iota(jnp.int32, (size, size), 1)
+    return at_row, at_col
+
+
 def prepare_kernel(
     cols,
     chg,
@@ -146,12 +152,10 @@
         send_ref[pl.ds(j, devices, stride=per_tile), :] = row
 
 
-def images_of(vectors, samples_ref, wide_ref):
+def widened(vectors, samples_ref, wide_ref):
     rows, channels = vectors.shape
-    cols = rows // KER
     high, low = split(vectors)
-    at_row = lax.broadcasted_iota(jnp.int32, (rows, rows), 0)
-    at_col = lax.broadcasted_iota(jnp.int32, (rows, rows), 1)
+    at_row, at_col = square(rows)
     flip = ((at_row // KER == at_col // KER) & (at_row % KER + at_col % KER == KER - 1)).astype(
         jnp.float32
     ).astype(jnp.bfloat16)
@@ -160,40 +164,63 @@
     twice = jnp.concatenate([high, high], axis=1)
     tiles = samples_ref.shape[0]
     tile = samples_ref.shape[-1]
-    for t in range(tiles):
+
+    def store(t):
         block = samples_ref[t].reshape(2 * channels, tile)
-        wide_ref[:, t * tile : (t + 1) * tile] = dot(twice, block) + dot(low, block[:channels])
-    images = []
-    for k in range(cols):
+        wide = dot(twice, block) + dot(low, block[:channels])
+        wide_ref[:, LANES + t * tile : LANES + (t + 1) * tile] = wide
+        if t == tiles - 1:
+            wide_ref[:, :LANES] = wide[:, tile - LANES :]
+
+    return store
+
+
+def store_images(t, tile, wide_ref, images_ref):
+    for k in range(wide_ref.shape[0] // KER):
         total = None
         for i in reversed(range(0, KER, SUB)):
-            part = wide_ref[k * KER + i : k * KER + i + SUB, :]
+            part = wide_ref[k * KER + i : k * KER + i + SUB, t * tile : (t + 1) * tile + LANES]
             total = part if total is None else pltpu.roll(total, SUB, 1) + part
         total = pltpu.roll(total, 0, 1, stride=1, stride_axis=0)
-        images.append(jnp.sum(total, axis=0, keepdims=True))
-    return images
-
-
-def normal_of(images, samples_ref, moved_ref):
-    cols = len(images)
-    positions = images[0].shape[1]
-    tiles = samples_ref.shape[0]
-    tile = samples_ref.shape[-1]
-    channels = samples_ref.shape[2] * samples_ref.shape[3]
+        total = jnp.sum(total, axis=0, keepdims=True)[:, LANES:]
+        images_ref[k : k + 1, t * tile : (t + 1) * tile] = total
+        if t == 0:
+            end = images_ref.shape[1]
+            images_ref[k : k + 1, end - LANES : end] = total[:, :LANES]
+
+
+def normal_tile(t, cols, samples_ref, images_ref, moved_ref):
+    _, parts, groups, chg, tile = samples_ref.shape
     rows = cols * KER
+    lanes = slice(t * tile, (t + 1) * tile)
     for k in range(cols):
-        base = jnp.broadcast_to(images[k], (SUB, positions))
-        base = pltpu.roll(base, positions - (KER - 1), 1, stride=1, stride_axis=0)
+        base = images_ref[k : k + 1, t * tile : (t + 1) * tile + LANES]
+        base = jnp.broadcast_to(base, (SUB, tile + LANES))
+        base = pltpu.roll(base, tile + LANES - (KER - 1), 1, stride=1, stride_axis=0)
         for j in range(0, KER, 2 * SUB):
             first = base if j == 0 else pltpu.roll(base, j, 1)
             second = pltpu.roll(base, j + SUB, 1)
-            high, low = split(jnp.concatenate([first, second], axis=0))
-            moved_ref[k * KER + j : k * KER + j + 2 * SUB, :] = high
-            moved_ref[rows + k * KER + j : rows + k * KER + j + 2 * SUB, :] = low
-    total = jnp.zeros((2 * rows, 2 * channels), jnp.float32)
-    for t in range(tiles):
-        block = samples_ref[t].reshape(2 * channels, tile)
-        total = total + dot(moved_ref[:, t * tile : (t + 1) * tile], block, ((1,), (1,)))
+            high, low = split(jnp.concatenate([first[:, :tile], second[:, :tile]], axis=0))
+            moved_ref[k * KER + j : k * KER + j + 2 * SUB, lanes] = high
+            moved_ref[rows + k * KER + j : rows + k * KER + j + 2 * SUB, lanes] = low
+    block = samples_ref[t].reshape(parts * groups * chg, tile)
+    return dot(moved_ref[:, lanes], block, ((1,), (1,)))
+
+
+def normal_of(vectors, samples_ref, wide_ref, images_ref, moved_ref):
+    tiles, _, groups, chg, tile = samples_ref.shape
+    rows, channels = vectors.shape
+    store = widened(vectors, samples_ref, wide_ref)
+    store(tiles - 1)
+    total = None
+    for t in range(tiles + 1):
+        if t < tiles - 1:
+            store(t)
+        if t < tiles:
+            store_images(t, tile, wide_ref, images_ref)
+        if t > 0:
+            part = normal_tile(t - 1, rows // KER, samples_ref, images_ref, moved_ref)
+            total = part if total is None else total + part
     return total[:rows, :channels] + (
         total[:rows, channels:] + total[rows:, :channels] + total[rows:, channels:]
     )
@@ -231,7 +258,7 @@
 
 
 def passes_kernel(orders, basis_ref, *refs):
-    *pieces, samples_ref, normal_ref, send_ref, group_ref, wide_ref, moved_ref = refs
+    *pieces, samples_ref, normal_ref, send_ref, group_ref, wide_ref, images_ref, moved_ref = refs
     tiles, _, groups, chg, tile = samples_ref.shape
     me = lax.axis_index("rows") * groups + lax.axis_index("coil")
     for (start, order), piece_ref in zip(orders, pieces):
@@ -255,25 +282,30 @@
             )
         )
     vectors = jnp.concatenate(rows, axis=0)
-    normal = normal_of(images_of(vectors, samples_ref, wide_ref), samples_ref, moved_ref)
+    normal = normal_of(vectors, samples_ref, wide_ref, images_ref, moved_ref)
     scaled = []
     for k in range(cols):
         part = normal[k * KER : (k + 1) * KER]
         scaled.append(part * (1.0 / jnp.max(jnp.abs(part))))
     normal = jnp.concatenate(scaled, axis=0)
     store_by_rows(normal, send_ref, 0)
-    normal = normal_of(images_of(normal, samples_ref, wide_ref), samples_ref, moved_ref)
+    normal = normal_of(normal, samples_ref, wide_ref, images_ref, moved_ref)
     normal_ref[...] = normal
     store_by_rows(normal, send_ref, 1)
     store_by_groups(normal_ref, group_ref)
 
 
-def images_kernel(samples_ref, vectors_ref, send_ref, wide_ref):
+def images_kernel(samples_ref, vectors_ref, send_ref, wide_ref, images_ref):
     tiles, groups, cols, reach = send_ref.shape
     tile = samples_ref.shape[-1]
-    images = jnp.concatenate(images_of(vectors_ref[...], samples_ref, wide_ref), axis=0)
-    positions = images.shape[1]
-    images = pltpu.roll(images, positions - (KER - 1), 1)
+    store = widened(vectors_ref[...], samples_ref, wide_ref)
+    store(tiles - 1)
+    for t in range(tiles):
+        if t < tiles - 1:
+            store(t)
+        store_images(t, tile, wide_ref, images_ref)
+    positions = tiles * tile
+    images = pltpu.roll(images_ref[:cols, :positions], positions - (KER - 1), 1)
     rim = reach - tile
     for t in range(tiles):
         if t == 0:
@@ -307,12 +339,6 @@
     return lax.dot_general(
         a, b, (dims, ((), ())), precision=lax.Precision.HIGHEST, preferred_element_type=jnp.float32
     )
-
-
-def square(size):
-    at_row = lax.broadcasted_iota(jnp.int32, (size, size), 0)
-    at_col = lax.broadcasted_iota(jnp.int32, (size, size), 1)
-    return at_row, at_col
 
 
 def gram_kernel(cols, per_tile, received_ref, kept_ref, given_ref, turned_ref):
@@ -440,14 +466,15 @@
 
 
 def moved_columns(values, order):
-    devices = len(order)
+    devices = len(order[0])
     at_row, at_col = square(values.shape[0])
     me = lax.axis_index("rows") * lax.axis_size("coil") + lax.axis_index("coil")
     slot = at_col % devices
     mask = jnp.zeros_like(slot)
     bit = 1
     while bit < devices:
-        mask = mask | jnp.where(slot & bit != 0, order[bit], 0)
+        step = jnp.where(2 * at_col < at_col.shape[1], order[0][bit], order[1][bit])
+        mask = mask | jnp.where(slot & bit != 0, step, 0)
         bit *= 2
     source = at_col - slot + lax.bitwise_xor(mask, jnp.full_like(mask, me))
     return exact(values, (at_row == source).astype(jnp.float32))
@@ -460,8 +487,10 @@
     both_ref,
     kspace_hbm,
     mask_hbm,
-    near_ref,
-    far_ref,
+    top_near_ref,
+    top_far_ref,
+    low_near_ref,
+    low_far_ref,
     recovered_ref,
     basis_ref,
     kspace_ref,
@@ -486,9 +515,9 @@
     images_high, images_low = split(images)
     stacked = jnp.concatenate([images_high, images_low], axis=0)
     chg, tile = kspace_ref.shape
-    lanes = near_ref.shape[1]
+    lanes = top_near_ref.shape[1]
     deep = KER * chg // lanes
-    step = cols * deep
+    step = cols // 2 * deep
     factor = moved_columns(both, order)
     estimate = jnp.zeros((chg, reach), jnp.float32)
     for a in range(0, deep, 2):
@@ -496,8 +525,9 @@
             jnp.concatenate(
                 [
                     ref[pl.ds(k * deep + a + i, ref.shape[0] // step, stride=step), :]
-                    for k in range(cols)
-                    for ref in (near_ref, far_ref)
+                    for refs in ((top_near_ref, top_far_ref), (low_near_ref, low_far_ref))
+                    for k in range(cols // 2)
+                    for ref in refs
                 ],
                 axis=0,
             )
@@ -613,23 +643,43 @@
 
 
 def total_beside(kept, given, near, order, images, groups, devices):
+    ways = []
+    mask = devices // 2
+    while mask >= groups:
+        ways.append(mask)
+        mask //= 2
+    half = near.shape[1] // 2
+    parts = [near[:, :half], near[:, half:]]
+    orders = [order, order]
+    ways = [ways, ways[-1:] + ways[:-1]]
+    step = 0
+
+    def advance():
+        for i in range(2):
+            parts[i], orders[i] = gather_round(
+                parts[i], orders[i], [ways[i][step]], devices, AXES
+            )
+
     total = kept + exchange(given, devices, 1, AXES)
-    mask = devices // 2
     for partners in rounds_of(2, devices):
         terms = [exchange(total, devices, way, AXES) for way in partners]
         total = total + terms[0]
         if len(terms) == 3:
             total = total + (terms[1] + terms[2])
-        if mask > groups:
-            near, order = gather_round(near, order, [mask], devices, AXES)
-            mask //= 2
-    while mask > groups:
-        near, order = gather_round(near, order, [mask], devices, AXES)
-        mask //= 2
+        if step < len(ways[0]) - 1:
+            advance()
+            step += 1
+    while step < len(ways[0]) - 1:
+        advance()
+        step += 1
     other = exchange(total, devices, 1, AXES)
-    near, total, other, images = lax.optimization_barrier((near, total, other, images))
-    far = exchange(near, devices, groups, AXES)
-    return (total, other), near, far, order + [m ^ groups for m in order], to_all(images)
+    *parts, total, other, images = lax.optimization_barrier((*parts, total, other, images))
+    pieces = []
+    for i in range(2):
+        mask = ways[i][-1]
+        pieces += [parts[i], exchange(parts[i], devices, mask, AXES)]
+        orders[i] = orders[i] + [m ^ mask for m in orders[i]]
+    return (total, other), pieces, orders, to_all(images)
 
 
 def column_shards(kspace, sample_mask, start_basis):
@@ -664,7 +714,8 @@
     halves = gather_samples(sampled, tiles, groups, basis_parts)
     starts = (0, chg // len(halves))
     orders = [(start, order) for start, half in zip(starts, halves) for _, order in half]
-    wide = pltpu.VMEM((rows, positions), f32)
+    wide = pltpu.VMEM((rows, LANES + positions), f32)
+    lines = pltpu.VMEM((SUB, positions + LANES), f32)
     moved = pltpu.VMEM((2 * rows, positions), bf16)
     samples, normal, send, group = call(
         functools.partial(passes_kernel, orders),
@@ -676,7 +727,7 @@
         ],
         basis_parts.reshape(tiles, groups, per_tile, lanes),
         *[piece for half in halves for piece, _ in half],
-        scratch=[wide, moved],
+        scratch=[wide, lines, moved],
         micros=12,
     )
     received = to_all(send.reshape(devices, 2 * per_tile, lanes))
@@ -686,7 +737,7 @@
         [((tiles, groups, cols, reach), f32)],
         samples,
         normal,
-        scratch=[wide],
+        scratch=[wide, lines],
         micros=2,
     )
     near, order = gather_group(group, devices)
@@ -697,7 +748,7 @@
         [half, half, ((rank, owned), f32)],
         received.reshape(devices * 2 * per_tile, lanes),
     )
-    gram, near, far, order, images = total_beside(
+    gram, pieces, order, images = total_beside(
         kept, given, near, order, images.reshape(devices, cols, reach), groups, devices
     )
     whole = ((rank, rank), f32)
@@ -721,8 +772,7 @@
         both,
         kspace,
         sample_mask,
-        near.reshape(-1, lanes),
-        far.reshape(-1, lanes),
+        *[piece.reshape(-1, lanes) for piece in pieces],
         scratch=[
             pltpu.VMEM((chg, tile), f32),
             pltpu.VMEM((chg, tile), sample_mask.dtype),
@@ -754,6 +804,8 @@
         and chg % (4 * SUB) == 0
         and (chg * groups) % LANES == 0
         and KER <= LANES
+        and rank // devices <= SUB
+        and rank // devices % 2 == 0
     )
 
 

time: 110 us -> 108 us (0.982)
  waiting for transfers between devices: 35.6 us -> 27.4 us
  starting transfers between devices: 35 us -> 39.8 us
    ppermute x24 -> x27, waiting for transfers between devices: 31.4 us -> 23.2 us  [exchange(): return lax.ppermute(block, axes, [(i, i ^ mask) for i in range(devices)])]
    ppermute x24 -> x27, starting transfers between devices: 24.7 us -> 29 us  [exchange(): return lax.ppermute(block, axes, [(i, i ^ mask) for i in range(devices)])]
  transfers between devices with their start and end apart: 27 -> 30, of which waited for: 15 -> 13; matrix products, arithmetic and copies ran while one was open for 2% -> 2% of each run, Pallas kernels for 14% -> 15%
where the time goes in v9:
time: 108 us
  starting transfers between devices  39.8 us (37%)
  Pallas kernels  36.3 us (34%)
  waiting for transfers between devices  27.4 us (25%)
  other arithmetic  1.84 us (2%)
  between operations  1.7 us (2%)
    pallas_call x6, Pallas kernels, call(): pl.pallas_call(kernel, out_shape=[jax.ShapeDtypeStruct(shape, kind) for s...  36.3 us
    ppermute x27, starting transfers between devices, exchange(): return lax.ppermute(block, axes, [(i, i ^ mask) for i in range(devices)])  29 us
    ppermute x27, waiting for transfers between devices, exchange(): return lax.ppermute(block, axes, [(i, i ^ mask) for i in range(devices)])  23.2 us
    all_to_all x3, starting transfers between devices, to_all(): return lax.all_to_all(pieces, axes, 0, 0, tiled=True)  10.8 us
    all_to_all x3, waiting for transfers between devices, to_all(): return lax.all_to_all(pieces, axes, 0, 0, tiled=True)  4.2 us
  transfers between devices with their start and end apart: 30, of which 13 were waited for; matrix products, arithmetic and copies ran while one was open for 2% of the time, Pallas kernels for 15%

profile of v9, /device:TPU:0, one launch (start us, length us, event | category | flops | bytes accessed | tf_op | source)
XLA Modules:
  0.0 107.9 jit_solution(18287799199155968584)
XLA Ops:
  0.6 1.9 %shard_map.50 = (f32[32,512]{1,0:T(8,128)}, f32[256,128]{1,0:T(8,128)}) custom-call(f32[32,512]{1,0:T(8,128)} %kspace_hbm.3, s32[32,512]{1,0:T(8,128)} %mask_hbm.3, f32[256,128]{1,0:T(8,128)} %bitcast.23), custom_call_target="tpu_custom_call" | custom-call | flops 1000000000 | tf_op jit(solution)/shard_map/pallas_call | solution.py:556
  2.5 4.1 %collective-permute-start.5 = (f32[1,32,512]{2,1,0:T(8,128)}, f32[1,32,512]{2,1,0:T(8,128)S(1)}, u32[]{:S(2)}, u32[]{:S(2)}) collective-permute-start(f32[1,32,512]{2,1,0:T(8,128)} %bitcast.19), channel_id=1, source_target_pairs={{0,16},{1,17},{2,18},{3,19},{4,20},{5,21},{6,22},{7,23},{8,24},{9,... | collective-permute-start | bytes 196616 | tf_op jit(solution)/shard_map/ppermute | solution.py:574
  6.6 3.8 %all-to-all-start = ((f32[32,8,128]{2,1,0:T(8,128)}), f32[32,8,128]{2,1,0:T(8,128)S(1)}, u32[]{:S(2)}, u32[]{:S(2)}) async-start(f32[32,8,128]{2,1,0:T(8,128)} %bitcast.22), calls=%async_computation | async-start | bytes 262144 | tf_op jit(solution)/shard_map/all_to_all | solution.py:635
  10.5 0.8 pad_maximum_fusion.5
  11.3 1.8 %collective-permute-start.6 = (f32[2,32,512]{2,1,0:T(8,128)S(1)}, f32[2,32,512]{2,1,0:T(8,128)S(1)}, u32[]{:S(2)}, u32[]{:S(2)}) collective-permute-start(f32[2,32,512]{2,1,0:T(8,128)S(1)} %pad_maximum_fusion.5), channel_id=1, source_target_pairs={{0,8},{1,9},{2,10},{3,11},{4,12},{5,13},{6,14},{7,15},{8,0},{9,1},... | collective-permute-start | bytes 393224 | tf_op jit(solution)/shard_map/ppermute | solution.py:574
  13.2 5.3 %collective-permute-done.6 = f32[2,32,512]{2,1,0:T(8,128)S(1)} collective-permute-done((f32[2,32,512]{2,1,0:T(8,128)S(1)}, f32[2,32,512]{2,1,0:T(8,128)S(1)}, u32[]{:S(2)}, u32[]{:S(2)}) %collective-permute-start.6) | collective-permute-done | bytes 131104 | tf_op jit(solution)/shard_map/ppermute | solution.py:574
  18.5 0.9 pad_maximum_fusion
  19.4 1.6 %collective-permute-start.7 = (f32[4,16,512]{2,1,0:T(8,128)S(1)}, f32[4,16,512]{2,1,0:T(8,128)S(1)}, u32[]{:S(2)}, u32[]{:S(2)}) collective-permute-start(f32[4,16,512]{2,1,0:T(8,128)S(1)} %get-tuple-element.57), channel_id=1, source_target_pairs={{0,4},{1,5},{2,6},{3,7},{4,0},{5,1},{6,2},{7,3},{8,12},{9,13},{10,... | collective-permute-start | bytes 393224 | tf_op jit(solution)/shard_map/ppermute | solution.py:574
  21.0 1.5 %collective-permute-start.11 = (f32[4,16,512]{2,1,0:T(8,128)S(1)}, f32[4,16,512]{2,1,0:T(8,128)S(1)}, u32[]{:S(2)}, u32[]{:S(2)}) collective-permute-start(f32[4,16,512]{2,1,0:T(8,128)S(1)} %get-tuple-element.56), channel_id=1, source_target_pairs={{0,2},{1,3},{2,0},{3,1},{4,6},{5,7},{6,4},{7,5},{8,10},{9,11},{10,... | collective-permute-start | bytes 393224 | tf_op jit(solution)/shard_map/ppermute | solution.py:574
  22.5 2.4 %collective-permute-done.7 = f32[4,16,512]{2,1,0:T(8,128)S(1)} collective-permute-done((f32[4,16,512]{2,1,0:T(8,128)S(1)}, f32[4,16,512]{2,1,0:T(8,128)S(1)}, u32[]{:S(2)}, u32[]{:S(2)}) %collective-permute-start.7) | collective-permute-done | bytes 131104 | tf_op jit(solution)/shard_map/ppermute | solution.py:574
  24.9 1.3 %collective-permute-start.8 = (f32[8,16,512]{2,1,0:T(8,128)S(1)}, f32[8,16,512]{2,1,0:T(8,128)S(1)}, u32[]{:S(2)}, u32[]{:S(2)}) collective-permute-start(f32[8,16,512]{2,1,0:T(8,128)S(1)} %pad_maximum_fusion.1.refs_0_), channel_id=1, source_target_pairs={{0,2},{1,3},{2,0},{3,1},{4,6},{5,7},{6,4},{7,5},{8,10},{9,11},{10,... | collective-permute-start | bytes 786440 | tf_op jit(solution)/shard_map/ppermute | solution.py:574
  26.2 1.5 %collective-permute-start.12 = (f32[8,16,512]{2,1,0:T(8,128)S(1)}, f32[8,16,512]{2,1,0:T(8,128)S(1)}, u32[]{:S(2)}, u32[]{:S(2)}) collective-permute-start(f32[8,16,512]{2,1,0:T(8,128)S(1)} %pad_maximum_fusion.2.refs_4_), channel_id=1, source_target_pairs={{0,4},{1,5},{2,6},{3,7},{4,0},{5,1},{6,2},{7,3},{8,12},{9,13},{10,... | collective-permute-start | bytes 786440 | tf_op jit(solution)/shard_map/ppermute | solution.py:574
  27.8 0.5 collective-permute-start.13
  28.3 4.0 %collective-permute-done.8.refs_1_ = f32[8,16,512]{2,1,0:T(8,128)S(1)} collective-permute-done((f32[8,16,512]{2,1,0:T(8,128)S(1)}, f32[8,16,512]{2,1,0:T(8,128)S(1)}, u32[]{:S(2)}, u32[]{:S(2)}) %collective-permute-start.8) | collective-permute-done | bytes 262176 | tf_op jit(solution)/shard_map/ppermute | solution.py:574
  32.3 0.8 collective-permute-done.12.refs_5_
  33.1 0.8 collective-permute-done.10.refs_3_
  33.8 0.8 collective-permute-done.14.refs_7_
  34.6 13.3 %shard_map.51 = (bf16[8,2,4,32,512]{4,3,2,1,0:T(8,128)(2,1)S(1)}, f32[256,128]{1,0:T(8,128)S(1)}, f32[8,4,2,8,128]{4,3,2,1,0:T(8,128)}, f32[4,64,128]{2,1,0:T(8,128)S(1)}) custom-call(f32[8,4,8,128]{3,2,1,0:T(8,128)S(1)} %bitcast.16, f32[8,16,512]{2,1,0:T(8,128)S(1)} %pad_maximum_fusion.1.refs_0_, f32[8,16,512]{2,1,0:T(8,128)S(1)} %collective-permute-done.8.refs_1_, ...), custom_call_target="tpu_custom_call" | custom-call | flops 12000000000 | tf_op jit(solution)/shard_map/pallas_call | solution.py:556
  47.9 3.8 %all-to-all-start.1 = ((f32[32,16,128]{2,1,0:T(8,128)}), f32[32,16,128]{2,1,0:T(8,128)S(1)}, u32[]{:S(2)}, u32[]{:S(2)}) async-start(f32[32,16,128]{2,1,0:T(8,128)} %bitcast.4), calls=%async_computation.1 | async-start | bytes 524288 | tf_op jit(solution)/shard_map/all_to_all | solution.py:635
  51.8 1.4 %collective-permute-start.17 = (f32[1,64,128]{2,1,0:T(8,128)S(1)}, f32[1,64,128]{2,1,0:T(8,128)S(1)}, u32[]{:S(2)}, u32[]{:S(2)}) collective-permute-start(f32[1,64,128]{2,1,0:T(8,128)S(1)} %get-tuple-element.61), channel_id=1, source_target_pairs={{0,3},{1,2},{2,1},{3,0},{4,7},{5,6},{6,5},{7,4},{8,11},{9,10},{10,... | collective-permute-start | bytes 98312 | tf_op jit(solution)/shard_map/ppermute | solution.py:574
  53.2 0.4 collective-permute-start.16
  53.6 0.2 collective-permute-start.15
  53.7 3.0 %shard_map.52 = f32[8,4,4,640]{3,2,1,0:T(4,128)} custom-call(bf16[8,2,4,32,512]{4,3,2,1,0:T(8,128)(2,1)S(1)} %get-tuple-element.38.samples_ref, f32[256,128]{1,0:T(8,128)S(1)} %get-tuple-element.39.vectors_ref), custom_call_target="tpu_custom_call" | custom-call | flops 2000000000 | tf_op jit(solution)/shard_map/pallas_call | solution.py:556
  56.8 1.2 %collective-permute-done.16 = f32[1,64,128]{2,1,0:T(8,128)S(1)} collective-permute-done((f32[1,64,128]{2,1,0:T(8,128)S(1)}, f32[1,64,128]{2,1,0:T(8,128)S(1)}, u32[]{:S(2)}, u32[]{:S(2)}) %collective-permute-start.16) | collective-permute-done | bytes 32800 | tf_op jit(solution)/shard_map/ppermute | solution.py:574
  58.0 4.2 %all-to-all-done.1 = f32[32,16,128]{2,1,0:T(8,128)S(1)} async-done(((f32[32,16,128]{2,1,0:T(8,128)}), f32[32,16,128]{2,1,0:T(8,128)S(1)}, u32[]{:S(2)}, u32[]{:S(2)}) %all-to-all-start.1) | async-done | bytes 262176 | tf_op jit(solution)/shard_map/all_to_all | solution.py:635
  62.2 1.0 collective-permute-start.20
  63.2 0.6 shard_map.53
  63.9 0.2 collective-permute-start.18
  64.1 1.0 collective-permute-done.22
  65.1 0.9 collective-permute-start.25
  65.9 1.4 %collective-permute-start.24 = (f32[72,128]{1,0:T(8,128)S(1)}, f32[72,128]{1,0:T(8,128)S(1)}, u32[]{:S(2)}, u32[]{:S(2)}) collective-permute-start(f32[72,128]{1,0:T(8,128)S(1)} %add.36), channel_id=1, source_target_pairs={{0,4},{1,5},{2,6},{3,7},{4,0},{5,1},{6,2},{7,3},{8,12},{9,13},{10,... | collective-permute-start | bytes 110600 | tf_op jit(solution)/shard_map/ppermute | solution.py:574
  67.4 1.2 %collective-permute-start.23 = (f32[72,128]{1,0:T(8,128)S(1)}, f32[72,128]{1,0:T(8,128)S(1)}, u32[]{:S(2)}, u32[]{:S(2)}) collective-permute-start(f32[72,128]{1,0:T(8,128)S(1)} %add.36), channel_id=1, source_target_pairs={{0,2},{1,3},{2,0},{3,1},{4,6},{5,7},{6,4},{7,5},{8,10},{9,11},{10,... | collective-permute-start | bytes 110600 | tf_op jit(solution)/shard_map/ppermute | solution.py:574
  68.6 1.9 %collective-permute-start.21 = (f32[8,32,128]{2,1,0:T(8,128)S(1)}, f32[8,32,128]{2,1,0:T(8,128)S(1)}, u32[]{:S(2)}, u32[]{:S(2)}) collective-permute-start(f32[8,32,128]{2,1,0:T(8,128)S(1)} %pad_maximum_fusion.8), channel_id=1, source_target_pairs={{0,16},{1,17},{2,18},{3,19},{4,20},{5,21},{6,22},{7,23},{8,24},{9,... | collective-permute-start | bytes 393224 | tf_op jit(solution)/shard_map/ppermute | solution.py:574
  70.5 0.8 collective-permute-done.23
  71.3 1.7 %collective-permute-start.28 = (f32[72,128]{1,0:T(8,128)S(1)}, f32[72,128]{1,0:T(8,128)S(1)}, u32[]{:S(2)}, u32[]{:S(2)}) collective-permute-start(f32[72,128]{1,0:T(8,128)S(1)} %add_add_fusion.1), channel_id=1, source_target_pairs={{0,24},{1,25},{2,26},{3,27},{4,28},{5,29},{6,30},{7,31},{8,16},{9,... | collective-permute-start | bytes 110600 | tf_op jit(solution)/shard_map/ppermute | solution.py:574
  73.1 0.7 collective-permute-start.27
  73.8 2.0 %collective-permute-start.26 = (f32[72,128]{1,0:T(8,128)S(1)}, f32[72,128]{1,0:T(8,128)S(1)}, u32[]{:S(2)}, u32[]{:S(2)}) collective-permute-start(f32[72,128]{1,0:T(8,128)S(1)} %add_add_fusion.1), channel_id=1, source_target_pairs={{0,8},{1,9},{2,10},{3,11},{4,12},{5,13},{6,14},{7,15},{8,0},{9,1},... | collective-permute-start | bytes 110600 | tf_op jit(solution)/shard_map/ppermute | solution.py:574
  75.9 1.7 %collective-permute-done.28 = f32[72,128]{1,0:T(8,128)S(1)} collective-permute-done((f32[72,128]{1,0:T(8,128)S(1)}, f32[72,128]{1,0:T(8,128)S(1)}, u32[]{:S(2)}, u32[]{:S(2)}) %collective-permute-start.28) | collective-permute-done | bytes 36896 | tf_op jit(solution)/shard_map/ppermute | solution.py:574
  77.6 2.7 %collective-permute-done.27 = f32[72,128]{1,0:T(8,128)S(1)} collective-permute-done((f32[72,128]{1,0:T(8,128)S(1)}, f32[72,128]{1,0:T(8,128)S(1)}, u32[]{:S(2)}, u32[]{:S(2)}) %collective-permute-start.27) | collective-permute-done | bytes 36896 | tf_op jit(solution)/shard_map/ppermute | solution.py:574
  80.4 1.8 %collective-permute-done.19 = f32[8,32,128]{2,1,0:T(8,128)S(1)} collective-permute-done((f32[8,32,128]{2,1,0:T(8,128)S(1)}, f32[8,32,128]{2,1,0:T(8,128)S(1)}, u32[]{:S(2)}, u32[]{:S(2)}) %collective-permute-start.19) | collective-permute-done | bytes 131104 | tf_op jit(solution)/shard_map/ppermute | solution.py:574
  82.3 3.1 %all-to-all-start.2 = ((f32[32,4,640]{2,1,0:T(4,128)}), f32[32,4,640]{2,1,0:T(4,128)S(1)}, u32[]{:S(2)}, u32[]{:S(2)}) async-start(f32[32,4,640]{2,1,0:T(4,128)} %bitcast.6), calls=%async_computation.2 | async-start | bytes 655360 | tf_op jit(solution)/shard_map/all_to_all | solution.py:635
  85.4 1.8 %collective-permute-start.30 = (f32[16,32,128]{2,1,0:T(8,128)S(1)}, f32[16,32,128]{2,1,0:T(8,128)S(1)}, u32[]{:S(2)}, u32[]{:S(2)}) collective-permute-start(f32[16,32,128]{2,1,0:T(8,128)S(1)} %pad_maximum_fusion.3), channel_id=1, source_target_pairs={{0,4},{1,5},{2,6},{3,7},{4,0},{5,1},{6,2},{7,3},{8,12},{9,13},{10,... | collective-permute-start | bytes 786440 | tf_op jit(solution)/shard_map/ppermute | solution.py:574
  87.2 1.5 %collective-permute-start.31 = (f32[16,32,128]{2,1,0:T(8,128)S(1)}, f32[16,32,128]{2,1,0:T(8,128)S(1)}, u32[]{:S(2)}, u32[]{:S(2)}) collective-permute-start(f32[16,32,128]{2,1,0:T(8,128)S(1)} %pad_maximum_fusion.4), channel_id=1, source_target_pairs={{0,8},{1,9},{2,10},{3,11},{4,12},{5,13},{6,14},{7,15},{8,0},{9,1},... | collective-permute-start | bytes 786440 | tf_op jit(solution)/shard_map/ppermute | solution.py:574
  88.7 12.6 %shard_map.54 = (f32[128,128]{1,0:T(8,128)S(1)}, f32[128,128]{1,0:T(8,128)S(1)}, s32[1]{0:T(128)}) custom-call(f32[72,128]{1,0:T(8,128)S(1)} %add_add_fusion.gram_ref, f32[72,128]{1,0:T(8,128)S(1)} %collective-permute-done.29.other_ref), custom_call_target="tpu_custom_call" | custom-call | flops 12000000000 | tf_op jit(solution)/shard_map/pallas_call | solution.py:556
  102.0 0.2 conditional.1
  102.3 0.1 reshape.50.images_ref
  102.4 0.4 copy-done
  102.9 4.9 %shard_map.55 = (f32[32,512]{1,0:T(8,128)}, f32[256,128]{1,0:T(8,128)}) custom-call(f32[128,640]{1,0:T(8,128)S(1)} %reshape.50.images_ref, f32[128,128]{1,0:T(8,128)S(1)} %get-tuple-element.64.both_ref, f32[32,512]{1,0:T(8,128)S(1)} %copy-done, s32[32,512]{1,0:T(8,128)S(1)} %copy-done.1, f32[512,128]{1,0:T(8,128)S(1)} %bitcast.14, f32[512,128]{1,0:T(8,128)S(1)} %bitcast.17, ...), custom_call_target="tpu_custom_call" | custom-call | flops 5000000000 | tf_op jit(solution)/shard_map/pallas_call | solution.py:556
  (39 shorter events, 0.5 us)
Async XLA Ops:
  2.5 8.0 %collective-permute-start.5 = (f32[1,32,512]{2,1,0:T(8,128)}, f32[1,32,512]{2,1,0:T(8,128)S(1)}, u32[]{:S(2)}, u32[]{:S(2)}) collective-permute-start(f32[1,32,512]{2,1,0:T(8,128)} %bitcast.19), channel_id=1, source_target_pairs={{0,16},{1,17},{2,18},{3,19},{4,20},{5,21},{6,22},{7,23},{8,24},{9,... | collective-permute-start | bytes 196616 | tf_op jit(solution)/shard_map/ppermute | solution.py:574
  6.6 12.7 %all-to-all-start = ((f32[32,8,128]{2,1,0:T(8,128)}), f32[32,8,128]{2,1,0:T(8,128)S(1)}, u32[]{:S(2)}, u32[]{:S(2)}) async-start(f32[32,8,128]{2,1,0:T(8,128)} %bitcast.22), calls=%async_computation | async-start | bytes 262144 | tf_op jit(solution)/shard_map/all_to_all | solution.py:635
  11.3 7.1 %collective-permute-start.6 = (f32[2,32,512]{2,1,0:T(8,128)S(1)}, f32[2,32,512]{2,1,0:T(8,128)S(1)}, u32[]{:S(2)}, u32[]{:S(2)}) collective-permute-start(f32[2,32,512]{2,1,0:T(8,128)S(1)} %pad_maximum_fusion.5), channel_id=1, source_target_pairs={{0,8},{1,9},{2,10},{3,11},{4,12},{5,13},{6,14},{7,15},{8,0},{9,1},... | collective-permute-start | bytes 393224 | tf_op jit(solution)/shard_map/ppermute | solution.py:574
  19.4 5.5 %collective-permute-start.7 = (f32[4,16,512]{2,1,0:T(8,128)S(1)}, f32[4,16,512]{2,1,0:T(8,128)S(1)}, u32[]{:S(2)}, u32[]{:S(2)}) collective-permute-start(f32[4,16,512]{2,1,0:T(8,128)S(1)} %get-tuple-element.57), channel_id=1, source_target_pairs={{0,4},{1,5},{2,6},{3,7},{4,0},{5,1},{6,2},{7,3},{8,12},{9,13},{10,... | collective-permute-start | bytes 393224 | tf_op jit(solution)/shard_map/ppermute | solution.py:574
  21.0 5.2 %collective-permute-start.11 = (f32[4,16,512]{2,1,0:T(8,128)S(1)}, f32[4,16,512]{2,1,0:T(8,128)S(1)}, u32[]{:S(2)}, u32[]{:S(2)}) collective-permute-start(f32[4,16,512]{2,1,0:T(8,128)S(1)} %get-tuple-element.56), channel_id=1, source_target_pairs={{0,2},{1,3},{2,0},{3,1},{4,6},{5,7},{6,4},{7,5},{8,10},{9,11},{10,... | collective-permute-start | bytes 393224 | tf_op jit(solution)/shard_map/ppermute | solution.py:574
  24.9 7.4 %collective-permute-start.8 = (f32[8,16,512]{2,1,0:T(8,128)S(1)}, f32[8,16,512]{2,1,0:T(8,128)S(1)}, u32[]{:S(2)}, u32[]{:S(2)}) collective-permute-start(f32[8,16,512]{2,1,0:T(8,128)S(1)} %pad_maximum_fusion.1.refs_0_), channel_id=1, source_target_pairs={{0,2},{1,3},{2,0},{3,1},{4,6},{5,7},{6,4},{7,5},{8,10},{9,11},{10,... | collective-permute-start | bytes 786440 | tf_op jit(solution)/shard_map/ppermute | solution.py:574
  26.2 6.8 %collective-permute-start.12 = (f32[8,16,512]{2,1,0:T(8,128)S(1)}, f32[8,16,512]{2,1,0:T(8,128)S(1)}, u32[]{:S(2)}, u32[]{:S(2)}) collective-permute-start(f32[8,16,512]{2,1,0:T(8,128)S(1)} %pad_maximum_fusion.2.refs_4_), channel_id=1, source_target_pairs={{0,4},{1,5},{2,6},{3,7},{4,0},{5,1},{6,2},{7,3},{8,12},{9,13},{10,... | collective-permute-start | bytes 786440 | tf_op jit(solution)/shard_map/ppermute | solution.py:574
  27.8 5.3 %collective-permute-start.9 = (f32[8,16,512]{2,1,0:T(8,128)S(1)}, f32[8,16,512]{2,1,0:T(8,128)S(1)}, u32[]{:S(2)}, u32[]{:S(2)}) collective-permute-start(f32[8,16,512]{2,1,0:T(8,128)S(1)} %pad_maximum_fusion.1.refs_0_), channel_id=1, source_target_pairs={{0,1},{1,0},{2,3},{3,2},{4,5},{5,4},{6,7},{7,6},{8,9},{9,8},{10,11... | collective-permute-start | bytes 786440 | tf_op jit(solution)/shard_map/ppermute | solution.py:574
  27.8 5.3 %collective-permute-start.13 = (f32[8,16,512]{2,1,0:T(8,128)S(1)}, f32[8,16,512]{2,1,0:T(8,128)S(1)}, u32[]{:S(2)}, u32[]{:S(2)}) collective-permute-start(f32[8,16,512]{2,1,0:T(8,128)S(1)} %pad_maximum_fusion.2.refs_4_), channel_id=1, source_target_pairs={{0,1},{1,0},{2,3},{3,2},{4,5},{5,4},{6,7},{7,6},{8,9},{9,8},{10,11... | collective-permute-start | bytes 786440 | tf_op jit(solution)/shard_map/ppermute | solution.py:574
  32.3 1.5 %collective-permute-start.10 = (f32[8,16,512]{2,1,0:T(8,128)S(1)}, f32[8,16,512]{2,1,0:T(8,128)S(1)}, u32[]{:S(2)}, u32[]{:S(2)}) collective-permute-start(f32[8,16,512]{2,1,0:T(8,128)S(1)} %collective-permute-done.8.refs_1_), channel_id=1, source_target_pairs={{0,1},{1,0},{2,3},{3,2},{4,5},{5,4},{6,7},{7,6},{8,9},{9,8},{10,11... | collective-permute-start | bytes 786440 | tf_op jit(solution)/shard_map/ppermute | solution.py:574
  33.1 1.5 %collective-permute-start.14 = (f32[8,16,512]{2,1,0:T(8,128)S(1)}, f32[8,16,512]{2,1,0:T(8,128)S(1)}, u32[]{:S(2)}, u32[]{:S(2)}) collective-permute-start(f32[8,16,512]{2,1,0:T(8,128)S(1)} %collective-permute-done.12.refs_5_), channel_id=1, source_target_pairs={{0,1},{1,0},{2,3},{3,2},{4,5},{5,4},{6,7},{7,6},{8,9},{9,8},{10,11... | collective-permute-start | bytes 786440 | tf_op jit(solution)/shard_map/ppermute | solution.py:574
  47.9 14.3 %all-to-all-start.1 = ((f32[32,16,128]{2,1,0:T(8,128)}), f32[32,16,128]{2,1,0:T(8,128)S(1)}, u32[]{:S(2)}, u32[]{:S(2)}) async-start(f32[32,16,128]{2,1,0:T(8,128)} %bitcast.4), calls=%async_computation.1 | async-start | bytes 524288 | tf_op jit(solution)/shard_map/all_to_all | solution.py:635
  51.8 5.0 %collective-permute-start.17 = (f32[1,64,128]{2,1,0:T(8,128)S(1)}, f32[1,64,128]{2,1,0:T(8,128)S(1)}, u32[]{:S(2)}, u32[]{:S(2)}) collective-permute-start(f32[1,64,128]{2,1,0:T(8,128)S(1)} %get-tuple-element.61), channel_id=1, source_target_pairs={{0,3},{1,2},{2,1},{3,0},{4,7},{5,6},{6,5},{7,4},{8,11},{9,10},{10,... | collective-permute-start | bytes 98312 | tf_op jit(solution)/shard_map/ppermute | solution.py:574
  53.2 4.8 %collective-permute-start.16 = (f32[1,64,128]{2,1,0:T(8,128)S(1)}, f32[1,64,128]{2,1,0:T(8,128)S(1)}, u32[]{:S(2)}, u32[]{:S(2)}) collective-permute-start(f32[1,64,128]{2,1,0:T(8,128)S(1)} %get-tuple-element.62), channel_id=1, source_target_pairs={{0,2},{1,3},{2,0},{3,1},{4,6},{5,7},{6,4},{7,5},{8,10},{9,11},{10,... | collective-permute-start | bytes 98312 | tf_op jit(solution)/shard_map/ppermute | solution.py:574
  53.6 4.4 %collective-permute-start.15 = (f32[1,64,128]{2,1,0:T(8,128)S(1)}, f32[1,64,128]{2,1,0:T(8,128)S(1)}, u32[]{:S(2)}, u32[]{:S(2)}) collective-permute-start(f32[1,64,128]{2,1,0:T(8,128)S(1)} %get-tuple-element.63), channel_id=1, source_target_pairs={{0,1},{1,0},{2,3},{3,2},{4,5},{5,4},{6,7},{7,6},{8,9},{9,8},{10,11... | collective-permute-start | bytes 98312 | tf_op jit(solution)/shard_map/ppermute | solution.py:574
  62.2 6.4 %collective-permute-start.20 = (f32[4,32,128]{2,1,0:T(8,128)S(1)}, f32[4,32,128]{2,1,0:T(8,128)S(1)}, u32[]{:S(2)}, u32[]{:S(2)}) collective-permute-start(f32[4,32,128]{2,1,0:T(8,128)S(1)} %get-tuple-element.58), channel_id=1, source_target_pairs={{0,4},{1,5},{2,6},{3,7},{4,0},{5,1},{6,2},{7,3},{8,12},{9,13},{10,... | collective-permute-start | bytes 196616 | tf_op jit(solution)/shard_map/ppermute | solution.py:574
  63.8 1.3 %collective-permute-start.22 = (f32[72,128]{1,0:T(8,128)S(1)}, f32[72,128]{1,0:T(8,128)S(1)}, u32[]{:S(2)}, u32[]{:S(2)}) collective-permute-start(f32[72,128]{1,0:T(8,128)S(1)} %get-tuple-element.44), channel_id=1, source_target_pairs={{0,1},{1,0},{2,3},{3,2},{4,5},{5,4},{6,7},{7,6},{8,9},{9,8},{10,11... | collective-permute-start | bytes 110600 | tf_op jit(solution)/shard_map/ppermute | solution.py:574
  63.9 11.9 %collective-permute-start.18 = (f32[4,32,128]{2,1,0:T(8,128)S(1)}, f32[4,32,128]{2,1,0:T(8,128)S(1)}, u32[]{:S(2)}, u32[]{:S(2)}) collective-permute-start(f32[4,32,128]{2,1,0:T(8,128)S(1)} %get-tuple-element.59), channel_id=1, source_target_pairs={{0,16},{1,17},{2,18},{3,19},{4,20},{5,21},{6,22},{7,23},{8,24},{9,... | collective-permute-start | bytes 196616 | tf_op jit(solution)/shard_map/ppermute | solution.py:574
  65.1 5.4 %collective-permute-start.25 = (f32[72,128]{1,0:T(8,128)S(1)}, f32[72,128]{1,0:T(8,128)S(1)}, u32[]{:S(2)}, u32[]{:S(2)}) collective-permute-start(f32[72,128]{1,0:T(8,128)S(1)} %add.36), channel_id=1, source_target_pairs={{0,6},{1,7},{2,4},{3,5},{4,2},{5,3},{6,0},{7,1},{8,14},{9,15},{10,... | collective-permute-start | bytes 110600 | tf_op jit(solution)/shard_map/ppermute | solution.py:574
  65.9 4.6 %collective-permute-start.24 = (f32[72,128]{1,0:T(8,128)S(1)}, f32[72,128]{1,0:T(8,128)S(1)}, u32[]{:S(2)}, u32[]{:S(2)}) collective-permute-start(f32[72,128]{1,0:T(8,128)S(1)} %add.36), channel_id=1, source_target_pairs={{0,4},{1,5},{2,6},{3,7},{4,0},{5,1},{6,2},{7,3},{8,12},{9,13},{10,... | collective-permute-start | bytes 110600 | tf_op jit(solution)/shard_map/ppermute | solution.py:574
  67.4 4.0 %collective-permute-start.23 = (f32[72,128]{1,0:T(8,128)S(1)}, f32[72,128]{1,0:T(8,128)S(1)}, u32[]{:S(2)}, u32[]{:S(2)}) collective-permute-start(f32[72,128]{1,0:T(8,128)S(1)} %add.36), channel_id=1, source_target_pairs={{0,2},{1,3},{2,0},{3,1},{4,6},{5,7},{6,4},{7,5},{8,10},{9,11},{10,... | collective-permute-start | bytes 110600 | tf_op jit(solution)/shard_map/ppermute | solution.py:574
  68.6 11.8 %collective-permute-start.21 = (f32[8,32,128]{2,1,0:T(8,128)S(1)}, f32[8,32,128]{2,1,0:T(8,128)S(1)}, u32[]{:S(2)}, u32[]{:S(2)}) collective-permute-start(f32[8,32,128]{2,1,0:T(8,128)S(1)} %pad_maximum_fusion.8), channel_id=1, source_target_pairs={{0,16},{1,17},{2,18},{3,19},{4,20},{5,21},{6,22},{7,23},{8,24},{9,... | collective-permute-start | bytes 393224 | tf_op jit(solution)/shard_map/ppermute | solution.py:574
  71.3 6.3 %collective-permute-start.28 = (f32[72,128]{1,0:T(8,128)S(1)}, f32[72,128]{1,0:T(8,128)S(1)}, u32[]{:S(2)}, u32[]{:S(2)}) collective-permute-start(f32[72,128]{1,0:T(8,128)S(1)} %add_add_fusion.1), channel_id=1, source_target_pairs={{0,24},{1,25},{2,26},{3,27},{4,28},{5,29},{6,30},{7,31},{8,16},{9,... | collective-permute-start | bytes 110600 | tf_op jit(solution)/shard_map/ppermute | solution.py:574
  73.1 7.2 %collective-permute-start.27 = (f32[72,128]{1,0:T(8,128)S(1)}, f32[72,128]{1,0:T(8,128)S(1)}, u32[]{:S(2)}, u32[]{:S(2)}) collective-permute-start(f32[72,128]{1,0:T(8,128)S(1)} %add_add_fusion.1), channel_id=1, source_target_pairs={{0,16},{1,17},{2,18},{3,19},{4,20},{5,21},{6,22},{7,23},{8,24},{9,... | collective-permute-start | bytes 110600 | tf_op jit(solution)/shard_map/ppermute | solution.py:574
  73.8 6.5 %collective-permute-start.26 = (f32[72,128]{1,0:T(8,128)S(1)}, f32[72,128]{1,0:T(8,128)S(1)}, u32[]{:S(2)}, u32[]{:S(2)}) collective-permute-start(f32[72,128]{1,0:T(8,128)S(1)} %add_add_fusion.1), channel_id=1, source_target_pairs={{0,8},{1,9},{2,10},{3,11},{4,12},{5,13},{6,14},{7,15},{8,0},{9,1},... | collective-permute-start | bytes 110600 | tf_op jit(solution)/shard_map/ppermute | solution.py:574
  75.8 6.4 %collective-permute-start.19 = (f32[8,32,128]{2,1,0:T(8,128)S(1)}, f32[8,32,128]{2,1,0:T(8,128)S(1)}, u32[]{:S(2)}, u32[]{:S(2)}) collective-permute-start(f32[8,32,128]{2,1,0:T(8,128)S(1)} %pad_maximum_fusion.7), channel_id=1, source_target_pairs={{0,8},{1,9},{2,10},{3,11},{4,12},{5,13},{6,14},{7,15},{8,0},{9,1},... | collective-permute-start | bytes 393224 | tf_op jit(solution)/shard_map/ppermute | solution.py:574
  80.3 2.0 %collective-permute-start.29 = (f32[72,128]{1,0:T(8,128)S(1)}, f32[72,128]{1,0:T(8,128)S(1)}, u32[]{:S(2)}, u32[]{:S(2)}) collective-permute-start(f32[72,128]{1,0:T(8,128)S(1)} %add_add_fusion.gram_ref), channel_id=1, source_target_pairs={{0,1},{1,0},{2,3},{3,2},{4,5},{5,4},{6,7},{7,6},{8,9},{9,8},{10,11... | collective-permute-start | bytes 110600 | tf_op jit(solution)/shard_map/ppermute | solution.py:574
  82.3 20.0 %all-to-all-start.2 = ((f32[32,4,640]{2,1,0:T(4,128)}), f32[32,4,640]{2,1,0:T(4,128)S(1)}, u32[]{:S(2)}, u32[]{:S(2)}) async-start(f32[32,4,640]{2,1,0:T(4,128)} %bitcast.6), calls=%async_computation.2 | async-start | bytes 655360 | tf_op jit(solution)/shard_map/all_to_all | solution.py:635
  85.4 17.0 %collective-permute-start.30 = (f32[16,32,128]{2,1,0:T(8,128)S(1)}, f32[16,32,128]{2,1,0:T(8,128)S(1)}, u32[]{:S(2)}, u32[]{:S(2)}) collective-permute-start(f32[16,32,128]{2,1,0:T(8,128)S(1)} %pad_maximum_fusion.3), channel_id=1, source_target_pairs={{0,4},{1,5},{2,6},{3,7},{4,0},{5,1},{6,2},{7,3},{8,12},{9,13},{10,... | collective-permute-start | bytes 786440 | tf_op jit(solution)/shard_map/ppermute | solution.py:574
  87.2 15.1 %collective-permute-start.31 = (f32[16,32,128]{2,1,0:T(8,128)S(1)}, f32[16,32,128]{2,1,0:T(8,128)S(1)}, u32[]{:S(2)}, u32[]{:S(2)}) collective-permute-start(f32[16,32,128]{2,1,0:T(8,128)S(1)} %pad_maximum_fusion.4), channel_id=1, source_target_pairs={{0,8},{1,9},{2,10},{3,11},{4,12},{5,13},{6,14},{7,15},{8,0},{9,1},... | collective-permute-start | bytes 786440 | tf_op jit(solution)/shard_map/ppermute | solution.py:574
  102.0 0.8 copy-start
  102.0 0.9 copy-start.1

commit v10 on v8

--- a/solution.py
+++ b/solution.py
@@ -112,6 +112,12 @@
     return dot(a_high, b_high, dims) + (dot(a_high, b_low, dims) + dot(a_low, b_high, dims))
 
 
+def square(size):
+    at_row = lax.broadcasted_iota(jnp.int32, (size, size), 0)
+    at_col = lax.broadcasted_iota(jnp.int32, (size, size), 1)
+    return at_row, at_col
+
+
 def prepare_kernel(
     cols,
     chg,
@@ -150,19 +156,15 @@
     rows, channels = vectors.shape
     cols = rows // KER
     high, low = split(vectors)
-    at_row = lax.broadcasted_iota(jnp.int32, (rows, rows), 0)
-    at_col = lax.broadcasted_iota(jnp.int32, (rows, rows), 1)
+    at_row, at_col = square(rows)
     flip = ((at_row // KER == at_col // KER) & (at_row % KER + at_col % KER == KER - 1)).astype(
         jnp.float32
     ).astype(jnp.bfloat16)
     both = dot(flip, jnp.concatenate([high, low], axis=1)).astype(jnp.bfloat16)
     high, low = both[:, :channels], both[:, channels:]
-    twice = jnp.concatenate([high, high], axis=1)
-    tiles = samples_ref.shape[0]
-    tile = samples_ref.shape[-1]
-    for t in range(tiles):
-        block = samples_ref[t].reshape(2 * channels, tile)
-        wide_ref[:, t * tile : (t + 1) * tile] = dot(twice, block) + dot(low, block[:channels])
+    positions = samples_ref.shape[-1]
+    block = samples_ref[...].reshape(3 * channels, positions)
+    wide_ref[...] = dot(jnp.concatenate([high, high, low], axis=1), block)
     images = []
     for k in range(cols):
         total = None
@@ -177,9 +179,7 @@
 def normal_of(images, samples_ref, moved_ref):
     cols = len(images)
     positions = images[0].shape[1]
-    tiles = samples_ref.shape[0]
-    tile = samples_ref.shape[-1]
-    channels = samples_ref.shape[2] * samples_ref.shape[3]
+    channels = samples_ref.shape[1] * samples_ref.shape[2]
     rows = cols * KER
     for k in range(cols):
         base = jnp.broadcast_to(images[k], (SUB, positions))
@@ -190,10 +190,8 @@
             high, low = split(jnp.concatenate([first, second], axis=0))
             moved_ref[k * KER + j : k * KER + j + 2 * SUB, :] = high
             moved_ref[rows + k * KER + j : rows + k * KER + j + 2 * SUB, :] = low
-    total = jnp.zeros((2 * rows, 2 * channels), jnp.float32)
-    for t in range(tiles):
-        block = samples_ref[t].reshape(2 * channels, tile)
-        total = total + dot(moved_ref[:, t * tile : (t + 1) * tile], block, ((1,), (1,)))
+    block = samples_ref[:2].reshape(2 * channels, positions)
+    total = dot(moved_ref[...], block, ((1,), (1,)))
     return total[:rows, :channels] + (
         total[:rows, channels:] + total[rows:, :channels] + total[rows:, channels:]
     )
@@ -232,7 +230,8 @@
 
 def passes_kernel(orders, basis_ref, *refs):
     *pieces, samples_ref, normal_ref, send_ref, group_ref, wide_ref, moved_ref = refs
-    tiles, _, groups, chg, tile = samples_ref.shape
+    _, groups, chg, _ = samples_ref.shape
+    tile = pieces[0].shape[-1]
     me = lax.axis_index("rows") * groups + lax.axis_index("coil")
     for (start, order), piece_ref in zip(orders, pieces):
         count = piece_ref.shape[1]
@@ -240,8 +239,9 @@
             high, low = split(piece_ref[slot])
             source = lax.bitwise_xor(me, mask)
             t, g = source // groups, source % groups
-            samples_ref[t, 0, g, start : start + count] = high
-            samples_ref[t, 1, g, start : start + count] = low
+            lanes = pl.ds(pl.multiple_of(t * tile, tile), tile)
+            for part, value in enumerate((high, low, high)):
+                samples_ref[part, g, start : start + count, lanes] = value
     cols = basis_ref.shape[-1] // chg
     rows = []
     for k in range(cols):
@@ -270,9 +270,9 @@
 
 def images_kernel(samples_ref, vectors_ref, send_ref, wide_ref):
     tiles, groups, cols, reach = send_ref.shape
-    tile = samples_ref.shape[-1]
     images = jnp.concatenate(images_of(vectors_ref[...], samples_ref, wide_ref), axis=0)
     positions = images.shape[1]
+    tile = positions // tiles
     images = pltpu.roll(images, positions - (KER - 1), 1)
     rim = reach - tile
     for t in range(tiles):
@@ -307,12 +307,6 @@
     return lax.dot_general(
         a, b, (dims, ((), ())), precision=lax.Precision.HIGHEST, preferred_element_type=jnp.float32
     )
-
-
-def square(size):
-    at_row = lax.broadcasted_iota(jnp.int32, (size, size), 0)
-    at_col = lax.broadcasted_iota(jnp.int32, (size, size), 1)
-    return at_row, at_col
 
 
 def gram_kernel(cols, per_tile, received_ref, kept_ref, given_ref, turned_ref):
@@ -417,12 +411,12 @@
     return jnp.concatenate(done, axis=0)
 
 
-def factors_kernel(gram_ref, other_ref, first_ref, both_ref, sound_ref):
+def factor_kernel(gram_ref, other_ref, inverse_ref, next_ref, sound_ref):
     gram, raw, line = load_grams(gram_ref, other_ref)
     inverse = inverse_factor(gram)
-    first_ref[...] = inverse
+    inverse_ref[...] = inverse
     gram = exact(exact(inverse, raw), inverse, ((1,), (1,)))
-    both_ref[...] = exact(inverse_factor(gram), inverse)
+    next_ref[...] = gram
     at_row, at_col = square(gram.shape[0])
     terms = jnp.sum(inverse * inverse * line, axis=1, keepdims=True)
     result = jnp.sum(jnp.where(at_row == at_col, gram, 0.0), axis=1, keepdims=True)
@@ -435,7 +429,7 @@
     gram_ref[...] = exact(turned, turned, ((1,), (1,)))
 
 
-def again_kernel(gram_ref, inverse_ref, both_ref):
+def both_kernel(gram_ref, inverse_ref, both_ref):
     both_ref[...] = exact(inverse_factor(gram_ref[...]), inverse_ref[...])
 
 
@@ -614,18 +608,20 @@
 
 def total_beside(kept, given, near, order, images, groups, devices):
     total = kept + exchange(given, devices, 1, AXES)
-    mask = devices // 2
-    for partners in rounds_of(2, devices):
-        terms = [exchange(total, devices, way, AXES) for way in partners]
-        total = total + terms[0]
-        if len(terms) == 3:
-            total = total + (terms[1] + terms[2])
-        if mask > groups:
-            near, order = gather_round(near, order, [mask], devices, AXES)
-            mask //= 2
-    while mask > groups:
-        near, order = gather_round(near, order, [mask], devices, AXES)
-        mask //= 2
+    mask = 2
+    while mask <= groups:
+        total = total + exchange(total, devices, mask, AXES)
+        mask *= 2
+    step = devices // 2
+    near, order = gather_round(near, order, [step], devices, AXES)
+    step //= 2
+    total, near = lax.optimization_barrier((total, near))
+    while mask < devices:
+        total = total + exchange(total, devices, mask, AXES)
+        mask *= 2
+    while step > groups:
+        near, order = gather_round(near, order, [step], devices, AXES)
+        step //= 2
     other = exchange(total, devices, 1, AXES)
     near, total, other, images = lax.optimization_barrier((near, total, other, images))
     far = exchange(near, devices, groups, AXES)
@@ -669,7 +665,7 @@
     samples, normal, send, group = call(
         functools.partial(passes_kernel, orders),
         [
-            ((tiles, 2, groups, chg, tile), bf16),
+            ((3, groups, chg, positions), bf16),
             ((rows, channels), f32),
             ((tiles, groups, 2, per_tile, lanes), f32),
             ((groups, rows * chg // lanes, lanes), f32),
@@ -701,8 +697,8 @@
         kept, given, near, order, images.reshape(devices, cols, reach), groups, devices
     )
     whole = ((rank, rank), f32)
-    first, both, sound = call(
-        factors_kernel, [whole, whole, ((1,), jnp.int32)], *gram, scalars=1, micros=12
+    first, second, sound = call(
+        factor_kernel, [whole, whole, ((1,), jnp.int32)], *gram, scalars=1, micros=12
     )
 
     def again():
@@ -711,9 +707,10 @@
         while mask < devices:
             gram = gram + exchange(gram, devices, mask, AXES)
             mask *= 2
-        return call(again_kernel, [whole], gram, first)[0]
-
-    both = lax.cond(sound[0] == 1, lambda: both, again)
+        return gram
+
+    second = lax.cond(sound[0] == 1, lambda: second, again)
+    (both,) = call(both_kernel, [whole], second, first, micros=0)
     recovered, basis = call(
         functools.partial(last_kernel, cols, order),
         [((chg, tile), f32), ((owned, rank), f32)],
@@ -754,6 +751,8 @@
         and chg % (4 * SUB) == 0
         and (chg * groups) % LANES == 0
         and KER <= LANES
+        and rank // devices <= SUB
+        and rank // devices % 2 == 0
     )
 
 

time: 110 us -> 112 us (1.018)
  local copies, waits for them, and re-layouts: 0.16 us -> 1.72 us
  waiting for transfers between devices: 35.6 us -> 36.9 us
    ppermute x24 -> x22, starting transfers between devices: 24.7 us -> 23 us  [exchange(): return lax.ppermute(block, axes, [(i, i ^ mask) for i in range(devices)])]
    unnamed x4 -> x8, local copies, waits for them, and re-layouts: 0.01 us -> 1.57 us
    ppermute x24 -> x22, waiting for transfers between devices: 31.4 us -> 32.7 us  [exchange(): return lax.ppermute(block, axes, [(i, i ^ mask) for i in range(devices)])]
    pallas_call x6 -> x7, Pallas kernels: 35.4 us -> 35.6 us  [call(): pl.pallas_call(kernel, out_shape=[jax.ShapeDtypeStruct(shape, kind) for s...]
  transfers between devices with their start and end apart: 27 -> 25, of which waited for: 15 -> 15; matrix products, arithmetic and copies ran while one was open for 2% -> 2% of each run, Pallas kernels for 14% -> 15%
where the time goes in v10:
time: 112 us
  waiting for transfers between devices  36.9 us (33%)
  Pallas kernels  35.6 us (32%)
  starting transfers between devices  34 us (30%)
  other arithmetic  1.85 us (2%)
  local copies, waits for them, and re-layouts  1.72 us (2%)
  between operations  1.69 us (2%)
    pallas_call x7, Pallas kernels, call(): pl.pallas_call(kernel, out_shape=[jax.ShapeDtypeStruct(shape, kind) for s...  35.6 us
    ppermute x22, waiting for transfers between devices, exchange(): return lax.ppermute(block, axes, [(i, i ^ mask) for i in range(devices)])  32.7 us
    ppermute x22, starting transfers between devices, exchange(): return lax.ppermute(block, axes, [(i, i ^ mask) for i in range(devices)])  23 us
    all_to_all x3, starting transfers between devices, to_all(): return lax.all_to_all(pieces, axes, 0, 0, tiled=True)  11 us
    all_to_all x3, waiting for transfers between devices, to_all(): return lax.all_to_all(pieces, axes, 0, 0, tiled=True)  4.2 us
  transfers between devices with their start and end apart: 25, of which 15 were waited for; matrix products, arithmetic and copies ran while one was open for 2% of the time, Pallas kernels for 15%

profile of v10, /device:TPU:0, one launch (start us, length us, event | category | flops | bytes accessed | tf_op | source)
XLA Modules:
  0.0 112.0 jit_solution(15003240287284962235)
XLA Ops:
  0.6 1.9 %shard_map.50 = (f32[32,512]{1,0:T(8,128)}, f32[256,128]{1,0:T(8,128)}) custom-call(f32[32,512]{1,0:T(8,128)} %kspace_hbm.3, s32[32,512]{1,0:T(8,128)} %mask_hbm.3, f32[256,128]{1,0:T(8,128)} %bitcast.19), custom_call_target="tpu_custom_call" | custom-call | flops 1000000000 | tf_op jit(solution)/shard_map/pallas_call | solution.py:520
  2.5 4.1 %collective-permute-start.5 = (f32[1,32,512]{2,1,0:T(8,128)}, f32[1,32,512]{2,1,0:T(8,128)S(1)}, u32[]{:S(2)}, u32[]{:S(2)}) collective-permute-start(f32[1,32,512]{2,1,0:T(8,128)} %bitcast.15), channel_id=1, source_target_pairs={{0,16},{1,17},{2,18},{3,19},{4,20},{5,21},{6,22},{7,23},{8,24},{9,... | collective-permute-start | bytes 196616 | tf_op jit(solution)/shard_map/ppermute | solution.py:538
  6.6 3.8 %all-to-all-start = ((f32[32,8,128]{2,1,0:T(8,128)}), f32[32,8,128]{2,1,0:T(8,128)S(1)}, u32[]{:S(2)}, u32[]{:S(2)}) async-start(f32[32,8,128]{2,1,0:T(8,128)} %bitcast.18), calls=%async_computation | async-start | bytes 262144 | tf_op jit(solution)/shard_map/all_to_all | solution.py:599
  10.5 0.8 pad_maximum_fusion.5
  11.3 1.8 %collective-permute-start.6 = (f32[2,32,512]{2,1,0:T(8,128)S(1)}, f32[2,32,512]{2,1,0:T(8,128)S(1)}, u32[]{:S(2)}, u32[]{:S(2)}) collective-permute-start(f32[2,32,512]{2,1,0:T(8,128)S(1)} %pad_maximum_fusion.5), channel_id=1, source_target_pairs={{0,8},{1,9},{2,10},{3,11},{4,12},{5,13},{6,14},{7,15},{8,0},{9,1},... | collective-permute-start | bytes 393224 | tf_op jit(solution)/shard_map/ppermute | solution.py:538
  13.2 5.3 %collective-permute-done.6 = f32[2,32,512]{2,1,0:T(8,128)S(1)} collective-permute-done((f32[2,32,512]{2,1,0:T(8,128)S(1)}, f32[2,32,512]{2,1,0:T(8,128)S(1)}, u32[]{:S(2)}, u32[]{:S(2)}) %collective-permute-start.6) | collective-permute-done | bytes 131104 | tf_op jit(solution)/shard_map/ppermute | solution.py:538
  18.5 0.9 pad_maximum_fusion.1
  19.4 1.6 %collective-permute-start.7 = (f32[4,16,512]{2,1,0:T(8,128)S(1)}, f32[4,16,512]{2,1,0:T(8,128)S(1)}, u32[]{:S(2)}, u32[]{:S(2)}) collective-permute-start(f32[4,16,512]{2,1,0:T(8,128)S(1)} %get-tuple-element.59), channel_id=1, source_target_pairs={{0,4},{1,5},{2,6},{3,7},{4,0},{5,1},{6,2},{7,3},{8,12},{9,13},{10,... | collective-permute-start | bytes 393224 | tf_op jit(solution)/shard_map/ppermute | solution.py:538
  21.0 1.5 %collective-permute-start.11 = (f32[4,16,512]{2,1,0:T(8,128)S(1)}, f32[4,16,512]{2,1,0:T(8,128)S(1)}, u32[]{:S(2)}, u32[]{:S(2)}) collective-permute-start(f32[4,16,512]{2,1,0:T(8,128)S(1)} %get-tuple-element.58), channel_id=1, source_target_pairs={{0,2},{1,3},{2,0},{3,1},{4,6},{5,7},{6,4},{7,5},{8,10},{9,11},{10,... | collective-permute-start | bytes 393224 | tf_op jit(solution)/shard_map/ppermute | solution.py:538
  22.5 2.4 %collective-permute-done.7 = f32[4,16,512]{2,1,0:T(8,128)S(1)} collective-permute-done((f32[4,16,512]{2,1,0:T(8,128)S(1)}, f32[4,16,512]{2,1,0:T(8,128)S(1)}, u32[]{:S(2)}, u32[]{:S(2)}) %collective-permute-start.7) | collective-permute-done | bytes 131104 | tf_op jit(solution)/shard_map/ppermute | solution.py:538
  24.9 1.3 %collective-permute-start.8 = (f32[8,16,512]{2,1,0:T(8,128)S(1)}, f32[8,16,512]{2,1,0:T(8,128)S(1)}, u32[]{:S(2)}, u32[]{:S(2)}) collective-permute-start(f32[8,16,512]{2,1,0:T(8,128)S(1)} %pad_maximum_fusion.2.refs_0_), channel_id=1, source_target_pairs={{0,2},{1,3},{2,0},{3,1},{4,6},{5,7},{6,4},{7,5},{8,10},{9,11},{10,... | collective-permute-start | bytes 786440 | tf_op jit(solution)/shard_map/ppermute | solution.py:538
  26.2 1.5 %collective-permute-start.12 = (f32[8,16,512]{2,1,0:T(8,128)S(1)}, f32[8,16,512]{2,1,0:T(8,128)S(1)}, u32[]{:S(2)}, u32[]{:S(2)}) collective-permute-start(f32[8,16,512]{2,1,0:T(8,128)S(1)} %pad_maximum_fusion.3.refs_4_), channel_id=1, source_target_pairs={{0,4},{1,5},{2,6},{3,7},{4,0},{5,1},{6,2},{7,3},{8,12},{9,13},{10,... | collective-permute-start | bytes 786440 | tf_op jit(solution)/shard_map/ppermute | solution.py:538
  27.8 0.5 collective-permute-start.13
  28.3 4.0 %collective-permute-done.8.refs_1_ = f32[8,16,512]{2,1,0:T(8,128)S(1)} collective-permute-done((f32[8,16,512]{2,1,0:T(8,128)S(1)}, f32[8,16,512]{2,1,0:T(8,128)S(1)}, u32[]{:S(2)}, u32[]{:S(2)}) %collective-permute-start.8) | collective-permute-done | bytes 262176 | tf_op jit(solution)/shard_map/ppermute | solution.py:538
  32.3 0.8 collective-permute-done.12.refs_5_
  33.1 0.8 collective-permute-done.10.refs_3_
  33.8 0.8 collective-permute-done.14.refs_7_
  34.6 12.6 %shard_map.51 = (bf16[3,4,32,4096]{3,2,1,0:T(8,128)(2,1)S(1)}, f32[256,128]{1,0:T(8,128)S(1)}, f32[8,4,2,8,128]{4,3,2,1,0:T(8,128)}, f32[4,64,128]{2,1,0:T(8,128)S(1)}) custom-call(f32[8,4,8,128]{3,2,1,0:T(8,128)S(1)} %bitcast.13, f32[8,16,512]{2,1,0:T(8,128)S(1)} %pad_maximum_fusion.2.refs_0_, f32[8,16,512]{2,1,0:T(8,128)S(1)} %collective-permute-done.8.refs_1_, ...), custom_call_target="tpu_custom_call" | custom-call | flops 12000000000 | tf_op jit(solution)/shard_map/pallas_call | solution.py:520
  47.2 0.7 copy-done.2
  47.9 3.8 %all-to-all-start.1 = ((f32[32,16,128]{2,1,0:T(8,128)}), f32[32,16,128]{2,1,0:T(8,128)S(1)}, u32[]{:S(2)}, u32[]{:S(2)}) async-start(f32[32,16,128]{2,1,0:T(8,128)} %bitcast.4), calls=%async_computation.1 | async-start | bytes 524288 | tf_op jit(solution)/shard_map/all_to_all | solution.py:599
  51.8 1.4 %collective-permute-start.17 = (f32[1,64,128]{2,1,0:T(8,128)S(1)}, f32[1,64,128]{2,1,0:T(8,128)S(1)}, u32[]{:S(2)}, u32[]{:S(2)}) collective-permute-start(f32[1,64,128]{2,1,0:T(8,128)S(1)} %get-tuple-element.61), channel_id=1, source_target_pairs={{0,3},{1,2},{2,1},{3,0},{4,7},{5,6},{6,5},{7,4},{8,11},{9,10},{10,... | collective-permute-start | bytes 98312 | tf_op jit(solution)/shard_map/ppermute | solution.py:538
  53.2 0.4 collective-permute-start.16
  53.5 0.2 collective-permute-start.15
  53.7 0.9 copy-done.3
  54.6 2.8 %shard_map.52 = f32[8,4,4,640]{3,2,1,0:T(4,128)} custom-call(bf16[3,4,32,4096]{3,2,1,0:T(8,128)(2,1)S(1)} %get-tuple-element.39.samples_ref, f32[256,128]{1,0:T(8,128)S(1)} %copy-done.3), custom_call_target="tpu_custom_call" | custom-call | flops 2000000000 | tf_op jit(solution)/shard_map/pallas_call | solution.py:520
  57.4 0.6 collective-permute-done.16
  58.0 4.2 %all-to-all-done.1 = f32[32,16,128]{2,1,0:T(8,128)S(1)} async-done(((f32[32,16,128]{2,1,0:T(8,128)}), f32[32,16,128]{2,1,0:T(8,128)S(1)}, u32[]{:S(2)}, u32[]{:S(2)}) %all-to-all-start.1) | async-done | bytes 262176 | tf_op jit(solution)/shard_map/all_to_all | solution.py:599
  62.1 0.3 collective-permute-start.21
  62.5 0.6 shard_map.53
  63.1 0.4 collective-permute-start.18
  63.4 0.9 collective-permute-done.18
  64.3 1.1 collective-permute-start.19
  65.4 2.9 %collective-permute-done.19 = f32[72,128]{1,0:T(8,128)S(1)} collective-permute-done((f32[72,128]{1,0:T(8,128)S(1)}, f32[72,128]{1,0:T(8,128)S(1)}, u32[]{:S(2)}, u32[]{:S(2)}) %collective-permute-start.19) | collective-permute-done | bytes 36896 | tf_op jit(solution)/shard_map/ppermute | solution.py:538
  68.3 0.8 collective-permute-start.20
  69.1 3.2 %collective-permute-done.20 = f32[72,128]{1,0:T(8,128)S(1)} collective-permute-done((f32[72,128]{1,0:T(8,128)S(1)}, f32[72,128]{1,0:T(8,128)S(1)}, u32[]{:S(2)}, u32[]{:S(2)}) %collective-permute-start.20) | collective-permute-done | bytes 36896 | tf_op jit(solution)/shard_map/ppermute | solution.py:538
  72.3 1.7 %collective-permute-start.22 = (f32[8,64,128]{2,1,0:T(8,128)S(1)}, f32[8,64,128]{2,1,0:T(8,128)S(1)}, u32[]{:S(2)}, u32[]{:S(2)}) collective-permute-start(f32[8,64,128]{2,1,0:T(8,128)S(1)} %pad_maximum_fusion.4), channel_id=1, source_target_pairs={{0,8},{1,9},{2,10},{3,11},{4,12},{5,13},{6,14},{7,15},{8,0},{9,1},... | collective-permute-start | bytes 786440 | tf_op jit(solution)/shard_map/ppermute | solution.py:538
  74.0 0.4 collective-permute-start.23
  74.4 5.5 %collective-permute-done.23 = f32[72,128]{1,0:T(8,128)S(1)} collective-permute-done((f32[72,128]{1,0:T(8,128)S(1)}, f32[72,128]{1,0:T(8,128)S(1)}, u32[]{:S(2)}, u32[]{:S(2)}) %collective-permute-start.23) | collective-permute-done | bytes 36896 | tf_op jit(solution)/shard_map/ppermute | solution.py:538
  79.9 2.2 %collective-permute-start.24 = (f32[72,128]{1,0:T(8,128)S(1)}, f32[72,128]{1,0:T(8,128)S(1)}, u32[]{:S(2)}, u32[]{:S(2)}) collective-permute-start(f32[72,128]{1,0:T(8,128)S(1)} %add.33), channel_id=1, source_target_pairs={{0,16},{1,17},{2,18},{3,19},{4,20},{5,21},{6,22},{7,23},{8,24},{9,... | collective-permute-start | bytes 110600 | tf_op jit(solution)/shard_map/ppermute | solution.py:538
  82.1 2.6 %collective-permute-done.24 = f32[72,128]{1,0:T(8,128)S(1)} collective-permute-done((f32[72,128]{1,0:T(8,128)S(1)}, f32[72,128]{1,0:T(8,128)S(1)}, u32[]{:S(2)}, u32[]{:S(2)}) %collective-permute-start.24) | collective-permute-done | bytes 36896 | tf_op jit(solution)/shard_map/ppermute | solution.py:538
  84.8 1.1 %collective-permute-done.25.other_ref = f32[72,128]{1,0:T(8,128)S(1)} collective-permute-done((f32[72,128]{1,0:T(8,128)S(1)}, f32[72,128]{1,0:T(8,128)S(1)}, u32[]{:S(2)}, u32[]{:S(2)}) %collective-permute-start.25) | collective-permute-done | bytes 36896 | tf_op jit(solution)/shard_map/ppermute | solution.py:538
  86.0 3.3 %all-to-all-start.2 = ((f32[32,4,640]{2,1,0:T(4,128)}), f32[32,4,640]{2,1,0:T(4,128)S(1)}, u32[]{:S(2)}, u32[]{:S(2)}) async-start(f32[32,4,640]{2,1,0:T(4,128)} %bitcast.6), calls=%async_computation.2 | async-start | bytes 655360 | tf_op jit(solution)/shard_map/all_to_all | solution.py:599
  89.3 1.8 %collective-permute-start.26 = (f32[16,64,128]{2,1,0:T(8,128)S(1)}, f32[16,64,128]{2,1,0:T(8,128)S(1)}, u32[]{:S(2)}, u32[]{:S(2)}) collective-permute-start(f32[16,64,128]{2,1,0:T(8,128)S(1)} %pad_maximum_fusion), channel_id=1, source_target_pairs={{0,4},{1,5},{2,6},{3,7},{4,0},{5,1},{6,2},{7,3},{8,12},{9,13},{10,... | collective-permute-start | bytes 1572872 | tf_op jit(solution)/shard_map/ppermute | solution.py:538
  91.2 7.0 %shard_map.54 = (f32[128,128]{1,0:T(8,128)S(1)}, f32[128,128]{1,0:T(8,128)S(1)}, s32[1]{0:T(128)}) custom-call(f32[72,128]{1,0:T(8,128)S(1)} %add.34.gram_ref, f32[72,128]{1,0:T(8,128)S(1)} %collective-permute-done.25.other_ref), custom_call_target="tpu_custom_call" | custom-call | flops 12000000000 | tf_op jit(solution)/shard_map/pallas_call | solution.py:520
  98.8 0.2 conditional.1
  99.1 5.9 %shard_map.55.both_ref = f32[128,128]{1,0:T(8,128)S(1)} custom-call(f32[128,128]{1,0:T(8,128)S(1)} %get-tuple-element.64.gram_ref, f32[128,128]{1,0:T(8,128)S(1)} %get-tuple-element.53.inverse_ref), custom_call_target="tpu_custom_call" | custom-call | tf_op jit(solution)/shard_map/pallas_call | solution.py:520
  105.1 1.8 %collective-permute-done.26 = f32[16,64,128]{2,1,0:T(8,128)S(1)} collective-permute-done((f32[16,64,128]{2,1,0:T(8,128)S(1)}, f32[16,64,128]{2,1,0:T(8,128)S(1)}, u32[]{:S(2)}, u32[]{:S(2)}) %collective-permute-start.26) | collective-permute-done | bytes 524320 | tf_op jit(solution)/shard_map/ppermute | solution.py:538
  106.9 4.9 %shard_map.56 = (f32[32,512]{1,0:T(8,128)}, f32[256,128]{1,0:T(8,128)}) custom-call(f32[128,640]{1,0:T(8,128)S(1)} %reshape.44.images_ref, f32[128,128]{1,0:T(8,128)S(1)} %shard_map.55.both_ref, f32[32,512]{1,0:T(8,128)S(1)} %copy-done, s32[32,512]{1,0:T(8,128)S(1)} %copy-done.1, f32[1024,128]{1,0:T(8,128)S(1)} %bitcast.11, f32[1024,128]{1,0:T(8,128)S(1)} %bitcast.14), custom_call_target="tpu_custom_call" | custom-call | flops 5000000000 | tf_op jit(solution)/shard_map/pallas_call | solution.py:520
  (33 shorter events, 0.4 us)
Async XLA Ops:
  2.5 8.0 %collective-permute-start.5 = (f32[1,32,512]{2,1,0:T(8,128)}, f32[1,32,512]{2,1,0:T(8,128)S(1)}, u32[]{:S(2)}, u32[]{:S(2)}) collective-permute-start(f32[1,32,512]{2,1,0:T(8,128)} %bitcast.15), channel_id=1, source_target_pairs={{0,16},{1,17},{2,18},{3,19},{4,20},{5,21},{6,22},{7,23},{8,24},{9,... | collective-permute-start | bytes 196616 | tf_op jit(solution)/shard_map/ppermute | solution.py:538
  6.6 12.7 %all-to-all-start = ((f32[32,8,128]{2,1,0:T(8,128)}), f32[32,8,128]{2,1,0:T(8,128)S(1)}, u32[]{:S(2)}, u32[]{:S(2)}) async-start(f32[32,8,128]{2,1,0:T(8,128)} %bitcast.18), calls=%async_computation | async-start | bytes 262144 | tf_op jit(solution)/shard_map/all_to_all | solution.py:599
  11.3 7.1 %collective-permute-start.6 = (f32[2,32,512]{2,1,0:T(8,128)S(1)}, f32[2,32,512]{2,1,0:T(8,128)S(1)}, u32[]{:S(2)}, u32[]{:S(2)}) collective-permute-start(f32[2,32,512]{2,1,0:T(8,128)S(1)} %pad_maximum_fusion.5), channel_id=1, source_target_pairs={{0,8},{1,9},{2,10},{3,11},{4,12},{5,13},{6,14},{7,15},{8,0},{9,1},... | collective-permute-start | bytes 393224 | tf_op jit(solution)/shard_map/ppermute | solution.py:538
  19.4 5.5 %collective-permute-start.7 = (f32[4,16,512]{2,1,0:T(8,128)S(1)}, f32[4,16,512]{2,1,0:T(8,128)S(1)}, u32[]{:S(2)}, u32[]{:S(2)}) collective-permute-start(f32[4,16,512]{2,1,0:T(8,128)S(1)} %get-tuple-element.59), channel_id=1, source_target_pairs={{0,4},{1,5},{2,6},{3,7},{4,0},{5,1},{6,2},{7,3},{8,12},{9,13},{10,... | collective-permute-start | bytes 393224 | tf_op jit(solution)/shard_map/ppermute | solution.py:538
  21.0 5.2 %collective-permute-start.11 = (f32[4,16,512]{2,1,0:T(8,128)S(1)}, f32[4,16,512]{2,1,0:T(8,128)S(1)}, u32[]{:S(2)}, u32[]{:S(2)}) collective-permute-start(f32[4,16,512]{2,1,0:T(8,128)S(1)} %get-tuple-element.58), channel_id=1, source_target_pairs={{0,2},{1,3},{2,0},{3,1},{4,6},{5,7},{6,4},{7,5},{8,10},{9,11},{10,... | collective-permute-start | bytes 393224 | tf_op jit(solution)/shard_map/ppermute | solution.py:538
  24.9 7.4 %collective-permute-start.8 = (f32[8,16,512]{2,1,0:T(8,128)S(1)}, f32[8,16,512]{2,1,0:T(8,128)S(1)}, u32[]{:S(2)}, u32[]{:S(2)}) collective-permute-start(f32[8,16,512]{2,1,0:T(8,128)S(1)} %pad_maximum_fusion.2.refs_0_), channel_id=1, source_target_pairs={{0,2},{1,3},{2,0},{3,1},{4,6},{5,7},{6,4},{7,5},{8,10},{9,11},{10,... | collective-permute-start | bytes 786440 | tf_op jit(solution)/shard_map/ppermute | solution.py:538
  26.2 6.8 %collective-permute-start.12 = (f32[8,16,512]{2,1,0:T(8,128)S(1)}, f32[8,16,512]{2,1,0:T(8,128)S(1)}, u32[]{:S(2)}, u32[]{:S(2)}) collective-permute-start(f32[8,16,512]{2,1,0:T(8,128)S(1)} %pad_maximum_fusion.3.refs_4_), channel_id=1, source_target_pairs={{0,4},{1,5},{2,6},{3,7},{4,0},{5,1},{6,2},{7,3},{8,12},{9,13},{10,... | collective-permute-start | bytes 786440 | tf_op jit(solution)/shard_map/ppermute | solution.py:538
  27.8 5.3 %collective-permute-start.9 = (f32[8,16,512]{2,1,0:T(8,128)S(1)}, f32[8,16,512]{2,1,0:T(8,128)S(1)}, u32[]{:S(2)}, u32[]{:S(2)}) collective-permute-start(f32[8,16,512]{2,1,0:T(8,128)S(1)} %pad_maximum_fusion.2.refs_0_), channel_id=1, source_target_pairs={{0,1},{1,0},{2,3},{3,2},{4,5},{5,4},{6,7},{7,6},{8,9},{9,8},{10,11... | collective-permute-start | bytes 786440 | tf_op jit(solution)/shard_map/ppermute | solution.py:538
  27.8 5.3 %collective-permute-start.13 = (f32[8,16,512]{2,1,0:T(8,128)S(1)}, f32[8,16,512]{2,1,0:T(8,128)S(1)}, u32[]{:S(2)}, u32[]{:S(2)}) collective-permute-start(f32[8,16,512]{2,1,0:T(8,128)S(1)} %pad_maximum_fusion.3.refs_4_), channel_id=1, source_target_pairs={{0,1},{1,0},{2,3},{3,2},{4,5},{5,4},{6,7},{7,6},{8,9},{9,8},{10,11... | collective-permute-start | bytes 786440 | tf_op jit(solution)/shard_map/ppermute | solution.py:538
  32.3 1.5 %collective-permute-start.10 = (f32[8,16,512]{2,1,0:T(8,128)S(1)}, f32[8,16,512]{2,1,0:T(8,128)S(1)}, u32[]{:S(2)}, u32[]{:S(2)}) collective-permute-start(f32[8,16,512]{2,1,0:T(8,128)S(1)} %collective-permute-done.8.refs_1_), channel_id=1, source_target_pairs={{0,1},{1,0},{2,3},{3,2},{4,5},{5,4},{6,7},{7,6},{8,9},{9,8},{10,11... | collective-permute-start | bytes 786440 | tf_op jit(solution)/shard_map/ppermute | solution.py:538
  33.1 1.5 %collective-permute-start.14 = (f32[8,16,512]{2,1,0:T(8,128)S(1)}, f32[8,16,512]{2,1,0:T(8,128)S(1)}, u32[]{:S(2)}, u32[]{:S(2)}) collective-permute-start(f32[8,16,512]{2,1,0:T(8,128)S(1)} %collective-permute-done.12.refs_5_), channel_id=1, source_target_pairs={{0,1},{1,0},{2,3},{3,2},{4,5},{5,4},{6,7},{7,6},{8,9},{9,8},{10,11... | collective-permute-start | bytes 786440 | tf_op jit(solution)/shard_map/ppermute | solution.py:538
  47.2 0.7 copy-start.2
  47.9 14.3 %all-to-all-start.1 = ((f32[32,16,128]{2,1,0:T(8,128)}), f32[32,16,128]{2,1,0:T(8,128)S(1)}, u32[]{:S(2)}, u32[]{:S(2)}) async-start(f32[32,16,128]{2,1,0:T(8,128)} %bitcast.4), calls=%async_computation.1 | async-start | bytes 524288 | tf_op jit(solution)/shard_map/all_to_all | solution.py:599
  51.8 5.6 %collective-permute-start.17 = (f32[1,64,128]{2,1,0:T(8,128)S(1)}, f32[1,64,128]{2,1,0:T(8,128)S(1)}, u32[]{:S(2)}, u32[]{:S(2)}) collective-permute-start(f32[1,64,128]{2,1,0:T(8,128)S(1)} %get-tuple-element.61), channel_id=1, source_target_pairs={{0,3},{1,2},{2,1},{3,0},{4,7},{5,6},{6,5},{7,4},{8,11},{9,10},{10,... | collective-permute-start | bytes 98312 | tf_op jit(solution)/shard_map/ppermute | solution.py:538
  53.2 4.8 %collective-permute-start.16 = (f32[1,64,128]{2,1,0:T(8,128)S(1)}, f32[1,64,128]{2,1,0:T(8,128)S(1)}, u32[]{:S(2)}, u32[]{:S(2)}) collective-permute-start(f32[1,64,128]{2,1,0:T(8,128)S(1)} %get-tuple-element.62), channel_id=1, source_target_pairs={{0,2},{1,3},{2,0},{3,1},{4,6},{5,7},{6,4},{7,5},{8,10},{9,11},{10,... | collective-permute-start | bytes 98312 | tf_op jit(solution)/shard_map/ppermute | solution.py:538
  53.5 4.4 %collective-permute-start.15 = (f32[1,64,128]{2,1,0:T(8,128)S(1)}, f32[1,64,128]{2,1,0:T(8,128)S(1)}, u32[]{:S(2)}, u32[]{:S(2)}) collective-permute-start(f32[1,64,128]{2,1,0:T(8,128)S(1)} %get-tuple-element.63), channel_id=1, source_target_pairs={{0,1},{1,0},{2,3},{3,2},{4,5},{5,4},{6,7},{7,6},{8,9},{9,8},{10,11... | collective-permute-start | bytes 98312 | tf_op jit(solution)/shard_map/ppermute | solution.py:538
  53.7 0.9 copy-start.3
  62.1 10.1 %collective-permute-start.21 = (f32[4,64,128]{2,1,0:T(8,128)S(1)}, f32[4,64,128]{2,1,0:T(8,128)S(1)}, u32[]{:S(2)}, u32[]{:S(2)}) collective-permute-start(f32[4,64,128]{2,1,0:T(8,128)S(1)} %pad_maximum_fusion.6), channel_id=1, source_target_pairs={{0,16},{1,17},{2,18},{3,19},{4,20},{5,21},{6,22},{7,23},{8,24},{9,... | collective-permute-start | bytes 393224 | tf_op jit(solution)/shard_map/ppermute | solution.py:538
  63.1 1.3 %collective-permute-start.18 = (f32[72,128]{1,0:T(8,128)S(1)}, f32[72,128]{1,0:T(8,128)S(1)}, u32[]{:S(2)}, u32[]{:S(2)}) collective-permute-start(f32[72,128]{1,0:T(8,128)S(1)} %get-tuple-element.44), channel_id=1, source_target_pairs={{0,1},{1,0},{2,3},{3,2},{4,5},{5,4},{6,7},{7,6},{8,9},{9,8},{10,11... | collective-permute-start | bytes 110600 | tf_op jit(solution)/shard_map/ppermute | solution.py:538
  64.3 4.0 %collective-permute-start.19 = (f32[72,128]{1,0:T(8,128)S(1)}, f32[72,128]{1,0:T(8,128)S(1)}, u32[]{:S(2)}, u32[]{:S(2)}) collective-permute-start(f32[72,128]{1,0:T(8,128)S(1)} %add.30), channel_id=1, source_target_pairs={{0,2},{1,3},{2,0},{3,1},{4,6},{5,7},{6,4},{7,5},{8,10},{9,11},{10,... | collective-permute-start | bytes 110600 | tf_op jit(solution)/shard_map/ppermute | solution.py:538
  68.3 4.0 %collective-permute-start.20 = (f32[72,128]{1,0:T(8,128)S(1)}, f32[72,128]{1,0:T(8,128)S(1)}, u32[]{:S(2)}, u32[]{:S(2)}) collective-permute-start(f32[72,128]{1,0:T(8,128)S(1)} %add.31), channel_id=1, source_target_pairs={{0,4},{1,5},{2,6},{3,7},{4,0},{5,1},{6,2},{7,3},{8,12},{9,13},{10,... | collective-permute-start | bytes 110600 | tf_op jit(solution)/shard_map/ppermute | solution.py:538
  72.3 12.5 %collective-permute-start.22 = (f32[8,64,128]{2,1,0:T(8,128)S(1)}, f32[8,64,128]{2,1,0:T(8,128)S(1)}, u32[]{:S(2)}, u32[]{:S(2)}) collective-permute-start(f32[8,64,128]{2,1,0:T(8,128)S(1)} %pad_maximum_fusion.4), channel_id=1, source_target_pairs={{0,8},{1,9},{2,10},{3,11},{4,12},{5,13},{6,14},{7,15},{8,0},{9,1},... | collective-permute-start | bytes 786440 | tf_op jit(solution)/shard_map/ppermute | solution.py:538
  74.0 5.9 %collective-permute-start.23 = (f32[72,128]{1,0:T(8,128)S(1)}, f32[72,128]{1,0:T(8,128)S(1)}, u32[]{:S(2)}, u32[]{:S(2)}) collective-permute-start(f32[72,128]{1,0:T(8,128)S(1)} %add.32), channel_id=1, source_target_pairs={{0,8},{1,9},{2,10},{3,11},{4,12},{5,13},{6,14},{7,15},{8,0},{9,1},... | collective-permute-start | bytes 110600 | tf_op jit(solution)/shard_map/ppermute | solution.py:538
  79.9 4.9 %collective-permute-start.24 = (f32[72,128]{1,0:T(8,128)S(1)}, f32[72,128]{1,0:T(8,128)S(1)}, u32[]{:S(2)}, u32[]{:S(2)}) collective-permute-start(f32[72,128]{1,0:T(8,128)S(1)} %add.33), channel_id=1, source_target_pairs={{0,16},{1,17},{2,18},{3,19},{4,20},{5,21},{6,22},{7,23},{8,24},{9,... | collective-permute-start | bytes 110600 | tf_op jit(solution)/shard_map/ppermute | solution.py:538
  84.8 1.2 %collective-permute-start.25 = (f32[72,128]{1,0:T(8,128)S(1)}, f32[72,128]{1,0:T(8,128)S(1)}, u32[]{:S(2)}, u32[]{:S(2)}) collective-permute-start(f32[72,128]{1,0:T(8,128)S(1)} %add.34.gram_ref), channel_id=1, source_target_pairs={{0,1},{1,0},{2,3},{3,2},{4,5},{5,4},{6,7},{7,6},{8,9},{9,8},{10,11... | collective-permute-start | bytes 110600 | tf_op jit(solution)/shard_map/ppermute | solution.py:538
  86.0 19.0 %all-to-all-start.2 = ((f32[32,4,640]{2,1,0:T(4,128)}), f32[32,4,640]{2,1,0:T(4,128)S(1)}, u32[]{:S(2)}, u32[]{:S(2)}) async-start(f32[32,4,640]{2,1,0:T(4,128)} %bitcast.6), calls=%async_computation.2 | async-start | bytes 655360 | tf_op jit(solution)/shard_map/all_to_all | solution.py:599
  89.3 17.6 %collective-permute-start.26 = (f32[16,64,128]{2,1,0:T(8,128)S(1)}, f32[16,64,128]{2,1,0:T(8,128)S(1)}, u32[]{:S(2)}, u32[]{:S(2)}) collective-permute-start(f32[16,64,128]{2,1,0:T(8,128)S(1)} %pad_maximum_fusion), channel_id=1, source_target_pairs={{0,4},{1,5},{2,6},{3,7},{4,0},{5,1},{6,2},{7,3},{8,12},{9,13},{10,... | collective-permute-start | bytes 1572872 | tf_op jit(solution)/shard_map/ppermute | solution.py:538
  98.1 8.8 %copy-start = (f32[32,512]{1,0:T(8,128)S(1)}, f32[32,512]{1,0:T(8,128)}, u32[]{:S(2)}) copy-start(f32[32,512]{1,0:T(8,128)} %kspace_hbm.3) | copy-start | bytes 196612
  98.1 8.8 %copy-start.1 = (s32[32,512]{1,0:T(8,128)S(1)}, s32[32,512]{1,0:T(8,128)}, u32[]{:S(2)}) copy-start(s32[32,512]{1,0:T(8,128)} %mask_hbm.3) | copy-start | bytes 196612

commit v11 on v8

--- a/solution.py
+++ b/solution.py
@@ -110,6 +110,12 @@
     a_high, a_low = split(a)
     b_high, b_low = split(b)
     return dot(a_high, b_high, dims) + (dot(a_high, b_low, dims) + dot(a_low, b_high, dims))
+
+
+def square(size):
+    at_row = lax.broadcasted_iota(jnp.int32, (size, size), 0)
+    at_col = lax.broadcasted_iota(jnp.int32, (size, size), 1)
+    return at_row, at_col
 
 
 def prepare_kernel(
@@ -307,12 +313,6 @@
     return lax.dot_general(
         a, b, (dims, ((), ())), precision=lax.Precision.HIGHEST, preferred_element_type=jnp.float32
     )
-
-
-def square(size):
-    at_row = lax.broadcasted_iota(jnp.int32, (size, size), 0)
-    at_col = lax.broadcasted_iota(jnp.int32, (size, size), 1)
-    return at_row, at_col
 
 
 def gram_kernel(cols, per_tile, received_ref, kept_ref, given_ref, turned_ref):
@@ -417,12 +417,12 @@
     return jnp.concatenate(done, axis=0)
 
 
-def factors_kernel(gram_ref, other_ref, first_ref, both_ref, sound_ref):
+def factor_kernel(gram_ref, other_ref, inverse_ref, next_ref, sound_ref):
     gram, raw, line = load_grams(gram_ref, other_ref)
     inverse = inverse_factor(gram)
-    first_ref[...] = inverse
+    inverse_ref[...] = inverse
     gram = exact(exact(inverse, raw), inverse, ((1,), (1,)))
-    both_ref[...] = exact(inverse_factor(gram), inverse)
+    next_ref[...] = gram
     at_row, at_col = square(gram.shape[0])
     terms = jnp.sum(inverse * inverse * line, axis=1, keepdims=True)
     result = jnp.sum(jnp.where(at_row == at_col, gram, 0.0), axis=1, keepdims=True)
@@ -435,19 +435,20 @@
     gram_ref[...] = exact(turned, turned, ((1,), (1,)))
 
 
-def again_kernel(gram_ref, inverse_ref, both_ref):
+def both_kernel(gram_ref, inverse_ref, both_ref):
     both_ref[...] = exact(inverse_factor(gram_ref[...]), inverse_ref[...])
 
 
 def moved_columns(values, order):
-    devices = len(order)
+    devices = len(order[0])
     at_row, at_col = square(values.shape[0])
     me = lax.axis_index("rows") * lax.axis_size("coil") + lax.axis_index("coil")
     slot = at_col % devices
     mask = jnp.zeros_like(slot)
     bit = 1
     while bit < devices:
-        mask = mask | jnp.where(slot & bit != 0, order[bit], 0)
+        step = jnp.where(2 * at_col < at_col.shape[1], order[0][bit], order[1][bit])
+        mask = mask | jnp.where(slot & bit != 0, step, 0)
         bit *= 2
     source = at_col - slot + lax.bitwise_xor(mask, jnp.full_like(mask, me))
     return exact(values, (at_row == source).astype(jnp.float32))
@@ -460,8 +461,10 @@
     both_ref,
     kspace_hbm,
     mask_hbm,
-    near_ref,
-    far_ref,
+    top_near_ref,
+    top_far_ref,
+    low_near_ref,
+    low_far_ref,
     recovered_ref,
     basis_ref,
     kspace_ref,
@@ -486,9 +489,9 @@
     images_high, images_low = split(images)
     stacked = jnp.concatenate([images_high, images_low], axis=0)
     chg, tile = kspace_ref.shape
-    lanes = near_ref.shape[1]
+    lanes = top_near_ref.shape[1]
     deep = KER * chg // lanes
-    step = cols * deep
+    step = cols // 2 * deep
     factor = moved_columns(both, order)
     estimate = jnp.zeros((chg, reach), jnp.float32)
     for a in range(0, deep, 2):
@@ -496,8 +499,9 @@
             jnp.concatenate(
                 [
                     ref[pl.ds(k * deep + a + i, ref.shape[0] // step, stride=step), :]
-                    for k in range(cols)
-                    for ref in (near_ref, far_ref)
+                    for refs in ((top_near_ref, top_far_ref), (low_near_ref, low_far_ref))
+                    for k in range(cols // 2)
+                    for ref in refs
                 ],
                 axis=0,
             )
@@ -572,32 +576,34 @@
 
 def gather_samples(sampled, tiles, groups, beside):
     devices = tiles * groups
-    near, masks = sampled[None], [0]
-    mask = devices // 2
-    while mask > groups:
-        near, masks = gather_round(near, masks, [mask], devices, AXES)
-        mask //= 2
-    near = after(near, beside)
-    half = near.shape[1] // 2
-    halves = []
-    for part, ways in (
-        (near[:, :half], (groups, groups // 2)),
-        (near[:, half:], (groups // 2, groups)),
-    ):
-        part, order = gather_round(part, masks, [ways[0]], devices, AXES)
-        pieces = [(part, order)]
-        mask = ways[1]
-        rest = groups // 4
-        while mask > 1:
-            pieces = pieces + [
-                (exchange(part, devices, mask, AXES), [m ^ mask for m in order])
-                for part, order in pieces
-            ]
-            mask, rest = rest, rest // 2
-        halves.append(
-            pieces
-            + [(exchange(part, devices, 1, AXES), [m ^ 1 for m in order]) for part, order in pieces]
-        )
+    first = devices // 2
+    near = sampled[None]
+    streams = [(near, [0]), (exchange(near, devices, first, AXES), [first])]
+    halves = [[], []]
+    for number, (near, masks) in enumerate(streams):
+        mask = first // 2
+        while mask > groups:
+            near, masks = gather_round(near, masks, [mask], devices, AXES)
+            mask //= 2
+        if number:
+            near = after(near, beside)
+        half = near.shape[1] // 2
+        for i, (part, ways) in enumerate(
+            (
+                (near[:, :half], (groups, groups // 2)),
+                (near[:, half:], (groups // 2, groups)),
+            )
+        ):
+            pieces = [gather_round(part, masks, [ways[0]], devices, AXES)]
+            mask = ways[1]
+            rest = groups // 4
+            while mask:
+                pieces = pieces + [
+                    (exchange(part, devices, mask, AXES), [m ^ mask for m in order])
+                    for part, order in pieces
+                ]
+                mask, rest = rest, rest // 2
+            halves[i] += pieces
     return halves
 
 
@@ -613,23 +619,43 @@
 
 
 def total_beside(kept, given, near, order, images, groups, devices):
+    ways = []
+    mask = devices // 2
+    while mask >= groups:
+        ways.append(mask)
+        mask //= 2
+    half = near.shape[1] // 2
+    parts = [near[:, :half], near[:, half:]]
+    orders = [order, order]
+    ways = [ways, ways[-1:] + ways[:-1]]
+    step = 0
+
+    def advance():
+        for i in range(2):
+            parts[i], orders[i] = gather_round(
+                parts[i], orders[i], [ways[i][step]], devices, AXES
+            )
+
     total = kept + exchange(given, devices, 1, AXES)
-    mask = devices // 2
     for partners in rounds_of(2, devices):
         terms = [exchange(total, devices, way, AXES) for way in partners]
         total = total + terms[0]
         if len(terms) == 3:
             total = total + (terms[1] + terms[2])
-        if mask > groups:
-            near, order = gather_round(near, order, [mask], devices, AXES)
-            mask //= 2
-    while mask > groups:
-        near, order = gather_round(near, order, [mask], devices, AXES)
-        mask //= 2
+        if step < len(ways[0]) - 1:
+            advance()
+            step += 1
+    while step < len(ways[0]) - 1:
+        advance()
+        step += 1
     other = exchange(total, devices, 1, AXES)
-    near, total, other, images = lax.optimization_barrier((near, total, other, images))
-    far = exchange(near, devices, groups, AXES)
-    return (total, other), near, far, order + [m ^ groups for m in order], to_all(images)
+    *parts, total, other, images = lax.optimization_barrier((*parts, total, other, images))
+    pieces = []
+    for i in range(2):
+        mask = ways[i][-1]
+        pieces += [parts[i], exchange(parts[i], devices, mask, AXES)]
+        orders[i] = orders[i] + [m ^ mask for m in orders[i]]
+    return (total, other), pieces, orders, to_all(images)
 
 
 def column_shards(kspace, sample_mask, start_basis):
@@ -697,12 +723,12 @@
         [half, half, ((rank, owned), f32)],
         received.reshape(devices * 2 * per_tile, lanes),
     )
-    gram, near, far, order, images = total_beside(
+    gram, pieces, order, images = total_beside(
         kept, given, near, order, images.reshape(devices, cols, reach), groups, devices
     )
     whole = ((rank, rank), f32)
-    first, both, sound = call(
-        factors_kernel, [whole, whole, ((1,), jnp.int32)], *gram, scalars=1, micros=12
+    first, second, sound = call(
+        factor_kernel, [whole, whole, ((1,), jnp.int32)], *gram, scalars=1, micros=12
     )
 
     def again():
@@ -711,9 +737,10 @@
         while mask < devices:
             gram = gram + exchange(gram, devices, mask, AXES)
             mask *= 2
-        return call(again_kernel, [whole], gram, first)[0]
-
-    both = lax.cond(sound[0] == 1, lambda: both, again)
+        return gram
+
+    second = lax.cond(sound[0] == 1, lambda: second, again)
+    (both,) = call(both_kernel, [whole], second, first, micros=0)
     recovered, basis = call(
         functools.partial(last_kernel, cols, order),
         [((chg, tile), f32), ((owned, rank), f32)],
@@ -721,8 +748,7 @@
         both,
         kspace,
         sample_mask,
-        near.reshape(-1, lanes),
-        far.reshape(-1, lanes),
+        *[piece.reshape(-1, lanes) for piece in pieces],
         scratch=[
             pltpu.VMEM((chg, tile), f32),
             pltpu.VMEM((chg, tile), sample_mask.dtype),
@@ -754,6 +780,8 @@
         and chg % (4 * SUB) == 0
         and (chg * groups) % LANES == 0
         and KER <= LANES
+        and rank // devices <= SUB
+        and rank // devices % 2 == 0
     )
 
 

time: 110 us -> 111 us (level)
  starting transfers between devices: 35 us -> 45.5 us
  waiting for transfers between devices: 35.6 us -> 26.1 us
    ppermute x24 -> x36, waiting for transfers between devices: 31.4 us -> 20.4 us  [exchange(): return lax.ppermute(block, axes, [(i, i ^ mask) for i in range(devices)])]
    ppermute x24 -> x36, starting transfers between devices: 24.7 us -> 33.1 us  [exchange(): return lax.ppermute(block, axes, [(i, i ^ mask) for i in range(devices)])]
    all_to_all x3, starting transfers between devices: 10.3 us -> 12.4 us  [to_all(): return lax.all_to_all(pieces, axes, 0, 0, tiled=True)]
    all_to_all x3, waiting for transfers between devices: 4.2 us -> 5.65 us  [to_all(): return lax.all_to_all(pieces, axes, 0, 0, tiled=True)]
    pallas_call x6 -> x7, Pallas kernels: 35.4 us -> 35.7 us  [call(): pl.pallas_call(kernel, out_shape=[jax.ShapeDtypeStruct(shape, kind) for s...]
  transfers between devices with their start and end apart: 27 -> 39, of which waited for: 15 -> 15; matrix products, arithmetic and copies ran while one was open for 2% -> 1% of each run, Pallas kernels for 14% -> 15%
where the time goes in v11:
time: 111 us; the launch traced here: 110 us
  starting transfers between devices  45.5 us (41%)
  Pallas kernels  35.7 us (32%)
  waiting for transfers between devices  26.1 us (24%)
  between operations  1.75 us (2%)
    pallas_call x7, Pallas kernels, call(): pl.pallas_call(kernel, out_shape=[jax.ShapeDtypeStruct(shape, kind) for s...  35.7 us
    ppermute x36, starting transfers between devices, exchange(): return lax.ppermute(block, axes, [(i, i ^ mask) for i in range(devices)])  33.1 us
    ppermute x36, waiting for transfers between devices, exchange(): return lax.ppermute(block, axes, [(i, i ^ mask) for i in range(devices)])  20.4 us
    all_to_all x3, starting transfers between devices, to_all(): return lax.all_to_all(pieces, axes, 0, 0, tiled=True)  12.4 us
    all_to_all x3, waiting for transfers between devices, to_all(): return lax.all_to_all(pieces, axes, 0, 0, tiled=True)  5.65 us
  transfers between devices with their start and end apart: 39, of which 15 were waited for; matrix products, arithmetic and copies ran while one was open for 1% of the time, Pallas kernels for 15%

profile of v11, /device:TPU:0, one launch (start us, length us, event | category | flops | bytes accessed | tf_op | source)
XLA Modules:
  0.0 110.4 jit_solution(14350845881539604024)
XLA Ops:
  0.6 1.9 %shard_map.50 = (f32[32,512]{1,0:T(8,128)}, f32[256,128]{1,0:T(8,128)}) custom-call(f32[32,512]{1,0:T(8,128)} %kspace_hbm.3, s32[32,512]{1,0:T(8,128)} %mask_hbm.3, f32[256,128]{1,0:T(8,128)} %bitcast.23), custom_call_target="tpu_custom_call" | custom-call | flops 1000000000 | tf_op jit(solution)/shard_map/pallas_call | solution.py:530
  2.5 3.1 %collective-permute-start.5 = (f32[1,32,512]{2,1,0:T(8,128)}, f32[1,32,512]{2,1,0:T(8,128)S(1)}, u32[]{:S(2)}, u32[]{:S(2)}) collective-permute-start(f32[1,32,512]{2,1,0:T(8,128)} %bitcast.20), channel_id=1, source_target_pairs={{0,8},{1,9},{2,10},{3,11},{4,12},{5,13},{6,14},{7,15},{8,0},{9,1},... | collective-permute-start | bytes 196616 | tf_op jit(solution)/shard_map/ppermute | solution.py:548
  5.6 2.6 %collective-permute-start.10 = (f32[1,32,512]{2,1,0:T(8,128)}, f32[1,32,512]{2,1,0:T(8,128)S(1)}, u32[]{:S(2)}, u32[]{:S(2)}) collective-permute-start(f32[1,32,512]{2,1,0:T(8,128)} %bitcast.21), channel_id=1, source_target_pairs={{0,16},{1,17},{2,18},{3,19},{4,20},{5,21},{6,22},{7,23},{8,24},{9,... | collective-permute-start | bytes 196616 | tf_op jit(solution)/shard_map/ppermute | solution.py:548
  8.2 0.8 pad_maximum_fusion.10
  9.0 1.8 %collective-permute-start.6 = (f32[2,16,512]{2,1,0:T(8,128)S(1)}, f32[2,16,512]{2,1,0:T(8,128)S(1)}, u32[]{:S(2)}, u32[]{:S(2)}) collective-permute-start(f32[2,16,512]{2,1,0:T(8,128)S(1)} %get-tuple-element.65), channel_id=1, source_target_pairs={{0,4},{1,5},{2,6},{3,7},{4,0},{5,1},{6,2},{7,3},{8,12},{9,13},{10,... | collective-permute-start | bytes 196616 | tf_op jit(solution)/shard_map/ppermute | solution.py:548
  10.9 5.6 %all-to-all-start = ((f32[32,8,128]{2,1,0:T(8,128)}), f32[32,8,128]{2,1,0:T(8,128)S(1)}, u32[]{:S(2)}, u32[]{:S(2)}) async-start(f32[32,8,128]{2,1,0:T(8,128)} %bitcast.19), calls=%async_computation | async-start | bytes 262144 | tf_op jit(solution)/shard_map/all_to_all | solution.py:611
  16.4 1.8 %collective-permute-start.16 = (f32[2,16,512]{2,1,0:T(8,128)S(1)}, f32[2,16,512]{2,1,0:T(8,128)S(1)}, u32[]{:S(2)}, u32[]{:S(2)}) collective-permute-start(f32[2,16,512]{2,1,0:T(8,128)S(1)} %get-tuple-element.64), channel_id=1, source_target_pairs={{0,2},{1,3},{2,0},{3,1},{4,6},{5,7},{6,4},{7,5},{8,10},{9,11},{10,... | collective-permute-start | bytes 196616 | tf_op jit(solution)/shard_map/ppermute | solution.py:548
  18.3 1.5 %collective-permute-start.11 = (f32[1,32,512]{2,1,0:T(8,128)S(1)}, f32[1,32,512]{2,1,0:T(8,128)S(1)}, u32[]{:S(2)}, u32[]{:S(2)}) collective-permute-start(f32[1,32,512]{2,1,0:T(8,128)S(1)} %collective-permute-done.10), channel_id=1, source_target_pairs={{0,8},{1,9},{2,10},{3,11},{4,12},{5,13},{6,14},{7,15},{8,0},{9,1},... | collective-permute-start | bytes 196616 | tf_op jit(solution)/shard_map/ppermute | solution.py:548
  19.8 0.6 collective-permute-start.7
  20.5 2.8 %collective-permute-done.11 = f32[1,32,512]{2,1,0:T(8,128)S(1)} collective-permute-done((f32[1,32,512]{2,1,0:T(8,128)S(1)}, f32[1,32,512]{2,1,0:T(8,128)S(1)}, u32[]{:S(2)}, u32[]{:S(2)}) %collective-permute-start.11) | collective-permute-done | bytes 65568 | tf_op jit(solution)/shard_map/ppermute | solution.py:548
  23.2 1.5 %all-to-all-done = f32[32,8,128]{2,1,0:T(8,128)S(1)} async-done(((f32[32,8,128]{2,1,0:T(8,128)}), f32[32,8,128]{2,1,0:T(8,128)S(1)}, u32[]{:S(2)}, u32[]{:S(2)}) %all-to-all-start) | async-done | bytes 131104 | tf_op jit(solution)/shard_map/all_to_all | solution.py:611
  24.7 0.9 collective-permute-start.12
  25.7 1.5 %collective-permute-start.17 = (f32[4,16,512]{2,1,0:T(8,128)S(1)}, f32[4,16,512]{2,1,0:T(8,128)S(1)}, u32[]{:S(2)}, u32[]{:S(2)}) collective-permute-start(f32[4,16,512]{2,1,0:T(8,128)S(1)} %pad_maximum_fusion.5.refs_8_), channel_id=1, source_target_pairs={{0,4},{1,5},{2,6},{3,7},{4,0},{5,1},{6,2},{7,3},{8,12},{9,13},{10,... | collective-permute-start | bytes 393224 | tf_op jit(solution)/shard_map/ppermute | solution.py:548
  27.4 2.3 %collective-permute-done.12 = f32[2,16,512]{2,1,0:T(8,128)S(1)} collective-permute-done((f32[2,16,512]{2,1,0:T(8,128)S(1)}, f32[2,16,512]{2,1,0:T(8,128)S(1)}, u32[]{:S(2)}, u32[]{:S(2)}) %collective-permute-start.12) | collective-permute-done | bytes 65568 | tf_op jit(solution)/shard_map/ppermute | solution.py:548
  29.7 1.8 %collective-permute-done.20 = f32[2,16,512]{2,1,0:T(8,128)S(1)} collective-permute-done((f32[2,16,512]{2,1,0:T(8,128)S(1)}, f32[2,16,512]{2,1,0:T(8,128)S(1)}, u32[]{:S(2)}, u32[]{:S(2)}) %collective-permute-start.20) | collective-permute-done | bytes 65568 | tf_op jit(solution)/shard_map/ppermute | solution.py:548
  31.7 1.4 %collective-permute-start.21 = (f32[4,16,512]{2,1,0:T(8,128)S(1)}, f32[4,16,512]{2,1,0:T(8,128)S(1)}, u32[]{:S(2)}, u32[]{:S(2)}) collective-permute-start(f32[4,16,512]{2,1,0:T(8,128)S(1)} %pad_maximum_fusion.6.refs_12_), channel_id=1, source_target_pairs={{0,4},{1,5},{2,6},{3,7},{4,0},{5,1},{6,2},{7,3},{8,12},{9,13},{10,... | collective-permute-start | bytes 393224 | tf_op jit(solution)/shard_map/ppermute | solution.py:548
  33.1 0.5 collective-permute-start.14
  33.7 2.8 %collective-permute-done.13.refs_5_ = f32[4,16,512]{2,1,0:T(8,128)S(1)} collective-permute-done((f32[4,16,512]{2,1,0:T(8,128)S(1)}, f32[4,16,512]{2,1,0:T(8,128)S(1)}, u32[]{:S(2)}, u32[]{:S(2)}) %collective-permute-start.13) | collective-permute-done | bytes 131104 | tf_op jit(solution)/shard_map/ppermute | solution.py:548
  36.7 0.3 collective-permute-start.23
  37.0 0.8 collective-permute-done.15.refs_7_
  37.8 0.2 collective-permute-done.23.refs_15_
  38.0 12.6 %shard_map.51 = (bf16[8,2,4,32,512]{4,3,2,1,0:T(8,128)(2,1)S(1)}, f32[256,128]{1,0:T(8,128)S(1)}, f32[8,4,2,8,128]{4,3,2,1,0:T(8,128)}, f32[4,64,128]{2,1,0:T(8,128)S(1)}) custom-call(f32[8,4,8,128]{3,2,1,0:T(8,128)S(1)} %bitcast.16, f32[4,16,512]{2,1,0:T(8,128)S(1)} %pad_maximum_fusion.2.refs_0_, f32[4,16,512]{2,1,0:T(8,128)S(1)} %collective-permute-done.7.refs_1_, ...), custom_call_target="tpu_custom_call" | custom-call | flops 12000000000 | tf_op jit(solution)/shard_map/pallas_call | solution.py:530
  50.6 3.8 %all-to-all-start.1 = ((f32[32,16,128]{2,1,0:T(8,128)}), f32[32,16,128]{2,1,0:T(8,128)S(1)}, u32[]{:S(2)}, u32[]{:S(2)}) async-start(f32[32,16,128]{2,1,0:T(8,128)} %bitcast.4), calls=%async_computation.1 | async-start | bytes 524288 | tf_op jit(solution)/shard_map/all_to_all | solution.py:611
  54.4 1.4 %collective-permute-start.26 = (f32[1,64,128]{2,1,0:T(8,128)S(1)}, f32[1,64,128]{2,1,0:T(8,128)S(1)}, u32[]{:S(2)}, u32[]{:S(2)}) collective-permute-start(f32[1,64,128]{2,1,0:T(8,128)S(1)} %get-tuple-element.59), channel_id=1, source_target_pairs={{0,3},{1,2},{2,1},{3,0},{4,7},{5,6},{6,5},{7,4},{8,11},{9,10},{10,... | collective-permute-start | bytes 98312 | tf_op jit(solution)/shard_map/ppermute | solution.py:548
  55.8 0.4 collective-permute-start.25
  56.3 2.9 %shard_map.52 = f32[8,4,4,640]{3,2,1,0:T(4,128)} custom-call(bf16[8,2,4,32,512]{4,3,2,1,0:T(8,128)(2,1)S(1)} %get-tuple-element.38.samples_ref, f32[256,128]{1,0:T(8,128)S(1)} %get-tuple-element.39.vectors_ref), custom_call_target="tpu_custom_call" | custom-call | flops 2000000000 | tf_op jit(solution)/shard_map/pallas_call | solution.py:530
  59.2 1.4 %collective-permute-done.25 = f32[1,64,128]{2,1,0:T(8,128)S(1)} collective-permute-done((f32[1,64,128]{2,1,0:T(8,128)S(1)}, f32[1,64,128]{2,1,0:T(8,128)S(1)}, u32[]{:S(2)}, u32[]{:S(2)}) %collective-permute-start.25) | collective-permute-done | bytes 32800 | tf_op jit(solution)/shard_map/ppermute | solution.py:548
  60.6 4.2 %all-to-all-done.1 = f32[32,16,128]{2,1,0:T(8,128)S(1)} async-done(((f32[32,16,128]{2,1,0:T(8,128)}), f32[32,16,128]{2,1,0:T(8,128)S(1)}, u32[]{:S(2)}, u32[]{:S(2)}) %all-to-all-start.1) | async-done | bytes 262176 | tf_op jit(solution)/shard_map/all_to_all | solution.py:611
  64.8 1.0 collective-permute-start.29
  65.8 0.6 shard_map.53
  66.7 1.0 collective-permute-done.31
  67.7 0.9 collective-permute-start.34
  68.5 1.4 %collective-permute-start.33 = (f32[72,128]{1,0:T(8,128)S(1)}, f32[72,128]{1,0:T(8,128)S(1)}, u32[]{:S(2)}, u32[]{:S(2)}) collective-permute-start(f32[72,128]{1,0:T(8,128)S(1)} %add.36), channel_id=1, source_target_pairs={{0,4},{1,5},{2,6},{3,7},{4,0},{5,1},{6,2},{7,3},{8,12},{9,13},{10,... | collective-permute-start | bytes 110600 | tf_op jit(solution)/shard_map/ppermute | solution.py:548
  70.0 1.2 %collective-permute-start.32 = (f32[72,128]{1,0:T(8,128)S(1)}, f32[72,128]{1,0:T(8,128)S(1)}, u32[]{:S(2)}, u32[]{:S(2)}) collective-permute-start(f32[72,128]{1,0:T(8,128)S(1)} %add.36), channel_id=1, source_target_pairs={{0,2},{1,3},{2,0},{3,1},{4,6},{5,7},{6,4},{7,5},{8,10},{9,11},{10,... | collective-permute-start | bytes 110600 | tf_op jit(solution)/shard_map/ppermute | solution.py:548
  71.2 1.9 %collective-permute-start.30 = (f32[8,32,128]{2,1,0:T(8,128)S(1)}, f32[8,32,128]{2,1,0:T(8,128)S(1)}, u32[]{:S(2)}, u32[]{:S(2)}) collective-permute-start(f32[8,32,128]{2,1,0:T(8,128)S(1)} %pad_maximum_fusion.9), channel_id=1, source_target_pairs={{0,16},{1,17},{2,18},{3,19},{4,20},{5,21},{6,22},{7,23},{8,24},{9,... | collective-permute-start | bytes 393224 | tf_op jit(solution)/shard_map/ppermute | solution.py:548
  73.1 0.8 collective-permute-done.32
  73.9 1.7 %collective-permute-start.37 = (f32[72,128]{1,0:T(8,128)S(1)}, f32[72,128]{1,0:T(8,128)S(1)}, u32[]{:S(2)}, u32[]{:S(2)}) collective-permute-start(f32[72,128]{1,0:T(8,128)S(1)} %add_add_fusion.1), channel_id=1, source_target_pairs={{0,24},{1,25},{2,26},{3,27},{4,28},{5,29},{6,30},{7,31},{8,16},{9,... | collective-permute-start | bytes 110600 | tf_op jit(solution)/shard_map/ppermute | solution.py:548
  75.7 0.7 collective-permute-start.36
  76.4 2.0 %collective-permute-start.35 = (f32[72,128]{1,0:T(8,128)S(1)}, f32[72,128]{1,0:T(8,128)S(1)}, u32[]{:S(2)}, u32[]{:S(2)}) collective-permute-start(f32[72,128]{1,0:T(8,128)S(1)} %add_add_fusion.1), channel_id=1, source_target_pairs={{0,8},{1,9},{2,10},{3,11},{4,12},{5,13},{6,14},{7,15},{8,0},{9,1},... | collective-permute-start | bytes 110600 | tf_op jit(solution)/shard_map/ppermute | solution.py:548
  78.5 1.7 %collective-permute-done.37 = f32[72,128]{1,0:T(8,128)S(1)} collective-permute-done((f32[72,128]{1,0:T(8,128)S(1)}, f32[72,128]{1,0:T(8,128)S(1)}, u32[]{:S(2)}, u32[]{:S(2)}) %collective-permute-start.37) | collective-permute-done | bytes 36896 | tf_op jit(solution)/shard_map/ppermute | solution.py:548
  80.2 2.7 %collective-permute-done.36 = f32[72,128]{1,0:T(8,128)S(1)} collective-permute-done((f32[72,128]{1,0:T(8,128)S(1)}, f32[72,128]{1,0:T(8,128)S(1)}, u32[]{:S(2)}, u32[]{:S(2)}) %collective-permute-start.36) | collective-permute-done | bytes 36896 | tf_op jit(solution)/shard_map/ppermute | solution.py:548
  83.0 1.8 %collective-permute-done.28 = f32[8,32,128]{2,1,0:T(8,128)S(1)} collective-permute-done((f32[8,32,128]{2,1,0:T(8,128)S(1)}, f32[8,32,128]{2,1,0:T(8,128)S(1)}, u32[]{:S(2)}, u32[]{:S(2)}) %collective-permute-start.28) | collective-permute-done | bytes 131104 | tf_op jit(solution)/shard_map/ppermute | solution.py:548
  84.9 3.1 %all-to-all-start.2 = ((f32[32,4,640]{2,1,0:T(4,128)}), f32[32,4,640]{2,1,0:T(4,128)S(1)}, u32[]{:S(2)}, u32[]{:S(2)}) async-start(f32[32,4,640]{2,1,0:T(4,128)} %bitcast.6), calls=%async_computation.2 | async-start | bytes 655360 | tf_op jit(solution)/shard_map/all_to_all | solution.py:611
  88.0 1.8 %collective-permute-start.39 = (f32[16,32,128]{2,1,0:T(8,128)S(1)}, f32[16,32,128]{2,1,0:T(8,128)S(1)}, u32[]{:S(2)}, u32[]{:S(2)}) collective-permute-start(f32[16,32,128]{2,1,0:T(8,128)S(1)} %pad_maximum_fusion), channel_id=1, source_target_pairs={{0,4},{1,5},{2,6},{3,7},{4,0},{5,1},{6,2},{7,3},{8,12},{9,13},{10,... | collective-permute-start | bytes 786440 | tf_op jit(solution)/shard_map/ppermute | solution.py:548
  89.8 1.5 %collective-permute-start.40 = (f32[16,32,128]{2,1,0:T(8,128)S(1)}, f32[16,32,128]{2,1,0:T(8,128)S(1)}, u32[]{:S(2)}, u32[]{:S(2)}) collective-permute-start(f32[16,32,128]{2,1,0:T(8,128)S(1)} %pad_maximum_fusion.1), channel_id=1, source_target_pairs={{0,8},{1,9},{2,10},{3,11},{4,12},{5,13},{6,14},{7,15},{8,0},{9,1},... | collective-permute-start | bytes 786440 | tf_op jit(solution)/shard_map/ppermute | solution.py:548
  91.3 7.0 %shard_map.54 = (f32[128,128]{1,0:T(8,128)S(1)}, f32[128,128]{1,0:T(8,128)S(1)}, s32[1]{0:T(128)}) custom-call(f32[72,128]{1,0:T(8,128)S(1)} %add_add_fusion.gram_ref, f32[72,128]{1,0:T(8,128)S(1)} %collective-permute-done.38.other_ref), custom_call_target="tpu_custom_call" | custom-call | flops 12000000000 | tf_op jit(solution)/shard_map/pallas_call | solution.py:530
  99.2 5.9 %shard_map.55.both_ref = f32[128,128]{1,0:T(8,128)S(1)} custom-call(f32[128,128]{1,0:T(8,128)S(1)} %get-tuple-element.66.gram_ref, f32[128,128]{1,0:T(8,128)S(1)} %get-tuple-element.50.inverse_ref), custom_call_target="tpu_custom_call" | custom-call | tf_op jit(solution)/shard_map/pallas_call | solution.py:530
  105.3 4.9 %shard_map.56 = (f32[32,512]{1,0:T(8,128)}, f32[256,128]{1,0:T(8,128)}) custom-call(f32[128,640]{1,0:T(8,128)S(1)} %reshape.50.images_ref, f32[128,128]{1,0:T(8,128)S(1)} %shard_map.55.both_ref, f32[32,512]{1,0:T(8,128)S(1)} %copy-done, s32[32,512]{1,0:T(8,128)S(1)} %copy-done.1, f32[512,128]{1,0:T(8,128)S(1)} %bitcast.14, f32[512,128]{1,0:T(8,128)S(1)} %bitcast.17, ...), custom_call_target="tpu_custom_call" | custom-call | flops 5000000000 | tf_op jit(solution)/shard_map/pallas_call | solution.py:530
  (60 shorter events, 2.0 us)
Async XLA Ops:
  2.5 5.7 %collective-permute-start.5 = (f32[1,32,512]{2,1,0:T(8,128)}, f32[1,32,512]{2,1,0:T(8,128)S(1)}, u32[]{:S(2)}, u32[]{:S(2)}) collective-permute-start(f32[1,32,512]{2,1,0:T(8,128)} %bitcast.20), channel_id=1, source_target_pairs={{0,8},{1,9},{2,10},{3,11},{4,12},{5,13},{6,14},{7,15},{8,0},{9,1},... | collective-permute-start | bytes 196616 | tf_op jit(solution)/shard_map/ppermute | solution.py:548
  5.6 12.6 %collective-permute-start.10 = (f32[1,32,512]{2,1,0:T(8,128)}, f32[1,32,512]{2,1,0:T(8,128)S(1)}, u32[]{:S(2)}, u32[]{:S(2)}) collective-permute-start(f32[1,32,512]{2,1,0:T(8,128)} %bitcast.21), channel_id=1, source_target_pairs={{0,16},{1,17},{2,18},{3,19},{4,20},{5,21},{6,22},{7,23},{8,24},{9,... | collective-permute-start | bytes 196616 | tf_op jit(solution)/shard_map/ppermute | solution.py:548
  9.0 10.7 %collective-permute-start.6 = (f32[2,16,512]{2,1,0:T(8,128)S(1)}, f32[2,16,512]{2,1,0:T(8,128)S(1)}, u32[]{:S(2)}, u32[]{:S(2)}) collective-permute-start(f32[2,16,512]{2,1,0:T(8,128)S(1)} %get-tuple-element.65), channel_id=1, source_target_pairs={{0,4},{1,5},{2,6},{3,7},{4,0},{5,1},{6,2},{7,3},{8,12},{9,13},{10,... | collective-permute-start | bytes 196616 | tf_op jit(solution)/shard_map/ppermute | solution.py:548
  10.9 13.8 %all-to-all-start = ((f32[32,8,128]{2,1,0:T(8,128)}), f32[32,8,128]{2,1,0:T(8,128)S(1)}, u32[]{:S(2)}, u32[]{:S(2)}) async-start(f32[32,8,128]{2,1,0:T(8,128)} %bitcast.19), calls=%async_computation | async-start | bytes 262144 | tf_op jit(solution)/shard_map/all_to_all | solution.py:611
  16.4 9.2 %collective-permute-start.16 = (f32[2,16,512]{2,1,0:T(8,128)S(1)}, f32[2,16,512]{2,1,0:T(8,128)S(1)}, u32[]{:S(2)}, u32[]{:S(2)}) collective-permute-start(f32[2,16,512]{2,1,0:T(8,128)S(1)} %get-tuple-element.64), channel_id=1, source_target_pairs={{0,2},{1,3},{2,0},{3,1},{4,6},{5,7},{6,4},{7,5},{8,10},{9,11},{10,... | collective-permute-start | bytes 196616 | tf_op jit(solution)/shard_map/ppermute | solution.py:548
  18.3 5.0 %collective-permute-start.11 = (f32[1,32,512]{2,1,0:T(8,128)S(1)}, f32[1,32,512]{2,1,0:T(8,128)S(1)}, u32[]{:S(2)}, u32[]{:S(2)}) collective-permute-start(f32[1,32,512]{2,1,0:T(8,128)S(1)} %collective-permute-done.10), channel_id=1, source_target_pairs={{0,8},{1,9},{2,10},{3,11},{4,12},{5,13},{6,14},{7,15},{8,0},{9,1},... | collective-permute-start | bytes 196616 | tf_op jit(solution)/shard_map/ppermute | solution.py:548
  19.8 11.9 %collective-permute-start.8 = (f32[4,16,512]{2,1,0:T(8,128)S(1)}, f32[4,16,512]{2,1,0:T(8,128)S(1)}, u32[]{:S(2)}, u32[]{:S(2)}) collective-permute-start(f32[4,16,512]{2,1,0:T(8,128)S(1)} %pad_maximum_fusion.2.refs_0_), channel_id=1, source_target_pairs={{0,1},{1,0},{2,3},{3,2},{4,5},{5,4},{6,7},{7,6},{8,9},{9,8},{10,11... | collective-permute-start | bytes 393224 | tf_op jit(solution)/shard_map/ppermute | solution.py:548
  19.8 7.4 %collective-permute-start.7 = (f32[4,16,512]{2,1,0:T(8,128)S(1)}, f32[4,16,512]{2,1,0:T(8,128)S(1)}, u32[]{:S(2)}, u32[]{:S(2)}) collective-permute-start(f32[4,16,512]{2,1,0:T(8,128)S(1)} %pad_maximum_fusion.2.refs_0_), channel_id=1, source_target_pairs={{0,2},{1,3},{2,0},{3,1},{4,6},{5,7},{6,4},{7,5},{8,10},{9,11},{10,... | collective-permute-start | bytes 393224 | tf_op jit(solution)/shard_map/ppermute | solution.py:548
  24.7 4.9 %collective-permute-start.12 = (f32[2,16,512]{2,1,0:T(8,128)S(1)}, f32[2,16,512]{2,1,0:T(8,128)S(1)}, u32[]{:S(2)}, u32[]{:S(2)}) collective-permute-start(f32[2,16,512]{2,1,0:T(8,128)S(1)} %get-tuple-element.63), channel_id=1, source_target_pairs={{0,4},{1,5},{2,6},{3,7},{4,0},{5,1},{6,2},{7,3},{8,12},{9,13},{10,... | collective-permute-start | bytes 196616 | tf_op jit(solution)/shard_map/ppermute | solution.py:548
  25.6 7.5 %collective-permute-start.18 = (f32[4,16,512]{2,1,0:T(8,128)S(1)}, f32[4,16,512]{2,1,0:T(8,128)S(1)}, u32[]{:S(2)}, u32[]{:S(2)}) collective-permute-start(f32[4,16,512]{2,1,0:T(8,128)S(1)} %pad_maximum_fusion.5.refs_8_), channel_id=1, source_target_pairs={{0,1},{1,0},{2,3},{3,2},{4,5},{5,4},{6,7},{7,6},{8,9},{9,8},{10,11... | collective-permute-start | bytes 393224 | tf_op jit(solution)/shard_map/ppermute | solution.py:548
  25.7 7.4 %collective-permute-start.17 = (f32[4,16,512]{2,1,0:T(8,128)S(1)}, f32[4,16,512]{2,1,0:T(8,128)S(1)}, u32[]{:S(2)}, u32[]{:S(2)}) collective-permute-start(f32[4,16,512]{2,1,0:T(8,128)S(1)} %pad_maximum_fusion.5.refs_8_), channel_id=1, source_target_pairs={{0,4},{1,5},{2,6},{3,7},{4,0},{5,1},{6,2},{7,3},{8,12},{9,13},{10,... | collective-permute-start | bytes 393224 | tf_op jit(solution)/shard_map/ppermute | solution.py:548
  27.2 4.3 %collective-permute-start.20 = (f32[2,16,512]{2,1,0:T(8,128)S(1)}, f32[2,16,512]{2,1,0:T(8,128)S(1)}, u32[]{:S(2)}, u32[]{:S(2)}) collective-permute-start(f32[2,16,512]{2,1,0:T(8,128)S(1)} %get-tuple-element.62), channel_id=1, source_target_pairs={{0,2},{1,3},{2,0},{3,1},{4,6},{5,7},{6,4},{7,5},{8,10},{9,11},{10,... | collective-permute-start | bytes 196616 | tf_op jit(solution)/shard_map/ppermute | solution.py:548
  29.6 3.9 %collective-permute-start.9 = (f32[4,16,512]{2,1,0:T(8,128)S(1)}, f32[4,16,512]{2,1,0:T(8,128)S(1)}, u32[]{:S(2)}, u32[]{:S(2)}) collective-permute-start(f32[4,16,512]{2,1,0:T(8,128)S(1)} %collective-permute-done.7.refs_1_), channel_id=1, source_target_pairs={{0,1},{1,0},{2,3},{3,2},{4,5},{5,4},{6,7},{7,6},{8,9},{9,8},{10,11... | collective-permute-start | bytes 393224 | tf_op jit(solution)/shard_map/ppermute | solution.py:548
  31.5 5.0 %collective-permute-start.13 = (f32[4,16,512]{2,1,0:T(8,128)S(1)}, f32[4,16,512]{2,1,0:T(8,128)S(1)}, u32[]{:S(2)}, u32[]{:S(2)}) collective-permute-start(f32[4,16,512]{2,1,0:T(8,128)S(1)} %pad_maximum_fusion.4.refs_4_), channel_id=1, source_target_pairs={{0,2},{1,3},{2,0},{3,1},{4,6},{5,7},{6,4},{7,5},{8,10},{9,11},{10,... | collective-permute-start | bytes 393224 | tf_op jit(solution)/shard_map/ppermute | solution.py:548
  31.7 5.0 %collective-permute-start.21 = (f32[4,16,512]{2,1,0:T(8,128)S(1)}, f32[4,16,512]{2,1,0:T(8,128)S(1)}, u32[]{:S(2)}, u32[]{:S(2)}) collective-permute-start(f32[4,16,512]{2,1,0:T(8,128)S(1)} %pad_maximum_fusion.6.refs_12_), channel_id=1, source_target_pairs={{0,4},{1,5},{2,6},{3,7},{4,0},{5,1},{6,2},{7,3},{8,12},{9,13},{10,... | collective-permute-start | bytes 393224 | tf_op jit(solution)/shard_map/ppermute | solution.py:548
  33.1 3.9 %collective-permute-start.19 = (f32[4,16,512]{2,1,0:T(8,128)S(1)}, f32[4,16,512]{2,1,0:T(8,128)S(1)}, u32[]{:S(2)}, u32[]{:S(2)}) collective-permute-start(f32[4,16,512]{2,1,0:T(8,128)S(1)} %collective-permute-done.17.refs_9_), channel_id=1, source_target_pairs={{0,1},{1,0},{2,3},{3,2},{4,5},{5,4},{6,7},{7,6},{8,9},{9,8},{10,11... | collective-permute-start | bytes 393224 | tf_op jit(solution)/shard_map/ppermute | solution.py:548
  33.1 3.9 %collective-permute-start.14 = (f32[4,16,512]{2,1,0:T(8,128)S(1)}, f32[4,16,512]{2,1,0:T(8,128)S(1)}, u32[]{:S(2)}, u32[]{:S(2)}) collective-permute-start(f32[4,16,512]{2,1,0:T(8,128)S(1)} %pad_maximum_fusion.4.refs_4_), channel_id=1, source_target_pairs={{0,1},{1,0},{2,3},{3,2},{4,5},{5,4},{6,7},{7,6},{8,9},{9,8},{10,11... | collective-permute-start | bytes 393224 | tf_op jit(solution)/shard_map/ppermute | solution.py:548
  33.6 3.4 %collective-permute-start.22 = (f32[4,16,512]{2,1,0:T(8,128)S(1)}, f32[4,16,512]{2,1,0:T(8,128)S(1)}, u32[]{:S(2)}, u32[]{:S(2)}) collective-permute-start(f32[4,16,512]{2,1,0:T(8,128)S(1)} %pad_maximum_fusion.6.refs_12_), channel_id=1, source_target_pairs={{0,1},{1,0},{2,3},{3,2},{4,5},{5,4},{6,7},{7,6},{8,9},{9,8},{10,11... | collective-permute-start | bytes 393224 | tf_op jit(solution)/shard_map/ppermute | solution.py:548
  36.5 1.3 %collective-permute-start.15 = (f32[4,16,512]{2,1,0:T(8,128)S(1)}, f32[4,16,512]{2,1,0:T(8,128)S(1)}, u32[]{:S(2)}, u32[]{:S(2)}) collective-permute-start(f32[4,16,512]{2,1,0:T(8,128)S(1)} %collective-permute-done.13.refs_5_), channel_id=1, source_target_pairs={{0,1},{1,0},{2,3},{3,2},{4,5},{5,4},{6,7},{7,6},{8,9},{9,8},{10,11... | collective-permute-start | bytes 393224 | tf_op jit(solution)/shard_map/ppermute | solution.py:548
  36.7 1.3 %collective-permute-start.23 = (f32[4,16,512]{2,1,0:T(8,128)S(1)}, f32[4,16,512]{2,1,0:T(8,128)S(1)}, u32[]{:S(2)}, u32[]{:S(2)}) collective-permute-start(f32[4,16,512]{2,1,0:T(8,128)S(1)} %collective-permute-done.21.refs_13_), channel_id=1, source_target_pairs={{0,1},{1,0},{2,3},{3,2},{4,5},{5,4},{6,7},{7,6},{8,9},{9,8},{10,11... | collective-permute-start | bytes 393224 | tf_op jit(solution)/shard_map/ppermute | solution.py:548
  50.6 14.2 %all-to-all-start.1 = ((f32[32,16,128]{2,1,0:T(8,128)}), f32[32,16,128]{2,1,0:T(8,128)S(1)}, u32[]{:S(2)}, u32[]{:S(2)}) async-start(f32[32,16,128]{2,1,0:T(8,128)} %bitcast.4), calls=%async_computation.1 | async-start | bytes 524288 | tf_op jit(solution)/shard_map/all_to_all | solution.py:611
  54.4 4.8 %collective-permute-start.26 = (f32[1,64,128]{2,1,0:T(8,128)S(1)}, f32[1,64,128]{2,1,0:T(8,128)S(1)}, u32[]{:S(2)}, u32[]{:S(2)}) collective-permute-start(f32[1,64,128]{2,1,0:T(8,128)S(1)} %get-tuple-element.59), channel_id=1, source_target_pairs={{0,3},{1,2},{2,1},{3,0},{4,7},{5,6},{6,5},{7,4},{8,11},{9,10},{10,... | collective-permute-start | bytes 98312 | tf_op jit(solution)/shard_map/ppermute | solution.py:548
  55.8 4.8 %collective-permute-start.25 = (f32[1,64,128]{2,1,0:T(8,128)S(1)}, f32[1,64,128]{2,1,0:T(8,128)S(1)}, u32[]{:S(2)}, u32[]{:S(2)}) collective-permute-start(f32[1,64,128]{2,1,0:T(8,128)S(1)} %get-tuple-element.60), channel_id=1, source_target_pairs={{0,2},{1,3},{2,0},{3,1},{4,6},{5,7},{6,4},{7,5},{8,10},{9,11},{10,... | collective-permute-start | bytes 98312 | tf_op jit(solution)/shard_map/ppermute | solution.py:548
  56.2 4.4 %collective-permute-start.24 = (f32[1,64,128]{2,1,0:T(8,128)S(1)}, f32[1,64,128]{2,1,0:T(8,128)S(1)}, u32[]{:S(2)}, u32[]{:S(2)}) collective-permute-start(f32[1,64,128]{2,1,0:T(8,128)S(1)} %get-tuple-element.61), channel_id=1, source_target_pairs={{0,1},{1,0},{2,3},{3,2},{4,5},{5,4},{6,7},{7,6},{8,9},{9,8},{10,11... | collective-permute-start | bytes 98312 | tf_op jit(solution)/shard_map/ppermute | solution.py:548
  64.8 6.4 %collective-permute-start.29 = (f32[4,32,128]{2,1,0:T(8,128)S(1)}, f32[4,32,128]{2,1,0:T(8,128)S(1)}, u32[]{:S(2)}, u32[]{:S(2)}) collective-permute-start(f32[4,32,128]{2,1,0:T(8,128)S(1)} %get-tuple-element.56), channel_id=1, source_target_pairs={{0,4},{1,5},{2,6},{3,7},{4,0},{5,1},{6,2},{7,3},{8,12},{9,13},{10,... | collective-permute-start | bytes 196616 | tf_op jit(solution)/shard_map/ppermute | solution.py:548
  66.4 1.3 %collective-permute-start.31 = (f32[72,128]{1,0:T(8,128)S(1)}, f32[72,128]{1,0:T(8,128)S(1)}, u32[]{:S(2)}, u32[]{:S(2)}) collective-permute-start(f32[72,128]{1,0:T(8,128)S(1)} %get-tuple-element.44), channel_id=1, source_target_pairs={{0,1},{1,0},{2,3},{3,2},{4,5},{5,4},{6,7},{7,6},{8,9},{9,8},{10,11... | collective-permute-start | bytes 110600 | tf_op jit(solution)/shard_map/ppermute | solution.py:548
  66.5 11.9 %collective-permute-start.27 = (f32[4,32,128]{2,1,0:T(8,128)S(1)}, f32[4,32,128]{2,1,0:T(8,128)S(1)}, u32[]{:S(2)}, u32[]{:S(2)}) collective-permute-start(f32[4,32,128]{2,1,0:T(8,128)S(1)} %get-tuple-element.57), channel_id=1, source_target_pairs={{0,16},{1,17},{2,18},{3,19},{4,20},{5,21},{6,22},{7,23},{8,24},{9,... | collective-permute-start | bytes 196616 | tf_op jit(solution)/shard_map/ppermute | solution.py:548
  67.7 5.4 %collective-permute-start.34 = (f32[72,128]{1,0:T(8,128)S(1)}, f32[72,128]{1,0:T(8,128)S(1)}, u32[]{:S(2)}, u32[]{:S(2)}) collective-permute-start(f32[72,128]{1,0:T(8,128)S(1)} %add.36), channel_id=1, source_target_pairs={{0,6},{1,7},{2,4},{3,5},{4,2},{5,3},{6,0},{7,1},{8,14},{9,15},{10,... | collective-permute-start | bytes 110600 | tf_op jit(solution)/shard_map/ppermute | solution.py:548
  68.5 4.6 %collective-permute-start.33 = (f32[72,128]{1,0:T(8,128)S(1)}, f32[72,128]{1,0:T(8,128)S(1)}, u32[]{:S(2)}, u32[]{:S(2)}) collective-permute-start(f32[72,128]{1,0:T(8,128)S(1)} %add.36), channel_id=1, source_target_pairs={{0,4},{1,5},{2,6},{3,7},{4,0},{5,1},{6,2},{7,3},{8,12},{9,13},{10,... | collective-permute-start | bytes 110600 | tf_op jit(solution)/shard_map/ppermute | solution.py:548
  70.0 4.0 %collective-permute-start.32 = (f32[72,128]{1,0:T(8,128)S(1)}, f32[72,128]{1,0:T(8,128)S(1)}, u32[]{:S(2)}, u32[]{:S(2)}) collective-permute-start(f32[72,128]{1,0:T(8,128)S(1)} %add.36), channel_id=1, source_target_pairs={{0,2},{1,3},{2,0},{3,1},{4,6},{5,7},{6,4},{7,5},{8,10},{9,11},{10,... | collective-permute-start | bytes 110600 | tf_op jit(solution)/shard_map/ppermute | solution.py:548
  71.2 11.8 %collective-permute-start.30 = (f32[8,32,128]{2,1,0:T(8,128)S(1)}, f32[8,32,128]{2,1,0:T(8,128)S(1)}, u32[]{:S(2)}, u32[]{:S(2)}) collective-permute-start(f32[8,32,128]{2,1,0:T(8,128)S(1)} %pad_maximum_fusion.9), channel_id=1, source_target_pairs={{0,16},{1,17},{2,18},{3,19},{4,20},{5,21},{6,22},{7,23},{8,24},{9,... | collective-permute-start | bytes 393224 | tf_op jit(solution)/shard_map/ppermute | solution.py:548
  73.9 6.3 %collective-permute-start.37 = (f32[72,128]{1,0:T(8,128)S(1)}, f32[72,128]{1,0:T(8,128)S(1)}, u32[]{:S(2)}, u32[]{:S(2)}) collective-permute-start(f32[72,128]{1,0:T(8,128)S(1)} %add_add_fusion.1), channel_id=1, source_target_pairs={{0,24},{1,25},{2,26},{3,27},{4,28},{5,29},{6,30},{7,31},{8,16},{9,... | collective-permute-start | bytes 110600 | tf_op jit(solution)/shard_map/ppermute | solution.py:548
  75.7 7.2 %collective-permute-start.36 = (f32[72,128]{1,0:T(8,128)S(1)}, f32[72,128]{1,0:T(8,128)S(1)}, u32[]{:S(2)}, u32[]{:S(2)}) collective-permute-start(f32[72,128]{1,0:T(8,128)S(1)} %add_add_fusion.1), channel_id=1, source_target_pairs={{0,16},{1,17},{2,18},{3,19},{4,20},{5,21},{6,22},{7,23},{8,24},{9,... | collective-permute-start | bytes 110600 | tf_op jit(solution)/shard_map/ppermute | solution.py:548
  76.4 6.5 %collective-permute-start.35 = (f32[72,128]{1,0:T(8,128)S(1)}, f32[72,128]{1,0:T(8,128)S(1)}, u32[]{:S(2)}, u32[]{:S(2)}) collective-permute-start(f32[72,128]{1,0:T(8,128)S(1)} %add_add_fusion.1), channel_id=1, source_target_pairs={{0,8},{1,9},{2,10},{3,11},{4,12},{5,13},{6,14},{7,15},{8,0},{9,1},... | collective-permute-start | bytes 110600 | tf_op jit(solution)/shard_map/ppermute | solution.py:548
  78.4 6.4 %collective-permute-start.28 = (f32[8,32,128]{2,1,0:T(8,128)S(1)}, f32[8,32,128]{2,1,0:T(8,128)S(1)}, u32[]{:S(2)}, u32[]{:S(2)}) collective-permute-start(f32[8,32,128]{2,1,0:T(8,128)S(1)} %pad_maximum_fusion.8), channel_id=1, source_target_pairs={{0,8},{1,9},{2,10},{3,11},{4,12},{5,13},{6,14},{7,15},{8,0},{9,1},... | collective-permute-start | bytes 393224 | tf_op jit(solution)/shard_map/ppermute | solution.py:548
  82.9 2.0 %collective-permute-start.38 = (f32[72,128]{1,0:T(8,128)S(1)}, f32[72,128]{1,0:T(8,128)S(1)}, u32[]{:S(2)}, u32[]{:S(2)}) collective-permute-start(f32[72,128]{1,0:T(8,128)S(1)} %add_add_fusion.gram_ref), channel_id=1, source_target_pairs={{0,1},{1,0},{2,3},{3,2},{4,5},{5,4},{6,7},{7,6},{8,9},{9,8},{10,11... | collective-permute-start | bytes 110600 | tf_op jit(solution)/shard_map/ppermute | solution.py:548
  84.9 20.2 %all-to-all-start.2 = ((f32[32,4,640]{2,1,0:T(4,128)}), f32[32,4,640]{2,1,0:T(4,128)S(1)}, u32[]{:S(2)}, u32[]{:S(2)}) async-start(f32[32,4,640]{2,1,0:T(4,128)} %bitcast.6), calls=%async_computation.2 | async-start | bytes 655360 | tf_op jit(solution)/shard_map/all_to_all | solution.py:611
  88.0 17.2 %collective-permute-start.39 = (f32[16,32,128]{2,1,0:T(8,128)S(1)}, f32[16,32,128]{2,1,0:T(8,128)S(1)}, u32[]{:S(2)}, u32[]{:S(2)}) collective-permute-start(f32[16,32,128]{2,1,0:T(8,128)S(1)} %pad_maximum_fusion), channel_id=1, source_target_pairs={{0,4},{1,5},{2,6},{3,7},{4,0},{5,1},{6,2},{7,3},{8,12},{9,13},{10,... | collective-permute-start | bytes 786440 | tf_op jit(solution)/shard_map/ppermute | solution.py:548
  89.8 15.4 %collective-permute-start.40 = (f32[16,32,128]{2,1,0:T(8,128)S(1)}, f32[16,32,128]{2,1,0:T(8,128)S(1)}, u32[]{:S(2)}, u32[]{:S(2)}) collective-permute-start(f32[16,32,128]{2,1,0:T(8,128)S(1)} %pad_maximum_fusion.1), channel_id=1, source_target_pairs={{0,8},{1,9},{2,10},{3,11},{4,12},{5,13},{6,14},{7,15},{8,0},{9,1},... | collective-permute-start | bytes 786440 | tf_op jit(solution)/shard_map/ppermute | solution.py:548
  98.9 6.3 %copy-start = (f32[32,512]{1,0:T(8,128)S(1)}, f32[32,512]{1,0:T(8,128)}, u32[]{:S(2)}) copy-start(f32[32,512]{1,0:T(8,128)} %kspace_hbm.3) | copy-start | bytes 196612
  98.9 6.3 %copy-start.1 = (s32[32,512]{1,0:T(8,128)S(1)}, s32[32,512]{1,0:T(8,128)}, u32[]{:S(2)}) copy-start(s32[32,512]{1,0:T(8,128)} %mask_hbm.3) | copy-start | bytes 196612

commit v12 on v11

--- a/solution.py
+++ b/solution.py
@@ -163,12 +163,15 @@
     ).astype(jnp.bfloat16)
     both = dot(flip, jnp.concatenate([high, low], axis=1)).astype(jnp.bfloat16)
     high, low = both[:, :channels], both[:, channels:]
-    twice = jnp.concatenate([high, high], axis=1)
+    zero = jnp.zeros_like(low)
+    both = jnp.concatenate(
+        [jnp.concatenate([high, high], axis=1), jnp.concatenate([low, zero], axis=1)], axis=0
+    )
     tiles = samples_ref.shape[0]
     tile = samples_ref.shape[-1]
     for t in range(tiles):
-        block = samples_ref[t].reshape(2 * channels, tile)
-        wide_ref[:, t * tile : (t + 1) * tile] = dot(twice, block) + dot(low, block[:channels])
+        wide = dot(both, samples_ref[t].reshape(2 * channels, tile))
+        wide_ref[:, t * tile : (t + 1) * tile] = wide[:rows] + wide[rows:]
     images = []
     for k in range(cols):
         total = None
@@ -373,7 +376,6 @@
         inverse = {}
         for k in range(SUB):
             root = lax.rsqrt(entry[k, k])
-            root = root * (1.5 - (0.5 * entry[k, k]) * (root * root))
             inverse[k, k] = root
             for i in range(k + 1, SUB):
                 entry[i, k] = entry[i, k] * root
@@ -439,9 +441,10 @@
     both_ref[...] = exact(inverse_factor(gram_ref[...]), inverse_ref[...])
 
 
-def moved_columns(values, order):
+def moved_columns(order, cols):
     devices = len(order[0])
-    at_row, at_col = square(values.shape[0])
+    at_row, at_col = square(devices * cols)
+    turn = at_col % cols * devices + at_col // cols
     me = lax.axis_index("rows") * lax.axis_size("coil") + lax.axis_index("coil")
     slot = at_col % devices
     mask = jnp.zeros_like(slot)
@@ -451,7 +454,21 @@
         mask = mask | jnp.where(slot & bit != 0, step, 0)
         bit *= 2
     source = at_col - slot + lax.bitwise_xor(mask, jnp.full_like(mask, me))
-    return exact(values, (at_row == source).astype(jnp.float32))
+    return [(at_row == place).astype(jnp.float32) for place in (turn, source)]
+
+
+def stacked_dot(a, b):
+    a_high, a_low = split(a)
+    b_high, b_low = split(b)
+    left = jnp.concatenate(
+        [
+            jnp.concatenate([a_high, a_high], axis=1),
+            jnp.concatenate([a_low, jnp.zeros_like(a_low)], axis=1),
+        ],
+        axis=0,
+    )
+    both = dot(left, jnp.concatenate([b_high, b_low], axis=0))
+    return both[: a.shape[0]] + both[a.shape[0] :]
 
 
 def last_kernel(
@@ -479,21 +496,17 @@
     for fetch in fetches:
         fetch.start()
     both = both_ref[...]
-    count, reach = images_ref.shape
-    devices = count // cols
-    at_row, at_col = square(count)
-    turn = ((at_row // devices == at_col % cols) & (at_row % devices == at_col // cols)).astype(
-        jnp.float32
-    )
-    images = exact(exact(both, turn), images_ref[...])
-    images_high, images_low = split(images)
-    stacked = jnp.concatenate([images_high, images_low], axis=0)
+    reach = images_ref.shape[1]
+    factors = [exact(both, moved) for moved in moved_columns(order, cols)]
     chg, tile = kspace_ref.shape
     lanes = top_near_ref.shape[1]
-    deep = KER * chg // lanes
+    fold = lanes // chg
+    deep = KER // fold
     step = cols // 2 * deep
-    factor = moved_columns(both, order)
-    estimate = jnp.zeros((chg, reach), jnp.float32)
+    lead = reach - tile - KER - 2 * SUB
+    images = stacked_dot(factors[0], images_ref[...]).T[lead:]
+    rim = reach - tile - SUB - lead
+    even, odd = None, None
     for a in range(0, deep, 2):
         turned = [
             jnp.concatenate(
@@ -507,18 +520,23 @@
             )
             for i in range(2)
         ]
-        vectors = dot3(jnp.concatenate(turned, axis=1), factor, ((0,), (1,)))
-        vectors_ref[a * lanes : (a + 2) * lanes, :] = vectors
-        high, low = split(vectors)
-        projected = dot(jnp.concatenate([high, high], axis=1), stacked) + dot(low, images_high)
-        for i in range(2 * lanes // chg):
-            j = a * lanes // chg + i
-            part = projected[i * chg : (i + 1) * chg]
-            estimate = estimate + (pltpu.roll(part, j, 1) if j else part)
+        vectors = stacked_dot(factors[1], jnp.concatenate(turned, axis=1))
+        vectors_ref[:, a * lanes : (a + 2) * lanes] = vectors
+        projected = stacked_dot(images, vectors)
+        shift = a * fold
+        part = projected[rim - shift : rim - shift + tile + SUB, :lanes]
+        even = part if even is None else even + part
+        part = projected[rim - SUB - shift : rim - shift + tile + SUB, lanes:]
+        odd = part if odd is None else odd + part
+    total = even + odd[SUB - fold : SUB - fold + tile + SUB]
+    estimate = total[SUB : SUB + tile]
+    for f in range(1, fold):
+        moved = pltpu.roll(total, lanes - f * chg, 1)
+        estimate = estimate + moved[SUB - f : SUB - f + tile]
+    estimate = estimate.T[:chg]
     owned = basis_ref.shape[0]
     start = pl.multiple_of(lax.axis_index("rows") * owned, owned)
-    basis_ref[...] = vectors_ref[pl.ds(start, owned), :]
-    estimate = estimate[:, reach - tile :]
+    basis_ref[...] = vectors_ref[:, pl.ds(start, owned)].T
     for fetch in fetches:
         fetch.wait()
     estimate = estimate / KER
@@ -574,37 +592,39 @@
     return part, order + [m ^ mask for mask in masks for m in order]
 
 
-def gather_samples(sampled, tiles, groups, beside):
+def gather_samples(sampled, basis, tiles, groups):
     devices = tiles * groups
-    first = devices // 2
-    near = sampled[None]
-    streams = [(near, [0]), (exchange(near, devices, first, AXES), [first])]
-    halves = [[], []]
-    for number, (near, masks) in enumerate(streams):
-        mask = first // 2
-        while mask > groups:
-            near, masks = gather_round(near, masks, [mask], devices, AXES)
-            mask //= 2
-        if number:
-            near = after(near, beside)
-        half = near.shape[1] // 2
-        for i, (part, ways) in enumerate(
-            (
-                (near[:, :half], (groups, groups // 2)),
-                (near[:, half:], (groups // 2, groups)),
-            )
-        ):
-            pieces = [gather_round(part, masks, [ways[0]], devices, AXES)]
-            mask = ways[1]
-            rest = groups // 4
-            while mask:
-                pieces = pieces + [
-                    (exchange(part, devices, mask, AXES), [m ^ mask for m in order])
-                    for part, order in pieces
-                ]
-                mask, rest = rest, rest // 2
-            halves[i] += pieces
-    return halves
+    near, masks = sampled[None], [0]
+    mask = devices // 2
+    while mask > groups:
+        near, masks = gather_round(near, masks, [mask], devices, AXES)
+        mask //= 2
+    half = near.shape[1] // 2
+    halves = []
+    for part, ways in (
+        (near[:, :half], (groups, groups // 2)),
+        (near[:, half:], (groups // 2, groups)),
+    ):
+        part, order = gather_round(part, masks, [ways[0]], devices, AXES)
+        if not halves:
+            basis = to_all(after(basis, part))
+        pieces = [(part, order)]
+        mask = ways[1]
+        rest = groups // 4
+        while mask > 1:
+            pieces = pieces + [
+                (exchange(part, devices, mask, AXES), [m ^ mask for m in order])
+                for part, order in pieces
+            ]
+            mask, rest = rest, rest // 2
+        if halves:
+            part, order = pieces[-1]
+            pieces[-1] = (after(part, basis), order)
+        halves.append(
+            pieces
+            + [(exchange(part, devices, 1, AXES), [m ^ 1 for m in order]) for part, order in pieces]
+        )
+    return halves, basis
 
 
 def to_all(pieces, axes=AXES):
@@ -686,8 +706,9 @@
         far=(0, 1, 2),
         limit=60,
     )
-    basis_parts = to_all(basis_send.reshape(devices, per_tile, lanes))
-    halves = gather_samples(sampled, tiles, groups, basis_parts)
+    halves, basis_parts = gather_samples(
+        sampled, basis_send.reshape(devices, per_tile, lanes), tiles, groups
+    )
     starts = (0, chg // len(halves))
     orders = [(start, order) for start, half in zip(starts, halves) for _, order in half]
     wide = pltpu.VMEM((rows, positions), f32)
@@ -752,7 +773,7 @@
         scratch=[
             pltpu.VMEM((chg, tile), f32),
             pltpu.VMEM((chg, tile), sample_mask.dtype),
-            pltpu.VMEM((KER * chg, rank), f32),
+            pltpu.VMEM((rank, KER * chg), f32),
             pltpu.SemaphoreType.DMA((2,)),
         ],
         far=(2, 3),
@@ -777,6 +798,8 @@
         and tile % LANES == 0
         and owned == SUB * chg
         and chg * (rank // devices) == LANES
+        and 2 * (LANES // chg) == SUB
+        and KER + 2 * SUB <= LANES
         and chg % (4 * SUB) == 0
         and (chg * groups) % LANES == 0
         and KER <= LANES

time: 111 us -> 115 us (1.036)
  waiting for transfers between devices: 26.1 us -> 32.2 us
  starting transfers between devices: 45.5 us -> 39.5 us
  local copies, waits for them, and re-layouts: 0.16 us -> 3.1 us
    all_to_all x3, waiting for transfers between devices: 5.65 us -> 11.7 us  [to_all(): return lax.all_to_all(pieces, axes, 0, 0, tiled=True)]
    ppermute x36 -> x27, starting transfers between devices: 33.1 us -> 29 us  [exchange(): return lax.ppermute(block, axes, [(i, i ^ mask) for i in range(devices)])]
    unnamed x4 -> x8, local copies, waits for them, and re-layouts: 0.01 us -> 2.94 us
    all_to_all x3, starting transfers between devices: 12.4 us -> 10.4 us  [to_all(): return lax.all_to_all(pieces, axes, 0, 0, tiled=True)]
    ppermute x36 -> x27, waiting for transfers between devices: 20.4 us -> 20.5 us  [exchange(): return lax.ppermute(block, axes, [(i, i ^ mask) for i in range(devices)])]
  transfers between devices with their start and end apart: 39 -> 30, of which waited for: 15 -> 13; matrix products, arithmetic and copies ran while one was open for 1% -> 0% of each run, Pallas kernels for 15% -> 13%
where the time goes in v12:
time: 115 us
  starting transfers between devices  39.5 us (34%)
  Pallas kernels  36.2 us (31%)
  waiting for transfers between devices  32.2 us (28%)
  local copies, waits for them, and re-layouts  3.1 us (3%)
  other arithmetic  1.84 us (2%)
  between operations  1.72 us (1%)
    pallas_call x7, Pallas kernels, call(): pl.pallas_call(kernel, out_shape=[jax.ShapeDtypeStruct(shape, kind) for s...  36.2 us
    ppermute x27, starting transfers between devices, exchange(): return lax.ppermute(block, axes, [(i, i ^ mask) for i in range(devices)])  29 us
    ppermute x27, waiting for transfers between devices, exchange(): return lax.ppermute(block, axes, [(i, i ^ mask) for i in range(devices)])  20.5 us
    all_to_all x3, waiting for transfers between devices, to_all(): return lax.all_to_all(pieces, axes, 0, 0, tiled=True)  11.7 us
    all_to_all x3, starting transfers between devices, to_all(): return lax.all_to_all(pieces, axes, 0, 0, tiled=True)  10.4 us
    unnamed x8, local copies, waits for them, and re-layouts  2.94 us
  transfers between devices with their start and end apart: 30, of which 13 were waited for; matrix products, arithmetic and copies ran while one was open for 0% of the time, Pallas kernels for 13%

profile of v12, /device:TPU:0, one launch (start us, length us, event | category | flops | bytes accessed | tf_op | source)
XLA Modules:
  0.0 114.8 jit_solution(13080862114315363767)
XLA Ops:
  0.6 1.9 %shard_map.50 = (f32[32,512]{1,0:T(8,128)}, f32[256,128]{1,0:T(8,128)}) custom-call(f32[32,512]{1,0:T(8,128)} %kspace_hbm.3, s32[32,512]{1,0:T(8,128)} %mask_hbm.3, f32[256,128]{1,0:T(8,128)} %bitcast.22), custom_call_target="tpu_custom_call" | custom-call | flops 1000000000 | tf_op jit(solution)/shard_map/pallas_call | solution.py:548
  2.5 4.1 %collective-permute-start.5 = (f32[1,32,512]{2,1,0:T(8,128)}, f32[1,32,512]{2,1,0:T(8,128)S(1)}, u32[]{:S(2)}, u32[]{:S(2)}) collective-permute-start(f32[1,32,512]{2,1,0:T(8,128)} %bitcast.19), channel_id=1, source_target_pairs={{0,16},{1,17},{2,18},{3,19},{4,20},{5,21},{6,22},{7,23},{8,24},{9,... | collective-permute-start | bytes 196616 | tf_op jit(solution)/shard_map/ppermute | solution.py:566
  6.6 3.9 %collective-permute-done.5 = f32[1,32,512]{2,1,0:T(8,128)S(1)} collective-permute-done((f32[1,32,512]{2,1,0:T(8,128)}, f32[1,32,512]{2,1,0:T(8,128)S(1)}, u32[]{:S(2)}, u32[]{:S(2)}) %collective-permute-start.5) | collective-permute-done | bytes 65568 | tf_op jit(solution)/shard_map/ppermute | solution.py:566
  10.5 0.8 pad_maximum_fusion.5
  11.3 0.7 collective-permute-start.6
  12.1 4.3 %collective-permute-done.6 = f32[2,32,512]{2,1,0:T(8,128)S(1)} collective-permute-done((f32[2,32,512]{2,1,0:T(8,128)S(1)}, f32[2,32,512]{2,1,0:T(8,128)S(1)}, u32[]{:S(2)}, u32[]{:S(2)}) %collective-permute-start.6) | collective-permute-done | bytes 131104 | tf_op jit(solution)/shard_map/ppermute | solution.py:566
  16.4 0.9 pad_maximum_fusion
  17.3 1.8 %collective-permute-start.11 = (f32[4,16,512]{2,1,0:T(8,128)S(1)}, f32[4,16,512]{2,1,0:T(8,128)S(1)}, u32[]{:S(2)}, u32[]{:S(2)}) collective-permute-start(f32[4,16,512]{2,1,0:T(8,128)S(1)} %get-tuple-element.58), channel_id=1, source_target_pairs={{0,2},{1,3},{2,0},{3,1},{4,6},{5,7},{6,4},{7,5},{8,10},{9,11},{10,... | collective-permute-start | bytes 393224 | tf_op jit(solution)/shard_map/ppermute | solution.py:566
  19.1 1.5 %collective-permute-start.7 = (f32[4,16,512]{2,1,0:T(8,128)S(1)}, f32[4,16,512]{2,1,0:T(8,128)S(1)}, u32[]{:S(2)}, u32[]{:S(2)}) collective-permute-start(f32[4,16,512]{2,1,0:T(8,128)S(1)} %get-tuple-element.59), channel_id=1, source_target_pairs={{0,4},{1,5},{2,6},{3,7},{4,0},{5,1},{6,2},{7,3},{8,12},{9,13},{10,... | collective-permute-start | bytes 393224 | tf_op jit(solution)/shard_map/ppermute | solution.py:566
  20.6 1.7 %collective-permute-done.11 = f32[4,16,512]{2,1,0:T(8,128)S(1)} collective-permute-done((f32[4,16,512]{2,1,0:T(8,128)S(1)}, f32[4,16,512]{2,1,0:T(8,128)S(1)}, u32[]{:S(2)}, u32[]{:S(2)}) %collective-permute-start.11) | collective-permute-done | bytes 131104 | tf_op jit(solution)/shard_map/ppermute | solution.py:566
  22.3 1.9 %collective-permute-start.12 = (f32[8,16,512]{2,1,0:T(8,128)S(1)}, f32[8,16,512]{2,1,0:T(8,128)S(1)}, u32[]{:S(2)}, u32[]{:S(2)}) collective-permute-start(f32[8,16,512]{2,1,0:T(8,128)S(1)} %pad_maximum_fusion.2.refs_4_), channel_id=1, source_target_pairs={{0,4},{1,5},{2,6},{3,7},{4,0},{5,1},{6,2},{7,3},{8,12},{9,13},{10,... | collective-permute-start | bytes 786440 | tf_op jit(solution)/shard_map/ppermute | solution.py:566
  24.2 1.1 collective-permute-done.7
  25.4 1.4 %collective-permute-start.8 = (f32[8,16,512]{2,1,0:T(8,128)S(1)}, f32[8,16,512]{2,1,0:T(8,128)S(1)}, u32[]{:S(2)}, u32[]{:S(2)}) collective-permute-start(f32[8,16,512]{2,1,0:T(8,128)S(1)} %pad_maximum_fusion.1.refs_0_), channel_id=1, source_target_pairs={{0,2},{1,3},{2,0},{3,1},{4,6},{5,7},{6,4},{7,5},{8,10},{9,11},{10,... | collective-permute-start | bytes 786440 | tf_op jit(solution)/shard_map/ppermute | solution.py:566
  26.8 4.6 %all-to-all-start = ((f32[32,8,128]{2,1,0:T(8,128)}), f32[32,8,128]{2,1,0:T(8,128)S(1)}, u32[]{:S(2)}, u32[]{:S(2)}) async-start(f32[32,8,128]{2,1,0:T(8,128)} %bitcast.1), calls=%async_computation | async-start | bytes 262144 | tf_op jit(solution)/shard_map/all_to_all | solution.py:631
  31.4 0.3 collective-permute-start.9
  31.9 7.7 %all-to-all-done = f32[32,8,128]{2,1,0:T(8,128)S(1)} async-done(((f32[32,8,128]{2,1,0:T(8,128)}), f32[32,8,128]{2,1,0:T(8,128)S(1)}, u32[]{:S(2)}, u32[]{:S(2)}) %all-to-all-start) | async-done | bytes 131104 | tf_op jit(solution)/shard_map/all_to_all | solution.py:631
  39.8 0.3 collective-permute-start.14
  40.1 1.0 collective-permute-done.10.refs_3_
  41.1 0.4 collective-permute-done.14.refs_7_
  41.5 15.7 %shard_map.51 = (bf16[8,2,4,32,512]{4,3,2,1,0:T(8,128)(2,1)S(1)}, f32[256,128]{1,0:T(8,128)S(1)}, f32[8,4,2,8,128]{4,3,2,1,0:T(8,128)}, f32[4,64,128]{2,1,0:T(8,128)S(1)}) custom-call(f32[8,4,8,128]{3,2,1,0:T(8,128)S(1)} %bitcast.16, f32[8,16,512]{2,1,0:T(8,128)S(1)} %pad_maximum_fusion.1.refs_0_, f32[8,16,512]{2,1,0:T(8,128)S(1)} %collective-permute-done.8.refs_1_, ...), custom_call_target="tpu_custom_call" | custom-call | flops 12000000000 | tf_op jit(solution)/shard_map/pallas_call | solution.py:548
  57.2 1.3 %copy-done.2 = bf16[8,2,4,32,512]{4,3,2,1,0:T(8,128)(2,1)} copy-done((bf16[8,2,4,32,512]{4,3,2,1,0:T(8,128)(2,1)}, bf16[8,2,4,32,512]{4,3,2,1,0:T(8,128)(2,1)S(1)}, u32[]{:S(2)}) %copy-start.2) | copy-done | bytes 2097176
  58.6 2.8 %all-to-all-start.1 = ((f32[32,16,128]{2,1,0:T(8,128)}), f32[32,16,128]{2,1,0:T(8,128)S(1)}, u32[]{:S(2)}, u32[]{:S(2)}) async-start(f32[32,16,128]{2,1,0:T(8,128)} %bitcast.4), calls=%async_computation.1 | async-start | bytes 524288 | tf_op jit(solution)/shard_map/all_to_all | solution.py:631
  61.4 1.3 %collective-permute-start.17 = (f32[1,64,128]{2,1,0:T(8,128)S(1)}, f32[1,64,128]{2,1,0:T(8,128)S(1)}, u32[]{:S(2)}, u32[]{:S(2)}) collective-permute-start(f32[1,64,128]{2,1,0:T(8,128)S(1)} %get-tuple-element.63), channel_id=1, source_target_pairs={{0,3},{1,2},{2,1},{3,0},{4,7},{5,6},{6,5},{7,4},{8,11},{9,10},{10,... | collective-permute-start | bytes 98312 | tf_op jit(solution)/shard_map/ppermute | solution.py:566
  62.7 0.4 collective-permute-start.16
  63.0 0.3 collective-permute-start.15
  63.3 1.6 %copy-done.3 = bf16[8,2,4,32,512]{4,3,2,1,0:T(8,128)(2,1)S(1)} copy-done((bf16[8,2,4,32,512]{4,3,2,1,0:T(8,128)(2,1)S(1)}, bf16[8,2,4,32,512]{4,3,2,1,0:T(8,128)(2,1)}, u32[]{:S(2)}) %copy-start.3) | copy-done | bytes 2097176
  64.9 2.8 %shard_map.52 = f32[8,4,4,640]{3,2,1,0:T(4,128)} custom-call(bf16[8,2,4,32,512]{4,3,2,1,0:T(8,128)(2,1)S(1)} %copy-done.3, f32[256,128]{1,0:T(8,128)S(1)} %get-tuple-element.41.vectors_ref), custom_call_target="tpu_custom_call" | custom-call | flops 2000000000 | tf_op jit(solution)/shard_map/pallas_call | solution.py:548
  67.7 4.1 %all-to-all-done.1 = f32[32,16,128]{2,1,0:T(8,128)S(1)} async-done(((f32[32,16,128]{2,1,0:T(8,128)}), f32[32,16,128]{2,1,0:T(8,128)S(1)}, u32[]{:S(2)}, u32[]{:S(2)}) %all-to-all-start.1) | async-done | bytes 262176 | tf_op jit(solution)/shard_map/all_to_all | solution.py:631
  71.8 1.0 collective-permute-start.20
  72.7 0.6 shard_map.53
  73.6 1.0 collective-permute-done.22
  74.6 0.8 collective-permute-start.25
  75.5 1.5 %collective-permute-start.24 = (f32[72,128]{1,0:T(8,128)S(1)}, f32[72,128]{1,0:T(8,128)S(1)}, u32[]{:S(2)}, u32[]{:S(2)}) collective-permute-start(f32[72,128]{1,0:T(8,128)S(1)} %add.36), channel_id=1, source_target_pairs={{0,4},{1,5},{2,6},{3,7},{4,0},{5,1},{6,2},{7,3},{8,12},{9,13},{10,... | collective-permute-start | bytes 110600 | tf_op jit(solution)/shard_map/ppermute | solution.py:566
  76.9 1.2 %collective-permute-start.23 = (f32[72,128]{1,0:T(8,128)S(1)}, f32[72,128]{1,0:T(8,128)S(1)}, u32[]{:S(2)}, u32[]{:S(2)}) collective-permute-start(f32[72,128]{1,0:T(8,128)S(1)} %add.36), channel_id=1, source_target_pairs={{0,2},{1,3},{2,0},{3,1},{4,6},{5,7},{6,4},{7,5},{8,10},{9,11},{10,... | collective-permute-start | bytes 110600 | tf_op jit(solution)/shard_map/ppermute | solution.py:566
  78.1 1.9 %collective-permute-start.21 = (f32[8,32,128]{2,1,0:T(8,128)S(1)}, f32[8,32,128]{2,1,0:T(8,128)S(1)}, u32[]{:S(2)}, u32[]{:S(2)}) collective-permute-start(f32[8,32,128]{2,1,0:T(8,128)S(1)} %pad_maximum_fusion.8), channel_id=1, source_target_pairs={{0,16},{1,17},{2,18},{3,19},{4,20},{5,21},{6,22},{7,23},{8,24},{9,... | collective-permute-start | bytes 393224 | tf_op jit(solution)/shard_map/ppermute | solution.py:566
  80.1 0.8 collective-permute-done.23
  80.9 1.7 %collective-permute-start.28 = (f32[72,128]{1,0:T(8,128)S(1)}, f32[72,128]{1,0:T(8,128)S(1)}, u32[]{:S(2)}, u32[]{:S(2)}) collective-permute-start(f32[72,128]{1,0:T(8,128)S(1)} %add_add_fusion.1), channel_id=1, source_target_pairs={{0,24},{1,25},{2,26},{3,27},{4,28},{5,29},{6,30},{7,31},{8,16},{9,... | collective-permute-start | bytes 110600 | tf_op jit(solution)/shard_map/ppermute | solution.py:566
  82.6 0.6 collective-permute-start.27
  83.3 2.1 %collective-permute-start.26 = (f32[72,128]{1,0:T(8,128)S(1)}, f32[72,128]{1,0:T(8,128)S(1)}, u32[]{:S(2)}, u32[]{:S(2)}) collective-permute-start(f32[72,128]{1,0:T(8,128)S(1)} %add_add_fusion.1), channel_id=1, source_target_pairs={{0,8},{1,9},{2,10},{3,11},{4,12},{5,13},{6,14},{7,15},{8,0},{9,1},... | collective-permute-start | bytes 110600 | tf_op jit(solution)/shard_map/ppermute | solution.py:566
  85.5 1.7 %collective-permute-done.28 = f32[72,128]{1,0:T(8,128)S(1)} collective-permute-done((f32[72,128]{1,0:T(8,128)S(1)}, f32[72,128]{1,0:T(8,128)S(1)}, u32[]{:S(2)}, u32[]{:S(2)}) %collective-permute-start.28) | collective-permute-done | bytes 36896 | tf_op jit(solution)/shard_map/ppermute | solution.py:566
  87.2 2.7 %collective-permute-done.27 = f32[72,128]{1,0:T(8,128)S(1)} collective-permute-done((f32[72,128]{1,0:T(8,128)S(1)}, f32[72,128]{1,0:T(8,128)S(1)}, u32[]{:S(2)}, u32[]{:S(2)}) %collective-permute-start.27) | collective-permute-done | bytes 36896 | tf_op jit(solution)/shard_map/ppermute | solution.py:566
  90.0 1.8 %collective-permute-done.19 = f32[8,32,128]{2,1,0:T(8,128)S(1)} collective-permute-done((f32[8,32,128]{2,1,0:T(8,128)S(1)}, f32[8,32,128]{2,1,0:T(8,128)S(1)}, u32[]{:S(2)}, u32[]{:S(2)}) %collective-permute-start.19) | collective-permute-done | bytes 131104 | tf_op jit(solution)/shard_map/ppermute | solution.py:566
  91.8 3.1 %all-to-all-start.2 = ((f32[32,4,640]{2,1,0:T(4,128)}), f32[32,4,640]{2,1,0:T(4,128)S(1)}, u32[]{:S(2)}, u32[]{:S(2)}) async-start(f32[32,4,640]{2,1,0:T(4,128)} %bitcast.6), calls=%async_computation.2 | async-start | bytes 655360 | tf_op jit(solution)/shard_map/all_to_all | solution.py:631
  95.0 1.8 %collective-permute-start.30 = (f32[16,32,128]{2,1,0:T(8,128)S(1)}, f32[16,32,128]{2,1,0:T(8,128)S(1)}, u32[]{:S(2)}, u32[]{:S(2)}) collective-permute-start(f32[16,32,128]{2,1,0:T(8,128)S(1)} %pad_maximum_fusion.3), channel_id=1, source_target_pairs={{0,4},{1,5},{2,6},{3,7},{4,0},{5,1},{6,2},{7,3},{8,12},{9,13},{10,... | collective-permute-start | bytes 786440 | tf_op jit(solution)/shard_map/ppermute | solution.py:566
  96.8 1.5 %collective-permute-start.31 = (f32[16,32,128]{2,1,0:T(8,128)S(1)}, f32[16,32,128]{2,1,0:T(8,128)S(1)}, u32[]{:S(2)}, u32[]{:S(2)}) collective-permute-start(f32[16,32,128]{2,1,0:T(8,128)S(1)} %pad_maximum_fusion.4), channel_id=1, source_target_pairs={{0,8},{1,9},{2,10},{3,11},{4,12},{5,13},{6,14},{7,15},{8,0},{9,1},... | collective-permute-start | bytes 786440 | tf_op jit(solution)/shard_map/ppermute | solution.py:566
  98.3 6.4 %shard_map.54 = (f32[128,128]{1,0:T(8,128)S(1)}, f32[128,128]{1,0:T(8,128)S(1)}, s32[1]{0:T(128)}) custom-call(f32[72,128]{1,0:T(8,128)S(1)} %add_add_fusion.gram_ref, f32[72,128]{1,0:T(8,128)S(1)} %collective-permute-done.29.other_ref), custom_call_target="tpu_custom_call" | custom-call | flops 12000000000 | tf_op jit(solution)/shard_map/pallas_call | solution.py:548
  105.6 5.0 %shard_map.55.both_ref = f32[128,128]{1,0:T(8,128)S(1)} custom-call(f32[128,128]{1,0:T(8,128)S(1)} %get-tuple-element.66.gram_ref, f32[128,128]{1,0:T(8,128)S(1)} %get-tuple-element.52.inverse_ref), custom_call_target="tpu_custom_call" | custom-call | tf_op jit(solution)/shard_map/pallas_call | solution.py:548
  110.8 3.8 %shard_map.56 = (f32[32,512]{1,0:T(8,128)}, f32[256,128]{1,0:T(8,128)}) custom-call(f32[128,640]{1,0:T(8,128)S(1)} %reshape.50.images_ref, f32[128,128]{1,0:T(8,128)S(1)} %shard_map.55.both_ref, f32[32,512]{1,0:T(8,128)S(1)} %copy-done, s32[32,512]{1,0:T(8,128)S(1)} %copy-done.1, f32[512,128]{1,0:T(8,128)S(1)} %bitcast.14, f32[512,128]{1,0:T(8,128)S(1)} %bitcast.17, ...), custom_call_target="tpu_custom_call" | custom-call | flops 5000000000 | tf_op jit(solution)/shard_map/pallas_call | solution.py:548
  (44 shorter events, 1.5 us)
Async XLA Ops:
  2.5 8.0 %collective-permute-start.5 = (f32[1,32,512]{2,1,0:T(8,128)}, f32[1,32,512]{2,1,0:T(8,128)S(1)}, u32[]{:S(2)}, u32[]{:S(2)}) collective-permute-start(f32[1,32,512]{2,1,0:T(8,128)} %bitcast.19), channel_id=1, source_target_pairs={{0,16},{1,17},{2,18},{3,19},{4,20},{5,21},{6,22},{7,23},{8,24},{9,... | collective-permute-start | bytes 196616 | tf_op jit(solution)/shard_map/ppermute | solution.py:566
  11.3 5.0 %collective-permute-start.6 = (f32[2,32,512]{2,1,0:T(8,128)S(1)}, f32[2,32,512]{2,1,0:T(8,128)S(1)}, u32[]{:S(2)}, u32[]{:S(2)}) collective-permute-start(f32[2,32,512]{2,1,0:T(8,128)S(1)} %pad_maximum_fusion.5), channel_id=1, source_target_pairs={{0,8},{1,9},{2,10},{3,11},{4,12},{5,13},{6,14},{7,15},{8,0},{9,1},... | collective-permute-start | bytes 393224 | tf_op jit(solution)/shard_map/ppermute | solution.py:566
  17.3 5.0 %collective-permute-start.11 = (f32[4,16,512]{2,1,0:T(8,128)S(1)}, f32[4,16,512]{2,1,0:T(8,128)S(1)}, u32[]{:S(2)}, u32[]{:S(2)}) collective-permute-start(f32[4,16,512]{2,1,0:T(8,128)S(1)} %get-tuple-element.58), channel_id=1, source_target_pairs={{0,2},{1,3},{2,0},{3,1},{4,6},{5,7},{6,4},{7,5},{8,10},{9,11},{10,... | collective-permute-start | bytes 393224 | tf_op jit(solution)/shard_map/ppermute | solution.py:566
  19.1 6.3 %collective-permute-start.7 = (f32[4,16,512]{2,1,0:T(8,128)S(1)}, f32[4,16,512]{2,1,0:T(8,128)S(1)}, u32[]{:S(2)}, u32[]{:S(2)}) collective-permute-start(f32[4,16,512]{2,1,0:T(8,128)S(1)} %get-tuple-element.59), channel_id=1, source_target_pairs={{0,4},{1,5},{2,6},{3,7},{4,0},{5,1},{6,2},{7,3},{8,12},{9,13},{10,... | collective-permute-start | bytes 393224 | tf_op jit(solution)/shard_map/ppermute | solution.py:566
  22.3 17.3 %collective-permute-start.12 = (f32[8,16,512]{2,1,0:T(8,128)S(1)}, f32[8,16,512]{2,1,0:T(8,128)S(1)}, u32[]{:S(2)}, u32[]{:S(2)}) collective-permute-start(f32[8,16,512]{2,1,0:T(8,128)S(1)} %pad_maximum_fusion.2.refs_4_), channel_id=1, source_target_pairs={{0,4},{1,5},{2,6},{3,7},{4,0},{5,1},{6,2},{7,3},{8,12},{9,13},{10,... | collective-permute-start | bytes 786440 | tf_op jit(solution)/shard_map/ppermute | solution.py:566
  25.4 14.2 %collective-permute-start.8 = (f32[8,16,512]{2,1,0:T(8,128)S(1)}, f32[8,16,512]{2,1,0:T(8,128)S(1)}, u32[]{:S(2)}, u32[]{:S(2)}) collective-permute-start(f32[8,16,512]{2,1,0:T(8,128)S(1)} %pad_maximum_fusion.1.refs_0_), channel_id=1, source_target_pairs={{0,2},{1,3},{2,0},{3,1},{4,6},{5,7},{6,4},{7,5},{8,10},{9,11},{10,... | collective-permute-start | bytes 786440 | tf_op jit(solution)/shard_map/ppermute | solution.py:566
  26.8 12.8 %all-to-all-start = ((f32[32,8,128]{2,1,0:T(8,128)}), f32[32,8,128]{2,1,0:T(8,128)S(1)}, u32[]{:S(2)}, u32[]{:S(2)}) async-start(f32[32,8,128]{2,1,0:T(8,128)} %bitcast.1), calls=%async_computation | async-start | bytes 262144 | tf_op jit(solution)/shard_map/all_to_all | solution.py:631
  31.4 8.8 %collective-permute-start.9 = (f32[8,16,512]{2,1,0:T(8,128)S(1)}, f32[8,16,512]{2,1,0:T(8,128)S(1)}, u32[]{:S(2)}, u32[]{:S(2)}) collective-permute-start(f32[8,16,512]{2,1,0:T(8,128)S(1)} %pad_maximum_fusion.1.refs_0_), channel_id=1, source_target_pairs={{0,1},{1,0},{2,3},{3,2},{4,5},{5,4},{6,7},{7,6},{8,9},{9,8},{10,11... | collective-permute-start | bytes 786440 | tf_op jit(solution)/shard_map/ppermute | solution.py:566
  31.7 8.4 %collective-permute-start.13 = (f32[8,16,512]{2,1,0:T(8,128)S(1)}, f32[8,16,512]{2,1,0:T(8,128)S(1)}, u32[]{:S(2)}, u32[]{:S(2)}) collective-permute-start(f32[8,16,512]{2,1,0:T(8,128)S(1)} %pad_maximum_fusion.2.refs_4_), channel_id=1, source_target_pairs={{0,1},{1,0},{2,3},{3,2},{4,5},{5,4},{6,7},{7,6},{8,9},{9,8},{10,11... | collective-permute-start | bytes 786440 | tf_op jit(solution)/shard_map/ppermute | solution.py:566
  39.6 1.5 %collective-permute-start.10 = (f32[8,16,512]{2,1,0:T(8,128)S(1)}, f32[8,16,512]{2,1,0:T(8,128)S(1)}, u32[]{:S(2)}, u32[]{:S(2)}) collective-permute-start(f32[8,16,512]{2,1,0:T(8,128)S(1)} %collective-permute-done.8.refs_1_), channel_id=1, source_target_pairs={{0,1},{1,0},{2,3},{3,2},{4,5},{5,4},{6,7},{7,6},{8,9},{9,8},{10,11... | collective-permute-start | bytes 786440 | tf_op jit(solution)/shard_map/ppermute | solution.py:566
  39.8 1.7 %collective-permute-start.14 = (f32[8,16,512]{2,1,0:T(8,128)S(1)}, f32[8,16,512]{2,1,0:T(8,128)S(1)}, u32[]{:S(2)}, u32[]{:S(2)}) collective-permute-start(f32[8,16,512]{2,1,0:T(8,128)S(1)} %collective-permute-done.12.refs_5_), channel_id=1, source_target_pairs={{0,1},{1,0},{2,3},{3,2},{4,5},{5,4},{6,7},{7,6},{8,9},{9,8},{10,11... | collective-permute-start | bytes 786440 | tf_op jit(solution)/shard_map/ppermute | solution.py:566
  57.2 1.3 %copy-start.2 = (bf16[8,2,4,32,512]{4,3,2,1,0:T(8,128)(2,1)}, bf16[8,2,4,32,512]{4,3,2,1,0:T(8,128)(2,1)S(1)}, u32[]{:S(2)}) copy-start(bf16[8,2,4,32,512]{4,3,2,1,0:T(8,128)(2,1)S(1)} %get-tuple-element.40.samples_ref) | copy-start | bytes 6291460
  58.6 13.2 %all-to-all-start.1 = ((f32[32,16,128]{2,1,0:T(8,128)}), f32[32,16,128]{2,1,0:T(8,128)S(1)}, u32[]{:S(2)}, u32[]{:S(2)}) async-start(f32[32,16,128]{2,1,0:T(8,128)} %bitcast.4), calls=%async_computation.1 | async-start | bytes 524288 | tf_op jit(solution)/shard_map/all_to_all | solution.py:631
  61.4 6.3 %collective-permute-start.17 = (f32[1,64,128]{2,1,0:T(8,128)S(1)}, f32[1,64,128]{2,1,0:T(8,128)S(1)}, u32[]{:S(2)}, u32[]{:S(2)}) collective-permute-start(f32[1,64,128]{2,1,0:T(8,128)S(1)} %get-tuple-element.63), channel_id=1, source_target_pairs={{0,3},{1,2},{2,1},{3,0},{4,7},{5,6},{6,5},{7,4},{8,11},{9,10},{10,... | collective-permute-start | bytes 98312 | tf_op jit(solution)/shard_map/ppermute | solution.py:566
  62.7 5.0 %collective-permute-start.16 = (f32[1,64,128]{2,1,0:T(8,128)S(1)}, f32[1,64,128]{2,1,0:T(8,128)S(1)}, u32[]{:S(2)}, u32[]{:S(2)}) collective-permute-start(f32[1,64,128]{2,1,0:T(8,128)S(1)} %get-tuple-element.64), channel_id=1, source_target_pairs={{0,2},{1,3},{2,0},{3,1},{4,6},{5,7},{6,4},{7,5},{8,10},{9,11},{10,... | collective-permute-start | bytes 98312 | tf_op jit(solution)/shard_map/ppermute | solution.py:566
  63.0 4.6 %collective-permute-start.15 = (f32[1,64,128]{2,1,0:T(8,128)S(1)}, f32[1,64,128]{2,1,0:T(8,128)S(1)}, u32[]{:S(2)}, u32[]{:S(2)}) collective-permute-start(f32[1,64,128]{2,1,0:T(8,128)S(1)} %get-tuple-element.65), channel_id=1, source_target_pairs={{0,1},{1,0},{2,3},{3,2},{4,5},{5,4},{6,7},{7,6},{8,9},{9,8},{10,11... | collective-permute-start | bytes 98312 | tf_op jit(solution)/shard_map/ppermute | solution.py:566
  63.3 1.6 %copy-start.3 = (bf16[8,2,4,32,512]{4,3,2,1,0:T(8,128)(2,1)S(1)}, bf16[8,2,4,32,512]{4,3,2,1,0:T(8,128)(2,1)}, u32[]{:S(2)}) copy-start(bf16[8,2,4,32,512]{4,3,2,1,0:T(8,128)(2,1)} %copy-done.2) | copy-start | bytes 6291460
  71.8 6.4 %collective-permute-start.20 = (f32[4,32,128]{2,1,0:T(8,128)S(1)}, f32[4,32,128]{2,1,0:T(8,128)S(1)}, u32[]{:S(2)}, u32[]{:S(2)}) collective-permute-start(f32[4,32,128]{2,1,0:T(8,128)S(1)} %get-tuple-element.60), channel_id=1, source_target_pairs={{0,4},{1,5},{2,6},{3,7},{4,0},{5,1},{6,2},{7,3},{8,12},{9,13},{10,... | collective-permute-start | bytes 196616 | tf_op jit(solution)/shard_map/ppermute | solution.py:566
  73.3 1.3 %collective-permute-start.22 = (f32[72,128]{1,0:T(8,128)S(1)}, f32[72,128]{1,0:T(8,128)S(1)}, u32[]{:S(2)}, u32[]{:S(2)}) collective-permute-start(f32[72,128]{1,0:T(8,128)S(1)} %get-tuple-element.46), channel_id=1, source_target_pairs={{0,1},{1,0},{2,3},{3,2},{4,5},{5,4},{6,7},{7,6},{8,9},{9,8},{10,11... | collective-permute-start | bytes 110600 | tf_op jit(solution)/shard_map/ppermute | solution.py:566
  73.4 11.9 %collective-permute-start.18 = (f32[4,32,128]{2,1,0:T(8,128)S(1)}, f32[4,32,128]{2,1,0:T(8,128)S(1)}, u32[]{:S(2)}, u32[]{:S(2)}) collective-permute-start(f32[4,32,128]{2,1,0:T(8,128)S(1)} %get-tuple-element.61), channel_id=1, source_target_pairs={{0,16},{1,17},{2,18},{3,19},{4,20},{5,21},{6,22},{7,23},{8,24},{9,... | collective-permute-start | bytes 196616 | tf_op jit(solution)/shard_map/ppermute | solution.py:566
  74.6 5.4 %collective-permute-start.25 = (f32[72,128]{1,0:T(8,128)S(1)}, f32[72,128]{1,0:T(8,128)S(1)}, u32[]{:S(2)}, u32[]{:S(2)}) collective-permute-start(f32[72,128]{1,0:T(8,128)S(1)} %add.36), channel_id=1, source_target_pairs={{0,6},{1,7},{2,4},{3,5},{4,2},{5,3},{6,0},{7,1},{8,14},{9,15},{10,... | collective-permute-start | bytes 110600 | tf_op jit(solution)/shard_map/ppermute | solution.py:566
  75.5 4.6 %collective-permute-start.24 = (f32[72,128]{1,0:T(8,128)S(1)}, f32[72,128]{1,0:T(8,128)S(1)}, u32[]{:S(2)}, u32[]{:S(2)}) collective-permute-start(f32[72,128]{1,0:T(8,128)S(1)} %add.36), channel_id=1, source_target_pairs={{0,4},{1,5},{2,6},{3,7},{4,0},{5,1},{6,2},{7,3},{8,12},{9,13},{10,... | collective-permute-start | bytes 110600 | tf_op jit(solution)/shard_map/ppermute | solution.py:566
  76.9 4.0 %collective-permute-start.23 = (f32[72,128]{1,0:T(8,128)S(1)}, f32[72,128]{1,0:T(8,128)S(1)}, u32[]{:S(2)}, u32[]{:S(2)}) collective-permute-start(f32[72,128]{1,0:T(8,128)S(1)} %add.36), channel_id=1, source_target_pairs={{0,2},{1,3},{2,0},{3,1},{4,6},{5,7},{6,4},{7,5},{8,10},{9,11},{10,... | collective-permute-start | bytes 110600 | tf_op jit(solution)/shard_map/ppermute | solution.py:566
  78.1 11.8 %collective-permute-start.21 = (f32[8,32,128]{2,1,0:T(8,128)S(1)}, f32[8,32,128]{2,1,0:T(8,128)S(1)}, u32[]{:S(2)}, u32[]{:S(2)}) collective-permute-start(f32[8,32,128]{2,1,0:T(8,128)S(1)} %pad_maximum_fusion.8), channel_id=1, source_target_pairs={{0,16},{1,17},{2,18},{3,19},{4,20},{5,21},{6,22},{7,23},{8,24},{9,... | collective-permute-start | bytes 393224 | tf_op jit(solution)/shard_map/ppermute | solution.py:566
  80.9 6.3 %collective-permute-start.28 = (f32[72,128]{1,0:T(8,128)S(1)}, f32[72,128]{1,0:T(8,128)S(1)}, u32[]{:S(2)}, u32[]{:S(2)}) collective-permute-start(f32[72,128]{1,0:T(8,128)S(1)} %add_add_fusion.1), channel_id=1, source_target_pairs={{0,24},{1,25},{2,26},{3,27},{4,28},{5,29},{6,30},{7,31},{8,16},{9,... | collective-permute-start | bytes 110600 | tf_op jit(solution)/shard_map/ppermute | solution.py:566
  82.6 7.2 %collective-permute-start.27 = (f32[72,128]{1,0:T(8,128)S(1)}, f32[72,128]{1,0:T(8,128)S(1)}, u32[]{:S(2)}, u32[]{:S(2)}) collective-permute-start(f32[72,128]{1,0:T(8,128)S(1)} %add_add_fusion.1), channel_id=1, source_target_pairs={{0,16},{1,17},{2,18},{3,19},{4,20},{5,21},{6,22},{7,23},{8,24},{9,... | collective-permute-start | bytes 110600 | tf_op jit(solution)/shard_map/ppermute | solution.py:566
  83.3 6.6 %collective-permute-start.26 = (f32[72,128]{1,0:T(8,128)S(1)}, f32[72,128]{1,0:T(8,128)S(1)}, u32[]{:S(2)}, u32[]{:S(2)}) collective-permute-start(f32[72,128]{1,0:T(8,128)S(1)} %add_add_fusion.1), channel_id=1, source_target_pairs={{0,8},{1,9},{2,10},{3,11},{4,12},{5,13},{6,14},{7,15},{8,0},{9,1},... | collective-permute-start | bytes 110600 | tf_op jit(solution)/shard_map/ppermute | solution.py:566
  85.4 6.4 %collective-permute-start.19 = (f32[8,32,128]{2,1,0:T(8,128)S(1)}, f32[8,32,128]{2,1,0:T(8,128)S(1)}, u32[]{:S(2)}, u32[]{:S(2)}) collective-permute-start(f32[8,32,128]{2,1,0:T(8,128)S(1)} %pad_maximum_fusion.7), channel_id=1, source_target_pairs={{0,8},{1,9},{2,10},{3,11},{4,12},{5,13},{6,14},{7,15},{8,0},{9,1},... | collective-permute-start | bytes 393224 | tf_op jit(solution)/shard_map/ppermute | solution.py:566
  89.9 2.0 %collective-permute-start.29 = (f32[72,128]{1,0:T(8,128)S(1)}, f32[72,128]{1,0:T(8,128)S(1)}, u32[]{:S(2)}, u32[]{:S(2)}) collective-permute-start(f32[72,128]{1,0:T(8,128)S(1)} %add_add_fusion.gram_ref), channel_id=1, source_target_pairs={{0,1},{1,0},{2,3},{3,2},{4,5},{5,4},{6,7},{7,6},{8,9},{9,8},{10,11... | collective-permute-start | bytes 110600 | tf_op jit(solution)/shard_map/ppermute | solution.py:566
  91.8 18.8 %all-to-all-start.2 = ((f32[32,4,640]{2,1,0:T(4,128)}), f32[32,4,640]{2,1,0:T(4,128)S(1)}, u32[]{:S(2)}, u32[]{:S(2)}) async-start(f32[32,4,640]{2,1,0:T(4,128)} %bitcast.6), calls=%async_computation.2 | async-start | bytes 655360 | tf_op jit(solution)/shard_map/all_to_all | solution.py:631
  95.0 15.8 %collective-permute-start.30 = (f32[16,32,128]{2,1,0:T(8,128)S(1)}, f32[16,32,128]{2,1,0:T(8,128)S(1)}, u32[]{:S(2)}, u32[]{:S(2)}) collective-permute-start(f32[16,32,128]{2,1,0:T(8,128)S(1)} %pad_maximum_fusion.3), channel_id=1, source_target_pairs={{0,4},{1,5},{2,6},{3,7},{4,0},{5,1},{6,2},{7,3},{8,12},{9,13},{10,... | collective-permute-start | bytes 786440 | tf_op jit(solution)/shard_map/ppermute | solution.py:566
  96.8 14.0 %collective-permute-start.31 = (f32[16,32,128]{2,1,0:T(8,128)S(1)}, f32[16,32,128]{2,1,0:T(8,128)S(1)}, u32[]{:S(2)}, u32[]{:S(2)}) collective-permute-start(f32[16,32,128]{2,1,0:T(8,128)S(1)} %pad_maximum_fusion.4), channel_id=1, source_target_pairs={{0,8},{1,9},{2,10},{3,11},{4,12},{5,13},{6,14},{7,15},{8,0},{9,1},... | collective-permute-start | bytes 786440 | tf_op jit(solution)/shard_map/ppermute | solution.py:566
  105.4 5.5 %copy-start = (f32[32,512]{1,0:T(8,128)S(1)}, f32[32,512]{1,0:T(8,128)}, u32[]{:S(2)}) copy-start(f32[32,512]{1,0:T(8,128)} %kspace_hbm.3) | copy-start | bytes 196612
  105.4 5.5 %copy-start.1 = (s32[32,512]{1,0:T(8,128)S(1)}, s32[32,512]{1,0:T(8,128)}, u32[]{:S(2)}) copy-start(s32[32,512]{1,0:T(8,128)} %mask_hbm.3) | copy-start | bytes 196612

commit v13 on v12

--- a/solution.py
+++ b/solution.py
@@ -118,32 +118,7 @@
     return at_row, at_col
 
 
-def prepare_kernel(
-    cols,
-    chg,
-    per_tile,
-    kspace_hbm,
-    mask_hbm,
-    basis_hbm,
-    sampled_ref,
-    send_ref,
-    kspace_ref,
-    mask_ref,
-    basis_ref,
-    sems,
-):
-    fetches = [
-        pltpu.make_async_copy(source, target, sems.at[i])
-        for i, (source, target) in enumerate(
-            [(kspace_hbm, kspace_ref), (mask_hbm, mask_ref), (basis_hbm, basis_ref)]
-        )
-    ]
-    for fetch in fetches:
-        fetch.start()
-    fetches[0].wait()
-    fetches[1].wait()
-    sampled_ref[...] = kspace_ref[...] * mask_ref[...].astype(jnp.float32)
-    fetches[2].wait()
+def prepare_kernel(cols, chg, per_tile, basis_ref, send_ref):
     turned = basis_ref[...].T
     devices = turned.shape[0] // cols
     for j in range(per_tile):
@@ -476,25 +451,16 @@
     order,
     images_ref,
     both_ref,
-    kspace_hbm,
-    mask_hbm,
+    kspace_ref,
+    mask_ref,
     top_near_ref,
     top_far_ref,
     low_near_ref,
     low_far_ref,
     recovered_ref,
     basis_ref,
-    kspace_ref,
-    mask_ref,
     vectors_ref,
-    sems,
 ):
-    fetches = [
-        pltpu.make_async_copy(kspace_hbm, kspace_ref, sems.at[0]),
-        pltpu.make_async_copy(mask_hbm, mask_ref, sems.at[1]),
-    ]
-    for fetch in fetches:
-        fetch.start()
     both = both_ref[...]
     reach = images_ref.shape[1]
     factors = [exact(both, moved) for moved in moved_columns(order, cols)]
@@ -537,21 +503,16 @@
     owned = basis_ref.shape[0]
     start = pl.multiple_of(lax.axis_index("rows") * owned, owned)
     basis_ref[...] = vectors_ref[:, pl.ds(start, owned)].T
-    for fetch in fetches:
-        fetch.wait()
     estimate = estimate / KER
     residual = mask_ref[...].astype(jnp.float32) * (kspace_ref[...] - estimate)
     recovered_ref[...] = estimate + residual - jnp.clip(residual, -threshold, threshold)
 
 
-def call(kernel, outs, *args, scratch=(), far=(), limit=40, scalars=0, micros=1):
+def call(kernel, outs, *args, scratch=(), limit=12, scalars=0, micros=1):
     return pl.pallas_call(
         kernel,
         out_shape=[jax.ShapeDtypeStruct(shape, kind) for shape, kind in outs],
-        in_specs=[
-            pl.BlockSpec(memory_space=pltpu.HBM if i in far else pltpu.VMEM)
-            for i in range(len(args))
-        ],
+        in_specs=[pl.BlockSpec(memory_space=pltpu.VMEM)] * len(args),
         out_specs=[pl.BlockSpec(memory_space=pltpu.VMEM)] * (len(outs) - scalars)
         + [pl.BlockSpec(memory_space=pltpu.SMEM)] * scalars,
         scratch_shapes=list(scratch),
@@ -599,6 +560,8 @@
     while mask > groups:
         near, masks = gather_round(near, masks, [mask], devices, AXES)
         mask //= 2
+    basis = to_all(basis)
+    near = after(near, basis)
     half = near.shape[1] // 2
     halves = []
     for part, ways in (
@@ -606,8 +569,6 @@
         (near[:, half:], (groups // 2, groups)),
     ):
         part, order = gather_round(part, masks, [ways[0]], devices, AXES)
-        if not halves:
-            basis = to_all(after(basis, part))
         pieces = [(part, order)]
         mask = ways[1]
         rest = groups // 4
@@ -617,9 +578,6 @@
                 for part, order in pieces
             ]
             mask, rest = rest, rest // 2
-        if halves:
-            part, order = pieces[-1]
-            pieces[-1] = (after(part, basis), order)
         halves.append(
             pieces
             + [(exchange(part, devices, 1, AXES), [m ^ 1 for m in order]) for part, order in pieces]
@@ -691,20 +649,11 @@
     rows = cols * KER
     lanes = cols * chg
 
-    sampled, basis_send = call(
+    sampled = kspace * sample_mask.astype(f32)
+    (basis_send,) = call(
         functools.partial(prepare_kernel, cols, chg, per_tile),
-        [((chg, tile), f32), ((devices * per_tile, lanes), f32)],
-        kspace,
-        sample_mask,
+        [((devices * per_tile, lanes), f32)],
         start_basis.reshape(owned, rank),
-        scratch=[
-            pltpu.VMEM((chg, tile), f32),
-            pltpu.VMEM((chg, tile), sample_mask.dtype),
-            pltpu.VMEM((owned, rank), f32),
-            pltpu.SemaphoreType.DMA((3,)),
-        ],
-        far=(0, 1, 2),
-        limit=60,
     )
     halves, basis_parts = gather_samples(
         sampled, basis_send.reshape(devices, per_tile, lanes), tiles, groups
@@ -724,6 +673,7 @@
         basis_parts.reshape(tiles, groups, per_tile, lanes),
         *[piece for half in halves for piece, _ in half],
         scratch=[wide, moved],
+        limit=24,
         micros=12,
     )
     received = to_all(send.reshape(devices, 2 * per_tile, lanes))
@@ -734,6 +684,7 @@
         samples,
         normal,
         scratch=[wide],
+        limit=16,
         micros=2,
     )
     near, order = gather_group(group, devices)
@@ -770,14 +721,8 @@
         kspace,
         sample_mask,
         *[piece.reshape(-1, lanes) for piece in pieces],
-        scratch=[
-            pltpu.VMEM((chg, tile), f32),
-            pltpu.VMEM((chg, tile), sample_mask.dtype),
-            pltpu.VMEM((rank, KER * chg), f32),
-            pltpu.SemaphoreType.DMA((2,)),
-        ],
-        far=(2, 3),
-        limit=40,
+        scratch=[pltpu.VMEM((rank, KER * chg), f32)],
+        limit=16,
         micros=5,
     )
     return (recovered, basis.reshape(1, owned, rank))

time: 115 us -> 108 us (0.939)
  starting transfers between devices: 39.5 us -> 37.4 us
  local copies, waits for them, and re-layouts: 3.1 us -> 1.07 us
  Pallas kernels: 36.2 us -> 35 us
  waiting for transfers between devices: 32.2 us -> 31 us
    all_to_all x3, waiting for transfers between devices: 11.7 us -> 4.95 us  [to_all(): return lax.all_to_all(pieces, axes, 0, 0, tiled=True)]
    ppermute x27, waiting for transfers between devices: 20.5 us -> 26 us  [exchange(): return lax.ppermute(block, axes, [(i, i ^ mask) for i in range(devices)])]
    unnamed x8 -> x6, local copies, waits for them, and re-layouts: 2.94 us -> 0.92 us
    concatenate x8, other arithmetic: 1.8 us -> 0.12 us  [gather_round(): jnp.concatenate([part] + [exchange(part, devices, mask, axes) for mask in...]
    ppermute x27, starting transfers between devices: 29 us -> 27.6 us  [exchange(): return lax.ppermute(block, axes, [(i, i ^ mask) for i in range(devices)])]
    pallas_call x7, Pallas kernels: 36.2 us -> 35 us  [call(): pl.pallas_call(kernel, out_shape=[jax.ShapeDtypeStruct(shape, kind) for s...]
  transfers between devices with their start and end apart: 30 -> 30, of which waited for: 13 -> 14; matrix products, arithmetic and copies ran while one was open for 0% -> 0% of each run, Pallas kernels for 13% -> 15%
where the time goes in v13:
time: 108 us; the launch traced here: 107 us
  starting transfers between devices  37.4 us (35%)
  Pallas kernels  35 us (32%)
  waiting for transfers between devices  31 us (29%)
  between operations  1.54 us (1%)
    pallas_call x7, Pallas kernels, call(): pl.pallas_call(kernel, out_shape=[jax.ShapeDtypeStruct(shape, kind) for s...  35 us
    ppermute x27, starting transfers between devices, exchange(): return lax.ppermute(block, axes, [(i, i ^ mask) for i in range(devices)])  27.6 us
    ppermute x27, waiting for transfers between devices, exchange(): return lax.ppermute(block, axes, [(i, i ^ mask) for i in range(devices)])  26 us
    all_to_all x3, starting transfers between devices, to_all(): return lax.all_to_all(pieces, axes, 0, 0, tiled=True)  9.71 us
    all_to_all x3, waiting for transfers between devices, to_all(): return lax.all_to_all(pieces, axes, 0, 0, tiled=True)  4.95 us
  transfers between devices with their start and end apart: 30, of which 14 were waited for; matrix products, arithmetic and copies ran while one was open for 0% of the time, Pallas kernels for 15%

profile of v13, /device:TPU:0, one launch (start us, length us, event | category | flops | bytes accessed | tf_op | source)
XLA Modules:
  0.0 107.2 jit_solution(15643098611679894659)
XLA Ops:
  0.6 0.9 multiply_bitcast_fusion
  1.5 4.1 %collective-permute-start.5 = (f32[1,32,512]{2,1,0:T(8,128)S(1)}, f32[1,32,512]{2,1,0:T(8,128)S(1)}, u32[]{:S(2)}, u32[]{:S(2)}) collective-permute-start(f32[1,32,512]{2,1,0:T(8,128)S(1)} %multiply_bitcast_fusion), channel_id=1, source_target_pairs={{0,16},{1,17},{2,18},{3,19},{4,20},{5,21},{6,22},{7,23},{8,24},{9,... | collective-permute-start | bytes 196616 | tf_op jit(solution)/shard_map/ppermute | solution.py:527
  5.6 0.9 copy-done.2
  6.5 0.9 shard_map.50
  7.4 3.8 %all-to-all-start = ((f32[32,8,128]{2,1,0:T(8,128)}), f32[32,8,128]{2,1,0:T(8,128)S(1)}, u32[]{:S(2)}, u32[]{:S(2)}) async-start(f32[32,8,128]{2,1,0:T(8,128)} %bitcast.1), calls=%async_computation | async-start | bytes 262144 | tf_op jit(solution)/shard_map/all_to_all | solution.py:589
  11.3 1.8 %collective-permute-start.6 = (f32[2,32,512]{2,1,0:T(8,128)S(1)}, f32[2,32,512]{2,1,0:T(8,128)S(1)}, u32[]{:S(2)}, u32[]{:S(2)}) collective-permute-start(f32[2,32,512]{2,1,0:T(8,128)S(1)} %pad_maximum_fusion.5), channel_id=1, source_target_pairs={{0,8},{1,9},{2,10},{3,11},{4,12},{5,13},{6,14},{7,15},{8,0},{9,1},... | collective-permute-start | bytes 393224 | tf_op jit(solution)/shard_map/ppermute | solution.py:527
  13.1 5.9 %collective-permute-done.6 = f32[2,32,512]{2,1,0:T(8,128)S(1)} collective-permute-done((f32[2,32,512]{2,1,0:T(8,128)S(1)}, f32[2,32,512]{2,1,0:T(8,128)S(1)}, u32[]{:S(2)}, u32[]{:S(2)}) %collective-permute-start.6) | collective-permute-done | bytes 131104 | tf_op jit(solution)/shard_map/ppermute | solution.py:527
  19.0 0.5 all-to-all-done
  19.5 1.1 %collective-permute-start.7 = (f32[4,16,512]{2,1,0:T(8,128)S(1)}, f32[4,16,512]{2,1,0:T(8,128)S(1)}, u32[]{:S(2)}, u32[]{:S(2)}) collective-permute-start(f32[4,16,512]{2,1,0:T(8,128)S(1)} %get-tuple-element.53), channel_id=1, source_target_pairs={{0,4},{1,5},{2,6},{3,7},{4,0},{5,1},{6,2},{7,3},{8,12},{9,13},{10,... | collective-permute-start | bytes 393224 | tf_op jit(solution)/shard_map/ppermute | solution.py:527
  20.6 1.5 %collective-permute-start.11 = (f32[4,16,512]{2,1,0:T(8,128)S(1)}, f32[4,16,512]{2,1,0:T(8,128)S(1)}, u32[]{:S(2)}, u32[]{:S(2)}) collective-permute-start(f32[4,16,512]{2,1,0:T(8,128)S(1)} %get-tuple-element.52), channel_id=1, source_target_pairs={{0,2},{1,3},{2,0},{3,1},{4,6},{5,7},{6,4},{7,5},{8,10},{9,11},{10,... | collective-permute-start | bytes 393224 | tf_op jit(solution)/shard_map/ppermute | solution.py:527
  22.1 3.5 %collective-permute-done.7 = f32[4,16,512]{2,1,0:T(8,128)S(1)} collective-permute-done((f32[4,16,512]{2,1,0:T(8,128)S(1)}, f32[4,16,512]{2,1,0:T(8,128)S(1)}, u32[]{:S(2)}, u32[]{:S(2)}) %collective-permute-start.7) | collective-permute-done | bytes 131104 | tf_op jit(solution)/shard_map/ppermute | solution.py:527
  25.6 0.2 collective-permute-start.8
  25.9 1.6 %collective-permute-start.12 = (f32[8,16,512]{2,1,0:T(8,128)S(1)}, f32[8,16,512]{2,1,0:T(8,128)S(1)}, u32[]{:S(2)}, u32[]{:S(2)}) collective-permute-start(f32[8,16,512]{2,1,0:T(8,128)S(1)} %pad_maximum_fusion.2.refs_4_), channel_id=1, source_target_pairs={{0,4},{1,5},{2,6},{3,7},{4,0},{5,1},{6,2},{7,3},{8,12},{9,13},{10,... | collective-permute-start | bytes 786440 | tf_op jit(solution)/shard_map/ppermute | solution.py:527
  27.5 0.5 collective-permute-start.13
  28.0 5.8 %collective-permute-done.8.refs_1_ = f32[8,16,512]{2,1,0:T(8,128)S(1)} collective-permute-done((f32[8,16,512]{2,1,0:T(8,128)S(1)}, f32[8,16,512]{2,1,0:T(8,128)S(1)}, u32[]{:S(2)}, u32[]{:S(2)}) %collective-permute-start.8) | collective-permute-done | bytes 262176 | tf_op jit(solution)/shard_map/ppermute | solution.py:527
  33.9 0.4 collective-permute-start.14
  34.3 1.0 collective-permute-done.10.refs_3_
  35.3 0.4 collective-permute-done.14.refs_7_
  35.7 15.7 %shard_map.51 = (bf16[8,2,4,32,512]{4,3,2,1,0:T(8,128)(2,1)S(1)}, f32[256,128]{1,0:T(8,128)S(1)}, f32[8,4,2,8,128]{4,3,2,1,0:T(8,128)}, f32[4,64,128]{2,1,0:T(8,128)S(1)}) custom-call(f32[8,4,8,128]{3,2,1,0:T(8,128)S(1)} %bitcast.17, f32[8,16,512]{2,1,0:T(8,128)S(1)} %pad_maximum_fusion.1.refs_0_, f32[8,16,512]{2,1,0:T(8,128)S(1)} %collective-permute-done.8.refs_1_, ...), custom_call_target="tpu_custom_call" | custom-call | flops 12000000000 | tf_op jit(solution)/shard_map/pallas_call | solution.py:512
  51.3 2.8 %all-to-all-start.1 = ((f32[32,16,128]{2,1,0:T(8,128)}), f32[32,16,128]{2,1,0:T(8,128)S(1)}, u32[]{:S(2)}, u32[]{:S(2)}) async-start(f32[32,16,128]{2,1,0:T(8,128)} %bitcast.4), calls=%async_computation.1 | async-start | bytes 524288 | tf_op jit(solution)/shard_map/all_to_all | solution.py:589
  54.1 1.3 %collective-permute-start.17 = (f32[1,64,128]{2,1,0:T(8,128)S(1)}, f32[1,64,128]{2,1,0:T(8,128)S(1)}, u32[]{:S(2)}, u32[]{:S(2)}) collective-permute-start(f32[1,64,128]{2,1,0:T(8,128)S(1)} %get-tuple-element.57), channel_id=1, source_target_pairs={{0,3},{1,2},{2,1},{3,0},{4,7},{5,6},{6,5},{7,4},{8,11},{9,10},{10,... | collective-permute-start | bytes 98312 | tf_op jit(solution)/shard_map/ppermute | solution.py:527
  55.4 0.3 collective-permute-start.16
  55.8 0.3 collective-permute-start.15
  56.1 2.8 %shard_map.52 = f32[8,4,4,640]{3,2,1,0:T(4,128)} custom-call(bf16[8,2,4,32,512]{4,3,2,1,0:T(8,128)(2,1)S(1)} %get-tuple-element.34.samples_ref, f32[256,128]{1,0:T(8,128)S(1)} %get-tuple-element.35.vectors_ref), custom_call_target="tpu_custom_call" | custom-call | flops 2000000000 | tf_op jit(solution)/shard_map/pallas_call | solution.py:512
  58.8 1.2 %collective-permute-done.16 = f32[1,64,128]{2,1,0:T(8,128)S(1)} collective-permute-done((f32[1,64,128]{2,1,0:T(8,128)S(1)}, f32[1,64,128]{2,1,0:T(8,128)S(1)}, u32[]{:S(2)}, u32[]{:S(2)}) %collective-permute-start.16) | collective-permute-done | bytes 32800 | tf_op jit(solution)/shard_map/ppermute | solution.py:527
  60.1 4.5 %all-to-all-done.1 = f32[32,16,128]{2,1,0:T(8,128)S(1)} async-done(((f32[32,16,128]{2,1,0:T(8,128)}), f32[32,16,128]{2,1,0:T(8,128)S(1)}, u32[]{:S(2)}, u32[]{:S(2)}) %all-to-all-start.1) | async-done | bytes 262176 | tf_op jit(solution)/shard_map/all_to_all | solution.py:589
  64.5 1.0 collective-permute-start.20
  65.5 0.6 shard_map.53
  66.2 0.2 collective-permute-start.18
  66.4 1.0 collective-permute-done.22
  67.4 0.8 collective-permute-start.25
  68.2 1.5 %collective-permute-start.24 = (f32[72,128]{1,0:T(8,128)S(1)}, f32[72,128]{1,0:T(8,128)S(1)}, u32[]{:S(2)}, u32[]{:S(2)}) collective-permute-start(f32[72,128]{1,0:T(8,128)S(1)} %add.36), channel_id=1, source_target_pairs={{0,4},{1,5},{2,6},{3,7},{4,0},{5,1},{6,2},{7,3},{8,12},{9,13},{10,... | collective-permute-start | bytes 110600 | tf_op jit(solution)/shard_map/ppermute | solution.py:527
  69.7 1.2 %collective-permute-start.23 = (f32[72,128]{1,0:T(8,128)S(1)}, f32[72,128]{1,0:T(8,128)S(1)}, u32[]{:S(2)}, u32[]{:S(2)}) collective-permute-start(f32[72,128]{1,0:T(8,128)S(1)} %add.36), channel_id=1, source_target_pairs={{0,2},{1,3},{2,0},{3,1},{4,6},{5,7},{6,4},{7,5},{8,10},{9,11},{10,... | collective-permute-start | bytes 110600 | tf_op jit(solution)/shard_map/ppermute | solution.py:527
  70.9 1.9 %collective-permute-start.21 = (f32[8,32,128]{2,1,0:T(8,128)S(1)}, f32[8,32,128]{2,1,0:T(8,128)S(1)}, u32[]{:S(2)}, u32[]{:S(2)}) collective-permute-start(f32[8,32,128]{2,1,0:T(8,128)S(1)} %pad_maximum_fusion.8), channel_id=1, source_target_pairs={{0,16},{1,17},{2,18},{3,19},{4,20},{5,21},{6,22},{7,23},{8,24},{9,... | collective-permute-start | bytes 393224 | tf_op jit(solution)/shard_map/ppermute | solution.py:527
  72.9 0.8 collective-permute-done.23
  73.7 1.7 %collective-permute-start.28 = (f32[72,128]{1,0:T(8,128)S(1)}, f32[72,128]{1,0:T(8,128)S(1)}, u32[]{:S(2)}, u32[]{:S(2)}) collective-permute-start(f32[72,128]{1,0:T(8,128)S(1)} %add_add_fusion.1), channel_id=1, source_target_pairs={{0,24},{1,25},{2,26},{3,27},{4,28},{5,29},{6,30},{7,31},{8,16},{9,... | collective-permute-start | bytes 110600 | tf_op jit(solution)/shard_map/ppermute | solution.py:527
  75.4 0.6 collective-permute-start.27
  76.0 2.1 %collective-permute-start.26 = (f32[72,128]{1,0:T(8,128)S(1)}, f32[72,128]{1,0:T(8,128)S(1)}, u32[]{:S(2)}, u32[]{:S(2)}) collective-permute-start(f32[72,128]{1,0:T(8,128)S(1)} %add_add_fusion.1), channel_id=1, source_target_pairs={{0,8},{1,9},{2,10},{3,11},{4,12},{5,13},{6,14},{7,15},{8,0},{9,1},... | collective-permute-start | bytes 110600 | tf_op jit(solution)/shard_map/ppermute | solution.py:527
  78.2 1.7 %collective-permute-done.28 = f32[72,128]{1,0:T(8,128)S(1)} collective-permute-done((f32[72,128]{1,0:T(8,128)S(1)}, f32[72,128]{1,0:T(8,128)S(1)}, u32[]{:S(2)}, u32[]{:S(2)}) %collective-permute-start.28) | collective-permute-done | bytes 36896 | tf_op jit(solution)/shard_map/ppermute | solution.py:527
  80.0 2.7 %collective-permute-done.27 = f32[72,128]{1,0:T(8,128)S(1)} collective-permute-done((f32[72,128]{1,0:T(8,128)S(1)}, f32[72,128]{1,0:T(8,128)S(1)}, u32[]{:S(2)}, u32[]{:S(2)}) %collective-permute-start.27) | collective-permute-done | bytes 36896 | tf_op jit(solution)/shard_map/ppermute | solution.py:527
  82.8 1.8 %collective-permute-done.19 = f32[8,32,128]{2,1,0:T(8,128)S(1)} collective-permute-done((f32[8,32,128]{2,1,0:T(8,128)S(1)}, f32[8,32,128]{2,1,0:T(8,128)S(1)}, u32[]{:S(2)}, u32[]{:S(2)}) %collective-permute-start.19) | collective-permute-done | bytes 131104 | tf_op jit(solution)/shard_map/ppermute | solution.py:527
  84.6 3.1 %all-to-all-start.2 = ((f32[32,4,640]{2,1,0:T(4,128)}), f32[32,4,640]{2,1,0:T(4,128)S(1)}, u32[]{:S(2)}, u32[]{:S(2)}) async-start(f32[32,4,640]{2,1,0:T(4,128)} %bitcast.6), calls=%async_computation.2 | async-start | bytes 655360 | tf_op jit(solution)/shard_map/all_to_all | solution.py:589
  87.8 1.8 %collective-permute-start.30 = (f32[16,32,128]{2,1,0:T(8,128)S(1)}, f32[16,32,128]{2,1,0:T(8,128)S(1)}, u32[]{:S(2)}, u32[]{:S(2)}) collective-permute-start(f32[16,32,128]{2,1,0:T(8,128)S(1)} %pad_maximum_fusion.3), channel_id=1, source_target_pairs={{0,4},{1,5},{2,6},{3,7},{4,0},{5,1},{6,2},{7,3},{8,12},{9,13},{10,... | collective-permute-start | bytes 786440 | tf_op jit(solution)/shard_map/ppermute | solution.py:527
  89.6 1.5 %collective-permute-start.31 = (f32[16,32,128]{2,1,0:T(8,128)S(1)}, f32[16,32,128]{2,1,0:T(8,128)S(1)}, u32[]{:S(2)}, u32[]{:S(2)}) collective-permute-start(f32[16,32,128]{2,1,0:T(8,128)S(1)} %pad_maximum_fusion.4), channel_id=1, source_target_pairs={{0,8},{1,9},{2,10},{3,11},{4,12},{5,13},{6,14},{7,15},{8,0},{9,1},... | collective-permute-start | bytes 786440 | tf_op jit(solution)/shard_map/ppermute | solution.py:527
  91.1 6.4 %shard_map.54 = (f32[128,128]{1,0:T(8,128)S(1)}, f32[128,128]{1,0:T(8,128)S(1)}, s32[1]{0:T(128)}) custom-call(f32[72,128]{1,0:T(8,128)S(1)} %add_add_fusion.gram_ref, f32[72,128]{1,0:T(8,128)S(1)} %collective-permute-done.29.other_ref), custom_call_target="tpu_custom_call" | custom-call | flops 12000000000 | tf_op jit(solution)/shard_map/pallas_call | solution.py:512
  98.2 0.2 conditional.1
  98.4 5.0 %shard_map.55.both_ref = f32[128,128]{1,0:T(8,128)S(1)} custom-call(f32[128,128]{1,0:T(8,128)S(1)} %get-tuple-element.60.gram_ref, f32[128,128]{1,0:T(8,128)S(1)} %get-tuple-element.46.inverse_ref), custom_call_target="tpu_custom_call" | custom-call | tf_op jit(solution)/shard_map/pallas_call | solution.py:512
  103.6 3.6 %shard_map.56 = (f32[32,512]{1,0:T(8,128)}, f32[256,128]{1,0:T(8,128)}) custom-call(f32[128,640]{1,0:T(8,128)S(1)} %reshape.50.images_ref, f32[128,128]{1,0:T(8,128)S(1)} %shard_map.55.both_ref, f32[32,512]{1,0:T(8,128)S(1)} %copy-done, s32[32,512]{1,0:T(8,128)S(1)} %copy-done.1, f32[512,128]{1,0:T(8,128)S(1)} %bitcast.15, f32[512,128]{1,0:T(8,128)S(1)} %bitcast.18, ...), custom_call_target="tpu_custom_call" | custom-call | flops 5000000000 | tf_op jit(solution)/shard_map/pallas_call | solution.py:512
  (43 shorter events, 0.7 us)
Async XLA Ops:
  1.5 9.7 %collective-permute-start.5 = (f32[1,32,512]{2,1,0:T(8,128)S(1)}, f32[1,32,512]{2,1,0:T(8,128)S(1)}, u32[]{:S(2)}, u32[]{:S(2)}) collective-permute-start(f32[1,32,512]{2,1,0:T(8,128)S(1)} %multiply_bitcast_fusion), channel_id=1, source_target_pairs={{0,16},{1,17},{2,18},{3,19},{4,20},{5,21},{6,22},{7,23},{8,24},{9,... | collective-permute-start | bytes 196616 | tf_op jit(solution)/shard_map/ppermute | solution.py:527
  5.6 0.9 copy-start.2
  7.4 12.1 %all-to-all-start = ((f32[32,8,128]{2,1,0:T(8,128)}), f32[32,8,128]{2,1,0:T(8,128)S(1)}, u32[]{:S(2)}, u32[]{:S(2)}) async-start(f32[32,8,128]{2,1,0:T(8,128)} %bitcast.1), calls=%async_computation | async-start | bytes 262144 | tf_op jit(solution)/shard_map/all_to_all | solution.py:589
  11.3 7.7 %collective-permute-start.6 = (f32[2,32,512]{2,1,0:T(8,128)S(1)}, f32[2,32,512]{2,1,0:T(8,128)S(1)}, u32[]{:S(2)}, u32[]{:S(2)}) collective-permute-start(f32[2,32,512]{2,1,0:T(8,128)S(1)} %pad_maximum_fusion.5), channel_id=1, source_target_pairs={{0,8},{1,9},{2,10},{3,11},{4,12},{5,13},{6,14},{7,15},{8,0},{9,1},... | collective-permute-start | bytes 393224 | tf_op jit(solution)/shard_map/ppermute | solution.py:527
  19.5 6.1 %collective-permute-start.7 = (f32[4,16,512]{2,1,0:T(8,128)S(1)}, f32[4,16,512]{2,1,0:T(8,128)S(1)}, u32[]{:S(2)}, u32[]{:S(2)}) collective-permute-start(f32[4,16,512]{2,1,0:T(8,128)S(1)} %get-tuple-element.53), channel_id=1, source_target_pairs={{0,4},{1,5},{2,6},{3,7},{4,0},{5,1},{6,2},{7,3},{8,12},{9,13},{10,... | collective-permute-start | bytes 393224 | tf_op jit(solution)/shard_map/ppermute | solution.py:527
  20.6 5.2 %collective-permute-start.11 = (f32[4,16,512]{2,1,0:T(8,128)S(1)}, f32[4,16,512]{2,1,0:T(8,128)S(1)}, u32[]{:S(2)}, u32[]{:S(2)}) collective-permute-start(f32[4,16,512]{2,1,0:T(8,128)S(1)} %get-tuple-element.52), channel_id=1, source_target_pairs={{0,2},{1,3},{2,0},{3,1},{4,6},{5,7},{6,4},{7,5},{8,10},{9,11},{10,... | collective-permute-start | bytes 393224 | tf_op jit(solution)/shard_map/ppermute | solution.py:527
  25.6 8.1 %collective-permute-start.8 = (f32[8,16,512]{2,1,0:T(8,128)S(1)}, f32[8,16,512]{2,1,0:T(8,128)S(1)}, u32[]{:S(2)}, u32[]{:S(2)}) collective-permute-start(f32[8,16,512]{2,1,0:T(8,128)S(1)} %pad_maximum_fusion.1.refs_0_), channel_id=1, source_target_pairs={{0,2},{1,3},{2,0},{3,1},{4,6},{5,7},{6,4},{7,5},{8,10},{9,11},{10,... | collective-permute-start | bytes 786440 | tf_op jit(solution)/shard_map/ppermute | solution.py:527
  25.9 8.0 %collective-permute-start.12 = (f32[8,16,512]{2,1,0:T(8,128)S(1)}, f32[8,16,512]{2,1,0:T(8,128)S(1)}, u32[]{:S(2)}, u32[]{:S(2)}) collective-permute-start(f32[8,16,512]{2,1,0:T(8,128)S(1)} %pad_maximum_fusion.2.refs_4_), channel_id=1, source_target_pairs={{0,4},{1,5},{2,6},{3,7},{4,0},{5,1},{6,2},{7,3},{8,12},{9,13},{10,... | collective-permute-start | bytes 786440 | tf_op jit(solution)/shard_map/ppermute | solution.py:527
  27.4 6.8 %collective-permute-start.9 = (f32[8,16,512]{2,1,0:T(8,128)S(1)}, f32[8,16,512]{2,1,0:T(8,128)S(1)}, u32[]{:S(2)}, u32[]{:S(2)}) collective-permute-start(f32[8,16,512]{2,1,0:T(8,128)S(1)} %pad_maximum_fusion.1.refs_0_), channel_id=1, source_target_pairs={{0,1},{1,0},{2,3},{3,2},{4,5},{5,4},{6,7},{7,6},{8,9},{9,8},{10,11... | collective-permute-start | bytes 786440 | tf_op jit(solution)/shard_map/ppermute | solution.py:527
  27.5 6.8 %collective-permute-start.13 = (f32[8,16,512]{2,1,0:T(8,128)S(1)}, f32[8,16,512]{2,1,0:T(8,128)S(1)}, u32[]{:S(2)}, u32[]{:S(2)}) collective-permute-start(f32[8,16,512]{2,1,0:T(8,128)S(1)} %pad_maximum_fusion.2.refs_4_), channel_id=1, source_target_pairs={{0,1},{1,0},{2,3},{3,2},{4,5},{5,4},{6,7},{7,6},{8,9},{9,8},{10,11... | collective-permute-start | bytes 786440 | tf_op jit(solution)/shard_map/ppermute | solution.py:527
  33.8 1.5 %collective-permute-start.10 = (f32[8,16,512]{2,1,0:T(8,128)S(1)}, f32[8,16,512]{2,1,0:T(8,128)S(1)}, u32[]{:S(2)}, u32[]{:S(2)}) collective-permute-start(f32[8,16,512]{2,1,0:T(8,128)S(1)} %collective-permute-done.8.refs_1_), channel_id=1, source_target_pairs={{0,1},{1,0},{2,3},{3,2},{4,5},{5,4},{6,7},{7,6},{8,9},{9,8},{10,11... | collective-permute-start | bytes 786440 | tf_op jit(solution)/shard_map/ppermute | solution.py:527
  33.9 1.8 %collective-permute-start.14 = (f32[8,16,512]{2,1,0:T(8,128)S(1)}, f32[8,16,512]{2,1,0:T(8,128)S(1)}, u32[]{:S(2)}, u32[]{:S(2)}) collective-permute-start(f32[8,16,512]{2,1,0:T(8,128)S(1)} %collective-permute-done.12.refs_5_), channel_id=1, source_target_pairs={{0,1},{1,0},{2,3},{3,2},{4,5},{5,4},{6,7},{7,6},{8,9},{9,8},{10,11... | collective-permute-start | bytes 786440 | tf_op jit(solution)/shard_map/ppermute | solution.py:527
  51.3 13.2 %all-to-all-start.1 = ((f32[32,16,128]{2,1,0:T(8,128)}), f32[32,16,128]{2,1,0:T(8,128)S(1)}, u32[]{:S(2)}, u32[]{:S(2)}) async-start(f32[32,16,128]{2,1,0:T(8,128)} %bitcast.4), calls=%async_computation.1 | async-start | bytes 524288 | tf_op jit(solution)/shard_map/all_to_all | solution.py:589
  54.1 4.7 %collective-permute-start.17 = (f32[1,64,128]{2,1,0:T(8,128)S(1)}, f32[1,64,128]{2,1,0:T(8,128)S(1)}, u32[]{:S(2)}, u32[]{:S(2)}) collective-permute-start(f32[1,64,128]{2,1,0:T(8,128)S(1)} %get-tuple-element.57), channel_id=1, source_target_pairs={{0,3},{1,2},{2,1},{3,0},{4,7},{5,6},{6,5},{7,4},{8,11},{9,10},{10,... | collective-permute-start | bytes 98312 | tf_op jit(solution)/shard_map/ppermute | solution.py:527
  55.4 4.6 %collective-permute-start.16 = (f32[1,64,128]{2,1,0:T(8,128)S(1)}, f32[1,64,128]{2,1,0:T(8,128)S(1)}, u32[]{:S(2)}, u32[]{:S(2)}) collective-permute-start(f32[1,64,128]{2,1,0:T(8,128)S(1)} %get-tuple-element.58), channel_id=1, source_target_pairs={{0,2},{1,3},{2,0},{3,1},{4,6},{5,7},{6,4},{7,5},{8,10},{9,11},{10,... | collective-permute-start | bytes 98312 | tf_op jit(solution)/shard_map/ppermute | solution.py:527
  55.8 4.3 %collective-permute-start.15 = (f32[1,64,128]{2,1,0:T(8,128)S(1)}, f32[1,64,128]{2,1,0:T(8,128)S(1)}, u32[]{:S(2)}, u32[]{:S(2)}) collective-permute-start(f32[1,64,128]{2,1,0:T(8,128)S(1)} %get-tuple-element.59), channel_id=1, source_target_pairs={{0,1},{1,0},{2,3},{3,2},{4,5},{5,4},{6,7},{7,6},{8,9},{9,8},{10,11... | collective-permute-start | bytes 98312 | tf_op jit(solution)/shard_map/ppermute | solution.py:527
  64.5 6.4 %collective-permute-start.20 = (f32[4,32,128]{2,1,0:T(8,128)S(1)}, f32[4,32,128]{2,1,0:T(8,128)S(1)}, u32[]{:S(2)}, u32[]{:S(2)}) collective-permute-start(f32[4,32,128]{2,1,0:T(8,128)S(1)} %get-tuple-element.54), channel_id=1, source_target_pairs={{0,4},{1,5},{2,6},{3,7},{4,0},{5,1},{6,2},{7,3},{8,12},{9,13},{10,... | collective-permute-start | bytes 196616 | tf_op jit(solution)/shard_map/ppermute | solution.py:527
  66.1 1.3 %collective-permute-start.22 = (f32[72,128]{1,0:T(8,128)S(1)}, f32[72,128]{1,0:T(8,128)S(1)}, u32[]{:S(2)}, u32[]{:S(2)}) collective-permute-start(f32[72,128]{1,0:T(8,128)S(1)} %get-tuple-element.40), channel_id=1, source_target_pairs={{0,1},{1,0},{2,3},{3,2},{4,5},{5,4},{6,7},{7,6},{8,9},{9,8},{10,11... | collective-permute-start | bytes 110600 | tf_op jit(solution)/shard_map/ppermute | solution.py:527
  66.2 11.9 %collective-permute-start.18 = (f32[4,32,128]{2,1,0:T(8,128)S(1)}, f32[4,32,128]{2,1,0:T(8,128)S(1)}, u32[]{:S(2)}, u32[]{:S(2)}) collective-permute-start(f32[4,32,128]{2,1,0:T(8,128)S(1)} %get-tuple-element.55), channel_id=1, source_target_pairs={{0,16},{1,17},{2,18},{3,19},{4,20},{5,21},{6,22},{7,23},{8,24},{9,... | collective-permute-start | bytes 196616 | tf_op jit(solution)/shard_map/ppermute | solution.py:527
  67.4 5.4 %collective-permute-start.25 = (f32[72,128]{1,0:T(8,128)S(1)}, f32[72,128]{1,0:T(8,128)S(1)}, u32[]{:S(2)}, u32[]{:S(2)}) collective-permute-start(f32[72,128]{1,0:T(8,128)S(1)} %add.36), channel_id=1, source_target_pairs={{0,6},{1,7},{2,4},{3,5},{4,2},{5,3},{6,0},{7,1},{8,14},{9,15},{10,... | collective-permute-start | bytes 110600 | tf_op jit(solution)/shard_map/ppermute | solution.py:527
  68.2 4.6 %collective-permute-start.24 = (f32[72,128]{1,0:T(8,128)S(1)}, f32[72,128]{1,0:T(8,128)S(1)}, u32[]{:S(2)}, u32[]{:S(2)}) collective-permute-start(f32[72,128]{1,0:T(8,128)S(1)} %add.36), channel_id=1, source_target_pairs={{0,4},{1,5},{2,6},{3,7},{4,0},{5,1},{6,2},{7,3},{8,12},{9,13},{10,... | collective-permute-start | bytes 110600 | tf_op jit(solution)/shard_map/ppermute | solution.py:527
  69.7 4.0 %collective-permute-start.23 = (f32[72,128]{1,0:T(8,128)S(1)}, f32[72,128]{1,0:T(8,128)S(1)}, u32[]{:S(2)}, u32[]{:S(2)}) collective-permute-start(f32[72,128]{1,0:T(8,128)S(1)} %add.36), channel_id=1, source_target_pairs={{0,2},{1,3},{2,0},{3,1},{4,6},{5,7},{6,4},{7,5},{8,10},{9,11},{10,... | collective-permute-start | bytes 110600 | tf_op jit(solution)/shard_map/ppermute | solution.py:527
  70.9 11.8 %collective-permute-start.21 = (f32[8,32,128]{2,1,0:T(8,128)S(1)}, f32[8,32,128]{2,1,0:T(8,128)S(1)}, u32[]{:S(2)}, u32[]{:S(2)}) collective-permute-start(f32[8,32,128]{2,1,0:T(8,128)S(1)} %pad_maximum_fusion.8), channel_id=1, source_target_pairs={{0,16},{1,17},{2,18},{3,19},{4,20},{5,21},{6,22},{7,23},{8,24},{9,... | collective-permute-start | bytes 393224 | tf_op jit(solution)/shard_map/ppermute | solution.py:527
  73.7 6.3 %collective-permute-start.28 = (f32[72,128]{1,0:T(8,128)S(1)}, f32[72,128]{1,0:T(8,128)S(1)}, u32[]{:S(2)}, u32[]{:S(2)}) collective-permute-start(f32[72,128]{1,0:T(8,128)S(1)} %add_add_fusion.1), channel_id=1, source_target_pairs={{0,24},{1,25},{2,26},{3,27},{4,28},{5,29},{6,30},{7,31},{8,16},{9,... | collective-permute-start | bytes 110600 | tf_op jit(solution)/shard_map/ppermute | solution.py:527
  75.4 7.2 %collective-permute-start.27 = (f32[72,128]{1,0:T(8,128)S(1)}, f32[72,128]{1,0:T(8,128)S(1)}, u32[]{:S(2)}, u32[]{:S(2)}) collective-permute-start(f32[72,128]{1,0:T(8,128)S(1)} %add_add_fusion.1), channel_id=1, source_target_pairs={{0,16},{1,17},{2,18},{3,19},{4,20},{5,21},{6,22},{7,23},{8,24},{9,... | collective-permute-start | bytes 110600 | tf_op jit(solution)/shard_map/ppermute | solution.py:527
  76.0 6.6 %collective-permute-start.26 = (f32[72,128]{1,0:T(8,128)S(1)}, f32[72,128]{1,0:T(8,128)S(1)}, u32[]{:S(2)}, u32[]{:S(2)}) collective-permute-start(f32[72,128]{1,0:T(8,128)S(1)} %add_add_fusion.1), channel_id=1, source_target_pairs={{0,8},{1,9},{2,10},{3,11},{4,12},{5,13},{6,14},{7,15},{8,0},{9,1},... | collective-permute-start | bytes 110600 | tf_op jit(solution)/shard_map/ppermute | solution.py:527
  78.2 6.4 %collective-permute-start.19 = (f32[8,32,128]{2,1,0:T(8,128)S(1)}, f32[8,32,128]{2,1,0:T(8,128)S(1)}, u32[]{:S(2)}, u32[]{:S(2)}) collective-permute-start(f32[8,32,128]{2,1,0:T(8,128)S(1)} %pad_maximum_fusion.7), channel_id=1, source_target_pairs={{0,8},{1,9},{2,10},{3,11},{4,12},{5,13},{6,14},{7,15},{8,0},{9,1},... | collective-permute-start | bytes 393224 | tf_op jit(solution)/shard_map/ppermute | solution.py:527
  82.7 2.0 %collective-permute-start.29 = (f32[72,128]{1,0:T(8,128)S(1)}, f32[72,128]{1,0:T(8,128)S(1)}, u32[]{:S(2)}, u32[]{:S(2)}) collective-permute-start(f32[72,128]{1,0:T(8,128)S(1)} %add_add_fusion.gram_ref), channel_id=1, source_target_pairs={{0,1},{1,0},{2,3},{3,2},{4,5},{5,4},{6,7},{7,6},{8,9},{9,8},{10,11... | collective-permute-start | bytes 110600 | tf_op jit(solution)/shard_map/ppermute | solution.py:527
  84.6 18.8 %all-to-all-start.2 = ((f32[32,4,640]{2,1,0:T(4,128)}), f32[32,4,640]{2,1,0:T(4,128)S(1)}, u32[]{:S(2)}, u32[]{:S(2)}) async-start(f32[32,4,640]{2,1,0:T(4,128)} %bitcast.6), calls=%async_computation.2 | async-start | bytes 655360 | tf_op jit(solution)/shard_map/all_to_all | solution.py:589
  87.8 15.8 %collective-permute-start.30 = (f32[16,32,128]{2,1,0:T(8,128)S(1)}, f32[16,32,128]{2,1,0:T(8,128)S(1)}, u32[]{:S(2)}, u32[]{:S(2)}) collective-permute-start(f32[16,32,128]{2,1,0:T(8,128)S(1)} %pad_maximum_fusion.3), channel_id=1, source_target_pairs={{0,4},{1,5},{2,6},{3,7},{4,0},{5,1},{6,2},{7,3},{8,12},{9,13},{10,... | collective-permute-start | bytes 786440 | tf_op jit(solution)/shard_map/ppermute | solution.py:527
  89.6 14.0 %collective-permute-start.31 = (f32[16,32,128]{2,1,0:T(8,128)S(1)}, f32[16,32,128]{2,1,0:T(8,128)S(1)}, u32[]{:S(2)}, u32[]{:S(2)}) collective-permute-start(f32[16,32,128]{2,1,0:T(8,128)S(1)} %pad_maximum_fusion.4), channel_id=1, source_target_pairs={{0,8},{1,9},{2,10},{3,11},{4,12},{5,13},{6,14},{7,15},{8,0},{9,1},... | collective-permute-start | bytes 786440 | tf_op jit(solution)/shard_map/ppermute | solution.py:527
  98.1 5.5 %copy-start = (f32[32,512]{1,0:T(8,128)S(1)}, f32[32,512]{1,0:T(8,128)}, u32[]{:S(2)}) copy-start(f32[32,512]{1,0:T(8,128)} %kspace_ref.1) | copy-start | bytes 196612
  98.1 5.5 %copy-start.1 = (s32[32,512]{1,0:T(8,128)S(1)}, s32[32,512]{1,0:T(8,128)}, u32[]{:S(2)}) copy-start(s32[32,512]{1,0:T(8,128)} %mask_ref.1) | copy-start | bytes 196612

commit v14 on v13

--- a/solution.py
+++ b/solution.py
@@ -138,15 +138,12 @@
     ).astype(jnp.bfloat16)
     both = dot(flip, jnp.concatenate([high, low], axis=1)).astype(jnp.bfloat16)
     high, low = both[:, :channels], both[:, channels:]
-    zero = jnp.zeros_like(low)
-    both = jnp.concatenate(
-        [jnp.concatenate([high, high], axis=1), jnp.concatenate([low, zero], axis=1)], axis=0
-    )
+    twice = jnp.concatenate([high, high], axis=1)
     tiles = samples_ref.shape[0]
     tile = samples_ref.shape[-1]
     for t in range(tiles):
-        wide = dot(both, samples_ref[t].reshape(2 * channels, tile))
-        wide_ref[:, t * tile : (t + 1) * tile] = wide[:rows] + wide[rows:]
+        block = samples_ref[t].reshape(2 * channels, tile)
+        wide_ref[:, t * tile : (t + 1) * tile] = dot(twice, block) + dot(low, block[:channels])
     images = []
     for k in range(cols):
         total = None
@@ -183,15 +180,15 @@
     )
 
 
-def store_by_rows(normal, send_ref, part):
-    tiles, groups, _, per_tile, lanes = send_ref.shape
+def store_by_rows(normal, send_ref):
+    tiles, groups, per_tile, lanes = send_ref.shape
     cols = normal.shape[0] // KER
     chg = normal.shape[1] // groups
     for g in range(groups):
         joined = jnp.concatenate(
             [normal[k * KER : (k + 1) * KER, g * chg : (g + 1) * chg] for k in range(cols)], axis=1
         )
-        send_ref[:, g, part] = joined.reshape(tiles, per_tile, lanes)
+        send_ref[:, g] = joined.reshape(tiles, per_tile, lanes)
 
 
 def store_by_groups(normal_ref, group_ref):
@@ -240,15 +237,14 @@
         )
     vectors = jnp.concatenate(rows, axis=0)
     normal = normal_of(images_of(vectors, samples_ref, wide_ref), samples_ref, moved_ref)
-    scaled = []
-    for k in range(cols):
-        part = normal[k * KER : (k + 1) * KER]
-        scaled.append(part * (1.0 / jnp.max(jnp.abs(part))))
-    normal = jnp.concatenate(scaled, axis=0)
-    store_by_rows(normal, send_ref, 0)
+    power = jnp.zeros((1, tile), jnp.float32)
+    for t in range(samples_ref.shape[0]):
+        value = samples_ref[t, 0].reshape(groups * chg, tile).astype(jnp.float32)
+        power = power + jnp.sum(value * value, axis=0, keepdims=True)
+    normal = normal * (groups * chg / jnp.sum(power))
     normal = normal_of(images_of(normal, samples_ref, wide_ref), samples_ref, moved_ref)
     normal_ref[...] = normal
-    store_by_rows(normal, send_ref, 1)
+    store_by_rows(normal, send_ref)
     store_by_groups(normal_ref, group_ref)
 
 
@@ -268,14 +264,11 @@
             send_ref[t, g] = part
 
 
-def gather_turned(received_ref, cols, per_tile, part):
+def gather_turned(received_ref, cols, per_tile):
     count, lanes = received_ref.shape
-    devices = count // (2 * per_tile)
+    devices = count // per_tile
     chg = lanes // cols
-    loaded = [
-        received_ref[pl.ds(part * per_tile + j, devices, stride=2 * per_tile), :]
-        for j in range(per_tile)
-    ]
+    loaded = [received_ref[pl.ds(j, devices, stride=per_tile), :] for j in range(per_tile)]
     return jnp.concatenate(
         [
             jnp.concatenate(
@@ -293,10 +286,9 @@
     )
 
 
-def gram_kernel(cols, per_tile, received_ref, kept_ref, given_ref, turned_ref):
-    turned = gather_turned(received_ref, cols, per_tile, 0)
-    first = exact(turned, turned, ((1,), (1,)))
-    turned = gather_turned(received_ref, cols, per_tile, 1)
+def gram_kernel(cols, per_tile, received_ref, basis_ref, kept_ref, given_ref, turned_ref):
+    turned = gather_turned(received_ref, cols, per_tile)
+    first = exact(basis_ref[...], turned, ((0,), (1,)))
     second = exact(turned, turned, ((1,), (1,)))
     turned_ref[...] = turned
     at_row, at_col = square(first.shape[0])
@@ -667,7 +659,7 @@
         [
             ((tiles, 2, groups, chg, tile), bf16),
             ((rows, channels), f32),
-            ((tiles, groups, 2, per_tile, lanes), f32),
+            ((tiles, groups, per_tile, lanes), f32),
             ((groups, rows * chg // lanes, lanes), f32),
         ],
         basis_parts.reshape(tiles, groups, per_tile, lanes),
@@ -676,7 +668,7 @@
         limit=24,
         micros=12,
     )
-    received = to_all(send.reshape(devices, 2 * per_tile, lanes))
+    received = to_all(send.reshape(devices, per_tile, lanes))
     reach = tile + LANES
     (images,) = call(
         images_kernel,
@@ -693,7 +685,8 @@
     kept, given, turned = call(
         functools.partial(gram_kernel, cols, per_tile),
         [half, half, ((rank, owned), f32)],
-        received.reshape(devices * 2 * per_tile, lanes),
+        received.reshape(devices * per_tile, lanes),
+        start_basis.reshape(owned, rank),
     )
     gram, pieces, order, images = total_beside(
         kept, given, near, order, images.reshape(devices, cols, reach), groups, devices

time: 108 us -> 101 us (0.935)
  waiting for transfers between devices: 31 us -> 27.4 us
  Pallas kernels: 35 us -> 31.5 us
    pallas_call x7, Pallas kernels: 35 us -> 31.5 us  [call(): pl.pallas_call(kernel, out_shape=[jax.ShapeDtypeStruct(shape, kind) for s...]
    all_to_all x3, waiting for transfers between devices: 4.95 us -> 3.07 us  [to_all(): return lax.all_to_all(pieces, axes, 0, 0, tiled=True)]
    ppermute x27, waiting for transfers between devices: 26 us -> 24.3 us  [exchange(): return lax.ppermute(block, axes, [(i, i ^ mask) for i in range(devices)])]
  transfers between devices with their start and end apart: 30 -> 30, of which waited for: 14 -> 14; matrix products, arithmetic and copies ran while one was open for 0% -> 0% of each run, Pallas kernels for 15% -> 16%
where the time goes in v14:
time: 101 us
  starting transfers between devices  38.2 us (38%)
  Pallas kernels  31.5 us (31%)
  waiting for transfers between devices  27.4 us (27%)
  between operations  1.53 us (2%)
  local copies, waits for them, and re-layouts  1.07 us (1%)
  other arithmetic  1.05 us (1%)
    pallas_call x7, Pallas kernels, call(): pl.pallas_call(kernel, out_shape=[jax.ShapeDtypeStruct(shape, kind) for s...  31.5 us
    ppermute x27, starting transfers between devices, exchange(): return lax.ppermute(block, axes, [(i, i ^ mask) for i in range(devices)])  28.6 us
    ppermute x27, waiting for transfers between devices, exchange(): return lax.ppermute(block, axes, [(i, i ^ mask) for i in range(devices)])  24.3 us
    all_to_all x3, starting transfers between devices, to_all(): return lax.all_to_all(pieces, axes, 0, 0, tiled=True)  9.68 us
    all_to_all x3, waiting for transfers between devices, to_all(): return lax.all_to_all(pieces, axes, 0, 0, tiled=True)  3.07 us
  transfers between devices with their start and end apart: 30, of which 14 were waited for; matrix products, arithmetic and copies ran while one was open for 0% of the time, Pallas kernels for 16%

profile of v14, /device:TPU:0, one launch (start us, length us, event | category | flops | bytes accessed | tf_op | source)
XLA Modules:
  0.0 101.1 jit_solution(16543500670377186469)
XLA Ops:
  0.6 0.9 multiply_bitcast_fusion
  1.5 4.1 %collective-permute-start.5 = (f32[1,32,512]{2,1,0:T(8,128)S(1)}, f32[1,32,512]{2,1,0:T(8,128)S(1)}, u32[]{:S(2)}, u32[]{:S(2)}) collective-permute-start(f32[1,32,512]{2,1,0:T(8,128)S(1)} %multiply_bitcast_fusion), channel_id=1, source_target_pairs={{0,16},{1,17},{2,18},{3,19},{4,20},{5,21},{6,22},{7,23},{8,24},{9,... | collective-permute-start | bytes 196616 | tf_op jit(solution)/shard_map/ppermute | solution.py:519
  5.6 0.9 copy-done.2
  6.5 0.9 shard_map.50
  7.4 3.8 %all-to-all-start = ((f32[32,8,128]{2,1,0:T(8,128)}), f32[32,8,128]{2,1,0:T(8,128)S(1)}, u32[]{:S(2)}, u32[]{:S(2)}) async-start(f32[32,8,128]{2,1,0:T(8,128)} %bitcast.1), calls=%async_computation | async-start | bytes 262144 | tf_op jit(solution)/shard_map/all_to_all | solution.py:581
  11.3 1.8 %collective-permute-start.6 = (f32[2,32,512]{2,1,0:T(8,128)S(1)}, f32[2,32,512]{2,1,0:T(8,128)S(1)}, u32[]{:S(2)}, u32[]{:S(2)}) collective-permute-start(f32[2,32,512]{2,1,0:T(8,128)S(1)} %pad_maximum_fusion.5), channel_id=1, source_target_pairs={{0,8},{1,9},{2,10},{3,11},{4,12},{5,13},{6,14},{7,15},{8,0},{9,1},... | collective-permute-start | bytes 393224 | tf_op jit(solution)/shard_map/ppermute | solution.py:519
  13.1 5.9 %collective-permute-done.6 = f32[2,32,512]{2,1,0:T(8,128)S(1)} collective-permute-done((f32[2,32,512]{2,1,0:T(8,128)S(1)}, f32[2,32,512]{2,1,0:T(8,128)S(1)}, u32[]{:S(2)}, u32[]{:S(2)}) %collective-permute-start.6) | collective-permute-done | bytes 131104 | tf_op jit(solution)/shard_map/ppermute | solution.py:519
  19.0 0.5 all-to-all-done
  19.5 1.1 %collective-permute-start.7 = (f32[4,16,512]{2,1,0:T(8,128)S(1)}, f32[4,16,512]{2,1,0:T(8,128)S(1)}, u32[]{:S(2)}, u32[]{:S(2)}) collective-permute-start(f32[4,16,512]{2,1,0:T(8,128)S(1)} %get-tuple-element.53), channel_id=1, source_target_pairs={{0,4},{1,5},{2,6},{3,7},{4,0},{5,1},{6,2},{7,3},{8,12},{9,13},{10,... | collective-permute-start | bytes 393224 | tf_op jit(solution)/shard_map/ppermute | solution.py:519
  20.6 1.5 %collective-permute-start.11 = (f32[4,16,512]{2,1,0:T(8,128)S(1)}, f32[4,16,512]{2,1,0:T(8,128)S(1)}, u32[]{:S(2)}, u32[]{:S(2)}) collective-permute-start(f32[4,16,512]{2,1,0:T(8,128)S(1)} %get-tuple-element.52), channel_id=1, source_target_pairs={{0,2},{1,3},{2,0},{3,1},{4,6},{5,7},{6,4},{7,5},{8,10},{9,11},{10,... | collective-permute-start | bytes 393224 | tf_op jit(solution)/shard_map/ppermute | solution.py:519
  22.1 3.5 %collective-permute-done.7 = f32[4,16,512]{2,1,0:T(8,128)S(1)} collective-permute-done((f32[4,16,512]{2,1,0:T(8,128)S(1)}, f32[4,16,512]{2,1,0:T(8,128)S(1)}, u32[]{:S(2)}, u32[]{:S(2)}) %collective-permute-start.7) | collective-permute-done | bytes 131104 | tf_op jit(solution)/shard_map/ppermute | solution.py:519
  25.9 1.6 %collective-permute-start.12 = (f32[8,16,512]{2,1,0:T(8,128)S(1)}, f32[8,16,512]{2,1,0:T(8,128)S(1)}, u32[]{:S(2)}, u32[]{:S(2)}) collective-permute-start(f32[8,16,512]{2,1,0:T(8,128)S(1)} %pad_maximum_fusion.2.refs_4_), channel_id=1, source_target_pairs={{0,4},{1,5},{2,6},{3,7},{4,0},{5,1},{6,2},{7,3},{8,12},{9,13},{10,... | collective-permute-start | bytes 786440 | tf_op jit(solution)/shard_map/ppermute | solution.py:519
  27.5 0.5 collective-permute-start.13
  28.0 5.8 %collective-permute-done.8.refs_1_ = f32[8,16,512]{2,1,0:T(8,128)S(1)} collective-permute-done((f32[8,16,512]{2,1,0:T(8,128)S(1)}, f32[8,16,512]{2,1,0:T(8,128)S(1)}, u32[]{:S(2)}, u32[]{:S(2)}) %collective-permute-start.8) | collective-permute-done | bytes 262176 | tf_op jit(solution)/shard_map/ppermute | solution.py:519
  33.9 0.4 collective-permute-start.14
  34.3 1.0 %collective-permute-done.10.refs_3_ = f32[8,16,512]{2,1,0:T(8,128)S(1)} collective-permute-done((f32[8,16,512]{2,1,0:T(8,128)S(1)}, f32[8,16,512]{2,1,0:T(8,128)S(1)}, u32[]{:S(2)}, u32[]{:S(2)}) %collective-permute-start.10) | collective-permute-done | bytes 262176 | tf_op jit(solution)/shard_map/ppermute | solution.py:519
  35.3 0.4 collective-permute-done.14.refs_7_
  35.7 12.3 %shard_map.51 = (bf16[8,2,4,32,512]{4,3,2,1,0:T(8,128)(2,1)S(1)}, f32[256,128]{1,0:T(8,128)S(1)}, f32[8,4,8,128]{3,2,1,0:T(8,128)}, f32[4,64,128]{2,1,0:T(8,128)S(1)}) custom-call(f32[8,4,8,128]{3,2,1,0:T(8,128)S(1)} %bitcast.16, f32[8,16,512]{2,1,0:T(8,128)S(1)} %pad_maximum_fusion.1.refs_0_, f32[8,16,512]{2,1,0:T(8,128)S(1)} %collective-permute-done.8.refs_1_, ...), custom_call_target="tpu_custom_call" | custom-call | flops 12000000000 | tf_op jit(solution)/shard_map/pallas_call | solution.py:504
  48.0 2.8 %all-to-all-start.1 = ((f32[32,8,128]{2,1,0:T(8,128)}), f32[32,8,128]{2,1,0:T(8,128)S(1)}, u32[]{:S(2)}, u32[]{:S(2)}) async-start(f32[32,8,128]{2,1,0:T(8,128)} %bitcast.4), calls=%async_computation.1 | async-start | bytes 262144 | tf_op jit(solution)/shard_map/all_to_all | solution.py:581
  50.7 1.3 %collective-permute-start.17 = (f32[1,64,128]{2,1,0:T(8,128)S(1)}, f32[1,64,128]{2,1,0:T(8,128)S(1)}, u32[]{:S(2)}, u32[]{:S(2)}) collective-permute-start(f32[1,64,128]{2,1,0:T(8,128)S(1)} %get-tuple-element.57), channel_id=1, source_target_pairs={{0,3},{1,2},{2,1},{3,0},{4,7},{5,6},{6,5},{7,4},{8,11},{9,10},{10,... | collective-permute-start | bytes 98312 | tf_op jit(solution)/shard_map/ppermute | solution.py:519
  52.0 0.3 collective-permute-start.16
  52.4 0.3 collective-permute-start.15
  52.7 2.8 %shard_map.52 = f32[8,4,4,640]{3,2,1,0:T(4,128)} custom-call(bf16[8,2,4,32,512]{4,3,2,1,0:T(8,128)(2,1)S(1)} %get-tuple-element.34.samples_ref, f32[256,128]{1,0:T(8,128)S(1)} %get-tuple-element.35.vectors_ref), custom_call_target="tpu_custom_call" | custom-call | flops 2000000000 | tf_op jit(solution)/shard_map/pallas_call | solution.py:504
  55.5 0.6 collective-permute-done.16
  56.2 2.6 %all-to-all-done.1 = f32[32,8,128]{2,1,0:T(8,128)S(1)} async-done(((f32[32,8,128]{2,1,0:T(8,128)}), f32[32,8,128]{2,1,0:T(8,128)S(1)}, u32[]{:S(2)}, u32[]{:S(2)}) %all-to-all-start.1) | async-done | bytes 131104 | tf_op jit(solution)/shard_map/all_to_all | solution.py:581
  58.8 0.7 collective-permute-start.20
  59.5 0.5 shard_map.53
  60.1 0.9 collective-permute-start.18
  61.0 0.3 collective-permute-done.22
  61.3 1.2 %collective-permute-start.25 = (f32[72,128]{1,0:T(8,128)S(1)}, f32[72,128]{1,0:T(8,128)S(1)}, u32[]{:S(2)}, u32[]{:S(2)}) collective-permute-start(f32[72,128]{1,0:T(8,128)S(1)} %add.36), channel_id=1, source_target_pairs={{0,6},{1,7},{2,4},{3,5},{4,2},{5,3},{6,0},{7,1},{8,14},{9,15},{10,... | collective-permute-start | bytes 110600 | tf_op jit(solution)/shard_map/ppermute | solution.py:519
  62.6 1.0 collective-permute-start.24
  63.6 1.3 %collective-permute-start.23 = (f32[72,128]{1,0:T(8,128)S(1)}, f32[72,128]{1,0:T(8,128)S(1)}, u32[]{:S(2)}, u32[]{:S(2)}) collective-permute-start(f32[72,128]{1,0:T(8,128)S(1)} %add.36), channel_id=1, source_target_pairs={{0,2},{1,3},{2,0},{3,1},{4,6},{5,7},{6,4},{7,5},{8,10},{9,11},{10,... | collective-permute-start | bytes 110600 | tf_op jit(solution)/shard_map/ppermute | solution.py:519
  64.8 1.9 %collective-permute-start.21 = (f32[8,32,128]{2,1,0:T(8,128)S(1)}, f32[8,32,128]{2,1,0:T(8,128)S(1)}, u32[]{:S(2)}, u32[]{:S(2)}) collective-permute-start(f32[8,32,128]{2,1,0:T(8,128)S(1)} %pad_maximum_fusion.8), channel_id=1, source_target_pairs={{0,16},{1,17},{2,18},{3,19},{4,20},{5,21},{6,22},{7,23},{8,24},{9,... | collective-permute-start | bytes 393224 | tf_op jit(solution)/shard_map/ppermute | solution.py:519
  66.8 0.7 collective-permute-done.23
  67.5 2.1 %collective-permute-start.28 = (f32[72,128]{1,0:T(8,128)S(1)}, f32[72,128]{1,0:T(8,128)S(1)}, u32[]{:S(2)}, u32[]{:S(2)}) collective-permute-start(f32[72,128]{1,0:T(8,128)S(1)} %add_add_fusion.1), channel_id=1, source_target_pairs={{0,24},{1,25},{2,26},{3,27},{4,28},{5,29},{6,30},{7,31},{8,16},{9,... | collective-permute-start | bytes 110600 | tf_op jit(solution)/shard_map/ppermute | solution.py:519
  69.6 0.8 collective-permute-start.27
  70.4 1.6 %collective-permute-start.26 = (f32[72,128]{1,0:T(8,128)S(1)}, f32[72,128]{1,0:T(8,128)S(1)}, u32[]{:S(2)}, u32[]{:S(2)}) collective-permute-start(f32[72,128]{1,0:T(8,128)S(1)} %add_add_fusion.1), channel_id=1, source_target_pairs={{0,8},{1,9},{2,10},{3,11},{4,12},{5,13},{6,14},{7,15},{8,0},{9,1},... | collective-permute-start | bytes 110600 | tf_op jit(solution)/shard_map/ppermute | solution.py:519
  72.0 0.5 collective-permute-start.19
  72.5 1.1 %collective-permute-done.28 = f32[72,128]{1,0:T(8,128)S(1)} collective-permute-done((f32[72,128]{1,0:T(8,128)S(1)}, f32[72,128]{1,0:T(8,128)S(1)}, u32[]{:S(2)}, u32[]{:S(2)}) %collective-permute-start.28) | collective-permute-done | bytes 36896 | tf_op jit(solution)/shard_map/ppermute | solution.py:519
  73.6 2.9 %collective-permute-done.27 = f32[72,128]{1,0:T(8,128)S(1)} collective-permute-done((f32[72,128]{1,0:T(8,128)S(1)}, f32[72,128]{1,0:T(8,128)S(1)}, u32[]{:S(2)}, u32[]{:S(2)}) %collective-permute-start.27) | collective-permute-done | bytes 36896 | tf_op jit(solution)/shard_map/ppermute | solution.py:519
  76.7 1.8 %collective-permute-done.19 = f32[8,32,128]{2,1,0:T(8,128)S(1)} collective-permute-done((f32[8,32,128]{2,1,0:T(8,128)S(1)}, f32[8,32,128]{2,1,0:T(8,128)S(1)}, u32[]{:S(2)}, u32[]{:S(2)}) %collective-permute-start.19) | collective-permute-done | bytes 131104 | tf_op jit(solution)/shard_map/ppermute | solution.py:519
  78.6 3.1 %all-to-all-start.2 = ((f32[32,4,640]{2,1,0:T(4,128)}), f32[32,4,640]{2,1,0:T(4,128)S(1)}, u32[]{:S(2)}, u32[]{:S(2)}) async-start(f32[32,4,640]{2,1,0:T(4,128)} %bitcast.6), calls=%async_computation.2 | async-start | bytes 655360 | tf_op jit(solution)/shard_map/all_to_all | solution.py:581
  81.7 1.8 %collective-permute-start.30 = (f32[16,32,128]{2,1,0:T(8,128)S(1)}, f32[16,32,128]{2,1,0:T(8,128)S(1)}, u32[]{:S(2)}, u32[]{:S(2)}) collective-permute-start(f32[16,32,128]{2,1,0:T(8,128)S(1)} %pad_maximum_fusion.3), channel_id=1, source_target_pairs={{0,4},{1,5},{2,6},{3,7},{4,0},{5,1},{6,2},{7,3},{8,12},{9,13},{10,... | collective-permute-start | bytes 786440 | tf_op jit(solution)/shard_map/ppermute | solution.py:519
  83.5 1.5 %collective-permute-start.31 = (f32[16,32,128]{2,1,0:T(8,128)S(1)}, f32[16,32,128]{2,1,0:T(8,128)S(1)}, u32[]{:S(2)}, u32[]{:S(2)}) collective-permute-start(f32[16,32,128]{2,1,0:T(8,128)S(1)} %pad_maximum_fusion.4), channel_id=1, source_target_pairs={{0,8},{1,9},{2,10},{3,11},{4,12},{5,13},{6,14},{7,15},{8,0},{9,1},... | collective-permute-start | bytes 786440 | tf_op jit(solution)/shard_map/ppermute | solution.py:519
  85.0 6.4 %shard_map.54 = (f32[128,128]{1,0:T(8,128)S(1)}, f32[128,128]{1,0:T(8,128)S(1)}, s32[1]{0:T(128)}) custom-call(f32[72,128]{1,0:T(8,128)S(1)} %add_add_fusion.gram_ref, f32[72,128]{1,0:T(8,128)S(1)} %collective-permute-done.29.other_ref), custom_call_target="tpu_custom_call" | custom-call | flops 12000000000 | tf_op jit(solution)/shard_map/pallas_call | solution.py:504
  92.1 0.2 conditional.1
  92.3 5.0 %shard_map.55.both_ref = f32[128,128]{1,0:T(8,128)S(1)} custom-call(f32[128,128]{1,0:T(8,128)S(1)} %get-tuple-element.60.gram_ref, f32[128,128]{1,0:T(8,128)S(1)} %get-tuple-element.46.inverse_ref), custom_call_target="tpu_custom_call" | custom-call | tf_op jit(solution)/shard_map/pallas_call | solution.py:504
  97.5 3.6 %shard_map.56 = (f32[32,512]{1,0:T(8,128)}, f32[256,128]{1,0:T(8,128)}) custom-call(f32[128,640]{1,0:T(8,128)S(1)} %reshape.51.images_ref, f32[128,128]{1,0:T(8,128)S(1)} %shard_map.55.both_ref, f32[32,512]{1,0:T(8,128)S(1)} %copy-done, s32[32,512]{1,0:T(8,128)S(1)} %copy-done.1, f32[512,128]{1,0:T(8,128)S(1)} %bitcast.15, f32[512,128]{1,0:T(8,128)S(1)} %bitcast.18, ...), custom_call_target="tpu_custom_call" | custom-call | flops 5000000000 | tf_op jit(solution)/shard_map/pallas_call | solution.py:504
  (45 shorter events, 0.8 us)
Async XLA Ops:
  1.5 9.7 %collective-permute-start.5 = (f32[1,32,512]{2,1,0:T(8,128)S(1)}, f32[1,32,512]{2,1,0:T(8,128)S(1)}, u32[]{:S(2)}, u32[]{:S(2)}) collective-permute-start(f32[1,32,512]{2,1,0:T(8,128)S(1)} %multiply_bitcast_fusion), channel_id=1, source_target_pairs={{0,16},{1,17},{2,18},{3,19},{4,20},{5,21},{6,22},{7,23},{8,24},{9,... | collective-permute-start | bytes 196616 | tf_op jit(solution)/shard_map/ppermute | solution.py:519
  5.6 0.9 copy-start.2
  7.4 12.1 %all-to-all-start = ((f32[32,8,128]{2,1,0:T(8,128)}), f32[32,8,128]{2,1,0:T(8,128)S(1)}, u32[]{:S(2)}, u32[]{:S(2)}) async-start(f32[32,8,128]{2,1,0:T(8,128)} %bitcast.1), calls=%async_computation | async-start | bytes 262144 | tf_op jit(solution)/shard_map/all_to_all | solution.py:581
  11.3 7.7 %collective-permute-start.6 = (f32[2,32,512]{2,1,0:T(8,128)S(1)}, f32[2,32,512]{2,1,0:T(8,128)S(1)}, u32[]{:S(2)}, u32[]{:S(2)}) collective-permute-start(f32[2,32,512]{2,1,0:T(8,128)S(1)} %pad_maximum_fusion.5), channel_id=1, source_target_pairs={{0,8},{1,9},{2,10},{3,11},{4,12},{5,13},{6,14},{7,15},{8,0},{9,1},... | collective-permute-start | bytes 393224 | tf_op jit(solution)/shard_map/ppermute | solution.py:519
  19.5 6.1 %collective-permute-start.7 = (f32[4,16,512]{2,1,0:T(8,128)S(1)}, f32[4,16,512]{2,1,0:T(8,128)S(1)}, u32[]{:S(2)}, u32[]{:S(2)}) collective-permute-start(f32[4,16,512]{2,1,0:T(8,128)S(1)} %get-tuple-element.53), channel_id=1, source_target_pairs={{0,4},{1,5},{2,6},{3,7},{4,0},{5,1},{6,2},{7,3},{8,12},{9,13},{10,... | collective-permute-start | bytes 393224 | tf_op jit(solution)/shard_map/ppermute | solution.py:519
  20.6 5.2 %collective-permute-start.11 = (f32[4,16,512]{2,1,0:T(8,128)S(1)}, f32[4,16,512]{2,1,0:T(8,128)S(1)}, u32[]{:S(2)}, u32[]{:S(2)}) collective-permute-start(f32[4,16,512]{2,1,0:T(8,128)S(1)} %get-tuple-element.52), channel_id=1, source_target_pairs={{0,2},{1,3},{2,0},{3,1},{4,6},{5,7},{6,4},{7,5},{8,10},{9,11},{10,... | collective-permute-start | bytes 393224 | tf_op jit(solution)/shard_map/ppermute | solution.py:519
  25.6 8.1 %collective-permute-start.8 = (f32[8,16,512]{2,1,0:T(8,128)S(1)}, f32[8,16,512]{2,1,0:T(8,128)S(1)}, u32[]{:S(2)}, u32[]{:S(2)}) collective-permute-start(f32[8,16,512]{2,1,0:T(8,128)S(1)} %pad_maximum_fusion.1.refs_0_), channel_id=1, source_target_pairs={{0,2},{1,3},{2,0},{3,1},{4,6},{5,7},{6,4},{7,5},{8,10},{9,11},{10,... | collective-permute-start | bytes 786440 | tf_op jit(solution)/shard_map/ppermute | solution.py:519
  25.9 8.0 %collective-permute-start.12 = (f32[8,16,512]{2,1,0:T(8,128)S(1)}, f32[8,16,512]{2,1,0:T(8,128)S(1)}, u32[]{:S(2)}, u32[]{:S(2)}) collective-permute-start(f32[8,16,512]{2,1,0:T(8,128)S(1)} %pad_maximum_fusion.2.refs_4_), channel_id=1, source_target_pairs={{0,4},{1,5},{2,6},{3,7},{4,0},{5,1},{6,2},{7,3},{8,12},{9,13},{10,... | collective-permute-start | bytes 786440 | tf_op jit(solution)/shard_map/ppermute | solution.py:519
  27.4 6.8 %collective-permute-start.9 = (f32[8,16,512]{2,1,0:T(8,128)S(1)}, f32[8,16,512]{2,1,0:T(8,128)S(1)}, u32[]{:S(2)}, u32[]{:S(2)}) collective-permute-start(f32[8,16,512]{2,1,0:T(8,128)S(1)} %pad_maximum_fusion.1.refs_0_), channel_id=1, source_target_pairs={{0,1},{1,0},{2,3},{3,2},{4,5},{5,4},{6,7},{7,6},{8,9},{9,8},{10,11... | collective-permute-start | bytes 786440 | tf_op jit(solution)/shard_map/ppermute | solution.py:519
  27.5 6.8 %collective-permute-start.13 = (f32[8,16,512]{2,1,0:T(8,128)S(1)}, f32[8,16,512]{2,1,0:T(8,128)S(1)}, u32[]{:S(2)}, u32[]{:S(2)}) collective-permute-start(f32[8,16,512]{2,1,0:T(8,128)S(1)} %pad_maximum_fusion.2.refs_4_), channel_id=1, source_target_pairs={{0,1},{1,0},{2,3},{3,2},{4,5},{5,4},{6,7},{7,6},{8,9},{9,8},{10,11... | collective-permute-start | bytes 786440 | tf_op jit(solution)/shard_map/ppermute | solution.py:519
  33.8 1.5 %collective-permute-start.10 = (f32[8,16,512]{2,1,0:T(8,128)S(1)}, f32[8,16,512]{2,1,0:T(8,128)S(1)}, u32[]{:S(2)}, u32[]{:S(2)}) collective-permute-start(f32[8,16,512]{2,1,0:T(8,128)S(1)} %collective-permute-done.8.refs_1_), channel_id=1, source_target_pairs={{0,1},{1,0},{2,3},{3,2},{4,5},{5,4},{6,7},{7,6},{8,9},{9,8},{10,11... | collective-permute-start | bytes 786440 | tf_op jit(solution)/shard_map/ppermute | solution.py:519
  33.9 1.8 %collective-permute-start.14 = (f32[8,16,512]{2,1,0:T(8,128)S(1)}, f32[8,16,512]{2,1,0:T(8,128)S(1)}, u32[]{:S(2)}, u32[]{:S(2)}) collective-permute-start(f32[8,16,512]{2,1,0:T(8,128)S(1)} %collective-permute-done.12.refs_5_), channel_id=1, source_target_pairs={{0,1},{1,0},{2,3},{3,2},{4,5},{5,4},{6,7},{7,6},{8,9},{9,8},{10,11... | collective-permute-start | bytes 786440 | tf_op jit(solution)/shard_map/ppermute | solution.py:519
  48.0 10.8 %all-to-all-start.1 = ((f32[32,8,128]{2,1,0:T(8,128)}), f32[32,8,128]{2,1,0:T(8,128)S(1)}, u32[]{:S(2)}, u32[]{:S(2)}) async-start(f32[32,8,128]{2,1,0:T(8,128)} %bitcast.4), calls=%async_computation.1 | async-start | bytes 262144 | tf_op jit(solution)/shard_map/all_to_all | solution.py:581
  50.7 4.8 %collective-permute-start.17 = (f32[1,64,128]{2,1,0:T(8,128)S(1)}, f32[1,64,128]{2,1,0:T(8,128)S(1)}, u32[]{:S(2)}, u32[]{:S(2)}) collective-permute-start(f32[1,64,128]{2,1,0:T(8,128)S(1)} %get-tuple-element.57), channel_id=1, source_target_pairs={{0,3},{1,2},{2,1},{3,0},{4,7},{5,6},{6,5},{7,4},{8,11},{9,10},{10,... | collective-permute-start | bytes 98312 | tf_op jit(solution)/shard_map/ppermute | solution.py:519
  52.0 4.1 %collective-permute-start.16 = (f32[1,64,128]{2,1,0:T(8,128)S(1)}, f32[1,64,128]{2,1,0:T(8,128)S(1)}, u32[]{:S(2)}, u32[]{:S(2)}) collective-permute-start(f32[1,64,128]{2,1,0:T(8,128)S(1)} %get-tuple-element.58), channel_id=1, source_target_pairs={{0,2},{1,3},{2,0},{3,1},{4,6},{5,7},{6,4},{7,5},{8,10},{9,11},{10,... | collective-permute-start | bytes 98312 | tf_op jit(solution)/shard_map/ppermute | solution.py:519
  52.4 3.8 %collective-permute-start.15 = (f32[1,64,128]{2,1,0:T(8,128)S(1)}, f32[1,64,128]{2,1,0:T(8,128)S(1)}, u32[]{:S(2)}, u32[]{:S(2)}) collective-permute-start(f32[1,64,128]{2,1,0:T(8,128)S(1)} %get-tuple-element.59), channel_id=1, source_target_pairs={{0,1},{1,0},{2,3},{3,2},{4,5},{5,4},{6,7},{7,6},{8,9},{9,8},{10,11... | collective-permute-start | bytes 98312 | tf_op jit(solution)/shard_map/ppermute | solution.py:519
  52.7 6.9 %copy-start.3 = (f32[1,256,128]{2,1,0:T(8,128)S(1)}, f32[1,256,128]{2,1,0:T(8,128)}, u32[]{:S(2)}) copy-start(f32[1,256,128]{2,1,0:T(8,128)} %param.7) | copy-start | bytes 393220
  58.8 6.0 %collective-permute-start.20 = (f32[4,32,128]{2,1,0:T(8,128)S(1)}, f32[4,32,128]{2,1,0:T(8,128)S(1)}, u32[]{:S(2)}, u32[]{:S(2)}) collective-permute-start(f32[4,32,128]{2,1,0:T(8,128)S(1)} %get-tuple-element.54), channel_id=1, source_target_pairs={{0,4},{1,5},{2,6},{3,7},{4,0},{5,1},{6,2},{7,3},{8,12},{9,13},{10,... | collective-permute-start | bytes 196616 | tf_op jit(solution)/shard_map/ppermute | solution.py:519
  60.0 1.3 %collective-permute-start.22 = (f32[72,128]{1,0:T(8,128)S(1)}, f32[72,128]{1,0:T(8,128)S(1)}, u32[]{:S(2)}, u32[]{:S(2)}) collective-permute-start(f32[72,128]{1,0:T(8,128)S(1)} %get-tuple-element.40), channel_id=1, source_target_pairs={{0,1},{1,0},{2,3},{3,2},{4,5},{5,4},{6,7},{7,6},{8,9},{9,8},{10,11... | collective-permute-start | bytes 110600 | tf_op jit(solution)/shard_map/ppermute | solution.py:519
  60.1 11.9 %collective-permute-start.18 = (f32[4,32,128]{2,1,0:T(8,128)S(1)}, f32[4,32,128]{2,1,0:T(8,128)S(1)}, u32[]{:S(2)}, u32[]{:S(2)}) collective-permute-start(f32[4,32,128]{2,1,0:T(8,128)S(1)} %get-tuple-element.55), channel_id=1, source_target_pairs={{0,16},{1,17},{2,18},{3,19},{4,20},{5,21},{6,22},{7,23},{8,24},{9,... | collective-permute-start | bytes 196616 | tf_op jit(solution)/shard_map/ppermute | solution.py:519
  61.3 5.4 %collective-permute-start.25 = (f32[72,128]{1,0:T(8,128)S(1)}, f32[72,128]{1,0:T(8,128)S(1)}, u32[]{:S(2)}, u32[]{:S(2)}) collective-permute-start(f32[72,128]{1,0:T(8,128)S(1)} %add.36), channel_id=1, source_target_pairs={{0,6},{1,7},{2,4},{3,5},{4,2},{5,3},{6,0},{7,1},{8,14},{9,15},{10,... | collective-permute-start | bytes 110600 | tf_op jit(solution)/shard_map/ppermute | solution.py:519
  62.6 4.2 %collective-permute-start.24 = (f32[72,128]{1,0:T(8,128)S(1)}, f32[72,128]{1,0:T(8,128)S(1)}, u32[]{:S(2)}, u32[]{:S(2)}) collective-permute-start(f32[72,128]{1,0:T(8,128)S(1)} %add.36), channel_id=1, source_target_pairs={{0,4},{1,5},{2,6},{3,7},{4,0},{5,1},{6,2},{7,3},{8,12},{9,13},{10,... | collective-permute-start | bytes 110600 | tf_op jit(solution)/shard_map/ppermute | solution.py:519
  63.6 4.0 %collective-permute-start.23 = (f32[72,128]{1,0:T(8,128)S(1)}, f32[72,128]{1,0:T(8,128)S(1)}, u32[]{:S(2)}, u32[]{:S(2)}) collective-permute-start(f32[72,128]{1,0:T(8,128)S(1)} %add.36), channel_id=1, source_target_pairs={{0,2},{1,3},{2,0},{3,1},{4,6},{5,7},{6,4},{7,5},{8,10},{9,11},{10,... | collective-permute-start | bytes 110600 | tf_op jit(solution)/shard_map/ppermute | solution.py:519
  64.8 11.8 %collective-permute-start.21 = (f32[8,32,128]{2,1,0:T(8,128)S(1)}, f32[8,32,128]{2,1,0:T(8,128)S(1)}, u32[]{:S(2)}, u32[]{:S(2)}) collective-permute-start(f32[8,32,128]{2,1,0:T(8,128)S(1)} %pad_maximum_fusion.8), channel_id=1, source_target_pairs={{0,16},{1,17},{2,18},{3,19},{4,20},{5,21},{6,22},{7,23},{8,24},{9,... | collective-permute-start | bytes 393224 | tf_op jit(solution)/shard_map/ppermute | solution.py:519
  67.5 6.1 %collective-permute-start.28 = (f32[72,128]{1,0:T(8,128)S(1)}, f32[72,128]{1,0:T(8,128)S(1)}, u32[]{:S(2)}, u32[]{:S(2)}) collective-permute-start(f32[72,128]{1,0:T(8,128)S(1)} %add_add_fusion.1), channel_id=1, source_target_pairs={{0,24},{1,25},{2,26},{3,27},{4,28},{5,29},{6,30},{7,31},{8,16},{9,... | collective-permute-start | bytes 110600 | tf_op jit(solution)/shard_map/ppermute | solution.py:519
  69.6 6.9 %collective-permute-start.27 = (f32[72,128]{1,0:T(8,128)S(1)}, f32[72,128]{1,0:T(8,128)S(1)}, u32[]{:S(2)}, u32[]{:S(2)}) collective-permute-start(f32[72,128]{1,0:T(8,128)S(1)} %add_add_fusion.1), channel_id=1, source_target_pairs={{0,16},{1,17},{2,18},{3,19},{4,20},{5,21},{6,22},{7,23},{8,24},{9,... | collective-permute-start | bytes 110600 | tf_op jit(solution)/shard_map/ppermute | solution.py:519
  70.4 6.1 %collective-permute-start.26 = (f32[72,128]{1,0:T(8,128)S(1)}, f32[72,128]{1,0:T(8,128)S(1)}, u32[]{:S(2)}, u32[]{:S(2)}) collective-permute-start(f32[72,128]{1,0:T(8,128)S(1)} %add_add_fusion.1), channel_id=1, source_target_pairs={{0,8},{1,9},{2,10},{3,11},{4,12},{5,13},{6,14},{7,15},{8,0},{9,1},... | collective-permute-start | bytes 110600 | tf_op jit(solution)/shard_map/ppermute | solution.py:519
  72.0 6.5 %collective-permute-start.19 = (f32[8,32,128]{2,1,0:T(8,128)S(1)}, f32[8,32,128]{2,1,0:T(8,128)S(1)}, u32[]{:S(2)}, u32[]{:S(2)}) collective-permute-start(f32[8,32,128]{2,1,0:T(8,128)S(1)} %pad_maximum_fusion.7), channel_id=1, source_target_pairs={{0,8},{1,9},{2,10},{3,11},{4,12},{5,13},{6,14},{7,15},{8,0},{9,1},... | collective-permute-start | bytes 393224 | tf_op jit(solution)/shard_map/ppermute | solution.py:519
  76.6 2.0 %collective-permute-start.29 = (f32[72,128]{1,0:T(8,128)S(1)}, f32[72,128]{1,0:T(8,128)S(1)}, u32[]{:S(2)}, u32[]{:S(2)}) collective-permute-start(f32[72,128]{1,0:T(8,128)S(1)} %add_add_fusion.gram_ref), channel_id=1, source_target_pairs={{0,1},{1,0},{2,3},{3,2},{4,5},{5,4},{6,7},{7,6},{8,9},{9,8},{10,11... | collective-permute-start | bytes 110600 | tf_op jit(solution)/shard_map/ppermute | solution.py:519
  78.6 18.8 %all-to-all-start.2 = ((f32[32,4,640]{2,1,0:T(4,128)}), f32[32,4,640]{2,1,0:T(4,128)S(1)}, u32[]{:S(2)}, u32[]{:S(2)}) async-start(f32[32,4,640]{2,1,0:T(4,128)} %bitcast.6), calls=%async_computation.2 | async-start | bytes 655360 | tf_op jit(solution)/shard_map/all_to_all | solution.py:581
  81.7 15.8 %collective-permute-start.30 = (f32[16,32,128]{2,1,0:T(8,128)S(1)}, f32[16,32,128]{2,1,0:T(8,128)S(1)}, u32[]{:S(2)}, u32[]{:S(2)}) collective-permute-start(f32[16,32,128]{2,1,0:T(8,128)S(1)} %pad_maximum_fusion.3), channel_id=1, source_target_pairs={{0,4},{1,5},{2,6},{3,7},{4,0},{5,1},{6,2},{7,3},{8,12},{9,13},{10,... | collective-permute-start | bytes 786440 | tf_op jit(solution)/shard_map/ppermute | solution.py:519
  83.5 14.0 %collective-permute-start.31 = (f32[16,32,128]{2,1,0:T(8,128)S(1)}, f32[16,32,128]{2,1,0:T(8,128)S(1)}, u32[]{:S(2)}, u32[]{:S(2)}) collective-permute-start(f32[16,32,128]{2,1,0:T(8,128)S(1)} %pad_maximum_fusion.4), channel_id=1, source_target_pairs={{0,8},{1,9},{2,10},{3,11},{4,12},{5,13},{6,14},{7,15},{8,0},{9,1},... | collective-permute-start | bytes 786440 | tf_op jit(solution)/shard_map/ppermute | solution.py:519
  92.0 5.5 %copy-start = (f32[32,512]{1,0:T(8,128)S(1)}, f32[32,512]{1,0:T(8,128)}, u32[]{:S(2)}) copy-start(f32[32,512]{1,0:T(8,128)} %kspace_ref.1) | copy-start | bytes 196612
  92.0 5.5 %copy-start.1 = (s32[32,512]{1,0:T(8,128)S(1)}, s32[32,512]{1,0:T(8,128)}, u32[]{:S(2)}) copy-start(s32[32,512]{1,0:T(8,128)} %mask_ref.1) | copy-start | bytes 196612

commit v15 on v14

--- a/solution.py
+++ b/solution.py
@@ -171,13 +171,14 @@
             high, low = split(jnp.concatenate([first, second], axis=0))
             moved_ref[k * KER + j : k * KER + j + 2 * SUB, :] = high
             moved_ref[rows + k * KER + j : rows + k * KER + j + 2 * SUB, :] = low
-    total = jnp.zeros((2 * rows, 2 * channels), jnp.float32)
+    high = jnp.zeros((rows, 2 * channels), jnp.float32)
+    low = jnp.zeros((rows, channels), jnp.float32)
     for t in range(tiles):
         block = samples_ref[t].reshape(2 * channels, tile)
-        total = total + dot(moved_ref[:, t * tile : (t + 1) * tile], block, ((1,), (1,)))
-    return total[:rows, :channels] + (
-        total[:rows, channels:] + total[rows:, :channels] + total[rows:, channels:]
-    )
+        lanes = slice(t * tile, (t + 1) * tile)
+        high = high + dot(moved_ref[:rows, lanes], block, ((1,), (1,)))
+        low = low + dot(moved_ref[rows:, lanes], block[:channels], ((1,), (1,)))
+    return high[:, :channels] + (high[:, channels:] + low)
 
 
 def store_by_rows(normal, send_ref):
@@ -409,7 +410,7 @@
 
 
 def moved_columns(order, cols):
-    devices = len(order[0])
+    devices = len(order)
     at_row, at_col = square(devices * cols)
     turn = at_col % cols * devices + at_col // cols
     me = lax.axis_index("rows") * lax.axis_size("coil") + lax.axis_index("coil")
@@ -417,8 +418,7 @@
     mask = jnp.zeros_like(slot)
     bit = 1
     while bit < devices:
-        step = jnp.where(2 * at_col < at_col.shape[1], order[0][bit], order[1][bit])
-        mask = mask | jnp.where(slot & bit != 0, step, 0)
+        mask = mask | jnp.where(slot & bit != 0, order[bit], 0)
         bit *= 2
     source = at_col - slot + lax.bitwise_xor(mask, jnp.full_like(mask, me))
     return [(at_row == place).astype(jnp.float32) for place in (turn, source)]
@@ -445,10 +445,8 @@
     both_ref,
     kspace_ref,
     mask_ref,
-    top_near_ref,
-    top_far_ref,
-    low_near_ref,
-    low_far_ref,
+    near_ref,
+    far_ref,
     recovered_ref,
     basis_ref,
     vectors_ref,
@@ -457,10 +455,10 @@
     reach = images_ref.shape[1]
     factors = [exact(both, moved) for moved in moved_columns(order, cols)]
     chg, tile = kspace_ref.shape
-    lanes = top_near_ref.shape[1]
+    lanes = near_ref.shape[1]
     fold = lanes // chg
     deep = KER // fold
-    step = cols // 2 * deep
+    step = cols * deep
     lead = reach - tile - KER - 2 * SUB
     images = stacked_dot(factors[0], images_ref[...]).T[lead:]
     rim = reach - tile - SUB - lead
@@ -470,9 +468,8 @@
             jnp.concatenate(
                 [
                     ref[pl.ds(k * deep + a + i, ref.shape[0] // step, stride=step), :]
-                    for refs in ((top_near_ref, top_far_ref), (low_near_ref, low_far_ref))
-                    for k in range(cols // 2)
-                    for ref in refs
+                    for k in range(cols)
+                    for ref in (near_ref, far_ref)
                 ],
                 axis=0,
             )
@@ -589,43 +586,25 @@
 
 
 def total_beside(kept, given, near, order, images, groups, devices):
-    ways = []
-    mask = devices // 2
-    while mask >= groups:
-        ways.append(mask)
-        mask //= 2
-    half = near.shape[1] // 2
-    parts = [near[:, :half], near[:, half:]]
-    orders = [order, order]
-    ways = [ways, ways[-1:] + ways[:-1]]
-    step = 0
-
-    def advance():
-        for i in range(2):
-            parts[i], orders[i] = gather_round(
-                parts[i], orders[i], [ways[i][step]], devices, AXES
-            )
-
     total = kept + exchange(given, devices, 1, AXES)
-    for partners in rounds_of(2, devices):
+    step = devices // 2
+    for number, partners in enumerate(rounds_of(2, devices)):
         terms = [exchange(total, devices, way, AXES) for way in partners]
         total = total + terms[0]
         if len(terms) == 3:
             total = total + (terms[1] + terms[2])
-        if step < len(ways[0]) - 1:
-            advance()
-            step += 1
-    while step < len(ways[0]) - 1:
-        advance()
-        step += 1
+        if step > groups:
+            near, order = gather_round(near, order, [step], devices, AXES)
+            step //= 2
+            if number == 0:
+                near, total = lax.optimization_barrier((near, total))
+    while step > groups:
+        near, order = gather_round(near, order, [step], devices, AXES)
+        step //= 2
     other = exchange(total, devices, 1, AXES)
-    *parts, total, other, images = lax.optimization_barrier((*parts, total, other, images))
-    pieces = []
-    for i in range(2):
-        mask = ways[i][-1]
-        pieces += [parts[i], exchange(parts[i], devices, mask, AXES)]
-        orders[i] = orders[i] + [m ^ mask for m in orders[i]]
-    return (total, other), pieces, orders, to_all(images)
+    near, total, other, images = lax.optimization_barrier((near, total, other, images))
+    far = exchange(near, devices, groups, AXES)
+    return (total, other), near, far, order + [m ^ groups for m in order], to_all(images)
 
 
 def column_shards(kspace, sample_mask, start_basis):
@@ -688,7 +667,7 @@
         received.reshape(devices * per_tile, lanes),
         start_basis.reshape(owned, rank),
     )
-    gram, pieces, order, images = total_beside(
+    gram, near, far, order, images = total_beside(
         kept, given, near, order, images.reshape(devices, cols, reach), groups, devices
     )
     whole = ((rank, rank), f32)
@@ -713,7 +692,8 @@
         both,
         kspace,
         sample_mask,
-        *[piece.reshape(-1, lanes) for piece in pieces],
+        near.reshape(-1, lanes),
+        far.reshape(-1, lanes),
         scratch=[pltpu.VMEM((rank, KER * chg), f32)],
         limit=16,
         micros=5,

time: 101 us -> 106 us (1.050)
  waiting for transfers between devices: 27.4 us -> 40.2 us
  starting transfers between devices: 38.2 us -> 33.5 us
  Pallas kernels: 31.5 us -> 28.6 us
    ppermute x27 -> x24, waiting for transfers between devices: 24.3 us -> 37.1 us  [exchange(): return lax.ppermute(block, axes, [(i, i ^ mask) for i in range(devices)])]
    ppermute x27 -> x24, starting transfers between devices: 28.6 us -> 24 us  [exchange(): return lax.ppermute(block, axes, [(i, i ^ mask) for i in range(devices)])]
    pallas_call x7, Pallas kernels: 31.5 us -> 28.6 us  [call(): pl.pallas_call(kernel, out_shape=[jax.ShapeDtypeStruct(shape, kind) for s...]
  transfers between devices with their start and end apart: 30 -> 27, of which waited for: 14 -> 18; matrix products, arithmetic and copies ran while one was open for 0% -> 0% of each run, Pallas kernels for 16% -> 14%
where the time goes in v15:
time: 106 us
  waiting for transfers between devices  40.2 us (38%)
  starting transfers between devices  33.5 us (32%)
  Pallas kernels  28.6 us (27%)
  between operations  1.48 us (1%)
  local copies, waits for them, and re-layouts  1.06 us (1%)
    ppermute x24, waiting for transfers between devices, exchange(): return lax.ppermute(block, axes, [(i, i ^ mask) for i in range(devices)])  37.1 us
    pallas_call x7, Pallas kernels, call(): pl.pallas_call(kernel, out_shape=[jax.ShapeDtypeStruct(shape, kind) for s...  28.6 us
    ppermute x24, starting transfers between devices, exchange(): return lax.ppermute(block, axes, [(i, i ^ mask) for i in range(devices)])  24 us
    all_to_all x3, starting transfers between devices, to_all(): return lax.all_to_all(pieces, axes, 0, 0, tiled=True)  9.44 us
    all_to_all x3, waiting for transfers between devices, to_all(): return lax.all_to_all(pieces, axes, 0, 0, tiled=True)  3.07 us
  transfers between devices with their start and end apart: 27, of which 18 were waited for; matrix products, arithmetic and copies ran while one was open for 0% of the time, Pallas kernels for 14%

profile of v15, /device:TPU:0, one launch (start us, length us, event | category | flops | bytes accessed | tf_op | source)
XLA Modules:
  0.0 106.1 jit_solution(8219195540404090208)
XLA Ops:
  0.6 0.9 multiply_bitcast_fusion
  1.5 4.1 %collective-permute-start.5 = (f32[1,32,512]{2,1,0:T(8,128)S(1)}, f32[1,32,512]{2,1,0:T(8,128)S(1)}, u32[]{:S(2)}, u32[]{:S(2)}) collective-permute-start(f32[1,32,512]{2,1,0:T(8,128)S(1)} %multiply_bitcast_fusion), channel_id=1, source_target_pairs={{0,16},{1,17},{2,18},{3,19},{4,20},{5,21},{6,22},{7,23},{8,24},{9,... | collective-permute-start | bytes 196616 | tf_op jit(solution)/shard_map/ppermute | solution.py:516
  5.6 0.9 copy-done.2
  6.5 0.9 shard_map.50
  7.4 3.8 %all-to-all-start = ((f32[32,8,128]{2,1,0:T(8,128)}), f32[32,8,128]{2,1,0:T(8,128)S(1)}, u32[]{:S(2)}, u32[]{:S(2)}) async-start(f32[32,8,128]{2,1,0:T(8,128)} %bitcast.1), calls=%async_computation | async-start | bytes 262144 | tf_op jit(solution)/shard_map/all_to_all | solution.py:578
  11.3 1.8 %collective-permute-start.6 = (f32[2,32,512]{2,1,0:T(8,128)S(1)}, f32[2,32,512]{2,1,0:T(8,128)S(1)}, u32[]{:S(2)}, u32[]{:S(2)}) collective-permute-start(f32[2,32,512]{2,1,0:T(8,128)S(1)} %pad_maximum_fusion.5), channel_id=1, source_target_pairs={{0,8},{1,9},{2,10},{3,11},{4,12},{5,13},{6,14},{7,15},{8,0},{9,1},... | collective-permute-start | bytes 393224 | tf_op jit(solution)/shard_map/ppermute | solution.py:516
  13.1 5.9 %collective-permute-done.6 = f32[2,32,512]{2,1,0:T(8,128)S(1)} collective-permute-done((f32[2,32,512]{2,1,0:T(8,128)S(1)}, f32[2,32,512]{2,1,0:T(8,128)S(1)}, u32[]{:S(2)}, u32[]{:S(2)}) %collective-permute-start.6) | collective-permute-done | bytes 131104 | tf_op jit(solution)/shard_map/ppermute | solution.py:516
  19.0 0.5 all-to-all-done
  19.5 1.1 %collective-permute-start.7 = (f32[4,16,512]{2,1,0:T(8,128)S(1)}, f32[4,16,512]{2,1,0:T(8,128)S(1)}, u32[]{:S(2)}, u32[]{:S(2)}) collective-permute-start(f32[4,16,512]{2,1,0:T(8,128)S(1)} %get-tuple-element.55), channel_id=1, source_target_pairs={{0,4},{1,5},{2,6},{3,7},{4,0},{5,1},{6,2},{7,3},{8,12},{9,13},{10,... | collective-permute-start | bytes 393224 | tf_op jit(solution)/shard_map/ppermute | solution.py:516
  20.6 1.5 %collective-permute-start.11 = (f32[4,16,512]{2,1,0:T(8,128)S(1)}, f32[4,16,512]{2,1,0:T(8,128)S(1)}, u32[]{:S(2)}, u32[]{:S(2)}) collective-permute-start(f32[4,16,512]{2,1,0:T(8,128)S(1)} %get-tuple-element.54), channel_id=1, source_target_pairs={{0,2},{1,3},{2,0},{3,1},{4,6},{5,7},{6,4},{7,5},{8,10},{9,11},{10,... | collective-permute-start | bytes 393224 | tf_op jit(solution)/shard_map/ppermute | solution.py:516
  22.1 3.5 %collective-permute-done.7 = f32[4,16,512]{2,1,0:T(8,128)S(1)} collective-permute-done((f32[4,16,512]{2,1,0:T(8,128)S(1)}, f32[4,16,512]{2,1,0:T(8,128)S(1)}, u32[]{:S(2)}, u32[]{:S(2)}) %collective-permute-start.7) | collective-permute-done | bytes 131104 | tf_op jit(solution)/shard_map/ppermute | solution.py:516
  25.9 1.6 %collective-permute-start.12 = (f32[8,16,512]{2,1,0:T(8,128)S(1)}, f32[8,16,512]{2,1,0:T(8,128)S(1)}, u32[]{:S(2)}, u32[]{:S(2)}) collective-permute-start(f32[8,16,512]{2,1,0:T(8,128)S(1)} %pad_maximum_fusion.3.refs_4_), channel_id=1, source_target_pairs={{0,4},{1,5},{2,6},{3,7},{4,0},{5,1},{6,2},{7,3},{8,12},{9,13},{10,... | collective-permute-start | bytes 786440 | tf_op jit(solution)/shard_map/ppermute | solution.py:516
  27.5 0.5 collective-permute-start.13
  28.0 5.8 %collective-permute-done.8.refs_1_ = f32[8,16,512]{2,1,0:T(8,128)S(1)} collective-permute-done((f32[8,16,512]{2,1,0:T(8,128)S(1)}, f32[8,16,512]{2,1,0:T(8,128)S(1)}, u32[]{:S(2)}, u32[]{:S(2)}) %collective-permute-start.8) | collective-permute-done | bytes 262176 | tf_op jit(solution)/shard_map/ppermute | solution.py:516
  33.9 0.4 collective-permute-start.14
  34.3 1.0 collective-permute-done.10.refs_3_
  35.3 0.4 collective-permute-done.14.refs_7_
  35.7 9.3 %shard_map.51 = (bf16[8,2,4,32,512]{4,3,2,1,0:T(8,128)(2,1)S(1)}, f32[256,128]{1,0:T(8,128)S(1)}, f32[8,4,8,128]{3,2,1,0:T(8,128)}, f32[4,64,128]{2,1,0:T(8,128)S(1)}) custom-call(f32[8,4,8,128]{3,2,1,0:T(8,128)S(1)} %bitcast.13, f32[8,16,512]{2,1,0:T(8,128)S(1)} %pad_maximum_fusion.2.refs_0_, f32[8,16,512]{2,1,0:T(8,128)S(1)} %collective-permute-done.8.refs_1_, ...), custom_call_target="tpu_custom_call" | custom-call | flops 12000000000 | tf_op jit(solution)/shard_map/pallas_call | solution.py:501
  45.0 2.8 %all-to-all-start.1 = ((f32[32,8,128]{2,1,0:T(8,128)}), f32[32,8,128]{2,1,0:T(8,128)S(1)}, u32[]{:S(2)}, u32[]{:S(2)}) async-start(f32[32,8,128]{2,1,0:T(8,128)} %bitcast.4), calls=%async_computation.1 | async-start | bytes 262144 | tf_op jit(solution)/shard_map/all_to_all | solution.py:578
  47.8 1.3 %collective-permute-start.17 = (f32[1,64,128]{2,1,0:T(8,128)S(1)}, f32[1,64,128]{2,1,0:T(8,128)S(1)}, u32[]{:S(2)}, u32[]{:S(2)}) collective-permute-start(f32[1,64,128]{2,1,0:T(8,128)S(1)} %get-tuple-element.57), channel_id=1, source_target_pairs={{0,3},{1,2},{2,1},{3,0},{4,7},{5,6},{6,5},{7,4},{8,11},{9,10},{10,... | collective-permute-start | bytes 98312 | tf_op jit(solution)/shard_map/ppermute | solution.py:516
  49.1 0.3 collective-permute-start.16
  49.4 0.3 collective-permute-start.15
  49.7 2.8 %shard_map.52 = f32[8,4,4,640]{3,2,1,0:T(4,128)} custom-call(bf16[8,2,4,32,512]{4,3,2,1,0:T(8,128)(2,1)S(1)} %get-tuple-element.35.samples_ref, f32[256,128]{1,0:T(8,128)S(1)} %get-tuple-element.36.vectors_ref), custom_call_target="tpu_custom_call" | custom-call | flops 2000000000 | tf_op jit(solution)/shard_map/pallas_call | solution.py:501
  52.6 0.6 collective-permute-done.16
  53.2 2.6 %all-to-all-done.1 = f32[32,8,128]{2,1,0:T(8,128)S(1)} async-done(((f32[32,8,128]{2,1,0:T(8,128)}), f32[32,8,128]{2,1,0:T(8,128)S(1)}, u32[]{:S(2)}, u32[]{:S(2)}) %all-to-all-start.1) | async-done | bytes 131104 | tf_op jit(solution)/shard_map/all_to_all | solution.py:578
  55.8 0.5 shard_map.53
  56.3 0.3 collective-permute-start.19
  56.6 1.0 collective-permute-done.19
  57.6 0.9 collective-permute-start.22
  58.5 1.0 collective-permute-start.21
  59.5 1.6 %collective-permute-start.20 = (f32[72,128]{1,0:T(8,128)S(1)}, f32[72,128]{1,0:T(8,128)S(1)}, u32[]{:S(2)}, u32[]{:S(2)}) collective-permute-start(f32[72,128]{1,0:T(8,128)S(1)} %add.36), channel_id=1, source_target_pairs={{0,2},{1,3},{2,0},{3,1},{4,6},{5,7},{6,4},{7,5},{8,10},{9,11},{10,... | collective-permute-start | bytes 110600 | tf_op jit(solution)/shard_map/ppermute | solution.py:516
  61.1 0.8 collective-permute-start.18
  61.9 0.6 collective-permute-done.22
  62.5 1.0 collective-permute-done.20
  63.5 6.1 %collective-permute-done.18 = f32[4,64,128]{2,1,0:T(8,128)S(1)} collective-permute-done((f32[4,64,128]{2,1,0:T(8,128)S(1)}, f32[4,64,128]{2,1,0:T(8,128)S(1)}, u32[]{:S(2)}, u32[]{:S(2)}) %collective-permute-start.18) | collective-permute-done | bytes 131104 | tf_op jit(solution)/shard_map/ppermute | solution.py:516
  69.6 1.2 %collective-permute-start.26 = (f32[72,128]{1,0:T(8,128)S(1)}, f32[72,128]{1,0:T(8,128)S(1)}, u32[]{:S(2)}, u32[]{:S(2)}) collective-permute-start(f32[72,128]{1,0:T(8,128)S(1)} %add_add_fusion.1), channel_id=1, source_target_pairs={{0,24},{1,25},{2,26},{3,27},{4,28},{5,29},{6,30},{7,31},{8,16},{9,... | collective-permute-start | bytes 110600 | tf_op jit(solution)/shard_map/ppermute | solution.py:516
  70.9 3.2 %collective-permute-start.24 = (f32[72,128]{1,0:T(8,128)S(1)}, f32[72,128]{1,0:T(8,128)S(1)}, u32[]{:S(2)}, u32[]{:S(2)}) collective-permute-start(f32[72,128]{1,0:T(8,128)S(1)} %add_add_fusion.1), channel_id=1, source_target_pairs={{0,8},{1,9},{2,10},{3,11},{4,12},{5,13},{6,14},{7,15},{8,0},{9,1},... | collective-permute-start | bytes 110600 | tf_op jit(solution)/shard_map/ppermute | solution.py:516
  74.1 1.6 %collective-permute-done.26 = f32[72,128]{1,0:T(8,128)S(1)} collective-permute-done((f32[72,128]{1,0:T(8,128)S(1)}, f32[72,128]{1,0:T(8,128)S(1)}, u32[]{:S(2)}, u32[]{:S(2)}) %collective-permute-start.26) | collective-permute-done | bytes 36896 | tf_op jit(solution)/shard_map/ppermute | solution.py:516
  75.7 0.6 collective-permute-done.25
  76.3 0.5 collective-permute-done.24
  76.8 5.2 %collective-permute-done.23 = f32[8,64,128]{2,1,0:T(8,128)S(1)} collective-permute-done((f32[8,64,128]{2,1,0:T(8,128)S(1)}, f32[8,64,128]{2,1,0:T(8,128)S(1)}, u32[]{:S(2)}, u32[]{:S(2)}) %collective-permute-start.23) | collective-permute-done | bytes 262176 | tf_op jit(solution)/shard_map/ppermute | solution.py:516
  82.0 2.9 %all-to-all-start.2 = ((f32[32,4,640]{2,1,0:T(4,128)}), f32[32,4,640]{2,1,0:T(4,128)S(1)}, u32[]{:S(2)}, u32[]{:S(2)}) async-start(f32[32,4,640]{2,1,0:T(4,128)} %bitcast.6), calls=%async_computation.2 | async-start | bytes 655360 | tf_op jit(solution)/shard_map/all_to_all | solution.py:578
  84.9 1.8 %collective-permute-start.28 = (f32[16,64,128]{2,1,0:T(8,128)S(1)}, f32[16,64,128]{2,1,0:T(8,128)S(1)}, u32[]{:S(2)}, u32[]{:S(2)}) collective-permute-start(f32[16,64,128]{2,1,0:T(8,128)S(1)} %pad_maximum_fusion), channel_id=1, source_target_pairs={{0,4},{1,5},{2,6},{3,7},{4,0},{5,1},{6,2},{7,3},{8,12},{9,13},{10,... | collective-permute-start | bytes 1572872 | tf_op jit(solution)/shard_map/ppermute | solution.py:516
  86.7 6.4 %shard_map.54 = (f32[128,128]{1,0:T(8,128)S(1)}, f32[128,128]{1,0:T(8,128)S(1)}, s32[1]{0:T(128)}) custom-call(f32[72,128]{1,0:T(8,128)S(1)} %add_add_fusion.gram_ref, f32[72,128]{1,0:T(8,128)S(1)} %collective-permute-done.27.other_ref), custom_call_target="tpu_custom_call" | custom-call | flops 12000000000 | tf_op jit(solution)/shard_map/pallas_call | solution.py:501
  93.8 0.2 conditional.1
  94.1 5.0 %shard_map.55.both_ref = f32[128,128]{1,0:T(8,128)S(1)} custom-call(f32[128,128]{1,0:T(8,128)S(1)} %get-tuple-element.60.gram_ref, f32[128,128]{1,0:T(8,128)S(1)} %get-tuple-element.49.inverse_ref), custom_call_target="tpu_custom_call" | custom-call | tf_op jit(solution)/shard_map/pallas_call | solution.py:501
  99.3 3.3 %collective-permute-done.28 = f32[16,64,128]{2,1,0:T(8,128)S(1)} collective-permute-done((f32[16,64,128]{2,1,0:T(8,128)S(1)}, f32[16,64,128]{2,1,0:T(8,128)S(1)}, u32[]{:S(2)}, u32[]{:S(2)}) %collective-permute-start.28) | collective-permute-done | bytes 524320 | tf_op jit(solution)/shard_map/ppermute | solution.py:516
  102.5 3.6 %shard_map.56 = (f32[32,512]{1,0:T(8,128)}, f32[256,128]{1,0:T(8,128)}) custom-call(f32[128,640]{1,0:T(8,128)S(1)} %reshape.45.images_ref, f32[128,128]{1,0:T(8,128)S(1)} %shard_map.55.both_ref, f32[32,512]{1,0:T(8,128)S(1)} %copy-done, s32[32,512]{1,0:T(8,128)S(1)} %copy-done.1, f32[1024,128]{1,0:T(8,128)S(1)} %bitcast.12, f32[1024,128]{1,0:T(8,128)S(1)} %bitcast.15), custom_call_target="tpu_custom_call" | custom-call | flops 5000000000 | tf_op jit(solution)/shard_map/pallas_call | solution.py:501
  (36 shorter events, 0.8 us)
Async XLA Ops:
  1.5 9.7 %collective-permute-start.5 = (f32[1,32,512]{2,1,0:T(8,128)S(1)}, f32[1,32,512]{2,1,0:T(8,128)S(1)}, u32[]{:S(2)}, u32[]{:S(2)}) collective-permute-start(f32[1,32,512]{2,1,0:T(8,128)S(1)} %multiply_bitcast_fusion), channel_id=1, source_target_pairs={{0,16},{1,17},{2,18},{3,19},{4,20},{5,21},{6,22},{7,23},{8,24},{9,... | collective-permute-start | bytes 196616 | tf_op jit(solution)/shard_map/ppermute | solution.py:516
  5.6 0.9 copy-start.2
  7.4 12.1 %all-to-all-start = ((f32[32,8,128]{2,1,0:T(8,128)}), f32[32,8,128]{2,1,0:T(8,128)S(1)}, u32[]{:S(2)}, u32[]{:S(2)}) async-start(f32[32,8,128]{2,1,0:T(8,128)} %bitcast.1), calls=%async_computation | async-start | bytes 262144 | tf_op jit(solution)/shard_map/all_to_all | solution.py:578
  11.3 7.7 %collective-permute-start.6 = (f32[2,32,512]{2,1,0:T(8,128)S(1)}, f32[2,32,512]{2,1,0:T(8,128)S(1)}, u32[]{:S(2)}, u32[]{:S(2)}) collective-permute-start(f32[2,32,512]{2,1,0:T(8,128)S(1)} %pad_maximum_fusion.5), channel_id=1, source_target_pairs={{0,8},{1,9},{2,10},{3,11},{4,12},{5,13},{6,14},{7,15},{8,0},{9,1},... | collective-permute-start | bytes 393224 | tf_op jit(solution)/shard_map/ppermute | solution.py:516
  19.5 6.1 %collective-permute-start.7 = (f32[4,16,512]{2,1,0:T(8,128)S(1)}, f32[4,16,512]{2,1,0:T(8,128)S(1)}, u32[]{:S(2)}, u32[]{:S(2)}) collective-permute-start(f32[4,16,512]{2,1,0:T(8,128)S(1)} %get-tuple-element.55), channel_id=1, source_target_pairs={{0,4},{1,5},{2,6},{3,7},{4,0},{5,1},{6,2},{7,3},{8,12},{9,13},{10,... | collective-permute-start | bytes 393224 | tf_op jit(solution)/shard_map/ppermute | solution.py:516
  20.6 5.2 %collective-permute-start.11 = (f32[4,16,512]{2,1,0:T(8,128)S(1)}, f32[4,16,512]{2,1,0:T(8,128)S(1)}, u32[]{:S(2)}, u32[]{:S(2)}) collective-permute-start(f32[4,16,512]{2,1,0:T(8,128)S(1)} %get-tuple-element.54), channel_id=1, source_target_pairs={{0,2},{1,3},{2,0},{3,1},{4,6},{5,7},{6,4},{7,5},{8,10},{9,11},{10,... | collective-permute-start | bytes 393224 | tf_op jit(solution)/shard_map/ppermute | solution.py:516
  25.6 8.1 %collective-permute-start.8 = (f32[8,16,512]{2,1,0:T(8,128)S(1)}, f32[8,16,512]{2,1,0:T(8,128)S(1)}, u32[]{:S(2)}, u32[]{:S(2)}) collective-permute-start(f32[8,16,512]{2,1,0:T(8,128)S(1)} %pad_maximum_fusion.2.refs_0_), channel_id=1, source_target_pairs={{0,2},{1,3},{2,0},{3,1},{4,6},{5,7},{6,4},{7,5},{8,10},{9,11},{10,... | collective-permute-start | bytes 786440 | tf_op jit(solution)/shard_map/ppermute | solution.py:516
  25.9 8.0 %collective-permute-start.12 = (f32[8,16,512]{2,1,0:T(8,128)S(1)}, f32[8,16,512]{2,1,0:T(8,128)S(1)}, u32[]{:S(2)}, u32[]{:S(2)}) collective-permute-start(f32[8,16,512]{2,1,0:T(8,128)S(1)} %pad_maximum_fusion.3.refs_4_), channel_id=1, source_target_pairs={{0,4},{1,5},{2,6},{3,7},{4,0},{5,1},{6,2},{7,3},{8,12},{9,13},{10,... | collective-permute-start | bytes 786440 | tf_op jit(solution)/shard_map/ppermute | solution.py:516
  27.4 6.8 %collective-permute-start.9 = (f32[8,16,512]{2,1,0:T(8,128)S(1)}, f32[8,16,512]{2,1,0:T(8,128)S(1)}, u32[]{:S(2)}, u32[]{:S(2)}) collective-permute-start(f32[8,16,512]{2,1,0:T(8,128)S(1)} %pad_maximum_fusion.2.refs_0_), channel_id=1, source_target_pairs={{0,1},{1,0},{2,3},{3,2},{4,5},{5,4},{6,7},{7,6},{8,9},{9,8},{10,11... | collective-permute-start | bytes 786440 | tf_op jit(solution)/shard_map/ppermute | solution.py:516
  27.5 6.8 %collective-permute-start.13 = (f32[8,16,512]{2,1,0:T(8,128)S(1)}, f32[8,16,512]{2,1,0:T(8,128)S(1)}, u32[]{:S(2)}, u32[]{:S(2)}) collective-permute-start(f32[8,16,512]{2,1,0:T(8,128)S(1)} %pad_maximum_fusion.3.refs_4_), channel_id=1, source_target_pairs={{0,1},{1,0},{2,3},{3,2},{4,5},{5,4},{6,7},{7,6},{8,9},{9,8},{10,11... | collective-permute-start | bytes 786440 | tf_op jit(solution)/shard_map/ppermute | solution.py:516
  33.8 1.5 %collective-permute-start.10 = (f32[8,16,512]{2,1,0:T(8,128)S(1)}, f32[8,16,512]{2,1,0:T(8,128)S(1)}, u32[]{:S(2)}, u32[]{:S(2)}) collective-permute-start(f32[8,16,512]{2,1,0:T(8,128)S(1)} %collective-permute-done.8.refs_1_), channel_id=1, source_target_pairs={{0,1},{1,0},{2,3},{3,2},{4,5},{5,4},{6,7},{7,6},{8,9},{9,8},{10,11... | collective-permute-start | bytes 786440 | tf_op jit(solution)/shard_map/ppermute | solution.py:516
  33.9 1.8 %collective-permute-start.14 = (f32[8,16,512]{2,1,0:T(8,128)S(1)}, f32[8,16,512]{2,1,0:T(8,128)S(1)}, u32[]{:S(2)}, u32[]{:S(2)}) collective-permute-start(f32[8,16,512]{2,1,0:T(8,128)S(1)} %collective-permute-done.12.refs_5_), channel_id=1, source_target_pairs={{0,1},{1,0},{2,3},{3,2},{4,5},{5,4},{6,7},{7,6},{8,9},{9,8},{10,11... | collective-permute-start | bytes 786440 | tf_op jit(solution)/shard_map/ppermute | solution.py:516
  45.0 10.8 %all-to-all-start.1 = ((f32[32,8,128]{2,1,0:T(8,128)}), f32[32,8,128]{2,1,0:T(8,128)S(1)}, u32[]{:S(2)}, u32[]{:S(2)}) async-start(f32[32,8,128]{2,1,0:T(8,128)} %bitcast.4), calls=%async_computation.1 | async-start | bytes 262144 | tf_op jit(solution)/shard_map/all_to_all | solution.py:578
  47.8 4.8 %collective-permute-start.17 = (f32[1,64,128]{2,1,0:T(8,128)S(1)}, f32[1,64,128]{2,1,0:T(8,128)S(1)}, u32[]{:S(2)}, u32[]{:S(2)}) collective-permute-start(f32[1,64,128]{2,1,0:T(8,128)S(1)} %get-tuple-element.57), channel_id=1, source_target_pairs={{0,3},{1,2},{2,1},{3,0},{4,7},{5,6},{6,5},{7,4},{8,11},{9,10},{10,... | collective-permute-start | bytes 98312 | tf_op jit(solution)/shard_map/ppermute | solution.py:516
  49.1 4.1 %collective-permute-start.16 = (f32[1,64,128]{2,1,0:T(8,128)S(1)}, f32[1,64,128]{2,1,0:T(8,128)S(1)}, u32[]{:S(2)}, u32[]{:S(2)}) collective-permute-start(f32[1,64,128]{2,1,0:T(8,128)S(1)} %get-tuple-element.58), channel_id=1, source_target_pairs={{0,2},{1,3},{2,0},{3,1},{4,6},{5,7},{6,4},{7,5},{8,10},{9,11},{10,... | collective-permute-start | bytes 98312 | tf_op jit(solution)/shard_map/ppermute | solution.py:516
  49.4 3.8 %collective-permute-start.15 = (f32[1,64,128]{2,1,0:T(8,128)S(1)}, f32[1,64,128]{2,1,0:T(8,128)S(1)}, u32[]{:S(2)}, u32[]{:S(2)}) collective-permute-start(f32[1,64,128]{2,1,0:T(8,128)S(1)} %get-tuple-element.59), channel_id=1, source_target_pairs={{0,1},{1,0},{2,3},{3,2},{4,5},{5,4},{6,7},{7,6},{8,9},{9,8},{10,11... | collective-permute-start | bytes 98312 | tf_op jit(solution)/shard_map/ppermute | solution.py:516
  49.7 6.1 %copy-start.3 = (f32[1,256,128]{2,1,0:T(8,128)S(1)}, f32[1,256,128]{2,1,0:T(8,128)}, u32[]{:S(2)}) copy-start(f32[1,256,128]{2,1,0:T(8,128)} %param.7) | copy-start | bytes 393220
  56.3 1.3 %collective-permute-start.19 = (f32[72,128]{1,0:T(8,128)S(1)}, f32[72,128]{1,0:T(8,128)S(1)}, u32[]{:S(2)}, u32[]{:S(2)}) collective-permute-start(f32[72,128]{1,0:T(8,128)S(1)} %get-tuple-element.41), channel_id=1, source_target_pairs={{0,1},{1,0},{2,3},{3,2},{4,5},{5,4},{6,7},{7,6},{8,9},{9,8},{10,11... | collective-permute-start | bytes 110600 | tf_op jit(solution)/shard_map/ppermute | solution.py:516
  57.6 4.9 %collective-permute-start.22 = (f32[72,128]{1,0:T(8,128)S(1)}, f32[72,128]{1,0:T(8,128)S(1)}, u32[]{:S(2)}, u32[]{:S(2)}) collective-permute-start(f32[72,128]{1,0:T(8,128)S(1)} %add.36), channel_id=1, source_target_pairs={{0,6},{1,7},{2,4},{3,5},{4,2},{5,3},{6,0},{7,1},{8,14},{9,15},{10,... | collective-permute-start | bytes 110600 | tf_op jit(solution)/shard_map/ppermute | solution.py:516
  58.5 4.0 %collective-permute-start.21 = (f32[72,128]{1,0:T(8,128)S(1)}, f32[72,128]{1,0:T(8,128)S(1)}, u32[]{:S(2)}, u32[]{:S(2)}) collective-permute-start(f32[72,128]{1,0:T(8,128)S(1)} %add.36), channel_id=1, source_target_pairs={{0,4},{1,5},{2,6},{3,7},{4,0},{5,1},{6,2},{7,3},{8,12},{9,13},{10,... | collective-permute-start | bytes 110600 | tf_op jit(solution)/shard_map/ppermute | solution.py:516
  59.5 4.0 %collective-permute-start.20 = (f32[72,128]{1,0:T(8,128)S(1)}, f32[72,128]{1,0:T(8,128)S(1)}, u32[]{:S(2)}, u32[]{:S(2)}) collective-permute-start(f32[72,128]{1,0:T(8,128)S(1)} %add.36), channel_id=1, source_target_pairs={{0,2},{1,3},{2,0},{3,1},{4,6},{5,7},{6,4},{7,5},{8,10},{9,11},{10,... | collective-permute-start | bytes 110600 | tf_op jit(solution)/shard_map/ppermute | solution.py:516
  61.1 8.5 %collective-permute-start.18 = (f32[4,64,128]{2,1,0:T(8,128)S(1)}, f32[4,64,128]{2,1,0:T(8,128)S(1)}, u32[]{:S(2)}, u32[]{:S(2)}) collective-permute-start(f32[4,64,128]{2,1,0:T(8,128)S(1)} %pad_maximum_fusion.6), channel_id=1, source_target_pairs={{0,16},{1,17},{2,18},{3,19},{4,20},{5,21},{6,22},{7,23},{8,24},{9,... | collective-permute-start | bytes 393224 | tf_op jit(solution)/shard_map/ppermute | solution.py:516
  69.6 6.1 %collective-permute-start.26 = (f32[72,128]{1,0:T(8,128)S(1)}, f32[72,128]{1,0:T(8,128)S(1)}, u32[]{:S(2)}, u32[]{:S(2)}) collective-permute-start(f32[72,128]{1,0:T(8,128)S(1)} %add_add_fusion.1), channel_id=1, source_target_pairs={{0,24},{1,25},{2,26},{3,27},{4,28},{5,29},{6,30},{7,31},{8,16},{9,... | collective-permute-start | bytes 110600 | tf_op jit(solution)/shard_map/ppermute | solution.py:516
  70.9 5.4 %collective-permute-start.25 = (f32[72,128]{1,0:T(8,128)S(1)}, f32[72,128]{1,0:T(8,128)S(1)}, u32[]{:S(2)}, u32[]{:S(2)}) collective-permute-start(f32[72,128]{1,0:T(8,128)S(1)} %add_add_fusion.1), channel_id=1, source_target_pairs={{0,16},{1,17},{2,18},{3,19},{4,20},{5,21},{6,22},{7,23},{8,24},{9,... | collective-permute-start | bytes 110600 | tf_op jit(solution)/shard_map/ppermute | solution.py:516
  70.9 5.9 %collective-permute-start.24 = (f32[72,128]{1,0:T(8,128)S(1)}, f32[72,128]{1,0:T(8,128)S(1)}, u32[]{:S(2)}, u32[]{:S(2)}) collective-permute-start(f32[72,128]{1,0:T(8,128)S(1)} %add_add_fusion.1), channel_id=1, source_target_pairs={{0,8},{1,9},{2,10},{3,11},{4,12},{5,13},{6,14},{7,15},{8,0},{9,1},... | collective-permute-start | bytes 110600 | tf_op jit(solution)/shard_map/ppermute | solution.py:516
  74.1 7.9 %collective-permute-start.23 = (f32[8,64,128]{2,1,0:T(8,128)S(1)}, f32[8,64,128]{2,1,0:T(8,128)S(1)}, u32[]{:S(2)}, u32[]{:S(2)}) collective-permute-start(f32[8,64,128]{2,1,0:T(8,128)S(1)} %pad_maximum_fusion.4), channel_id=1, source_target_pairs={{0,8},{1,9},{2,10},{3,11},{4,12},{5,13},{6,14},{7,15},{8,0},{9,1},... | collective-permute-start | bytes 786440 | tf_op jit(solution)/shard_map/ppermute | solution.py:516
  76.7 5.3 %collective-permute-start.27 = (f32[72,128]{1,0:T(8,128)S(1)}, f32[72,128]{1,0:T(8,128)S(1)}, u32[]{:S(2)}, u32[]{:S(2)}) collective-permute-start(f32[72,128]{1,0:T(8,128)S(1)} %add_add_fusion.gram_ref), channel_id=1, source_target_pairs={{0,1},{1,0},{2,3},{3,2},{4,5},{5,4},{6,7},{7,6},{8,9},{9,8},{10,11... | collective-permute-start | bytes 110600 | tf_op jit(solution)/shard_map/ppermute | solution.py:516
  82.0 17.1 %all-to-all-start.2 = ((f32[32,4,640]{2,1,0:T(4,128)}), f32[32,4,640]{2,1,0:T(4,128)S(1)}, u32[]{:S(2)}, u32[]{:S(2)}) async-start(f32[32,4,640]{2,1,0:T(4,128)} %bitcast.6), calls=%async_computation.2 | async-start | bytes 655360 | tf_op jit(solution)/shard_map/all_to_all | solution.py:578
  84.9 17.6 %collective-permute-start.28 = (f32[16,64,128]{2,1,0:T(8,128)S(1)}, f32[16,64,128]{2,1,0:T(8,128)S(1)}, u32[]{:S(2)}, u32[]{:S(2)}) collective-permute-start(f32[16,64,128]{2,1,0:T(8,128)S(1)} %pad_maximum_fusion), channel_id=1, source_target_pairs={{0,4},{1,5},{2,6},{3,7},{4,0},{5,1},{6,2},{7,3},{8,12},{9,13},{10,... | collective-permute-start | bytes 1572872 | tf_op jit(solution)/shard_map/ppermute | solution.py:516
  93.8 8.7 %copy-start = (f32[32,512]{1,0:T(8,128)S(1)}, f32[32,512]{1,0:T(8,128)}, u32[]{:S(2)}) copy-start(f32[32,512]{1,0:T(8,128)} %kspace_ref.1) | copy-start | bytes 196612
  93.8 8.7 %copy-start.1 = (s32[32,512]{1,0:T(8,128)S(1)}, s32[32,512]{1,0:T(8,128)}, u32[]{:S(2)}) copy-start(s32[32,512]{1,0:T(8,128)} %mask_ref.1) | copy-start | bytes 196612

commit v16 on v14

--- a/solution.py
+++ b/solution.py
@@ -138,12 +138,13 @@
     ).astype(jnp.bfloat16)
     both = dot(flip, jnp.concatenate([high, low], axis=1)).astype(jnp.bfloat16)
     high, low = both[:, :channels], both[:, channels:]
-    twice = jnp.concatenate([high, high], axis=1)
+    parts = jnp.concatenate([high, high, low], axis=1)
     tiles = samples_ref.shape[0]
     tile = samples_ref.shape[-1]
     for t in range(tiles):
         block = samples_ref[t].reshape(2 * channels, tile)
-        wide_ref[:, t * tile : (t + 1) * tile] = dot(twice, block) + dot(low, block[:channels])
+        block = jnp.concatenate([block, block[:channels]], axis=0)
+        wide_ref[:, t * tile : (t + 1) * tile] = dot(parts, block)
     images = []
     for k in range(cols):
         total = None
@@ -171,13 +172,14 @@
             high, low = split(jnp.concatenate([first, second], axis=0))
             moved_ref[k * KER + j : k * KER + j + 2 * SUB, :] = high
             moved_ref[rows + k * KER + j : rows + k * KER + j + 2 * SUB, :] = low
-    total = jnp.zeros((2 * rows, 2 * channels), jnp.float32)
+    high = jnp.zeros((rows, 2 * channels), jnp.float32)
+    low = jnp.zeros((rows, channels), jnp.float32)
     for t in range(tiles):
         block = samples_ref[t].reshape(2 * channels, tile)
-        total = total + dot(moved_ref[:, t * tile : (t + 1) * tile], block, ((1,), (1,)))
-    return total[:rows, :channels] + (
-        total[:rows, channels:] + total[rows:, :channels] + total[rows:, channels:]
-    )
+        lanes = slice(t * tile, (t + 1) * tile)
+        high = high + dot(moved_ref[:rows, lanes], block, ((1,), (1,)))
+        low = low + dot(moved_ref[rows:, lanes], block[:channels], ((1,), (1,)))
+    return high[:, :channels] + (high[:, channels:] + low)
 
 
 def store_by_rows(normal, send_ref):

time: 101 us -> 98.4 us (0.974)
  Pallas kernels: 31.5 us -> 28.4 us
    pallas_call x7, Pallas kernels: 31.5 us -> 28.4 us  [call(): pl.pallas_call(kernel, out_shape=[jax.ShapeDtypeStruct(shape, kind) for s...]
where the time goes in v16:
time: 98.4 us; the launch traced here: 98 us
  starting transfers between devices  38.2 us (39%)
  Pallas kernels  28.4 us (29%)
  waiting for transfers between devices  27.5 us (28%)
  between operations  1.53 us (2%)
  local copies, waits for them, and re-layouts  1.07 us (1%)
  other arithmetic  1.05 us (1%)
    ppermute x27, starting transfers between devices, exchange(): return lax.ppermute(block, axes, [(i, i ^ mask) for i in range(devices)])  28.5 us
    pallas_call x7, Pallas kernels, call(): pl.pallas_call(kernel, out_shape=[jax.ShapeDtypeStruct(shape, kind) for s...  28.4 us
    ppermute x27, waiting for transfers between devices, exchange(): return lax.ppermute(block, axes, [(i, i ^ mask) for i in range(devices)])  24.5 us
    all_to_all x3, starting transfers between devices, to_all(): return lax.all_to_all(pieces, axes, 0, 0, tiled=True)  9.68 us
    all_to_all x3, waiting for transfers between devices, to_all(): return lax.all_to_all(pieces, axes, 0, 0, tiled=True)  3.07 us
  transfers between devices with their start and end apart: 30, of which 14 were waited for; matrix products, arithmetic and copies ran while one was open for 0% of the time, Pallas kernels for 16%

profile of v16, /device:TPU:0, one launch (start us, length us, event | category | flops | bytes accessed | tf_op | source)
XLA Modules:
  0.0 98.0 jit_solution(5615423129848717285)
XLA Ops:
  0.6 0.9 multiply_bitcast_fusion
  1.5 4.1 %collective-permute-start.5 = (f32[1,32,512]{2,1,0:T(8,128)S(1)}, f32[1,32,512]{2,1,0:T(8,128)S(1)}, u32[]{:S(2)}, u32[]{:S(2)}) collective-permute-start(f32[1,32,512]{2,1,0:T(8,128)S(1)} %multiply_bitcast_fusion), channel_id=1, source_target_pairs={{0,16},{1,17},{2,18},{3,19},{4,20},{5,21},{6,22},{7,23},{8,24},{9,... | collective-permute-start | bytes 196616 | tf_op jit(solution)/shard_map/ppermute | solution.py:521
  5.6 0.9 copy-done.2
  6.5 0.9 shard_map.50
  7.4 3.8 %all-to-all-start = ((f32[32,8,128]{2,1,0:T(8,128)}), f32[32,8,128]{2,1,0:T(8,128)S(1)}, u32[]{:S(2)}, u32[]{:S(2)}) async-start(f32[32,8,128]{2,1,0:T(8,128)} %bitcast.1), calls=%async_computation | async-start | bytes 262144 | tf_op jit(solution)/shard_map/all_to_all | solution.py:583
  11.3 1.8 %collective-permute-start.6 = (f32[2,32,512]{2,1,0:T(8,128)S(1)}, f32[2,32,512]{2,1,0:T(8,128)S(1)}, u32[]{:S(2)}, u32[]{:S(2)}) collective-permute-start(f32[2,32,512]{2,1,0:T(8,128)S(1)} %pad_maximum_fusion.5), channel_id=1, source_target_pairs={{0,8},{1,9},{2,10},{3,11},{4,12},{5,13},{6,14},{7,15},{8,0},{9,1},... | collective-permute-start | bytes 393224 | tf_op jit(solution)/shard_map/ppermute | solution.py:521
  13.1 5.9 %collective-permute-done.6 = f32[2,32,512]{2,1,0:T(8,128)S(1)} collective-permute-done((f32[2,32,512]{2,1,0:T(8,128)S(1)}, f32[2,32,512]{2,1,0:T(8,128)S(1)}, u32[]{:S(2)}, u32[]{:S(2)}) %collective-permute-start.6) | collective-permute-done | bytes 131104 | tf_op jit(solution)/shard_map/ppermute | solution.py:521
  19.0 0.5 all-to-all-done
  19.5 1.1 %collective-permute-start.7 = (f32[4,16,512]{2,1,0:T(8,128)S(1)}, f32[4,16,512]{2,1,0:T(8,128)S(1)}, u32[]{:S(2)}, u32[]{:S(2)}) collective-permute-start(f32[4,16,512]{2,1,0:T(8,128)S(1)} %get-tuple-element.53), channel_id=1, source_target_pairs={{0,4},{1,5},{2,6},{3,7},{4,0},{5,1},{6,2},{7,3},{8,12},{9,13},{10,... | collective-permute-start | bytes 393224 | tf_op jit(solution)/shard_map/ppermute | solution.py:521
  20.6 1.5 %collective-permute-start.11 = (f32[4,16,512]{2,1,0:T(8,128)S(1)}, f32[4,16,512]{2,1,0:T(8,128)S(1)}, u32[]{:S(2)}, u32[]{:S(2)}) collective-permute-start(f32[4,16,512]{2,1,0:T(8,128)S(1)} %get-tuple-element.52), channel_id=1, source_target_pairs={{0,2},{1,3},{2,0},{3,1},{4,6},{5,7},{6,4},{7,5},{8,10},{9,11},{10,... | collective-permute-start | bytes 393224 | tf_op jit(solution)/shard_map/ppermute | solution.py:521
  22.1 3.5 %collective-permute-done.7 = f32[4,16,512]{2,1,0:T(8,128)S(1)} collective-permute-done((f32[4,16,512]{2,1,0:T(8,128)S(1)}, f32[4,16,512]{2,1,0:T(8,128)S(1)}, u32[]{:S(2)}, u32[]{:S(2)}) %collective-permute-start.7) | collective-permute-done | bytes 131104 | tf_op jit(solution)/shard_map/ppermute | solution.py:521
  25.9 1.6 %collective-permute-start.12 = (f32[8,16,512]{2,1,0:T(8,128)S(1)}, f32[8,16,512]{2,1,0:T(8,128)S(1)}, u32[]{:S(2)}, u32[]{:S(2)}) collective-permute-start(f32[8,16,512]{2,1,0:T(8,128)S(1)} %pad_maximum_fusion.2.refs_4_), channel_id=1, source_target_pairs={{0,4},{1,5},{2,6},{3,7},{4,0},{5,1},{6,2},{7,3},{8,12},{9,13},{10,... | collective-permute-start | bytes 786440 | tf_op jit(solution)/shard_map/ppermute | solution.py:521
  27.5 0.5 collective-permute-start.13
  28.0 5.8 %collective-permute-done.8.refs_1_ = f32[8,16,512]{2,1,0:T(8,128)S(1)} collective-permute-done((f32[8,16,512]{2,1,0:T(8,128)S(1)}, f32[8,16,512]{2,1,0:T(8,128)S(1)}, u32[]{:S(2)}, u32[]{:S(2)}) %collective-permute-start.8) | collective-permute-done | bytes 262176 | tf_op jit(solution)/shard_map/ppermute | solution.py:521
  33.9 0.4 collective-permute-start.14
  34.3 1.0 %collective-permute-done.10.refs_3_ = f32[8,16,512]{2,1,0:T(8,128)S(1)} collective-permute-done((f32[8,16,512]{2,1,0:T(8,128)S(1)}, f32[8,16,512]{2,1,0:T(8,128)S(1)}, u32[]{:S(2)}, u32[]{:S(2)}) %collective-permute-start.10) | collective-permute-done | bytes 262176 | tf_op jit(solution)/shard_map/ppermute | solution.py:521
  35.3 0.4 collective-permute-done.14.refs_7_
  35.7 9.3 %shard_map.51 = (bf16[8,2,4,32,512]{4,3,2,1,0:T(8,128)(2,1)S(1)}, f32[256,128]{1,0:T(8,128)S(1)}, f32[8,4,8,128]{3,2,1,0:T(8,128)}, f32[4,64,128]{2,1,0:T(8,128)S(1)}) custom-call(f32[8,4,8,128]{3,2,1,0:T(8,128)S(1)} %bitcast.16, f32[8,16,512]{2,1,0:T(8,128)S(1)} %pad_maximum_fusion.1.refs_0_, f32[8,16,512]{2,1,0:T(8,128)S(1)} %collective-permute-done.8.refs_1_, ...), custom_call_target="tpu_custom_call" | custom-call | flops 12000000000 | tf_op jit(solution)/shard_map/pallas_call | solution.py:506
  44.9 2.8 %all-to-all-start.1 = ((f32[32,8,128]{2,1,0:T(8,128)}), f32[32,8,128]{2,1,0:T(8,128)S(1)}, u32[]{:S(2)}, u32[]{:S(2)}) async-start(f32[32,8,128]{2,1,0:T(8,128)} %bitcast.4), calls=%async_computation.1 | async-start | bytes 262144 | tf_op jit(solution)/shard_map/all_to_all | solution.py:583
  47.7 1.3 %collective-permute-start.17 = (f32[1,64,128]{2,1,0:T(8,128)S(1)}, f32[1,64,128]{2,1,0:T(8,128)S(1)}, u32[]{:S(2)}, u32[]{:S(2)}) collective-permute-start(f32[1,64,128]{2,1,0:T(8,128)S(1)} %get-tuple-element.57), channel_id=1, source_target_pairs={{0,3},{1,2},{2,1},{3,0},{4,7},{5,6},{6,5},{7,4},{8,11},{9,10},{10,... | collective-permute-start | bytes 98312 | tf_op jit(solution)/shard_map/ppermute | solution.py:521
  49.0 0.3 collective-permute-start.16
  49.4 0.3 collective-permute-start.15
  49.6 2.8 %shard_map.52 = f32[8,4,4,640]{3,2,1,0:T(4,128)} custom-call(bf16[8,2,4,32,512]{4,3,2,1,0:T(8,128)(2,1)S(1)} %get-tuple-element.34.samples_ref, f32[256,128]{1,0:T(8,128)S(1)} %get-tuple-element.35.vectors_ref), custom_call_target="tpu_custom_call" | custom-call | flops 2000000000 | tf_op jit(solution)/shard_map/pallas_call | solution.py:506
  52.4 0.7 collective-permute-done.16
  53.1 2.6 %all-to-all-done.1 = f32[32,8,128]{2,1,0:T(8,128)S(1)} async-done(((f32[32,8,128]{2,1,0:T(8,128)}), f32[32,8,128]{2,1,0:T(8,128)S(1)}, u32[]{:S(2)}, u32[]{:S(2)}) %all-to-all-start.1) | async-done | bytes 131104 | tf_op jit(solution)/shard_map/all_to_all | solution.py:583
  55.8 0.7 collective-permute-start.20
  56.5 0.5 shard_map.53
  57.1 0.9 collective-permute-start.18
  58.0 0.3 collective-permute-done.22
  58.3 1.2 %collective-permute-start.25 = (f32[72,128]{1,0:T(8,128)S(1)}, f32[72,128]{1,0:T(8,128)S(1)}, u32[]{:S(2)}, u32[]{:S(2)}) collective-permute-start(f32[72,128]{1,0:T(8,128)S(1)} %add.36), channel_id=1, source_target_pairs={{0,6},{1,7},{2,4},{3,5},{4,2},{5,3},{6,0},{7,1},{8,14},{9,15},{10,... | collective-permute-start | bytes 110600 | tf_op jit(solution)/shard_map/ppermute | solution.py:521
  59.5 1.0 %collective-permute-start.24 = (f32[72,128]{1,0:T(8,128)S(1)}, f32[72,128]{1,0:T(8,128)S(1)}, u32[]{:S(2)}, u32[]{:S(2)}) collective-permute-start(f32[72,128]{1,0:T(8,128)S(1)} %add.36), channel_id=1, source_target_pairs={{0,4},{1,5},{2,6},{3,7},{4,0},{5,1},{6,2},{7,3},{8,12},{9,13},{10,... | collective-permute-start | bytes 110600 | tf_op jit(solution)/shard_map/ppermute | solution.py:521
  60.5 1.3 %collective-permute-start.23 = (f32[72,128]{1,0:T(8,128)S(1)}, f32[72,128]{1,0:T(8,128)S(1)}, u32[]{:S(2)}, u32[]{:S(2)}) collective-permute-start(f32[72,128]{1,0:T(8,128)S(1)} %add.36), channel_id=1, source_target_pairs={{0,2},{1,3},{2,0},{3,1},{4,6},{5,7},{6,4},{7,5},{8,10},{9,11},{10,... | collective-permute-start | bytes 110600 | tf_op jit(solution)/shard_map/ppermute | solution.py:521
  61.8 1.9 %collective-permute-start.21 = (f32[8,32,128]{2,1,0:T(8,128)S(1)}, f32[8,32,128]{2,1,0:T(8,128)S(1)}, u32[]{:S(2)}, u32[]{:S(2)}) collective-permute-start(f32[8,32,128]{2,1,0:T(8,128)S(1)} %pad_maximum_fusion.8), channel_id=1, source_target_pairs={{0,16},{1,17},{2,18},{3,19},{4,20},{5,21},{6,22},{7,23},{8,24},{9,... | collective-permute-start | bytes 393224 | tf_op jit(solution)/shard_map/ppermute | solution.py:521
  63.7 0.7 collective-permute-done.23
  64.5 2.1 %collective-permute-start.28 = (f32[72,128]{1,0:T(8,128)S(1)}, f32[72,128]{1,0:T(8,128)S(1)}, u32[]{:S(2)}, u32[]{:S(2)}) collective-permute-start(f32[72,128]{1,0:T(8,128)S(1)} %add_add_fusion.1), channel_id=1, source_target_pairs={{0,24},{1,25},{2,26},{3,27},{4,28},{5,29},{6,30},{7,31},{8,16},{9,... | collective-permute-start | bytes 110600 | tf_op jit(solution)/shard_map/ppermute | solution.py:521
  66.6 0.8 collective-permute-start.27
  67.3 1.6 %collective-permute-start.26 = (f32[72,128]{1,0:T(8,128)S(1)}, f32[72,128]{1,0:T(8,128)S(1)}, u32[]{:S(2)}, u32[]{:S(2)}) collective-permute-start(f32[72,128]{1,0:T(8,128)S(1)} %add_add_fusion.1), channel_id=1, source_target_pairs={{0,8},{1,9},{2,10},{3,11},{4,12},{5,13},{6,14},{7,15},{8,0},{9,1},... | collective-permute-start | bytes 110600 | tf_op jit(solution)/shard_map/ppermute | solution.py:521
  69.0 0.5 collective-permute-start.19
  69.4 1.1 %collective-permute-done.28 = f32[72,128]{1,0:T(8,128)S(1)} collective-permute-done((f32[72,128]{1,0:T(8,128)S(1)}, f32[72,128]{1,0:T(8,128)S(1)}, u32[]{:S(2)}, u32[]{:S(2)}) %collective-permute-start.28) | collective-permute-done | bytes 36896 | tf_op jit(solution)/shard_map/ppermute | solution.py:521
  70.6 2.9 %collective-permute-done.27 = f32[72,128]{1,0:T(8,128)S(1)} collective-permute-done((f32[72,128]{1,0:T(8,128)S(1)}, f32[72,128]{1,0:T(8,128)S(1)}, u32[]{:S(2)}, u32[]{:S(2)}) %collective-permute-start.27) | collective-permute-done | bytes 36896 | tf_op jit(solution)/shard_map/ppermute | solution.py:521
  73.6 1.8 %collective-permute-done.19 = f32[8,32,128]{2,1,0:T(8,128)S(1)} collective-permute-done((f32[8,32,128]{2,1,0:T(8,128)S(1)}, f32[8,32,128]{2,1,0:T(8,128)S(1)}, u32[]{:S(2)}, u32[]{:S(2)}) %collective-permute-start.19) | collective-permute-done | bytes 131104 | tf_op jit(solution)/shard_map/ppermute | solution.py:521
  75.5 3.1 %all-to-all-start.2 = ((f32[32,4,640]{2,1,0:T(4,128)}), f32[32,4,640]{2,1,0:T(4,128)S(1)}, u32[]{:S(2)}, u32[]{:S(2)}) async-start(f32[32,4,640]{2,1,0:T(4,128)} %bitcast.6), calls=%async_computation.2 | async-start | bytes 655360 | tf_op jit(solution)/shard_map/all_to_all | solution.py:583
  78.6 1.8 %collective-permute-start.30 = (f32[16,32,128]{2,1,0:T(8,128)S(1)}, f32[16,32,128]{2,1,0:T(8,128)S(1)}, u32[]{:S(2)}, u32[]{:S(2)}) collective-permute-start(f32[16,32,128]{2,1,0:T(8,128)S(1)} %pad_maximum_fusion.3), channel_id=1, source_target_pairs={{0,4},{1,5},{2,6},{3,7},{4,0},{5,1},{6,2},{7,3},{8,12},{9,13},{10,... | collective-permute-start | bytes 786440 | tf_op jit(solution)/shard_map/ppermute | solution.py:521
  80.5 1.5 %collective-permute-start.31 = (f32[16,32,128]{2,1,0:T(8,128)S(1)}, f32[16,32,128]{2,1,0:T(8,128)S(1)}, u32[]{:S(2)}, u32[]{:S(2)}) collective-permute-start(f32[16,32,128]{2,1,0:T(8,128)S(1)} %pad_maximum_fusion.4), channel_id=1, source_target_pairs={{0,8},{1,9},{2,10},{3,11},{4,12},{5,13},{6,14},{7,15},{8,0},{9,1},... | collective-permute-start | bytes 786440 | tf_op jit(solution)/shard_map/ppermute | solution.py:521
  81.9 6.4 %shard_map.54 = (f32[128,128]{1,0:T(8,128)S(1)}, f32[128,128]{1,0:T(8,128)S(1)}, s32[1]{0:T(128)}) custom-call(f32[72,128]{1,0:T(8,128)S(1)} %add_add_fusion.gram_ref, f32[72,128]{1,0:T(8,128)S(1)} %collective-permute-done.29.other_ref), custom_call_target="tpu_custom_call" | custom-call | flops 12000000000 | tf_op jit(solution)/shard_map/pallas_call | solution.py:506
  89.0 0.2 conditional.1
  89.3 5.0 %shard_map.55.both_ref = f32[128,128]{1,0:T(8,128)S(1)} custom-call(f32[128,128]{1,0:T(8,128)S(1)} %get-tuple-element.60.gram_ref, f32[128,128]{1,0:T(8,128)S(1)} %get-tuple-element.46.inverse_ref), custom_call_target="tpu_custom_call" | custom-call | tf_op jit(solution)/shard_map/pallas_call | solution.py:506
  94.5 3.6 %shard_map.56 = (f32[32,512]{1,0:T(8,128)}, f32[256,128]{1,0:T(8,128)}) custom-call(f32[128,640]{1,0:T(8,128)S(1)} %reshape.51.images_ref, f32[128,128]{1,0:T(8,128)S(1)} %shard_map.55.both_ref, f32[32,512]{1,0:T(8,128)S(1)} %copy-done, s32[32,512]{1,0:T(8,128)S(1)} %copy-done.1, f32[512,128]{1,0:T(8,128)S(1)} %bitcast.15, f32[512,128]{1,0:T(8,128)S(1)} %bitcast.18, ...), custom_call_target="tpu_custom_call" | custom-call | flops 5000000000 | tf_op jit(solution)/shard_map/pallas_call | solution.py:506
  (45 shorter events, 0.8 us)
Async XLA Ops:
  1.5 9.7 %collective-permute-start.5 = (f32[1,32,512]{2,1,0:T(8,128)S(1)}, f32[1,32,512]{2,1,0:T(8,128)S(1)}, u32[]{:S(2)}, u32[]{:S(2)}) collective-permute-start(f32[1,32,512]{2,1,0:T(8,128)S(1)} %multiply_bitcast_fusion), channel_id=1, source_target_pairs={{0,16},{1,17},{2,18},{3,19},{4,20},{5,21},{6,22},{7,23},{8,24},{9,... | collective-permute-start | bytes 196616 | tf_op jit(solution)/shard_map/ppermute | solution.py:521
  5.6 0.9 copy-start.2
  7.4 12.1 %all-to-all-start = ((f32[32,8,128]{2,1,0:T(8,128)}), f32[32,8,128]{2,1,0:T(8,128)S(1)}, u32[]{:S(2)}, u32[]{:S(2)}) async-start(f32[32,8,128]{2,1,0:T(8,128)} %bitcast.1), calls=%async_computation | async-start | bytes 262144 | tf_op jit(solution)/shard_map/all_to_all | solution.py:583
  11.3 7.7 %collective-permute-start.6 = (f32[2,32,512]{2,1,0:T(8,128)S(1)}, f32[2,32,512]{2,1,0:T(8,128)S(1)}, u32[]{:S(2)}, u32[]{:S(2)}) collective-permute-start(f32[2,32,512]{2,1,0:T(8,128)S(1)} %pad_maximum_fusion.5), channel_id=1, source_target_pairs={{0,8},{1,9},{2,10},{3,11},{4,12},{5,13},{6,14},{7,15},{8,0},{9,1},... | collective-permute-start | bytes 393224 | tf_op jit(solution)/shard_map/ppermute | solution.py:521
  19.5 6.1 %collective-permute-start.7 = (f32[4,16,512]{2,1,0:T(8,128)S(1)}, f32[4,16,512]{2,1,0:T(8,128)S(1)}, u32[]{:S(2)}, u32[]{:S(2)}) collective-permute-start(f32[4,16,512]{2,1,0:T(8,128)S(1)} %get-tuple-element.53), channel_id=1, source_target_pairs={{0,4},{1,5},{2,6},{3,7},{4,0},{5,1},{6,2},{7,3},{8,12},{9,13},{10,... | collective-permute-start | bytes 393224 | tf_op jit(solution)/shard_map/ppermute | solution.py:521
  20.6 5.2 %collective-permute-start.11 = (f32[4,16,512]{2,1,0:T(8,128)S(1)}, f32[4,16,512]{2,1,0:T(8,128)S(1)}, u32[]{:S(2)}, u32[]{:S(2)}) collective-permute-start(f32[4,16,512]{2,1,0:T(8,128)S(1)} %get-tuple-element.52), channel_id=1, source_target_pairs={{0,2},{1,3},{2,0},{3,1},{4,6},{5,7},{6,4},{7,5},{8,10},{9,11},{10,... | collective-permute-start | bytes 393224 | tf_op jit(solution)/shard_map/ppermute | solution.py:521
  25.6 8.1 %collective-permute-start.8 = (f32[8,16,512]{2,1,0:T(8,128)S(1)}, f32[8,16,512]{2,1,0:T(8,128)S(1)}, u32[]{:S(2)}, u32[]{:S(2)}) collective-permute-start(f32[8,16,512]{2,1,0:T(8,128)S(1)} %pad_maximum_fusion.1.refs_0_), channel_id=1, source_target_pairs={{0,2},{1,3},{2,0},{3,1},{4,6},{5,7},{6,4},{7,5},{8,10},{9,11},{10,... | collective-permute-start | bytes 786440 | tf_op jit(solution)/shard_map/ppermute | solution.py:521
  25.9 8.0 %collective-permute-start.12 = (f32[8,16,512]{2,1,0:T(8,128)S(1)}, f32[8,16,512]{2,1,0:T(8,128)S(1)}, u32[]{:S(2)}, u32[]{:S(2)}) collective-permute-start(f32[8,16,512]{2,1,0:T(8,128)S(1)} %pad_maximum_fusion.2.refs_4_), channel_id=1, source_target_pairs={{0,4},{1,5},{2,6},{3,7},{4,0},{5,1},{6,2},{7,3},{8,12},{9,13},{10,... | collective-permute-start | bytes 786440 | tf_op jit(solution)/shard_map/ppermute | solution.py:521
  27.4 6.8 %collective-permute-start.9 = (f32[8,16,512]{2,1,0:T(8,128)S(1)}, f32[8,16,512]{2,1,0:T(8,128)S(1)}, u32[]{:S(2)}, u32[]{:S(2)}) collective-permute-start(f32[8,16,512]{2,1,0:T(8,128)S(1)} %pad_maximum_fusion.1.refs_0_), channel_id=1, source_target_pairs={{0,1},{1,0},{2,3},{3,2},{4,5},{5,4},{6,7},{7,6},{8,9},{9,8},{10,11... | collective-permute-start | bytes 786440 | tf_op jit(solution)/shard_map/ppermute | solution.py:521
  27.5 6.8 %collective-permute-start.13 = (f32[8,16,512]{2,1,0:T(8,128)S(1)}, f32[8,16,512]{2,1,0:T(8,128)S(1)}, u32[]{:S(2)}, u32[]{:S(2)}) collective-permute-start(f32[8,16,512]{2,1,0:T(8,128)S(1)} %pad_maximum_fusion.2.refs_4_), channel_id=1, source_target_pairs={{0,1},{1,0},{2,3},{3,2},{4,5},{5,4},{6,7},{7,6},{8,9},{9,8},{10,11... | collective-permute-start | bytes 786440 | tf_op jit(solution)/shard_map/ppermute | solution.py:521
  33.8 1.5 %collective-permute-start.10 = (f32[8,16,512]{2,1,0:T(8,128)S(1)}, f32[8,16,512]{2,1,0:T(8,128)S(1)}, u32[]{:S(2)}, u32[]{:S(2)}) collective-permute-start(f32[8,16,512]{2,1,0:T(8,128)S(1)} %collective-permute-done.8.refs_1_), channel_id=1, source_target_pairs={{0,1},{1,0},{2,3},{3,2},{4,5},{5,4},{6,7},{7,6},{8,9},{9,8},{10,11... | collective-permute-start | bytes 786440 | tf_op jit(solution)/shard_map/ppermute | solution.py:521
  33.9 1.8 %collective-permute-start.14 = (f32[8,16,512]{2,1,0:T(8,128)S(1)}, f32[8,16,512]{2,1,0:T(8,128)S(1)}, u32[]{:S(2)}, u32[]{:S(2)}) collective-permute-start(f32[8,16,512]{2,1,0:T(8,128)S(1)} %collective-permute-done.12.refs_5_), channel_id=1, source_target_pairs={{0,1},{1,0},{2,3},{3,2},{4,5},{5,4},{6,7},{7,6},{8,9},{9,8},{10,11... | collective-permute-start | bytes 786440 | tf_op jit(solution)/shard_map/ppermute | solution.py:521
  44.9 10.8 %all-to-all-start.1 = ((f32[32,8,128]{2,1,0:T(8,128)}), f32[32,8,128]{2,1,0:T(8,128)S(1)}, u32[]{:S(2)}, u32[]{:S(2)}) async-start(f32[32,8,128]{2,1,0:T(8,128)} %bitcast.4), calls=%async_computation.1 | async-start | bytes 262144 | tf_op jit(solution)/shard_map/all_to_all | solution.py:583
  47.7 4.7 %collective-permute-start.17 = (f32[1,64,128]{2,1,0:T(8,128)S(1)}, f32[1,64,128]{2,1,0:T(8,128)S(1)}, u32[]{:S(2)}, u32[]{:S(2)}) collective-permute-start(f32[1,64,128]{2,1,0:T(8,128)S(1)} %get-tuple-element.57), channel_id=1, source_target_pairs={{0,3},{1,2},{2,1},{3,0},{4,7},{5,6},{6,5},{7,4},{8,11},{9,10},{10,... | collective-permute-start | bytes 98312 | tf_op jit(solution)/shard_map/ppermute | solution.py:521
  49.0 4.1 %collective-permute-start.16 = (f32[1,64,128]{2,1,0:T(8,128)S(1)}, f32[1,64,128]{2,1,0:T(8,128)S(1)}, u32[]{:S(2)}, u32[]{:S(2)}) collective-permute-start(f32[1,64,128]{2,1,0:T(8,128)S(1)} %get-tuple-element.58), channel_id=1, source_target_pairs={{0,2},{1,3},{2,0},{3,1},{4,6},{5,7},{6,4},{7,5},{8,10},{9,11},{10,... | collective-permute-start | bytes 98312 | tf_op jit(solution)/shard_map/ppermute | solution.py:521
  49.4 3.8 %collective-permute-start.15 = (f32[1,64,128]{2,1,0:T(8,128)S(1)}, f32[1,64,128]{2,1,0:T(8,128)S(1)}, u32[]{:S(2)}, u32[]{:S(2)}) collective-permute-start(f32[1,64,128]{2,1,0:T(8,128)S(1)} %get-tuple-element.59), channel_id=1, source_target_pairs={{0,1},{1,0},{2,3},{3,2},{4,5},{5,4},{6,7},{7,6},{8,9},{9,8},{10,11... | collective-permute-start | bytes 98312 | tf_op jit(solution)/shard_map/ppermute | solution.py:521
  49.6 6.9 %copy-start.3 = (f32[1,256,128]{2,1,0:T(8,128)S(1)}, f32[1,256,128]{2,1,0:T(8,128)}, u32[]{:S(2)}) copy-start(f32[1,256,128]{2,1,0:T(8,128)} %param.7) | copy-start | bytes 393220
  55.8 6.0 %collective-permute-start.20 = (f32[4,32,128]{2,1,0:T(8,128)S(1)}, f32[4,32,128]{2,1,0:T(8,128)S(1)}, u32[]{:S(2)}, u32[]{:S(2)}) collective-permute-start(f32[4,32,128]{2,1,0:T(8,128)S(1)} %get-tuple-element.54), channel_id=1, source_target_pairs={{0,4},{1,5},{2,6},{3,7},{4,0},{5,1},{6,2},{7,3},{8,12},{9,13},{10,... | collective-permute-start | bytes 196616 | tf_op jit(solution)/shard_map/ppermute | solution.py:521
  57.0 1.3 %collective-permute-start.22 = (f32[72,128]{1,0:T(8,128)S(1)}, f32[72,128]{1,0:T(8,128)S(1)}, u32[]{:S(2)}, u32[]{:S(2)}) collective-permute-start(f32[72,128]{1,0:T(8,128)S(1)} %get-tuple-element.40), channel_id=1, source_target_pairs={{0,1},{1,0},{2,3},{3,2},{4,5},{5,4},{6,7},{7,6},{8,9},{9,8},{10,11... | collective-permute-start | bytes 110600 | tf_op jit(solution)/shard_map/ppermute | solution.py:521
  57.1 11.9 %collective-permute-start.18 = (f32[4,32,128]{2,1,0:T(8,128)S(1)}, f32[4,32,128]{2,1,0:T(8,128)S(1)}, u32[]{:S(2)}, u32[]{:S(2)}) collective-permute-start(f32[4,32,128]{2,1,0:T(8,128)S(1)} %get-tuple-element.55), channel_id=1, source_target_pairs={{0,16},{1,17},{2,18},{3,19},{4,20},{5,21},{6,22},{7,23},{8,24},{9,... | collective-permute-start | bytes 196616 | tf_op jit(solution)/shard_map/ppermute | solution.py:521
  58.3 5.4 %collective-permute-start.25 = (f32[72,128]{1,0:T(8,128)S(1)}, f32[72,128]{1,0:T(8,128)S(1)}, u32[]{:S(2)}, u32[]{:S(2)}) collective-permute-start(f32[72,128]{1,0:T(8,128)S(1)} %add.36), channel_id=1, source_target_pairs={{0,6},{1,7},{2,4},{3,5},{4,2},{5,3},{6,0},{7,1},{8,14},{9,15},{10,... | collective-permute-start | bytes 110600 | tf_op jit(solution)/shard_map/ppermute | solution.py:521
  59.5 4.2 %collective-permute-start.24 = (f32[72,128]{1,0:T(8,128)S(1)}, f32[72,128]{1,0:T(8,128)S(1)}, u32[]{:S(2)}, u32[]{:S(2)}) collective-permute-start(f32[72,128]{1,0:T(8,128)S(1)} %add.36), channel_id=1, source_target_pairs={{0,4},{1,5},{2,6},{3,7},{4,0},{5,1},{6,2},{7,3},{8,12},{9,13},{10,... | collective-permute-start | bytes 110600 | tf_op jit(solution)/shard_map/ppermute | solution.py:521
  60.5 4.0 %collective-permute-start.23 = (f32[72,128]{1,0:T(8,128)S(1)}, f32[72,128]{1,0:T(8,128)S(1)}, u32[]{:S(2)}, u32[]{:S(2)}) collective-permute-start(f32[72,128]{1,0:T(8,128)S(1)} %add.36), channel_id=1, source_target_pairs={{0,2},{1,3},{2,0},{3,1},{4,6},{5,7},{6,4},{7,5},{8,10},{9,11},{10,... | collective-permute-start | bytes 110600 | tf_op jit(solution)/shard_map/ppermute | solution.py:521
  61.8 11.8 %collective-permute-start.21 = (f32[8,32,128]{2,1,0:T(8,128)S(1)}, f32[8,32,128]{2,1,0:T(8,128)S(1)}, u32[]{:S(2)}, u32[]{:S(2)}) collective-permute-start(f32[8,32,128]{2,1,0:T(8,128)S(1)} %pad_maximum_fusion.8), channel_id=1, source_target_pairs={{0,16},{1,17},{2,18},{3,19},{4,20},{5,21},{6,22},{7,23},{8,24},{9,... | collective-permute-start | bytes 393224 | tf_op jit(solution)/shard_map/ppermute | solution.py:521
  64.5 6.1 %collective-permute-start.28 = (f32[72,128]{1,0:T(8,128)S(1)}, f32[72,128]{1,0:T(8,128)S(1)}, u32[]{:S(2)}, u32[]{:S(2)}) collective-permute-start(f32[72,128]{1,0:T(8,128)S(1)} %add_add_fusion.1), channel_id=1, source_target_pairs={{0,24},{1,25},{2,26},{3,27},{4,28},{5,29},{6,30},{7,31},{8,16},{9,... | collective-permute-start | bytes 110600 | tf_op jit(solution)/shard_map/ppermute | solution.py:521
  66.6 7.0 %collective-permute-start.27 = (f32[72,128]{1,0:T(8,128)S(1)}, f32[72,128]{1,0:T(8,128)S(1)}, u32[]{:S(2)}, u32[]{:S(2)}) collective-permute-start(f32[72,128]{1,0:T(8,128)S(1)} %add_add_fusion.1), channel_id=1, source_target_pairs={{0,16},{1,17},{2,18},{3,19},{4,20},{5,21},{6,22},{7,23},{8,24},{9,... | collective-permute-start | bytes 110600 | tf_op jit(solution)/shard_map/ppermute | solution.py:521
  67.3 6.2 %collective-permute-start.26 = (f32[72,128]{1,0:T(8,128)S(1)}, f32[72,128]{1,0:T(8,128)S(1)}, u32[]{:S(2)}, u32[]{:S(2)}) collective-permute-start(f32[72,128]{1,0:T(8,128)S(1)} %add_add_fusion.1), channel_id=1, source_target_pairs={{0,8},{1,9},{2,10},{3,11},{4,12},{5,13},{6,14},{7,15},{8,0},{9,1},... | collective-permute-start | bytes 110600 | tf_op jit(solution)/shard_map/ppermute | solution.py:521
  69.0 6.5 %collective-permute-start.19 = (f32[8,32,128]{2,1,0:T(8,128)S(1)}, f32[8,32,128]{2,1,0:T(8,128)S(1)}, u32[]{:S(2)}, u32[]{:S(2)}) collective-permute-start(f32[8,32,128]{2,1,0:T(8,128)S(1)} %pad_maximum_fusion.7), channel_id=1, source_target_pairs={{0,8},{1,9},{2,10},{3,11},{4,12},{5,13},{6,14},{7,15},{8,0},{9,1},... | collective-permute-start | bytes 393224 | tf_op jit(solution)/shard_map/ppermute | solution.py:521
  73.5 2.0 %collective-permute-start.29 = (f32[72,128]{1,0:T(8,128)S(1)}, f32[72,128]{1,0:T(8,128)S(1)}, u32[]{:S(2)}, u32[]{:S(2)}) collective-permute-start(f32[72,128]{1,0:T(8,128)S(1)} %add_add_fusion.gram_ref), channel_id=1, source_target_pairs={{0,1},{1,0},{2,3},{3,2},{4,5},{5,4},{6,7},{7,6},{8,9},{9,8},{10,11... | collective-permute-start | bytes 110600 | tf_op jit(solution)/shard_map/ppermute | solution.py:521
  75.5 18.8 %all-to-all-start.2 = ((f32[32,4,640]{2,1,0:T(4,128)}), f32[32,4,640]{2,1,0:T(4,128)S(1)}, u32[]{:S(2)}, u32[]{:S(2)}) async-start(f32[32,4,640]{2,1,0:T(4,128)} %bitcast.6), calls=%async_computation.2 | async-start | bytes 655360 | tf_op jit(solution)/shard_map/all_to_all | solution.py:583
  78.6 15.8 %collective-permute-start.30 = (f32[16,32,128]{2,1,0:T(8,128)S(1)}, f32[16,32,128]{2,1,0:T(8,128)S(1)}, u32[]{:S(2)}, u32[]{:S(2)}) collective-permute-start(f32[16,32,128]{2,1,0:T(8,128)S(1)} %pad_maximum_fusion.3), channel_id=1, source_target_pairs={{0,4},{1,5},{2,6},{3,7},{4,0},{5,1},{6,2},{7,3},{8,12},{9,13},{10,... | collective-permute-start | bytes 786440 | tf_op jit(solution)/shard_map/ppermute | solution.py:521
  80.5 14.0 %collective-permute-start.31 = (f32[16,32,128]{2,1,0:T(8,128)S(1)}, f32[16,32,128]{2,1,0:T(8,128)S(1)}, u32[]{:S(2)}, u32[]{:S(2)}) collective-permute-start(f32[16,32,128]{2,1,0:T(8,128)S(1)} %pad_maximum_fusion.4), channel_id=1, source_target_pairs={{0,8},{1,9},{2,10},{3,11},{4,12},{5,13},{6,14},{7,15},{8,0},{9,1},... | collective-permute-start | bytes 786440 | tf_op jit(solution)/shard_map/ppermute | solution.py:521
  89.0 5.5 %copy-start = (f32[32,512]{1,0:T(8,128)S(1)}, f32[32,512]{1,0:T(8,128)}, u32[]{:S(2)}) copy-start(f32[32,512]{1,0:T(8,128)} %kspace_ref.1) | copy-start | bytes 196612
  89.0 5.5 %copy-start.1 = (s32[32,512]{1,0:T(8,128)S(1)}, s32[32,512]{1,0:T(8,128)}, u32[]{:S(2)}) copy-start(s32[32,512]{1,0:T(8,128)} %mask_ref.1) | copy-start | bytes 196612

commit v17 on v16

--- a/solution.py
+++ b/solution.py
@@ -553,9 +553,9 @@
     mask = devices // 2
     while mask > groups:
         near, masks = gather_round(near, masks, [mask], devices, AXES)
+        if len(masks) == 2:
+            basis = to_all(after(basis, near))
         mask //= 2
-    basis = to_all(basis)
-    near = after(near, basis)
     half = near.shape[1] // 2
     halves = []
     for part, ways in (
@@ -563,6 +563,8 @@
         (near[:, half:], (groups // 2, groups)),
     ):
         part, order = gather_round(part, masks, [ways[0]], devices, AXES)
+        if halves:
+            part = after(part, basis)
         pieces = [(part, order)]
         mask = ways[1]
         rest = groups // 4
@@ -614,6 +616,7 @@
         total = total + terms[0]
         if len(terms) == 3:
             total = total + (terms[1] + terms[2])
+        images = after(images, terms[0])
         if step < len(ways[0]) - 1:
             advance()
             step += 1
@@ -621,7 +624,7 @@
         advance()
         step += 1
     other = exchange(total, devices, 1, AXES)
-    *parts, total, other, images = lax.optimization_barrier((*parts, total, other, images))
+    *parts, total, other = lax.optimization_barrier((*parts, total, other))
     pieces = []
     for i in range(2):
         mask = ways[i][-1]

time: 98.4 us -> 99 us (level)
  starting transfers between devices: 38.2 us -> 41.7 us
  waiting for transfers between devices: 27.5 us -> 24.8 us
    all_to_all x3, starting transfers between devices: 9.68 us -> 13.3 us  [to_all(): return lax.all_to_all(pieces, axes, 0, 0, tiled=True)]
    ppermute x27, waiting for transfers between devices: 24.5 us -> 21 us  [exchange(): return lax.ppermute(block, axes, [(i, i ^ mask) for i in range(devices)])]
  transfers between devices with their start and end apart: 30 -> 30, of which waited for: 14 -> 13; matrix products, arithmetic and copies ran while one was open for 0% -> 0% of each run, Pallas kernels for 16% -> 16%
where the time goes in v17:
time: 99 us; the launch traced here: 98.7 us
  starting transfers between devices  41.7 us (42%)
  Pallas kernels  28.4 us (29%)
  waiting for transfers between devices  24.8 us (25%)
  between operations  1.55 us (2%)
  local copies, waits for them, and re-layouts  1.07 us (1%)
  other arithmetic  1.04 us (1%)
    pallas_call x7, Pallas kernels, call(): pl.pallas_call(kernel, out_shape=[jax.ShapeDtypeStruct(shape, kind) for s...  28.4 us
    ppermute x27, starting transfers between devices, exchange(): return lax.ppermute(block, axes, [(i, i ^ mask) for i in range(devices)])  28.4 us
    ppermute x27, waiting for transfers between devices, exchange(): return lax.ppermute(block, axes, [(i, i ^ mask) for i in range(devices)])  21 us
    all_to_all x3, starting transfers between devices, to_all(): return lax.all_to_all(pieces, axes, 0, 0, tiled=True)  13.3 us
    all_to_all x3, waiting for transfers between devices, to_all(): return lax.all_to_all(pieces, axes, 0, 0, tiled=True)  3.82 us
  transfers between devices with their start and end apart: 30, of which 13 were waited for; matrix products, arithmetic and copies ran while one was open for 0% of the time, Pallas kernels for 16%

profile of v17, /device:TPU:0, one launch (start us, length us, event | category | flops | bytes accessed | tf_op | source)
XLA Modules:
  0.0 98.7 jit_solution(16426094972886888973)
XLA Ops:
  0.6 0.9 multiply_bitcast_fusion
  1.5 4.1 %collective-permute-start.5 = (f32[1,32,512]{2,1,0:T(8,128)S(1)}, f32[1,32,512]{2,1,0:T(8,128)S(1)}, u32[]{:S(2)}, u32[]{:S(2)}) collective-permute-start(f32[1,32,512]{2,1,0:T(8,128)S(1)} %multiply_bitcast_fusion), channel_id=1, source_target_pairs={{0,16},{1,17},{2,18},{3,19},{4,20},{5,21},{6,22},{7,23},{8,24},{9,... | collective-permute-start | bytes 196616 | tf_op jit(solution)/shard_map/ppermute | solution.py:521
  5.6 3.6 %collective-permute-done.5 = f32[1,32,512]{2,1,0:T(8,128)S(1)} collective-permute-done((f32[1,32,512]{2,1,0:T(8,128)S(1)}, f32[1,32,512]{2,1,0:T(8,128)S(1)}, u32[]{:S(2)}, u32[]{:S(2)}) %collective-permute-start.5) | collective-permute-done | bytes 65568 | tf_op jit(solution)/shard_map/ppermute | solution.py:521
  9.3 0.6 collective-permute-start.6
  9.9 0.9 copy-done.2
  10.8 0.9 shard_map.50
  11.7 5.6 %all-to-all-start = ((f32[32,8,128]{2,1,0:T(8,128)}), f32[32,8,128]{2,1,0:T(8,128)S(1)}, u32[]{:S(2)}, u32[]{:S(2)}) async-start(f32[32,8,128]{2,1,0:T(8,128)} %bitcast.1), calls=%async_computation | async-start | bytes 262144 | tf_op jit(solution)/shard_map/all_to_all | solution.py:585
  17.4 1.8 %collective-permute-start.11 = (f32[4,16,512]{2,1,0:T(8,128)S(1)}, f32[4,16,512]{2,1,0:T(8,128)S(1)}, u32[]{:S(2)}, u32[]{:S(2)}) collective-permute-start(f32[4,16,512]{2,1,0:T(8,128)S(1)} %get-tuple-element.56), channel_id=1, source_target_pairs={{0,2},{1,3},{2,0},{3,1},{4,6},{5,7},{6,4},{7,5},{8,10},{9,11},{10,... | collective-permute-start | bytes 393224 | tf_op jit(solution)/shard_map/ppermute | solution.py:521
  19.2 1.5 %collective-permute-start.7 = (f32[4,16,512]{2,1,0:T(8,128)S(1)}, f32[4,16,512]{2,1,0:T(8,128)S(1)}, u32[]{:S(2)}, u32[]{:S(2)}) collective-permute-start(f32[4,16,512]{2,1,0:T(8,128)S(1)} %get-tuple-element.57), channel_id=1, source_target_pairs={{0,4},{1,5},{2,6},{3,7},{4,0},{5,1},{6,2},{7,3},{8,12},{9,13},{10,... | collective-permute-start | bytes 393224 | tf_op jit(solution)/shard_map/ppermute | solution.py:521
  20.7 3.5 %collective-permute-done.11 = f32[4,16,512]{2,1,0:T(8,128)S(1)} collective-permute-done((f32[4,16,512]{2,1,0:T(8,128)S(1)}, f32[4,16,512]{2,1,0:T(8,128)S(1)}, u32[]{:S(2)}, u32[]{:S(2)}) %collective-permute-start.11) | collective-permute-done | bytes 131104 | tf_op jit(solution)/shard_map/ppermute | solution.py:521
  24.3 1.3 %all-to-all-done = f32[32,8,128]{2,1,0:T(8,128)S(1)} async-done(((f32[32,8,128]{2,1,0:T(8,128)}), f32[32,8,128]{2,1,0:T(8,128)S(1)}, u32[]{:S(2)}, u32[]{:S(2)}) %all-to-all-start) | async-done | bytes 131104 | tf_op jit(solution)/shard_map/all_to_all | solution.py:585
  25.6 0.5 collective-permute-start.8
  26.1 1.4 %collective-permute-start.12 = (f32[8,16,512]{2,1,0:T(8,128)S(1)}, f32[8,16,512]{2,1,0:T(8,128)S(1)}, u32[]{:S(2)}, u32[]{:S(2)}) collective-permute-start(f32[8,16,512]{2,1,0:T(8,128)S(1)} %pad_maximum_fusion.2.refs_4_), channel_id=1, source_target_pairs={{0,4},{1,5},{2,6},{3,7},{4,0},{5,1},{6,2},{7,3},{8,12},{9,13},{10,... | collective-permute-start | bytes 786440 | tf_op jit(solution)/shard_map/ppermute | solution.py:521
  27.5 0.5 collective-permute-start.13
  28.0 6.1 %collective-permute-done.8.refs_1_ = f32[8,16,512]{2,1,0:T(8,128)S(1)} collective-permute-done((f32[8,16,512]{2,1,0:T(8,128)S(1)}, f32[8,16,512]{2,1,0:T(8,128)S(1)}, u32[]{:S(2)}, u32[]{:S(2)}) %collective-permute-start.8) | collective-permute-done | bytes 262176 | tf_op jit(solution)/shard_map/ppermute | solution.py:521
  34.2 0.4 collective-permute-start.14
  34.6 1.0 %collective-permute-done.10.refs_3_ = f32[8,16,512]{2,1,0:T(8,128)S(1)} collective-permute-done((f32[8,16,512]{2,1,0:T(8,128)S(1)}, f32[8,16,512]{2,1,0:T(8,128)S(1)}, u32[]{:S(2)}, u32[]{:S(2)}) %collective-permute-start.10) | collective-permute-done | bytes 262176 | tf_op jit(solution)/shard_map/ppermute | solution.py:521
  35.6 0.4 collective-permute-done.14.refs_7_
  36.0 9.3 %shard_map.51 = (bf16[8,2,4,32,512]{4,3,2,1,0:T(8,128)(2,1)S(1)}, f32[256,128]{1,0:T(8,128)S(1)}, f32[8,4,8,128]{3,2,1,0:T(8,128)}, f32[4,64,128]{2,1,0:T(8,128)S(1)}) custom-call(f32[8,4,8,128]{3,2,1,0:T(8,128)S(1)} %bitcast.16, f32[8,16,512]{2,1,0:T(8,128)S(1)} %pad_maximum_fusion.1.refs_0_, f32[8,16,512]{2,1,0:T(8,128)S(1)} %collective-permute-done.8.refs_1_, ...), custom_call_target="tpu_custom_call" | custom-call | flops 12000000000 | tf_op jit(solution)/shard_map/pallas_call | solution.py:506
  45.3 4.0 %all-to-all-start.1 = ((f32[32,8,128]{2,1,0:T(8,128)}), f32[32,8,128]{2,1,0:T(8,128)S(1)}, u32[]{:S(2)}, u32[]{:S(2)}) async-start(f32[32,8,128]{2,1,0:T(8,128)} %bitcast.5), calls=%async_computation.1 | async-start | bytes 262144 | tf_op jit(solution)/shard_map/all_to_all | solution.py:585
  49.3 1.6 %collective-permute-start.17 = (f32[1,64,128]{2,1,0:T(8,128)S(1)}, f32[1,64,128]{2,1,0:T(8,128)S(1)}, u32[]{:S(2)}, u32[]{:S(2)}) collective-permute-start(f32[1,64,128]{2,1,0:T(8,128)S(1)} %get-tuple-element.61), channel_id=1, source_target_pairs={{0,3},{1,2},{2,1},{3,0},{4,7},{5,6},{6,5},{7,4},{8,11},{9,10},{10,... | collective-permute-start | bytes 98312 | tf_op jit(solution)/shard_map/ppermute | solution.py:521
  50.9 0.4 collective-permute-start.16
  51.3 2.8 %shard_map.52 = f32[8,4,4,640]{3,2,1,0:T(4,128)} custom-call(bf16[8,2,4,32,512]{4,3,2,1,0:T(8,128)(2,1)S(1)} %get-tuple-element.36.samples_ref, f32[256,128]{1,0:T(8,128)S(1)} %get-tuple-element.37.vectors_ref), custom_call_target="tpu_custom_call" | custom-call | flops 2000000000 | tf_op jit(solution)/shard_map/pallas_call | solution.py:506
  54.1 0.9 collective-permute-done.16
  55.1 2.5 %all-to-all-done.1 = f32[32,8,128]{2,1,0:T(8,128)S(1)} async-done(((f32[32,8,128]{2,1,0:T(8,128)}), f32[32,8,128]{2,1,0:T(8,128)S(1)}, u32[]{:S(2)}, u32[]{:S(2)}) %all-to-all-start.1) | async-done | bytes 131104 | tf_op jit(solution)/shard_map/all_to_all | solution.py:585
  57.6 0.7 collective-permute-start.25
  58.3 0.5 shard_map.53
  58.9 0.9 collective-permute-start.23
  59.8 0.3 collective-permute-done.18
  60.1 1.2 %collective-permute-start.21 = (f32[72,128]{1,0:T(8,128)S(1)}, f32[72,128]{1,0:T(8,128)S(1)}, u32[]{:S(2)}, u32[]{:S(2)}) collective-permute-start(f32[72,128]{1,0:T(8,128)S(1)} %add.36), channel_id=1, source_target_pairs={{0,6},{1,7},{2,4},{3,5},{4,2},{5,3},{6,0},{7,1},{8,14},{9,15},{10,... | collective-permute-start | bytes 110600 | tf_op jit(solution)/shard_map/ppermute | solution.py:521
  61.3 1.0 %collective-permute-start.20 = (f32[72,128]{1,0:T(8,128)S(1)}, f32[72,128]{1,0:T(8,128)S(1)}, u32[]{:S(2)}, u32[]{:S(2)}) collective-permute-start(f32[72,128]{1,0:T(8,128)S(1)} %add.36), channel_id=1, source_target_pairs={{0,4},{1,5},{2,6},{3,7},{4,0},{5,1},{6,2},{7,3},{8,12},{9,13},{10,... | collective-permute-start | bytes 110600 | tf_op jit(solution)/shard_map/ppermute | solution.py:521
  62.3 1.3 %collective-permute-start.19 = (f32[72,128]{1,0:T(8,128)S(1)}, f32[72,128]{1,0:T(8,128)S(1)}, u32[]{:S(2)}, u32[]{:S(2)}) collective-permute-start(f32[72,128]{1,0:T(8,128)S(1)} %add.36), channel_id=1, source_target_pairs={{0,2},{1,3},{2,0},{3,1},{4,6},{5,7},{6,4},{7,5},{8,10},{9,11},{10,... | collective-permute-start | bytes 110600 | tf_op jit(solution)/shard_map/ppermute | solution.py:521
  63.6 1.9 %collective-permute-start.26 = (f32[8,32,128]{2,1,0:T(8,128)S(1)}, f32[8,32,128]{2,1,0:T(8,128)S(1)}, u32[]{:S(2)}, u32[]{:S(2)}) collective-permute-start(f32[8,32,128]{2,1,0:T(8,128)S(1)} %pad_maximum_fusion.8), channel_id=1, source_target_pairs={{0,16},{1,17},{2,18},{3,19},{4,20},{5,21},{6,22},{7,23},{8,24},{9,... | collective-permute-start | bytes 393224 | tf_op jit(solution)/shard_map/ppermute | solution.py:521
  65.6 0.7 collective-permute-done.19
  66.3 2.1 %collective-permute-start.28 = (f32[72,128]{1,0:T(8,128)S(1)}, f32[72,128]{1,0:T(8,128)S(1)}, u32[]{:S(2)}, u32[]{:S(2)}) collective-permute-start(f32[72,128]{1,0:T(8,128)S(1)} %add_add_fusion.1), channel_id=1, source_target_pairs={{0,24},{1,25},{2,26},{3,27},{4,28},{5,29},{6,30},{7,31},{8,16},{9,... | collective-permute-start | bytes 110600 | tf_op jit(solution)/shard_map/ppermute | solution.py:521
  68.4 0.8 collective-permute-start.27
  69.2 1.6 %collective-permute-start.22 = (f32[72,128]{1,0:T(8,128)S(1)}, f32[72,128]{1,0:T(8,128)S(1)}, u32[]{:S(2)}, u32[]{:S(2)}) collective-permute-start(f32[72,128]{1,0:T(8,128)S(1)} %add_add_fusion.1), channel_id=1, source_target_pairs={{0,8},{1,9},{2,10},{3,11},{4,12},{5,13},{6,14},{7,15},{8,0},{9,1},... | collective-permute-start | bytes 110600 | tf_op jit(solution)/shard_map/ppermute | solution.py:521
  70.8 0.5 collective-permute-start.24
  71.3 3.3 %collective-permute-done.22 = f32[72,128]{1,0:T(8,128)S(1)} collective-permute-done((f32[72,128]{1,0:T(8,128)S(1)}, f32[72,128]{1,0:T(8,128)S(1)}, u32[]{:S(2)}, u32[]{:S(2)}) %collective-permute-start.22) | collective-permute-done | bytes 36896 | tf_op jit(solution)/shard_map/ppermute | solution.py:521
  74.6 3.6 %all-to-all-start.2 = ((f32[32,4,640]{2,1,0:T(4,128)}), f32[32,4,640]{2,1,0:T(4,128)S(1)}, u32[]{:S(2)}, u32[]{:S(2)}) async-start(f32[32,4,640]{2,1,0:T(4,128)} %bitcast.4), calls=%async_computation.2 | async-start | bytes 655360 | tf_op jit(solution)/shard_map/all_to_all | solution.py:585
  78.3 0.3 collective-permute-start.29
  78.7 0.9 collective-permute-done.29.other_ref
  79.6 1.8 %collective-permute-start.30 = (f32[16,32,128]{2,1,0:T(8,128)S(1)}, f32[16,32,128]{2,1,0:T(8,128)S(1)}, u32[]{:S(2)}, u32[]{:S(2)}) collective-permute-start(f32[16,32,128]{2,1,0:T(8,128)S(1)} %pad_maximum_fusion.3), channel_id=1, source_target_pairs={{0,4},{1,5},{2,6},{3,7},{4,0},{5,1},{6,2},{7,3},{8,12},{9,13},{10,... | collective-permute-start | bytes 786440 | tf_op jit(solution)/shard_map/ppermute | solution.py:521
  81.3 1.5 %collective-permute-start.31 = (f32[16,32,128]{2,1,0:T(8,128)S(1)}, f32[16,32,128]{2,1,0:T(8,128)S(1)}, u32[]{:S(2)}, u32[]{:S(2)}) collective-permute-start(f32[16,32,128]{2,1,0:T(8,128)S(1)} %pad_maximum_fusion.4), channel_id=1, source_target_pairs={{0,8},{1,9},{2,10},{3,11},{4,12},{5,13},{6,14},{7,15},{8,0},{9,1},... | collective-permute-start | bytes 786440 | tf_op jit(solution)/shard_map/ppermute | solution.py:521
  82.8 6.4 %shard_map.54 = (f32[128,128]{1,0:T(8,128)S(1)}, f32[128,128]{1,0:T(8,128)S(1)}, s32[1]{0:T(128)}) custom-call(f32[72,128]{1,0:T(8,128)S(1)} %add_add_fusion.gram_ref, f32[72,128]{1,0:T(8,128)S(1)} %collective-permute-done.29.other_ref), custom_call_target="tpu_custom_call" | custom-call | flops 12000000000 | tf_op jit(solution)/shard_map/pallas_call | solution.py:506
  89.9 5.0 %shard_map.55.both_ref = f32[128,128]{1,0:T(8,128)S(1)} custom-call(f32[128,128]{1,0:T(8,128)S(1)} %get-tuple-element.64.gram_ref, f32[128,128]{1,0:T(8,128)S(1)} %get-tuple-element.50.inverse_ref), custom_call_target="tpu_custom_call" | custom-call | tf_op jit(solution)/shard_map/pallas_call | solution.py:506
  95.0 0.1 reshape.51.images_ref
  95.1 3.6 %shard_map.56 = (f32[32,512]{1,0:T(8,128)}, f32[256,128]{1,0:T(8,128)}) custom-call(f32[128,640]{1,0:T(8,128)S(1)} %reshape.51.images_ref, f32[128,128]{1,0:T(8,128)S(1)} %shard_map.55.both_ref, f32[32,512]{1,0:T(8,128)S(1)} %copy-done, s32[32,512]{1,0:T(8,128)S(1)} %copy-done.1, f32[512,128]{1,0:T(8,128)S(1)} %bitcast.15, f32[512,128]{1,0:T(8,128)S(1)} %bitcast.18, ...), custom_call_target="tpu_custom_call" | custom-call | flops 5000000000 | tf_op jit(solution)/shard_map/pallas_call | solution.py:506
  (45 shorter events, 0.4 us)
Async XLA Ops:
  1.5 7.8 %collective-permute-start.5 = (f32[1,32,512]{2,1,0:T(8,128)S(1)}, f32[1,32,512]{2,1,0:T(8,128)S(1)}, u32[]{:S(2)}, u32[]{:S(2)}) collective-permute-start(f32[1,32,512]{2,1,0:T(8,128)S(1)} %multiply_bitcast_fusion), channel_id=1, source_target_pairs={{0,16},{1,17},{2,18},{3,19},{4,20},{5,21},{6,22},{7,23},{8,24},{9,... | collective-permute-start | bytes 196616 | tf_op jit(solution)/shard_map/ppermute | solution.py:521
  9.3 8.1 %collective-permute-start.6 = (f32[2,32,512]{2,1,0:T(8,128)S(1)}, f32[2,32,512]{2,1,0:T(8,128)S(1)}, u32[]{:S(2)}, u32[]{:S(2)}) collective-permute-start(f32[2,32,512]{2,1,0:T(8,128)S(1)} %pad_maximum_fusion.5), channel_id=1, source_target_pairs={{0,8},{1,9},{2,10},{3,11},{4,12},{5,13},{6,14},{7,15},{8,0},{9,1},... | collective-permute-start | bytes 393224 | tf_op jit(solution)/shard_map/ppermute | solution.py:521
  9.9 0.9 copy-start.2
  11.7 13.9 %all-to-all-start = ((f32[32,8,128]{2,1,0:T(8,128)}), f32[32,8,128]{2,1,0:T(8,128)S(1)}, u32[]{:S(2)}, u32[]{:S(2)}) async-start(f32[32,8,128]{2,1,0:T(8,128)} %bitcast.1), calls=%async_computation | async-start | bytes 262144 | tf_op jit(solution)/shard_map/all_to_all | solution.py:585
  17.4 6.8 %collective-permute-start.11 = (f32[4,16,512]{2,1,0:T(8,128)S(1)}, f32[4,16,512]{2,1,0:T(8,128)S(1)}, u32[]{:S(2)}, u32[]{:S(2)}) collective-permute-start(f32[4,16,512]{2,1,0:T(8,128)S(1)} %get-tuple-element.56), channel_id=1, source_target_pairs={{0,2},{1,3},{2,0},{3,1},{4,6},{5,7},{6,4},{7,5},{8,10},{9,11},{10,... | collective-permute-start | bytes 393224 | tf_op jit(solution)/shard_map/ppermute | solution.py:521
  19.2 6.3 %collective-permute-start.7 = (f32[4,16,512]{2,1,0:T(8,128)S(1)}, f32[4,16,512]{2,1,0:T(8,128)S(1)}, u32[]{:S(2)}, u32[]{:S(2)}) collective-permute-start(f32[4,16,512]{2,1,0:T(8,128)S(1)} %get-tuple-element.57), channel_id=1, source_target_pairs={{0,4},{1,5},{2,6},{3,7},{4,0},{5,1},{6,2},{7,3},{8,12},{9,13},{10,... | collective-permute-start | bytes 393224 | tf_op jit(solution)/shard_map/ppermute | solution.py:521
  25.6 8.5 %collective-permute-start.8 = (f32[8,16,512]{2,1,0:T(8,128)S(1)}, f32[8,16,512]{2,1,0:T(8,128)S(1)}, u32[]{:S(2)}, u32[]{:S(2)}) collective-permute-start(f32[8,16,512]{2,1,0:T(8,128)S(1)} %pad_maximum_fusion.1.refs_0_), channel_id=1, source_target_pairs={{0,2},{1,3},{2,0},{3,1},{4,6},{5,7},{6,4},{7,5},{8,10},{9,11},{10,... | collective-permute-start | bytes 786440 | tf_op jit(solution)/shard_map/ppermute | solution.py:521
  26.1 8.1 %collective-permute-start.12 = (f32[8,16,512]{2,1,0:T(8,128)S(1)}, f32[8,16,512]{2,1,0:T(8,128)S(1)}, u32[]{:S(2)}, u32[]{:S(2)}) collective-permute-start(f32[8,16,512]{2,1,0:T(8,128)S(1)} %pad_maximum_fusion.2.refs_4_), channel_id=1, source_target_pairs={{0,4},{1,5},{2,6},{3,7},{4,0},{5,1},{6,2},{7,3},{8,12},{9,13},{10,... | collective-permute-start | bytes 786440 | tf_op jit(solution)/shard_map/ppermute | solution.py:521
  27.5 7.1 %collective-permute-start.9 = (f32[8,16,512]{2,1,0:T(8,128)S(1)}, f32[8,16,512]{2,1,0:T(8,128)S(1)}, u32[]{:S(2)}, u32[]{:S(2)}) collective-permute-start(f32[8,16,512]{2,1,0:T(8,128)S(1)} %pad_maximum_fusion.1.refs_0_), channel_id=1, source_target_pairs={{0,1},{1,0},{2,3},{3,2},{4,5},{5,4},{6,7},{7,6},{8,9},{9,8},{10,11... | collective-permute-start | bytes 786440 | tf_op jit(solution)/shard_map/ppermute | solution.py:521
  27.5 7.1 %collective-permute-start.13 = (f32[8,16,512]{2,1,0:T(8,128)S(1)}, f32[8,16,512]{2,1,0:T(8,128)S(1)}, u32[]{:S(2)}, u32[]{:S(2)}) collective-permute-start(f32[8,16,512]{2,1,0:T(8,128)S(1)} %pad_maximum_fusion.2.refs_4_), channel_id=1, source_target_pairs={{0,1},{1,0},{2,3},{3,2},{4,5},{5,4},{6,7},{7,6},{8,9},{9,8},{10,11... | collective-permute-start | bytes 786440 | tf_op jit(solution)/shard_map/ppermute | solution.py:521
  34.1 1.5 %collective-permute-start.10 = (f32[8,16,512]{2,1,0:T(8,128)S(1)}, f32[8,16,512]{2,1,0:T(8,128)S(1)}, u32[]{:S(2)}, u32[]{:S(2)}) collective-permute-start(f32[8,16,512]{2,1,0:T(8,128)S(1)} %collective-permute-done.8.refs_1_), channel_id=1, source_target_pairs={{0,1},{1,0},{2,3},{3,2},{4,5},{5,4},{6,7},{7,6},{8,9},{9,8},{10,11... | collective-permute-start | bytes 786440 | tf_op jit(solution)/shard_map/ppermute | solution.py:521
  34.2 1.8 %collective-permute-start.14 = (f32[8,16,512]{2,1,0:T(8,128)S(1)}, f32[8,16,512]{2,1,0:T(8,128)S(1)}, u32[]{:S(2)}, u32[]{:S(2)}) collective-permute-start(f32[8,16,512]{2,1,0:T(8,128)S(1)} %collective-permute-done.12.refs_5_), channel_id=1, source_target_pairs={{0,1},{1,0},{2,3},{3,2},{4,5},{5,4},{6,7},{7,6},{8,9},{9,8},{10,11... | collective-permute-start | bytes 786440 | tf_op jit(solution)/shard_map/ppermute | solution.py:521
  45.3 12.3 %all-to-all-start.1 = ((f32[32,8,128]{2,1,0:T(8,128)}), f32[32,8,128]{2,1,0:T(8,128)S(1)}, u32[]{:S(2)}, u32[]{:S(2)}) async-start(f32[32,8,128]{2,1,0:T(8,128)} %bitcast.5), calls=%async_computation.1 | async-start | bytes 262144 | tf_op jit(solution)/shard_map/all_to_all | solution.py:585
  49.3 4.7 %collective-permute-start.17 = (f32[1,64,128]{2,1,0:T(8,128)S(1)}, f32[1,64,128]{2,1,0:T(8,128)S(1)}, u32[]{:S(2)}, u32[]{:S(2)}) collective-permute-start(f32[1,64,128]{2,1,0:T(8,128)S(1)} %get-tuple-element.61), channel_id=1, source_target_pairs={{0,3},{1,2},{2,1},{3,0},{4,7},{5,6},{6,5},{7,4},{8,11},{9,10},{10,... | collective-permute-start | bytes 98312 | tf_op jit(solution)/shard_map/ppermute | solution.py:521
  50.9 4.1 %collective-permute-start.16 = (f32[1,64,128]{2,1,0:T(8,128)S(1)}, f32[1,64,128]{2,1,0:T(8,128)S(1)}, u32[]{:S(2)}, u32[]{:S(2)}) collective-permute-start(f32[1,64,128]{2,1,0:T(8,128)S(1)} %get-tuple-element.62), channel_id=1, source_target_pairs={{0,2},{1,3},{2,0},{3,1},{4,6},{5,7},{6,4},{7,5},{8,10},{9,11},{10,... | collective-permute-start | bytes 98312 | tf_op jit(solution)/shard_map/ppermute | solution.py:521
  51.3 3.7 %collective-permute-start.15 = (f32[1,64,128]{2,1,0:T(8,128)S(1)}, f32[1,64,128]{2,1,0:T(8,128)S(1)}, u32[]{:S(2)}, u32[]{:S(2)}) collective-permute-start(f32[1,64,128]{2,1,0:T(8,128)S(1)} %get-tuple-element.63), channel_id=1, source_target_pairs={{0,1},{1,0},{2,3},{3,2},{4,5},{5,4},{6,7},{7,6},{8,9},{9,8},{10,11... | collective-permute-start | bytes 98312 | tf_op jit(solution)/shard_map/ppermute | solution.py:521
  51.3 7.0 %copy-start.3 = (f32[1,256,128]{2,1,0:T(8,128)S(1)}, f32[1,256,128]{2,1,0:T(8,128)}, u32[]{:S(2)}) copy-start(f32[1,256,128]{2,1,0:T(8,128)} %param.7) | copy-start | bytes 393220
  57.6 6.0 %collective-permute-start.25 = (f32[4,32,128]{2,1,0:T(8,128)S(1)}, f32[4,32,128]{2,1,0:T(8,128)S(1)}, u32[]{:S(2)}, u32[]{:S(2)}) collective-permute-start(f32[4,32,128]{2,1,0:T(8,128)S(1)} %get-tuple-element.58), channel_id=1, source_target_pairs={{0,4},{1,5},{2,6},{3,7},{4,0},{5,1},{6,2},{7,3},{8,12},{9,13},{10,... | collective-permute-start | bytes 196616 | tf_op jit(solution)/shard_map/ppermute | solution.py:521
  58.8 1.3 %collective-permute-start.18 = (f32[72,128]{1,0:T(8,128)S(1)}, f32[72,128]{1,0:T(8,128)S(1)}, u32[]{:S(2)}, u32[]{:S(2)}) collective-permute-start(f32[72,128]{1,0:T(8,128)S(1)} %get-tuple-element.42), channel_id=1, source_target_pairs={{0,1},{1,0},{2,3},{3,2},{4,5},{5,4},{6,7},{7,6},{8,9},{9,8},{10,11... | collective-permute-start | bytes 110600 | tf_op jit(solution)/shard_map/ppermute | solution.py:521
  58.9 11.9 %collective-permute-start.23 = (f32[4,32,128]{2,1,0:T(8,128)S(1)}, f32[4,32,128]{2,1,0:T(8,128)S(1)}, u32[]{:S(2)}, u32[]{:S(2)}) collective-permute-start(f32[4,32,128]{2,1,0:T(8,128)S(1)} %get-tuple-element.59), channel_id=1, source_target_pairs={{0,16},{1,17},{2,18},{3,19},{4,20},{5,21},{6,22},{7,23},{8,24},{9,... | collective-permute-start | bytes 196616 | tf_op jit(solution)/shard_map/ppermute | solution.py:521
  60.1 5.4 %collective-permute-start.21 = (f32[72,128]{1,0:T(8,128)S(1)}, f32[72,128]{1,0:T(8,128)S(1)}, u32[]{:S(2)}, u32[]{:S(2)}) collective-permute-start(f32[72,128]{1,0:T(8,128)S(1)} %add.36), channel_id=1, source_target_pairs={{0,6},{1,7},{2,4},{3,5},{4,2},{5,3},{6,0},{7,1},{8,14},{9,15},{10,... | collective-permute-start | bytes 110600 | tf_op jit(solution)/shard_map/ppermute | solution.py:521
  61.3 4.2 %collective-permute-start.20 = (f32[72,128]{1,0:T(8,128)S(1)}, f32[72,128]{1,0:T(8,128)S(1)}, u32[]{:S(2)}, u32[]{:S(2)}) collective-permute-start(f32[72,128]{1,0:T(8,128)S(1)} %add.36), channel_id=1, source_target_pairs={{0,4},{1,5},{2,6},{3,7},{4,0},{5,1},{6,2},{7,3},{8,12},{9,13},{10,... | collective-permute-start | bytes 110600 | tf_op jit(solution)/shard_map/ppermute | solution.py:521
  62.3 4.0 %collective-permute-start.19 = (f32[72,128]{1,0:T(8,128)S(1)}, f32[72,128]{1,0:T(8,128)S(1)}, u32[]{:S(2)}, u32[]{:S(2)}) collective-permute-start(f32[72,128]{1,0:T(8,128)S(1)} %add.36), channel_id=1, source_target_pairs={{0,2},{1,3},{2,0},{3,1},{4,6},{5,7},{6,4},{7,5},{8,10},{9,11},{10,... | collective-permute-start | bytes 110600 | tf_op jit(solution)/shard_map/ppermute | solution.py:521
  63.6 15.0 %collective-permute-start.26 = (f32[8,32,128]{2,1,0:T(8,128)S(1)}, f32[8,32,128]{2,1,0:T(8,128)S(1)}, u32[]{:S(2)}, u32[]{:S(2)}) collective-permute-start(f32[8,32,128]{2,1,0:T(8,128)S(1)} %pad_maximum_fusion.8), channel_id=1, source_target_pairs={{0,16},{1,17},{2,18},{3,19},{4,20},{5,21},{6,22},{7,23},{8,24},{9,... | collective-permute-start | bytes 393224 | tf_op jit(solution)/shard_map/ppermute | solution.py:521
  66.3 11.9 %collective-permute-start.28 = (f32[72,128]{1,0:T(8,128)S(1)}, f32[72,128]{1,0:T(8,128)S(1)}, u32[]{:S(2)}, u32[]{:S(2)}) collective-permute-start(f32[72,128]{1,0:T(8,128)S(1)} %add_add_fusion.1), channel_id=1, source_target_pairs={{0,24},{1,25},{2,26},{3,27},{4,28},{5,29},{6,30},{7,31},{8,16},{9,... | collective-permute-start | bytes 110600 | tf_op jit(solution)/shard_map/ppermute | solution.py:521
  68.4 9.9 %collective-permute-start.27 = (f32[72,128]{1,0:T(8,128)S(1)}, f32[72,128]{1,0:T(8,128)S(1)}, u32[]{:S(2)}, u32[]{:S(2)}) collective-permute-start(f32[72,128]{1,0:T(8,128)S(1)} %add_add_fusion.1), channel_id=1, source_target_pairs={{0,16},{1,17},{2,18},{3,19},{4,20},{5,21},{6,22},{7,23},{8,24},{9,... | collective-permute-start | bytes 110600 | tf_op jit(solution)/shard_map/ppermute | solution.py:521
  69.2 5.4 %collective-permute-start.22 = (f32[72,128]{1,0:T(8,128)S(1)}, f32[72,128]{1,0:T(8,128)S(1)}, u32[]{:S(2)}, u32[]{:S(2)}) collective-permute-start(f32[72,128]{1,0:T(8,128)S(1)} %add_add_fusion.1), channel_id=1, source_target_pairs={{0,8},{1,9},{2,10},{3,11},{4,12},{5,13},{6,14},{7,15},{8,0},{9,1},... | collective-permute-start | bytes 110600 | tf_op jit(solution)/shard_map/ppermute | solution.py:521
  70.8 7.8 %collective-permute-start.24 = (f32[8,32,128]{2,1,0:T(8,128)S(1)}, f32[8,32,128]{2,1,0:T(8,128)S(1)}, u32[]{:S(2)}, u32[]{:S(2)}) collective-permute-start(f32[8,32,128]{2,1,0:T(8,128)S(1)} %pad_maximum_fusion.7), channel_id=1, source_target_pairs={{0,8},{1,9},{2,10},{3,11},{4,12},{5,13},{6,14},{7,15},{8,0},{9,1},... | collective-permute-start | bytes 393224 | tf_op jit(solution)/shard_map/ppermute | solution.py:521
  74.6 20.4 %all-to-all-start.2 = ((f32[32,4,640]{2,1,0:T(4,128)}), f32[32,4,640]{2,1,0:T(4,128)S(1)}, u32[]{:S(2)}, u32[]{:S(2)}) async-start(f32[32,4,640]{2,1,0:T(4,128)} %bitcast.4), calls=%async_computation.2 | async-start | bytes 655360 | tf_op jit(solution)/shard_map/all_to_all | solution.py:585
  78.3 1.3 %collective-permute-start.29 = (f32[72,128]{1,0:T(8,128)S(1)}, f32[72,128]{1,0:T(8,128)S(1)}, u32[]{:S(2)}, u32[]{:S(2)}) collective-permute-start(f32[72,128]{1,0:T(8,128)S(1)} %add_add_fusion.gram_ref), channel_id=1, source_target_pairs={{0,1},{1,0},{2,3},{3,2},{4,5},{5,4},{6,7},{7,6},{8,9},{9,8},{10,11... | collective-permute-start | bytes 110600 | tf_op jit(solution)/shard_map/ppermute | solution.py:521
  79.6 15.5 %collective-permute-start.30 = (f32[16,32,128]{2,1,0:T(8,128)S(1)}, f32[16,32,128]{2,1,0:T(8,128)S(1)}, u32[]{:S(2)}, u32[]{:S(2)}) collective-permute-start(f32[16,32,128]{2,1,0:T(8,128)S(1)} %pad_maximum_fusion.3), channel_id=1, source_target_pairs={{0,4},{1,5},{2,6},{3,7},{4,0},{5,1},{6,2},{7,3},{8,12},{9,13},{10,... | collective-permute-start | bytes 786440 | tf_op jit(solution)/shard_map/ppermute | solution.py:521
  81.3 13.8 %collective-permute-start.31 = (f32[16,32,128]{2,1,0:T(8,128)S(1)}, f32[16,32,128]{2,1,0:T(8,128)S(1)}, u32[]{:S(2)}, u32[]{:S(2)}) collective-permute-start(f32[16,32,128]{2,1,0:T(8,128)S(1)} %pad_maximum_fusion.4), channel_id=1, source_target_pairs={{0,8},{1,9},{2,10},{3,11},{4,12},{5,13},{6,14},{7,15},{8,0},{9,1},... | collective-permute-start | bytes 786440 | tf_op jit(solution)/shard_map/ppermute | solution.py:521
  89.9 5.2 %copy-start = (f32[32,512]{1,0:T(8,128)S(1)}, f32[32,512]{1,0:T(8,128)}, u32[]{:S(2)}) copy-start(f32[32,512]{1,0:T(8,128)} %kspace_ref.1) | copy-start | bytes 196612
  89.9 5.2 %copy-start.1 = (s32[32,512]{1,0:T(8,128)S(1)}, s32[32,512]{1,0:T(8,128)}, u32[]{:S(2)}) copy-start(s32[32,512]{1,0:T(8,128)} %mask_ref.1) | copy-start | bytes 196612

commit v18 on v16

--- a/solution.py
+++ b/solution.py
@@ -172,14 +172,14 @@
             high, low = split(jnp.concatenate([first, second], axis=0))
             moved_ref[k * KER + j : k * KER + j + 2 * SUB, :] = high
             moved_ref[rows + k * KER + j : rows + k * KER + j + 2 * SUB, :] = low
-    high = jnp.zeros((rows, 2 * channels), jnp.float32)
-    low = jnp.zeros((rows, channels), jnp.float32)
+    total = jnp.zeros((rows, channels), jnp.float32)
     for t in range(tiles):
         block = samples_ref[t].reshape(2 * channels, tile)
+        block = jnp.concatenate([block[:channels], block[channels:], block[:channels]], axis=1)
         lanes = slice(t * tile, (t + 1) * tile)
-        high = high + dot(moved_ref[:rows, lanes], block, ((1,), (1,)))
-        low = low + dot(moved_ref[rows:, lanes], block[:channels], ((1,), (1,)))
-    return high[:, :channels] + (high[:, channels:] + low)
+        high, low = moved_ref[:rows, lanes], moved_ref[rows:, lanes]
+        total = total + dot(jnp.concatenate([high, high, low], axis=1), block, ((1,), (1,)))
+    return total
 
 
 def store_by_rows(normal, send_ref):
@@ -682,7 +682,7 @@
         micros=2,
     )
     near, order = gather_group(group, devices)
-    received, near = lax.optimization_barrier((received, images, near))[::2]
+    received = after(received, images, near)
     half = ((rank // 2 + SUB, rank), f32)
     kept, given, turned = call(
         functools.partial(gram_kernel, cols, per_tile),

time: 98.4 us -> 108 us (1.098)
  Pallas kernels: 28.4 us -> 37.6 us
  starting transfers between devices: 38.2 us -> 42.8 us
  waiting for transfers between devices: 27.5 us -> 23.1 us
    pallas_call x7, Pallas kernels: 28.4 us -> 37.6 us  [call(): pl.pallas_call(kernel, out_shape=[jax.ShapeDtypeStruct(shape, kind) for s...]
    ppermute x27, starting transfers between devices: 28.5 us -> 32.6 us  [exchange(): return lax.ppermute(block, axes, [(i, i ^ mask) for i in range(devices)])]
    all_to_all x3, waiting for transfers between devices: 3.07 us -> 0.47 us  [to_all(): return lax.all_to_all(pieces, axes, 0, 0, tiled=True)]
    ppermute x27, waiting for transfers between devices: 24.5 us -> 22.6 us  [exchange(): return lax.ppermute(block, axes, [(i, i ^ mask) for i in range(devices)])]
  transfers between devices with their start and end apart: 30 -> 30, of which waited for: 14 -> 14; matrix products, arithmetic and copies ran while one was open for 0% -> 0% of each run, Pallas kernels for 16% -> 15%
where the time goes in v18:
time: 108 us; the launch traced here: 107 us
  starting transfers between devices  42.8 us (40%)
  Pallas kernels  37.6 us (35%)
  waiting for transfers between devices  23.1 us (21%)
  between operations  1.54 us (1%)
    pallas_call x7, Pallas kernels, call(): pl.pallas_call(kernel, out_shape=[jax.ShapeDtypeStruct(shape, kind) for s...  37.6 us
    ppermute x27, starting transfers between devices, exchange(): return lax.ppermute(block, axes, [(i, i ^ mask) for i in range(devices)])  32.6 us
    ppermute x27, waiting for transfers between devices, exchange(): return lax.ppermute(block, axes, [(i, i ^ mask) for i in range(devices)])  22.6 us
    all_to_all x3, starting transfers between devices, to_all(): return lax.all_to_all(pieces, axes, 0, 0, tiled=True)  10.2 us
  transfers between devices with their start and end apart: 30, of which 14 were waited for; matrix products, arithmetic and copies ran while one was open for 0% of the time, Pallas kernels for 15%

profile of v18, /device:TPU:0, one launch (start us, length us, event | category | flops | bytes accessed | tf_op | source)
XLA Modules:
  0.0 107.4 jit_solution(10862624272759190725)
XLA Ops:
  0.6 0.9 multiply_bitcast_fusion
  1.5 4.1 %collective-permute-start.5 = (f32[1,32,512]{2,1,0:T(8,128)S(1)}, f32[1,32,512]{2,1,0:T(8,128)S(1)}, u32[]{:S(2)}, u32[]{:S(2)}) collective-permute-start(f32[1,32,512]{2,1,0:T(8,128)S(1)} %multiply_bitcast_fusion), channel_id=1, source_target_pairs={{0,16},{1,17},{2,18},{3,19},{4,20},{5,21},{6,22},{7,23},{8,24},{9,... | collective-permute-start | bytes 196616 | tf_op jit(solution)/shard_map/ppermute | solution.py:521
  5.6 0.9 copy-done.2
  6.5 0.9 shard_map.50
  7.4 3.8 %all-to-all-start = ((f32[32,8,128]{2,1,0:T(8,128)}), f32[32,8,128]{2,1,0:T(8,128)S(1)}, u32[]{:S(2)}, u32[]{:S(2)}) async-start(f32[32,8,128]{2,1,0:T(8,128)} %bitcast.1), calls=%async_computation | async-start | bytes 262144 | tf_op jit(solution)/shard_map/all_to_all | solution.py:583
  11.3 1.8 %collective-permute-start.6 = (f32[2,32,512]{2,1,0:T(8,128)S(1)}, f32[2,32,512]{2,1,0:T(8,128)S(1)}, u32[]{:S(2)}, u32[]{:S(2)}) collective-permute-start(f32[2,32,512]{2,1,0:T(8,128)S(1)} %pad_maximum_fusion.5), channel_id=1, source_target_pairs={{0,8},{1,9},{2,10},{3,11},{4,12},{5,13},{6,14},{7,15},{8,0},{9,1},... | collective-permute-start | bytes 393224 | tf_op jit(solution)/shard_map/ppermute | solution.py:521
  13.1 5.9 %collective-permute-done.6 = f32[2,32,512]{2,1,0:T(8,128)S(1)} collective-permute-done((f32[2,32,512]{2,1,0:T(8,128)S(1)}, f32[2,32,512]{2,1,0:T(8,128)S(1)}, u32[]{:S(2)}, u32[]{:S(2)}) %collective-permute-start.6) | collective-permute-done | bytes 131104 | tf_op jit(solution)/shard_map/ppermute | solution.py:521
  19.0 0.5 all-to-all-done
  19.5 1.1 %collective-permute-start.7 = (f32[4,16,512]{2,1,0:T(8,128)S(1)}, f32[4,16,512]{2,1,0:T(8,128)S(1)}, u32[]{:S(2)}, u32[]{:S(2)}) collective-permute-start(f32[4,16,512]{2,1,0:T(8,128)S(1)} %get-tuple-element.51), channel_id=1, source_target_pairs={{0,4},{1,5},{2,6},{3,7},{4,0},{5,1},{6,2},{7,3},{8,12},{9,13},{10,... | collective-permute-start | bytes 393224 | tf_op jit(solution)/shard_map/ppermute | solution.py:521
  20.6 1.5 %collective-permute-start.11 = (f32[4,16,512]{2,1,0:T(8,128)S(1)}, f32[4,16,512]{2,1,0:T(8,128)S(1)}, u32[]{:S(2)}, u32[]{:S(2)}) collective-permute-start(f32[4,16,512]{2,1,0:T(8,128)S(1)} %get-tuple-element.50), channel_id=1, source_target_pairs={{0,2},{1,3},{2,0},{3,1},{4,6},{5,7},{6,4},{7,5},{8,10},{9,11},{10,... | collective-permute-start | bytes 393224 | tf_op jit(solution)/shard_map/ppermute | solution.py:521
  22.1 3.5 %collective-permute-done.7 = f32[4,16,512]{2,1,0:T(8,128)S(1)} collective-permute-done((f32[4,16,512]{2,1,0:T(8,128)S(1)}, f32[4,16,512]{2,1,0:T(8,128)S(1)}, u32[]{:S(2)}, u32[]{:S(2)}) %collective-permute-start.7) | collective-permute-done | bytes 131104 | tf_op jit(solution)/shard_map/ppermute | solution.py:521
  25.9 1.6 %collective-permute-start.12 = (f32[8,16,512]{2,1,0:T(8,128)S(1)}, f32[8,16,512]{2,1,0:T(8,128)S(1)}, u32[]{:S(2)}, u32[]{:S(2)}) collective-permute-start(f32[8,16,512]{2,1,0:T(8,128)S(1)} %pad_maximum_fusion.2.refs_4_), channel_id=1, source_target_pairs={{0,4},{1,5},{2,6},{3,7},{4,0},{5,1},{6,2},{7,3},{8,12},{9,13},{10,... | collective-permute-start | bytes 786440 | tf_op jit(solution)/shard_map/ppermute | solution.py:521
  27.5 0.5 collective-permute-start.13
  28.0 5.8 %collective-permute-done.8.refs_1_ = f32[8,16,512]{2,1,0:T(8,128)S(1)} collective-permute-done((f32[8,16,512]{2,1,0:T(8,128)S(1)}, f32[8,16,512]{2,1,0:T(8,128)S(1)}, u32[]{:S(2)}, u32[]{:S(2)}) %collective-permute-start.8) | collective-permute-done | bytes 262176 | tf_op jit(solution)/shard_map/ppermute | solution.py:521
  33.9 0.4 collective-permute-start.14
  34.3 1.0 collective-permute-done.10.refs_3_
  35.3 0.4 collective-permute-done.14.refs_7_
  35.7 18.4 %shard_map.51 = (bf16[8,2,4,32,512]{4,3,2,1,0:T(8,128)(2,1)S(1)}, f32[256,128]{1,0:T(8,128)S(1)}, f32[8,4,8,128]{3,2,1,0:T(8,128)}, f32[4,64,128]{2,1,0:T(8,128)S(1)}) custom-call(f32[8,4,8,128]{3,2,1,0:T(8,128)S(1)} %bitcast.16, f32[8,16,512]{2,1,0:T(8,128)S(1)} %pad_maximum_fusion.1.refs_0_, f32[8,16,512]{2,1,0:T(8,128)S(1)} %collective-permute-done.8.refs_1_, ...), custom_call_target="tpu_custom_call" | custom-call | flops 12000000000 | tf_op jit(solution)/shard_map/pallas_call | solution.py:506
  54.1 2.8 %all-to-all-start.1 = ((f32[32,8,128]{2,1,0:T(8,128)}), f32[32,8,128]{2,1,0:T(8,128)S(1)}, u32[]{:S(2)}, u32[]{:S(2)}) async-start(f32[32,8,128]{2,1,0:T(8,128)} %bitcast.4), calls=%async_computation.1 | async-start | bytes 262144 | tf_op jit(solution)/shard_map/all_to_all | solution.py:583
  56.9 1.3 %collective-permute-start.17 = (f32[1,64,128]{2,1,0:T(8,128)S(1)}, f32[1,64,128]{2,1,0:T(8,128)S(1)}, u32[]{:S(2)}, u32[]{:S(2)}) collective-permute-start(f32[1,64,128]{2,1,0:T(8,128)S(1)} %get-tuple-element.55), channel_id=1, source_target_pairs={{0,3},{1,2},{2,1},{3,0},{4,7},{5,6},{6,5},{7,4},{8,11},{9,10},{10,... | collective-permute-start | bytes 98312 | tf_op jit(solution)/shard_map/ppermute | solution.py:521
  58.2 0.3 collective-permute-start.16
  58.5 0.3 collective-permute-start.15
  58.8 2.8 %shard_map.52 = f32[8,4,4,640]{3,2,1,0:T(4,128)} custom-call(bf16[8,2,4,32,512]{4,3,2,1,0:T(8,128)(2,1)S(1)} %get-tuple-element.34.samples_ref, f32[256,128]{1,0:T(8,128)S(1)} %get-tuple-element.35.vectors_ref), custom_call_target="tpu_custom_call" | custom-call | flops 2000000000 | tf_op jit(solution)/shard_map/pallas_call | solution.py:506
  61.6 0.7 collective-permute-done.16
  62.3 1.5 %collective-permute-start.20 = (f32[4,32,128]{2,1,0:T(8,128)S(1)}, f32[4,32,128]{2,1,0:T(8,128)S(1)}, u32[]{:S(2)}, u32[]{:S(2)}) collective-permute-start(f32[4,32,128]{2,1,0:T(8,128)S(1)} %get-tuple-element.52), channel_id=1, source_target_pairs={{0,4},{1,5},{2,6},{3,7},{4,0},{5,1},{6,2},{7,3},{8,12},{9,13},{10,... | collective-permute-start | bytes 196616 | tf_op jit(solution)/shard_map/ppermute | solution.py:521
  63.9 2.6 %collective-permute-start.18 = (f32[4,32,128]{2,1,0:T(8,128)S(1)}, f32[4,32,128]{2,1,0:T(8,128)S(1)}, u32[]{:S(2)}, u32[]{:S(2)}) collective-permute-start(f32[4,32,128]{2,1,0:T(8,128)S(1)} %get-tuple-element.53), channel_id=1, source_target_pairs={{0,16},{1,17},{2,18},{3,19},{4,20},{5,21},{6,22},{7,23},{8,24},{9,... | collective-permute-start | bytes 196616 | tf_op jit(solution)/shard_map/ppermute | solution.py:521
  66.5 0.5 shard_map.53
  67.1 2.2 %collective-permute-start.21 = (f32[8,32,128]{2,1,0:T(8,128)S(1)}, f32[8,32,128]{2,1,0:T(8,128)S(1)}, u32[]{:S(2)}, u32[]{:S(2)}) collective-permute-start(f32[8,32,128]{2,1,0:T(8,128)S(1)} %pad_maximum_fusion.8), channel_id=1, source_target_pairs={{0,16},{1,17},{2,18},{3,19},{4,20},{5,21},{6,22},{7,23},{8,24},{9,... | collective-permute-start | bytes 393224 | tf_op jit(solution)/shard_map/ppermute | solution.py:521
  69.4 1.9 %collective-permute-start.25 = (f32[72,128]{1,0:T(8,128)S(1)}, f32[72,128]{1,0:T(8,128)S(1)}, u32[]{:S(2)}, u32[]{:S(2)}) collective-permute-start(f32[72,128]{1,0:T(8,128)S(1)} %add.36), channel_id=1, source_target_pairs={{0,6},{1,7},{2,4},{3,5},{4,2},{5,3},{6,0},{7,1},{8,14},{9,15},{10,... | collective-permute-start | bytes 110600 | tf_op jit(solution)/shard_map/ppermute | solution.py:521
  71.3 0.8 collective-permute-start.24
  72.1 0.8 collective-permute-start.23
  72.9 1.7 %collective-permute-start.19 = (f32[8,32,128]{2,1,0:T(8,128)S(1)}, f32[8,32,128]{2,1,0:T(8,128)S(1)}, u32[]{:S(2)}, u32[]{:S(2)}) collective-permute-start(f32[8,32,128]{2,1,0:T(8,128)S(1)} %pad_maximum_fusion.7), channel_id=1, source_target_pairs={{0,8},{1,9},{2,10},{3,11},{4,12},{5,13},{6,14},{7,15},{8,0},{9,1},... | collective-permute-start | bytes 393224 | tf_op jit(solution)/shard_map/ppermute | solution.py:521
  74.6 0.6 collective-permute-done.24
  75.2 0.8 collective-permute-done.23
  76.1 1.4 %collective-permute-start.28 = (f32[72,128]{1,0:T(8,128)S(1)}, f32[72,128]{1,0:T(8,128)S(1)}, u32[]{:S(2)}, u32[]{:S(2)}) collective-permute-start(f32[72,128]{1,0:T(8,128)S(1)} %add_add_fusion.1), channel_id=1, source_target_pairs={{0,24},{1,25},{2,26},{3,27},{4,28},{5,29},{6,30},{7,31},{8,16},{9,... | collective-permute-start | bytes 110600 | tf_op jit(solution)/shard_map/ppermute | solution.py:521
  77.5 1.4 %collective-permute-start.27 = (f32[72,128]{1,0:T(8,128)S(1)}, f32[72,128]{1,0:T(8,128)S(1)}, u32[]{:S(2)}, u32[]{:S(2)}) collective-permute-start(f32[72,128]{1,0:T(8,128)S(1)} %add_add_fusion.1), channel_id=1, source_target_pairs={{0,16},{1,17},{2,18},{3,19},{4,20},{5,21},{6,22},{7,23},{8,24},{9,... | collective-permute-start | bytes 110600 | tf_op jit(solution)/shard_map/ppermute | solution.py:521
  78.9 1.6 %collective-permute-start.26 = (f32[72,128]{1,0:T(8,128)S(1)}, f32[72,128]{1,0:T(8,128)S(1)}, u32[]{:S(2)}, u32[]{:S(2)}) collective-permute-start(f32[72,128]{1,0:T(8,128)S(1)} %add_add_fusion.1), channel_id=1, source_target_pairs={{0,8},{1,9},{2,10},{3,11},{4,12},{5,13},{6,14},{7,15},{8,0},{9,1},... | collective-permute-start | bytes 110600 | tf_op jit(solution)/shard_map/ppermute | solution.py:521
  80.6 1.3 %collective-permute-done.28 = f32[72,128]{1,0:T(8,128)S(1)} collective-permute-done((f32[72,128]{1,0:T(8,128)S(1)}, f32[72,128]{1,0:T(8,128)S(1)}, u32[]{:S(2)}, u32[]{:S(2)}) %collective-permute-start.28) | collective-permute-done | bytes 36896 | tf_op jit(solution)/shard_map/ppermute | solution.py:521
  81.9 0.8 collective-permute-done.27
  82.7 0.4 collective-permute-done.26
  83.2 1.2 %collective-permute-done.29.other_ref = f32[72,128]{1,0:T(8,128)S(1)} collective-permute-done((f32[72,128]{1,0:T(8,128)S(1)}, f32[72,128]{1,0:T(8,128)S(1)}, u32[]{:S(2)}, u32[]{:S(2)}) %collective-permute-start.29) | collective-permute-done | bytes 36896 | tf_op jit(solution)/shard_map/ppermute | solution.py:521
  84.4 3.6 %all-to-all-start.2 = ((f32[32,4,640]{2,1,0:T(4,128)}), f32[32,4,640]{2,1,0:T(4,128)S(1)}, u32[]{:S(2)}, u32[]{:S(2)}) async-start(f32[32,4,640]{2,1,0:T(4,128)} %bitcast.6), calls=%async_computation.2 | async-start | bytes 655360 | tf_op jit(solution)/shard_map/all_to_all | solution.py:583
  88.0 1.8 %collective-permute-start.30 = (f32[16,32,128]{2,1,0:T(8,128)S(1)}, f32[16,32,128]{2,1,0:T(8,128)S(1)}, u32[]{:S(2)}, u32[]{:S(2)}) collective-permute-start(f32[16,32,128]{2,1,0:T(8,128)S(1)} %pad_maximum_fusion.3), channel_id=1, source_target_pairs={{0,4},{1,5},{2,6},{3,7},{4,0},{5,1},{6,2},{7,3},{8,12},{9,13},{10,... | collective-permute-start | bytes 786440 | tf_op jit(solution)/shard_map/ppermute | solution.py:521
  89.8 1.5 %collective-permute-start.31 = (f32[16,32,128]{2,1,0:T(8,128)S(1)}, f32[16,32,128]{2,1,0:T(8,128)S(1)}, u32[]{:S(2)}, u32[]{:S(2)}) collective-permute-start(f32[16,32,128]{2,1,0:T(8,128)S(1)} %pad_maximum_fusion.4), channel_id=1, source_target_pairs={{0,8},{1,9},{2,10},{3,11},{4,12},{5,13},{6,14},{7,15},{8,0},{9,1},... | collective-permute-start | bytes 786440 | tf_op jit(solution)/shard_map/ppermute | solution.py:521
  91.3 6.4 %shard_map.54 = (f32[128,128]{1,0:T(8,128)S(1)}, f32[128,128]{1,0:T(8,128)S(1)}, s32[1]{0:T(128)}) custom-call(f32[72,128]{1,0:T(8,128)S(1)} %add_add_fusion.gram_ref, f32[72,128]{1,0:T(8,128)S(1)} %collective-permute-done.29.other_ref), custom_call_target="tpu_custom_call" | custom-call | flops 12000000000 | tf_op jit(solution)/shard_map/pallas_call | solution.py:506
  98.4 0.2 conditional.1
  98.6 5.0 %shard_map.55.both_ref = f32[128,128]{1,0:T(8,128)S(1)} custom-call(f32[128,128]{1,0:T(8,128)S(1)} %get-tuple-element.58.gram_ref, f32[128,128]{1,0:T(8,128)S(1)} %get-tuple-element.44.inverse_ref), custom_call_target="tpu_custom_call" | custom-call | tf_op jit(solution)/shard_map/pallas_call | solution.py:506
  103.8 3.6 %shard_map.56 = (f32[32,512]{1,0:T(8,128)}, f32[256,128]{1,0:T(8,128)}) custom-call(f32[128,640]{1,0:T(8,128)S(1)} %reshape.51.images_ref, f32[128,128]{1,0:T(8,128)S(1)} %shard_map.55.both_ref, f32[32,512]{1,0:T(8,128)S(1)} %copy-done, s32[32,512]{1,0:T(8,128)S(1)} %copy-done.1, f32[512,128]{1,0:T(8,128)S(1)} %bitcast.15, f32[512,128]{1,0:T(8,128)S(1)} %bitcast.18, ...), custom_call_target="tpu_custom_call" | custom-call | flops 5000000000 | tf_op jit(solution)/shard_map/pallas_call | solution.py:506
  (45 shorter events, 0.8 us)
Async XLA Ops:
  1.5 9.7 %collective-permute-start.5 = (f32[1,32,512]{2,1,0:T(8,128)S(1)}, f32[1,32,512]{2,1,0:T(8,128)S(1)}, u32[]{:S(2)}, u32[]{:S(2)}) collective-permute-start(f32[1,32,512]{2,1,0:T(8,128)S(1)} %multiply_bitcast_fusion), channel_id=1, source_target_pairs={{0,16},{1,17},{2,18},{3,19},{4,20},{5,21},{6,22},{7,23},{8,24},{9,... | collective-permute-start | bytes 196616 | tf_op jit(solution)/shard_map/ppermute | solution.py:521
  5.6 0.9 copy-start.2
  7.4 12.1 %all-to-all-start = ((f32[32,8,128]{2,1,0:T(8,128)}), f32[32,8,128]{2,1,0:T(8,128)S(1)}, u32[]{:S(2)}, u32[]{:S(2)}) async-start(f32[32,8,128]{2,1,0:T(8,128)} %bitcast.1), calls=%async_computation | async-start | bytes 262144 | tf_op jit(solution)/shard_map/all_to_all | solution.py:583
  11.3 7.7 %collective-permute-start.6 = (f32[2,32,512]{2,1,0:T(8,128)S(1)}, f32[2,32,512]{2,1,0:T(8,128)S(1)}, u32[]{:S(2)}, u32[]{:S(2)}) collective-permute-start(f32[2,32,512]{2,1,0:T(8,128)S(1)} %pad_maximum_fusion.5), channel_id=1, source_target_pairs={{0,8},{1,9},{2,10},{3,11},{4,12},{5,13},{6,14},{7,15},{8,0},{9,1},... | collective-permute-start | bytes 393224 | tf_op jit(solution)/shard_map/ppermute | solution.py:521
  19.5 6.1 %collective-permute-start.7 = (f32[4,16,512]{2,1,0:T(8,128)S(1)}, f32[4,16,512]{2,1,0:T(8,128)S(1)}, u32[]{:S(2)}, u32[]{:S(2)}) collective-permute-start(f32[4,16,512]{2,1,0:T(8,128)S(1)} %get-tuple-element.51), channel_id=1, source_target_pairs={{0,4},{1,5},{2,6},{3,7},{4,0},{5,1},{6,2},{7,3},{8,12},{9,13},{10,... | collective-permute-start | bytes 393224 | tf_op jit(solution)/shard_map/ppermute | solution.py:521
  20.6 5.2 %collective-permute-start.11 = (f32[4,16,512]{2,1,0:T(8,128)S(1)}, f32[4,16,512]{2,1,0:T(8,128)S(1)}, u32[]{:S(2)}, u32[]{:S(2)}) collective-permute-start(f32[4,16,512]{2,1,0:T(8,128)S(1)} %get-tuple-element.50), channel_id=1, source_target_pairs={{0,2},{1,3},{2,0},{3,1},{4,6},{5,7},{6,4},{7,5},{8,10},{9,11},{10,... | collective-permute-start | bytes 393224 | tf_op jit(solution)/shard_map/ppermute | solution.py:521
  25.6 8.1 %collective-permute-start.8 = (f32[8,16,512]{2,1,0:T(8,128)S(1)}, f32[8,16,512]{2,1,0:T(8,128)S(1)}, u32[]{:S(2)}, u32[]{:S(2)}) collective-permute-start(f32[8,16,512]{2,1,0:T(8,128)S(1)} %pad_maximum_fusion.1.refs_0_), channel_id=1, source_target_pairs={{0,2},{1,3},{2,0},{3,1},{4,6},{5,7},{6,4},{7,5},{8,10},{9,11},{10,... | collective-permute-start | bytes 786440 | tf_op jit(solution)/shard_map/ppermute | solution.py:521
  25.9 8.0 %collective-permute-start.12 = (f32[8,16,512]{2,1,0:T(8,128)S(1)}, f32[8,16,512]{2,1,0:T(8,128)S(1)}, u32[]{:S(2)}, u32[]{:S(2)}) collective-permute-start(f32[8,16,512]{2,1,0:T(8,128)S(1)} %pad_maximum_fusion.2.refs_4_), channel_id=1, source_target_pairs={{0,4},{1,5},{2,6},{3,7},{4,0},{5,1},{6,2},{7,3},{8,12},{9,13},{10,... | collective-permute-start | bytes 786440 | tf_op jit(solution)/shard_map/ppermute | solution.py:521
  27.4 6.8 %collective-permute-start.9 = (f32[8,16,512]{2,1,0:T(8,128)S(1)}, f32[8,16,512]{2,1,0:T(8,128)S(1)}, u32[]{:S(2)}, u32[]{:S(2)}) collective-permute-start(f32[8,16,512]{2,1,0:T(8,128)S(1)} %pad_maximum_fusion.1.refs_0_), channel_id=1, source_target_pairs={{0,1},{1,0},{2,3},{3,2},{4,5},{5,4},{6,7},{7,6},{8,9},{9,8},{10,11... | collective-permute-start | bytes 786440 | tf_op jit(solution)/shard_map/ppermute | solution.py:521
  27.5 6.8 %collective-permute-start.13 = (f32[8,16,512]{2,1,0:T(8,128)S(1)}, f32[8,16,512]{2,1,0:T(8,128)S(1)}, u32[]{:S(2)}, u32[]{:S(2)}) collective-permute-start(f32[8,16,512]{2,1,0:T(8,128)S(1)} %pad_maximum_fusion.2.refs_4_), channel_id=1, source_target_pairs={{0,1},{1,0},{2,3},{3,2},{4,5},{5,4},{6,7},{7,6},{8,9},{9,8},{10,11... | collective-permute-start | bytes 786440 | tf_op jit(solution)/shard_map/ppermute | solution.py:521
  33.8 1.5 %collective-permute-start.10 = (f32[8,16,512]{2,1,0:T(8,128)S(1)}, f32[8,16,512]{2,1,0:T(8,128)S(1)}, u32[]{:S(2)}, u32[]{:S(2)}) collective-permute-start(f32[8,16,512]{2,1,0:T(8,128)S(1)} %collective-permute-done.8.refs_1_), channel_id=1, source_target_pairs={{0,1},{1,0},{2,3},{3,2},{4,5},{5,4},{6,7},{7,6},{8,9},{9,8},{10,11... | collective-permute-start | bytes 786440 | tf_op jit(solution)/shard_map/ppermute | solution.py:521
  33.9 1.8 %collective-permute-start.14 = (f32[8,16,512]{2,1,0:T(8,128)S(1)}, f32[8,16,512]{2,1,0:T(8,128)S(1)}, u32[]{:S(2)}, u32[]{:S(2)}) collective-permute-start(f32[8,16,512]{2,1,0:T(8,128)S(1)} %collective-permute-done.12.refs_5_), channel_id=1, source_target_pairs={{0,1},{1,0},{2,3},{3,2},{4,5},{5,4},{6,7},{7,6},{8,9},{9,8},{10,11... | collective-permute-start | bytes 786440 | tf_op jit(solution)/shard_map/ppermute | solution.py:521
  54.1 12.4 %all-to-all-start.1 = ((f32[32,8,128]{2,1,0:T(8,128)}), f32[32,8,128]{2,1,0:T(8,128)S(1)}, u32[]{:S(2)}, u32[]{:S(2)}) async-start(f32[32,8,128]{2,1,0:T(8,128)} %bitcast.4), calls=%async_computation.1 | async-start | bytes 262144 | tf_op jit(solution)/shard_map/all_to_all | solution.py:583
  56.9 4.7 %collective-permute-start.17 = (f32[1,64,128]{2,1,0:T(8,128)S(1)}, f32[1,64,128]{2,1,0:T(8,128)S(1)}, u32[]{:S(2)}, u32[]{:S(2)}) collective-permute-start(f32[1,64,128]{2,1,0:T(8,128)S(1)} %get-tuple-element.55), channel_id=1, source_target_pairs={{0,3},{1,2},{2,1},{3,0},{4,7},{5,6},{6,5},{7,4},{8,11},{9,10},{10,... | collective-permute-start | bytes 98312 | tf_op jit(solution)/shard_map/ppermute | solution.py:521
  58.2 4.1 %collective-permute-start.16 = (f32[1,64,128]{2,1,0:T(8,128)S(1)}, f32[1,64,128]{2,1,0:T(8,128)S(1)}, u32[]{:S(2)}, u32[]{:S(2)}) collective-permute-start(f32[1,64,128]{2,1,0:T(8,128)S(1)} %get-tuple-element.56), channel_id=1, source_target_pairs={{0,2},{1,3},{2,0},{3,1},{4,6},{5,7},{6,4},{7,5},{8,10},{9,11},{10,... | collective-permute-start | bytes 98312 | tf_op jit(solution)/shard_map/ppermute | solution.py:521
  58.5 3.8 %collective-permute-start.15 = (f32[1,64,128]{2,1,0:T(8,128)S(1)}, f32[1,64,128]{2,1,0:T(8,128)S(1)}, u32[]{:S(2)}, u32[]{:S(2)}) collective-permute-start(f32[1,64,128]{2,1,0:T(8,128)S(1)} %get-tuple-element.57), channel_id=1, source_target_pairs={{0,1},{1,0},{2,3},{3,2},{4,5},{5,4},{6,7},{7,6},{8,9},{9,8},{10,11... | collective-permute-start | bytes 98312 | tf_op jit(solution)/shard_map/ppermute | solution.py:521
  58.8 7.7 %copy-start.3 = (f32[1,256,128]{2,1,0:T(8,128)S(1)}, f32[1,256,128]{2,1,0:T(8,128)}, u32[]{:S(2)}) copy-start(f32[1,256,128]{2,1,0:T(8,128)} %param.7) | copy-start | bytes 393220
  62.3 4.8 %collective-permute-start.20 = (f32[4,32,128]{2,1,0:T(8,128)S(1)}, f32[4,32,128]{2,1,0:T(8,128)S(1)}, u32[]{:S(2)}, u32[]{:S(2)}) collective-permute-start(f32[4,32,128]{2,1,0:T(8,128)S(1)} %get-tuple-element.52), channel_id=1, source_target_pairs={{0,4},{1,5},{2,6},{3,7},{4,0},{5,1},{6,2},{7,3},{8,12},{9,13},{10,... | collective-permute-start | bytes 196616 | tf_op jit(solution)/shard_map/ppermute | solution.py:521
  63.9 9.0 %collective-permute-start.18 = (f32[4,32,128]{2,1,0:T(8,128)S(1)}, f32[4,32,128]{2,1,0:T(8,128)S(1)}, u32[]{:S(2)}, u32[]{:S(2)}) collective-permute-start(f32[4,32,128]{2,1,0:T(8,128)S(1)} %get-tuple-element.53), channel_id=1, source_target_pairs={{0,16},{1,17},{2,18},{3,19},{4,20},{5,21},{6,22},{7,23},{8,24},{9,... | collective-permute-start | bytes 196616 | tf_op jit(solution)/shard_map/ppermute | solution.py:521
  67.0 2.3 %collective-permute-start.22 = (f32[72,128]{1,0:T(8,128)S(1)}, f32[72,128]{1,0:T(8,128)S(1)}, u32[]{:S(2)}, u32[]{:S(2)}) collective-permute-start(f32[72,128]{1,0:T(8,128)S(1)} %get-tuple-element.38), channel_id=1, source_target_pairs={{0,1},{1,0},{2,3},{3,2},{4,5},{5,4},{6,7},{7,6},{8,9},{9,8},{10,11... | collective-permute-start | bytes 110600 | tf_op jit(solution)/shard_map/ppermute | solution.py:521
  67.1 13.4 %collective-permute-start.21 = (f32[8,32,128]{2,1,0:T(8,128)S(1)}, f32[8,32,128]{2,1,0:T(8,128)S(1)}, u32[]{:S(2)}, u32[]{:S(2)}) collective-permute-start(f32[8,32,128]{2,1,0:T(8,128)S(1)} %pad_maximum_fusion.8), channel_id=1, source_target_pairs={{0,16},{1,17},{2,18},{3,19},{4,20},{5,21},{6,22},{7,23},{8,24},{9,... | collective-permute-start | bytes 393224 | tf_op jit(solution)/shard_map/ppermute | solution.py:521
  69.4 5.3 %collective-permute-start.25 = (f32[72,128]{1,0:T(8,128)S(1)}, f32[72,128]{1,0:T(8,128)S(1)}, u32[]{:S(2)}, u32[]{:S(2)}) collective-permute-start(f32[72,128]{1,0:T(8,128)S(1)} %add.36), channel_id=1, source_target_pairs={{0,6},{1,7},{2,4},{3,5},{4,2},{5,3},{6,0},{7,1},{8,14},{9,15},{10,... | collective-permute-start | bytes 110600 | tf_op jit(solution)/shard_map/ppermute | solution.py:521
  71.3 4.0 %collective-permute-start.24 = (f32[72,128]{1,0:T(8,128)S(1)}, f32[72,128]{1,0:T(8,128)S(1)}, u32[]{:S(2)}, u32[]{:S(2)}) collective-permute-start(f32[72,128]{1,0:T(8,128)S(1)} %add.36), channel_id=1, source_target_pairs={{0,4},{1,5},{2,6},{3,7},{4,0},{5,1},{6,2},{7,3},{8,12},{9,13},{10,... | collective-permute-start | bytes 110600 | tf_op jit(solution)/shard_map/ppermute | solution.py:521
  72.1 4.0 %collective-permute-start.23 = (f32[72,128]{1,0:T(8,128)S(1)}, f32[72,128]{1,0:T(8,128)S(1)}, u32[]{:S(2)}, u32[]{:S(2)}) collective-permute-start(f32[72,128]{1,0:T(8,128)S(1)} %add.36), channel_id=1, source_target_pairs={{0,2},{1,3},{2,0},{3,1},{4,6},{5,7},{6,4},{7,5},{8,10},{9,11},{10,... | collective-permute-start | bytes 110600 | tf_op jit(solution)/shard_map/ppermute | solution.py:521
  72.9 10.3 %collective-permute-start.19 = (f32[8,32,128]{2,1,0:T(8,128)S(1)}, f32[8,32,128]{2,1,0:T(8,128)S(1)}, u32[]{:S(2)}, u32[]{:S(2)}) collective-permute-start(f32[8,32,128]{2,1,0:T(8,128)S(1)} %pad_maximum_fusion.7), channel_id=1, source_target_pairs={{0,8},{1,9},{2,10},{3,11},{4,12},{5,13},{6,14},{7,15},{8,0},{9,1},... | collective-permute-start | bytes 393224 | tf_op jit(solution)/shard_map/ppermute | solution.py:521
  76.1 5.8 %collective-permute-start.28 = (f32[72,128]{1,0:T(8,128)S(1)}, f32[72,128]{1,0:T(8,128)S(1)}, u32[]{:S(2)}, u32[]{:S(2)}) collective-permute-start(f32[72,128]{1,0:T(8,128)S(1)} %add_add_fusion.1), channel_id=1, source_target_pairs={{0,24},{1,25},{2,26},{3,27},{4,28},{5,29},{6,30},{7,31},{8,16},{9,... | collective-permute-start | bytes 110600 | tf_op jit(solution)/shard_map/ppermute | solution.py:521
  77.5 5.2 %collective-permute-start.27 = (f32[72,128]{1,0:T(8,128)S(1)}, f32[72,128]{1,0:T(8,128)S(1)}, u32[]{:S(2)}, u32[]{:S(2)}) collective-permute-start(f32[72,128]{1,0:T(8,128)S(1)} %add_add_fusion.1), channel_id=1, source_target_pairs={{0,16},{1,17},{2,18},{3,19},{4,20},{5,21},{6,22},{7,23},{8,24},{9,... | collective-permute-start | bytes 110600 | tf_op jit(solution)/shard_map/ppermute | solution.py:521
  78.9 4.2 %collective-permute-start.26 = (f32[72,128]{1,0:T(8,128)S(1)}, f32[72,128]{1,0:T(8,128)S(1)}, u32[]{:S(2)}, u32[]{:S(2)}) collective-permute-start(f32[72,128]{1,0:T(8,128)S(1)} %add_add_fusion.1), channel_id=1, source_target_pairs={{0,8},{1,9},{2,10},{3,11},{4,12},{5,13},{6,14},{7,15},{8,0},{9,1},... | collective-permute-start | bytes 110600 | tf_op jit(solution)/shard_map/ppermute | solution.py:521
  83.1 1.3 %collective-permute-start.29 = (f32[72,128]{1,0:T(8,128)S(1)}, f32[72,128]{1,0:T(8,128)S(1)}, u32[]{:S(2)}, u32[]{:S(2)}) collective-permute-start(f32[72,128]{1,0:T(8,128)S(1)} %add_add_fusion.gram_ref), channel_id=1, source_target_pairs={{0,1},{1,0},{2,3},{3,2},{4,5},{5,4},{6,7},{7,6},{8,9},{9,8},{10,11... | collective-permute-start | bytes 110600 | tf_op jit(solution)/shard_map/ppermute | solution.py:521
  84.4 19.3 %all-to-all-start.2 = ((f32[32,4,640]{2,1,0:T(4,128)}), f32[32,4,640]{2,1,0:T(4,128)S(1)}, u32[]{:S(2)}, u32[]{:S(2)}) async-start(f32[32,4,640]{2,1,0:T(4,128)} %bitcast.6), calls=%async_computation.2 | async-start | bytes 655360 | tf_op jit(solution)/shard_map/all_to_all | solution.py:583
  88.0 15.8 %collective-permute-start.30 = (f32[16,32,128]{2,1,0:T(8,128)S(1)}, f32[16,32,128]{2,1,0:T(8,128)S(1)}, u32[]{:S(2)}, u32[]{:S(2)}) collective-permute-start(f32[16,32,128]{2,1,0:T(8,128)S(1)} %pad_maximum_fusion.3), channel_id=1, source_target_pairs={{0,4},{1,5},{2,6},{3,7},{4,0},{5,1},{6,2},{7,3},{8,12},{9,13},{10,... | collective-permute-start | bytes 786440 | tf_op jit(solution)/shard_map/ppermute | solution.py:521
  89.8 14.0 %collective-permute-start.31 = (f32[16,32,128]{2,1,0:T(8,128)S(1)}, f32[16,32,128]{2,1,0:T(8,128)S(1)}, u32[]{:S(2)}, u32[]{:S(2)}) collective-permute-start(f32[16,32,128]{2,1,0:T(8,128)S(1)} %pad_maximum_fusion.4), channel_id=1, source_target_pairs={{0,8},{1,9},{2,10},{3,11},{4,12},{5,13},{6,14},{7,15},{8,0},{9,1},... | collective-permute-start | bytes 786440 | tf_op jit(solution)/shard_map/ppermute | solution.py:521
  98.3 5.5 %copy-start = (f32[32,512]{1,0:T(8,128)S(1)}, f32[32,512]{1,0:T(8,128)}, u32[]{:S(2)}) copy-start(f32[32,512]{1,0:T(8,128)} %kspace_ref.1) | copy-start | bytes 196612
  98.4 5.5 %copy-start.1 = (s32[32,512]{1,0:T(8,128)S(1)}, s32[32,512]{1,0:T(8,128)}, u32[]{:S(2)}) copy-start(s32[32,512]{1,0:T(8,128)} %mask_ref.1) | copy-start | bytes 196612

commit v19 on v16

--- a/solution.py
+++ b/solution.py
@@ -173,12 +173,13 @@
             moved_ref[k * KER + j : k * KER + j + 2 * SUB, :] = high
             moved_ref[rows + k * KER + j : rows + k * KER + j + 2 * SUB, :] = low
     high = jnp.zeros((rows, 2 * channels), jnp.float32)
+    for t in range(tiles):
+        block = samples_ref[t].reshape(2 * channels, tile)
+        high = high + dot(moved_ref[:rows, t * tile : (t + 1) * tile], block, ((1,), (1,)))
     low = jnp.zeros((rows, channels), jnp.float32)
     for t in range(tiles):
-        block = samples_ref[t].reshape(2 * channels, tile)
-        lanes = slice(t * tile, (t + 1) * tile)
-        high = high + dot(moved_ref[:rows, lanes], block, ((1,), (1,)))
-        low = low + dot(moved_ref[rows:, lanes], block[:channels], ((1,), (1,)))
+        block = samples_ref[t, 0].reshape(channels, tile)
+        low = low + dot(moved_ref[rows:, t * tile : (t + 1) * tile], block, ((1,), (1,)))
     return high[:, :channels] + (high[:, channels:] + low)
 
 
@@ -609,7 +610,7 @@
             )
 
     total = kept + exchange(given, devices, 1, AXES)
-    for partners in rounds_of(2, devices):
+    for partners in reversed(rounds_of(2, devices)):
         terms = [exchange(total, devices, way, AXES) for way in partners]
         total = total + terms[0]
         if len(terms) == 3:
@@ -682,7 +683,7 @@
         micros=2,
     )
     near, order = gather_group(group, devices)
-    received, near = lax.optimization_barrier((received, images, near))[::2]
+    received = after(received, images, near)
     half = ((rank // 2 + SUB, rank), f32)
     kept, given, turned = call(
         functools.partial(gram_kernel, cols, per_tile),

time: 98.4 us -> 101 us (1.026)
  starting transfers between devices: 38.2 us -> 41.3 us
    ppermute x27, starting transfers between devices: 28.5 us -> 31.7 us  [exchange(): return lax.ppermute(block, axes, [(i, i ^ mask) for i in range(devices)])]
    all_to_all x3, waiting for transfers between devices: 3.07 us -> 0.47 us  [to_all(): return lax.all_to_all(pieces, axes, 0, 0, tiled=True)]
    ppermute x27, waiting for transfers between devices: 24.5 us -> 26.8 us  [exchange(): return lax.ppermute(block, axes, [(i, i ^ mask) for i in range(devices)])]
  transfers between devices with their start and end apart: 30 -> 30, of which waited for: 14 -> 14; matrix products, arithmetic and copies ran while one was open for 0% -> 0% of each run, Pallas kernels for 16% -> 15%
where the time goes in v19:
time: 101 us
  starting transfers between devices  41.3 us (41%)
  Pallas kernels  28.4 us (28%)
  waiting for transfers between devices  27.3 us (27%)
  between operations  1.54 us (2%)
  local copies, waits for them, and re-layouts  1.07 us (1%)
  other arithmetic  1.05 us (1%)
    ppermute x27, starting transfers between devices, exchange(): return lax.ppermute(block, axes, [(i, i ^ mask) for i in range(devices)])  31.7 us
    pallas_call x7, Pallas kernels, call(): pl.pallas_call(kernel, out_shape=[jax.ShapeDtypeStruct(shape, kind) for s...  28.4 us
    ppermute x27, waiting for transfers between devices, exchange(): return lax.ppermute(block, axes, [(i, i ^ mask) for i in range(devices)])  26.8 us
    all_to_all x3, starting transfers between devices, to_all(): return lax.all_to_all(pieces, axes, 0, 0, tiled=True)  9.56 us
  transfers between devices with their start and end apart: 30, of which 14 were waited for; matrix products, arithmetic and copies ran while one was open for 0% of the time, Pallas kernels for 15%

profile of v19, /device:TPU:0, one launch (start us, length us, event | category | flops | bytes accessed | tf_op | source)
XLA Modules:
  0.0 100.9 jit_solution(14989765268381379956)
XLA Ops:
  0.6 0.9 multiply_bitcast_fusion
  1.5 4.1 %collective-permute-start.5 = (f32[1,32,512]{2,1,0:T(8,128)S(1)}, f32[1,32,512]{2,1,0:T(8,128)S(1)}, u32[]{:S(2)}, u32[]{:S(2)}) collective-permute-start(f32[1,32,512]{2,1,0:T(8,128)S(1)} %multiply_bitcast_fusion), channel_id=1, source_target_pairs={{0,16},{1,17},{2,18},{3,19},{4,20},{5,21},{6,22},{7,23},{8,24},{9,... | collective-permute-start | bytes 196616 | tf_op jit(solution)/shard_map/ppermute | solution.py:522
  5.6 0.9 copy-done.2
  6.5 0.9 shard_map.50
  7.4 3.8 %all-to-all-start = ((f32[32,8,128]{2,1,0:T(8,128)}), f32[32,8,128]{2,1,0:T(8,128)S(1)}, u32[]{:S(2)}, u32[]{:S(2)}) async-start(f32[32,8,128]{2,1,0:T(8,128)} %bitcast.1), calls=%async_computation | async-start | bytes 262144 | tf_op jit(solution)/shard_map/all_to_all | solution.py:584
  11.3 1.8 %collective-permute-start.6 = (f32[2,32,512]{2,1,0:T(8,128)S(1)}, f32[2,32,512]{2,1,0:T(8,128)S(1)}, u32[]{:S(2)}, u32[]{:S(2)}) collective-permute-start(f32[2,32,512]{2,1,0:T(8,128)S(1)} %pad_maximum_fusion.5), channel_id=1, source_target_pairs={{0,8},{1,9},{2,10},{3,11},{4,12},{5,13},{6,14},{7,15},{8,0},{9,1},... | collective-permute-start | bytes 393224 | tf_op jit(solution)/shard_map/ppermute | solution.py:522
  13.1 5.9 %collective-permute-done.6 = f32[2,32,512]{2,1,0:T(8,128)S(1)} collective-permute-done((f32[2,32,512]{2,1,0:T(8,128)S(1)}, f32[2,32,512]{2,1,0:T(8,128)S(1)}, u32[]{:S(2)}, u32[]{:S(2)}) %collective-permute-start.6) | collective-permute-done | bytes 131104 | tf_op jit(solution)/shard_map/ppermute | solution.py:522
  19.0 0.5 all-to-all-done
  19.5 1.1 %collective-permute-start.7 = (f32[4,16,512]{2,1,0:T(8,128)S(1)}, f32[4,16,512]{2,1,0:T(8,128)S(1)}, u32[]{:S(2)}, u32[]{:S(2)}) collective-permute-start(f32[4,16,512]{2,1,0:T(8,128)S(1)} %get-tuple-element.51), channel_id=1, source_target_pairs={{0,4},{1,5},{2,6},{3,7},{4,0},{5,1},{6,2},{7,3},{8,12},{9,13},{10,... | collective-permute-start | bytes 393224 | tf_op jit(solution)/shard_map/ppermute | solution.py:522
  20.6 1.5 %collective-permute-start.11 = (f32[4,16,512]{2,1,0:T(8,128)S(1)}, f32[4,16,512]{2,1,0:T(8,128)S(1)}, u32[]{:S(2)}, u32[]{:S(2)}) collective-permute-start(f32[4,16,512]{2,1,0:T(8,128)S(1)} %get-tuple-element.50), channel_id=1, source_target_pairs={{0,2},{1,3},{2,0},{3,1},{4,6},{5,7},{6,4},{7,5},{8,10},{9,11},{10,... | collective-permute-start | bytes 393224 | tf_op jit(solution)/shard_map/ppermute | solution.py:522
  22.1 3.5 %collective-permute-done.7 = f32[4,16,512]{2,1,0:T(8,128)S(1)} collective-permute-done((f32[4,16,512]{2,1,0:T(8,128)S(1)}, f32[4,16,512]{2,1,0:T(8,128)S(1)}, u32[]{:S(2)}, u32[]{:S(2)}) %collective-permute-start.7) | collective-permute-done | bytes 131104 | tf_op jit(solution)/shard_map/ppermute | solution.py:522
  25.9 1.6 %collective-permute-start.12 = (f32[8,16,512]{2,1,0:T(8,128)S(1)}, f32[8,16,512]{2,1,0:T(8,128)S(1)}, u32[]{:S(2)}, u32[]{:S(2)}) collective-permute-start(f32[8,16,512]{2,1,0:T(8,128)S(1)} %pad_maximum_fusion.2.refs_4_), channel_id=1, source_target_pairs={{0,4},{1,5},{2,6},{3,7},{4,0},{5,1},{6,2},{7,3},{8,12},{9,13},{10,... | collective-permute-start | bytes 786440 | tf_op jit(solution)/shard_map/ppermute | solution.py:522
  27.5 0.5 collective-permute-start.13
  28.0 5.8 %collective-permute-done.8.refs_1_ = f32[8,16,512]{2,1,0:T(8,128)S(1)} collective-permute-done((f32[8,16,512]{2,1,0:T(8,128)S(1)}, f32[8,16,512]{2,1,0:T(8,128)S(1)}, u32[]{:S(2)}, u32[]{:S(2)}) %collective-permute-start.8) | collective-permute-done | bytes 262176 | tf_op jit(solution)/shard_map/ppermute | solution.py:522
  33.9 0.4 collective-permute-start.14
  34.3 1.0 %collective-permute-done.10.refs_3_ = f32[8,16,512]{2,1,0:T(8,128)S(1)} collective-permute-done((f32[8,16,512]{2,1,0:T(8,128)S(1)}, f32[8,16,512]{2,1,0:T(8,128)S(1)}, u32[]{:S(2)}, u32[]{:S(2)}) %collective-permute-start.10) | collective-permute-done | bytes 262176 | tf_op jit(solution)/shard_map/ppermute | solution.py:522
  35.3 0.4 collective-permute-done.14.refs_7_
  35.7 9.3 %shard_map.51 = (bf16[8,2,4,32,512]{4,3,2,1,0:T(8,128)(2,1)S(1)}, f32[256,128]{1,0:T(8,128)S(1)}, f32[8,4,8,128]{3,2,1,0:T(8,128)}, f32[4,64,128]{2,1,0:T(8,128)S(1)}) custom-call(f32[8,4,8,128]{3,2,1,0:T(8,128)S(1)} %bitcast.16, f32[8,16,512]{2,1,0:T(8,128)S(1)} %pad_maximum_fusion.1.refs_0_, f32[8,16,512]{2,1,0:T(8,128)S(1)} %collective-permute-done.8.refs_1_, ...), custom_call_target="tpu_custom_call" | custom-call | flops 12000000000 | tf_op jit(solution)/shard_map/pallas_call | solution.py:507
  44.9 2.8 %all-to-all-start.1 = ((f32[32,8,128]{2,1,0:T(8,128)}), f32[32,8,128]{2,1,0:T(8,128)S(1)}, u32[]{:S(2)}, u32[]{:S(2)}) async-start(f32[32,8,128]{2,1,0:T(8,128)} %bitcast.4), calls=%async_computation.1 | async-start | bytes 262144 | tf_op jit(solution)/shard_map/all_to_all | solution.py:584
  47.7 1.3 %collective-permute-start.17 = (f32[1,64,128]{2,1,0:T(8,128)S(1)}, f32[1,64,128]{2,1,0:T(8,128)S(1)}, u32[]{:S(2)}, u32[]{:S(2)}) collective-permute-start(f32[1,64,128]{2,1,0:T(8,128)S(1)} %get-tuple-element.55), channel_id=1, source_target_pairs={{0,3},{1,2},{2,1},{3,0},{4,7},{5,6},{6,5},{7,4},{8,11},{9,10},{10,... | collective-permute-start | bytes 98312 | tf_op jit(solution)/shard_map/ppermute | solution.py:522
  49.0 0.3 collective-permute-start.16
  49.4 0.3 collective-permute-start.15
  49.6 2.8 %shard_map.52 = f32[8,4,4,640]{3,2,1,0:T(4,128)} custom-call(bf16[8,2,4,32,512]{4,3,2,1,0:T(8,128)(2,1)S(1)} %get-tuple-element.34.samples_ref, f32[256,128]{1,0:T(8,128)S(1)} %get-tuple-element.35.vectors_ref), custom_call_target="tpu_custom_call" | custom-call | flops 2000000000 | tf_op jit(solution)/shard_map/pallas_call | solution.py:507
  52.4 0.7 collective-permute-done.16
  53.2 1.5 %collective-permute-start.20 = (f32[4,32,128]{2,1,0:T(8,128)S(1)}, f32[4,32,128]{2,1,0:T(8,128)S(1)}, u32[]{:S(2)}, u32[]{:S(2)}) collective-permute-start(f32[4,32,128]{2,1,0:T(8,128)S(1)} %get-tuple-element.52), channel_id=1, source_target_pairs={{0,4},{1,5},{2,6},{3,7},{4,0},{5,1},{6,2},{7,3},{8,12},{9,13},{10,... | collective-permute-start | bytes 196616 | tf_op jit(solution)/shard_map/ppermute | solution.py:522
  54.7 2.6 %collective-permute-start.18 = (f32[4,32,128]{2,1,0:T(8,128)S(1)}, f32[4,32,128]{2,1,0:T(8,128)S(1)}, u32[]{:S(2)}, u32[]{:S(2)}) collective-permute-start(f32[4,32,128]{2,1,0:T(8,128)S(1)} %get-tuple-element.53), channel_id=1, source_target_pairs={{0,16},{1,17},{2,18},{3,19},{4,20},{5,21},{6,22},{7,23},{8,24},{9,... | collective-permute-start | bytes 196616 | tf_op jit(solution)/shard_map/ppermute | solution.py:522
  57.3 0.5 shard_map.53
  57.9 2.2 %collective-permute-start.21 = (f32[8,32,128]{2,1,0:T(8,128)S(1)}, f32[8,32,128]{2,1,0:T(8,128)S(1)}, u32[]{:S(2)}, u32[]{:S(2)}) collective-permute-start(f32[8,32,128]{2,1,0:T(8,128)S(1)} %pad_maximum_fusion.8), channel_id=1, source_target_pairs={{0,16},{1,17},{2,18},{3,19},{4,20},{5,21},{6,22},{7,23},{8,24},{9,... | collective-permute-start | bytes 393224 | tf_op jit(solution)/shard_map/ppermute | solution.py:522
  60.2 1.7 %collective-permute-start.25 = (f32[72,128]{1,0:T(8,128)S(1)}, f32[72,128]{1,0:T(8,128)S(1)}, u32[]{:S(2)}, u32[]{:S(2)}) collective-permute-start(f32[72,128]{1,0:T(8,128)S(1)} %add.36), channel_id=1, source_target_pairs={{0,24},{1,25},{2,26},{3,27},{4,28},{5,29},{6,30},{7,31},{8,16},{9,... | collective-permute-start | bytes 110600 | tf_op jit(solution)/shard_map/ppermute | solution.py:522
  61.8 1.5 %collective-permute-start.24 = (f32[72,128]{1,0:T(8,128)S(1)}, f32[72,128]{1,0:T(8,128)S(1)}, u32[]{:S(2)}, u32[]{:S(2)}) collective-permute-start(f32[72,128]{1,0:T(8,128)S(1)} %add.36), channel_id=1, source_target_pairs={{0,16},{1,17},{2,18},{3,19},{4,20},{5,21},{6,22},{7,23},{8,24},{9,... | collective-permute-start | bytes 110600 | tf_op jit(solution)/shard_map/ppermute | solution.py:522
  63.3 1.3 %collective-permute-start.23 = (f32[72,128]{1,0:T(8,128)S(1)}, f32[72,128]{1,0:T(8,128)S(1)}, u32[]{:S(2)}, u32[]{:S(2)}) collective-permute-start(f32[72,128]{1,0:T(8,128)S(1)} %add.36), channel_id=1, source_target_pairs={{0,8},{1,9},{2,10},{3,11},{4,12},{5,13},{6,14},{7,15},{8,0},{9,1},... | collective-permute-start | bytes 110600 | tf_op jit(solution)/shard_map/ppermute | solution.py:522
  64.6 0.8 collective-permute-start.19
  65.4 1.6 %collective-permute-done.25 = f32[72,128]{1,0:T(8,128)S(1)} collective-permute-done((f32[72,128]{1,0:T(8,128)S(1)}, f32[72,128]{1,0:T(8,128)S(1)}, u32[]{:S(2)}, u32[]{:S(2)}) %collective-permute-start.25) | collective-permute-done | bytes 36896 | tf_op jit(solution)/shard_map/ppermute | solution.py:522
  67.0 3.8 %collective-permute-done.24 = f32[72,128]{1,0:T(8,128)S(1)} collective-permute-done((f32[72,128]{1,0:T(8,128)S(1)}, f32[72,128]{1,0:T(8,128)S(1)}, u32[]{:S(2)}, u32[]{:S(2)}) %collective-permute-start.24) | collective-permute-done | bytes 36896 | tf_op jit(solution)/shard_map/ppermute | solution.py:522
  70.8 1.3 %collective-permute-start.28 = (f32[72,128]{1,0:T(8,128)S(1)}, f32[72,128]{1,0:T(8,128)S(1)}, u32[]{:S(2)}, u32[]{:S(2)}) collective-permute-start(f32[72,128]{1,0:T(8,128)S(1)} %add_add_fusion.1), channel_id=1, source_target_pairs={{0,6},{1,7},{2,4},{3,5},{4,2},{5,3},{6,0},{7,1},{8,14},{9,15},{10,... | collective-permute-start | bytes 110600 | tf_op jit(solution)/shard_map/ppermute | solution.py:522
  72.1 1.2 %collective-permute-start.27 = (f32[72,128]{1,0:T(8,128)S(1)}, f32[72,128]{1,0:T(8,128)S(1)}, u32[]{:S(2)}, u32[]{:S(2)}) collective-permute-start(f32[72,128]{1,0:T(8,128)S(1)} %add_add_fusion.1), channel_id=1, source_target_pairs={{0,4},{1,5},{2,6},{3,7},{4,0},{5,1},{6,2},{7,3},{8,12},{9,13},{10,... | collective-permute-start | bytes 110600 | tf_op jit(solution)/shard_map/ppermute | solution.py:522
  73.3 1.1 %collective-permute-start.26 = (f32[72,128]{1,0:T(8,128)S(1)}, f32[72,128]{1,0:T(8,128)S(1)}, u32[]{:S(2)}, u32[]{:S(2)}) collective-permute-start(f32[72,128]{1,0:T(8,128)S(1)} %add_add_fusion.1), channel_id=1, source_target_pairs={{0,2},{1,3},{2,0},{3,1},{4,6},{5,7},{6,4},{7,5},{8,10},{9,11},{10,... | collective-permute-start | bytes 110600 | tf_op jit(solution)/shard_map/ppermute | solution.py:522
  74.4 1.3 %collective-permute-done.28 = f32[72,128]{1,0:T(8,128)S(1)} collective-permute-done((f32[72,128]{1,0:T(8,128)S(1)}, f32[72,128]{1,0:T(8,128)S(1)}, u32[]{:S(2)}, u32[]{:S(2)}) %collective-permute-start.28) | collective-permute-done | bytes 36896 | tf_op jit(solution)/shard_map/ppermute | solution.py:522
  75.7 0.3 collective-permute-done.27
  76.0 1.2 %collective-permute-done.26 = f32[72,128]{1,0:T(8,128)S(1)} collective-permute-done((f32[72,128]{1,0:T(8,128)S(1)}, f32[72,128]{1,0:T(8,128)S(1)}, u32[]{:S(2)}, u32[]{:S(2)}) %collective-permute-start.26) | collective-permute-done | bytes 36896 | tf_op jit(solution)/shard_map/ppermute | solution.py:522
  77.4 1.2 %collective-permute-done.29.other_ref = f32[72,128]{1,0:T(8,128)S(1)} collective-permute-done((f32[72,128]{1,0:T(8,128)S(1)}, f32[72,128]{1,0:T(8,128)S(1)}, u32[]{:S(2)}, u32[]{:S(2)}) %collective-permute-start.29) | collective-permute-done | bytes 36896 | tf_op jit(solution)/shard_map/ppermute | solution.py:522
  78.5 3.0 %all-to-all-start.2 = ((f32[32,4,640]{2,1,0:T(4,128)}), f32[32,4,640]{2,1,0:T(4,128)S(1)}, u32[]{:S(2)}, u32[]{:S(2)}) async-start(f32[32,4,640]{2,1,0:T(4,128)} %bitcast.6), calls=%async_computation.2 | async-start | bytes 655360 | tf_op jit(solution)/shard_map/all_to_all | solution.py:584
  81.5 1.8 %collective-permute-start.30 = (f32[16,32,128]{2,1,0:T(8,128)S(1)}, f32[16,32,128]{2,1,0:T(8,128)S(1)}, u32[]{:S(2)}, u32[]{:S(2)}) collective-permute-start(f32[16,32,128]{2,1,0:T(8,128)S(1)} %pad_maximum_fusion.3), channel_id=1, source_target_pairs={{0,4},{1,5},{2,6},{3,7},{4,0},{5,1},{6,2},{7,3},{8,12},{9,13},{10,... | collective-permute-start | bytes 786440 | tf_op jit(solution)/shard_map/ppermute | solution.py:522
  83.3 1.5 %collective-permute-start.31 = (f32[16,32,128]{2,1,0:T(8,128)S(1)}, f32[16,32,128]{2,1,0:T(8,128)S(1)}, u32[]{:S(2)}, u32[]{:S(2)}) collective-permute-start(f32[16,32,128]{2,1,0:T(8,128)S(1)} %pad_maximum_fusion.4), channel_id=1, source_target_pairs={{0,8},{1,9},{2,10},{3,11},{4,12},{5,13},{6,14},{7,15},{8,0},{9,1},... | collective-permute-start | bytes 786440 | tf_op jit(solution)/shard_map/ppermute | solution.py:522
  84.8 6.4 %shard_map.54 = (f32[128,128]{1,0:T(8,128)S(1)}, f32[128,128]{1,0:T(8,128)S(1)}, s32[1]{0:T(128)}) custom-call(f32[72,128]{1,0:T(8,128)S(1)} %add_add_fusion.gram_ref, f32[72,128]{1,0:T(8,128)S(1)} %collective-permute-done.29.other_ref), custom_call_target="tpu_custom_call" | custom-call | flops 12000000000 | tf_op jit(solution)/shard_map/pallas_call | solution.py:507
  91.9 0.2 conditional.1
  92.1 5.0 %shard_map.55.both_ref = f32[128,128]{1,0:T(8,128)S(1)} custom-call(f32[128,128]{1,0:T(8,128)S(1)} %get-tuple-element.58.gram_ref, f32[128,128]{1,0:T(8,128)S(1)} %get-tuple-element.44.inverse_ref), custom_call_target="tpu_custom_call" | custom-call | tf_op jit(solution)/shard_map/pallas_call | solution.py:507
  97.3 3.6 %shard_map.56 = (f32[32,512]{1,0:T(8,128)}, f32[256,128]{1,0:T(8,128)}) custom-call(f32[128,640]{1,0:T(8,128)S(1)} %reshape.51.images_ref, f32[128,128]{1,0:T(8,128)S(1)} %shard_map.55.both_ref, f32[32,512]{1,0:T(8,128)S(1)} %copy-done, s32[32,512]{1,0:T(8,128)S(1)} %copy-done.1, f32[512,128]{1,0:T(8,128)S(1)} %bitcast.15, f32[512,128]{1,0:T(8,128)S(1)} %bitcast.18, ...), custom_call_target="tpu_custom_call" | custom-call | flops 5000000000 | tf_op jit(solution)/shard_map/pallas_call | solution.py:507
  (45 shorter events, 0.8 us)
Async XLA Ops:
  1.5 9.7 %collective-permute-start.5 = (f32[1,32,512]{2,1,0:T(8,128)S(1)}, f32[1,32,512]{2,1,0:T(8,128)S(1)}, u32[]{:S(2)}, u32[]{:S(2)}) collective-permute-start(f32[1,32,512]{2,1,0:T(8,128)S(1)} %multiply_bitcast_fusion), channel_id=1, source_target_pairs={{0,16},{1,17},{2,18},{3,19},{4,20},{5,21},{6,22},{7,23},{8,24},{9,... | collective-permute-start | bytes 196616 | tf_op jit(solution)/shard_map/ppermute | solution.py:522
  5.6 0.9 copy-start.2
  7.4 12.1 %all-to-all-start = ((f32[32,8,128]{2,1,0:T(8,128)}), f32[32,8,128]{2,1,0:T(8,128)S(1)}, u32[]{:S(2)}, u32[]{:S(2)}) async-start(f32[32,8,128]{2,1,0:T(8,128)} %bitcast.1), calls=%async_computation | async-start | bytes 262144 | tf_op jit(solution)/shard_map/all_to_all | solution.py:584
  11.3 7.7 %collective-permute-start.6 = (f32[2,32,512]{2,1,0:T(8,128)S(1)}, f32[2,32,512]{2,1,0:T(8,128)S(1)}, u32[]{:S(2)}, u32[]{:S(2)}) collective-permute-start(f32[2,32,512]{2,1,0:T(8,128)S(1)} %pad_maximum_fusion.5), channel_id=1, source_target_pairs={{0,8},{1,9},{2,10},{3,11},{4,12},{5,13},{6,14},{7,15},{8,0},{9,1},... | collective-permute-start | bytes 393224 | tf_op jit(solution)/shard_map/ppermute | solution.py:522
  19.5 6.1 %collective-permute-start.7 = (f32[4,16,512]{2,1,0:T(8,128)S(1)}, f32[4,16,512]{2,1,0:T(8,128)S(1)}, u32[]{:S(2)}, u32[]{:S(2)}) collective-permute-start(f32[4,16,512]{2,1,0:T(8,128)S(1)} %get-tuple-element.51), channel_id=1, source_target_pairs={{0,4},{1,5},{2,6},{3,7},{4,0},{5,1},{6,2},{7,3},{8,12},{9,13},{10,... | collective-permute-start | bytes 393224 | tf_op jit(solution)/shard_map/ppermute | solution.py:522
  20.6 5.2 %collective-permute-start.11 = (f32[4,16,512]{2,1,0:T(8,128)S(1)}, f32[4,16,512]{2,1,0:T(8,128)S(1)}, u32[]{:S(2)}, u32[]{:S(2)}) collective-permute-start(f32[4,16,512]{2,1,0:T(8,128)S(1)} %get-tuple-element.50), channel_id=1, source_target_pairs={{0,2},{1,3},{2,0},{3,1},{4,6},{5,7},{6,4},{7,5},{8,10},{9,11},{10,... | collective-permute-start | bytes 393224 | tf_op jit(solution)/shard_map/ppermute | solution.py:522
  25.6 8.1 %collective-permute-start.8 = (f32[8,16,512]{2,1,0:T(8,128)S(1)}, f32[8,16,512]{2,1,0:T(8,128)S(1)}, u32[]{:S(2)}, u32[]{:S(2)}) collective-permute-start(f32[8,16,512]{2,1,0:T(8,128)S(1)} %pad_maximum_fusion.1.refs_0_), channel_id=1, source_target_pairs={{0,2},{1,3},{2,0},{3,1},{4,6},{5,7},{6,4},{7,5},{8,10},{9,11},{10,... | collective-permute-start | bytes 786440 | tf_op jit(solution)/shard_map/ppermute | solution.py:522
  25.9 8.0 %collective-permute-start.12 = (f32[8,16,512]{2,1,0:T(8,128)S(1)}, f32[8,16,512]{2,1,0:T(8,128)S(1)}, u32[]{:S(2)}, u32[]{:S(2)}) collective-permute-start(f32[8,16,512]{2,1,0:T(8,128)S(1)} %pad_maximum_fusion.2.refs_4_), channel_id=1, source_target_pairs={{0,4},{1,5},{2,6},{3,7},{4,0},{5,1},{6,2},{7,3},{8,12},{9,13},{10,... | collective-permute-start | bytes 786440 | tf_op jit(solution)/shard_map/ppermute | solution.py:522
  27.4 6.8 %collective-permute-start.9 = (f32[8,16,512]{2,1,0:T(8,128)S(1)}, f32[8,16,512]{2,1,0:T(8,128)S(1)}, u32[]{:S(2)}, u32[]{:S(2)}) collective-permute-start(f32[8,16,512]{2,1,0:T(8,128)S(1)} %pad_maximum_fusion.1.refs_0_), channel_id=1, source_target_pairs={{0,1},{1,0},{2,3},{3,2},{4,5},{5,4},{6,7},{7,6},{8,9},{9,8},{10,11... | collective-permute-start | bytes 786440 | tf_op jit(solution)/shard_map/ppermute | solution.py:522
  27.5 6.8 %collective-permute-start.13 = (f32[8,16,512]{2,1,0:T(8,128)S(1)}, f32[8,16,512]{2,1,0:T(8,128)S(1)}, u32[]{:S(2)}, u32[]{:S(2)}) collective-permute-start(f32[8,16,512]{2,1,0:T(8,128)S(1)} %pad_maximum_fusion.2.refs_4_), channel_id=1, source_target_pairs={{0,1},{1,0},{2,3},{3,2},{4,5},{5,4},{6,7},{7,6},{8,9},{9,8},{10,11... | collective-permute-start | bytes 786440 | tf_op jit(solution)/shard_map/ppermute | solution.py:522
  33.8 1.5 %collective-permute-start.10 = (f32[8,16,512]{2,1,0:T(8,128)S(1)}, f32[8,16,512]{2,1,0:T(8,128)S(1)}, u32[]{:S(2)}, u32[]{:S(2)}) collective-permute-start(f32[8,16,512]{2,1,0:T(8,128)S(1)} %collective-permute-done.8.refs_1_), channel_id=1, source_target_pairs={{0,1},{1,0},{2,3},{3,2},{4,5},{5,4},{6,7},{7,6},{8,9},{9,8},{10,11... | collective-permute-start | bytes 786440 | tf_op jit(solution)/shard_map/ppermute | solution.py:522
  33.9 1.8 %collective-permute-start.14 = (f32[8,16,512]{2,1,0:T(8,128)S(1)}, f32[8,16,512]{2,1,0:T(8,128)S(1)}, u32[]{:S(2)}, u32[]{:S(2)}) collective-permute-start(f32[8,16,512]{2,1,0:T(8,128)S(1)} %collective-permute-done.12.refs_5_), channel_id=1, source_target_pairs={{0,1},{1,0},{2,3},{3,2},{4,5},{5,4},{6,7},{7,6},{8,9},{9,8},{10,11... | collective-permute-start | bytes 786440 | tf_op jit(solution)/shard_map/ppermute | solution.py:522
  44.9 12.4 %all-to-all-start.1 = ((f32[32,8,128]{2,1,0:T(8,128)}), f32[32,8,128]{2,1,0:T(8,128)S(1)}, u32[]{:S(2)}, u32[]{:S(2)}) async-start(f32[32,8,128]{2,1,0:T(8,128)} %bitcast.4), calls=%async_computation.1 | async-start | bytes 262144 | tf_op jit(solution)/shard_map/all_to_all | solution.py:584
  47.7 4.7 %collective-permute-start.17 = (f32[1,64,128]{2,1,0:T(8,128)S(1)}, f32[1,64,128]{2,1,0:T(8,128)S(1)}, u32[]{:S(2)}, u32[]{:S(2)}) collective-permute-start(f32[1,64,128]{2,1,0:T(8,128)S(1)} %get-tuple-element.55), channel_id=1, source_target_pairs={{0,3},{1,2},{2,1},{3,0},{4,7},{5,6},{6,5},{7,4},{8,11},{9,10},{10,... | collective-permute-start | bytes 98312 | tf_op jit(solution)/shard_map/ppermute | solution.py:522
  49.0 4.1 %collective-permute-start.16 = (f32[1,64,128]{2,1,0:T(8,128)S(1)}, f32[1,64,128]{2,1,0:T(8,128)S(1)}, u32[]{:S(2)}, u32[]{:S(2)}) collective-permute-start(f32[1,64,128]{2,1,0:T(8,128)S(1)} %get-tuple-element.56), channel_id=1, source_target_pairs={{0,2},{1,3},{2,0},{3,1},{4,6},{5,7},{6,4},{7,5},{8,10},{9,11},{10,... | collective-permute-start | bytes 98312 | tf_op jit(solution)/shard_map/ppermute | solution.py:522
  49.4 3.8 %collective-permute-start.15 = (f32[1,64,128]{2,1,0:T(8,128)S(1)}, f32[1,64,128]{2,1,0:T(8,128)S(1)}, u32[]{:S(2)}, u32[]{:S(2)}) collective-permute-start(f32[1,64,128]{2,1,0:T(8,128)S(1)} %get-tuple-element.57), channel_id=1, source_target_pairs={{0,1},{1,0},{2,3},{3,2},{4,5},{5,4},{6,7},{7,6},{8,9},{9,8},{10,11... | collective-permute-start | bytes 98312 | tf_op jit(solution)/shard_map/ppermute | solution.py:522
  49.6 7.7 %copy-start.3 = (f32[1,256,128]{2,1,0:T(8,128)S(1)}, f32[1,256,128]{2,1,0:T(8,128)}, u32[]{:S(2)}) copy-start(f32[1,256,128]{2,1,0:T(8,128)} %param.7) | copy-start | bytes 393220
  53.2 4.8 %collective-permute-start.20 = (f32[4,32,128]{2,1,0:T(8,128)S(1)}, f32[4,32,128]{2,1,0:T(8,128)S(1)}, u32[]{:S(2)}, u32[]{:S(2)}) collective-permute-start(f32[4,32,128]{2,1,0:T(8,128)S(1)} %get-tuple-element.52), channel_id=1, source_target_pairs={{0,4},{1,5},{2,6},{3,7},{4,0},{5,1},{6,2},{7,3},{8,12},{9,13},{10,... | collective-permute-start | bytes 196616 | tf_op jit(solution)/shard_map/ppermute | solution.py:522
  54.7 9.9 %collective-permute-start.18 = (f32[4,32,128]{2,1,0:T(8,128)S(1)}, f32[4,32,128]{2,1,0:T(8,128)S(1)}, u32[]{:S(2)}, u32[]{:S(2)}) collective-permute-start(f32[4,32,128]{2,1,0:T(8,128)S(1)} %get-tuple-element.53), channel_id=1, source_target_pairs={{0,16},{1,17},{2,18},{3,19},{4,20},{5,21},{6,22},{7,23},{8,24},{9,... | collective-permute-start | bytes 196616 | tf_op jit(solution)/shard_map/ppermute | solution.py:522
  57.8 2.3 %collective-permute-start.22 = (f32[72,128]{1,0:T(8,128)S(1)}, f32[72,128]{1,0:T(8,128)S(1)}, u32[]{:S(2)}, u32[]{:S(2)}) collective-permute-start(f32[72,128]{1,0:T(8,128)S(1)} %get-tuple-element.38), channel_id=1, source_target_pairs={{0,1},{1,0},{2,3},{3,2},{4,5},{5,4},{6,7},{7,6},{8,9},{9,8},{10,11... | collective-permute-start | bytes 110600 | tf_op jit(solution)/shard_map/ppermute | solution.py:522
  57.9 16.4 %collective-permute-start.21 = (f32[8,32,128]{2,1,0:T(8,128)S(1)}, f32[8,32,128]{2,1,0:T(8,128)S(1)}, u32[]{:S(2)}, u32[]{:S(2)}) collective-permute-start(f32[8,32,128]{2,1,0:T(8,128)S(1)} %pad_maximum_fusion.8), channel_id=1, source_target_pairs={{0,16},{1,17},{2,18},{3,19},{4,20},{5,21},{6,22},{7,23},{8,24},{9,... | collective-permute-start | bytes 393224 | tf_op jit(solution)/shard_map/ppermute | solution.py:522
  60.2 6.8 %collective-permute-start.25 = (f32[72,128]{1,0:T(8,128)S(1)}, f32[72,128]{1,0:T(8,128)S(1)}, u32[]{:S(2)}, u32[]{:S(2)}) collective-permute-start(f32[72,128]{1,0:T(8,128)S(1)} %add.36), channel_id=1, source_target_pairs={{0,24},{1,25},{2,26},{3,27},{4,28},{5,29},{6,30},{7,31},{8,16},{9,... | collective-permute-start | bytes 110600 | tf_op jit(solution)/shard_map/ppermute | solution.py:522
  61.8 9.0 %collective-permute-start.24 = (f32[72,128]{1,0:T(8,128)S(1)}, f32[72,128]{1,0:T(8,128)S(1)}, u32[]{:S(2)}, u32[]{:S(2)}) collective-permute-start(f32[72,128]{1,0:T(8,128)S(1)} %add.36), channel_id=1, source_target_pairs={{0,16},{1,17},{2,18},{3,19},{4,20},{5,21},{6,22},{7,23},{8,24},{9,... | collective-permute-start | bytes 110600 | tf_op jit(solution)/shard_map/ppermute | solution.py:522
  63.3 7.5 %collective-permute-start.23 = (f32[72,128]{1,0:T(8,128)S(1)}, f32[72,128]{1,0:T(8,128)S(1)}, u32[]{:S(2)}, u32[]{:S(2)}) collective-permute-start(f32[72,128]{1,0:T(8,128)S(1)} %add.36), channel_id=1, source_target_pairs={{0,8},{1,9},{2,10},{3,11},{4,12},{5,13},{6,14},{7,15},{8,0},{9,1},... | collective-permute-start | bytes 110600 | tf_op jit(solution)/shard_map/ppermute | solution.py:522
  64.6 12.7 %collective-permute-start.19 = (f32[8,32,128]{2,1,0:T(8,128)S(1)}, f32[8,32,128]{2,1,0:T(8,128)S(1)}, u32[]{:S(2)}, u32[]{:S(2)}) collective-permute-start(f32[8,32,128]{2,1,0:T(8,128)S(1)} %pad_maximum_fusion.7), channel_id=1, source_target_pairs={{0,8},{1,9},{2,10},{3,11},{4,12},{5,13},{6,14},{7,15},{8,0},{9,1},... | collective-permute-start | bytes 393224 | tf_op jit(solution)/shard_map/ppermute | solution.py:522
  70.8 4.9 %collective-permute-start.28 = (f32[72,128]{1,0:T(8,128)S(1)}, f32[72,128]{1,0:T(8,128)S(1)}, u32[]{:S(2)}, u32[]{:S(2)}) collective-permute-start(f32[72,128]{1,0:T(8,128)S(1)} %add_add_fusion.1), channel_id=1, source_target_pairs={{0,6},{1,7},{2,4},{3,5},{4,2},{5,3},{6,0},{7,1},{8,14},{9,15},{10,... | collective-permute-start | bytes 110600 | tf_op jit(solution)/shard_map/ppermute | solution.py:522
  72.1 4.0 %collective-permute-start.27 = (f32[72,128]{1,0:T(8,128)S(1)}, f32[72,128]{1,0:T(8,128)S(1)}, u32[]{:S(2)}, u32[]{:S(2)}) collective-permute-start(f32[72,128]{1,0:T(8,128)S(1)} %add_add_fusion.1), channel_id=1, source_target_pairs={{0,4},{1,5},{2,6},{3,7},{4,0},{5,1},{6,2},{7,3},{8,12},{9,13},{10,... | collective-permute-start | bytes 110600 | tf_op jit(solution)/shard_map/ppermute | solution.py:522
  73.3 4.0 %collective-permute-start.26 = (f32[72,128]{1,0:T(8,128)S(1)}, f32[72,128]{1,0:T(8,128)S(1)}, u32[]{:S(2)}, u32[]{:S(2)}) collective-permute-start(f32[72,128]{1,0:T(8,128)S(1)} %add_add_fusion.1), channel_id=1, source_target_pairs={{0,2},{1,3},{2,0},{3,1},{4,6},{5,7},{6,4},{7,5},{8,10},{9,11},{10,... | collective-permute-start | bytes 110600 | tf_op jit(solution)/shard_map/ppermute | solution.py:522
  77.2 1.3 %collective-permute-start.29 = (f32[72,128]{1,0:T(8,128)S(1)}, f32[72,128]{1,0:T(8,128)S(1)}, u32[]{:S(2)}, u32[]{:S(2)}) collective-permute-start(f32[72,128]{1,0:T(8,128)S(1)} %add_add_fusion.gram_ref), channel_id=1, source_target_pairs={{0,1},{1,0},{2,3},{3,2},{4,5},{5,4},{6,7},{7,6},{8,9},{9,8},{10,11... | collective-permute-start | bytes 110600 | tf_op jit(solution)/shard_map/ppermute | solution.py:522
  78.5 18.7 %all-to-all-start.2 = ((f32[32,4,640]{2,1,0:T(4,128)}), f32[32,4,640]{2,1,0:T(4,128)S(1)}, u32[]{:S(2)}, u32[]{:S(2)}) async-start(f32[32,4,640]{2,1,0:T(4,128)} %bitcast.6), calls=%async_computation.2 | async-start | bytes 655360 | tf_op jit(solution)/shard_map/all_to_all | solution.py:584
  81.5 15.8 %collective-permute-start.30 = (f32[16,32,128]{2,1,0:T(8,128)S(1)}, f32[16,32,128]{2,1,0:T(8,128)S(1)}, u32[]{:S(2)}, u32[]{:S(2)}) collective-permute-start(f32[16,32,128]{2,1,0:T(8,128)S(1)} %pad_maximum_fusion.3), channel_id=1, source_target_pairs={{0,4},{1,5},{2,6},{3,7},{4,0},{5,1},{6,2},{7,3},{8,12},{9,13},{10,... | collective-permute-start | bytes 786440 | tf_op jit(solution)/shard_map/ppermute | solution.py:522
  83.3 14.0 %collective-permute-start.31 = (f32[16,32,128]{2,1,0:T(8,128)S(1)}, f32[16,32,128]{2,1,0:T(8,128)S(1)}, u32[]{:S(2)}, u32[]{:S(2)}) collective-permute-start(f32[16,32,128]{2,1,0:T(8,128)S(1)} %pad_maximum_fusion.4), channel_id=1, source_target_pairs={{0,8},{1,9},{2,10},{3,11},{4,12},{5,13},{6,14},{7,15},{8,0},{9,1},... | collective-permute-start | bytes 786440 | tf_op jit(solution)/shard_map/ppermute | solution.py:522
  91.9 5.5 %copy-start = (f32[32,512]{1,0:T(8,128)S(1)}, f32[32,512]{1,0:T(8,128)}, u32[]{:S(2)}) copy-start(f32[32,512]{1,0:T(8,128)} %kspace_ref.1) | copy-start | bytes 196612
  91.9 5.5 %copy-start.1 = (s32[32,512]{1,0:T(8,128)S(1)}, s32[32,512]{1,0:T(8,128)}, u32[]{:S(2)}) copy-start(s32[32,512]{1,0:T(8,128)} %mask_ref.1) | copy-start | bytes 196612

commit v20 on v16

--- a/solution.py
+++ b/solution.py
@@ -614,6 +614,7 @@
         total = total + terms[0]
         if len(terms) == 3:
             total = total + (terms[1] + terms[2])
+        images = after(images, terms[0])
         if step < len(ways[0]) - 1:
             advance()
             step += 1
@@ -621,7 +622,7 @@
         advance()
         step += 1
     other = exchange(total, devices, 1, AXES)
-    *parts, total, other, images = lax.optimization_barrier((*parts, total, other, images))
+    *parts, total, other = lax.optimization_barrier((*parts, total, other))
     pieces = []
     for i in range(2):
         mask = ways[i][-1]

time: 98.4 us -> 97.2 us (0.988)
  waiting for transfers between devices: 27.5 us -> 26 us
    ppermute x27, waiting for transfers between devices: 24.5 us -> 22.9 us  [exchange(): return lax.ppermute(block, axes, [(i, i ^ mask) for i in range(devices)])]
  transfers between devices with their start and end apart: 30 -> 30, of which waited for: 14 -> 13; matrix products, arithmetic and copies ran while one was open for 0% -> 0% of each run, Pallas kernels for 16% -> 16%
where the time goes in v20:
time: 97.2 us; the launch traced here: 96.9 us
  starting transfers between devices  38.7 us (40%)
  Pallas kernels  28.5 us (29%)
  waiting for transfers between devices  26 us (27%)
  between operations  1.54 us (2%)
  local copies, waits for them, and re-layouts  1.07 us (1%)
  other arithmetic  1.05 us (1%)
    ppermute x27, starting transfers between devices, exchange(): return lax.ppermute(block, axes, [(i, i ^ mask) for i in range(devices)])  28.7 us
    pallas_call x7, Pallas kernels, call(): pl.pallas_call(kernel, out_shape=[jax.ShapeDtypeStruct(shape, kind) for s...  28.5 us
    ppermute x27, waiting for transfers between devices, exchange(): return lax.ppermute(block, axes, [(i, i ^ mask) for i in range(devices)])  22.9 us
    all_to_all x3, starting transfers between devices, to_all(): return lax.all_to_all(pieces, axes, 0, 0, tiled=True)  10.1 us
    all_to_all x3, waiting for transfers between devices, to_all(): return lax.all_to_all(pieces, axes, 0, 0, tiled=True)  3.08 us
  transfers between devices with their start and end apart: 30, of which 13 were waited for; matrix products, arithmetic and copies ran while one was open for 0% of the time, Pallas kernels for 16%

profile of v20, /device:TPU:0, one launch (start us, length us, event | category | flops | bytes accessed | tf_op | source)
XLA Modules:
  0.0 96.9 jit_solution(3925828225672205712)
XLA Ops:
  0.6 0.9 multiply_bitcast_fusion
  1.5 4.1 %collective-permute-start.5 = (f32[1,32,512]{2,1,0:T(8,128)S(1)}, f32[1,32,512]{2,1,0:T(8,128)S(1)}, u32[]{:S(2)}, u32[]{:S(2)}) collective-permute-start(f32[1,32,512]{2,1,0:T(8,128)S(1)} %multiply_bitcast_fusion), channel_id=1, source_target_pairs={{0,16},{1,17},{2,18},{3,19},{4,20},{5,21},{6,22},{7,23},{8,24},{9,... | collective-permute-start | bytes 196616 | tf_op jit(solution)/shard_map/ppermute | solution.py:521
  5.6 0.9 copy-done.2
  6.5 0.9 shard_map.50
  7.4 3.8 %all-to-all-start = ((f32[32,8,128]{2,1,0:T(8,128)}), f32[32,8,128]{2,1,0:T(8,128)S(1)}, u32[]{:S(2)}, u32[]{:S(2)}) async-start(f32[32,8,128]{2,1,0:T(8,128)} %bitcast.1), calls=%async_computation | async-start | bytes 262144 | tf_op jit(solution)/shard_map/all_to_all | solution.py:583
  11.3 1.8 %collective-permute-start.6 = (f32[2,32,512]{2,1,0:T(8,128)S(1)}, f32[2,32,512]{2,1,0:T(8,128)S(1)}, u32[]{:S(2)}, u32[]{:S(2)}) collective-permute-start(f32[2,32,512]{2,1,0:T(8,128)S(1)} %pad_maximum_fusion.5), channel_id=1, source_target_pairs={{0,8},{1,9},{2,10},{3,11},{4,12},{5,13},{6,14},{7,15},{8,0},{9,1},... | collective-permute-start | bytes 393224 | tf_op jit(solution)/shard_map/ppermute | solution.py:521
  13.1 5.9 %collective-permute-done.6 = f32[2,32,512]{2,1,0:T(8,128)S(1)} collective-permute-done((f32[2,32,512]{2,1,0:T(8,128)S(1)}, f32[2,32,512]{2,1,0:T(8,128)S(1)}, u32[]{:S(2)}, u32[]{:S(2)}) %collective-permute-start.6) | collective-permute-done | bytes 131104 | tf_op jit(solution)/shard_map/ppermute | solution.py:521
  19.0 0.5 all-to-all-done
  19.5 1.1 %collective-permute-start.7 = (f32[4,16,512]{2,1,0:T(8,128)S(1)}, f32[4,16,512]{2,1,0:T(8,128)S(1)}, u32[]{:S(2)}, u32[]{:S(2)}) collective-permute-start(f32[4,16,512]{2,1,0:T(8,128)S(1)} %get-tuple-element.55), channel_id=1, source_target_pairs={{0,4},{1,5},{2,6},{3,7},{4,0},{5,1},{6,2},{7,3},{8,12},{9,13},{10,... | collective-permute-start | bytes 393224 | tf_op jit(solution)/shard_map/ppermute | solution.py:521
  20.6 1.5 %collective-permute-start.11 = (f32[4,16,512]{2,1,0:T(8,128)S(1)}, f32[4,16,512]{2,1,0:T(8,128)S(1)}, u32[]{:S(2)}, u32[]{:S(2)}) collective-permute-start(f32[4,16,512]{2,1,0:T(8,128)S(1)} %get-tuple-element.54), channel_id=1, source_target_pairs={{0,2},{1,3},{2,0},{3,1},{4,6},{5,7},{6,4},{7,5},{8,10},{9,11},{10,... | collective-permute-start | bytes 393224 | tf_op jit(solution)/shard_map/ppermute | solution.py:521
  22.1 3.5 %collective-permute-done.7 = f32[4,16,512]{2,1,0:T(8,128)S(1)} collective-permute-done((f32[4,16,512]{2,1,0:T(8,128)S(1)}, f32[4,16,512]{2,1,0:T(8,128)S(1)}, u32[]{:S(2)}, u32[]{:S(2)}) %collective-permute-start.7) | collective-permute-done | bytes 131104 | tf_op jit(solution)/shard_map/ppermute | solution.py:521
  25.6 0.2 collective-permute-start.8
  25.9 1.6 %collective-permute-start.12 = (f32[8,16,512]{2,1,0:T(8,128)S(1)}, f32[8,16,512]{2,1,0:T(8,128)S(1)}, u32[]{:S(2)}, u32[]{:S(2)}) collective-permute-start(f32[8,16,512]{2,1,0:T(8,128)S(1)} %pad_maximum_fusion.2.refs_4_), channel_id=1, source_target_pairs={{0,4},{1,5},{2,6},{3,7},{4,0},{5,1},{6,2},{7,3},{8,12},{9,13},{10,... | collective-permute-start | bytes 786440 | tf_op jit(solution)/shard_map/ppermute | solution.py:521
  27.5 0.5 collective-permute-start.13
  28.0 5.8 %collective-permute-done.8.refs_1_ = f32[8,16,512]{2,1,0:T(8,128)S(1)} collective-permute-done((f32[8,16,512]{2,1,0:T(8,128)S(1)}, f32[8,16,512]{2,1,0:T(8,128)S(1)}, u32[]{:S(2)}, u32[]{:S(2)}) %collective-permute-start.8) | collective-permute-done | bytes 262176 | tf_op jit(solution)/shard_map/ppermute | solution.py:521
  33.9 0.4 collective-permute-start.14
  34.3 1.0 %collective-permute-done.10.refs_3_ = f32[8,16,512]{2,1,0:T(8,128)S(1)} collective-permute-done((f32[8,16,512]{2,1,0:T(8,128)S(1)}, f32[8,16,512]{2,1,0:T(8,128)S(1)}, u32[]{:S(2)}, u32[]{:S(2)}) %collective-permute-start.10) | collective-permute-done | bytes 262176 | tf_op jit(solution)/shard_map/ppermute | solution.py:521
  35.3 0.4 collective-permute-done.14.refs_7_
  35.7 9.3 %shard_map.51 = (bf16[8,2,4,32,512]{4,3,2,1,0:T(8,128)(2,1)S(1)}, f32[256,128]{1,0:T(8,128)S(1)}, f32[8,4,8,128]{3,2,1,0:T(8,128)}, f32[4,64,128]{2,1,0:T(8,128)S(1)}) custom-call(f32[8,4,8,128]{3,2,1,0:T(8,128)S(1)} %bitcast.16, f32[8,16,512]{2,1,0:T(8,128)S(1)} %pad_maximum_fusion.1.refs_0_, f32[8,16,512]{2,1,0:T(8,128)S(1)} %collective-permute-done.8.refs_1_, ...), custom_call_target="tpu_custom_call" | custom-call | flops 12000000000 | tf_op jit(solution)/shard_map/pallas_call | solution.py:506
  44.9 2.6 %all-to-all-start.1 = ((f32[32,8,128]{2,1,0:T(8,128)}), f32[32,8,128]{2,1,0:T(8,128)S(1)}, u32[]{:S(2)}, u32[]{:S(2)}) async-start(f32[32,8,128]{2,1,0:T(8,128)} %bitcast.5), calls=%async_computation.1 | async-start | bytes 262144 | tf_op jit(solution)/shard_map/all_to_all | solution.py:583
  47.5 1.5 %collective-permute-start.17 = (f32[1,64,128]{2,1,0:T(8,128)S(1)}, f32[1,64,128]{2,1,0:T(8,128)S(1)}, u32[]{:S(2)}, u32[]{:S(2)}) collective-permute-start(f32[1,64,128]{2,1,0:T(8,128)S(1)} %get-tuple-element.59), channel_id=1, source_target_pairs={{0,3},{1,2},{2,1},{3,0},{4,7},{5,6},{6,5},{7,4},{8,11},{9,10},{10,... | collective-permute-start | bytes 98312 | tf_op jit(solution)/shard_map/ppermute | solution.py:521
  49.0 0.4 collective-permute-start.16
  49.5 2.8 %shard_map.52 = f32[8,4,4,640]{3,2,1,0:T(4,128)} custom-call(bf16[8,2,4,32,512]{4,3,2,1,0:T(8,128)(2,1)S(1)} %get-tuple-element.34.samples_ref, f32[256,128]{1,0:T(8,128)S(1)} %get-tuple-element.35.vectors_ref), custom_call_target="tpu_custom_call" | custom-call | flops 2000000000 | tf_op jit(solution)/shard_map/pallas_call | solution.py:506
  52.2 0.9 collective-permute-done.16
  53.1 2.6 %all-to-all-done.1 = f32[32,8,128]{2,1,0:T(8,128)S(1)} async-done(((f32[32,8,128]{2,1,0:T(8,128)}), f32[32,8,128]{2,1,0:T(8,128)S(1)}, u32[]{:S(2)}, u32[]{:S(2)}) %all-to-all-start.1) | async-done | bytes 131104 | tf_op jit(solution)/shard_map/all_to_all | solution.py:583
  55.8 0.7 collective-permute-start.25
  56.5 0.5 shard_map.53
  57.1 0.9 collective-permute-start.23
  58.0 0.3 collective-permute-done.18
  58.3 1.2 %collective-permute-start.21 = (f32[72,128]{1,0:T(8,128)S(1)}, f32[72,128]{1,0:T(8,128)S(1)}, u32[]{:S(2)}, u32[]{:S(2)}) collective-permute-start(f32[72,128]{1,0:T(8,128)S(1)} %add.36), channel_id=1, source_target_pairs={{0,6},{1,7},{2,4},{3,5},{4,2},{5,3},{6,0},{7,1},{8,14},{9,15},{10,... | collective-permute-start | bytes 110600 | tf_op jit(solution)/shard_map/ppermute | solution.py:521
  59.5 1.0 %collective-permute-start.20 = (f32[72,128]{1,0:T(8,128)S(1)}, f32[72,128]{1,0:T(8,128)S(1)}, u32[]{:S(2)}, u32[]{:S(2)}) collective-permute-start(f32[72,128]{1,0:T(8,128)S(1)} %add.36), channel_id=1, source_target_pairs={{0,4},{1,5},{2,6},{3,7},{4,0},{5,1},{6,2},{7,3},{8,12},{9,13},{10,... | collective-permute-start | bytes 110600 | tf_op jit(solution)/shard_map/ppermute | solution.py:521
  60.5 1.3 %collective-permute-start.19 = (f32[72,128]{1,0:T(8,128)S(1)}, f32[72,128]{1,0:T(8,128)S(1)}, u32[]{:S(2)}, u32[]{:S(2)}) collective-permute-start(f32[72,128]{1,0:T(8,128)S(1)} %add.36), channel_id=1, source_target_pairs={{0,2},{1,3},{2,0},{3,1},{4,6},{5,7},{6,4},{7,5},{8,10},{9,11},{10,... | collective-permute-start | bytes 110600 | tf_op jit(solution)/shard_map/ppermute | solution.py:521
  61.8 1.9 %collective-permute-start.26 = (f32[8,32,128]{2,1,0:T(8,128)S(1)}, f32[8,32,128]{2,1,0:T(8,128)S(1)}, u32[]{:S(2)}, u32[]{:S(2)}) collective-permute-start(f32[8,32,128]{2,1,0:T(8,128)S(1)} %pad_maximum_fusion.8), channel_id=1, source_target_pairs={{0,16},{1,17},{2,18},{3,19},{4,20},{5,21},{6,22},{7,23},{8,24},{9,... | collective-permute-start | bytes 393224 | tf_op jit(solution)/shard_map/ppermute | solution.py:521
  63.7 0.7 collective-permute-done.19
  64.5 2.1 %collective-permute-start.28 = (f32[72,128]{1,0:T(8,128)S(1)}, f32[72,128]{1,0:T(8,128)S(1)}, u32[]{:S(2)}, u32[]{:S(2)}) collective-permute-start(f32[72,128]{1,0:T(8,128)S(1)} %add_add_fusion.1), channel_id=1, source_target_pairs={{0,24},{1,25},{2,26},{3,27},{4,28},{5,29},{6,30},{7,31},{8,16},{9,... | collective-permute-start | bytes 110600 | tf_op jit(solution)/shard_map/ppermute | solution.py:521
  66.6 0.8 collective-permute-start.27
  67.3 1.6 %collective-permute-start.22 = (f32[72,128]{1,0:T(8,128)S(1)}, f32[72,128]{1,0:T(8,128)S(1)}, u32[]{:S(2)}, u32[]{:S(2)}) collective-permute-start(f32[72,128]{1,0:T(8,128)S(1)} %add_add_fusion.1), channel_id=1, source_target_pairs={{0,8},{1,9},{2,10},{3,11},{4,12},{5,13},{6,14},{7,15},{8,0},{9,1},... | collective-permute-start | bytes 110600 | tf_op jit(solution)/shard_map/ppermute | solution.py:521
  69.0 0.5 collective-permute-start.24
  69.5 3.3 %collective-permute-done.22 = f32[72,128]{1,0:T(8,128)S(1)} collective-permute-done((f32[72,128]{1,0:T(8,128)S(1)}, f32[72,128]{1,0:T(8,128)S(1)}, u32[]{:S(2)}, u32[]{:S(2)}) %collective-permute-start.22) | collective-permute-done | bytes 36896 | tf_op jit(solution)/shard_map/ppermute | solution.py:521
  72.8 3.7 %all-to-all-start.2 = ((f32[32,4,640]{2,1,0:T(4,128)}), f32[32,4,640]{2,1,0:T(4,128)S(1)}, u32[]{:S(2)}, u32[]{:S(2)}) async-start(f32[32,4,640]{2,1,0:T(4,128)} %bitcast.4), calls=%async_computation.2 | async-start | bytes 655360 | tf_op jit(solution)/shard_map/all_to_all | solution.py:583
  76.5 0.3 collective-permute-start.29
  76.8 0.9 collective-permute-done.29.other_ref
  77.7 1.8 %collective-permute-start.30 = (f32[16,32,128]{2,1,0:T(8,128)S(1)}, f32[16,32,128]{2,1,0:T(8,128)S(1)}, u32[]{:S(2)}, u32[]{:S(2)}) collective-permute-start(f32[16,32,128]{2,1,0:T(8,128)S(1)} %pad_maximum_fusion.3), channel_id=1, source_target_pairs={{0,4},{1,5},{2,6},{3,7},{4,0},{5,1},{6,2},{7,3},{8,12},{9,13},{10,... | collective-permute-start | bytes 786440 | tf_op jit(solution)/shard_map/ppermute | solution.py:521
  79.5 1.5 %collective-permute-start.31 = (f32[16,32,128]{2,1,0:T(8,128)S(1)}, f32[16,32,128]{2,1,0:T(8,128)S(1)}, u32[]{:S(2)}, u32[]{:S(2)}) collective-permute-start(f32[16,32,128]{2,1,0:T(8,128)S(1)} %pad_maximum_fusion.4), channel_id=1, source_target_pairs={{0,8},{1,9},{2,10},{3,11},{4,12},{5,13},{6,14},{7,15},{8,0},{9,1},... | collective-permute-start | bytes 786440 | tf_op jit(solution)/shard_map/ppermute | solution.py:521
  81.0 6.4 %shard_map.54 = (f32[128,128]{1,0:T(8,128)S(1)}, f32[128,128]{1,0:T(8,128)S(1)}, s32[1]{0:T(128)}) custom-call(f32[72,128]{1,0:T(8,128)S(1)} %add_add_fusion.gram_ref, f32[72,128]{1,0:T(8,128)S(1)} %collective-permute-done.29.other_ref), custom_call_target="tpu_custom_call" | custom-call | flops 12000000000 | tf_op jit(solution)/shard_map/pallas_call | solution.py:506
  88.1 5.0 %shard_map.55.both_ref = f32[128,128]{1,0:T(8,128)S(1)} custom-call(f32[128,128]{1,0:T(8,128)S(1)} %get-tuple-element.62.gram_ref, f32[128,128]{1,0:T(8,128)S(1)} %get-tuple-element.48.inverse_ref), custom_call_target="tpu_custom_call" | custom-call | tf_op jit(solution)/shard_map/pallas_call | solution.py:506
  93.1 0.1 reshape.51.images_ref
  93.3 3.6 %shard_map.56 = (f32[32,512]{1,0:T(8,128)}, f32[256,128]{1,0:T(8,128)}) custom-call(f32[128,640]{1,0:T(8,128)S(1)} %reshape.51.images_ref, f32[128,128]{1,0:T(8,128)S(1)} %shard_map.55.both_ref, f32[32,512]{1,0:T(8,128)S(1)} %copy-done, s32[32,512]{1,0:T(8,128)S(1)} %copy-done.1, f32[512,128]{1,0:T(8,128)S(1)} %bitcast.15, f32[512,128]{1,0:T(8,128)S(1)} %bitcast.18, ...), custom_call_target="tpu_custom_call" | custom-call | flops 5000000000 | tf_op jit(solution)/shard_map/pallas_call | solution.py:506
  (45 shorter events, 0.5 us)
Async XLA Ops:
  1.5 9.7 %collective-permute-start.5 = (f32[1,32,512]{2,1,0:T(8,128)S(1)}, f32[1,32,512]{2,1,0:T(8,128)S(1)}, u32[]{:S(2)}, u32[]{:S(2)}) collective-permute-start(f32[1,32,512]{2,1,0:T(8,128)S(1)} %multiply_bitcast_fusion), channel_id=1, source_target_pairs={{0,16},{1,17},{2,18},{3,19},{4,20},{5,21},{6,22},{7,23},{8,24},{9,... | collective-permute-start | bytes 196616 | tf_op jit(solution)/shard_map/ppermute | solution.py:521
  5.6 0.9 copy-start.2
  7.4 12.1 %all-to-all-start = ((f32[32,8,128]{2,1,0:T(8,128)}), f32[32,8,128]{2,1,0:T(8,128)S(1)}, u32[]{:S(2)}, u32[]{:S(2)}) async-start(f32[32,8,128]{2,1,0:T(8,128)} %bitcast.1), calls=%async_computation | async-start | bytes 262144 | tf_op jit(solution)/shard_map/all_to_all | solution.py:583
  11.3 7.7 %collective-permute-start.6 = (f32[2,32,512]{2,1,0:T(8,128)S(1)}, f32[2,32,512]{2,1,0:T(8,128)S(1)}, u32[]{:S(2)}, u32[]{:S(2)}) collective-permute-start(f32[2,32,512]{2,1,0:T(8,128)S(1)} %pad_maximum_fusion.5), channel_id=1, source_target_pairs={{0,8},{1,9},{2,10},{3,11},{4,12},{5,13},{6,14},{7,15},{8,0},{9,1},... | collective-permute-start | bytes 393224 | tf_op jit(solution)/shard_map/ppermute | solution.py:521
  19.5 6.1 %collective-permute-start.7 = (f32[4,16,512]{2,1,0:T(8,128)S(1)}, f32[4,16,512]{2,1,0:T(8,128)S(1)}, u32[]{:S(2)}, u32[]{:S(2)}) collective-permute-start(f32[4,16,512]{2,1,0:T(8,128)S(1)} %get-tuple-element.55), channel_id=1, source_target_pairs={{0,4},{1,5},{2,6},{3,7},{4,0},{5,1},{6,2},{7,3},{8,12},{9,13},{10,... | collective-permute-start | bytes 393224 | tf_op jit(solution)/shard_map/ppermute | solution.py:521
  20.6 5.2 %collective-permute-start.11 = (f32[4,16,512]{2,1,0:T(8,128)S(1)}, f32[4,16,512]{2,1,0:T(8,128)S(1)}, u32[]{:S(2)}, u32[]{:S(2)}) collective-permute-start(f32[4,16,512]{2,1,0:T(8,128)S(1)} %get-tuple-element.54), channel_id=1, source_target_pairs={{0,2},{1,3},{2,0},{3,1},{4,6},{5,7},{6,4},{7,5},{8,10},{9,11},{10,... | collective-permute-start | bytes 393224 | tf_op jit(solution)/shard_map/ppermute | solution.py:521
  25.6 8.1 %collective-permute-start.8 = (f32[8,16,512]{2,1,0:T(8,128)S(1)}, f32[8,16,512]{2,1,0:T(8,128)S(1)}, u32[]{:S(2)}, u32[]{:S(2)}) collective-permute-start(f32[8,16,512]{2,1,0:T(8,128)S(1)} %pad_maximum_fusion.1.refs_0_), channel_id=1, source_target_pairs={{0,2},{1,3},{2,0},{3,1},{4,6},{5,7},{6,4},{7,5},{8,10},{9,11},{10,... | collective-permute-start | bytes 786440 | tf_op jit(solution)/shard_map/ppermute | solution.py:521
  25.9 8.0 %collective-permute-start.12 = (f32[8,16,512]{2,1,0:T(8,128)S(1)}, f32[8,16,512]{2,1,0:T(8,128)S(1)}, u32[]{:S(2)}, u32[]{:S(2)}) collective-permute-start(f32[8,16,512]{2,1,0:T(8,128)S(1)} %pad_maximum_fusion.2.refs_4_), channel_id=1, source_target_pairs={{0,4},{1,5},{2,6},{3,7},{4,0},{5,1},{6,2},{7,3},{8,12},{9,13},{10,... | collective-permute-start | bytes 786440 | tf_op jit(solution)/shard_map/ppermute | solution.py:521
  27.4 6.8 %collective-permute-start.9 = (f32[8,16,512]{2,1,0:T(8,128)S(1)}, f32[8,16,512]{2,1,0:T(8,128)S(1)}, u32[]{:S(2)}, u32[]{:S(2)}) collective-permute-start(f32[8,16,512]{2,1,0:T(8,128)S(1)} %pad_maximum_fusion.1.refs_0_), channel_id=1, source_target_pairs={{0,1},{1,0},{2,3},{3,2},{4,5},{5,4},{6,7},{7,6},{8,9},{9,8},{10,11... | collective-permute-start | bytes 786440 | tf_op jit(solution)/shard_map/ppermute | solution.py:521
  27.5 6.8 %collective-permute-start.13 = (f32[8,16,512]{2,1,0:T(8,128)S(1)}, f32[8,16,512]{2,1,0:T(8,128)S(1)}, u32[]{:S(2)}, u32[]{:S(2)}) collective-permute-start(f32[8,16,512]{2,1,0:T(8,128)S(1)} %pad_maximum_fusion.2.refs_4_), channel_id=1, source_target_pairs={{0,1},{1,0},{2,3},{3,2},{4,5},{5,4},{6,7},{7,6},{8,9},{9,8},{10,11... | collective-permute-start | bytes 786440 | tf_op jit(solution)/shard_map/ppermute | solution.py:521
  33.8 1.5 %collective-permute-start.10 = (f32[8,16,512]{2,1,0:T(8,128)S(1)}, f32[8,16,512]{2,1,0:T(8,128)S(1)}, u32[]{:S(2)}, u32[]{:S(2)}) collective-permute-start(f32[8,16,512]{2,1,0:T(8,128)S(1)} %collective-permute-done.8.refs_1_), channel_id=1, source_target_pairs={{0,1},{1,0},{2,3},{3,2},{4,5},{5,4},{6,7},{7,6},{8,9},{9,8},{10,11... | collective-permute-start | bytes 786440 | tf_op jit(solution)/shard_map/ppermute | solution.py:521
  33.9 1.8 %collective-permute-start.14 = (f32[8,16,512]{2,1,0:T(8,128)S(1)}, f32[8,16,512]{2,1,0:T(8,128)S(1)}, u32[]{:S(2)}, u32[]{:S(2)}) collective-permute-start(f32[8,16,512]{2,1,0:T(8,128)S(1)} %collective-permute-done.12.refs_5_), channel_id=1, source_target_pairs={{0,1},{1,0},{2,3},{3,2},{4,5},{5,4},{6,7},{7,6},{8,9},{9,8},{10,11... | collective-permute-start | bytes 786440 | tf_op jit(solution)/shard_map/ppermute | solution.py:521
  44.9 10.8 %all-to-all-start.1 = ((f32[32,8,128]{2,1,0:T(8,128)}), f32[32,8,128]{2,1,0:T(8,128)S(1)}, u32[]{:S(2)}, u32[]{:S(2)}) async-start(f32[32,8,128]{2,1,0:T(8,128)} %bitcast.5), calls=%async_computation.1 | async-start | bytes 262144 | tf_op jit(solution)/shard_map/all_to_all | solution.py:583
  47.5 4.7 %collective-permute-start.17 = (f32[1,64,128]{2,1,0:T(8,128)S(1)}, f32[1,64,128]{2,1,0:T(8,128)S(1)}, u32[]{:S(2)}, u32[]{:S(2)}) collective-permute-start(f32[1,64,128]{2,1,0:T(8,128)S(1)} %get-tuple-element.59), channel_id=1, source_target_pairs={{0,3},{1,2},{2,1},{3,0},{4,7},{5,6},{6,5},{7,4},{8,11},{9,10},{10,... | collective-permute-start | bytes 98312 | tf_op jit(solution)/shard_map/ppermute | solution.py:521
  49.0 4.1 %collective-permute-start.16 = (f32[1,64,128]{2,1,0:T(8,128)S(1)}, f32[1,64,128]{2,1,0:T(8,128)S(1)}, u32[]{:S(2)}, u32[]{:S(2)}) collective-permute-start(f32[1,64,128]{2,1,0:T(8,128)S(1)} %get-tuple-element.60), channel_id=1, source_target_pairs={{0,2},{1,3},{2,0},{3,1},{4,6},{5,7},{6,4},{7,5},{8,10},{9,11},{10,... | collective-permute-start | bytes 98312 | tf_op jit(solution)/shard_map/ppermute | solution.py:521
  49.4 3.7 %collective-permute-start.15 = (f32[1,64,128]{2,1,0:T(8,128)S(1)}, f32[1,64,128]{2,1,0:T(8,128)S(1)}, u32[]{:S(2)}, u32[]{:S(2)}) collective-permute-start(f32[1,64,128]{2,1,0:T(8,128)S(1)} %get-tuple-element.61), channel_id=1, source_target_pairs={{0,1},{1,0},{2,3},{3,2},{4,5},{5,4},{6,7},{7,6},{8,9},{9,8},{10,11... | collective-permute-start | bytes 98312 | tf_op jit(solution)/shard_map/ppermute | solution.py:521
  49.5 7.0 %copy-start.3 = (f32[1,256,128]{2,1,0:T(8,128)S(1)}, f32[1,256,128]{2,1,0:T(8,128)}, u32[]{:S(2)}) copy-start(f32[1,256,128]{2,1,0:T(8,128)} %param.7) | copy-start | bytes 393220
  55.8 6.0 %collective-permute-start.25 = (f32[4,32,128]{2,1,0:T(8,128)S(1)}, f32[4,32,128]{2,1,0:T(8,128)S(1)}, u32[]{:S(2)}, u32[]{:S(2)}) collective-permute-start(f32[4,32,128]{2,1,0:T(8,128)S(1)} %get-tuple-element.56), channel_id=1, source_target_pairs={{0,4},{1,5},{2,6},{3,7},{4,0},{5,1},{6,2},{7,3},{8,12},{9,13},{10,... | collective-permute-start | bytes 196616 | tf_op jit(solution)/shard_map/ppermute | solution.py:521
  57.0 1.3 %collective-permute-start.18 = (f32[72,128]{1,0:T(8,128)S(1)}, f32[72,128]{1,0:T(8,128)S(1)}, u32[]{:S(2)}, u32[]{:S(2)}) collective-permute-start(f32[72,128]{1,0:T(8,128)S(1)} %get-tuple-element.40), channel_id=1, source_target_pairs={{0,1},{1,0},{2,3},{3,2},{4,5},{5,4},{6,7},{7,6},{8,9},{9,8},{10,11... | collective-permute-start | bytes 110600 | tf_op jit(solution)/shard_map/ppermute | solution.py:521
  57.1 11.9 %collective-permute-start.23 = (f32[4,32,128]{2,1,0:T(8,128)S(1)}, f32[4,32,128]{2,1,0:T(8,128)S(1)}, u32[]{:S(2)}, u32[]{:S(2)}) collective-permute-start(f32[4,32,128]{2,1,0:T(8,128)S(1)} %get-tuple-element.57), channel_id=1, source_target_pairs={{0,16},{1,17},{2,18},{3,19},{4,20},{5,21},{6,22},{7,23},{8,24},{9,... | collective-permute-start | bytes 196616 | tf_op jit(solution)/shard_map/ppermute | solution.py:521
  58.3 5.4 %collective-permute-start.21 = (f32[72,128]{1,0:T(8,128)S(1)}, f32[72,128]{1,0:T(8,128)S(1)}, u32[]{:S(2)}, u32[]{:S(2)}) collective-permute-start(f32[72,128]{1,0:T(8,128)S(1)} %add.36), channel_id=1, source_target_pairs={{0,6},{1,7},{2,4},{3,5},{4,2},{5,3},{6,0},{7,1},{8,14},{9,15},{10,... | collective-permute-start | bytes 110600 | tf_op jit(solution)/shard_map/ppermute | solution.py:521
  59.5 4.2 %collective-permute-start.20 = (f32[72,128]{1,0:T(8,128)S(1)}, f32[72,128]{1,0:T(8,128)S(1)}, u32[]{:S(2)}, u32[]{:S(2)}) collective-permute-start(f32[72,128]{1,0:T(8,128)S(1)} %add.36), channel_id=1, source_target_pairs={{0,4},{1,5},{2,6},{3,7},{4,0},{5,1},{6,2},{7,3},{8,12},{9,13},{10,... | collective-permute-start | bytes 110600 | tf_op jit(solution)/shard_map/ppermute | solution.py:521
  60.5 4.0 %collective-permute-start.19 = (f32[72,128]{1,0:T(8,128)S(1)}, f32[72,128]{1,0:T(8,128)S(1)}, u32[]{:S(2)}, u32[]{:S(2)}) collective-permute-start(f32[72,128]{1,0:T(8,128)S(1)} %add.36), channel_id=1, source_target_pairs={{0,2},{1,3},{2,0},{3,1},{4,6},{5,7},{6,4},{7,5},{8,10},{9,11},{10,... | collective-permute-start | bytes 110600 | tf_op jit(solution)/shard_map/ppermute | solution.py:521
  61.8 15.0 %collective-permute-start.26 = (f32[8,32,128]{2,1,0:T(8,128)S(1)}, f32[8,32,128]{2,1,0:T(8,128)S(1)}, u32[]{:S(2)}, u32[]{:S(2)}) collective-permute-start(f32[8,32,128]{2,1,0:T(8,128)S(1)} %pad_maximum_fusion.8), channel_id=1, source_target_pairs={{0,16},{1,17},{2,18},{3,19},{4,20},{5,21},{6,22},{7,23},{8,24},{9,... | collective-permute-start | bytes 393224 | tf_op jit(solution)/shard_map/ppermute | solution.py:521
  64.5 11.9 %collective-permute-start.28 = (f32[72,128]{1,0:T(8,128)S(1)}, f32[72,128]{1,0:T(8,128)S(1)}, u32[]{:S(2)}, u32[]{:S(2)}) collective-permute-start(f32[72,128]{1,0:T(8,128)S(1)} %add_add_fusion.1), channel_id=1, source_target_pairs={{0,24},{1,25},{2,26},{3,27},{4,28},{5,29},{6,30},{7,31},{8,16},{9,... | collective-permute-start | bytes 110600 | tf_op jit(solution)/shard_map/ppermute | solution.py:521
  66.6 9.9 %collective-permute-start.27 = (f32[72,128]{1,0:T(8,128)S(1)}, f32[72,128]{1,0:T(8,128)S(1)}, u32[]{:S(2)}, u32[]{:S(2)}) collective-permute-start(f32[72,128]{1,0:T(8,128)S(1)} %add_add_fusion.1), channel_id=1, source_target_pairs={{0,16},{1,17},{2,18},{3,19},{4,20},{5,21},{6,22},{7,23},{8,24},{9,... | collective-permute-start | bytes 110600 | tf_op jit(solution)/shard_map/ppermute | solution.py:521
  67.3 5.4 %collective-permute-start.22 = (f32[72,128]{1,0:T(8,128)S(1)}, f32[72,128]{1,0:T(8,128)S(1)}, u32[]{:S(2)}, u32[]{:S(2)}) collective-permute-start(f32[72,128]{1,0:T(8,128)S(1)} %add_add_fusion.1), channel_id=1, source_target_pairs={{0,8},{1,9},{2,10},{3,11},{4,12},{5,13},{6,14},{7,15},{8,0},{9,1},... | collective-permute-start | bytes 110600 | tf_op jit(solution)/shard_map/ppermute | solution.py:521
  69.0 7.8 %collective-permute-start.24 = (f32[8,32,128]{2,1,0:T(8,128)S(1)}, f32[8,32,128]{2,1,0:T(8,128)S(1)}, u32[]{:S(2)}, u32[]{:S(2)}) collective-permute-start(f32[8,32,128]{2,1,0:T(8,128)S(1)} %pad_maximum_fusion.7), channel_id=1, source_target_pairs={{0,8},{1,9},{2,10},{3,11},{4,12},{5,13},{6,14},{7,15},{8,0},{9,1},... | collective-permute-start | bytes 393224 | tf_op jit(solution)/shard_map/ppermute | solution.py:521
  72.8 20.4 %all-to-all-start.2 = ((f32[32,4,640]{2,1,0:T(4,128)}), f32[32,4,640]{2,1,0:T(4,128)S(1)}, u32[]{:S(2)}, u32[]{:S(2)}) async-start(f32[32,4,640]{2,1,0:T(4,128)} %bitcast.4), calls=%async_computation.2 | async-start | bytes 655360 | tf_op jit(solution)/shard_map/all_to_all | solution.py:583
  76.5 1.3 %collective-permute-start.29 = (f32[72,128]{1,0:T(8,128)S(1)}, f32[72,128]{1,0:T(8,128)S(1)}, u32[]{:S(2)}, u32[]{:S(2)}) collective-permute-start(f32[72,128]{1,0:T(8,128)S(1)} %add_add_fusion.gram_ref), channel_id=1, source_target_pairs={{0,1},{1,0},{2,3},{3,2},{4,5},{5,4},{6,7},{7,6},{8,9},{9,8},{10,11... | collective-permute-start | bytes 110600 | tf_op jit(solution)/shard_map/ppermute | solution.py:521
  77.7 15.5 %collective-permute-start.30 = (f32[16,32,128]{2,1,0:T(8,128)S(1)}, f32[16,32,128]{2,1,0:T(8,128)S(1)}, u32[]{:S(2)}, u32[]{:S(2)}) collective-permute-start(f32[16,32,128]{2,1,0:T(8,128)S(1)} %pad_maximum_fusion.3), channel_id=1, source_target_pairs={{0,4},{1,5},{2,6},{3,7},{4,0},{5,1},{6,2},{7,3},{8,12},{9,13},{10,... | collective-permute-start | bytes 786440 | tf_op jit(solution)/shard_map/ppermute | solution.py:521
  79.5 13.8 %collective-permute-start.31 = (f32[16,32,128]{2,1,0:T(8,128)S(1)}, f32[16,32,128]{2,1,0:T(8,128)S(1)}, u32[]{:S(2)}, u32[]{:S(2)}) collective-permute-start(f32[16,32,128]{2,1,0:T(8,128)S(1)} %pad_maximum_fusion.4), channel_id=1, source_target_pairs={{0,8},{1,9},{2,10},{3,11},{4,12},{5,13},{6,14},{7,15},{8,0},{9,1},... | collective-permute-start | bytes 786440 | tf_op jit(solution)/shard_map/ppermute | solution.py:521
  88.0 5.2 %copy-start = (f32[32,512]{1,0:T(8,128)S(1)}, f32[32,512]{1,0:T(8,128)}, u32[]{:S(2)}) copy-start(f32[32,512]{1,0:T(8,128)} %kspace_ref.1) | copy-start | bytes 196612
  88.1 5.2 %copy-start.1 = (s32[32,512]{1,0:T(8,128)S(1)}, s32[32,512]{1,0:T(8,128)}, u32[]{:S(2)}) copy-start(s32[32,512]{1,0:T(8,128)} %mask_ref.1) | copy-start | bytes 196612
